TPU v7x, 32 devices: a whole 2x2x4 slice. The times are simulated.
32 devices in a mesh: seq: 2 (over x), expert: 4 (over y, core), mp: 4 (over z).
Axes of the slice: x: 2, y: 2, z: 4, core: 2. Of those that a mesh axis runs over, the one named last changes fastest.
Arguments:
- tokens: bfloat16 [256, 6144], P(('seq', 'expert', 'mp')), may hold values from -6 to 6
- out_grad: bfloat16 [256, 6144], P(('seq', 'expert', 'mp')), may hold values from -3 to 3
- kept_mask: int32 [256], P(('seq', 'expert', 'mp')), may hold values 0 or 1
- routes: int32 [256, 2], P(('seq', 'expert', 'mp')), may hold values from 0 to 3, all different within a row; in each aligned block of 8 rows (0 to 7, 8 to 15, ...) at most 4 rows name the same one
- router: bfloat16 [6144, 4], replicated, may hold values from -0.078125 to 0.078125
- gate_weight: bfloat16 [4, 6144, 8192], P('expert', None, ('seq', 'mp')), may hold values from -0.078125 to 0.078125
- up_weight: bfloat16 [4, 6144, 8192], P('expert', None, ('seq', 'mp')), may hold values from -0.078125 to 0.078125
- down_weight: bfloat16 [4, 8192, 6144], P('expert', ('seq', 'mp')), may hold values from -0.0625 to 0.0625
Outputs:
- d_tokens: bfloat16 [256, 6144], P(('seq', 'expert', 'mp'))
- gate_grad: float32 [256, 2], P(('seq', 'expert', 'mp'))
Inputs may be any that keep to these rules, and one draw needn't show every extreme that they name: `routes`: among the 8 rows of one device, at most 4 name any one expert, and in every draw some expert is named by exactly 4 rows of some device.
All inputs are finite; a program needn't handle non-finite values. No bound on the sum of `kept_mask` on one device may be relied on, other than what follows from the above.
Results may differ from a plain program's by a relative error of at most 0.02.
Values may be sent and summed in bfloat16 or wider, within the bound.
No kernel may reach another device: no remote copies, remote signals or barrier semaphores. Data moves between devices by JAX's collectives and lax.ppermute only.
A program may use at most 128 MiB of HBM per device.

v0:
```python
import jax
import jax.numpy as jnp
from jax import lax
from jax.sharding import PartitionSpec as P


def on_device(tokens, out_grad, kept_mask, routes, router, gate_weight, up_weight, down_weight):
    row_count = tokens.shape[0]
    width = tokens.shape[1]
    expert_count = lax.axis_size("expert")
    capacity = max(3 * row_count // 8, 2 * row_count // expert_count)
    logits = jnp.dot(tokens, router, preferred_element_type=jnp.float32)
    columns = lax.broadcasted_iota(jnp.int32, (row_count, expert_count), 1)
    first_hot = (routes[:, 0:1] == columns).astype(jnp.float32)
    second_hot = (routes[:, 1:2] == columns).astype(jnp.float32)
    first_logit = jnp.sum(logits * first_hot, axis=1)
    second_logit = jnp.sum(logits * second_hot, axis=1)
    gate_first = jax.nn.sigmoid(first_logit - second_logit)
    gate_second = jax.nn.sigmoid(second_logit - first_logit)
    keep_rows = kept_mask.astype(jnp.float32)
    chosen = ((first_hot + second_hot) * keep_rows[:, None]).astype(jnp.int32)
    position = jnp.cumsum(chosen, axis=0) - 1
    slot_iota = lax.broadcasted_iota(jnp.int32, (row_count, expert_count, capacity), 2)
    select_mask = (chosen[:, :, None] == 1) & (position[:, :, None] == slot_iota)
    select_bf = select_mask.astype(jnp.bfloat16)
    select_full = select_mask.astype(jnp.float32)
    token_send = jnp.einsum(
        "tec,td->ecd", select_bf, tokens, preferred_element_type=jnp.float32
    ).astype(jnp.bfloat16)
    grad_send = jnp.einsum(
        "tec,td->ecd", select_bf, out_grad, preferred_element_type=jnp.float32
    ).astype(jnp.bfloat16)
    gate_table = first_hot * gate_first[:, None] + second_hot * gate_second[:, None]
    gate_send = jnp.einsum(
        "tec,te->ec", select_full, gate_table, precision=lax.Precision.HIGHEST
    ).astype(jnp.bfloat16)
    token_recv, grad_recv, gate_recv = (
        lax.all_to_all(token_send, "expert", split_axis=0, concat_axis=0, tiled=True),
        lax.all_to_all(grad_send, "expert", split_axis=0, concat_axis=0, tiled=True),
        lax.all_to_all(gate_send, "expert", split_axis=0, concat_axis=0, tiled=True),
    )
    token_all, grad_all, gate_all = (
        lax.all_gather(token_recv, ("seq", "mp"), axis=0, tiled=True),
        lax.all_gather(grad_recv, ("seq", "mp"), axis=0, tiled=True),
        lax.all_gather(gate_recv, ("seq", "mp"), axis=0, tiled=True),
    )
    token_all = token_all.reshape(-1, width)
    grad_all = grad_all.reshape(-1, width)
    gate_all = gate_all.reshape(-1)
    gate_local = gate_weight[0]
    up_local = up_weight[0]
    down_local = down_weight[0]
    pre_gate = jnp.dot(token_all, gate_local, preferred_element_type=jnp.float32)
    pre_up = jnp.dot(token_all, up_local, preferred_element_type=jnp.float32)
    sigma = jax.nn.sigmoid(pre_gate)
    act = pre_gate * sigma
    hidden = act * pre_up
    grad_hidden = jnp.dot(grad_all, down_local.T, preferred_element_type=jnp.float32)
    gate_dot = jnp.sum(grad_hidden * hidden, axis=1)
    scaled = gate_all.astype(jnp.float32)[:, None] * grad_hidden
    grad_gate = (scaled * pre_up * sigma * (1.0 + pre_gate * (1.0 - sigma))).astype(jnp.bfloat16)
    grad_up = (scaled * act).astype(jnp.bfloat16)
    expert_grad = jnp.dot(grad_gate, gate_local.T, preferred_element_type=jnp.float32)
    expert_grad = expert_grad + jnp.dot(grad_up, up_local.T, preferred_element_type=jnp.float32)
    grad_own = lax.psum_scatter(
        expert_grad.astype(jnp.bfloat16), ("seq", "mp"), scatter_dimension=0, tiled=True
    ).astype(jnp.float32)
    dot_own = lax.psum_scatter(gate_dot, ("seq", "mp"), scatter_dimension=0, tiled=True)
    grad_back, dot_back = (
        lax.all_to_all(
            grad_own.reshape(expert_count, capacity, width).astype(jnp.bfloat16),
            "expert",
            split_axis=0,
            concat_axis=0,
            tiled=True,
        ).astype(jnp.float32),
        lax.all_to_all(
            dot_own.reshape(expert_count, capacity).astype(jnp.bfloat16),
            "expert",
            split_axis=0,
            concat_axis=0,
            tiled=True,
        ).astype(jnp.float32),
    )
    expert_sum = jnp.einsum("tec,ecd->td", select_full, grad_back, precision=lax.Precision.HIGHEST)
    dot_table = jnp.einsum("tec,ec->te", select_full, dot_back, precision=lax.Precision.HIGHEST)
    dot_first = jnp.sum(dot_table * first_hot, axis=1)
    dot_second = jnp.sum(dot_table * second_hot, axis=1)
    product = gate_first * gate_second * keep_rows
    grad_first = product * (dot_first - dot_second)
    grad_second = product * (dot_second - dot_first)
    logit_grad = first_hot * grad_first[:, None] + second_hot * grad_second[:, None]
    router_term = jnp.dot(logit_grad, router.astype(jnp.float32).T, precision=lax.Precision.HIGHEST)
    d_tokens = ((expert_sum + router_term) * keep_rows[:, None]).astype(jnp.bfloat16)
    gate_grad = jnp.stack([grad_first, grad_second], axis=1)
    return (d_tokens, gate_grad)


def solution(mesh):
    return jax.shard_map(
        on_device,
        mesh=mesh,
        in_specs=(
            P(("seq", "expert", "mp"), None),
            P(("seq", "expert", "mp"), None),
            P(("seq", "expert", "mp")),
            P(("seq", "expert", "mp"), None),
            P(),
            P("expert", None, ("seq", "mp")),
            P("expert", None, ("seq", "mp")),
            P("expert", ("seq", "mp"), None),
        ),
        out_specs=(P(("seq", "expert", "mp"), None), P(("seq", "expert", "mp"), None)),
        check_vma=False,
    )
```

profile of v0, /device:TPU:0, one launch (start us, length us, event | category | flops | bytes accessed | tf_op | source)
XLA Modules:
  0.0 279.3 jit_solution(13650934659943927859)
XLA Ops:
  7.2 0.0 copy-start
  7.2 0.0 all-gather.6.cloned.1.call-start
  7.2 0.7 convert_element_type.92
  7.9 0.8 slice_bitcast_fusion.1
  8.7 0.2 reduce_window_sum.11
  8.9 0.0 copy-done
  8.9 0.2 convolution_convert_fusion
  9.1 9.5 %all_to_all.36 = bf16[4,4,6144]{2,1,0:T(4,128)(2,1)} all-to-all(bf16[4,4,6144]{2,1,0:T(4,128)(2,1)S(1)} %convolution_convert_fusion), channel_id=1, replica_groups=mesh['seq'=2,'expert'=4,'mp'=4] {'expert'}, dimensions={0} | all-to-all | bytes 393216 | tf_op jit(solution)/shard_map/all_to_all | solution.py:38
  18.6 0.0 all-gather.6.cloned.1.call-update
  18.6 0.0 all-gather.4.cloned.1.call-start
  18.6 1.1 convolution_convert_fusion.1
  19.7 8.4 %all_to_all.37 = bf16[4,4,6144]{2,1,0:T(4,128)(2,1)} all-to-all(bf16[4,4,6144]{2,1,0:T(4,128)(2,1)S(1)} %convolution_convert_fusion.1), channel_id=1, replica_groups=mesh['seq'=2,'expert'=4,'mp'=4] {'expert'}, dimensions={0} | all-to-all | bytes 393216 | tf_op jit(solution)/shard_map/all_to_all | solution.py:39
  28.1 0.0 all-gather.4.cloned.1.call-update
  28.1 0.0 reduce-scatter.2.cloned.1.call-start
  28.2 1.2 dynamic-slice
  30.1 33.4 %all-gather.6.cloned.1.call-done = bf16[32,4,6144]{2,1,0:T(4,128)(2,1)} async-done(((bf16[4,4,6144]{2,1,0:T(4,128)(2,1)}), bf16[32,4,6144]{2,1,0:T(4,128)(2,1)}) %all-gather.6.cloned.1.call-update) | async-done | bytes 1572880 | tf_op jit(solution)/shard_map/all_gather | solution.py:43
  63.5 2.7 reshape.179
  66.2 6.4 %fusion.2 = f32[128,1024]{1,0:T(8,128)S(1)} fusion(bf16[128,6144]{1,0:T(8,128)(2,1)S(1)} %reshape.179, bf16[1,6144,1024]{2,1,0:T(8,128)(2,1)} %param.13), kind=kOutput, calls=%fused_computation.2 | convolution fusion | flops 1610612736 | bytes 14680064 | tf_op jit(solution)/shard_map/dot_general | solution.py:53
  72.6 6.4 %fusion.6 = f32[128,1024]{1,0:T(8,128)S(1)} fusion(bf16[128,6144]{1,0:T(8,128)(2,1)S(1)} %reshape.179, bf16[1,6144,1024]{2,1,0:T(8,128)(2,1)} %param.14), kind=kOutput, calls=%fused_computation.6 | convolution fusion | flops 1610612736 | bytes 14680064 | tf_op jit(solution)/shard_map/dot_general | solution.py:54
  79.0 29.7 %all-gather.4.cloned.1.call-done = bf16[32,4,6144]{2,1,0:T(4,128)(2,1)} async-done(((bf16[4,4,6144]{2,1,0:T(4,128)(2,1)}), bf16[32,4,6144]{2,1,0:T(4,128)(2,1)}) %all-gather.4.cloned.1.call-update) | async-done | bytes 1572880 | tf_op jit(solution)/shard_map/all_gather | solution.py:44
  108.6 2.7 reshape.178
  111.3 0.0 copy-start.1
  111.3 0.0 copy-start.2
  111.4 8.9 %multiply_reduce_fusion = (f32[128]{0:T(128)S(1)}, f32[128,1024]{1,0:T(8,128)S(1)}) fusion(f32[128,1024]{1,0:T(8,128)S(1)} %fusion.6, f32[128,1024]{1,0:T(8,128)S(1)} %fusion.2, bf16[128,6144]{1,0:T(8,128)(2,1)S(1)} %reshape.178, bf16[1,1024,6144]{2,1,0:T(8,128)(2,1)} %param.15), kind=kOutput, calls=%fused_computation.18 | convolution fusion | flops 1611530112 | bytes 15729152 | tf_op jit(solution)/shard_map/dot_general | solution.py:58
  120.3 19.3 %all-reduce = bf16[128]{0:T(256)(128)(2,1)S(1)} all-reduce(f32[128]{0:T(128)S(1)} %get-tuple-element.13), channel_id=4, replica_groups=mesh['seq'=2,'expert'=4,'mp'=4] {'seq','mp'}, use_global_device_ids=true, to_apply=%region_5.6.clone | all-reduce | flops 128 | bytes 768
  139.6 0.1 dynamic-slice.3
  139.7 0.1 convert_element_type.108
  139.8 6.3 %all_to_all.38 = bf16[4,1,4]{2,1,0:T(2,128)(2,1)S(1)} all-to-all(bf16[4,1,4]{2,1,0:T(2,128)(2,1)S(1)} %convert_element_type.108), channel_id=1, replica_groups=mesh['seq'=2,'expert'=4,'mp'=4] {'expert'}, dimensions={0} | all-to-all | bytes 64 | tf_op jit(solution)/shard_map/all_to_all | solution.py:77
  146.1 0.1 fusion.30
  146.2 0.0 copy-done.1
  146.2 0.2 select_reduce_fusion.3
  146.4 0.0 copy-done.2
  146.4 0.1 fusion.40
  146.6 6.1 %all_to_all.39 = bf16[4,1,4]{2,1,0:T(2,128)(2,1)S(1)} all-to-all(bf16[4,1,4]{2,1,0:T(2,128)(2,1)S(1)} %copy.21), channel_id=1, replica_groups=mesh['seq'=2,'expert'=4,'mp'=4] {'expert'}, dimensions={0} | all-to-all | bytes 64 | tf_op jit(solution)/shard_map/all_to_all | solution.py:40
  152.7 27.1 %all-gather = bf16[32,1,4]{2,1,0:T(2,128)(2,1)S(1)} all-gather(bf16[4,1,4]{2,1,0:T(2,128)(2,1)S(1)} %all_to_all.39), channel_id=2, replica_groups=mesh['seq'=2,'expert'=4,'mp'=4] {'seq','mp'}, dimensions={0}, use_global_device_ids=true | all-gather | bytes 288 | tf_op jit(solution)/shard_map/all_gather | solution.py:45
  179.7 0.1 convert_reduce_fusion
  179.8 0.1 reshape.180
  179.9 8.9 %fusion = f32[128,6144]{1,0:T(8,128)S(1)} fusion(bf16[1,6144,1024]{2,1,0:T(8,128)(2,1)} %param.13, f32[128,1024]{1,0:T(8,128)S(1)} %fusion.2, f32[128,1024]{1,0:T(8,128)S(1)} %fusion.6, f32[128,1024]{1,0:T(8,128)S(1)} %get-tuple-element.14, f32[128]{0:T(128)S(1)} %reshape.180), kind=kOutput, calls=%fused_computation | convolution fusion | flops 1612054528 | bytes 17302016 | tf_op jit(solution)/shard_map/dot_general | solution.py:63
  188.8 10.1 %fusion.13 = bf16[128,6144]{1,0:T(8,128)(2,1)} fusion(f32[128,6144]{1,0:T(8,128)S(1)} %fusion, bf16[1,6144,1024]{2,1,0:T(8,128)(2,1)} %param.14, f32[128,1024]{1,0:T(8,128)S(1)} %get-tuple-element.14, f32[128]{0:T(128)S(1)} %reshape.180, f32[128,1024]{1,0:T(8,128)S(1)} %fusion.2), kind=kOutput, calls=%fused_computation.11 | convolution fusion | flops 1613103104 | bytes 18350592 | tf_op jit(solution)/shard_map/dot_general | solution.py:64
  198.9 0.0 reduce-scatter.2.cloned.1.call-update
  199.0 62.2 %reduce-scatter.2.cloned.1.call-done = bf16[16,6144]{1,0:T(8,128)(2,1)} async-done(((bf16[128,6144]{1,0:T(8,128)(2,1)}), bf16[16,6144]{1,0:T(8,128)(2,1)}) %reduce-scatter.2.cloned.1.call-update) | async-done | bytes 196624 | tf_op jit(solution)/shard_map/reduce_scatter | solution.py:65
  261.2 1.7 convert_element_type.102
  262.8 3.4 %all-to-all-start.3 = ((bf16[4,4,6144]{2,1,0:T(4,128)(2,1)}), bf16[4,4,6144]{2,1,0:T(4,128)(2,1)S(1)}, u32[]{:S(2)}, u32[]{:S(2)}) async-start(bf16[4,4,6144]{2,1,0:T(4,128)(2,1)} %convert_element_type.102), calls=%async_computation.4 | async-start | bytes 393216 | tf_op jit(solution)/shard_map/all_to_all | solution.py:70
  266.2 0.6 pad_maximum_fusion
  266.8 4.7 %all-to-all-done.3 = bf16[4,4,6144]{2,1,0:T(4,128)(2,1)S(1)} async-done(((bf16[4,4,6144]{2,1,0:T(4,128)(2,1)}), bf16[4,4,6144]{2,1,0:T(4,128)(2,1)S(1)}, u32[]{:S(2)}, u32[]{:S(2)}) %all-to-all-start.3) | async-done | bytes 196640 | tf_op jit(solution)/shard_map/all_to_all | solution.py:70
  271.5 0.3 convolution_bitcast_fusion
  271.9 0.9 fusion.17
  (10 shorter events, 0.1 us)
Async XLA Ops:
  7.2 1.7 copy-start
  7.2 56.3 %all-gather.6.cloned.1.call-start = ((), (), s32[]{:S(2)}) async-start(), calls=%async_computation.7 | async-start | bytes 1769472 | tf_op jit(solution)/shard_map/all_gather | solution.py:43
  18.6 90.0 %all-gather.4.cloned.1.call-start = ((), (), s32[]{:S(2)}) async-start(), calls=%async_computation.6 | async-start | bytes 1769472 | tf_op jit(solution)/shard_map/all_gather | solution.py:44
  28.1 233.0 %reduce-scatter.2.cloned.1.call-start = ((), (), s32[]{:S(2)}) async-start(), calls=%async_computation.8 | async-start | bytes 1769472 | tf_op jit(solution)/shard_map/reduce_scatter | solution.py:65
  111.3 34.9 %copy-start.1 = (bf16[6144,4]{0,1:T(4,128)(2,1)S(1)}, bf16[6144,4]{0,1:T(4,128)(2,1)}, u32[]{:S(2)}) copy-start(bf16[6144,4]{0,1:T(4,128)(2,1)} %param.12) | copy-start | bytes 147460
  111.3 35.0 %copy-start.2 = (s32[8]{0:T(128)S(1)}, s32[8]{0:T(128)}, u32[]{:S(2)}) copy-start(s32[8]{0:T(128)} %param.10) | copy-start | bytes 100
  262.8 8.7 %all-to-all-start.3 = ((bf16[4,4,6144]{2,1,0:T(4,128)(2,1)}), bf16[4,4,6144]{2,1,0:T(4,128)(2,1)S(1)}, u32[]{:S(2)}, u32[]{:S(2)}) async-start(bf16[4,4,6144]{2,1,0:T(4,128)(2,1)} %convert_element_type.102), calls=%async_computation.4 | async-start | bytes 393216 | tf_op jit(solution)/shard_map/all_to_all | solution.py:70
Sparse Core Ops, SparseCore 0:
  18.7 44.7 all-gather.5
  65.6 42.9 all-gather.3
  199.1 62.0 reduce-scatter.1
where the time goes:
time: 280 us; the launch traced here: 279 us
  waiting for transfers between devices  130 us (46%)
  blocking collectives  76.7 us (27%)
  matrix products  43.7 us (16%)
  between operations  14.5 us (5%)
  local copies, waits for them, and re-layouts  9.35 us (3%)
  starting transfers between devices  3.49 us (1%)
    reduce_scatter x1, waiting for transfers between devices, on_device(): lax.psum_scatter(expert_grad.astype(jnp.bfloat16), ('seq', 'mp'), scatter...  62.2 us
    all_gather x1, waiting for transfers between devices, on_device(): lax.all_gather(token_recv, ('seq', 'mp'), axis=0, tiled=True)  33.4 us
    all_gather x1, waiting for transfers between devices, on_device(): lax.all_gather(grad_recv, ('seq', 'mp'), axis=0, tiled=True)  29.7 us
    all_gather x1, blocking collectives, on_device(): lax.all_gather(gate_recv, ('seq', 'mp'), axis=0, tiled=True)  27.1 us
    unnamed x1, blocking collectives  19.3 us
    dot_general x1, matrix products, on_device(): jnp.dot(grad_up, up_local.T, preferred_element_type=jnp.float32)  10.1 us
    all_to_all x1, blocking collectives, on_device(): lax.all_to_all(token_send, 'expert', split_axis=0, concat_axis=0, tiled=T...  9.48 us
    dot_general x1, matrix products, on_device(): jnp.dot(grad_gate, gate_local.T, preferred_element_type=jnp.float32)  8.93 us
  transfers between devices with their start and end apart: 4, of which 4 were waited for; matrix products, arithmetic and copies ran while one was open for 7% of the time, Pallas kernels for 0%

commit v1 on v0

--- a/solution.py
+++ b/solution.py
@@ -4,7 +4,7 @@
 from jax.sharding import PartitionSpec as P
 
 
-def on_device(tokens, out_grad, kept_mask, routes, router, gate_weight, up_weight, down_weight):
+def routed_plan(tokens, out_grad, kept_mask, routes, router, gate_weight, up_weight, down_weight):
     row_count = tokens.shape[0]
     width = tokens.shape[1]
     expert_count = lax.axis_size("expert")
@@ -95,10 +95,123 @@
     gate_grad = jnp.stack([grad_first, grad_second], axis=1)
     return (d_tokens, gate_grad)
 
+def shift(value, axis, step):
+    size = lax.axis_size(axis)
+    return lax.ppermute(value, axis, [((i + step) % size, i) for i in range(size)])
+
+
+def swap(value, axis, bit):
+    return lax.ppermute(value, axis, [(i ^ bit, i) for i in range(lax.axis_size(axis))])
+
+
+def swap_x(value):
+    return swap(value, "seq", 1)
+
+
+def swap_y(value):
+    return swap(value, "expert", 2)
+
+
+def swap_core(value):
+    return swap(value, "expert", 1)
+
+
+def gather(rows):
+    columns = rows.shape[1] // 256 * 128
+    z_rows = jnp.concatenate([rows] + [shift(rows, "mp", k) for k in range(1, lax.axis_size("mp"))], axis=0)
+    halves = []
+    for half, first, second in ((z_rows[:, :columns], swap_x, swap_y), (z_rows[:, columns:], swap_y, swap_x)):
+        near = first(half)
+        far = second(jnp.concatenate([half, near], axis=0))
+        far = jnp.split(far, 2, axis=0)
+        blocks = [half, near] + far if first is swap_x else [half, far[0], near, far[1]]
+        mine = jnp.concatenate(blocks, axis=0)
+        halves.append(jnp.concatenate([mine, swap_core(mine)], axis=0))
+    return halves
+
+
+def scatter_half(partial, first, second):
+    rows = partial.shape[0] // 2
+    total = partial[:rows].astype(jnp.float32) + swap_core(partial[rows:]).astype(jnp.float32)
+    own, by_x, by_y, by_both = jnp.split(total, 4, axis=0)
+    near, far = (by_x, [by_y, by_both]) if first is swap_x else (by_y, [by_x, by_both])
+    rest = second(jnp.concatenate(far, axis=0).astype(jnp.bfloat16)).astype(jnp.float32)
+    rest_own, rest_near = jnp.split(rest, 2, axis=0)
+    return own + rest_own + first((near + rest_near).astype(jnp.bfloat16)).astype(jnp.float32)
+
+
+def scatter_z(total):
+    size = lax.axis_size("mp")
+    rows = total.shape[0] // size
+    result = total[:rows]
+    for k in range(1, size):
+        result = result + shift(total[k * rows:(k + 1) * rows].astype(jnp.bfloat16), "mp", size - k).astype(jnp.float32)
+    return result
+
+
+def gathered_plan(tokens, out_grad, kept_mask, routes, router, gate_weight, up_weight, down_weight):
+    row_count, width = tokens.shape
+    expert_count = lax.axis_size("expert")
+    columns = lax.broadcasted_iota(jnp.int32, (row_count, expert_count), 1)
+    first_hot = (routes[:, 0:1] == columns).astype(jnp.float32)
+    second_hot = (routes[:, 1:2] == columns).astype(jnp.float32)
+    keep_rows = kept_mask.astype(jnp.float32)
+    token_halves = gather(tokens)
+    logits = jnp.dot(tokens, router, preferred_element_type=jnp.float32)
+    first_logit = jnp.sum(logits * first_hot, axis=1)
+    second_logit = jnp.sum(logits * second_hot, axis=1)
+    gate_first = jax.nn.sigmoid(first_logit - second_logit)
+    gate_second = jax.nn.sigmoid(second_logit - first_logit)
+    gate_table = (first_hot * gate_first[:, None] + second_hot * gate_second[:, None]) * keep_rows[:, None]
+    gate_table = jnp.pad(gate_table.astype(jnp.bfloat16), ((0, 0), (0, 256 - expert_count)))
+    grad_halves = gather(jnp.concatenate([gate_table, out_grad], axis=1))
+    half = width // 2
+    expert = lax.axis_index("expert")
+    first_grad = grad_halves[0][:, 256:]
+    gates = grad_halves[0][:, :expert_count].astype(jnp.float32)
+    gate_all = jnp.sum(jnp.where(lax.broadcasted_iota(jnp.int32, gates.shape, 1) == expert, gates, 0.0), axis=1)
+    second_grad = grad_halves[1]
+    gate_local, up_local, down_local = gate_weight[0], up_weight[0], down_weight[0]
+
+    def dot(a, b):
+        return jnp.dot(a, b, preferred_element_type=jnp.float32)
+
+    token_all = jnp.concatenate(token_halves, axis=1)
+    grad_all = jnp.concatenate([first_grad, second_grad], axis=1)
+    pre_gate = dot(token_all, gate_local)
+    pre_up = dot(token_all, up_local)
+    sigma = jax.nn.sigmoid(pre_gate)
+    act = pre_gate * sigma
+    hidden = act * pre_up
+    grad_hidden = dot(grad_all, down_local.T)
+    gate_dot = jnp.sum(grad_hidden * hidden, axis=1)
+    scaled = gate_all[:, None] * grad_hidden
+    grad_gate = (scaled * pre_up * sigma * (1.0 + pre_gate * (1.0 - sigma))).astype(jnp.bfloat16)
+    grad_up = (scaled * act).astype(jnp.bfloat16)
+    dots = jnp.where(lax.broadcasted_iota(jnp.int32, (gate_dot.shape[0], 128), 1) == expert, gate_dot[:, None], 0.0)
+    low = dot(grad_gate, gate_local[:half].T) + dot(grad_up, up_local[:half].T)
+    high = dot(grad_gate, gate_local[half:].T) + dot(grad_up, up_local[half:].T)
+    low = scatter_half(jnp.concatenate([low.astype(jnp.bfloat16), dots.astype(jnp.bfloat16)], axis=1), swap_x, swap_y)
+    high = scatter_half(high.astype(jnp.bfloat16), swap_y, swap_x)
+    total = scatter_z(jnp.concatenate([low, high], axis=1))
+    expert_sum = jnp.concatenate([total[:, :half], total[:, half + 128:]], axis=1)
+    dot_table = total[:, half:half + expert_count]
+    dot_first = jnp.sum(dot_table * first_hot, axis=1)
+    dot_second = jnp.sum(dot_table * second_hot, axis=1)
+    product = gate_first * gate_second * keep_rows
+    grad_first = product * (dot_first - dot_second)
+    grad_second = product * (dot_second - dot_first)
+    logit_grad = first_hot * grad_first[:, None] + second_hot * grad_second[:, None]
+    router_term = jnp.dot(logit_grad, router.astype(jnp.float32).T, precision=lax.Precision.HIGHEST)
+    d_tokens = ((expert_sum + router_term) * keep_rows[:, None]).astype(jnp.bfloat16)
+    gate_grad = jnp.stack([grad_first, grad_second], axis=1)
+    return (d_tokens, gate_grad)
+
 
 def solution(mesh):
+    gathers = mesh.shape["seq"] == 2 and mesh.shape["expert"] == 4
     return jax.shard_map(
-        on_device,
+        gathered_plan if gathers else routed_plan,
         mesh=mesh,
         in_specs=(
             P(("seq", "expert", "mp"), None),

time: 280 us -> 125 us (0.45)
  waiting for transfers between devices: 130 us -> 42.4 us
  blocking collectives: 76.7 us -> 0 us
  starting transfers between devices: 3.49 us -> 37.9 us
  between operations: 14.5 us -> 1.11 us
  local copies, waits for them, and re-layouts: 9.35 us -> 2.34 us
  matrix products: 43.7 us -> 37.1 us
    all_gather x2 -> x0, waiting for transfers between devices: 63.1 us -> none  [the longest x1 33.4 us: on_device(): lax.all_gather(token_recv, ('seq', 'mp'), axis=0, tiled=True)]
    reduce_scatter x1 -> x0, waiting for transfers between devices: 62.2 us -> none  [on_device(): lax.psum_scatter(expert_grad.astype(jnp.bfloat16), ('seq', 'mp'), scatter...]
    ppermute x0 -> x27, waiting for transfers between devices: none -> 42.4 us  [the longest x18 31.6 us: swap(): lax.ppermute(value, axis, [(i ^ bit, i) for i in range(lax.axis_size(axis...]
    ppermute x0 -> x27, starting transfers between devices: none -> 37.9 us  [the longest x9 21.3 us: shift(): lax.ppermute(value, axis, [((i + step) % size, i) for i in range(size)])]
    all_to_all x4 -> x0, blocking collectives: 30.3 us -> none  [the longest x1 9.48 us: on_device(): lax.all_to_all(token_send, 'expert', split_axis=0, concat_axis=0, tiled=T...]
    all_gather x1 -> x0, blocking collectives: 27.1 us -> none  [on_device(): lax.all_gather(gate_recv, ('seq', 'mp'), axis=0, tiled=True)]
    unnamed x1 -> x0, blocking collectives: 19.3 us -> none
    dot_general x12 -> x9, matrix products: 43.7 us -> 37.1 us  [the longest x7 34.9 us: dot(): return jnp.dot(a, b, preferred_element_type=jnp.float32)]
  transfers between devices with their start and end apart: 4 -> 27, of which waited for: 4 -> 16; matrix products, arithmetic and copies ran while one was open for 7% -> 7% of each run, Pallas kernels for 0% -> 0%
where the time goes in v1:
time: 125 us
  waiting for transfers between devices  42.4 us (34%)
  starting transfers between devices  37.9 us (30%)
  matrix products  37.1 us (30%)
  other arithmetic  4.02 us (3%)
  local copies, waits for them, and re-layouts  2.34 us (2%)
    dot_general x7, matrix products, dot(): return jnp.dot(a, b, preferred_element_type=jnp.float32)  34.9 us
    ppermute x18, waiting for transfers between devices, swap(): lax.ppermute(value, axis, [(i ^ bit, i) for i in range(lax.axis_size(axis...  31.6 us
    ppermute x9, starting transfers between devices, shift(): lax.ppermute(value, axis, [((i + step) % size, i) for i in range(size)])  21.3 us
    ppermute x18, starting transfers between devices, swap(): lax.ppermute(value, axis, [(i ^ bit, i) for i in range(lax.axis_size(axis...  16.7 us
    ppermute x9, waiting for transfers between devices, shift(): lax.ppermute(value, axis, [((i + step) % size, i) for i in range(size)])  10.8 us
  transfers between devices with their start and end apart: 27, of which 16 were waited for; matrix products, arithmetic and copies ran while one was open for 7% of the time, Pallas kernels for 0%

profile of v1, /device:TPU:0, one launch (start us, length us, event | category | flops | bytes accessed | tf_op | source)
XLA Modules:
  0.0 124.9 jit_solution(4469829529035068047)
XLA Ops:
  0.7 0.8 slice_bitcast_fusion
  1.4 0.7 convert_element_type.76
  2.1 1.2 select_reduce_fusion.4
  3.4 0.9 pad_maximum_fusion.18
  4.3 5.0 %collective-permute-start = (bf16[8,6400]{1,0:T(8,128)(2,1)S(1)}, bf16[8,6400]{1,0:T(8,128)(2,1)S(1)}, u32[]{:S(2)}, u32[]{:S(2)}) collective-permute-start(bf16[8,6400]{1,0:T(8,128)(2,1)S(1)} %pad_maximum_fusion.18), channel_id=1, source_target_pairs={{1,0},{2,1},{3,2},{0,3},{5,4},{6,5},{7,6},{4,7},{9,8},{10,9},{11,1... | collective-permute-start | bytes 307208 | tf_op jit(solution)/shard_map/ppermute | solution.py:100
  9.3 1.0 collective-permute-start.2
  10.4 2.8 %collective-permute-start.9 = (bf16[8,6144]{1,0:T(8,128)(2,1)}, bf16[8,6144]{1,0:T(8,128)(2,1)S(1)}, u32[]{:S(2)}, u32[]{:S(2)}) collective-permute-start(bf16[8,6144]{1,0:T(8,128)(2,1)} %param.8), channel_id=1, source_target_pairs={{1,0},{2,1},{3,2},{0,3},{5,4},{6,5},{7,6},{4,7},{9,8},{10,9},{11,1... | collective-permute-start | bytes 294920 | tf_op jit(solution)/shard_map/ppermute | solution.py:100
  13.2 1.1 collective-permute-start.10
  14.3 0.9 constant_dynamic-update-slice_fusion.8
  15.2 3.9 %collective-permute-done.9 = bf16[8,6144]{1,0:T(8,128)(2,1)S(1)} collective-permute-done((bf16[8,6144]{1,0:T(8,128)(2,1)}, bf16[8,6144]{1,0:T(8,128)(2,1)S(1)}, u32[]{:S(2)}, u32[]{:S(2)}) %collective-permute-start.9) | collective-permute-done | bytes 98336 | tf_op jit(solution)/shard_map/ppermute | solution.py:100
  19.2 5.7 %collective-permute-start.11 = (bf16[8,6144]{1,0:T(8,128)(2,1)}, bf16[8,6144]{1,0:T(8,128)(2,1)S(1)}, u32[]{:S(2)}, u32[]{:S(2)}) collective-permute-start(bf16[8,6144]{1,0:T(8,128)(2,1)} %param.8), channel_id=1, source_target_pairs={{3,0},{0,1},{1,2},{2,3},{7,4},{4,5},{5,6},{6,7},{11,8},{8,9},{9,10... | collective-permute-start | bytes 294920 | tf_op jit(solution)/shard_map/ppermute | solution.py:100
  24.9 2.0 %collective-permute-done.10 = bf16[8,6144]{1,0:T(8,128)(2,1)S(1)} collective-permute-done((bf16[8,6144]{1,0:T(8,128)(2,1)}, bf16[8,6144]{1,0:T(8,128)(2,1)S(1)}, u32[]{:S(2)}, u32[]{:S(2)}) %collective-permute-start.10) | collective-permute-done | bytes 98336 | tf_op jit(solution)/shard_map/ppermute | solution.py:100
  27.4 1.6 %collective-permute-start.15 = (bf16[32,3072]{1,0:T(8,128)(2,1)S(1)}, bf16[32,3072]{1,0:T(8,128)(2,1)S(1)}, u32[]{:S(2)}, u32[]{:S(2)}) collective-permute-start(bf16[32,3072]{1,0:T(8,128)(2,1)S(1)} %get-tuple-element.26), channel_id=1, source_target_pairs={{8,0},{12,4},{0,8},{4,12},{9,1},{13,5},{1,9},{5,13},{10,2},{14,6},... | collective-permute-start | bytes 589832 | tf_op jit(solution)/shard_map/ppermute | solution.py:104
  29.0 1.5 %collective-permute-start.12 = (bf16[32,3072]{1,0:T(8,128)(2,1)S(1)}, bf16[32,3072]{1,0:T(8,128)(2,1)S(1)}, u32[]{:S(2)}, u32[]{:S(2)}) collective-permute-start(bf16[32,3072]{1,0:T(8,128)(2,1)S(1)} %get-tuple-element.24), channel_id=1, source_target_pairs={{16,0},{0,16},{17,1},{1,17},{18,2},{2,18},{19,3},{3,19},{20,4},{4,... | collective-permute-start | bytes 589832 | tf_op jit(solution)/shard_map/ppermute | solution.py:104
  30.6 0.6 collective-permute-start.6
  31.7 3.5 %collective-permute-done.15 = bf16[32,3072]{1,0:T(8,128)(2,1)S(1)} collective-permute-done((bf16[32,3072]{1,0:T(8,128)(2,1)S(1)}, bf16[32,3072]{1,0:T(8,128)(2,1)S(1)}, u32[]{:S(2)}, u32[]{:S(2)}) %collective-permute-start.15) | collective-permute-done | bytes 196640 | tf_op jit(solution)/shard_map/ppermute | solution.py:104
  35.2 1.0 collective-permute-start.16
  36.2 0.7 collective-permute-done.12
  36.9 1.7 %collective-permute-start.13 = (bf16[64,3072]{1,0:T(8,128)(2,1)S(1)}, bf16[64,3072]{1,0:T(8,128)(2,1)S(1)}, u32[]{:S(2)}, u32[]{:S(2)}) collective-permute-start(bf16[64,3072]{1,0:T(8,128)(2,1)S(1)} %pad_maximum_fusion.15), channel_id=1, source_target_pairs={{8,0},{12,4},{0,8},{4,12},{9,1},{13,5},{1,9},{5,13},{10,2},{14,6},... | collective-permute-start | bytes 1179656 | tf_op jit(solution)/shard_map/ppermute | solution.py:104
  38.5 1.0 collective-permute-done.6
  39.6 1.0 collective-permute-start.7
  40.6 0.7 collective-permute-done.3
  41.3 1.7 %collective-permute-start.4 = (bf16[64,3200]{1,0:T(8,128)(2,1)S(1)}, bf16[64,3200]{1,0:T(8,128)(2,1)S(1)}, u32[]{:S(2)}, u32[]{:S(2)}) collective-permute-start(bf16[64,3200]{1,0:T(8,128)(2,1)S(1)} %pad_maximum_fusion.13), channel_id=1, source_target_pairs={{8,0},{12,4},{0,8},{4,12},{9,1},{13,5},{1,9},{5,13},{10,2},{14,6},... | collective-permute-start | bytes 1228808 | tf_op jit(solution)/shard_map/ppermute | solution.py:104
  42.9 6.7 %collective-permute-done.16 = bf16[64,3072]{1,0:T(8,128)(2,1)S(1)} collective-permute-done((bf16[64,3072]{1,0:T(8,128)(2,1)S(1)}, bf16[64,3072]{1,0:T(8,128)(2,1)S(1)}, u32[]{:S(2)}, u32[]{:S(2)}) %collective-permute-start.16) | collective-permute-done | bytes 393248 | tf_op jit(solution)/shard_map/ppermute | solution.py:104
  50.5 4.5 %collective-permute-done.7 = bf16[64,3200]{1,0:T(8,128)(2,1)S(1)} collective-permute-done((bf16[64,3200]{1,0:T(8,128)(2,1)S(1)}, bf16[64,3200]{1,0:T(8,128)(2,1)S(1)}, u32[]{:S(2)}, u32[]{:S(2)}) %collective-permute-start.7) | collective-permute-done | bytes 409632 | tf_op jit(solution)/shard_map/ppermute | solution.py:104
  56.0 4.5 %fusion.2 = f32[256,1024]{1,0:T(8,128)} fusion(bf16[1,6144,1024]{2,1,0:T(8,128)(2,1)S(1)} %copy-done.5, bf16[256,3072]{1,0:T(8,128)(2,1)S(1)} %constant_dynamic-update-slice_fusion.9, bf16[128,3072]{1,0:T(8,128)(2,1)S(1)} %collective-permute-done.14, bf16[64,3072]{1,0:T(8,128)(2,1)S(1)} %collective-permute-done.13, ...), kind=kOutput, calls=%fused_computation.2 | convolution fusion | flops 3236954112 | bytes 16777216 | tf_op jit(solution)/shard_map/dot_general | solution.py:177
  60.8 8.1 %fusion.4 = f32[256,1024]{1,0:T(8,128)S(1)} fusion(bf16[1,1024,6144]{2,1,0:T(8,128)(2,1)} %param.15, bf16[128,3200]{1,0:T(8,128)(2,1)S(1)} %collective-permute-done.5, bf16[64,3200]{1,0:T(8,128)(2,1)S(1)} %collective-permute-done.4, bf16[32,3200]{1,0:T(8,128)(2,1)S(1)} %collective-permute-done.3, bf16[32,3200]{1,0:T(8,128)(2,1)S(1)} %get-tuple-element.20, ...), kind=kOutput, calls=%fused_computation.4 | convolution fusion | flops 3236954112 | bytes 16908288 | tf_op jit(solution)/shard_map/dot_general | solution.py:177
  69.0 8.8 %multiply_convert_fusion.1 = (bf16[256,1024]{1,0:T(8,128)(2,1)S(1)}, bf16[256]{0:T(256)(128)(2,1)S(1)}, bf16[256,1024]{1,0:T(8,128)(2,1)S(1)}) fusion(f32[256,1024]{1,0:T(8,128)} %fusion.2, f32[256,1024]{1,0:T(8,128)S(1)} %fusion.4, f32[256]{0:T(256)S(1)} %select_reduce_fusion, bf16[1,6144,1024]{2,1,0:T(8,128)(2,1)} %param.13, ...), kind=kOutput, calls=%fused_computation.35 | convolution fusion | flops 3241410304 | bytes 18875904 | tf_op jit(solution)/shard_map/dot_general | solution.py:177
  77.8 5.0 %fusion.6 = f32[256,3072]{1,0:T(8,128)S(1)} fusion(bf16[256,1024]{1,0:T(8,128)(2,1)S(1)} %get-tuple-element.12, bf16[1,6144,1024]{2,1,0:T(8,128)(2,1)} %param.14), kind=kOutput, calls=%fused_computation.6 | convolution fusion | flops 1610612736 | bytes 9961472 | tf_op jit(solution)/shard_map/dot_general | solution.py:177
  82.8 4.8 %fusion.10 = f32[256,3072]{1,0:T(8,128)S(1)} fusion(bf16[256,1024]{1,0:T(8,128)(2,1)S(1)} %get-tuple-element.12, bf16[1,6144,1024]{2,1,0:T(8,128)(2,1)} %param.14), kind=kOutput, calls=%fused_computation.10 | convolution fusion | flops 1610612736 | bytes 9961472 | tf_op jit(solution)/shard_map/dot_general | solution.py:177
  87.6 1.9 %fusion.24 = bf16[256,3072]{1,0:T(8,128)(2,1)S(1)} fusion(f32[256,3072]{1,0:T(8,128)S(1)} %fusion.6, bf16[256,1024]{1,0:T(8,128)(2,1)S(1)} %get-tuple-element.8, bf16[1,6144,1024]{2,1,0:T(8,128)(2,1)S(1)} %bitcast.47), kind=kOutput, calls=%fused_computation.20 | convolution fusion | flops 1612185600 | bytes 11534336 | tf_op jit(solution)/shard_map/dot_general | solution.py:177
  89.7 1.8 %fusion.27 = bf16[256,3072]{1,0:T(8,128)(2,1)S(1)} fusion(f32[256,3072]{1,0:T(8,128)S(1)} %fusion.10, bf16[256,1024]{1,0:T(8,128)(2,1)S(1)} %get-tuple-element.8, bf16[1,6144,1024]{2,1,0:T(8,128)(2,1)S(1)} %bitcast.47), kind=kOutput, calls=%fused_computation.21 | convolution fusion | flops 1612185600 | bytes 11534336 | tf_op jit(solution)/shard_map/dot_general | solution.py:177
  91.7 0.6 collective-permute-start.18
  92.5 1.6 %collective-permute-start.22 = (bf16[64,3072]{1,0:T(8,128)(2,1)S(1)}, bf16[64,3072]{1,0:T(8,128)(2,1)S(1)}, u32[]{:S(2)}, u32[]{:S(2)}) collective-permute-start(bf16[64,3072]{1,0:T(8,128)(2,1)S(1)} %pad_maximum_fusion.17), channel_id=1, source_target_pairs={{16,0},{0,16},{17,1},{1,17},{18,2},{2,18},{19,3},{3,19},{20,4},{4,... | collective-permute-start | bytes 1179656 | tf_op jit(solution)/shard_map/ppermute | solution.py:104
  94.4 1.1 collective-permute-start.19
  95.6 8.1 %collective-permute-done.22 = bf16[64,3072]{1,0:T(8,128)(2,1)S(1)} collective-permute-done((bf16[64,3072]{1,0:T(8,128)(2,1)S(1)}, bf16[64,3072]{1,0:T(8,128)(2,1)S(1)}, u32[]{:S(2)}, u32[]{:S(2)}) %collective-permute-start.22) | collective-permute-done | bytes 393248 | tf_op jit(solution)/shard_map/ppermute | solution.py:104
  103.8 1.1 collective-permute-start.23
  104.9 1.9 %collective-permute-done.19 = bf16[64,3200]{1,0:T(8,128)(2,1)S(1)} collective-permute-done((bf16[64,3200]{1,0:T(8,128)(2,1)S(1)}, bf16[64,3200]{1,0:T(8,128)(2,1)S(1)}, u32[]{:S(2)}, u32[]{:S(2)}) %collective-permute-start.19) | collective-permute-done | bytes 409632 | tf_op jit(solution)/shard_map/ppermute | solution.py:104
  106.9 1.6 %collective-permute-start.20 = (bf16[32,3200]{1,0:T(8,128)(2,1)S(1)}, bf16[32,3200]{1,0:T(8,128)(2,1)S(1)}, u32[]{:S(2)}, u32[]{:S(2)}) collective-permute-start(bf16[32,3200]{1,0:T(8,128)(2,1)S(1)} %fusion.37), channel_id=1, source_target_pairs={{16,0},{0,16},{17,1},{1,17},{18,2},{2,18},{19,3},{3,19},{20,4},{4,... | collective-permute-start | bytes 614408 | tf_op jit(solution)/shard_map/ppermute | solution.py:104
  108.5 2.0 %collective-permute-done.23 = bf16[32,3072]{1,0:T(8,128)(2,1)S(1)} collective-permute-done((bf16[32,3072]{1,0:T(8,128)(2,1)S(1)}, bf16[32,3072]{1,0:T(8,128)(2,1)S(1)}, u32[]{:S(2)}, u32[]{:S(2)}) %collective-permute-start.23) | collective-permute-done | bytes 196640 | tf_op jit(solution)/shard_map/ppermute | solution.py:104
  110.5 2.4 %collective-permute-done.20 = bf16[32,3200]{1,0:T(8,128)(2,1)S(1)} collective-permute-done((bf16[32,3200]{1,0:T(8,128)(2,1)S(1)}, bf16[32,3200]{1,0:T(8,128)(2,1)S(1)}, u32[]{:S(2)}, u32[]{:S(2)}) %collective-permute-start.20) | collective-permute-done | bytes 204832 | tf_op jit(solution)/shard_map/ppermute | solution.py:104
  113.1 1.1 collective-permute-start.24
  114.3 1.6 %collective-permute-start.25 = (bf16[8,6272]{1,0:T(8,128)(2,1)S(1)}, bf16[8,6272]{1,0:T(8,128)(2,1)S(1)}, u32[]{:S(2)}, u32[]{:S(2)}) collective-permute-start(bf16[8,6272]{1,0:T(8,128)(2,1)S(1)} %get-tuple-element.23), channel_id=1, source_target_pairs={{2,0},{3,1},{0,2},{1,3},{6,4},{7,5},{4,6},{5,7},{10,8},{11,9},{8,1... | collective-permute-start | bytes 301064 | tf_op jit(solution)/shard_map/ppermute | solution.py:100
  115.9 2.8 %collective-permute-start.26 = (bf16[8,6272]{1,0:T(8,128)(2,1)S(1)}, bf16[8,6272]{1,0:T(8,128)(2,1)S(1)}, u32[]{:S(2)}, u32[]{:S(2)}) collective-permute-start(bf16[8,6272]{1,0:T(8,128)(2,1)S(1)} %get-tuple-element.22), channel_id=1, source_target_pairs={{1,0},{2,1},{3,2},{0,3},{5,4},{6,5},{7,6},{4,7},{9,8},{10,9},{11,1... | collective-permute-start | bytes 301064 | tf_op jit(solution)/shard_map/ppermute | solution.py:100
  118.7 1.7 %collective-permute-done.24 = bf16[8,6272]{1,0:T(8,128)(2,1)S(1)} collective-permute-done((bf16[8,6272]{1,0:T(8,128)(2,1)S(1)}, bf16[8,6272]{1,0:T(8,128)(2,1)S(1)}, u32[]{:S(2)}, u32[]{:S(2)}) %collective-permute-start.24) | collective-permute-done | bytes 100384 | tf_op jit(solution)/shard_map/ppermute | solution.py:100
  120.4 2.6 %collective-permute-done.25 = bf16[8,6272]{1,0:T(8,128)(2,1)S(1)} collective-permute-done((bf16[8,6272]{1,0:T(8,128)(2,1)S(1)}, bf16[8,6272]{1,0:T(8,128)(2,1)S(1)}, u32[]{:S(2)}, u32[]{:S(2)}) %collective-permute-start.25) | collective-permute-done | bytes 100384 | tf_op jit(solution)/shard_map/ppermute | solution.py:100
  123.4 0.6 pad_maximum_fusion.19
  123.9 0.9 fusion.46
  (87 shorter events, 5.1 us)
Async XLA Ops:
  0.6 1.4 %copy-start = (bf16[6144,4]{0,1:T(4,128)(2,1)S(1)}, bf16[6144,4]{0,1:T(4,128)(2,1)}, u32[]{:S(2)}) copy-start(bf16[6144,4]{0,1:T(4,128)(2,1)} %param.12) | copy-start | bytes 147460
  0.6 29.9 %copy-start.1 = (bf16[8,6144]{1,0:T(8,128)(2,1)S(1)}, bf16[8,6144]{1,0:T(8,128)(2,1)}, u32[]{:S(2)}) copy-start(bf16[8,6144]{1,0:T(8,128)(2,1)} %param.9) | copy-start | bytes 294916
  4.3 26.2 %collective-permute-start = (bf16[8,6400]{1,0:T(8,128)(2,1)S(1)}, bf16[8,6400]{1,0:T(8,128)(2,1)S(1)}, u32[]{:S(2)}, u32[]{:S(2)}) collective-permute-start(bf16[8,6400]{1,0:T(8,128)(2,1)S(1)} %pad_maximum_fusion.18), channel_id=1, source_target_pairs={{1,0},{2,1},{3,2},{0,3},{5,4},{6,5},{7,6},{4,7},{9,8},{10,9},{11,1... | collective-permute-start | bytes 307208 | tf_op jit(solution)/shard_map/ppermute | solution.py:100
  9.3 21.2 %collective-permute-start.1 = (bf16[8,6400]{1,0:T(8,128)(2,1)S(1)}, bf16[8,6400]{1,0:T(8,128)(2,1)S(1)}, u32[]{:S(2)}, u32[]{:S(2)}) collective-permute-start(bf16[8,6400]{1,0:T(8,128)(2,1)S(1)} %pad_maximum_fusion.18), channel_id=1, source_target_pairs={{2,0},{3,1},{0,2},{1,3},{6,4},{7,5},{4,6},{5,7},{10,8},{11,9},{8,1... | collective-permute-start | bytes 307208 | tf_op jit(solution)/shard_map/ppermute | solution.py:100
  9.3 21.2 %collective-permute-start.2 = (bf16[8,6400]{1,0:T(8,128)(2,1)S(1)}, bf16[8,6400]{1,0:T(8,128)(2,1)S(1)}, u32[]{:S(2)}, u32[]{:S(2)}) collective-permute-start(bf16[8,6400]{1,0:T(8,128)(2,1)S(1)} %pad_maximum_fusion.18), channel_id=1, source_target_pairs={{3,0},{0,1},{1,2},{2,3},{7,4},{4,5},{5,6},{6,7},{11,8},{8,9},{9,10... | collective-permute-start | bytes 307208 | tf_op jit(solution)/shard_map/ppermute | solution.py:100
  10.4 8.8 %collective-permute-start.9 = (bf16[8,6144]{1,0:T(8,128)(2,1)}, bf16[8,6144]{1,0:T(8,128)(2,1)S(1)}, u32[]{:S(2)}, u32[]{:S(2)}) collective-permute-start(bf16[8,6144]{1,0:T(8,128)(2,1)} %param.8), channel_id=1, source_target_pairs={{1,0},{2,1},{3,2},{0,3},{5,4},{6,5},{7,6},{4,7},{9,8},{10,9},{11,1... | collective-permute-start | bytes 294920 | tf_op jit(solution)/shard_map/ppermute | solution.py:100
  13.2 13.7 %collective-permute-start.10 = (bf16[8,6144]{1,0:T(8,128)(2,1)}, bf16[8,6144]{1,0:T(8,128)(2,1)S(1)}, u32[]{:S(2)}, u32[]{:S(2)}) collective-permute-start(bf16[8,6144]{1,0:T(8,128)(2,1)} %param.8), channel_id=1, source_target_pairs={{2,0},{3,1},{0,2},{1,3},{6,4},{7,5},{4,6},{5,7},{10,8},{11,9},{8,1... | collective-permute-start | bytes 294920 | tf_op jit(solution)/shard_map/ppermute | solution.py:100
  19.2 8.2 %collective-permute-start.11 = (bf16[8,6144]{1,0:T(8,128)(2,1)}, bf16[8,6144]{1,0:T(8,128)(2,1)S(1)}, u32[]{:S(2)}, u32[]{:S(2)}) collective-permute-start(bf16[8,6144]{1,0:T(8,128)(2,1)} %param.8), channel_id=1, source_target_pairs={{3,0},{0,1},{1,2},{2,3},{7,4},{4,5},{5,6},{6,7},{11,8},{8,9},{9,10... | collective-permute-start | bytes 294920 | tf_op jit(solution)/shard_map/ppermute | solution.py:100
  27.4 7.8 %collective-permute-start.15 = (bf16[32,3072]{1,0:T(8,128)(2,1)S(1)}, bf16[32,3072]{1,0:T(8,128)(2,1)S(1)}, u32[]{:S(2)}, u32[]{:S(2)}) collective-permute-start(bf16[32,3072]{1,0:T(8,128)(2,1)S(1)} %get-tuple-element.26), channel_id=1, source_target_pairs={{8,0},{12,4},{0,8},{4,12},{9,1},{13,5},{1,9},{5,13},{10,2},{14,6},... | collective-permute-start | bytes 589832 | tf_op jit(solution)/shard_map/ppermute | solution.py:104
  29.0 7.8 %collective-permute-start.12 = (bf16[32,3072]{1,0:T(8,128)(2,1)S(1)}, bf16[32,3072]{1,0:T(8,128)(2,1)S(1)}, u32[]{:S(2)}, u32[]{:S(2)}) collective-permute-start(bf16[32,3072]{1,0:T(8,128)(2,1)S(1)} %get-tuple-element.24), channel_id=1, source_target_pairs={{16,0},{0,16},{17,1},{1,17},{18,2},{2,18},{19,3},{3,19},{20,4},{4,... | collective-permute-start | bytes 589832 | tf_op jit(solution)/shard_map/ppermute | solution.py:104
  30.6 9.0 %collective-permute-start.6 = (bf16[32,3200]{1,0:T(8,128)(2,1)S(1)}, bf16[32,3200]{1,0:T(8,128)(2,1)S(1)}, u32[]{:S(2)}, u32[]{:S(2)}) collective-permute-start(bf16[32,3200]{1,0:T(8,128)(2,1)S(1)} %get-tuple-element.18), channel_id=1, source_target_pairs={{8,0},{12,4},{0,8},{4,12},{9,1},{13,5},{1,9},{5,13},{10,2},{14,6},... | collective-permute-start | bytes 614408 | tf_op jit(solution)/shard_map/ppermute | solution.py:104
  31.2 10.1 %collective-permute-start.3 = (bf16[32,3200]{1,0:T(8,128)(2,1)S(1)}, bf16[32,3200]{1,0:T(8,128)(2,1)S(1)}, u32[]{:S(2)}, u32[]{:S(2)}) collective-permute-start(bf16[32,3200]{1,0:T(8,128)(2,1)S(1)} %get-tuple-element.20), channel_id=1, source_target_pairs={{16,0},{0,16},{17,1},{1,17},{18,2},{2,18},{19,3},{3,19},{20,4},{4,... | collective-permute-start | bytes 614408 | tf_op jit(solution)/shard_map/ppermute | solution.py:104
  35.2 14.5 %collective-permute-start.16 = (bf16[64,3072]{1,0:T(8,128)(2,1)S(1)}, bf16[64,3072]{1,0:T(8,128)(2,1)S(1)}, u32[]{:S(2)}, u32[]{:S(2)}) collective-permute-start(bf16[64,3072]{1,0:T(8,128)(2,1)S(1)} %pad_maximum_fusion.16), channel_id=1, source_target_pairs={{16,0},{0,16},{17,1},{1,17},{18,2},{2,18},{19,3},{3,19},{20,4},{4,... | collective-permute-start | bytes 1179656 | tf_op jit(solution)/shard_map/ppermute | solution.py:104
  36.9 13.0 %collective-permute-start.13 = (bf16[64,3072]{1,0:T(8,128)(2,1)S(1)}, bf16[64,3072]{1,0:T(8,128)(2,1)S(1)}, u32[]{:S(2)}, u32[]{:S(2)}) collective-permute-start(bf16[64,3072]{1,0:T(8,128)(2,1)S(1)} %pad_maximum_fusion.15), channel_id=1, source_target_pairs={{8,0},{12,4},{0,8},{4,12},{9,1},{13,5},{1,9},{5,13},{10,2},{14,6},... | collective-permute-start | bytes 1179656 | tf_op jit(solution)/shard_map/ppermute | solution.py:104
  39.6 16.5 %copy-start.5 = (bf16[1,6144,1024]{2,1,0:T(8,128)(2,1)S(1)}, bf16[1,6144,1024]{2,1,0:T(8,128)(2,1)}, u32[]{:S(2)}) copy-start(bf16[1,6144,1024]{2,1,0:T(8,128)(2,1)} %param.14) | copy-start | bytes 37748740
  39.6 15.4 %collective-permute-start.7 = (bf16[64,3200]{1,0:T(8,128)(2,1)S(1)}, bf16[64,3200]{1,0:T(8,128)(2,1)S(1)}, u32[]{:S(2)}, u32[]{:S(2)}) collective-permute-start(bf16[64,3200]{1,0:T(8,128)(2,1)S(1)} %pad_maximum_fusion.14), channel_id=1, source_target_pairs={{16,0},{0,16},{17,1},{1,17},{18,2},{2,18},{19,3},{3,19},{20,4},{4,... | collective-permute-start | bytes 1228808 | tf_op jit(solution)/shard_map/ppermute | solution.py:104
  41.3 14.0 %collective-permute-start.4 = (bf16[64,3200]{1,0:T(8,128)(2,1)S(1)}, bf16[64,3200]{1,0:T(8,128)(2,1)S(1)}, u32[]{:S(2)}, u32[]{:S(2)}) collective-permute-start(bf16[64,3200]{1,0:T(8,128)(2,1)S(1)} %pad_maximum_fusion.13), channel_id=1, source_target_pairs={{8,0},{12,4},{0,8},{4,12},{9,1},{13,5},{1,9},{5,13},{10,2},{14,6},... | collective-permute-start | bytes 1228808 | tf_op jit(solution)/shard_map/ppermute | solution.py:104
  49.8 6.1 %collective-permute-start.17 = (bf16[128,3072]{1,0:T(8,128)(2,1)S(1)}, bf16[128,3072]{1,0:T(8,128)(2,1)S(1)}, u32[]{:S(2)}, u32[]{:S(2)}) collective-permute-start(bf16[128,3072]{1,0:T(8,128)(2,1)S(1)} %pad_maximum_fusion.11), channel_id=1, source_target_pairs={{4,0},{0,4},{12,8},{8,12},{5,1},{1,5},{13,9},{9,13},{6,2},{2,6},{1... | collective-permute-start | bytes 2359304 | tf_op jit(solution)/shard_map/ppermute | solution.py:104
  49.9 6.1 %collective-permute-start.14 = (bf16[128,3072]{1,0:T(8,128)(2,1)S(1)}, bf16[128,3072]{1,0:T(8,128)(2,1)S(1)}, u32[]{:S(2)}, u32[]{:S(2)}) collective-permute-start(bf16[128,3072]{1,0:T(8,128)(2,1)S(1)} %pad_maximum_fusion.10), channel_id=1, source_target_pairs={{4,0},{0,4},{12,8},{8,12},{5,1},{1,5},{13,9},{9,13},{6,2},{2,6},{1... | collective-permute-start | bytes 2359304 | tf_op jit(solution)/shard_map/ppermute | solution.py:104
  55.2 5.4 %collective-permute-start.8 = (bf16[128,3200]{1,0:T(8,128)(2,1)S(1)}, bf16[128,3200]{1,0:T(8,128)(2,1)S(1)}, u32[]{:S(2)}, u32[]{:S(2)}) collective-permute-start(bf16[128,3200]{1,0:T(8,128)(2,1)S(1)} %pad_maximum_fusion.9), channel_id=1, source_target_pairs={{4,0},{0,4},{12,8},{8,12},{5,1},{1,5},{13,9},{9,13},{6,2},{2,6},{1... | collective-permute-start | bytes 2457608 | tf_op jit(solution)/shard_map/ppermute | solution.py:104
  55.3 5.3 %collective-permute-start.5 = (bf16[128,3200]{1,0:T(8,128)(2,1)S(1)}, bf16[128,3200]{1,0:T(8,128)(2,1)S(1)}, u32[]{:S(2)}, u32[]{:S(2)}) collective-permute-start(bf16[128,3200]{1,0:T(8,128)(2,1)S(1)} %pad_maximum_fusion.8), channel_id=1, source_target_pairs={{4,0},{0,4},{12,8},{8,12},{5,1},{1,5},{13,9},{9,13},{6,2},{2,6},{1... | collective-permute-start | bytes 2457608 | tf_op jit(solution)/shard_map/ppermute | solution.py:104
  56.0 4.6 %copy-start.2 = (bf16[256,3072]{1,0:T(8,128)(2,1)}, bf16[256,3072]{1,0:T(8,128)(2,1)S(1)}, u32[]{:S(2)}) copy-start(bf16[256,3072]{1,0:T(8,128)(2,1)S(1)} %constant_dynamic-update-slice_fusion.9) | copy-start | bytes 4718596
  60.8 8.2 %copy-start.3 = (bf16[256,3072]{1,0:T(8,128)(2,1)S(1)}, bf16[256,3072]{1,0:T(8,128)(2,1)}, u32[]{:S(2)}) copy-start(bf16[256,3072]{1,0:T(8,128)(2,1)} %copy-done.2) | copy-start | bytes 4718596
  77.8 9.8 %slice-start = ((s8[12582912]{0:T(1024)(128)(4,1)}), s8[4194304]{0:T(1024)(128)(4,1)S(1)}, s32[]{:S(2)}) async-start(s8[12582912]{0:T(1024)(128)(4,1)} %bitcast.46), calls=%async_computation | async-start | bytes 8388608
  77.8 9.8 %slice-start.1 = ((s8[12582912]{0:T(1024)(128)(4,1)}), s8[4194304]{0:T(1024)(128)(4,1)S(1)}, s32[]{:S(2)}) async-start(s8[12582912]{0:T(1024)(128)(4,1)} %bitcast.46), calls=%async_computation.1 | async-start | bytes 8388608
  82.8 4.8 %slice-start.2 = ((s8[12582912]{0:T(1024)(128)(4,1)}), s8[4194304]{0:T(1024)(128)(4,1)S(1)}, s32[]{:S(2)}) async-start(s8[12582912]{0:T(1024)(128)(4,1)} %bitcast.46), calls=%async_computation.2 | async-start | bytes 8388608
  89.6 2.7 %collective-permute-start.21 = (bf16[128,3072]{1,0:T(8,128)(2,1)S(1)}, bf16[128,3072]{1,0:T(8,128)(2,1)S(1)}, u32[]{:S(2)}, u32[]{:S(2)}) collective-permute-start(bf16[128,3072]{1,0:T(8,128)(2,1)S(1)} %slice.124), channel_id=1, source_target_pairs={{4,0},{0,4},{12,8},{8,12},{5,1},{1,5},{13,9},{9,13},{6,2},{2,6},{1... | collective-permute-start | bytes 2359304 | tf_op jit(solution)/shard_map/ppermute | solution.py:104
  91.7 2.5 %collective-permute-start.18 = (bf16[128,3200]{1,0:T(8,128)(2,1)S(1)}, bf16[128,3200]{1,0:T(8,128)(2,1)S(1)}, u32[]{:S(2)}, u32[]{:S(2)}) collective-permute-start(bf16[128,3200]{1,0:T(8,128)(2,1)S(1)} %pad_maximum_fusion.7), channel_id=1, source_target_pairs={{4,0},{0,4},{12,8},{8,12},{5,1},{1,5},{13,9},{9,13},{6,2},{2,6},{1... | collective-permute-start | bytes 2457608 | tf_op jit(solution)/shard_map/ppermute | solution.py:104
  92.5 11.1 %collective-permute-start.22 = (bf16[64,3072]{1,0:T(8,128)(2,1)S(1)}, bf16[64,3072]{1,0:T(8,128)(2,1)S(1)}, u32[]{:S(2)}, u32[]{:S(2)}) collective-permute-start(bf16[64,3072]{1,0:T(8,128)(2,1)S(1)} %pad_maximum_fusion.17), channel_id=1, source_target_pairs={{16,0},{0,16},{17,1},{1,17},{18,2},{2,18},{19,3},{3,19},{20,4},{4,... | collective-permute-start | bytes 1179656 | tf_op jit(solution)/shard_map/ppermute | solution.py:104
  94.4 12.4 %collective-permute-start.19 = (bf16[64,3200]{1,0:T(8,128)(2,1)S(1)}, bf16[64,3200]{1,0:T(8,128)(2,1)S(1)}, u32[]{:S(2)}, u32[]{:S(2)}) collective-permute-start(bf16[64,3200]{1,0:T(8,128)(2,1)S(1)} %concatenate.99), channel_id=1, source_target_pairs={{8,0},{12,4},{0,8},{4,12},{9,1},{13,5},{1,9},{5,13},{10,2},{14,6},... | collective-permute-start | bytes 1228808 | tf_op jit(solution)/shard_map/ppermute | solution.py:104
  103.8 6.7 %collective-permute-start.23 = (bf16[32,3072]{1,0:T(8,128)(2,1)S(1)}, bf16[32,3072]{1,0:T(8,128)(2,1)S(1)}, u32[]{:S(2)}, u32[]{:S(2)}) collective-permute-start(bf16[32,3072]{1,0:T(8,128)(2,1)S(1)} %fusion.39), channel_id=1, source_target_pairs={{8,0},{12,4},{0,8},{4,12},{9,1},{13,5},{1,9},{5,13},{10,2},{14,6},... | collective-permute-start | bytes 589832 | tf_op jit(solution)/shard_map/ppermute | solution.py:104
  106.9 6.0 %collective-permute-start.20 = (bf16[32,3200]{1,0:T(8,128)(2,1)S(1)}, bf16[32,3200]{1,0:T(8,128)(2,1)S(1)}, u32[]{:S(2)}, u32[]{:S(2)}) collective-permute-start(bf16[32,3200]{1,0:T(8,128)(2,1)S(1)} %fusion.37), channel_id=1, source_target_pairs={{16,0},{0,16},{17,1},{1,17},{18,2},{2,18},{19,3},{3,19},{20,4},{4,... | collective-permute-start | bytes 614408 | tf_op jit(solution)/shard_map/ppermute | solution.py:104
  113.0 10.3 %copy-start.4 = (s32[8]{0:T(128)S(1)}, s32[8]{0:T(128)}, u32[]{:S(2)}) copy-start(s32[8]{0:T(128)} %param.10) | copy-start | bytes 100
  113.1 7.3 %collective-permute-start.24 = (bf16[8,6272]{1,0:T(8,128)(2,1)S(1)}, bf16[8,6272]{1,0:T(8,128)(2,1)S(1)}, u32[]{:S(2)}, u32[]{:S(2)}) collective-permute-start(bf16[8,6272]{1,0:T(8,128)(2,1)S(1)} %get-tuple-element.21), channel_id=1, source_target_pairs={{3,0},{0,1},{1,2},{2,3},{7,4},{4,5},{5,6},{6,7},{11,8},{8,9},{9,10... | collective-permute-start | bytes 301064 | tf_op jit(solution)/shard_map/ppermute | solution.py:100
  114.3 8.8 %collective-permute-start.25 = (bf16[8,6272]{1,0:T(8,128)(2,1)S(1)}, bf16[8,6272]{1,0:T(8,128)(2,1)S(1)}, u32[]{:S(2)}, u32[]{:S(2)}) collective-permute-start(bf16[8,6272]{1,0:T(8,128)(2,1)S(1)} %get-tuple-element.23), channel_id=1, source_target_pairs={{2,0},{3,1},{0,2},{1,3},{6,4},{7,5},{4,6},{5,7},{10,8},{11,9},{8,1... | collective-permute-start | bytes 301064 | tf_op jit(solution)/shard_map/ppermute | solution.py:100
  115.9 7.2 %collective-permute-start.26 = (bf16[8,6272]{1,0:T(8,128)(2,1)S(1)}, bf16[8,6272]{1,0:T(8,128)(2,1)S(1)}, u32[]{:S(2)}, u32[]{:S(2)}) collective-permute-start(bf16[8,6272]{1,0:T(8,128)(2,1)S(1)} %get-tuple-element.22), channel_id=1, source_target_pairs={{1,0},{2,1},{3,2},{0,3},{5,4},{6,5},{7,6},{4,7},{9,8},{10,9},{11,1... | collective-permute-start | bytes 301064 | tf_op jit(solution)/shard_map/ppermute | solution.py:100

commit v2 on v1

--- a/solution.py
+++ b/solution.py
@@ -116,9 +116,13 @@
     return swap(value, "expert", 1)
 
 
-def gather(rows):
-    columns = rows.shape[1] // 256 * 128
-    z_rows = jnp.concatenate([rows] + [shift(rows, "mp", k) for k in range(1, lax.axis_size("mp"))], axis=0)
+def gather_z(rows):
+    return [rows] + [shift(rows, "mp", k) for k in range(1, lax.axis_size("mp"))]
+
+
+def gather_rest(z_rows):
+    z_rows = jnp.concatenate(z_rows, axis=0)
+    columns = z_rows.shape[1] // 256 * 128
     halves = []
     for half, first, second in ((z_rows[:, :columns], swap_x, swap_y), (z_rows[:, columns:], swap_y, swap_x)):
         near = first(half)
@@ -156,7 +160,7 @@
     first_hot = (routes[:, 0:1] == columns).astype(jnp.float32)
     second_hot = (routes[:, 1:2] == columns).astype(jnp.float32)
     keep_rows = kept_mask.astype(jnp.float32)
-    token_halves = gather(tokens)
+    token_z = gather_z(tokens)
     logits = jnp.dot(tokens, router, preferred_element_type=jnp.float32)
     first_logit = jnp.sum(logits * first_hot, axis=1)
     second_logit = jnp.sum(logits * second_hot, axis=1)
@@ -164,7 +168,10 @@
     gate_second = jax.nn.sigmoid(second_logit - first_logit)
     gate_table = (first_hot * gate_first[:, None] + second_hot * gate_second[:, None]) * keep_rows[:, None]
     gate_table = jnp.pad(gate_table.astype(jnp.bfloat16), ((0, 0), (0, 256 - expert_count)))
-    grad_halves = gather(jnp.concatenate([gate_table, out_grad], axis=1))
+    grad_rows, token_z[1] = lax.optimization_barrier((jnp.concatenate([gate_table, out_grad], axis=1), token_z[1]))
+    grad_z = gather_z(grad_rows)
+    token_halves = gather_rest(token_z)
+    grad_halves = gather_rest(grad_z)
     half = width // 2
     expert = lax.axis_index("expert")
     first_grad = grad_halves[0][:, 256:]
@@ -190,12 +197,13 @@
     grad_up = (scaled * act).astype(jnp.bfloat16)
     dots = jnp.where(lax.broadcasted_iota(jnp.int32, (gate_dot.shape[0], 128), 1) == expert, gate_dot[:, None], 0.0)
     low = dot(grad_gate, gate_local[:half].T) + dot(grad_up, up_local[:half].T)
+    low = jnp.concatenate([low.astype(jnp.bfloat16), dots.astype(jnp.bfloat16)], axis=1)
+    low, grad_gate, grad_up = lax.optimization_barrier((low, grad_gate, grad_up))
     high = dot(grad_gate, gate_local[half:].T) + dot(grad_up, up_local[half:].T)
-    low = scatter_half(jnp.concatenate([low.astype(jnp.bfloat16), dots.astype(jnp.bfloat16)], axis=1), swap_x, swap_y)
-    high = scatter_half(high.astype(jnp.bfloat16), swap_y, swap_x)
-    total = scatter_z(jnp.concatenate([low, high], axis=1))
-    expert_sum = jnp.concatenate([total[:, :half], total[:, half + 128:]], axis=1)
-    dot_table = total[:, half:half + expert_count]
+    low = scatter_z(scatter_half(low, swap_x, swap_y))
+    high = scatter_z(scatter_half(high.astype(jnp.bfloat16), swap_y, swap_x))
+    expert_sum = jnp.concatenate([low[:, :half], high], axis=1)
+    dot_table = low[:, half:half + expert_count]
     dot_first = jnp.sum(dot_table * first_hot, axis=1)
     dot_second = jnp.sum(dot_table * second_hot, axis=1)
     product = gate_first * gate_second * keep_rows

time: 125 us -> 122 us (0.976)
  waiting for transfers between devices: 42.4 us -> 37.6 us
  matrix products: 37.1 us -> 40 us
    dot_general x7, matrix products: 34.9 us -> 37.9 us  [dot(): return jnp.dot(a, b, preferred_element_type=jnp.float32)]
    ppermute x9 -> x12, waiting for transfers between devices: 10.8 us -> 7.84 us  [shift(): lax.ppermute(value, axis, [((i + step) % size, i) for i in range(size)])]
    ppermute x18, waiting for transfers between devices: 31.6 us -> 29.8 us  [swap(): lax.ppermute(value, axis, [(i ^ bit, i) for i in range(lax.axis_size(axis...]
    ppermute x9 -> x12, starting transfers between devices: 21.3 us -> 19.9 us  [shift(): lax.ppermute(value, axis, [((i + step) % size, i) for i in range(size)])]
  transfers between devices with their start and end apart: 27 -> 30, of which waited for: 16 -> 11; matrix products, arithmetic and copies ran while one was open for 7% -> 9% of each run, Pallas kernels for 0% -> 0%
where the time goes in v2:
time: 122 us
  matrix products  40 us (33%)
  waiting for transfers between devices  37.6 us (31%)
  starting transfers between devices  36.9 us (30%)
  other arithmetic  3.93 us (3%)
  local copies, waits for them, and re-layouts  2.42 us (2%)
    dot_general x7, matrix products, dot(): return jnp.dot(a, b, preferred_element_type=jnp.float32)  37.9 us
    ppermute x18, waiting for transfers between devices, swap(): lax.ppermute(value, axis, [(i ^ bit, i) for i in range(lax.axis_size(axis...  29.8 us
    ppermute x12, starting transfers between devices, shift(): lax.ppermute(value, axis, [((i + step) % size, i) for i in range(size)])  19.9 us
    ppermute x18, starting transfers between devices, swap(): lax.ppermute(value, axis, [(i ^ bit, i) for i in range(lax.axis_size(axis...  17 us
    ppermute x12, waiting for transfers between devices, shift(): lax.ppermute(value, axis, [((i + step) % size, i) for i in range(size)])  7.84 us
  transfers between devices with their start and end apart: 30, of which 11 were waited for; matrix products, arithmetic and copies ran while one was open for 9% of the time, Pallas kernels for 0%

profile of v2, /device:TPU:0, one launch (start us, length us, event | category | flops | bytes accessed | tf_op | source)
XLA Modules:
  0.0 122.1 jit_solution(15881634830655132596)
XLA Ops:
  0.6 5.1 %collective-permute-start = (bf16[8,6144]{1,0:T(8,128)(2,1)}, bf16[8,6144]{1,0:T(8,128)(2,1)S(1)}, u32[]{:S(2)}, u32[]{:S(2)}) collective-permute-start(bf16[8,6144]{1,0:T(8,128)(2,1)} %param.8), channel_id=1, source_target_pairs={{1,0},{2,1},{3,2},{0,3},{5,4},{6,5},{7,6},{4,7},{9,8},{10,9},{11,1... | collective-permute-start | bytes 294920 | tf_op jit(solution)/shard_map/ppermute | solution.py:100
  5.7 1.0 collective-permute-start.11
  6.8 0.9 constant_dynamic-update-slice_fusion.12
  7.7 0.8 slice_bitcast_fusion
  8.5 0.7 convert_element_type.88
  9.1 1.2 select_reduce_fusion.4
  10.4 0.9 fusion.42
  11.4 2.9 %collective-permute-start.1 = (bf16[8,6400]{1,0:T(8,128)(2,1)S(1)}, bf16[8,6400]{1,0:T(8,128)(2,1)S(1)}, u32[]{:S(2)}, u32[]{:S(2)}) collective-permute-start(bf16[8,6400]{1,0:T(8,128)(2,1)S(1)} %fusion.42), channel_id=1, source_target_pairs={{1,0},{2,1},{3,2},{0,3},{5,4},{6,5},{7,6},{4,7},{9,8},{10,9},{11,1... | collective-permute-start | bytes 307208 | tf_op jit(solution)/shard_map/ppermute | solution.py:100
  14.2 1.1 collective-permute-start.2
  15.5 1.6 %collective-permute-start.12 = (bf16[32,3072]{1,0:T(8,128)(2,1)S(1)}, bf16[32,3072]{1,0:T(8,128)(2,1)S(1)}, u32[]{:S(2)}, u32[]{:S(2)}) collective-permute-start(bf16[32,3072]{1,0:T(8,128)(2,1)S(1)} %get-tuple-element.35), channel_id=1, source_target_pairs={{16,0},{0,16},{17,1},{1,17},{18,2},{2,18},{19,3},{3,19},{20,4},{4,... | collective-permute-start | bytes 589832 | tf_op jit(solution)/shard_map/ppermute | solution.py:104
  17.1 1.5 %collective-permute-start.15 = (bf16[32,3072]{1,0:T(8,128)(2,1)S(1)}, bf16[32,3072]{1,0:T(8,128)(2,1)S(1)}, u32[]{:S(2)}, u32[]{:S(2)}) collective-permute-start(bf16[32,3072]{1,0:T(8,128)(2,1)S(1)} %get-tuple-element.37), channel_id=1, source_target_pairs={{8,0},{12,4},{0,8},{4,12},{9,1},{13,5},{1,9},{5,13},{10,2},{14,6},... | collective-permute-start | bytes 589832 | tf_op jit(solution)/shard_map/ppermute | solution.py:104
  18.6 5.2 %collective-permute-done.2 = bf16[8,6400]{1,0:T(8,128)(2,1)S(1)} collective-permute-done((bf16[8,6400]{1,0:T(8,128)(2,1)S(1)}, bf16[8,6400]{1,0:T(8,128)(2,1)S(1)}, u32[]{:S(2)}, u32[]{:S(2)}) %collective-permute-start.2) | collective-permute-done | bytes 102432 | tf_op jit(solution)/shard_map/ppermute | solution.py:100
  23.9 1.6 %collective-permute-start.4 = (bf16[32,3200]{1,0:T(8,128)(2,1)S(1)}, bf16[32,3200]{1,0:T(8,128)(2,1)S(1)}, u32[]{:S(2)}, u32[]{:S(2)}) collective-permute-start(bf16[32,3200]{1,0:T(8,128)(2,1)S(1)} %get-tuple-element.34), channel_id=1, source_target_pairs={{16,0},{0,16},{17,1},{1,17},{18,2},{2,18},{19,3},{3,19},{20,4},{4,... | collective-permute-start | bytes 614408 | tf_op jit(solution)/shard_map/ppermute | solution.py:104
  25.4 1.5 %collective-permute-start.7 = (bf16[32,3200]{1,0:T(8,128)(2,1)S(1)}, bf16[32,3200]{1,0:T(8,128)(2,1)S(1)}, u32[]{:S(2)}, u32[]{:S(2)}) collective-permute-start(bf16[32,3200]{1,0:T(8,128)(2,1)S(1)} %get-tuple-element.32), channel_id=1, source_target_pairs={{8,0},{12,4},{0,8},{4,12},{9,1},{13,5},{1,9},{5,13},{10,2},{14,6},... | collective-permute-start | bytes 614408 | tf_op jit(solution)/shard_map/ppermute | solution.py:104
  27.0 0.6 collective-permute-start.13
  27.6 0.6 collective-permute-start.16
  28.2 3.2 %collective-permute-done.4 = bf16[32,3200]{1,0:T(8,128)(2,1)S(1)} collective-permute-done((bf16[32,3200]{1,0:T(8,128)(2,1)S(1)}, bf16[32,3200]{1,0:T(8,128)(2,1)S(1)}, u32[]{:S(2)}, u32[]{:S(2)}) %collective-permute-start.4) | collective-permute-done | bytes 204832 | tf_op jit(solution)/shard_map/ppermute | solution.py:104
  31.5 1.6 %collective-permute-start.5 = (bf16[64,3200]{1,0:T(8,128)(2,1)S(1)}, bf16[64,3200]{1,0:T(8,128)(2,1)S(1)}, u32[]{:S(2)}, u32[]{:S(2)}) collective-permute-start(bf16[64,3200]{1,0:T(8,128)(2,1)S(1)} %pad_maximum_fusion.11), channel_id=1, source_target_pairs={{8,0},{12,4},{0,8},{4,12},{9,1},{13,5},{1,9},{5,13},{10,2},{14,6},... | collective-permute-start | bytes 1228808 | tf_op jit(solution)/shard_map/ppermute | solution.py:104
  33.1 0.4 collective-permute-done.7
  33.5 1.7 %collective-permute-start.8 = (bf16[64,3200]{1,0:T(8,128)(2,1)S(1)}, bf16[64,3200]{1,0:T(8,128)(2,1)S(1)}, u32[]{:S(2)}, u32[]{:S(2)}) collective-permute-start(bf16[64,3200]{1,0:T(8,128)(2,1)S(1)} %pad_maximum_fusion.12), channel_id=1, source_target_pairs={{16,0},{0,16},{17,1},{1,17},{18,2},{2,18},{19,3},{3,19},{20,4},{4,... | collective-permute-start | bytes 1228808 | tf_op jit(solution)/shard_map/ppermute | solution.py:104
  35.2 6.7 %collective-permute-done.13 = bf16[64,3072]{1,0:T(8,128)(2,1)S(1)} collective-permute-done((bf16[64,3072]{1,0:T(8,128)(2,1)S(1)}, bf16[64,3072]{1,0:T(8,128)(2,1)S(1)}, u32[]{:S(2)}, u32[]{:S(2)}) %collective-permute-start.13) | collective-permute-done | bytes 393248 | tf_op jit(solution)/shard_map/ppermute | solution.py:104
  42.1 0.6 collective-permute-start.17
  42.7 5.2 %collective-permute-done.5 = bf16[64,3200]{1,0:T(8,128)(2,1)S(1)} collective-permute-done((bf16[64,3200]{1,0:T(8,128)(2,1)S(1)}, bf16[64,3200]{1,0:T(8,128)(2,1)S(1)}, u32[]{:S(2)}, u32[]{:S(2)}) %collective-permute-start.5) | collective-permute-done | bytes 409632 | tf_op jit(solution)/shard_map/ppermute | solution.py:104
  48.3 0.5 collective-permute-start.9
  49.0 4.5 %fusion.2 = f32[256,1024]{1,0:T(8,128)} fusion(bf16[1,6144,1024]{2,1,0:T(8,128)(2,1)S(1)} %copy-done.4, bf16[256,3072]{1,0:T(8,128)(2,1)S(1)} %constant_dynamic-update-slice_fusion.13, bf16[128,3072]{1,0:T(8,128)(2,1)S(1)} %collective-permute-done.14, bf16[64,3072]{1,0:T(8,128)(2,1)S(1)} %collective-permute-done.13, ...), kind=kOutput, calls=%fused_computation.2 | convolution fusion | flops 3236954112 | bytes 16777216 | tf_op jit(solution)/shard_map/dot_general | solution.py:184
  53.7 8.1 %fusion.4 = f32[256,1024]{1,0:T(8,128)S(1)} fusion(bf16[1,1024,6144]{2,1,0:T(8,128)(2,1)} %param.15, bf16[128,3200]{1,0:T(8,128)(2,1)S(1)} %collective-permute-done.6, bf16[64,3200]{1,0:T(8,128)(2,1)S(1)} %collective-permute-done.5, bf16[32,3200]{1,0:T(8,128)(2,1)S(1)} %collective-permute-done.4, bf16[32,3200]{1,0:T(8,128)(2,1)S(1)} %get-tuple-element.34, ...), kind=kOutput, calls=%fused_computation.4 | convolution fusion | flops 3236954112 | bytes 16908288 | tf_op jit(solution)/shard_map/dot_general | solution.py:184
  61.9 8.9 %multiply_convert_fusion.1 = (bf16[256,1024]{1,0:T(8,128)(2,1)S(1)}, bf16[256]{0:T(256)(128)(2,1)S(1)}, bf16[256,1024]{1,0:T(8,128)(2,1)S(1)}) fusion(f32[256,1024]{1,0:T(8,128)} %fusion.2, f32[256,1024]{1,0:T(8,128)S(1)} %fusion.4, f32[256]{0:T(256)S(1)} %select_reduce_fusion, bf16[1,6144,1024]{2,1,0:T(8,128)(2,1)} %param.13, ...), kind=kOutput, calls=%fused_computation.34 | convolution fusion | flops 3241410304 | bytes 18875904 | tf_op jit(solution)/shard_map/dot_general | solution.py:184
  70.8 5.0 %fusion.10 = f32[256,3072]{1,0:T(8,128)S(1)} fusion(bf16[256,1024]{1,0:T(8,128)(2,1)S(1)} %get-tuple-element.11, bf16[1,6144,1024]{2,1,0:T(8,128)(2,1)} %param.14), kind=kOutput, calls=%fused_computation.10 | convolution fusion | flops 1610612736 | bytes 9961472 | tf_op jit(solution)/shard_map/dot_general | solution.py:184
  75.8 4.8 %fusion.27 = bf16[256,3072]{1,0:T(8,128)(2,1)S(1)} fusion(f32[256,3072]{1,0:T(8,128)S(1)} %fusion.10, bf16[256,1024]{1,0:T(8,128)(2,1)S(1)} %get-tuple-element.10, bf16[1,6144,1024]{2,1,0:T(8,128)(2,1)} %param.13), kind=kOutput, calls=%fused_computation.21 | convolution fusion | flops 1612185600 | bytes 11534336 | tf_op jit(solution)/shard_map/dot_general | solution.py:184
  80.9 1.8 %fusion.6 = f32[256,3072]{1,0:T(8,128)S(1)} fusion(bf16[256,1024]{1,0:T(8,128)(2,1)S(1)} %get-tuple-element.11, bf16[1,6144,1024]{2,1,0:T(8,128)(2,1)S(1)} %bitcast.47), kind=kOutput, calls=%fused_computation.6 | convolution fusion | flops 1610612736 | bytes 9961472 | tf_op jit(solution)/shard_map/dot_general | solution.py:184
  82.7 4.7 %fusion.24 = bf16[256,3072]{1,0:T(8,128)(2,1)S(1)} fusion(f32[256,3072]{1,0:T(8,128)S(1)} %fusion.6, bf16[256,1024]{1,0:T(8,128)(2,1)S(1)} %get-tuple-element.10, bf16[1,6144,1024]{2,1,0:T(8,128)(2,1)} %param.13), kind=kOutput, calls=%fused_computation.20 | convolution fusion | flops 1612185600 | bytes 11534336 | tf_op jit(solution)/shard_map/dot_general | solution.py:184
  87.7 0.6 collective-permute-start.18
  88.2 1.6 %collective-permute-done.24 = bf16[128,3072]{1,0:T(8,128)(2,1)S(1)} collective-permute-done((bf16[128,3072]{1,0:T(8,128)(2,1)S(1)}, bf16[128,3072]{1,0:T(8,128)(2,1)S(1)}, u32[]{:S(2)}, u32[]{:S(2)}) %collective-permute-start.24) | collective-permute-done | bytes 786464 | tf_op jit(solution)/shard_map/ppermute | solution.py:104
  90.2 0.6 collective-permute-start.25
  91.3 1.6 %collective-permute-start.19 = (bf16[64,3200]{1,0:T(8,128)(2,1)S(1)}, bf16[64,3200]{1,0:T(8,128)(2,1)S(1)}, u32[]{:S(2)}, u32[]{:S(2)}) collective-permute-start(bf16[64,3200]{1,0:T(8,128)(2,1)S(1)} %concatenate.95), channel_id=1, source_target_pairs={{8,0},{12,4},{0,8},{4,12},{9,1},{13,5},{1,9},{5,13},{10,2},{14,6},... | collective-permute-start | bytes 1228808 | tf_op jit(solution)/shard_map/ppermute | solution.py:104
  92.9 8.5 %collective-permute-done.25 = bf16[64,3072]{1,0:T(8,128)(2,1)S(1)} collective-permute-done((bf16[64,3072]{1,0:T(8,128)(2,1)S(1)}, bf16[64,3072]{1,0:T(8,128)(2,1)S(1)}, u32[]{:S(2)}, u32[]{:S(2)}) %collective-permute-start.25) | collective-permute-done | bytes 393248 | tf_op jit(solution)/shard_map/ppermute | solution.py:104
  101.5 1.6 %collective-permute-start.26 = (bf16[32,3072]{1,0:T(8,128)(2,1)S(1)}, bf16[32,3072]{1,0:T(8,128)(2,1)S(1)}, u32[]{:S(2)}, u32[]{:S(2)}) collective-permute-start(bf16[32,3072]{1,0:T(8,128)(2,1)S(1)} %fusion.37), channel_id=1, source_target_pairs={{8,0},{12,4},{0,8},{4,12},{9,1},{13,5},{1,9},{5,13},{10,2},{14,6},... | collective-permute-start | bytes 589832 | tf_op jit(solution)/shard_map/ppermute | solution.py:104
  103.2 0.8 collective-permute-start.20
  104.0 3.7 %collective-permute-done.26 = bf16[32,3072]{1,0:T(8,128)(2,1)S(1)} collective-permute-done((bf16[32,3072]{1,0:T(8,128)(2,1)S(1)}, bf16[32,3072]{1,0:T(8,128)(2,1)S(1)}, u32[]{:S(2)}, u32[]{:S(2)}) %collective-permute-start.26) | collective-permute-done | bytes 196640 | tf_op jit(solution)/shard_map/ppermute | solution.py:104
  107.7 1.0 collective-permute-start.27
  108.8 2.0 %collective-permute-start.28 = (bf16[8,3072]{1,0:T(8,128)(2,1)S(1)}, bf16[8,3072]{1,0:T(8,128)(2,1)S(1)}, u32[]{:S(2)}, u32[]{:S(2)}) collective-permute-start(bf16[8,3072]{1,0:T(8,128)(2,1)S(1)} %get-tuple-element.46), channel_id=1, source_target_pairs={{2,0},{3,1},{0,2},{1,3},{6,4},{7,5},{4,6},{5,7},{10,8},{11,9},{8,1... | collective-permute-start | bytes 147464 | tf_op jit(solution)/shard_map/ppermute | solution.py:100
  110.8 2.8 %collective-permute-start.29 = (bf16[8,3072]{1,0:T(8,128)(2,1)S(1)}, bf16[8,3072]{1,0:T(8,128)(2,1)S(1)}, u32[]{:S(2)}, u32[]{:S(2)}) collective-permute-start(bf16[8,3072]{1,0:T(8,128)(2,1)S(1)} %get-tuple-element.45), channel_id=1, source_target_pairs={{1,0},{2,1},{3,2},{0,3},{5,4},{6,5},{7,6},{4,7},{9,8},{10,9},{11,1... | collective-permute-start | bytes 147464 | tf_op jit(solution)/shard_map/ppermute | solution.py:100
  113.8 0.6 collective-permute-start.22
  114.4 3.3 %collective-permute-start.23 = (bf16[8,3200]{1,0:T(8,128)(2,1)S(1)}, bf16[8,3200]{1,0:T(8,128)(2,1)S(1)}, u32[]{:S(2)}, u32[]{:S(2)}) collective-permute-start(bf16[8,3200]{1,0:T(8,128)(2,1)S(1)} %get-tuple-element.42), channel_id=1, source_target_pairs={{1,0},{2,1},{3,2},{0,3},{5,4},{6,5},{7,6},{4,7},{9,8},{10,9},{11,1... | collective-permute-start | bytes 153608 | tf_op jit(solution)/shard_map/ppermute | solution.py:100
  117.7 2.0 %collective-permute-done.21 = bf16[8,3200]{1,0:T(8,128)(2,1)S(1)} collective-permute-done((bf16[8,3200]{1,0:T(8,128)(2,1)S(1)}, bf16[8,3200]{1,0:T(8,128)(2,1)S(1)}, u32[]{:S(2)}, u32[]{:S(2)}) %collective-permute-start.21) | collective-permute-done | bytes 51232 | tf_op jit(solution)/shard_map/ppermute | solution.py:100
  119.7 0.6 collective-permute-done.23
  120.6 0.6 pad_maximum_fusion.16
  121.1 0.9 fusion.41
  (95 shorter events, 3.2 us)
Async XLA Ops:
  0.6 8.5 %copy-start = (bf16[6144,4]{0,1:T(4,128)(2,1)S(1)}, bf16[6144,4]{0,1:T(4,128)(2,1)}, u32[]{:S(2)}) copy-start(bf16[6144,4]{0,1:T(4,128)(2,1)} %param.12) | copy-start | bytes 147460
  0.6 10.7 %collective-permute-start = (bf16[8,6144]{1,0:T(8,128)(2,1)}, bf16[8,6144]{1,0:T(8,128)(2,1)S(1)}, u32[]{:S(2)}, u32[]{:S(2)}) collective-permute-start(bf16[8,6144]{1,0:T(8,128)(2,1)} %param.8), channel_id=1, source_target_pairs={{1,0},{2,1},{3,2},{0,3},{5,4},{6,5},{7,6},{4,7},{9,8},{10,9},{11,1... | collective-permute-start | bytes 294920 | tf_op jit(solution)/shard_map/ppermute | solution.py:100
  5.7 9.7 %collective-permute-start.10 = (bf16[8,6144]{1,0:T(8,128)(2,1)}, bf16[8,6144]{1,0:T(8,128)(2,1)S(1)}, u32[]{:S(2)}, u32[]{:S(2)}) collective-permute-start(bf16[8,6144]{1,0:T(8,128)(2,1)} %param.8), channel_id=1, source_target_pairs={{2,0},{3,1},{0,2},{1,3},{6,4},{7,5},{4,6},{5,7},{10,8},{11,9},{8,1... | collective-permute-start | bytes 294920 | tf_op jit(solution)/shard_map/ppermute | solution.py:100
  5.7 9.7 %collective-permute-start.11 = (bf16[8,6144]{1,0:T(8,128)(2,1)}, bf16[8,6144]{1,0:T(8,128)(2,1)S(1)}, u32[]{:S(2)}, u32[]{:S(2)}) collective-permute-start(bf16[8,6144]{1,0:T(8,128)(2,1)} %param.8), channel_id=1, source_target_pairs={{3,0},{0,1},{1,2},{2,3},{7,4},{4,5},{5,6},{6,7},{11,8},{8,9},{9,10... | collective-permute-start | bytes 294920 | tf_op jit(solution)/shard_map/ppermute | solution.py:100
  11.4 7.2 %collective-permute-start.1 = (bf16[8,6400]{1,0:T(8,128)(2,1)S(1)}, bf16[8,6400]{1,0:T(8,128)(2,1)S(1)}, u32[]{:S(2)}, u32[]{:S(2)}) collective-permute-start(bf16[8,6400]{1,0:T(8,128)(2,1)S(1)} %fusion.42), channel_id=1, source_target_pairs={{1,0},{2,1},{3,2},{0,3},{5,4},{6,5},{7,6},{4,7},{9,8},{10,9},{11,1... | collective-permute-start | bytes 307208 | tf_op jit(solution)/shard_map/ppermute | solution.py:100
  14.2 9.6 %collective-permute-start.2 = (bf16[8,6400]{1,0:T(8,128)(2,1)S(1)}, bf16[8,6400]{1,0:T(8,128)(2,1)S(1)}, u32[]{:S(2)}, u32[]{:S(2)}) collective-permute-start(bf16[8,6400]{1,0:T(8,128)(2,1)S(1)} %fusion.42), channel_id=1, source_target_pairs={{2,0},{3,1},{0,2},{1,3},{6,4},{7,5},{4,6},{5,7},{10,8},{11,9},{8,1... | collective-permute-start | bytes 307208 | tf_op jit(solution)/shard_map/ppermute | solution.py:100
  15.4 8.4 %collective-permute-start.3 = (bf16[8,6400]{1,0:T(8,128)(2,1)S(1)}, bf16[8,6400]{1,0:T(8,128)(2,1)S(1)}, u32[]{:S(2)}, u32[]{:S(2)}) collective-permute-start(bf16[8,6400]{1,0:T(8,128)(2,1)S(1)} %fusion.42), channel_id=1, source_target_pairs={{3,0},{0,1},{1,2},{2,3},{7,4},{4,5},{5,6},{6,7},{11,8},{8,9},{9,10... | collective-permute-start | bytes 307208 | tf_op jit(solution)/shard_map/ppermute | solution.py:100
  15.5 11.5 %collective-permute-start.12 = (bf16[32,3072]{1,0:T(8,128)(2,1)S(1)}, bf16[32,3072]{1,0:T(8,128)(2,1)S(1)}, u32[]{:S(2)}, u32[]{:S(2)}) collective-permute-start(bf16[32,3072]{1,0:T(8,128)(2,1)S(1)} %get-tuple-element.35), channel_id=1, source_target_pairs={{16,0},{0,16},{17,1},{1,17},{18,2},{2,18},{19,3},{3,19},{20,4},{4,... | collective-permute-start | bytes 589832 | tf_op jit(solution)/shard_map/ppermute | solution.py:104
  17.1 10.5 %collective-permute-start.15 = (bf16[32,3072]{1,0:T(8,128)(2,1)S(1)}, bf16[32,3072]{1,0:T(8,128)(2,1)S(1)}, u32[]{:S(2)}, u32[]{:S(2)}) collective-permute-start(bf16[32,3072]{1,0:T(8,128)(2,1)S(1)} %get-tuple-element.37), channel_id=1, source_target_pairs={{8,0},{12,4},{0,8},{4,12},{9,1},{13,5},{1,9},{5,13},{10,2},{14,6},... | collective-permute-start | bytes 589832 | tf_op jit(solution)/shard_map/ppermute | solution.py:104
  23.9 7.5 %collective-permute-start.4 = (bf16[32,3200]{1,0:T(8,128)(2,1)S(1)}, bf16[32,3200]{1,0:T(8,128)(2,1)S(1)}, u32[]{:S(2)}, u32[]{:S(2)}) collective-permute-start(bf16[32,3200]{1,0:T(8,128)(2,1)S(1)} %get-tuple-element.34), channel_id=1, source_target_pairs={{16,0},{0,16},{17,1},{1,17},{18,2},{2,18},{19,3},{3,19},{20,4},{4,... | collective-permute-start | bytes 614408 | tf_op jit(solution)/shard_map/ppermute | solution.py:104
  25.4 8.0 %collective-permute-start.7 = (bf16[32,3200]{1,0:T(8,128)(2,1)S(1)}, bf16[32,3200]{1,0:T(8,128)(2,1)S(1)}, u32[]{:S(2)}, u32[]{:S(2)}) collective-permute-start(bf16[32,3200]{1,0:T(8,128)(2,1)S(1)} %get-tuple-element.32), channel_id=1, source_target_pairs={{8,0},{12,4},{0,8},{4,12},{9,1},{13,5},{1,9},{5,13},{10,2},{14,6},... | collective-permute-start | bytes 614408 | tf_op jit(solution)/shard_map/ppermute | solution.py:104
  27.0 14.9 %collective-permute-start.13 = (bf16[64,3072]{1,0:T(8,128)(2,1)S(1)}, bf16[64,3072]{1,0:T(8,128)(2,1)S(1)}, u32[]{:S(2)}, u32[]{:S(2)}) collective-permute-start(bf16[64,3072]{1,0:T(8,128)(2,1)S(1)} %pad_maximum_fusion.13), channel_id=1, source_target_pairs={{8,0},{12,4},{0,8},{4,12},{9,1},{13,5},{1,9},{5,13},{10,2},{14,6},... | collective-permute-start | bytes 1179656 | tf_op jit(solution)/shard_map/ppermute | solution.py:104
  27.6 14.4 %collective-permute-start.16 = (bf16[64,3072]{1,0:T(8,128)(2,1)S(1)}, bf16[64,3072]{1,0:T(8,128)(2,1)S(1)}, u32[]{:S(2)}, u32[]{:S(2)}) collective-permute-start(bf16[64,3072]{1,0:T(8,128)(2,1)S(1)} %pad_maximum_fusion.14), channel_id=1, source_target_pairs={{16,0},{0,16},{17,1},{1,17},{18,2},{2,18},{19,3},{3,19},{20,4},{4,... | collective-permute-start | bytes 1179656 | tf_op jit(solution)/shard_map/ppermute | solution.py:104
  31.4 17.5 %copy-start.4 = (bf16[1,6144,1024]{2,1,0:T(8,128)(2,1)S(1)}, bf16[1,6144,1024]{2,1,0:T(8,128)(2,1)}, u32[]{:S(2)}) copy-start(bf16[1,6144,1024]{2,1,0:T(8,128)(2,1)} %param.14) | copy-start | bytes 37748740
  31.5 16.5 %collective-permute-start.5 = (bf16[64,3200]{1,0:T(8,128)(2,1)S(1)}, bf16[64,3200]{1,0:T(8,128)(2,1)S(1)}, u32[]{:S(2)}, u32[]{:S(2)}) collective-permute-start(bf16[64,3200]{1,0:T(8,128)(2,1)S(1)} %pad_maximum_fusion.11), channel_id=1, source_target_pairs={{8,0},{12,4},{0,8},{4,12},{9,1},{13,5},{1,9},{5,13},{10,2},{14,6},... | collective-permute-start | bytes 1228808 | tf_op jit(solution)/shard_map/ppermute | solution.py:104
  33.5 14.6 %collective-permute-start.8 = (bf16[64,3200]{1,0:T(8,128)(2,1)S(1)}, bf16[64,3200]{1,0:T(8,128)(2,1)S(1)}, u32[]{:S(2)}, u32[]{:S(2)}) collective-permute-start(bf16[64,3200]{1,0:T(8,128)(2,1)S(1)} %pad_maximum_fusion.12), channel_id=1, source_target_pairs={{16,0},{0,16},{17,1},{1,17},{18,2},{2,18},{19,3},{3,19},{20,4},{4,... | collective-permute-start | bytes 1228808 | tf_op jit(solution)/shard_map/ppermute | solution.py:104
  41.9 7.0 %collective-permute-start.14 = (bf16[128,3072]{1,0:T(8,128)(2,1)S(1)}, bf16[128,3072]{1,0:T(8,128)(2,1)S(1)}, u32[]{:S(2)}, u32[]{:S(2)}) collective-permute-start(bf16[128,3072]{1,0:T(8,128)(2,1)S(1)} %pad_maximum_fusion.9), channel_id=1, source_target_pairs={{4,0},{0,4},{12,8},{8,12},{5,1},{1,5},{13,9},{9,13},{6,2},{2,6},{1... | collective-permute-start | bytes 2359304 | tf_op jit(solution)/shard_map/ppermute | solution.py:104
  42.1 6.7 %collective-permute-start.17 = (bf16[128,3072]{1,0:T(8,128)(2,1)S(1)}, bf16[128,3072]{1,0:T(8,128)(2,1)S(1)}, u32[]{:S(2)}, u32[]{:S(2)}) collective-permute-start(bf16[128,3072]{1,0:T(8,128)(2,1)S(1)} %pad_maximum_fusion.10), channel_id=1, source_target_pairs={{4,0},{0,4},{12,8},{8,12},{5,1},{1,5},{13,9},{9,13},{6,2},{2,6},{1... | collective-permute-start | bytes 2359304 | tf_op jit(solution)/shard_map/ppermute | solution.py:104
  48.0 5.5 %collective-permute-start.6 = (bf16[128,3200]{1,0:T(8,128)(2,1)S(1)}, bf16[128,3200]{1,0:T(8,128)(2,1)S(1)}, u32[]{:S(2)}, u32[]{:S(2)}) collective-permute-start(bf16[128,3200]{1,0:T(8,128)(2,1)S(1)} %pad_maximum_fusion.7), channel_id=1, source_target_pairs={{4,0},{0,4},{12,8},{8,12},{5,1},{1,5},{13,9},{9,13},{6,2},{2,6},{1... | collective-permute-start | bytes 2457608 | tf_op jit(solution)/shard_map/ppermute | solution.py:104
  48.3 5.4 %collective-permute-start.9 = (bf16[128,3200]{1,0:T(8,128)(2,1)S(1)}, bf16[128,3200]{1,0:T(8,128)(2,1)S(1)}, u32[]{:S(2)}, u32[]{:S(2)}) collective-permute-start(bf16[128,3200]{1,0:T(8,128)(2,1)S(1)} %pad_maximum_fusion.8), channel_id=1, source_target_pairs={{4,0},{0,4},{12,8},{8,12},{5,1},{1,5},{13,9},{9,13},{6,2},{2,6},{1... | collective-permute-start | bytes 2457608 | tf_op jit(solution)/shard_map/ppermute | solution.py:104
  48.9 4.6 %copy-start.1 = (bf16[256,3072]{1,0:T(8,128)(2,1)}, bf16[256,3072]{1,0:T(8,128)(2,1)S(1)}, u32[]{:S(2)}) copy-start(bf16[256,3072]{1,0:T(8,128)(2,1)S(1)} %constant_dynamic-update-slice_fusion.13) | copy-start | bytes 4718596
  53.7 8.2 %copy-start.2 = (bf16[256,3072]{1,0:T(8,128)(2,1)S(1)}, bf16[256,3072]{1,0:T(8,128)(2,1)}, u32[]{:S(2)}) copy-start(bf16[256,3072]{1,0:T(8,128)(2,1)} %copy-done.1) | copy-start | bytes 4718596
  70.8 10.1 %slice-start = ((s8[12582912]{0:T(1024)(128)(4,1)}), s8[4194304]{0:T(1024)(128)(4,1)S(1)}, s32[]{:S(2)}) async-start(s8[12582912]{0:T(1024)(128)(4,1)} %bitcast.46), calls=%async_computation | async-start | bytes 8388608
  70.8 10.1 %slice-start.1 = ((s8[12582912]{0:T(1024)(128)(4,1)}), s8[4194304]{0:T(1024)(128)(4,1)S(1)}, s32[]{:S(2)}) async-start(s8[12582912]{0:T(1024)(128)(4,1)} %bitcast.46), calls=%async_computation.1 | async-start | bytes 8388608
  75.8 5.1 %slice-start.2 = ((s8[12582912]{0:T(1024)(128)(4,1)}), s8[4194304]{0:T(1024)(128)(4,1)S(1)}, s32[]{:S(2)}) async-start(s8[12582912]{0:T(1024)(128)(4,1)} %bitcast.46), calls=%async_computation.2 | async-start | bytes 8388608
  87.5 2.4 %collective-permute-start.24 = (bf16[128,3072]{1,0:T(8,128)(2,1)S(1)}, bf16[128,3072]{1,0:T(8,128)(2,1)S(1)}, u32[]{:S(2)}, u32[]{:S(2)}) collective-permute-start(bf16[128,3072]{1,0:T(8,128)(2,1)S(1)} %slice.142), channel_id=1, source_target_pairs={{4,0},{0,4},{12,8},{8,12},{5,1},{1,5},{13,9},{9,13},{6,2},{2,6},{1... | collective-permute-start | bytes 2359304 | tf_op jit(solution)/shard_map/ppermute | solution.py:104
  87.7 3.4 %collective-permute-start.18 = (bf16[128,3200]{1,0:T(8,128)(2,1)S(1)}, bf16[128,3200]{1,0:T(8,128)(2,1)S(1)}, u32[]{:S(2)}, u32[]{:S(2)}) collective-permute-start(bf16[128,3200]{1,0:T(8,128)(2,1)S(1)} %slice.115), channel_id=1, source_target_pairs={{4,0},{0,4},{12,8},{8,12},{5,1},{1,5},{13,9},{9,13},{6,2},{2,6},{1... | collective-permute-start | bytes 2457608 | tf_op jit(solution)/shard_map/ppermute | solution.py:104
  90.2 11.2 %collective-permute-start.25 = (bf16[64,3072]{1,0:T(8,128)(2,1)S(1)}, bf16[64,3072]{1,0:T(8,128)(2,1)S(1)}, u32[]{:S(2)}, u32[]{:S(2)}) collective-permute-start(bf16[64,3072]{1,0:T(8,128)(2,1)S(1)} %pad_maximum_fusion.15), channel_id=1, source_target_pairs={{16,0},{0,16},{17,1},{1,17},{18,2},{2,18},{19,3},{3,19},{20,4},{4,... | collective-permute-start | bytes 1179656 | tf_op jit(solution)/shard_map/ppermute | solution.py:104
  91.3 11.8 %collective-permute-start.19 = (bf16[64,3200]{1,0:T(8,128)(2,1)S(1)}, bf16[64,3200]{1,0:T(8,128)(2,1)S(1)}, u32[]{:S(2)}, u32[]{:S(2)}) collective-permute-start(bf16[64,3200]{1,0:T(8,128)(2,1)S(1)} %concatenate.95), channel_id=1, source_target_pairs={{8,0},{12,4},{0,8},{4,12},{9,1},{13,5},{1,9},{5,13},{10,2},{14,6},... | collective-permute-start | bytes 1228808 | tf_op jit(solution)/shard_map/ppermute | solution.py:104
  101.5 6.2 %collective-permute-start.26 = (bf16[32,3072]{1,0:T(8,128)(2,1)S(1)}, bf16[32,3072]{1,0:T(8,128)(2,1)S(1)}, u32[]{:S(2)}, u32[]{:S(2)}) collective-permute-start(bf16[32,3072]{1,0:T(8,128)(2,1)S(1)} %fusion.37), channel_id=1, source_target_pairs={{8,0},{12,4},{0,8},{4,12},{9,1},{13,5},{1,9},{5,13},{10,2},{14,6},... | collective-permute-start | bytes 589832 | tf_op jit(solution)/shard_map/ppermute | solution.py:104
  103.1 17.4 %copy-start.3 = (s32[8]{0:T(128)S(1)}, s32[8]{0:T(128)}, u32[]{:S(2)}) copy-start(s32[8]{0:T(128)} %param.10) | copy-start | bytes 100
  103.2 10.4 %collective-permute-start.20 = (bf16[32,3200]{1,0:T(8,128)(2,1)S(1)}, bf16[32,3200]{1,0:T(8,128)(2,1)S(1)}, u32[]{:S(2)}, u32[]{:S(2)}) collective-permute-start(bf16[32,3200]{1,0:T(8,128)(2,1)S(1)} %fusion.35), channel_id=1, source_target_pairs={{16,0},{0,16},{17,1},{1,17},{18,2},{2,18},{19,3},{3,19},{20,4},{4,... | collective-permute-start | bytes 614408 | tf_op jit(solution)/shard_map/ppermute | solution.py:104
  107.7 6.6 %collective-permute-start.27 = (bf16[8,3072]{1,0:T(8,128)(2,1)S(1)}, bf16[8,3072]{1,0:T(8,128)(2,1)S(1)}, u32[]{:S(2)}, u32[]{:S(2)}) collective-permute-start(bf16[8,3072]{1,0:T(8,128)(2,1)S(1)} %get-tuple-element.44), channel_id=1, source_target_pairs={{3,0},{0,1},{1,2},{2,3},{7,4},{4,5},{5,6},{6,7},{11,8},{8,9},{9,10... | collective-permute-start | bytes 147464 | tf_op jit(solution)/shard_map/ppermute | solution.py:100
  108.8 8.8 %collective-permute-start.28 = (bf16[8,3072]{1,0:T(8,128)(2,1)S(1)}, bf16[8,3072]{1,0:T(8,128)(2,1)S(1)}, u32[]{:S(2)}, u32[]{:S(2)}) collective-permute-start(bf16[8,3072]{1,0:T(8,128)(2,1)S(1)} %get-tuple-element.46), channel_id=1, source_target_pairs={{2,0},{3,1},{0,2},{1,3},{6,4},{7,5},{4,6},{5,7},{10,8},{11,9},{8,1... | collective-permute-start | bytes 147464 | tf_op jit(solution)/shard_map/ppermute | solution.py:100
  110.8 6.8 %collective-permute-start.29 = (bf16[8,3072]{1,0:T(8,128)(2,1)S(1)}, bf16[8,3072]{1,0:T(8,128)(2,1)S(1)}, u32[]{:S(2)}, u32[]{:S(2)}) collective-permute-start(bf16[8,3072]{1,0:T(8,128)(2,1)S(1)} %get-tuple-element.45), channel_id=1, source_target_pairs={{1,0},{2,1},{3,2},{0,3},{5,4},{6,5},{7,6},{4,7},{9,8},{10,9},{11,1... | collective-permute-start | bytes 147464 | tf_op jit(solution)/shard_map/ppermute | solution.py:100
  113.8 6.0 %collective-permute-start.21 = (bf16[8,3200]{1,0:T(8,128)(2,1)S(1)}, bf16[8,3200]{1,0:T(8,128)(2,1)S(1)}, u32[]{:S(2)}, u32[]{:S(2)}) collective-permute-start(bf16[8,3200]{1,0:T(8,128)(2,1)S(1)} %get-tuple-element.41), channel_id=1, source_target_pairs={{3,0},{0,1},{1,2},{2,3},{7,4},{4,5},{5,6},{6,7},{11,8},{8,9},{9,10... | collective-permute-start | bytes 153608 | tf_op jit(solution)/shard_map/ppermute | solution.py:100
  113.8 5.9 %collective-permute-start.22 = (bf16[8,3200]{1,0:T(8,128)(2,1)S(1)}, bf16[8,3200]{1,0:T(8,128)(2,1)S(1)}, u32[]{:S(2)}, u32[]{:S(2)}) collective-permute-start(bf16[8,3200]{1,0:T(8,128)(2,1)S(1)} %get-tuple-element.43), channel_id=1, source_target_pairs={{2,0},{3,1},{0,2},{1,3},{6,4},{7,5},{4,6},{5,7},{10,8},{11,9},{8,1... | collective-permute-start | bytes 153608 | tf_op jit(solution)/shard_map/ppermute | solution.py:100
  114.4 5.9 %collective-permute-start.23 = (bf16[8,3200]{1,0:T(8,128)(2,1)S(1)}, bf16[8,3200]{1,0:T(8,128)(2,1)S(1)}, u32[]{:S(2)}, u32[]{:S(2)}) collective-permute-start(bf16[8,3200]{1,0:T(8,128)(2,1)S(1)} %get-tuple-element.42), channel_id=1, source_target_pairs={{1,0},{2,1},{3,2},{0,3},{5,4},{6,5},{7,6},{4,7},{9,8},{10,9},{11,1... | collective-permute-start | bytes 153608 | tf_op jit(solution)/shard_map/ppermute | solution.py:100

commit v3 on v2

--- a/solution.py
+++ b/solution.py
@@ -1,7 +1,19 @@
+import functools
+import math
+
 import jax
 import jax.numpy as jnp
 from jax import lax
+from jax.experimental import pallas as pl
+from jax.experimental.pallas import tpu as pltpu
 from jax.sharding import PartitionSpec as P
+
+TOKEN_PART = 512
+HIDDEN_PART = 256
+COLUMN_PART = 512
+TOKEN_VMEM = 16 * 2 ** 20
+GRAD_VMEM = 20 * 2 ** 20
+OUTPUT_VMEM = 16 * 2 ** 20
 
 
 def routed_plan(tokens, out_grad, kept_mask, routes, router, gate_weight, up_weight, down_weight):
@@ -120,23 +132,25 @@
     return [rows] + [shift(rows, "mp", k) for k in range(1, lax.axis_size("mp"))]
 
 
-def gather_rest(z_rows):
-    z_rows = jnp.concatenate(z_rows, axis=0)
-    columns = z_rows.shape[1] // 256 * 128
-    halves = []
-    for half, first, second in ((z_rows[:, :columns], swap_x, swap_y), (z_rows[:, columns:], swap_y, swap_x)):
-        near = first(half)
-        far = second(jnp.concatenate([half, near], axis=0))
-        far = jnp.split(far, 2, axis=0)
-        blocks = [half, near] + far if first is swap_x else [half, far[0], near, far[1]]
-        mine = jnp.concatenate(blocks, axis=0)
-        halves.append(jnp.concatenate([mine, swap_core(mine)], axis=0))
-    return halves
-
-
-def scatter_half(partial, first, second):
-    rows = partial.shape[0] // 2
-    total = partial[:rows].astype(jnp.float32) + swap_core(partial[rows:]).astype(jnp.float32)
+def gather_near(z_rows, cut):
+    rows = jnp.concatenate(z_rows, axis=0)
+    low, high = rows[:, :cut], rows[:, cut:]
+    return [low, swap_x(low)], [high, swap_y(high)]
+
+
+def gather_far(low, high):
+    return swap_y(jnp.concatenate(low, axis=0)), swap_x(jnp.concatenate(high, axis=0))
+
+
+def gather_core(low, low_far, high, high_far):
+    high_far = jnp.split(high_far, 2, axis=0)
+    low = jnp.concatenate(low + [low_far], axis=0)
+    high = jnp.concatenate([high[0], high_far[0], high[1], high_far[1]], axis=0)
+    return tuple(jnp.concatenate([mine, swap_core(mine)], axis=0) for mine in (low, high))
+
+
+def scatter_half(kept, sent, first, second):
+    total = kept + swap_core(sent).astype(jnp.float32)
     own, by_x, by_y, by_both = jnp.split(total, 4, axis=0)
     near, far = (by_x, [by_y, by_both]) if first is swap_x else (by_y, [by_x, by_both])
     rest = second(jnp.concatenate(far, axis=0).astype(jnp.bfloat16)).astype(jnp.float32)
@@ -153,6 +167,172 @@
     return result
 
 
+def product(a, b, b_dim):
+    return lax.dot_general(a, b, (((1,), (b_dim,)), ((), ())), preferred_element_type=jnp.float32)
+
+
+def part_of(length, wanted):
+    return math.gcd(length, wanted)
+
+
+def token_kernel(low, high, gate_weight, up_weight, pre_gate, pre_up, gate_copy, up_copy, gate_sems, up_sems):
+    half = low.shape[1]
+    depth = part_of(half, TOKEN_PART)
+    steps = half // depth
+
+    def copies(index):
+        rows = pl.ds(pl.multiple_of(index * depth, depth), depth)
+        return (
+            pltpu.make_async_copy(gate_weight.at[0, rows], gate_copy.at[rows], gate_sems.at[index]),
+            pltpu.make_async_copy(up_weight.at[0, rows], up_copy.at[rows], up_sems.at[index]),
+        )
+
+    @pl.loop(0, 2 * steps)
+    def _(index):
+        for copy in copies(index):
+            copy.start()
+
+    pre_gate[...] = jnp.zeros_like(pre_gate)
+    pre_up[...] = jnp.zeros_like(pre_up)
+    for first, part in ((0, low), (steps, high)):
+
+        @pl.loop(0, steps)
+        def _(step):
+            for copy in copies(first + step):
+                copy.wait()
+            rows = pl.ds(pl.multiple_of((first + step) * depth, depth), depth)
+            values = part[:, pl.ds(pl.multiple_of(step * depth, depth), depth)]
+            pre_gate[...] += product(values, gate_copy[rows, :], 0)
+            pre_up[...] += product(values, up_copy[rows, :], 0)
+
+
+def multiply_tokens(low, high, gate_weight, up_weight):
+    rows, half = low.shape
+    width, hidden = gate_weight.shape[1:]
+    steps = width // part_of(half, TOKEN_PART)
+    return pl.pallas_call(
+        token_kernel,
+        out_shape=(
+            pltpu.VMEM((rows, hidden), jnp.float32),
+            pltpu.VMEM((rows, hidden), jnp.float32),
+            pltpu.VMEM((width, hidden), jnp.bfloat16),
+            pltpu.VMEM((width, hidden), jnp.bfloat16),
+        ),
+        in_specs=[pl.BlockSpec(memory_space=pltpu.VMEM)] * 2 + [pl.BlockSpec(memory_space=pl.ANY)] * 2,
+        out_specs=(pl.BlockSpec(memory_space=pltpu.VMEM),) * 4,
+        scratch_shapes=[pltpu.SemaphoreType.DMA((steps,)), pltpu.SemaphoreType.DMA((steps,))],
+        compiler_params=pltpu.CompilerParams(vmem_limit_bytes=TOKEN_VMEM),
+        cost_estimate=pl.CostEstimate(
+            flops=4 * rows * width * hidden, bytes_accessed=4 * width * hidden, transcendentals=0
+        ),
+    )(low, high, gate_weight, up_weight)
+
+
+def grad_kernel(
+    expert, low, high, pre_gate, pre_up, down_weight, grad_gate, grad_up, dots, gate_rows, dot_sums, down, down_sems
+):
+    table = low.shape[1] - high.shape[1]
+    half = high.shape[1]
+    hidden = down.shape[0]
+    depth = part_of(hidden, HIDDEN_PART)
+    steps = hidden // depth
+
+    def copy_of(index):
+        rows = pl.ds(pl.multiple_of(index * depth, depth), depth)
+        return pltpu.make_async_copy(down_weight.at[0, rows], down.at[rows], down_sems.at[index])
+
+    @pl.loop(0, steps)
+    def _(index):
+        copy_of(index).start()
+
+    lanes = lax.broadcasted_iota(jnp.int32, (low.shape[0], table), 1)
+    gate_rows[...] = jnp.sum(
+        jnp.where(lanes == expert[0], low[:, :table].astype(jnp.float32), 0.0), axis=1, keepdims=True
+    )
+    dot_sums[...] = jnp.zeros_like(dot_sums)
+
+    @pl.loop(0, steps)
+    def _(step):
+        copy_of(step).wait()
+        span = pl.ds(pl.multiple_of(step * depth, depth), depth)
+        grad_hidden = product(low[:, table:], down[span, :half], 1) + product(high[...], down[span, half:], 1)
+        gates = pre_gate[:, span]
+        ups = pre_up[:, span]
+        sigma = jax.nn.sigmoid(gates)
+        act = gates * sigma
+        dot_sums[...] += jnp.sum(grad_hidden * (act * ups), axis=1, keepdims=True)
+        scaled = gate_rows[...] * grad_hidden
+        grad_gate[:, span] = (scaled * ups * sigma * (1.0 + gates * (1.0 - sigma))).astype(jnp.bfloat16)
+        grad_up[:, span] = (scaled * act).astype(jnp.bfloat16)
+
+    dots[...] = jnp.where(lanes == expert[0], dot_sums[...], 0.0).astype(jnp.bfloat16)
+
+
+def multiply_grads(expert, low, high, pre_gate, pre_up, down_weight):
+    rows, hidden = pre_gate.shape
+    width = down_weight.shape[2]
+    table = low.shape[1] - high.shape[1]
+    return pl.pallas_call(
+        grad_kernel,
+        out_shape=(
+            pltpu.VMEM((rows, hidden), jnp.bfloat16),
+            pltpu.VMEM((rows, hidden), jnp.bfloat16),
+            pltpu.VMEM((rows, table), jnp.bfloat16),
+        ),
+        in_specs=[pl.BlockSpec(memory_space=pltpu.SMEM)]
+        + [pl.BlockSpec(memory_space=pltpu.VMEM)] * 4
+        + [pl.BlockSpec(memory_space=pl.ANY)],
+        out_specs=(pl.BlockSpec(memory_space=pltpu.VMEM),) * 3,
+        scratch_shapes=[
+            pltpu.VMEM((rows, 1), jnp.float32),
+            pltpu.VMEM((rows, 1), jnp.float32),
+            pltpu.VMEM((hidden, width), jnp.bfloat16),
+            pltpu.SemaphoreType.DMA((hidden // part_of(hidden, HIDDEN_PART),)),
+        ],
+        compiler_params=pltpu.CompilerParams(vmem_limit_bytes=GRAD_VMEM),
+        cost_estimate=pl.CostEstimate(
+            flops=2 * rows * width * hidden, bytes_accessed=2 * width * hidden, transcendentals=rows * hidden
+        ),
+    )(expert, low, high, pre_gate, pre_up, down_weight)
+
+
+def output_kernel(first, grad_gate, grad_up, gate_copy, up_copy, *refs):
+    dots, kept, sent = refs if len(refs) == 3 else (None,) + refs
+    rows = kept.shape[0]
+    columns = kept.shape[1] - (0 if dots is None else dots.shape[1])
+    part = part_of(columns, COLUMN_PART)
+
+    @pl.loop(0, columns // part)
+    def _(step):
+        span = pl.ds(pl.multiple_of(first + step * part, part), part)
+        place = pl.ds(pl.multiple_of(step * part, part), part)
+        result = product(grad_gate[...], gate_copy[span, :], 1) + product(grad_up[...], up_copy[span, :], 1)
+        kept[:, place] = result[:rows]
+        sent[:, place] = result[rows:].astype(jnp.bfloat16)
+
+    if dots is not None:
+        kept[:, columns:] = dots[:rows, :].astype(jnp.float32)
+        sent[:, columns:] = dots[rows:, :]
+
+
+def multiply_outputs(first, columns, grad_gate, grad_up, gate_copy, up_copy, *dots):
+    rows, hidden = grad_gate.shape
+    total = columns + sum(value.shape[1] for value in dots)
+    return pl.pallas_call(
+        functools.partial(output_kernel, first),
+        out_shape=(
+            pltpu.VMEM((rows // 2, total), jnp.float32),
+            pltpu.VMEM((rows // 2, total), jnp.bfloat16),
+        ),
+        in_specs=[pl.BlockSpec(memory_space=pltpu.VMEM)] * (4 + len(dots)),
+        out_specs=(pl.BlockSpec(memory_space=pltpu.VMEM),) * 2,
+        compiler_params=pltpu.CompilerParams(vmem_limit_bytes=OUTPUT_VMEM),
+        cost_estimate=pl.CostEstimate(
+            flops=4 * rows * columns * hidden, bytes_accessed=4 * rows * columns, transcendentals=0
+        ),
+    )(grad_gate, grad_up, gate_copy, up_copy, *dots)
+
+
 def gathered_plan(tokens, out_grad, kept_mask, routes, router, gate_weight, up_weight, down_weight):
     row_count, width = tokens.shape
     expert_count = lax.axis_size("expert")
@@ -160,6 +340,8 @@
     first_hot = (routes[:, 0:1] == columns).astype(jnp.float32)
     second_hot = (routes[:, 1:2] == columns).astype(jnp.float32)
     keep_rows = kept_mask.astype(jnp.float32)
+    half = width // 2
+    table = 128
     token_z = gather_z(tokens)
     logits = jnp.dot(tokens, router, preferred_element_type=jnp.float32)
     first_logit = jnp.sum(logits * first_hot, axis=1)
@@ -167,41 +349,25 @@
     gate_first = jax.nn.sigmoid(first_logit - second_logit)
     gate_second = jax.nn.sigmoid(second_logit - first_logit)
     gate_table = (first_hot * gate_first[:, None] + second_hot * gate_second[:, None]) * keep_rows[:, None]
-    gate_table = jnp.pad(gate_table.astype(jnp.bfloat16), ((0, 0), (0, 256 - expert_count)))
+    gate_table = jnp.pad(gate_table.astype(jnp.bfloat16), ((0, 0), (0, table - expert_count)))
     grad_rows, token_z[1] = lax.optimization_barrier((jnp.concatenate([gate_table, out_grad], axis=1), token_z[1]))
     grad_z = gather_z(grad_rows)
-    token_halves = gather_rest(token_z)
-    grad_halves = gather_rest(grad_z)
-    half = width // 2
-    expert = lax.axis_index("expert")
-    first_grad = grad_halves[0][:, 256:]
-    gates = grad_halves[0][:, :expert_count].astype(jnp.float32)
-    gate_all = jnp.sum(jnp.where(lax.broadcasted_iota(jnp.int32, gates.shape, 1) == expert, gates, 0.0), axis=1)
-    second_grad = grad_halves[1]
-    gate_local, up_local, down_local = gate_weight[0], up_weight[0], down_weight[0]
-
-    def dot(a, b):
-        return jnp.dot(a, b, preferred_element_type=jnp.float32)
-
-    token_all = jnp.concatenate(token_halves, axis=1)
-    grad_all = jnp.concatenate([first_grad, second_grad], axis=1)
-    pre_gate = dot(token_all, gate_local)
-    pre_up = dot(token_all, up_local)
-    sigma = jax.nn.sigmoid(pre_gate)
-    act = pre_gate * sigma
-    hidden = act * pre_up
-    grad_hidden = dot(grad_all, down_local.T)
-    gate_dot = jnp.sum(grad_hidden * hidden, axis=1)
-    scaled = gate_all[:, None] * grad_hidden
-    grad_gate = (scaled * pre_up * sigma * (1.0 + pre_gate * (1.0 - sigma))).astype(jnp.bfloat16)
-    grad_up = (scaled * act).astype(jnp.bfloat16)
-    dots = jnp.where(lax.broadcasted_iota(jnp.int32, (gate_dot.shape[0], 128), 1) == expert, gate_dot[:, None], 0.0)
-    low = dot(grad_gate, gate_local[:half].T) + dot(grad_up, up_local[:half].T)
-    low = jnp.concatenate([low.astype(jnp.bfloat16), dots.astype(jnp.bfloat16)], axis=1)
-    low, grad_gate, grad_up = lax.optimization_barrier((low, grad_gate, grad_up))
-    high = dot(grad_gate, gate_local[half:].T) + dot(grad_up, up_local[half:].T)
-    low = scatter_z(scatter_half(low, swap_x, swap_y))
-    high = scatter_z(scatter_half(high.astype(jnp.bfloat16), swap_y, swap_x))
+    token_near = gather_near(token_z, half)
+    token_far = gather_far(*token_near)
+    grad_z, token_far = lax.optimization_barrier((grad_z, token_far))
+    grad_near = gather_near(grad_z, half + table)
+    token_halves = gather_core(token_near[0], token_far[0], token_near[1], token_far[1])
+    grad_far = gather_far(*grad_near)
+    pre_gate, pre_up, gate_copy, up_copy = multiply_tokens(*token_halves, gate_weight, up_weight)
+    grad_far, pre_gate = lax.optimization_barrier((grad_far, pre_gate))
+    grad_halves = gather_core(grad_near[0], grad_far[0], grad_near[1], grad_far[1])
+    expert = lax.axis_index("expert").astype(jnp.int32).reshape(1)
+    grad_gate, grad_up, dots = multiply_grads(expert, *grad_halves, pre_gate, pre_up, down_weight)
+    kept, sent = multiply_outputs(0, half, grad_gate, grad_up, gate_copy, up_copy, dots)
+    sent, grad_gate = lax.optimization_barrier((sent, grad_gate))
+    low = scatter_z(scatter_half(kept, sent, swap_x, swap_y))
+    kept, sent = multiply_outputs(half, half, grad_gate, grad_up, gate_copy, up_copy)
+    high = scatter_z(scatter_half(kept, sent, swap_y, swap_x))
     expert_sum = jnp.concatenate([low[:, :half], high], axis=1)
     dot_table = low[:, half:half + expert_count]
     dot_first = jnp.sum(dot_table * first_hot, axis=1)

time: 122 us -> 123 us (level)
  matrix products: 40 us -> 2.15 us
  Pallas kernels: 0 us -> 25.2 us
  local copies, waits for them, and re-layouts: 2.42 us -> 16.8 us
  starting transfers between devices: 36.9 us -> 33.1 us
  other arithmetic: 3.93 us -> 5.26 us
    dot_general x7 -> x0, matrix products: 37.9 us -> none  [dot(): return jnp.dot(a, b, preferred_element_type=jnp.float32)]
    pallas_call x0 -> x4, Pallas kernels: none -> 25.2 us  [the longest x1 10.6 us: multiply_tokens(): pl.pallas_call(token_kernel, out_shape=(pltpu.VMEM((rows, hidden), jnp.fl...]
    unnamed x26 -> x22, local copies, waits for them, and re-layouts: 1.09 us -> 14.8 us
    ppermute x12, waiting for transfers between devices: 7.84 us -> 10.9 us  [shift(): lax.ppermute(value, axis, [((i + step) % size, i) for i in range(size)])]
    ppermute x18, starting transfers between devices: 17 us -> 14.2 us  [swap(): lax.ppermute(value, axis, [(i ^ bit, i) for i in range(lax.axis_size(axis...]
    ppermute x18, waiting for transfers between devices: 29.8 us -> 27.8 us  [swap(): lax.ppermute(value, axis, [(i ^ bit, i) for i in range(lax.axis_size(axis...]
    concatenate x9 -> x10, other arithmetic: 0.46 us -> 2.06 us  [the longest x2 0.81 us: gather_far(): jnp.concatenate(high, axis=0)]
  transfers between devices with their start and end apart: 30 -> 30, of which waited for: 11 -> 15; matrix products, arithmetic and copies ran while one was open for 9% -> 6% of each run, Pallas kernels for 0% -> 9%
where the time goes in v3:
time: 123 us; the launch traced here: 122 us
  waiting for transfers between devices  38.7 us (31%)
  starting transfers between devices  33.1 us (27%)
  Pallas kernels  25.2 us (20%)
  local copies, waits for them, and re-layouts  16.8 us (14%)
  other arithmetic  5.26 us (4%)
  matrix products  2.15 us (2%)
    ppermute x18, waiting for transfers between devices, swap(): lax.ppermute(value, axis, [(i ^ bit, i) for i in range(lax.axis_size(axis...  27.8 us
    ppermute x12, starting transfers between devices, shift(): lax.ppermute(value, axis, [((i + step) % size, i) for i in range(size)])  19 us
    unnamed x22, local copies, waits for them, and re-layouts  14.8 us
    ppermute x18, starting transfers between devices, swap(): lax.ppermute(value, axis, [(i ^ bit, i) for i in range(lax.axis_size(axis...  14.2 us
    ppermute x12, waiting for transfers between devices, shift(): lax.ppermute(value, axis, [((i + step) % size, i) for i in range(size)])  10.9 us
    pallas_call x1, Pallas kernels, multiply_tokens(): pl.pallas_call(token_kernel, out_shape=(pltpu.VMEM((rows, hidden), jnp.fl...  10.6 us
    pallas_call x2, Pallas kernels, multiply_outputs(): pl.pallas_call(functools.partial(output_kernel, first), out_shape=(pltpu....  8.99 us
    pallas_call x1, Pallas kernels, multiply_grads(): pl.pallas_call(grad_kernel, out_shape=(pltpu.VMEM((rows, hidden), jnp.bfl...  5.62 us
  transfers between devices with their start and end apart: 30, of which 15 were waited for; matrix products, arithmetic and copies ran while one was open for 6% of the time, Pallas kernels for 9%

profile of v3, /device:TPU:0, one launch (start us, length us, event | category | flops | bytes accessed | tf_op | source)
XLA Modules:
  0.0 122.3 jit_solution(9000932060012098087)
XLA Ops:
  0.6 5.1 %collective-permute-start = (bf16[8,6144]{1,0:T(8,128)(2,1)}, bf16[8,6144]{1,0:T(8,128)(2,1)S(1)}, u32[]{:S(2)}, u32[]{:S(2)}) collective-permute-start(bf16[8,6144]{1,0:T(8,128)(2,1)} %param.8), channel_id=1, source_target_pairs={{1,0},{2,1},{3,2},{0,3},{5,4},{6,5},{7,6},{4,7},{9,8},{10,9},{11,1... | collective-permute-start | bytes 294920 | tf_op jit(solution)/shard_map/ppermute | solution.py:112
  5.8 1.0 collective-permute-start.5
  6.8 0.8 slice_bitcast_fusion
  7.5 0.7 convert_element_type.64
  8.2 1.2 select_reduce_fusion.3
  9.5 0.9 fusion.9
  10.4 0.9 constant_dynamic-update-slice_fusion.3
  11.3 3.4 %collective-permute-done.4 = bf16[8,6144]{1,0:T(8,128)(2,1)S(1)} collective-permute-done((bf16[8,6144]{1,0:T(8,128)(2,1)}, bf16[8,6144]{1,0:T(8,128)(2,1)S(1)}, u32[]{:S(2)}, u32[]{:S(2)}) %collective-permute-start.4) | collective-permute-done | bytes 98336 | tf_op jit(solution)/shard_map/ppermute | solution.py:112
  14.8 1.6 %collective-permute-start.6 = (bf16[32,3072]{1,0:T(8,128)(2,1)S(1)}, bf16[32,3072]{1,0:T(8,128)(2,1)S(1)}, u32[]{:S(2)}, u32[]{:S(2)}) collective-permute-start(bf16[32,3072]{1,0:T(8,128)(2,1)S(1)} %get-tuple-element.72), channel_id=1, source_target_pairs={{16,0},{0,16},{17,1},{1,17},{18,2},{2,18},{19,3},{3,19},{20,4},{4,... | collective-permute-start | bytes 589832 | tf_op jit(solution)/shard_map/ppermute | solution.py:116
  16.4 1.5 %collective-permute-start.8 = (bf16[32,3072]{1,0:T(8,128)(2,1)S(1)}, bf16[32,3072]{1,0:T(8,128)(2,1)S(1)}, u32[]{:S(2)}, u32[]{:S(2)}) collective-permute-start(bf16[32,3072]{1,0:T(8,128)(2,1)S(1)} %get-tuple-element.71), channel_id=1, source_target_pairs={{8,0},{12,4},{0,8},{4,12},{9,1},{13,5},{1,9},{5,13},{10,2},{14,6},... | collective-permute-start | bytes 589832 | tf_op jit(solution)/shard_map/ppermute | solution.py:116
  17.9 3.3 %collective-permute-done.6 = bf16[32,3072]{1,0:T(8,128)(2,1)S(1)} collective-permute-done((bf16[32,3072]{1,0:T(8,128)(2,1)S(1)}, bf16[32,3072]{1,0:T(8,128)(2,1)S(1)}, u32[]{:S(2)}, u32[]{:S(2)}) %collective-permute-start.6) | collective-permute-done | bytes 196640 | tf_op jit(solution)/shard_map/ppermute | solution.py:116
  21.2 0.8 pad_maximum_fusion.7
  22.0 1.5 %collective-permute-start.7 = (bf16[64,3072]{1,0:T(8,128)(2,1)}, bf16[64,3072]{1,0:T(8,128)(2,1)S(1)}, u32[]{:S(2)}, u32[]{:S(2)}) collective-permute-start(bf16[64,3072]{1,0:T(8,128)(2,1)} %pad_maximum_fusion.7), channel_id=1, source_target_pairs={{8,0},{12,4},{0,8},{4,12},{9,1},{13,5},{1,9},{5,13},{10,2},{14,6},... | collective-permute-start | bytes 1179656 | tf_op jit(solution)/shard_map/ppermute | solution.py:116
  23.5 0.8 pad_maximum_fusion.8
  24.3 1.5 %collective-permute-start.9 = (bf16[64,3072]{1,0:T(8,128)(2,1)}, bf16[64,3072]{1,0:T(8,128)(2,1)S(1)}, u32[]{:S(2)}, u32[]{:S(2)}) collective-permute-start(bf16[64,3072]{1,0:T(8,128)(2,1)} %pad_maximum_fusion.8), channel_id=1, source_target_pairs={{16,0},{0,16},{17,1},{1,17},{18,2},{2,18},{19,3},{3,19},{20,4},{4,... | collective-permute-start | bytes 1179656 | tf_op jit(solution)/shard_map/ppermute | solution.py:116
  25.8 1.3 %collective-permute-start.1 = (bf16[8,6272]{1,0:T(8,128)(2,1)S(1)}, bf16[8,6272]{1,0:T(8,128)(2,1)S(1)}, u32[]{:S(2)}, u32[]{:S(2)}) collective-permute-start(bf16[8,6272]{1,0:T(8,128)(2,1)S(1)} %fusion.9), channel_id=1, source_target_pairs={{1,0},{2,1},{3,2},{0,3},{5,4},{6,5},{7,6},{4,7},{9,8},{10,9},{11,1... | collective-permute-start | bytes 301064 | tf_op jit(solution)/shard_map/ppermute | solution.py:112
  27.1 0.7 collective-permute-start.2
  27.7 2.0 %collective-permute-start.3 = (bf16[8,6272]{1,0:T(8,128)(2,1)S(1)}, bf16[8,6272]{1,0:T(8,128)(2,1)}, u32[]{:S(2)}, u32[]{:S(2)}) collective-permute-start(bf16[8,6272]{1,0:T(8,128)(2,1)S(1)} %fusion.9), channel_id=1, source_target_pairs={{3,0},{0,1},{1,2},{2,3},{7,4},{4,5},{5,6},{6,7},{11,8},{8,9},{9,10... | collective-permute-start | bytes 301064 | tf_op jit(solution)/shard_map/ppermute | solution.py:112
  29.8 1.7 %collective-permute-done.1 = bf16[8,6272]{1,0:T(8,128)(2,1)S(1)} collective-permute-done((bf16[8,6272]{1,0:T(8,128)(2,1)S(1)}, bf16[8,6272]{1,0:T(8,128)(2,1)S(1)}, u32[]{:S(2)}, u32[]{:S(2)}) %collective-permute-start.1) | collective-permute-done | bytes 100384 | tf_op jit(solution)/shard_map/ppermute | solution.py:112
  31.5 3.5 %collective-permute-done.2 = bf16[8,6272]{1,0:T(8,128)(2,1)S(1)} collective-permute-done((bf16[8,6272]{1,0:T(8,128)(2,1)S(1)}, bf16[8,6272]{1,0:T(8,128)(2,1)S(1)}, u32[]{:S(2)}, u32[]{:S(2)}) %collective-permute-start.2) | collective-permute-done | bytes 100384 | tf_op jit(solution)/shard_map/ppermute | solution.py:112
  35.1 0.9 constant_dynamic-update-slice_fusion.4
  36.3 0.6 collective-permute-start.12
  37.7 5.9 %collective-permute-done.12 = bf16[32,3072]{1,0:T(8,128)(2,1)S(1)} collective-permute-done((bf16[32,3072]{1,0:T(8,128)(2,1)S(1)}, bf16[32,3072]{1,0:T(8,128)(2,1)S(1)}, u32[]{:S(2)}, u32[]{:S(2)}) %collective-permute-start.12) | collective-permute-done | bytes 196640 | tf_op jit(solution)/shard_map/ppermute | solution.py:116
  43.7 0.6 collective-permute-start.13
  44.5 1.6 %collective-permute-start.11 = (bf16[64,3200]{1,0:T(8,128)(2,1)S(1)}, bf16[64,3200]{1,0:T(8,128)(2,1)S(1)}, u32[]{:S(2)}, u32[]{:S(2)}) collective-permute-start(bf16[64,3200]{1,0:T(8,128)(2,1)S(1)} %pad_maximum_fusion.6), channel_id=1, source_target_pairs={{8,0},{12,4},{0,8},{4,12},{9,1},{13,5},{1,9},{5,13},{10,2},{14,6},... | collective-permute-start | bytes 1228808 | tf_op jit(solution)/shard_map/ppermute | solution.py:116
  46.3 10.6 %shard_map.95 = (f32[256,1024]{1,0:T(8,128)S(1)}, f32[256,1024]{1,0:T(8,128)S(1)}, bf16[6144,1024]{1,0:T(8,128)(2,1)S(1)}, bf16[6144,1024]{1,0:T(8,128)(2,1)S(1)}) custom-call(bf16[256,3072]{1,0:T(8,128)(2,1)S(1)} %pad_maximum_fusion.1.low, bf16[256,3072]{1,0:T(8,128)(2,1)S(1)} %constant_dynamic-update-slice_fusion.8.high, ...), custom_call_target="tpu_custom_call" | custom-call | flops 6442450944 | bytes 25165824 | tf_op jit(solution)/shard_map/pallas_call | solution.py:213
  56.9 4.5 %copy-done.1 = bf16[6144,1024]{1,0:T(8,128)(2,1)} copy-done((bf16[6144,1024]{1,0:T(8,128)(2,1)}, bf16[6144,1024]{1,0:T(8,128)(2,1)S(1)}, u32[]{:S(2)}) %copy-start.1) | copy-done | bytes 12582936
  62.3 1.6 %collective-permute-done.17 = bf16[128,3072]{1,0:T(8,128)(2,1)S(1)} collective-permute-done((bf16[128,3072]{1,0:T(8,128)(2,1)S(1)}, bf16[128,3072]{1,0:T(8,128)(2,1)S(1)}, u32[]{:S(2)}, u32[]{:S(2)}) %collective-permute-start.17) | collective-permute-done | bytes 786464 | tf_op jit(solution)/shard_map/ppermute | solution.py:116
  64.0 1.1 collective-permute-done.16
  65.2 4.6 %copy-done.3 = bf16[1,1024,6144]{2,1,0:T(8,128)(2,1)S(1)} copy-done((bf16[1,1024,6144]{2,1,0:T(8,128)(2,1)S(1)}, bf16[1,1024,6144]{2,1,0:T(8,128)(2,1)}, u32[]{:S(2)}) %copy-start.3) | copy-done | bytes 12582936
  69.8 5.6 %shard_map.96 = (bf16[256,1024]{1,0:T(8,128)(2,1)S(1)}, bf16[256,1024]{1,0:T(8,128)(2,1)S(1)}, bf16[256,128]{1,0:T(8,128)(2,1)S(1)}) custom-call(s32[1]{0:T(128)} %bitcast.expert, bf16[256,3200]{1,0:T(8,128)(2,1)S(1)} %pad_maximum_fusion.low, bf16[256,3072]{1,0:T(8,128)(2,1)S(1)} %constant_dynamic-update-slice_fusion.13.high, ...), custom_call_target="tpu_custom_call" | custom-call | flops 3221225472 | bytes 12582912 | tf_op jit(solution)/shard_map/pallas_call | solution.py:275
  75.4 4.6 %copy-done.2 = bf16[6144,1024]{1,0:T(8,128)(2,1)S(1)} copy-done((bf16[6144,1024]{1,0:T(8,128)(2,1)S(1)}, bf16[6144,1024]{1,0:T(8,128)(2,1)}, u32[]{:S(2)}) %copy-start.2) | copy-done | bytes 12582936
  80.0 4.5 %shard_map.97 = (f32[128,3200]{1,0:T(8,128)S(1)}, bf16[128,3200]{1,0:T(8,128)(2,1)S(1)}) custom-call(bf16[256,1024]{1,0:T(8,128)(2,1)S(1)} %get-tuple-element.47.grad_gate, bf16[256,1024]{1,0:T(8,128)(2,1)S(1)} %get-tuple-element.40.grad_up, bf16[6144,1024]{1,0:T(8,128)(2,1)S(1)} %get-tuple-element.41.gate_copy, bf16[6144,1024]{1,0:T(8,128)(2,1)S(1)} %copy-done.2, ...), custom_call_target="tpu_custom_call" | custom-call | flops 3221225472 | bytes 3145728 | tf_op jit(solution)/shard_map/pallas_call | solution.py:321
  84.5 4.5 %shard_map.98 = (f32[128,3072]{1,0:T(8,128)S(1)}, bf16[128,3072]{1,0:T(8,128)(2,1)S(1)}) custom-call(bf16[256,1024]{1,0:T(8,128)(2,1)S(1)} %get-tuple-element.47.grad_gate, bf16[256,1024]{1,0:T(8,128)(2,1)S(1)} %get-tuple-element.40.grad_up, bf16[6144,1024]{1,0:T(8,128)(2,1)S(1)} %get-tuple-element.41.gate_copy, bf16[6144,1024]{1,0:T(8,128)(2,1)S(1)} %copy-done.2), custom_call_target="tpu_custom_call" | custom-call | flops 3221225472 | bytes 3145728 | tf_op jit(solution)/shard_map/pallas_call | solution.py:321
  89.6 1.8 %collective-permute-done.24 = bf16[128,3072]{1,0:T(8,128)(2,1)S(1)} collective-permute-done((bf16[128,3072]{1,0:T(8,128)(2,1)S(1)}, bf16[128,3072]{1,0:T(8,128)(2,1)S(1)}, u32[]{:S(2)}, u32[]{:S(2)}) %collective-permute-start.24) | collective-permute-done | bytes 786464 | tf_op jit(solution)/shard_map/ppermute | solution.py:116
  91.7 0.6 collective-permute-start.25
  92.7 1.1 collective-permute-start.19
  93.8 9.1 %collective-permute-done.25 = bf16[64,3072]{1,0:T(8,128)(2,1)S(1)} collective-permute-done((bf16[64,3072]{1,0:T(8,128)(2,1)S(1)}, bf16[64,3072]{1,0:T(8,128)(2,1)S(1)}, u32[]{:S(2)}, u32[]{:S(2)}) %collective-permute-start.25) | collective-permute-done | bytes 393248 | tf_op jit(solution)/shard_map/ppermute | solution.py:116
  103.0 0.6 collective-permute-start.26
  103.6 0.7 collective-permute-done.19
  104.4 1.0 collective-permute-start.20
  105.4 3.8 %collective-permute-done.26 = bf16[32,3072]{1,0:T(8,128)(2,1)S(1)} collective-permute-done((bf16[32,3072]{1,0:T(8,128)(2,1)S(1)}, bf16[32,3072]{1,0:T(8,128)(2,1)S(1)}, u32[]{:S(2)}, u32[]{:S(2)}) %collective-permute-start.26) | collective-permute-done | bytes 196640 | tf_op jit(solution)/shard_map/ppermute | solution.py:116
  109.3 1.9 %collective-permute-start.28 = (bf16[8,3072]{1,0:T(8,128)(2,1)S(1)}, bf16[8,3072]{1,0:T(8,128)(2,1)S(1)}, u32[]{:S(2)}, u32[]{:S(2)}) collective-permute-start(bf16[8,3072]{1,0:T(8,128)(2,1)S(1)} %get-tuple-element.78), channel_id=1, source_target_pairs={{2,0},{3,1},{0,2},{1,3},{6,4},{7,5},{4,6},{5,7},{10,8},{11,9},{8,1... | collective-permute-start | bytes 147464 | tf_op jit(solution)/shard_map/ppermute | solution.py:112
  111.2 2.6 %collective-permute-start.29 = (bf16[8,3072]{1,0:T(8,128)(2,1)S(1)}, bf16[8,3072]{1,0:T(8,128)(2,1)S(1)}, u32[]{:S(2)}, u32[]{:S(2)}) collective-permute-start(bf16[8,3072]{1,0:T(8,128)(2,1)S(1)} %get-tuple-element.77), channel_id=1, source_target_pairs={{1,0},{2,1},{3,2},{0,3},{5,4},{6,5},{7,6},{4,7},{9,8},{10,9},{11,1... | collective-permute-start | bytes 147464 | tf_op jit(solution)/shard_map/ppermute | solution.py:112
  114.0 1.4 %collective-permute-start.22 = (bf16[8,3200]{1,0:T(8,128)(2,1)S(1)}, bf16[8,3200]{1,0:T(8,128)(2,1)S(1)}, u32[]{:S(2)}, u32[]{:S(2)}) collective-permute-start(bf16[8,3200]{1,0:T(8,128)(2,1)S(1)} %get-tuple-element.75), channel_id=1, source_target_pairs={{2,0},{3,1},{0,2},{1,3},{6,4},{7,5},{4,6},{5,7},{10,8},{11,9},{8,1... | collective-permute-start | bytes 153608 | tf_op jit(solution)/shard_map/ppermute | solution.py:112
  115.4 2.8 %collective-permute-start.23 = (bf16[8,3200]{1,0:T(8,128)(2,1)S(1)}, bf16[8,3200]{1,0:T(8,128)(2,1)S(1)}, u32[]{:S(2)}, u32[]{:S(2)}) collective-permute-start(bf16[8,3200]{1,0:T(8,128)(2,1)S(1)} %get-tuple-element.74), channel_id=1, source_target_pairs={{1,0},{2,1},{3,2},{0,3},{5,4},{6,5},{7,6},{4,7},{9,8},{10,9},{11,1... | collective-permute-start | bytes 153608 | tf_op jit(solution)/shard_map/ppermute | solution.py:112
  118.3 1.6 %collective-permute-done.21 = bf16[8,3200]{1,0:T(8,128)(2,1)S(1)} collective-permute-done((bf16[8,3200]{1,0:T(8,128)(2,1)S(1)}, bf16[8,3200]{1,0:T(8,128)(2,1)S(1)}, u32[]{:S(2)}, u32[]{:S(2)}) %collective-permute-start.21) | collective-permute-done | bytes 51232 | tf_op jit(solution)/shard_map/ppermute | solution.py:112
  121.3 0.9 fusion.6
  (81 shorter events, 5.9 us)
Async XLA Ops:
  0.6 7.5 %copy-start = (bf16[6144,4]{0,1:T(4,128)(2,1)S(1)}, bf16[6144,4]{0,1:T(4,128)(2,1)}, u32[]{:S(2)}) copy-start(bf16[6144,4]{0,1:T(4,128)(2,1)} %param.12) | copy-start | bytes 147460
  0.6 10.7 %collective-permute-start = (bf16[8,6144]{1,0:T(8,128)(2,1)}, bf16[8,6144]{1,0:T(8,128)(2,1)S(1)}, u32[]{:S(2)}, u32[]{:S(2)}) collective-permute-start(bf16[8,6144]{1,0:T(8,128)(2,1)} %param.8), channel_id=1, source_target_pairs={{1,0},{2,1},{3,2},{0,3},{5,4},{6,5},{7,6},{4,7},{9,8},{10,9},{11,1... | collective-permute-start | bytes 294920 | tf_op jit(solution)/shard_map/ppermute | solution.py:112
  5.7 9.0 %collective-permute-start.4 = (bf16[8,6144]{1,0:T(8,128)(2,1)}, bf16[8,6144]{1,0:T(8,128)(2,1)S(1)}, u32[]{:S(2)}, u32[]{:S(2)}) collective-permute-start(bf16[8,6144]{1,0:T(8,128)(2,1)} %param.8), channel_id=1, source_target_pairs={{2,0},{3,1},{0,2},{1,3},{6,4},{7,5},{4,6},{5,7},{10,8},{11,9},{8,1... | collective-permute-start | bytes 294920 | tf_op jit(solution)/shard_map/ppermute | solution.py:112
  5.8 9.0 %collective-permute-start.5 = (bf16[8,6144]{1,0:T(8,128)(2,1)}, bf16[8,6144]{1,0:T(8,128)(2,1)S(1)}, u32[]{:S(2)}, u32[]{:S(2)}) collective-permute-start(bf16[8,6144]{1,0:T(8,128)(2,1)} %param.8), channel_id=1, source_target_pairs={{3,0},{0,1},{1,2},{2,3},{7,4},{4,5},{5,6},{6,7},{11,8},{8,9},{9,10... | collective-permute-start | bytes 294920 | tf_op jit(solution)/shard_map/ppermute | solution.py:112
  14.8 6.4 %collective-permute-start.6 = (bf16[32,3072]{1,0:T(8,128)(2,1)S(1)}, bf16[32,3072]{1,0:T(8,128)(2,1)S(1)}, u32[]{:S(2)}, u32[]{:S(2)}) collective-permute-start(bf16[32,3072]{1,0:T(8,128)(2,1)S(1)} %get-tuple-element.72), channel_id=1, source_target_pairs={{16,0},{0,16},{17,1},{1,17},{18,2},{2,18},{19,3},{3,19},{20,4},{4,... | collective-permute-start | bytes 589832 | tf_op jit(solution)/shard_map/ppermute | solution.py:116
  16.4 7.1 %collective-permute-start.8 = (bf16[32,3072]{1,0:T(8,128)(2,1)S(1)}, bf16[32,3072]{1,0:T(8,128)(2,1)S(1)}, u32[]{:S(2)}, u32[]{:S(2)}) collective-permute-start(bf16[32,3072]{1,0:T(8,128)(2,1)S(1)} %get-tuple-element.71), channel_id=1, source_target_pairs={{8,0},{12,4},{0,8},{4,12},{9,1},{13,5},{1,9},{5,13},{10,2},{14,6},... | collective-permute-start | bytes 589832 | tf_op jit(solution)/shard_map/ppermute | solution.py:116
  22.0 13.1 %collective-permute-start.7 = (bf16[64,3072]{1,0:T(8,128)(2,1)}, bf16[64,3072]{1,0:T(8,128)(2,1)S(1)}, u32[]{:S(2)}, u32[]{:S(2)}) collective-permute-start(bf16[64,3072]{1,0:T(8,128)(2,1)} %pad_maximum_fusion.7), channel_id=1, source_target_pairs={{8,0},{12,4},{0,8},{4,12},{9,1},{13,5},{1,9},{5,13},{10,2},{14,6},... | collective-permute-start | bytes 1179656 | tf_op jit(solution)/shard_map/ppermute | solution.py:116
  24.3 10.8 %collective-permute-start.9 = (bf16[64,3072]{1,0:T(8,128)(2,1)}, bf16[64,3072]{1,0:T(8,128)(2,1)S(1)}, u32[]{:S(2)}, u32[]{:S(2)}) collective-permute-start(bf16[64,3072]{1,0:T(8,128)(2,1)} %pad_maximum_fusion.8), channel_id=1, source_target_pairs={{16,0},{0,16},{17,1},{1,17},{18,2},{2,18},{19,3},{3,19},{20,4},{4,... | collective-permute-start | bytes 1179656 | tf_op jit(solution)/shard_map/ppermute | solution.py:116
  25.8 5.7 %collective-permute-start.1 = (bf16[8,6272]{1,0:T(8,128)(2,1)S(1)}, bf16[8,6272]{1,0:T(8,128)(2,1)S(1)}, u32[]{:S(2)}, u32[]{:S(2)}) collective-permute-start(bf16[8,6272]{1,0:T(8,128)(2,1)S(1)} %fusion.9), channel_id=1, source_target_pairs={{1,0},{2,1},{3,2},{0,3},{5,4},{6,5},{7,6},{4,7},{9,8},{10,9},{11,1... | collective-permute-start | bytes 301064 | tf_op jit(solution)/shard_map/ppermute | solution.py:112
  27.1 8.0 %collective-permute-start.2 = (bf16[8,6272]{1,0:T(8,128)(2,1)S(1)}, bf16[8,6272]{1,0:T(8,128)(2,1)S(1)}, u32[]{:S(2)}, u32[]{:S(2)}) collective-permute-start(bf16[8,6272]{1,0:T(8,128)(2,1)S(1)} %fusion.9), channel_id=1, source_target_pairs={{2,0},{3,1},{0,2},{1,3},{6,4},{7,5},{4,6},{5,7},{10,8},{11,9},{8,1... | collective-permute-start | bytes 301064 | tf_op jit(solution)/shard_map/ppermute | solution.py:112
  27.7 7.3 %collective-permute-start.3 = (bf16[8,6272]{1,0:T(8,128)(2,1)S(1)}, bf16[8,6272]{1,0:T(8,128)(2,1)}, u32[]{:S(2)}, u32[]{:S(2)}) collective-permute-start(bf16[8,6272]{1,0:T(8,128)(2,1)S(1)} %fusion.9), channel_id=1, source_target_pairs={{3,0},{0,1},{1,2},{2,3},{7,4},{4,5},{5,6},{6,7},{11,8},{8,9},{9,10... | collective-permute-start | bytes 301064 | tf_op jit(solution)/shard_map/ppermute | solution.py:112
  36.2 10.0 %collective-permute-start.15 = (bf16[128,3072]{1,0:T(8,128)(2,1)S(1)}, bf16[128,3072]{1,0:T(8,128)(2,1)S(1)}, u32[]{:S(2)}, u32[]{:S(2)}) collective-permute-start(bf16[128,3072]{1,0:T(8,128)(2,1)S(1)} %pad_maximum_fusion.4), channel_id=1, source_target_pairs={{4,0},{0,4},{12,8},{8,12},{5,1},{1,5},{13,9},{9,13},{6,2},{2,6},{1... | collective-permute-start | bytes 2359304 | tf_op jit(solution)/shard_map/ppermute | solution.py:116
  36.3 7.4 %collective-permute-start.12 = (bf16[32,3072]{1,0:T(8,128)(2,1)S(1)}, bf16[32,3072]{1,0:T(8,128)(2,1)S(1)}, u32[]{:S(2)}, u32[]{:S(2)}) collective-permute-start(bf16[32,3072]{1,0:T(8,128)(2,1)S(1)} %get-tuple-element.63), channel_id=1, source_target_pairs={{8,0},{12,4},{0,8},{4,12},{9,1},{13,5},{1,9},{5,13},{10,2},{14,6},... | collective-permute-start | bytes 589832 | tf_op jit(solution)/shard_map/ppermute | solution.py:116
  36.9 9.2 %collective-permute-start.14 = (bf16[128,3072]{1,0:T(8,128)(2,1)S(1)}, bf16[128,3072]{1,0:T(8,128)(2,1)S(1)}, u32[]{:S(2)}, u32[]{:S(2)}) collective-permute-start(bf16[128,3072]{1,0:T(8,128)(2,1)S(1)} %pad_maximum_fusion.3), channel_id=1, source_target_pairs={{4,0},{0,4},{12,8},{8,12},{5,1},{1,5},{13,9},{9,13},{6,2},{2,6},{1... | collective-permute-start | bytes 2359304 | tf_op jit(solution)/shard_map/ppermute | solution.py:116
  37.2 7.3 %collective-permute-start.10 = (bf16[32,3200]{1,0:T(8,128)(2,1)S(1)}, bf16[32,3200]{1,0:T(8,128)(2,1)S(1)}, u32[]{:S(2)}, u32[]{:S(2)}) collective-permute-start(bf16[32,3200]{1,0:T(8,128)(2,1)S(1)} %slice.74), channel_id=1, source_target_pairs={{16,0},{0,16},{17,1},{1,17},{18,2},{2,18},{19,3},{3,19},{20,4},{4,... | collective-permute-start | bytes 614408 | tf_op jit(solution)/shard_map/ppermute | solution.py:116
  43.7 17.8 %collective-permute-start.13 = (bf16[64,3072]{1,0:T(8,128)(2,1)S(1)}, bf16[64,3072]{1,0:T(8,128)(2,1)S(1)}, u32[]{:S(2)}, u32[]{:S(2)}) collective-permute-start(bf16[64,3072]{1,0:T(8,128)(2,1)S(1)} %pad_maximum_fusion.9), channel_id=1, source_target_pairs={{16,0},{0,16},{17,1},{1,17},{18,2},{2,18},{19,3},{3,19},{20,4},{4,... | collective-permute-start | bytes 1179656 | tf_op jit(solution)/shard_map/ppermute | solution.py:116
  44.5 16.9 %collective-permute-start.11 = (bf16[64,3200]{1,0:T(8,128)(2,1)S(1)}, bf16[64,3200]{1,0:T(8,128)(2,1)S(1)}, u32[]{:S(2)}, u32[]{:S(2)}) collective-permute-start(bf16[64,3200]{1,0:T(8,128)(2,1)S(1)} %pad_maximum_fusion.6), channel_id=1, source_target_pairs={{8,0},{12,4},{0,8},{4,12},{9,1},{13,5},{1,9},{5,13},{10,2},{14,6},... | collective-permute-start | bytes 1228808 | tf_op jit(solution)/shard_map/ppermute | solution.py:116
  56.9 4.5 %copy-start.1 = (bf16[6144,1024]{1,0:T(8,128)(2,1)}, bf16[6144,1024]{1,0:T(8,128)(2,1)S(1)}, u32[]{:S(2)}) copy-start(bf16[6144,1024]{1,0:T(8,128)(2,1)S(1)} %get-tuple-element.42.up_copy) | copy-start | bytes 37748740
  61.6 2.4 %collective-permute-start.17 = (bf16[128,3072]{1,0:T(8,128)(2,1)S(1)}, bf16[128,3072]{1,0:T(8,128)(2,1)S(1)}, u32[]{:S(2)}, u32[]{:S(2)}) collective-permute-start(bf16[128,3072]{1,0:T(8,128)(2,1)S(1)} %pad_maximum_fusion.5), channel_id=1, source_target_pairs={{4,0},{0,4},{12,8},{8,12},{5,1},{1,5},{13,9},{9,13},{6,2},{2,6},{1... | collective-permute-start | bytes 2359304 | tf_op jit(solution)/shard_map/ppermute | solution.py:116
  61.7 3.4 %collective-permute-start.16 = (bf16[128,3200]{1,0:T(8,128)(2,1)S(1)}, bf16[128,3200]{1,0:T(8,128)(2,1)S(1)}, u32[]{:S(2)}, u32[]{:S(2)}) collective-permute-start(bf16[128,3200]{1,0:T(8,128)(2,1)S(1)} %pad_maximum_fusion.2), channel_id=1, source_target_pairs={{4,0},{0,4},{12,8},{8,12},{5,1},{1,5},{13,9},{9,13},{6,2},{2,6},{1... | collective-permute-start | bytes 2457608 | tf_op jit(solution)/shard_map/ppermute | solution.py:116
  65.2 4.6 %copy-start.3 = (bf16[1,1024,6144]{2,1,0:T(8,128)(2,1)S(1)}, bf16[1,1024,6144]{2,1,0:T(8,128)(2,1)}, u32[]{:S(2)}) copy-start(bf16[1,1024,6144]{2,1,0:T(8,128)(2,1)} %down_weight.1) | copy-start | bytes 37748740
  75.4 4.6 %copy-start.2 = (bf16[6144,1024]{1,0:T(8,128)(2,1)S(1)}, bf16[6144,1024]{1,0:T(8,128)(2,1)}, u32[]{:S(2)}) copy-start(bf16[6144,1024]{1,0:T(8,128)(2,1)} %copy-done.1) | copy-start | bytes 37748740
  89.0 2.4 %collective-permute-start.24 = (bf16[128,3072]{1,0:T(8,128)(2,1)S(1)}, bf16[128,3072]{1,0:T(8,128)(2,1)S(1)}, u32[]{:S(2)}, u32[]{:S(2)}) collective-permute-start(bf16[128,3072]{1,0:T(8,128)(2,1)S(1)} %get-tuple-element.49), channel_id=1, source_target_pairs={{4,0},{0,4},{12,8},{8,12},{5,1},{1,5},{13,9},{9,13},{6,2},{2,6},{1... | collective-permute-start | bytes 2359304 | tf_op jit(solution)/shard_map/ppermute | solution.py:116
  89.2 3.3 %collective-permute-start.18 = (bf16[128,3200]{1,0:T(8,128)(2,1)S(1)}, bf16[128,3200]{1,0:T(8,128)(2,1)S(1)}, u32[]{:S(2)}, u32[]{:S(2)}) collective-permute-start(bf16[128,3200]{1,0:T(8,128)(2,1)S(1)} %get-tuple-element.46), channel_id=1, source_target_pairs={{4,0},{0,4},{12,8},{8,12},{5,1},{1,5},{13,9},{9,13},{6,2},{2,6},{1... | collective-permute-start | bytes 2457608 | tf_op jit(solution)/shard_map/ppermute | solution.py:116
  91.7 11.2 %collective-permute-start.25 = (bf16[64,3072]{1,0:T(8,128)(2,1)S(1)}, bf16[64,3072]{1,0:T(8,128)(2,1)S(1)}, u32[]{:S(2)}, u32[]{:S(2)}) collective-permute-start(bf16[64,3072]{1,0:T(8,128)(2,1)S(1)} %pad_maximum_fusion.10), channel_id=1, source_target_pairs={{16,0},{0,16},{17,1},{1,17},{18,2},{2,18},{19,3},{3,19},{20,4},{4,... | collective-permute-start | bytes 1179656 | tf_op jit(solution)/shard_map/ppermute | solution.py:116
  92.7 11.6 %collective-permute-start.19 = (bf16[64,3200]{1,0:T(8,128)(2,1)S(1)}, bf16[64,3200]{1,0:T(8,128)(2,1)S(1)}, u32[]{:S(2)}, u32[]{:S(2)}) collective-permute-start(bf16[64,3200]{1,0:T(8,128)(2,1)S(1)} %concatenate.79), channel_id=1, source_target_pairs={{8,0},{12,4},{0,8},{4,12},{9,1},{13,5},{1,9},{5,13},{10,2},{14,6},... | collective-permute-start | bytes 1228808 | tf_op jit(solution)/shard_map/ppermute | solution.py:116
  103.0 6.2 %collective-permute-start.26 = (bf16[32,3072]{1,0:T(8,128)(2,1)S(1)}, bf16[32,3072]{1,0:T(8,128)(2,1)S(1)}, u32[]{:S(2)}, u32[]{:S(2)}) collective-permute-start(bf16[32,3072]{1,0:T(8,128)(2,1)S(1)} %fusion.2), channel_id=1, source_target_pairs={{8,0},{12,4},{0,8},{4,12},{9,1},{13,5},{1,9},{5,13},{10,2},{14,6},... | collective-permute-start | bytes 589832 | tf_op jit(solution)/shard_map/ppermute | solution.py:116
  104.4 9.4 %collective-permute-start.20 = (bf16[32,3200]{1,0:T(8,128)(2,1)S(1)}, bf16[32,3200]{1,0:T(8,128)(2,1)S(1)}, u32[]{:S(2)}, u32[]{:S(2)}) collective-permute-start(bf16[32,3200]{1,0:T(8,128)(2,1)S(1)} %fusion), channel_id=1, source_target_pairs={{16,0},{0,16},{17,1},{1,17},{18,2},{2,18},{19,3},{3,19},{20,4},{4,... | collective-permute-start | bytes 614408 | tf_op jit(solution)/shard_map/ppermute | solution.py:116
  109.2 11.5 %copy-start.4 = (s32[8]{0:T(128)S(1)}, s32[8]{0:T(128)}, u32[]{:S(2)}) copy-start(s32[8]{0:T(128)} %param.10) | copy-start | bytes 100
  109.3 6.1 %collective-permute-start.27 = (bf16[8,3072]{1,0:T(8,128)(2,1)S(1)}, bf16[8,3072]{1,0:T(8,128)(2,1)S(1)}, u32[]{:S(2)}, u32[]{:S(2)}) collective-permute-start(bf16[8,3072]{1,0:T(8,128)(2,1)S(1)} %get-tuple-element.76), channel_id=1, source_target_pairs={{3,0},{0,1},{1,2},{2,3},{7,4},{4,5},{5,6},{6,7},{11,8},{8,9},{9,10... | collective-permute-start | bytes 147464 | tf_op jit(solution)/shard_map/ppermute | solution.py:112
  109.3 8.9 %collective-permute-start.28 = (bf16[8,3072]{1,0:T(8,128)(2,1)S(1)}, bf16[8,3072]{1,0:T(8,128)(2,1)S(1)}, u32[]{:S(2)}, u32[]{:S(2)}) collective-permute-start(bf16[8,3072]{1,0:T(8,128)(2,1)S(1)} %get-tuple-element.78), channel_id=1, source_target_pairs={{2,0},{3,1},{0,2},{1,3},{6,4},{7,5},{4,6},{5,7},{10,8},{11,9},{8,1... | collective-permute-start | bytes 147464 | tf_op jit(solution)/shard_map/ppermute | solution.py:112
  111.2 7.0 %collective-permute-start.29 = (bf16[8,3072]{1,0:T(8,128)(2,1)S(1)}, bf16[8,3072]{1,0:T(8,128)(2,1)S(1)}, u32[]{:S(2)}, u32[]{:S(2)}) collective-permute-start(bf16[8,3072]{1,0:T(8,128)(2,1)S(1)} %get-tuple-element.77), channel_id=1, source_target_pairs={{1,0},{2,1},{3,2},{0,3},{5,4},{6,5},{7,6},{4,7},{9,8},{10,9},{11,1... | collective-permute-start | bytes 147464 | tf_op jit(solution)/shard_map/ppermute | solution.py:112
  113.9 6.0 %collective-permute-start.21 = (bf16[8,3200]{1,0:T(8,128)(2,1)S(1)}, bf16[8,3200]{1,0:T(8,128)(2,1)S(1)}, u32[]{:S(2)}, u32[]{:S(2)}) collective-permute-start(bf16[8,3200]{1,0:T(8,128)(2,1)S(1)} %get-tuple-element.73), channel_id=1, source_target_pairs={{3,0},{0,1},{1,2},{2,3},{7,4},{4,5},{5,6},{6,7},{11,8},{8,9},{9,10... | collective-permute-start | bytes 153608 | tf_op jit(solution)/shard_map/ppermute | solution.py:112
  114.0 5.9 %collective-permute-start.22 = (bf16[8,3200]{1,0:T(8,128)(2,1)S(1)}, bf16[8,3200]{1,0:T(8,128)(2,1)S(1)}, u32[]{:S(2)}, u32[]{:S(2)}) collective-permute-start(bf16[8,3200]{1,0:T(8,128)(2,1)S(1)} %get-tuple-element.75), channel_id=1, source_target_pairs={{2,0},{3,1},{0,2},{1,3},{6,4},{7,5},{4,6},{5,7},{10,8},{11,9},{8,1... | collective-permute-start | bytes 153608 | tf_op jit(solution)/shard_map/ppermute | solution.py:112
  115.4 5.1 %collective-permute-start.23 = (bf16[8,3200]{1,0:T(8,128)(2,1)S(1)}, bf16[8,3200]{1,0:T(8,128)(2,1)S(1)}, u32[]{:S(2)}, u32[]{:S(2)}) collective-permute-start(bf16[8,3200]{1,0:T(8,128)(2,1)S(1)} %get-tuple-element.74), channel_id=1, source_target_pairs={{1,0},{2,1},{3,2},{0,3},{5,4},{6,5},{7,6},{4,7},{9,8},{10,9},{11,1... | collective-permute-start | bytes 153608 | tf_op jit(solution)/shard_map/ppermute | solution.py:112

commit v4 on v3

--- a/solution.py
+++ b/solution.py
@@ -175,6 +175,10 @@
     return math.gcd(length, wanted)
 
 
+def in_hbm(value):
+    return pltpu.with_memory_space_constraint(value, pltpu.HBM)
+
+
 def token_kernel(low, high, gate_weight, up_weight, pre_gate, pre_up, gate_copy, up_copy, gate_sems, up_sems):
     half = low.shape[1]
     depth = part_of(half, TOKEN_PART)
@@ -225,7 +229,7 @@
         cost_estimate=pl.CostEstimate(
             flops=4 * rows * width * hidden, bytes_accessed=4 * width * hidden, transcendentals=0
         ),
-    )(low, high, gate_weight, up_weight)
+    )(low, high, in_hbm(gate_weight), in_hbm(up_weight))
 
 
 def grad_kernel(
@@ -293,7 +297,7 @@
         cost_estimate=pl.CostEstimate(
             flops=2 * rows * width * hidden, bytes_accessed=2 * width * hidden, transcendentals=rows * hidden
         ),
-    )(expert, low, high, pre_gate, pre_up, down_weight)
+    )(expert, low, high, pre_gate, pre_up, in_hbm(down_weight))
 
 
 def output_kernel(first, grad_gate, grad_up, gate_copy, up_copy, *refs):

time: 123 us -> 110 us (0.89)
  local copies, waits for them, and re-layouts: 16.8 us -> 3.09 us
    unnamed x22 -> x16, local copies, waits for them, and re-layouts: 14.8 us -> 1.1 us
  transfers between devices with their start and end apart: 30 -> 30, of which waited for: 15 -> 15; matrix products, arithmetic and copies ran while one was open for 6% -> 7% of each run, Pallas kernels for 9% -> 10%
where the time goes in v4:
time: 110 us; the launch traced here: 109 us
  waiting for transfers between devices  38.7 us (35%)
  starting transfers between devices  33.2 us (30%)
  Pallas kernels  26 us (24%)
  other arithmetic  5.25 us (5%)
  local copies, waits for them, and re-layouts  3.09 us (3%)
  matrix products  2.14 us (2%)
    ppermute x18, waiting for transfers between devices, swap(): lax.ppermute(value, axis, [(i ^ bit, i) for i in range(lax.axis_size(axis...  27.8 us
    ppermute x12, starting transfers between devices, shift(): lax.ppermute(value, axis, [((i + step) % size, i) for i in range(size)])  19 us
    ppermute x18, starting transfers between devices, swap(): lax.ppermute(value, axis, [(i ^ bit, i) for i in range(lax.axis_size(axis...  14.2 us
    ppermute x12, waiting for transfers between devices, shift(): lax.ppermute(value, axis, [((i + step) % size, i) for i in range(size)])  10.9 us
    pallas_call x1, Pallas kernels, multiply_tokens(): pl.pallas_call(token_kernel, out_shape=(pltpu.VMEM((rows, hidden), jnp.fl...  10.6 us
    pallas_call x2, Pallas kernels, multiply_outputs(): pl.pallas_call(functools.partial(output_kernel, first), out_shape=(pltpu....  8.92 us
    pallas_call x1, Pallas kernels, multiply_grads(): pl.pallas_call(grad_kernel, out_shape=(pltpu.VMEM((rows, hidden), jnp.bfl...  6.55 us
  transfers between devices with their start and end apart: 30, of which 15 were waited for; matrix products, arithmetic and copies ran while one was open for 7% of the time, Pallas kernels for 10%

profile of v4, /device:TPU:0, one launch (start us, length us, event | category | flops | bytes accessed | tf_op | source)
XLA Modules:
  0.0 109.4 jit_solution(18370098441460722127)
XLA Ops:
  0.6 5.1 %collective-permute-start = (bf16[8,6144]{1,0:T(8,128)(2,1)}, bf16[8,6144]{1,0:T(8,128)(2,1)S(1)}, u32[]{:S(2)}, u32[]{:S(2)}) collective-permute-start(bf16[8,6144]{1,0:T(8,128)(2,1)} %param.8), channel_id=1, source_target_pairs={{1,0},{2,1},{3,2},{0,3},{5,4},{6,5},{7,6},{4,7},{9,8},{10,9},{11,1... | collective-permute-start | bytes 294920 | tf_op jit(solution)/shard_map/ppermute | solution.py:112
  5.8 1.0 collective-permute-start.5
  6.8 0.8 slice_bitcast_fusion
  7.5 0.7 convert_element_type.64
  8.2 1.2 %select_reduce_fusion.3 = (f32[8]{0:T(128)S(1)}, f32[8]{0:T(128)S(1)}) fusion(s32[8]{0:T(128)S(1)} %get-tuple-element.84, s32[8]{0:T(128)S(1)} %get-tuple-element.83, bf16[8,6144]{1,0:T(8,128)(2,1)} %param.8, bf16[6144,4]{0,1:T(4,128)(2,1)S(1)} %copy-done), kind=kOutput, calls=%fused_computation.61 | convolution fusion | flops 393392 | bytes 147584 | tf_op jit(solution)/shard_map/dot_general | solution.py:350
  9.5 0.9 fusion.9
  10.4 0.9 constant_dynamic-update-slice_fusion.3
  11.3 3.4 %collective-permute-done.4 = bf16[8,6144]{1,0:T(8,128)(2,1)S(1)} collective-permute-done((bf16[8,6144]{1,0:T(8,128)(2,1)}, bf16[8,6144]{1,0:T(8,128)(2,1)S(1)}, u32[]{:S(2)}, u32[]{:S(2)}) %collective-permute-start.4) | collective-permute-done | bytes 98336 | tf_op jit(solution)/shard_map/ppermute | solution.py:112
  14.8 1.6 %collective-permute-start.6 = (bf16[32,3072]{1,0:T(8,128)(2,1)S(1)}, bf16[32,3072]{1,0:T(8,128)(2,1)S(1)}, u32[]{:S(2)}, u32[]{:S(2)}) collective-permute-start(bf16[32,3072]{1,0:T(8,128)(2,1)S(1)} %get-tuple-element.72), channel_id=1, source_target_pairs={{16,0},{0,16},{17,1},{1,17},{18,2},{2,18},{19,3},{3,19},{20,4},{4,... | collective-permute-start | bytes 589832 | tf_op jit(solution)/shard_map/ppermute | solution.py:116
  16.4 1.5 %collective-permute-start.8 = (bf16[32,3072]{1,0:T(8,128)(2,1)S(1)}, bf16[32,3072]{1,0:T(8,128)(2,1)S(1)}, u32[]{:S(2)}, u32[]{:S(2)}) collective-permute-start(bf16[32,3072]{1,0:T(8,128)(2,1)S(1)} %get-tuple-element.71), channel_id=1, source_target_pairs={{8,0},{12,4},{0,8},{4,12},{9,1},{13,5},{1,9},{5,13},{10,2},{14,6},... | collective-permute-start | bytes 589832 | tf_op jit(solution)/shard_map/ppermute | solution.py:116
  17.9 3.3 %collective-permute-done.6 = bf16[32,3072]{1,0:T(8,128)(2,1)S(1)} collective-permute-done((bf16[32,3072]{1,0:T(8,128)(2,1)S(1)}, bf16[32,3072]{1,0:T(8,128)(2,1)S(1)}, u32[]{:S(2)}, u32[]{:S(2)}) %collective-permute-start.6) | collective-permute-done | bytes 196640 | tf_op jit(solution)/shard_map/ppermute | solution.py:116
  21.2 0.8 pad_maximum_fusion.7
  22.0 1.5 %collective-permute-start.7 = (bf16[64,3072]{1,0:T(8,128)(2,1)}, bf16[64,3072]{1,0:T(8,128)(2,1)S(1)}, u32[]{:S(2)}, u32[]{:S(2)}) collective-permute-start(bf16[64,3072]{1,0:T(8,128)(2,1)} %pad_maximum_fusion.7), channel_id=1, source_target_pairs={{8,0},{12,4},{0,8},{4,12},{9,1},{13,5},{1,9},{5,13},{10,2},{14,6},... | collective-permute-start | bytes 1179656 | tf_op jit(solution)/shard_map/ppermute | solution.py:116
  23.5 0.8 pad_maximum_fusion.8
  24.3 1.5 %collective-permute-start.9 = (bf16[64,3072]{1,0:T(8,128)(2,1)}, bf16[64,3072]{1,0:T(8,128)(2,1)S(1)}, u32[]{:S(2)}, u32[]{:S(2)}) collective-permute-start(bf16[64,3072]{1,0:T(8,128)(2,1)} %pad_maximum_fusion.8), channel_id=1, source_target_pairs={{16,0},{0,16},{17,1},{1,17},{18,2},{2,18},{19,3},{3,19},{20,4},{4,... | collective-permute-start | bytes 1179656 | tf_op jit(solution)/shard_map/ppermute | solution.py:116
  25.8 1.3 %collective-permute-start.1 = (bf16[8,6272]{1,0:T(8,128)(2,1)S(1)}, bf16[8,6272]{1,0:T(8,128)(2,1)S(1)}, u32[]{:S(2)}, u32[]{:S(2)}) collective-permute-start(bf16[8,6272]{1,0:T(8,128)(2,1)S(1)} %fusion.9), channel_id=1, source_target_pairs={{1,0},{2,1},{3,2},{0,3},{5,4},{6,5},{7,6},{4,7},{9,8},{10,9},{11,1... | collective-permute-start | bytes 301064 | tf_op jit(solution)/shard_map/ppermute | solution.py:112
  27.0 0.7 collective-permute-start.2
  27.7 2.0 %collective-permute-start.3 = (bf16[8,6272]{1,0:T(8,128)(2,1)S(1)}, bf16[8,6272]{1,0:T(8,128)(2,1)}, u32[]{:S(2)}, u32[]{:S(2)}) collective-permute-start(bf16[8,6272]{1,0:T(8,128)(2,1)S(1)} %fusion.9), channel_id=1, source_target_pairs={{3,0},{0,1},{1,2},{2,3},{7,4},{4,5},{5,6},{6,7},{11,8},{8,9},{9,10... | collective-permute-start | bytes 301064 | tf_op jit(solution)/shard_map/ppermute | solution.py:112
  29.7 1.7 %collective-permute-done.1 = bf16[8,6272]{1,0:T(8,128)(2,1)S(1)} collective-permute-done((bf16[8,6272]{1,0:T(8,128)(2,1)S(1)}, bf16[8,6272]{1,0:T(8,128)(2,1)S(1)}, u32[]{:S(2)}, u32[]{:S(2)}) %collective-permute-start.1) | collective-permute-done | bytes 100384 | tf_op jit(solution)/shard_map/ppermute | solution.py:112
  31.5 3.5 %collective-permute-done.2 = bf16[8,6272]{1,0:T(8,128)(2,1)S(1)} collective-permute-done((bf16[8,6272]{1,0:T(8,128)(2,1)S(1)}, bf16[8,6272]{1,0:T(8,128)(2,1)S(1)}, u32[]{:S(2)}, u32[]{:S(2)}) %collective-permute-start.2) | collective-permute-done | bytes 100384 | tf_op jit(solution)/shard_map/ppermute | solution.py:112
  35.1 0.9 constant_dynamic-update-slice_fusion.4
  36.3 0.6 collective-permute-start.12
  37.7 5.9 %collective-permute-done.12 = bf16[32,3072]{1,0:T(8,128)(2,1)S(1)} collective-permute-done((bf16[32,3072]{1,0:T(8,128)(2,1)S(1)}, bf16[32,3072]{1,0:T(8,128)(2,1)S(1)}, u32[]{:S(2)}, u32[]{:S(2)}) %collective-permute-start.12) | collective-permute-done | bytes 196640 | tf_op jit(solution)/shard_map/ppermute | solution.py:116
  43.7 0.6 collective-permute-start.13
  44.5 1.6 %collective-permute-start.11 = (bf16[64,3200]{1,0:T(8,128)(2,1)S(1)}, bf16[64,3200]{1,0:T(8,128)(2,1)S(1)}, u32[]{:S(2)}, u32[]{:S(2)}) collective-permute-start(bf16[64,3200]{1,0:T(8,128)(2,1)S(1)} %pad_maximum_fusion.6), channel_id=1, source_target_pairs={{8,0},{12,4},{0,8},{4,12},{9,1},{13,5},{1,9},{5,13},{10,2},{14,6},... | collective-permute-start | bytes 1228808 | tf_op jit(solution)/shard_map/ppermute | solution.py:116
  46.3 10.6 %shard_map.95 = (f32[256,1024]{1,0:T(8,128)S(1)}, f32[256,1024]{1,0:T(8,128)S(1)}, bf16[6144,1024]{1,0:T(8,128)(2,1)S(1)}, bf16[6144,1024]{1,0:T(8,128)(2,1)S(1)}) custom-call(bf16[256,3072]{1,0:T(8,128)(2,1)S(1)} %pad_maximum_fusion.1.low, bf16[256,3072]{1,0:T(8,128)(2,1)S(1)} %constant_dynamic-update-slice_fusion.8.high, ...), custom_call_target="tpu_custom_call" | custom-call | flops 6442450944 | bytes 25165824 | tf_op jit(solution)/shard_map/pallas_call | solution.py:217
  57.1 0.6 collective-permute-start.16
  57.7 1.6 %collective-permute-done.17 = bf16[128,3072]{1,0:T(8,128)(2,1)S(1)} collective-permute-done((bf16[128,3072]{1,0:T(8,128)(2,1)S(1)}, bf16[128,3072]{1,0:T(8,128)(2,1)S(1)}, u32[]{:S(2)}, u32[]{:S(2)}) %collective-permute-start.17) | collective-permute-done | bytes 786464 | tf_op jit(solution)/shard_map/ppermute | solution.py:116
  59.4 1.1 %collective-permute-done.16 = bf16[128,3200]{1,0:T(8,128)(2,1)S(1)} collective-permute-done((bf16[128,3200]{1,0:T(8,128)(2,1)S(1)}, bf16[128,3200]{1,0:T(8,128)(2,1)S(1)}, u32[]{:S(2)}, u32[]{:S(2)}) %collective-permute-start.16) | collective-permute-done | bytes 819232 | tf_op jit(solution)/shard_map/ppermute | solution.py:116
  60.6 6.5 %shard_map.96 = (bf16[256,1024]{1,0:T(8,128)(2,1)S(1)}, bf16[256,1024]{1,0:T(8,128)(2,1)S(1)}, bf16[256,128]{1,0:T(8,128)(2,1)S(1)}) custom-call(s32[1]{0:T(128)} %bitcast.expert, bf16[256,3200]{1,0:T(8,128)(2,1)S(1)} %pad_maximum_fusion.low, bf16[256,3072]{1,0:T(8,128)(2,1)S(1)} %constant_dynamic-update-slice_fusion.13.high, ...), custom_call_target="tpu_custom_call" | custom-call | flops 3221225472 | bytes 12582912 | tf_op jit(solution)/shard_map/pallas_call | solution.py:279
  67.2 4.5 %shard_map.97 = (f32[128,3200]{1,0:T(8,128)S(1)}, bf16[128,3200]{1,0:T(8,128)(2,1)S(1)}) custom-call(bf16[256,1024]{1,0:T(8,128)(2,1)S(1)} %get-tuple-element.47.grad_gate, bf16[256,1024]{1,0:T(8,128)(2,1)S(1)} %get-tuple-element.40.grad_up, bf16[6144,1024]{1,0:T(8,128)(2,1)S(1)} %get-tuple-element.41.gate_copy, ...), custom_call_target="tpu_custom_call" | custom-call | flops 3221225472 | bytes 3145728 | tf_op jit(solution)/shard_map/pallas_call | solution.py:325
  71.7 4.5 %shard_map.98 = (f32[128,3072]{1,0:T(8,128)S(1)}, bf16[128,3072]{1,0:T(8,128)(2,1)S(1)}) custom-call(bf16[256,1024]{1,0:T(8,128)(2,1)S(1)} %get-tuple-element.47.grad_gate, bf16[256,1024]{1,0:T(8,128)(2,1)S(1)} %get-tuple-element.40.grad_up, bf16[6144,1024]{1,0:T(8,128)(2,1)S(1)} %get-tuple-element.41.gate_copy, bf16[6144,1024]{1,0:T(8,128)(2,1)S(1)} %get-tuple-element.42.up_copy), custom_call_target="tpu_custom_call" | custom-call | flops 3221225472 | bytes 3145728 | tf_op jit(solution)/shard_map/pallas_call | solution.py:325
  76.7 1.8 %collective-permute-done.24 = bf16[128,3072]{1,0:T(8,128)(2,1)S(1)} collective-permute-done((bf16[128,3072]{1,0:T(8,128)(2,1)S(1)}, bf16[128,3072]{1,0:T(8,128)(2,1)S(1)}, u32[]{:S(2)}, u32[]{:S(2)}) %collective-permute-start.24) | collective-permute-done | bytes 786464 | tf_op jit(solution)/shard_map/ppermute | solution.py:116
  78.8 0.6 collective-permute-start.25
  79.8 1.1 collective-permute-start.19
  80.9 9.1 %collective-permute-done.25 = bf16[64,3072]{1,0:T(8,128)(2,1)S(1)} collective-permute-done((bf16[64,3072]{1,0:T(8,128)(2,1)S(1)}, bf16[64,3072]{1,0:T(8,128)(2,1)S(1)}, u32[]{:S(2)}, u32[]{:S(2)}) %collective-permute-start.25) | collective-permute-done | bytes 393248 | tf_op jit(solution)/shard_map/ppermute | solution.py:116
  90.1 0.6 collective-permute-start.26
  90.7 0.7 collective-permute-done.19
  91.5 1.0 collective-permute-start.20
  92.5 3.8 %collective-permute-done.26 = bf16[32,3072]{1,0:T(8,128)(2,1)S(1)} collective-permute-done((bf16[32,3072]{1,0:T(8,128)(2,1)S(1)}, bf16[32,3072]{1,0:T(8,128)(2,1)S(1)}, u32[]{:S(2)}, u32[]{:S(2)}) %collective-permute-start.26) | collective-permute-done | bytes 196640 | tf_op jit(solution)/shard_map/ppermute | solution.py:116
  96.4 1.9 %collective-permute-start.28 = (bf16[8,3072]{1,0:T(8,128)(2,1)S(1)}, bf16[8,3072]{1,0:T(8,128)(2,1)S(1)}, u32[]{:S(2)}, u32[]{:S(2)}) collective-permute-start(bf16[8,3072]{1,0:T(8,128)(2,1)S(1)} %get-tuple-element.78), channel_id=1, source_target_pairs={{2,0},{3,1},{0,2},{1,3},{6,4},{7,5},{4,6},{5,7},{10,8},{11,9},{8,1... | collective-permute-start | bytes 147464 | tf_op jit(solution)/shard_map/ppermute | solution.py:112
  98.3 2.7 %collective-permute-start.29 = (bf16[8,3072]{1,0:T(8,128)(2,1)S(1)}, bf16[8,3072]{1,0:T(8,128)(2,1)S(1)}, u32[]{:S(2)}, u32[]{:S(2)}) collective-permute-start(bf16[8,3072]{1,0:T(8,128)(2,1)S(1)} %get-tuple-element.77), channel_id=1, source_target_pairs={{1,0},{2,1},{3,2},{0,3},{5,4},{6,5},{7,6},{4,7},{9,8},{10,9},{11,1... | collective-permute-start | bytes 147464 | tf_op jit(solution)/shard_map/ppermute | solution.py:112
  101.1 1.4 %collective-permute-start.22 = (bf16[8,3200]{1,0:T(8,128)(2,1)S(1)}, bf16[8,3200]{1,0:T(8,128)(2,1)S(1)}, u32[]{:S(2)}, u32[]{:S(2)}) collective-permute-start(bf16[8,3200]{1,0:T(8,128)(2,1)S(1)} %get-tuple-element.75), channel_id=1, source_target_pairs={{2,0},{3,1},{0,2},{1,3},{6,4},{7,5},{4,6},{5,7},{10,8},{11,9},{8,1... | collective-permute-start | bytes 153608 | tf_op jit(solution)/shard_map/ppermute | solution.py:112
  102.5 2.8 %collective-permute-start.23 = (bf16[8,3200]{1,0:T(8,128)(2,1)S(1)}, bf16[8,3200]{1,0:T(8,128)(2,1)S(1)}, u32[]{:S(2)}, u32[]{:S(2)}) collective-permute-start(bf16[8,3200]{1,0:T(8,128)(2,1)S(1)} %get-tuple-element.74), channel_id=1, source_target_pairs={{1,0},{2,1},{3,2},{0,3},{5,4},{6,5},{7,6},{4,7},{9,8},{10,9},{11,1... | collective-permute-start | bytes 153608 | tf_op jit(solution)/shard_map/ppermute | solution.py:112
  105.4 1.6 %collective-permute-done.21 = bf16[8,3200]{1,0:T(8,128)(2,1)S(1)} collective-permute-done((bf16[8,3200]{1,0:T(8,128)(2,1)S(1)}, bf16[8,3200]{1,0:T(8,128)(2,1)S(1)}, u32[]{:S(2)}, u32[]{:S(2)}) %collective-permute-start.21) | collective-permute-done | bytes 51232 | tf_op jit(solution)/shard_map/ppermute | solution.py:112
  107.0 0.6 collective-permute-done.23
  107.9 0.6 pad_maximum_fusion.11
  108.4 0.9 fusion.6
  (75 shorter events, 4.2 us)
Async XLA Ops:
  0.6 7.5 %copy-start = (bf16[6144,4]{0,1:T(4,128)(2,1)S(1)}, bf16[6144,4]{0,1:T(4,128)(2,1)}, u32[]{:S(2)}) copy-start(bf16[6144,4]{0,1:T(4,128)(2,1)} %param.12) | copy-start | bytes 147460
  0.6 10.7 %collective-permute-start = (bf16[8,6144]{1,0:T(8,128)(2,1)}, bf16[8,6144]{1,0:T(8,128)(2,1)S(1)}, u32[]{:S(2)}, u32[]{:S(2)}) collective-permute-start(bf16[8,6144]{1,0:T(8,128)(2,1)} %param.8), channel_id=1, source_target_pairs={{1,0},{2,1},{3,2},{0,3},{5,4},{6,5},{7,6},{4,7},{9,8},{10,9},{11,1... | collective-permute-start | bytes 294920 | tf_op jit(solution)/shard_map/ppermute | solution.py:112
  5.7 9.0 %collective-permute-start.4 = (bf16[8,6144]{1,0:T(8,128)(2,1)}, bf16[8,6144]{1,0:T(8,128)(2,1)S(1)}, u32[]{:S(2)}, u32[]{:S(2)}) collective-permute-start(bf16[8,6144]{1,0:T(8,128)(2,1)} %param.8), channel_id=1, source_target_pairs={{2,0},{3,1},{0,2},{1,3},{6,4},{7,5},{4,6},{5,7},{10,8},{11,9},{8,1... | collective-permute-start | bytes 294920 | tf_op jit(solution)/shard_map/ppermute | solution.py:112
  5.8 9.0 %collective-permute-start.5 = (bf16[8,6144]{1,0:T(8,128)(2,1)}, bf16[8,6144]{1,0:T(8,128)(2,1)S(1)}, u32[]{:S(2)}, u32[]{:S(2)}) collective-permute-start(bf16[8,6144]{1,0:T(8,128)(2,1)} %param.8), channel_id=1, source_target_pairs={{3,0},{0,1},{1,2},{2,3},{7,4},{4,5},{5,6},{6,7},{11,8},{8,9},{9,10... | collective-permute-start | bytes 294920 | tf_op jit(solution)/shard_map/ppermute | solution.py:112
  14.8 6.4 %collective-permute-start.6 = (bf16[32,3072]{1,0:T(8,128)(2,1)S(1)}, bf16[32,3072]{1,0:T(8,128)(2,1)S(1)}, u32[]{:S(2)}, u32[]{:S(2)}) collective-permute-start(bf16[32,3072]{1,0:T(8,128)(2,1)S(1)} %get-tuple-element.72), channel_id=1, source_target_pairs={{16,0},{0,16},{17,1},{1,17},{18,2},{2,18},{19,3},{3,19},{20,4},{4,... | collective-permute-start | bytes 589832 | tf_op jit(solution)/shard_map/ppermute | solution.py:116
  16.4 7.1 %collective-permute-start.8 = (bf16[32,3072]{1,0:T(8,128)(2,1)S(1)}, bf16[32,3072]{1,0:T(8,128)(2,1)S(1)}, u32[]{:S(2)}, u32[]{:S(2)}) collective-permute-start(bf16[32,3072]{1,0:T(8,128)(2,1)S(1)} %get-tuple-element.71), channel_id=1, source_target_pairs={{8,0},{12,4},{0,8},{4,12},{9,1},{13,5},{1,9},{5,13},{10,2},{14,6},... | collective-permute-start | bytes 589832 | tf_op jit(solution)/shard_map/ppermute | solution.py:116
  22.0 13.1 %collective-permute-start.7 = (bf16[64,3072]{1,0:T(8,128)(2,1)}, bf16[64,3072]{1,0:T(8,128)(2,1)S(1)}, u32[]{:S(2)}, u32[]{:S(2)}) collective-permute-start(bf16[64,3072]{1,0:T(8,128)(2,1)} %pad_maximum_fusion.7), channel_id=1, source_target_pairs={{8,0},{12,4},{0,8},{4,12},{9,1},{13,5},{1,9},{5,13},{10,2},{14,6},... | collective-permute-start | bytes 1179656 | tf_op jit(solution)/shard_map/ppermute | solution.py:116
  24.3 10.8 %collective-permute-start.9 = (bf16[64,3072]{1,0:T(8,128)(2,1)}, bf16[64,3072]{1,0:T(8,128)(2,1)S(1)}, u32[]{:S(2)}, u32[]{:S(2)}) collective-permute-start(bf16[64,3072]{1,0:T(8,128)(2,1)} %pad_maximum_fusion.8), channel_id=1, source_target_pairs={{16,0},{0,16},{17,1},{1,17},{18,2},{2,18},{19,3},{3,19},{20,4},{4,... | collective-permute-start | bytes 1179656 | tf_op jit(solution)/shard_map/ppermute | solution.py:116
  25.8 5.7 %collective-permute-start.1 = (bf16[8,6272]{1,0:T(8,128)(2,1)S(1)}, bf16[8,6272]{1,0:T(8,128)(2,1)S(1)}, u32[]{:S(2)}, u32[]{:S(2)}) collective-permute-start(bf16[8,6272]{1,0:T(8,128)(2,1)S(1)} %fusion.9), channel_id=1, source_target_pairs={{1,0},{2,1},{3,2},{0,3},{5,4},{6,5},{7,6},{4,7},{9,8},{10,9},{11,1... | collective-permute-start | bytes 301064 | tf_op jit(solution)/shard_map/ppermute | solution.py:112
  27.0 8.0 %collective-permute-start.2 = (bf16[8,6272]{1,0:T(8,128)(2,1)S(1)}, bf16[8,6272]{1,0:T(8,128)(2,1)S(1)}, u32[]{:S(2)}, u32[]{:S(2)}) collective-permute-start(bf16[8,6272]{1,0:T(8,128)(2,1)S(1)} %fusion.9), channel_id=1, source_target_pairs={{2,0},{3,1},{0,2},{1,3},{6,4},{7,5},{4,6},{5,7},{10,8},{11,9},{8,1... | collective-permute-start | bytes 301064 | tf_op jit(solution)/shard_map/ppermute | solution.py:112
  27.7 7.3 %collective-permute-start.3 = (bf16[8,6272]{1,0:T(8,128)(2,1)S(1)}, bf16[8,6272]{1,0:T(8,128)(2,1)}, u32[]{:S(2)}, u32[]{:S(2)}) collective-permute-start(bf16[8,6272]{1,0:T(8,128)(2,1)S(1)} %fusion.9), channel_id=1, source_target_pairs={{3,0},{0,1},{1,2},{2,3},{7,4},{4,5},{5,6},{6,7},{11,8},{8,9},{9,10... | collective-permute-start | bytes 301064 | tf_op jit(solution)/shard_map/ppermute | solution.py:112
  36.2 10.0 %collective-permute-start.15 = (bf16[128,3072]{1,0:T(8,128)(2,1)S(1)}, bf16[128,3072]{1,0:T(8,128)(2,1)S(1)}, u32[]{:S(2)}, u32[]{:S(2)}) collective-permute-start(bf16[128,3072]{1,0:T(8,128)(2,1)S(1)} %pad_maximum_fusion.4), channel_id=1, source_target_pairs={{4,0},{0,4},{12,8},{8,12},{5,1},{1,5},{13,9},{9,13},{6,2},{2,6},{1... | collective-permute-start | bytes 2359304 | tf_op jit(solution)/shard_map/ppermute | solution.py:116
  36.3 7.4 %collective-permute-start.12 = (bf16[32,3072]{1,0:T(8,128)(2,1)S(1)}, bf16[32,3072]{1,0:T(8,128)(2,1)S(1)}, u32[]{:S(2)}, u32[]{:S(2)}) collective-permute-start(bf16[32,3072]{1,0:T(8,128)(2,1)S(1)} %get-tuple-element.63), channel_id=1, source_target_pairs={{8,0},{12,4},{0,8},{4,12},{9,1},{13,5},{1,9},{5,13},{10,2},{14,6},... | collective-permute-start | bytes 589832 | tf_op jit(solution)/shard_map/ppermute | solution.py:116
  36.9 9.2 %collective-permute-start.14 = (bf16[128,3072]{1,0:T(8,128)(2,1)S(1)}, bf16[128,3072]{1,0:T(8,128)(2,1)S(1)}, u32[]{:S(2)}, u32[]{:S(2)}) collective-permute-start(bf16[128,3072]{1,0:T(8,128)(2,1)S(1)} %pad_maximum_fusion.3), channel_id=1, source_target_pairs={{4,0},{0,4},{12,8},{8,12},{5,1},{1,5},{13,9},{9,13},{6,2},{2,6},{1... | collective-permute-start | bytes 2359304 | tf_op jit(solution)/shard_map/ppermute | solution.py:116
  37.2 7.3 %collective-permute-start.10 = (bf16[32,3200]{1,0:T(8,128)(2,1)S(1)}, bf16[32,3200]{1,0:T(8,128)(2,1)S(1)}, u32[]{:S(2)}, u32[]{:S(2)}) collective-permute-start(bf16[32,3200]{1,0:T(8,128)(2,1)S(1)} %slice.74), channel_id=1, source_target_pairs={{16,0},{0,16},{17,1},{1,17},{18,2},{2,18},{19,3},{3,19},{20,4},{4,... | collective-permute-start | bytes 614408 | tf_op jit(solution)/shard_map/ppermute | solution.py:116
  43.7 13.2 %collective-permute-start.13 = (bf16[64,3072]{1,0:T(8,128)(2,1)S(1)}, bf16[64,3072]{1,0:T(8,128)(2,1)S(1)}, u32[]{:S(2)}, u32[]{:S(2)}) collective-permute-start(bf16[64,3072]{1,0:T(8,128)(2,1)S(1)} %pad_maximum_fusion.9), channel_id=1, source_target_pairs={{16,0},{0,16},{17,1},{1,17},{18,2},{2,18},{19,3},{3,19},{20,4},{4,... | collective-permute-start | bytes 1179656 | tf_op jit(solution)/shard_map/ppermute | solution.py:116
  44.5 12.4 %collective-permute-start.11 = (bf16[64,3200]{1,0:T(8,128)(2,1)S(1)}, bf16[64,3200]{1,0:T(8,128)(2,1)S(1)}, u32[]{:S(2)}, u32[]{:S(2)}) collective-permute-start(bf16[64,3200]{1,0:T(8,128)(2,1)S(1)} %pad_maximum_fusion.6), channel_id=1, source_target_pairs={{8,0},{12,4},{0,8},{4,12},{9,1},{13,5},{1,9},{5,13},{10,2},{14,6},... | collective-permute-start | bytes 1228808 | tf_op jit(solution)/shard_map/ppermute | solution.py:116
  57.0 2.4 %collective-permute-start.17 = (bf16[128,3072]{1,0:T(8,128)(2,1)S(1)}, bf16[128,3072]{1,0:T(8,128)(2,1)S(1)}, u32[]{:S(2)}, u32[]{:S(2)}) collective-permute-start(bf16[128,3072]{1,0:T(8,128)(2,1)S(1)} %pad_maximum_fusion.5), channel_id=1, source_target_pairs={{4,0},{0,4},{12,8},{8,12},{5,1},{1,5},{13,9},{9,13},{6,2},{2,6},{1... | collective-permute-start | bytes 2359304 | tf_op jit(solution)/shard_map/ppermute | solution.py:116
  57.1 3.4 %collective-permute-start.16 = (bf16[128,3200]{1,0:T(8,128)(2,1)S(1)}, bf16[128,3200]{1,0:T(8,128)(2,1)S(1)}, u32[]{:S(2)}, u32[]{:S(2)}) collective-permute-start(bf16[128,3200]{1,0:T(8,128)(2,1)S(1)} %pad_maximum_fusion.2), channel_id=1, source_target_pairs={{4,0},{0,4},{12,8},{8,12},{5,1},{1,5},{13,9},{9,13},{6,2},{2,6},{1... | collective-permute-start | bytes 2457608 | tf_op jit(solution)/shard_map/ppermute | solution.py:116
  76.1 2.4 %collective-permute-start.24 = (bf16[128,3072]{1,0:T(8,128)(2,1)S(1)}, bf16[128,3072]{1,0:T(8,128)(2,1)S(1)}, u32[]{:S(2)}, u32[]{:S(2)}) collective-permute-start(bf16[128,3072]{1,0:T(8,128)(2,1)S(1)} %get-tuple-element.49), channel_id=1, source_target_pairs={{4,0},{0,4},{12,8},{8,12},{5,1},{1,5},{13,9},{9,13},{6,2},{2,6},{1... | collective-permute-start | bytes 2359304 | tf_op jit(solution)/shard_map/ppermute | solution.py:116
  76.3 3.3 %collective-permute-start.18 = (bf16[128,3200]{1,0:T(8,128)(2,1)S(1)}, bf16[128,3200]{1,0:T(8,128)(2,1)S(1)}, u32[]{:S(2)}, u32[]{:S(2)}) collective-permute-start(bf16[128,3200]{1,0:T(8,128)(2,1)S(1)} %get-tuple-element.46), channel_id=1, source_target_pairs={{4,0},{0,4},{12,8},{8,12},{5,1},{1,5},{13,9},{9,13},{6,2},{2,6},{1... | collective-permute-start | bytes 2457608 | tf_op jit(solution)/shard_map/ppermute | solution.py:116
  78.8 11.2 %collective-permute-start.25 = (bf16[64,3072]{1,0:T(8,128)(2,1)S(1)}, bf16[64,3072]{1,0:T(8,128)(2,1)S(1)}, u32[]{:S(2)}, u32[]{:S(2)}) collective-permute-start(bf16[64,3072]{1,0:T(8,128)(2,1)S(1)} %pad_maximum_fusion.10), channel_id=1, source_target_pairs={{16,0},{0,16},{17,1},{1,17},{18,2},{2,18},{19,3},{3,19},{20,4},{4,... | collective-permute-start | bytes 1179656 | tf_op jit(solution)/shard_map/ppermute | solution.py:116
  79.8 11.6 %collective-permute-start.19 = (bf16[64,3200]{1,0:T(8,128)(2,1)S(1)}, bf16[64,3200]{1,0:T(8,128)(2,1)S(1)}, u32[]{:S(2)}, u32[]{:S(2)}) collective-permute-start(bf16[64,3200]{1,0:T(8,128)(2,1)S(1)} %concatenate.79), channel_id=1, source_target_pairs={{8,0},{12,4},{0,8},{4,12},{9,1},{13,5},{1,9},{5,13},{10,2},{14,6},... | collective-permute-start | bytes 1228808 | tf_op jit(solution)/shard_map/ppermute | solution.py:116
  90.1 6.2 %collective-permute-start.26 = (bf16[32,3072]{1,0:T(8,128)(2,1)S(1)}, bf16[32,3072]{1,0:T(8,128)(2,1)S(1)}, u32[]{:S(2)}, u32[]{:S(2)}) collective-permute-start(bf16[32,3072]{1,0:T(8,128)(2,1)S(1)} %fusion.2), channel_id=1, source_target_pairs={{8,0},{12,4},{0,8},{4,12},{9,1},{13,5},{1,9},{5,13},{10,2},{14,6},... | collective-permute-start | bytes 589832 | tf_op jit(solution)/shard_map/ppermute | solution.py:116
  91.5 9.5 %collective-permute-start.20 = (bf16[32,3200]{1,0:T(8,128)(2,1)S(1)}, bf16[32,3200]{1,0:T(8,128)(2,1)S(1)}, u32[]{:S(2)}, u32[]{:S(2)}) collective-permute-start(bf16[32,3200]{1,0:T(8,128)(2,1)S(1)} %fusion), channel_id=1, source_target_pairs={{16,0},{0,16},{17,1},{1,17},{18,2},{2,18},{19,3},{3,19},{20,4},{4,... | collective-permute-start | bytes 614408 | tf_op jit(solution)/shard_map/ppermute | solution.py:116
  96.3 11.5 %copy-start.1 = (s32[8]{0:T(128)S(1)}, s32[8]{0:T(128)}, u32[]{:S(2)}) copy-start(s32[8]{0:T(128)} %param.10) | copy-start | bytes 100
  96.4 6.1 %collective-permute-start.27 = (bf16[8,3072]{1,0:T(8,128)(2,1)S(1)}, bf16[8,3072]{1,0:T(8,128)(2,1)S(1)}, u32[]{:S(2)}, u32[]{:S(2)}) collective-permute-start(bf16[8,3072]{1,0:T(8,128)(2,1)S(1)} %get-tuple-element.76), channel_id=1, source_target_pairs={{3,0},{0,1},{1,2},{2,3},{7,4},{4,5},{5,6},{6,7},{11,8},{8,9},{9,10... | collective-permute-start | bytes 147464 | tf_op jit(solution)/shard_map/ppermute | solution.py:112
  96.4 8.9 %collective-permute-start.28 = (bf16[8,3072]{1,0:T(8,128)(2,1)S(1)}, bf16[8,3072]{1,0:T(8,128)(2,1)S(1)}, u32[]{:S(2)}, u32[]{:S(2)}) collective-permute-start(bf16[8,3072]{1,0:T(8,128)(2,1)S(1)} %get-tuple-element.78), channel_id=1, source_target_pairs={{2,0},{3,1},{0,2},{1,3},{6,4},{7,5},{4,6},{5,7},{10,8},{11,9},{8,1... | collective-permute-start | bytes 147464 | tf_op jit(solution)/shard_map/ppermute | solution.py:112
  98.3 7.0 %collective-permute-start.29 = (bf16[8,3072]{1,0:T(8,128)(2,1)S(1)}, bf16[8,3072]{1,0:T(8,128)(2,1)S(1)}, u32[]{:S(2)}, u32[]{:S(2)}) collective-permute-start(bf16[8,3072]{1,0:T(8,128)(2,1)S(1)} %get-tuple-element.77), channel_id=1, source_target_pairs={{1,0},{2,1},{3,2},{0,3},{5,4},{6,5},{7,6},{4,7},{9,8},{10,9},{11,1... | collective-permute-start | bytes 147464 | tf_op jit(solution)/shard_map/ppermute | solution.py:112
  101.1 6.0 %collective-permute-start.21 = (bf16[8,3200]{1,0:T(8,128)(2,1)S(1)}, bf16[8,3200]{1,0:T(8,128)(2,1)S(1)}, u32[]{:S(2)}, u32[]{:S(2)}) collective-permute-start(bf16[8,3200]{1,0:T(8,128)(2,1)S(1)} %get-tuple-element.73), channel_id=1, source_target_pairs={{3,0},{0,1},{1,2},{2,3},{7,4},{4,5},{5,6},{6,7},{11,8},{8,9},{9,10... | collective-permute-start | bytes 153608 | tf_op jit(solution)/shard_map/ppermute | solution.py:112
  101.1 5.9 %collective-permute-start.22 = (bf16[8,3200]{1,0:T(8,128)(2,1)S(1)}, bf16[8,3200]{1,0:T(8,128)(2,1)S(1)}, u32[]{:S(2)}, u32[]{:S(2)}) collective-permute-start(bf16[8,3200]{1,0:T(8,128)(2,1)S(1)} %get-tuple-element.75), channel_id=1, source_target_pairs={{2,0},{3,1},{0,2},{1,3},{6,4},{7,5},{4,6},{5,7},{10,8},{11,9},{8,1... | collective-permute-start | bytes 153608 | tf_op jit(solution)/shard_map/ppermute | solution.py:112
  102.5 5.1 %collective-permute-start.23 = (bf16[8,3200]{1,0:T(8,128)(2,1)S(1)}, bf16[8,3200]{1,0:T(8,128)(2,1)S(1)}, u32[]{:S(2)}, u32[]{:S(2)}) collective-permute-start(bf16[8,3200]{1,0:T(8,128)(2,1)S(1)} %get-tuple-element.74), channel_id=1, source_target_pairs={{1,0},{2,1},{3,2},{0,3},{5,4},{6,5},{7,6},{4,7},{9,8},{10,9},{11,1... | collective-permute-start | bytes 153608 | tf_op jit(solution)/shard_map/ppermute | solution.py:112

commit v5 on v4

--- a/solution.py
+++ b/solution.py
@@ -128,6 +128,10 @@
     return swap(value, "expert", 1)
 
 
+def after_others(values, others):
+    return lax.optimization_barrier((values, others))[0]
+
+
 def gather_z(rows):
     return [rows] + [shift(rows, "mp", k) for k in range(1, lax.axis_size("mp"))]
 
@@ -149,13 +153,26 @@
     return tuple(jnp.concatenate([mine, swap_core(mine)], axis=0) for mine in (low, high))
 
 
-def scatter_half(kept, sent, first, second):
-    total = kept + swap_core(sent).astype(jnp.float32)
-    own, by_x, by_y, by_both = jnp.split(total, 4, axis=0)
-    near, far = (by_x, [by_y, by_both]) if first is swap_x else (by_y, [by_x, by_both])
-    rest = second(jnp.concatenate(far, axis=0).astype(jnp.bfloat16)).astype(jnp.float32)
-    rest_own, rest_near = jnp.split(rest, 2, axis=0)
-    return own + rest_own + first((near + rest_near).astype(jnp.bfloat16)).astype(jnp.float32)
+def scatter_core(kept, sent):
+    return kept + swap_core(sent).astype(jnp.float32)
+
+
+def send(value, exchange):
+    return exchange(value.astype(jnp.bfloat16)).astype(jnp.float32)
+
+
+def scatter_far(total, cut):
+    low, low_x, low_y, low_both = jnp.split(total[:, :cut], 4, axis=0)
+    high, high_x, high_y, high_both = jnp.split(total[:, cut:], 4, axis=0)
+    low_far = send(jnp.concatenate([low_y, low_both], axis=0), swap_y)
+    high_far = send(jnp.concatenate([high_x, high_both], axis=0), swap_x)
+    return jnp.concatenate([low, low_x], axis=0) + low_far, jnp.concatenate([high, high_y], axis=0) + high_far
+
+
+def scatter_near(low, high):
+    low, low_x = jnp.split(low, 2, axis=0)
+    high, high_y = jnp.split(high, 2, axis=0)
+    return jnp.concatenate([low + send(low_x, swap_x), high + send(high_y, swap_y)], axis=1)
 
 
 def scatter_z(total):
@@ -163,7 +180,7 @@
     rows = total.shape[0] // size
     result = total[:rows]
     for k in range(1, size):
-        result = result + shift(total[k * rows:(k + 1) * rows].astype(jnp.bfloat16), "mp", size - k).astype(jnp.float32)
+        result = result + send(total[k * rows:(k + 1) * rows], lambda value: shift(value, "mp", size - k))
     return result
 
 
@@ -179,57 +196,59 @@
     return pltpu.with_memory_space_constraint(value, pltpu.HBM)
 
 
-def token_kernel(low, high, gate_weight, up_weight, pre_gate, pre_up, gate_copy, up_copy, gate_sems, up_sems):
-    half = low.shape[1]
-    depth = part_of(half, TOKEN_PART)
-    steps = half // depth
+def token_kernel(first, tokens, gate_weight, up_weight, *refs):
+    before, (pre_gate, pre_up, gate_copy, up_copy, gate_sems, up_sems) = refs[:-6], refs[-6:]
+    width = tokens.shape[1]
+    depth = part_of(width, TOKEN_PART)
+    steps = width // depth
 
     def copies(index):
+        source = pl.ds(pl.multiple_of(first + index * depth, depth), depth)
         rows = pl.ds(pl.multiple_of(index * depth, depth), depth)
         return (
-            pltpu.make_async_copy(gate_weight.at[0, rows], gate_copy.at[rows], gate_sems.at[index]),
-            pltpu.make_async_copy(up_weight.at[0, rows], up_copy.at[rows], up_sems.at[index]),
+            pltpu.make_async_copy(gate_weight.at[0, source], gate_copy.at[rows], gate_sems.at[index]),
+            pltpu.make_async_copy(up_weight.at[0, source], up_copy.at[rows], up_sems.at[index]),
         )
 
-    @pl.loop(0, 2 * steps)
+    @pl.loop(0, steps)
     def _(index):
         for copy in copies(index):
             copy.start()
 
-    pre_gate[...] = jnp.zeros_like(pre_gate)
-    pre_up[...] = jnp.zeros_like(pre_up)
-    for first, part in ((0, low), (steps, high)):
-
-        @pl.loop(0, steps)
-        def _(step):
-            for copy in copies(first + step):
-                copy.wait()
-            rows = pl.ds(pl.multiple_of((first + step) * depth, depth), depth)
-            values = part[:, pl.ds(pl.multiple_of(step * depth, depth), depth)]
-            pre_gate[...] += product(values, gate_copy[rows, :], 0)
-            pre_up[...] += product(values, up_copy[rows, :], 0)
-
-
-def multiply_tokens(low, high, gate_weight, up_weight):
-    rows, half = low.shape
-    width, hidden = gate_weight.shape[1:]
-    steps = width // part_of(half, TOKEN_PART)
+    pre_gate[...] = before[0][...] if before else jnp.zeros_like(pre_gate)
+    pre_up[...] = before[1][...] if before else jnp.zeros_like(pre_up)
+
+    @pl.loop(0, steps)
+    def _(step):
+        for copy in copies(step):
+            copy.wait()
+        rows = pl.ds(pl.multiple_of(step * depth, depth), depth)
+        pre_gate[...] += product(tokens[:, rows], gate_copy[rows, :], 0)
+        pre_up[...] += product(tokens[:, rows], up_copy[rows, :], 0)
+
+
+def multiply_tokens(first, tokens, gate_weight, up_weight, *before):
+    rows, width = tokens.shape
+    hidden = gate_weight.shape[2]
+    steps = width // part_of(width, TOKEN_PART)
     return pl.pallas_call(
-        token_kernel,
+        functools.partial(token_kernel, first),
         out_shape=(
             pltpu.VMEM((rows, hidden), jnp.float32),
             pltpu.VMEM((rows, hidden), jnp.float32),
             pltpu.VMEM((width, hidden), jnp.bfloat16),
             pltpu.VMEM((width, hidden), jnp.bfloat16),
         ),
-        in_specs=[pl.BlockSpec(memory_space=pltpu.VMEM)] * 2 + [pl.BlockSpec(memory_space=pl.ANY)] * 2,
+        in_specs=[pl.BlockSpec(memory_space=pltpu.VMEM)]
+        + [pl.BlockSpec(memory_space=pl.ANY)] * 2
+        + [pl.BlockSpec(memory_space=pltpu.VMEM)] * len(before),
         out_specs=(pl.BlockSpec(memory_space=pltpu.VMEM),) * 4,
         scratch_shapes=[pltpu.SemaphoreType.DMA((steps,)), pltpu.SemaphoreType.DMA((steps,))],
         compiler_params=pltpu.CompilerParams(vmem_limit_bytes=TOKEN_VMEM),
         cost_estimate=pl.CostEstimate(
             flops=4 * rows * width * hidden, bytes_accessed=4 * width * hidden, transcendentals=0
         ),
-    )(low, high, in_hbm(gate_weight), in_hbm(up_weight))
+    )(tokens, in_hbm(gate_weight), in_hbm(up_weight), *before)
 
 
 def grad_kernel(
@@ -300,7 +319,7 @@
     )(expert, low, high, pre_gate, pre_up, in_hbm(down_weight))
 
 
-def output_kernel(first, grad_gate, grad_up, gate_copy, up_copy, *refs):
+def output_kernel(grad_gate, grad_up, gate_copy, up_copy, *refs):
     dots, kept, sent = refs if len(refs) == 3 else (None,) + refs
     rows = kept.shape[0]
     columns = kept.shape[1] - (0 if dots is None else dots.shape[1])
@@ -308,22 +327,22 @@
 
     @pl.loop(0, columns // part)
     def _(step):
-        span = pl.ds(pl.multiple_of(first + step * part, part), part)
-        place = pl.ds(pl.multiple_of(step * part, part), part)
+        span = pl.ds(pl.multiple_of(step * part, part), part)
         result = product(grad_gate[...], gate_copy[span, :], 1) + product(grad_up[...], up_copy[span, :], 1)
-        kept[:, place] = result[:rows]
-        sent[:, place] = result[rows:].astype(jnp.bfloat16)
+        kept[:, span] = result[:rows]
+        sent[:, span] = result[rows:].astype(jnp.bfloat16)
 
     if dots is not None:
         kept[:, columns:] = dots[:rows, :].astype(jnp.float32)
         sent[:, columns:] = dots[rows:, :]
 
 
-def multiply_outputs(first, columns, grad_gate, grad_up, gate_copy, up_copy, *dots):
+def multiply_outputs(grad_gate, grad_up, gate_copy, up_copy, *dots):
     rows, hidden = grad_gate.shape
+    columns = gate_copy.shape[0]
     total = columns + sum(value.shape[1] for value in dots)
     return pl.pallas_call(
-        functools.partial(output_kernel, first),
+        output_kernel,
         out_shape=(
             pltpu.VMEM((rows // 2, total), jnp.float32),
             pltpu.VMEM((rows // 2, total), jnp.bfloat16),
@@ -354,26 +373,29 @@
     gate_second = jax.nn.sigmoid(second_logit - first_logit)
     gate_table = (first_hot * gate_first[:, None] + second_hot * gate_second[:, None]) * keep_rows[:, None]
     gate_table = jnp.pad(gate_table.astype(jnp.bfloat16), ((0, 0), (0, table - expert_count)))
-    grad_rows, token_z[1] = lax.optimization_barrier((jnp.concatenate([gate_table, out_grad], axis=1), token_z[1]))
-    grad_z = gather_z(grad_rows)
+    grad_z = gather_z(after_others(jnp.concatenate([gate_table, out_grad], axis=1), token_z[1]))
     token_near = gather_near(token_z, half)
-    token_far = gather_far(*token_near)
-    grad_z, token_far = lax.optimization_barrier((grad_z, token_far))
-    grad_near = gather_near(grad_z, half + table)
-    token_halves = gather_core(token_near[0], token_far[0], token_near[1], token_far[1])
-    grad_far = gather_far(*grad_near)
-    pre_gate, pre_up, gate_copy, up_copy = multiply_tokens(*token_halves, gate_weight, up_weight)
-    grad_far, pre_gate = lax.optimization_barrier((grad_far, pre_gate))
+    token_far = gather_far(*after_others(token_near, grad_z[1]))
+    grad_near = gather_near(after_others(grad_z, token_far), half + table)
+    token_low, token_high = gather_core(token_near[0], token_far[0], token_near[1], token_far[1])
+    before = multiply_tokens(0, token_low, gate_weight, up_weight)
+    grad_far = gather_far(*after_others(grad_near, before[0]))
+    after = multiply_tokens(half, token_high, gate_weight, up_weight, before[0], before[1])
+    grad_far = after_others(grad_far, after[0])
     grad_halves = gather_core(grad_near[0], grad_far[0], grad_near[1], grad_far[1])
     expert = lax.axis_index("expert").astype(jnp.int32).reshape(1)
-    grad_gate, grad_up, dots = multiply_grads(expert, *grad_halves, pre_gate, pre_up, down_weight)
-    kept, sent = multiply_outputs(0, half, grad_gate, grad_up, gate_copy, up_copy, dots)
-    sent, grad_gate = lax.optimization_barrier((sent, grad_gate))
-    low = scatter_z(scatter_half(kept, sent, swap_x, swap_y))
-    kept, sent = multiply_outputs(half, half, grad_gate, grad_up, gate_copy, up_copy)
-    high = scatter_z(scatter_half(kept, sent, swap_y, swap_x))
-    expert_sum = jnp.concatenate([low[:, :half], high], axis=1)
-    dot_table = low[:, half:half + expert_count]
+    grad_gate, grad_up, dots = multiply_grads(expert, *grad_halves, after[0], after[1], down_weight)
+    kept, sent = multiply_outputs(grad_gate, grad_up, before[2], before[3], dots)
+    chunk = scatter_core(kept, sent)
+    kept, sent = multiply_outputs(grad_gate, grad_up, after[2], after[3])
+    chunk = scatter_far(after_others(chunk, sent), half // 2)
+    later = scatter_core(kept, sent)
+    chunk = scatter_near(*after_others(chunk, later))
+    later = scatter_far(later, half // 2)
+    chunk = scatter_z(after_others(chunk, later))
+    later = scatter_z(scatter_near(*later))
+    expert_sum = jnp.concatenate([chunk[:, :half], later], axis=1)
+    dot_table = chunk[:, half:half + expert_count]
     dot_first = jnp.sum(dot_table * first_hot, axis=1)
     dot_second = jnp.sum(dot_table * second_hot, axis=1)
     product = gate_first * gate_second * keep_rows

time: 110 us -> 107 us (0.973)
  waiting for transfers between devices: 38.7 us -> 27.1 us
  starting transfers between devices: 33.2 us -> 41 us
  Pallas kernels: 26 us -> 27.6 us
    ppermute x18 -> x22, waiting for transfers between devices: 27.8 us -> 12.9 us  [swap(): lax.ppermute(value, axis, [(i ^ bit, i) for i in range(lax.axis_size(axis...]
    ppermute x18 -> x22, starting transfers between devices: 14.2 us -> 20.8 us  [swap(): lax.ppermute(value, axis, [(i ^ bit, i) for i in range(lax.axis_size(axis...]
    ppermute x12, waiting for transfers between devices: 10.9 us -> 14.2 us  [shift(): lax.ppermute(value, axis, [((i + step) % size, i) for i in range(size)])]
    pallas_call x3 -> x4, Pallas kernels: 19.5 us -> 21 us  [the longest x2 12.1 us: multiply_tokens(): pl.pallas_call(functools.partial(token_kernel, first), out_shape=(pltpu.V...]
    ppermute x12, starting transfers between devices: 19 us -> 20.3 us  [shift(): lax.ppermute(value, axis, [((i + step) % size, i) for i in range(size)])]
  transfers between devices with their start and end apart: 30 -> 34, of which waited for: 15 -> 14; matrix products, arithmetic and copies ran while one was open for 7% -> 6% of each run, Pallas kernels for 10% -> 15%
where the time goes in v5:
time: 107 us
  starting transfers between devices  41 us (38%)
  Pallas kernels  27.6 us (26%)
  waiting for transfers between devices  27.1 us (25%)
  other arithmetic  4.51 us (4%)
  local copies, waits for them, and re-layouts  3.23 us (3%)
  matrix products  2.15 us (2%)
  between operations  1.16 us (1%)
    ppermute x22, starting transfers between devices, swap(): lax.ppermute(value, axis, [(i ^ bit, i) for i in range(lax.axis_size(axis...  20.8 us
    ppermute x12, starting transfers between devices, shift(): lax.ppermute(value, axis, [((i + step) % size, i) for i in range(size)])  20.3 us
    ppermute x12, waiting for transfers between devices, shift(): lax.ppermute(value, axis, [((i + step) % size, i) for i in range(size)])  14.2 us
    ppermute x22, waiting for transfers between devices, swap(): lax.ppermute(value, axis, [(i ^ bit, i) for i in range(lax.axis_size(axis...  12.9 us
    pallas_call x2, Pallas kernels, multiply_tokens(): pl.pallas_call(functools.partial(token_kernel, first), out_shape=(pltpu.V...  12.1 us
    pallas_call x2, Pallas kernels, multiply_outputs(): pl.pallas_call(output_kernel, out_shape=(pltpu.VMEM((rows // 2, total), j...  8.98 us
    pallas_call x1, Pallas kernels, multiply_grads(): pl.pallas_call(grad_kernel, out_shape=(pltpu.VMEM((rows, hidden), jnp.bfl...  6.56 us
  transfers between devices with their start and end apart: 34, of which 14 were waited for; matrix products, arithmetic and copies ran while one was open for 6% of the time, Pallas kernels for 15%

profile of v5, /device:TPU:0, one launch (start us, length us, event | category | flops | bytes accessed | tf_op | source)
XLA Modules:
  0.0 106.8 jit_solution(13769076616092860290)
XLA Ops:
  0.7 5.1 %collective-permute-start = (bf16[8,6144]{1,0:T(8,128)(2,1)}, bf16[8,6144]{1,0:T(8,128)(2,1)S(1)}, u32[]{:S(2)}, u32[]{:S(2)}) collective-permute-start(bf16[8,6144]{1,0:T(8,128)(2,1)} %param.8), channel_id=1, source_target_pairs={{1,0},{2,1},{3,2},{0,3},{5,4},{6,5},{7,6},{4,7},{9,8},{10,9},{11,1... | collective-permute-start | bytes 294920 | tf_op jit(solution)/shard_map/ppermute | solution.py:112
  5.8 1.0 collective-permute-start.5
  6.8 0.9 constant_dynamic-update-slice_fusion.3
  7.7 0.8 slice_bitcast_fusion
  8.5 0.7 convert_element_type.76
  9.1 1.2 %select_reduce_fusion.3 = (f32[8]{0:T(128)S(1)}, f32[8]{0:T(128)S(1)}) fusion(s32[8]{0:T(128)S(1)} %get-tuple-element.106, s32[8]{0:T(128)S(1)} %get-tuple-element.105, bf16[8,6144]{1,0:T(8,128)(2,1)} %param.8, bf16[6144,4]{0,1:T(4,128)(2,1)S(1)} %copy-done), kind=kOutput, calls=%fused_computation.69 | convolution fusion | flops 393392 | bytes 147584 | tf_op jit(solution)/shard_map/dot_general | solution.py:369
  10.5 4.3 %collective-permute-done.4 = bf16[8,6144]{1,0:T(8,128)(2,1)S(1)} collective-permute-done((bf16[8,6144]{1,0:T(8,128)(2,1)}, bf16[8,6144]{1,0:T(8,128)(2,1)S(1)}, u32[]{:S(2)}, u32[]{:S(2)}) %collective-permute-start.4) | collective-permute-done | bytes 98336 | tf_op jit(solution)/shard_map/ppermute | solution.py:112
  14.8 1.6 %collective-permute-start.6 = (bf16[32,3072]{1,0:T(8,128)(2,1)S(1)}, bf16[32,3072]{1,0:T(8,128)(2,1)S(1)}, u32[]{:S(2)}, u32[]{:S(2)}) collective-permute-start(bf16[32,3072]{1,0:T(8,128)(2,1)S(1)} %get-tuple-element.37), channel_id=1, source_target_pairs={{16,0},{0,16},{17,1},{1,17},{18,2},{2,18},{19,3},{3,19},{20,4},{4,... | collective-permute-start | bytes 589832 | tf_op jit(solution)/shard_map/ppermute | solution.py:116
  16.4 1.5 %collective-permute-start.7 = (bf16[32,3072]{1,0:T(8,128)(2,1)S(1)}, bf16[32,3072]{1,0:T(8,128)(2,1)S(1)}, u32[]{:S(2)}, u32[]{:S(2)}) collective-permute-start(bf16[32,3072]{1,0:T(8,128)(2,1)S(1)} %get-tuple-element.39), channel_id=1, source_target_pairs={{8,0},{12,4},{0,8},{4,12},{9,1},{13,5},{1,9},{5,13},{10,2},{14,6},... | collective-permute-start | bytes 589832 | tf_op jit(solution)/shard_map/ppermute | solution.py:116
  17.9 2.0 %collective-permute-start.1 = (bf16[8,6272]{1,0:T(8,128)(2,1)S(1)}, bf16[8,6272]{1,0:T(8,128)(2,1)S(1)}, u32[]{:S(2)}, u32[]{:S(2)}) collective-permute-start(bf16[8,6272]{1,0:T(8,128)(2,1)S(1)} %fusion.4), channel_id=1, source_target_pairs={{1,0},{2,1},{3,2},{0,3},{5,4},{6,5},{7,6},{4,7},{9,8},{10,9},{11,1... | collective-permute-start | bytes 301064 | tf_op jit(solution)/shard_map/ppermute | solution.py:112
  19.9 2.7 %collective-permute-done.1 = bf16[8,6272]{1,0:T(8,128)(2,1)S(1)} collective-permute-done((bf16[8,6272]{1,0:T(8,128)(2,1)S(1)}, bf16[8,6272]{1,0:T(8,128)(2,1)S(1)}, u32[]{:S(2)}, u32[]{:S(2)}) %collective-permute-start.1) | collective-permute-done | bytes 100384 | tf_op jit(solution)/shard_map/ppermute | solution.py:112
  22.6 0.8 pad_maximum_fusion.10
  23.9 0.8 pad_maximum_fusion.9
  24.7 1.3 %collective-permute-start.8 = (bf16[64,3072]{1,0:T(8,128)(2,1)}, bf16[64,3072]{1,0:T(8,128)(2,1)S(1)}, u32[]{:S(2)}, u32[]{:S(2)}) collective-permute-start(bf16[64,3072]{1,0:T(8,128)(2,1)} %pad_maximum_fusion.9), channel_id=1, source_target_pairs={{8,0},{12,4},{0,8},{4,12},{9,1},{13,5},{1,9},{5,13},{10,2},{14,6},... | collective-permute-start | bytes 1179656 | tf_op jit(solution)/shard_map/ppermute | solution.py:116
  26.0 2.0 %collective-permute-start.2 = (bf16[8,6272]{1,0:T(8,128)(2,1)S(1)}, bf16[8,6272]{1,0:T(8,128)(2,1)S(1)}, u32[]{:S(2)}, u32[]{:S(2)}) collective-permute-start(bf16[8,6272]{1,0:T(8,128)(2,1)S(1)} %fusion.4), channel_id=1, source_target_pairs={{2,0},{3,1},{0,2},{1,3},{6,4},{7,5},{4,6},{5,7},{10,8},{11,9},{8,1... | collective-permute-start | bytes 301064 | tf_op jit(solution)/shard_map/ppermute | solution.py:112
  28.0 1.5 %collective-permute-start.3 = (bf16[8,6272]{1,0:T(8,128)(2,1)S(1)}, bf16[8,6272]{1,0:T(8,128)(2,1)}, u32[]{:S(2)}, u32[]{:S(2)}) collective-permute-start(bf16[8,6272]{1,0:T(8,128)(2,1)S(1)} %fusion.4), channel_id=1, source_target_pairs={{3,0},{0,1},{1,2},{2,3},{7,4},{4,5},{5,6},{6,7},{11,8},{8,9},{9,10... | collective-permute-start | bytes 301064 | tf_op jit(solution)/shard_map/ppermute | solution.py:112
  29.5 3.3 %collective-permute-done.2 = bf16[8,6272]{1,0:T(8,128)(2,1)S(1)} collective-permute-done((bf16[8,6272]{1,0:T(8,128)(2,1)S(1)}, bf16[8,6272]{1,0:T(8,128)(2,1)S(1)}, u32[]{:S(2)}, u32[]{:S(2)}) %collective-permute-start.2) | collective-permute-done | bytes 100384 | tf_op jit(solution)/shard_map/ppermute | solution.py:112
  32.8 1.7 %collective-permute-done.3 = bf16[8,6272]{1,0:T(8,128)(2,1)} collective-permute-done((bf16[8,6272]{1,0:T(8,128)(2,1)S(1)}, bf16[8,6272]{1,0:T(8,128)(2,1)}, u32[]{:S(2)}, u32[]{:S(2)}) %collective-permute-start.3) | collective-permute-done | bytes 100384 | tf_op jit(solution)/shard_map/ppermute | solution.py:112
  34.6 0.9 constant_dynamic-update-slice_fusion.4
  36.4 1.0 collective-permute-start.11
  37.4 1.5 %collective-permute-start.10 = (bf16[32,3200]{1,0:T(8,128)(2,1)S(1)}, bf16[32,3200]{1,0:T(8,128)(2,1)S(1)}, u32[]{:S(2)}, u32[]{:S(2)}) collective-permute-start(bf16[32,3200]{1,0:T(8,128)(2,1)S(1)} %slice.98), channel_id=1, source_target_pairs={{16,0},{0,16},{17,1},{1,17},{18,2},{2,18},{19,3},{3,19},{20,4},{4,... | collective-permute-start | bytes 614408 | tf_op jit(solution)/shard_map/ppermute | solution.py:116
  39.3 6.0 %shard_map.95 = (f32[256,1024]{1,0:T(8,128)S(1)}, f32[256,1024]{1,0:T(8,128)S(1)}, bf16[3072,1024]{1,0:T(8,128)(2,1)S(1)}, bf16[3072,1024]{1,0:T(8,128)(2,1)S(1)}) custom-call(bf16[256,3072]{1,0:T(8,128)(2,1)S(1)} %pad_maximum_fusion.1.tokens, bf16[1,6144,1024]{2,1,0:T(8,128)(2,1)} %gate_weight.3, bf16[1,6144,1024]{2,1,0:T(8,128)(2,1)} %up_weight.3), custom_call_target="tpu_custom_call" | custom-call | flops 3221225472 | bytes 12582912 | tf_op jit(solution)/shard_map/pallas_call | solution.py:234
  45.3 1.6 %collective-permute-start.14 = (bf16[64,3072]{1,0:T(8,128)(2,1)S(1)}, bf16[64,3072]{1,0:T(8,128)(2,1)S(1)}, u32[]{:S(2)}, u32[]{:S(2)}) collective-permute-start(bf16[64,3072]{1,0:T(8,128)(2,1)S(1)} %pad_maximum_fusion.11), channel_id=1, source_target_pairs={{16,0},{0,16},{17,1},{1,17},{18,2},{2,18},{19,3},{3,19},{20,4},{4,... | collective-permute-start | bytes 1179656 | tf_op jit(solution)/shard_map/ppermute | solution.py:116
  46.9 1.0 collective-permute-start.13
  48.0 6.1 %shard_map.96 = (f32[256,1024]{1,0:T(8,128)S(1)}, f32[256,1024]{1,0:T(8,128)S(1)}, bf16[3072,1024]{1,0:T(8,128)(2,1)S(1)}, bf16[3072,1024]{1,0:T(8,128)(2,1)S(1)}) custom-call(bf16[256,3072]{1,0:T(8,128)(2,1)S(1)} %constant_dynamic-update-slice_fusion.8.tokens, bf16[1,6144,1024]{2,1,0:T(8,128)(2,1)} %gate_weight.3, bf16[1,6144,1024]{2,1,0:T(8,128)(2,1)} %up_weight.3, ...), custom_call_target="tpu_custom_call" | custom-call | flops 3221225472 | bytes 12582912 | tf_op jit(solution)/shard_map/pallas_call | solution.py:234
  54.1 2.4 %collective-permute-done.14 = bf16[64,3072]{1,0:T(8,128)(2,1)S(1)} collective-permute-done((bf16[64,3072]{1,0:T(8,128)(2,1)S(1)}, bf16[64,3072]{1,0:T(8,128)(2,1)S(1)}, u32[]{:S(2)}, u32[]{:S(2)}) %collective-permute-start.14) | collective-permute-done | bytes 393248 | tf_op jit(solution)/shard_map/ppermute | solution.py:116
  56.5 1.7 %collective-permute-done.13 = bf16[64,3200]{1,0:T(8,128)(2,1)S(1)} collective-permute-done((bf16[64,3200]{1,0:T(8,128)(2,1)S(1)}, bf16[64,3200]{1,0:T(8,128)(2,1)S(1)}, u32[]{:S(2)}, u32[]{:S(2)}) %collective-permute-start.13) | collective-permute-done | bytes 409632 | tf_op jit(solution)/shard_map/ppermute | solution.py:116
  59.0 1.6 %collective-permute-done.17 = bf16[128,3072]{1,0:T(8,128)(2,1)S(1)} collective-permute-done((bf16[128,3072]{1,0:T(8,128)(2,1)S(1)}, bf16[128,3072]{1,0:T(8,128)(2,1)S(1)}, u32[]{:S(2)}, u32[]{:S(2)}) %collective-permute-start.17) | collective-permute-done | bytes 786464 | tf_op jit(solution)/shard_map/ppermute | solution.py:116
  60.7 1.1 %collective-permute-done.16 = bf16[128,3200]{1,0:T(8,128)(2,1)S(1)} collective-permute-done((bf16[128,3200]{1,0:T(8,128)(2,1)S(1)}, bf16[128,3200]{1,0:T(8,128)(2,1)S(1)}, u32[]{:S(2)}, u32[]{:S(2)}) %collective-permute-start.16) | collective-permute-done | bytes 819232 | tf_op jit(solution)/shard_map/ppermute | solution.py:116
  61.9 6.6 %shard_map.97 = (bf16[256,1024]{1,0:T(8,128)(2,1)S(1)}, bf16[256,1024]{1,0:T(8,128)(2,1)S(1)}, bf16[256,128]{1,0:T(8,128)(2,1)S(1)}) custom-call(s32[1]{0:T(128)} %bitcast.expert, bf16[256,3200]{1,0:T(8,128)(2,1)S(1)} %pad_maximum_fusion.low, bf16[256,3072]{1,0:T(8,128)(2,1)S(1)} %constant_dynamic-update-slice_fusion.13.high, ...), custom_call_target="tpu_custom_call" | custom-call | flops 3221225472 | bytes 12582912 | tf_op jit(solution)/shard_map/pallas_call | solution.py:298
  68.5 4.5 %shard_map.99 = (f32[128,3072]{1,0:T(8,128)S(1)}, bf16[128,3072]{1,0:T(8,128)(2,1)S(1)}) custom-call(bf16[256,1024]{1,0:T(8,128)(2,1)S(1)} %get-tuple-element.55.grad_gate, bf16[256,1024]{1,0:T(8,128)(2,1)S(1)} %get-tuple-element.56.grad_up, bf16[3072,1024]{1,0:T(8,128)(2,1)S(1)} %get-tuple-element.62.gate_copy, bf16[3072,1024]{1,0:T(8,128)(2,1)S(1)} %get-tuple-element.63.up_copy), custom_call_target="tpu_custom_call" | custom-call | flops 3221225472 | bytes 3145728 | tf_op jit(solution)/shard_map/pallas_call | solution.py:344
  73.2 4.5 %shard_map.98 = (f32[128,3200]{1,0:T(8,128)S(1)}, bf16[128,3200]{1,0:T(8,128)(2,1)S(1)}) custom-call(bf16[256,1024]{1,0:T(8,128)(2,1)S(1)} %get-tuple-element.55.grad_gate, bf16[256,1024]{1,0:T(8,128)(2,1)S(1)} %get-tuple-element.56.grad_up, bf16[3072,1024]{1,0:T(8,128)(2,1)S(1)} %get-tuple-element.57.gate_copy, ...), custom_call_target="tpu_custom_call" | custom-call | flops 3221225472 | bytes 3145728 | tf_op jit(solution)/shard_map/pallas_call | solution.py:344
  78.5 0.6 collective-permute-start.25
  79.1 1.0 collective-permute-start.24
  80.5 1.5 %collective-permute-start.20 = (bf16[64,1664]{1,0:T(8,128)(2,1)S(1)}, bf16[64,1664]{1,0:T(8,128)(2,1)S(1)}, u32[]{:S(2)}, u32[]{:S(2)}) collective-permute-start(bf16[64,1664]{1,0:T(8,128)(2,1)S(1)} %pad_maximum_fusion.12), channel_id=1, source_target_pairs={{16,0},{0,16},{17,1},{1,17},{18,2},{2,18},{19,3},{3,19},{20,4},{4,... | collective-permute-start | bytes 638984 | tf_op jit(solution)/shard_map/ppermute | solution.py:116
  82.0 1.0 collective-permute-start.19
  83.1 3.2 %collective-permute-done.25 = bf16[64,1536]{1,0:T(8,128)(2,1)S(1)} collective-permute-done((bf16[64,1536]{1,0:T(8,128)(2,1)S(1)}, bf16[64,1536]{1,0:T(8,128)(2,1)S(1)}, u32[]{:S(2)}, u32[]{:S(2)}) %collective-permute-start.25) | collective-permute-done | bytes 196640 | tf_op jit(solution)/shard_map/ppermute | solution.py:116
  86.3 1.1 collective-permute-start.30
  87.4 1.0 collective-permute-start.29
  88.5 2.5 %collective-permute-done.19 = bf16[64,1536]{1,0:T(8,128)(2,1)S(1)} collective-permute-done((bf16[64,1536]{1,0:T(8,128)(2,1)S(1)}, bf16[64,1536]{1,0:T(8,128)(2,1)S(1)}, u32[]{:S(2)}, u32[]{:S(2)}) %collective-permute-start.19) | collective-permute-done | bytes 196640 | tf_op jit(solution)/shard_map/ppermute | solution.py:116
  91.1 1.6 %collective-permute-start.22 = (bf16[32,1536]{1,0:T(8,128)(2,1)S(1)}, bf16[32,1536]{1,0:T(8,128)(2,1)S(1)}, u32[]{:S(2)}, u32[]{:S(2)}) collective-permute-start(bf16[32,1536]{1,0:T(8,128)(2,1)S(1)} %split.125), channel_id=1, source_target_pairs={{16,0},{0,16},{17,1},{1,17},{18,2},{2,18},{19,3},{3,19},{20,4},{4,... | collective-permute-start | bytes 294920 | tf_op jit(solution)/shard_map/ppermute | solution.py:116
  92.7 1.1 collective-permute-start.23
  94.2 1.7 %collective-permute-start.32 = (bf16[8,3072]{1,0:T(8,128)(2,1)S(1)}, bf16[8,3072]{1,0:T(8,128)(2,1)S(1)}, u32[]{:S(2)}, u32[]{:S(2)}) collective-permute-start(bf16[8,3072]{1,0:T(8,128)(2,1)S(1)} %get-tuple-element.100), channel_id=1, source_target_pairs={{2,0},{3,1},{0,2},{1,3},{6,4},{7,5},{4,6},{5,7},{10,8},{11,9},{8,1... | collective-permute-start | bytes 147464 | tf_op jit(solution)/shard_map/ppermute | solution.py:112
  95.9 2.4 %collective-permute-start.33 = (bf16[8,3072]{1,0:T(8,128)(2,1)S(1)}, bf16[8,3072]{1,0:T(8,128)(2,1)S(1)}, u32[]{:S(2)}, u32[]{:S(2)}) collective-permute-start(bf16[8,3072]{1,0:T(8,128)(2,1)S(1)} %get-tuple-element.99), channel_id=1, source_target_pairs={{1,0},{2,1},{3,2},{0,3},{5,4},{6,5},{7,6},{4,7},{9,8},{10,9},{11,1... | collective-permute-start | bytes 147464 | tf_op jit(solution)/shard_map/ppermute | solution.py:112
  98.5 1.6 %collective-permute-start.27 = (bf16[8,3200]{1,0:T(8,128)(2,1)S(1)}, bf16[8,3200]{1,0:T(8,128)(2,1)S(1)}, u32[]{:S(2)}, u32[]{:S(2)}) collective-permute-start(bf16[8,3200]{1,0:T(8,128)(2,1)S(1)} %get-tuple-element.97), channel_id=1, source_target_pairs={{2,0},{3,1},{0,2},{1,3},{6,4},{7,5},{4,6},{5,7},{10,8},{11,9},{8,1... | collective-permute-start | bytes 153608 | tf_op jit(solution)/shard_map/ppermute | solution.py:112
  100.3 2.6 %collective-permute-start.28 = (bf16[8,3200]{1,0:T(8,128)(2,1)S(1)}, bf16[8,3200]{1,0:T(8,128)(2,1)S(1)}, u32[]{:S(2)}, u32[]{:S(2)}) collective-permute-start(bf16[8,3200]{1,0:T(8,128)(2,1)S(1)} %get-tuple-element.96), channel_id=1, source_target_pairs={{1,0},{2,1},{3,2},{0,3},{5,4},{6,5},{7,6},{4,7},{9,8},{10,9},{11,1... | collective-permute-start | bytes 153608 | tf_op jit(solution)/shard_map/ppermute | solution.py:112
  102.9 1.5 %collective-permute-done.26 = bf16[8,3200]{1,0:T(8,128)(2,1)S(1)} collective-permute-done((bf16[8,3200]{1,0:T(8,128)(2,1)S(1)}, bf16[8,3200]{1,0:T(8,128)(2,1)S(1)}, u32[]{:S(2)}, u32[]{:S(2)}) %collective-permute-start.26) | collective-permute-done | bytes 51232 | tf_op jit(solution)/shard_map/ppermute | solution.py:112
  105.8 0.9 fusion.3
  (101 shorter events, 6.9 us)
Async XLA Ops:
  0.6 8.5 %copy-start = (bf16[6144,4]{0,1:T(4,128)(2,1)S(1)}, bf16[6144,4]{0,1:T(4,128)(2,1)}, u32[]{:S(2)}) copy-start(bf16[6144,4]{0,1:T(4,128)(2,1)} %param.12) | copy-start | bytes 147460
  0.6 17.2 %copy-start.1 = (bf16[8,6144]{1,0:T(8,128)(2,1)S(1)}, bf16[8,6144]{1,0:T(8,128)(2,1)}, u32[]{:S(2)}) copy-start(bf16[8,6144]{1,0:T(8,128)(2,1)} %param.9) | copy-start | bytes 294916
  0.7 9.8 %collective-permute-start = (bf16[8,6144]{1,0:T(8,128)(2,1)}, bf16[8,6144]{1,0:T(8,128)(2,1)S(1)}, u32[]{:S(2)}, u32[]{:S(2)}) collective-permute-start(bf16[8,6144]{1,0:T(8,128)(2,1)} %param.8), channel_id=1, source_target_pairs={{1,0},{2,1},{3,2},{0,3},{5,4},{6,5},{7,6},{4,7},{9,8},{10,9},{11,1... | collective-permute-start | bytes 294920 | tf_op jit(solution)/shard_map/ppermute | solution.py:112
  5.8 9.0 %collective-permute-start.4 = (bf16[8,6144]{1,0:T(8,128)(2,1)}, bf16[8,6144]{1,0:T(8,128)(2,1)S(1)}, u32[]{:S(2)}, u32[]{:S(2)}) collective-permute-start(bf16[8,6144]{1,0:T(8,128)(2,1)} %param.8), channel_id=1, source_target_pairs={{2,0},{3,1},{0,2},{1,3},{6,4},{7,5},{4,6},{5,7},{10,8},{11,9},{8,1... | collective-permute-start | bytes 294920 | tf_op jit(solution)/shard_map/ppermute | solution.py:112
  5.8 9.0 %collective-permute-start.5 = (bf16[8,6144]{1,0:T(8,128)(2,1)}, bf16[8,6144]{1,0:T(8,128)(2,1)S(1)}, u32[]{:S(2)}, u32[]{:S(2)}) collective-permute-start(bf16[8,6144]{1,0:T(8,128)(2,1)} %param.8), channel_id=1, source_target_pairs={{3,0},{0,1},{1,2},{2,3},{7,4},{4,5},{5,6},{6,7},{11,8},{8,9},{9,10... | collective-permute-start | bytes 294920 | tf_op jit(solution)/shard_map/ppermute | solution.py:112
  14.8 7.8 %collective-permute-start.6 = (bf16[32,3072]{1,0:T(8,128)(2,1)S(1)}, bf16[32,3072]{1,0:T(8,128)(2,1)S(1)}, u32[]{:S(2)}, u32[]{:S(2)}) collective-permute-start(bf16[32,3072]{1,0:T(8,128)(2,1)S(1)} %get-tuple-element.37), channel_id=1, source_target_pairs={{16,0},{0,16},{17,1},{1,17},{18,2},{2,18},{19,3},{3,19},{20,4},{4,... | collective-permute-start | bytes 589832 | tf_op jit(solution)/shard_map/ppermute | solution.py:116
  16.4 6.2 %collective-permute-start.7 = (bf16[32,3072]{1,0:T(8,128)(2,1)S(1)}, bf16[32,3072]{1,0:T(8,128)(2,1)S(1)}, u32[]{:S(2)}, u32[]{:S(2)}) collective-permute-start(bf16[32,3072]{1,0:T(8,128)(2,1)S(1)} %get-tuple-element.39), channel_id=1, source_target_pairs={{8,0},{12,4},{0,8},{4,12},{9,1},{13,5},{1,9},{5,13},{10,2},{14,6},... | collective-permute-start | bytes 589832 | tf_op jit(solution)/shard_map/ppermute | solution.py:116
  17.9 4.7 %collective-permute-start.1 = (bf16[8,6272]{1,0:T(8,128)(2,1)S(1)}, bf16[8,6272]{1,0:T(8,128)(2,1)S(1)}, u32[]{:S(2)}, u32[]{:S(2)}) collective-permute-start(bf16[8,6272]{1,0:T(8,128)(2,1)S(1)} %fusion.4), channel_id=1, source_target_pairs={{1,0},{2,1},{3,2},{0,3},{5,4},{6,5},{7,6},{4,7},{9,8},{10,9},{11,1... | collective-permute-start | bytes 301064 | tf_op jit(solution)/shard_map/ppermute | solution.py:112
  23.4 11.2 %collective-permute-start.9 = (bf16[64,3072]{1,0:T(8,128)(2,1)}, bf16[64,3072]{1,0:T(8,128)(2,1)S(1)}, u32[]{:S(2)}, u32[]{:S(2)}) collective-permute-start(bf16[64,3072]{1,0:T(8,128)(2,1)} %pad_maximum_fusion.10), channel_id=1, source_target_pairs={{16,0},{0,16},{17,1},{1,17},{18,2},{2,18},{19,3},{3,19},{20,4},{4,... | collective-permute-start | bytes 1179656 | tf_op jit(solution)/shard_map/ppermute | solution.py:116
  24.7 9.8 %collective-permute-start.8 = (bf16[64,3072]{1,0:T(8,128)(2,1)}, bf16[64,3072]{1,0:T(8,128)(2,1)S(1)}, u32[]{:S(2)}, u32[]{:S(2)}) collective-permute-start(bf16[64,3072]{1,0:T(8,128)(2,1)} %pad_maximum_fusion.9), channel_id=1, source_target_pairs={{8,0},{12,4},{0,8},{4,12},{9,1},{13,5},{1,9},{5,13},{10,2},{14,6},... | collective-permute-start | bytes 1179656 | tf_op jit(solution)/shard_map/ppermute | solution.py:116
  26.0 6.8 %collective-permute-start.2 = (bf16[8,6272]{1,0:T(8,128)(2,1)S(1)}, bf16[8,6272]{1,0:T(8,128)(2,1)S(1)}, u32[]{:S(2)}, u32[]{:S(2)}) collective-permute-start(bf16[8,6272]{1,0:T(8,128)(2,1)S(1)} %fusion.4), channel_id=1, source_target_pairs={{2,0},{3,1},{0,2},{1,3},{6,4},{7,5},{4,6},{5,7},{10,8},{11,9},{8,1... | collective-permute-start | bytes 301064 | tf_op jit(solution)/shard_map/ppermute | solution.py:112
  28.0 6.5 %collective-permute-start.3 = (bf16[8,6272]{1,0:T(8,128)(2,1)S(1)}, bf16[8,6272]{1,0:T(8,128)(2,1)}, u32[]{:S(2)}, u32[]{:S(2)}) collective-permute-start(bf16[8,6272]{1,0:T(8,128)(2,1)S(1)} %fusion.4), channel_id=1, source_target_pairs={{3,0},{0,1},{1,2},{2,3},{7,4},{4,5},{5,6},{6,7},{11,8},{8,9},{9,10... | collective-permute-start | bytes 301064 | tf_op jit(solution)/shard_map/ppermute | solution.py:112
  35.7 12.3 %collective-permute-start.15 = (bf16[128,3072]{1,0:T(8,128)(2,1)S(1)}, bf16[128,3072]{1,0:T(8,128)(2,1)S(1)}, u32[]{:S(2)}, u32[]{:S(2)}) collective-permute-start(bf16[128,3072]{1,0:T(8,128)(2,1)S(1)} %pad_maximum_fusion.4), channel_id=1, source_target_pairs={{4,0},{0,4},{12,8},{8,12},{5,1},{1,5},{13,9},{9,13},{6,2},{2,6},{1... | collective-permute-start | bytes 2359304 | tf_op jit(solution)/shard_map/ppermute | solution.py:116
  35.8 3.3 %collective-permute-start.12 = (bf16[128,3072]{1,0:T(8,128)(2,1)S(1)}, bf16[128,3072]{1,0:T(8,128)(2,1)S(1)}, u32[]{:S(2)}, u32[]{:S(2)}) collective-permute-start(bf16[128,3072]{1,0:T(8,128)(2,1)S(1)} %pad_maximum_fusion.3), channel_id=1, source_target_pairs={{4,0},{0,4},{12,8},{8,12},{5,1},{1,5},{13,9},{9,13},{6,2},{2,6},{1... | collective-permute-start | bytes 2359304 | tf_op jit(solution)/shard_map/ppermute | solution.py:116
  36.4 8.9 %collective-permute-start.11 = (bf16[32,3072]{1,0:T(8,128)(2,1)S(1)}, bf16[32,3072]{1,0:T(8,128)(2,1)S(1)}, u32[]{:S(2)}, u32[]{:S(2)}) collective-permute-start(bf16[32,3072]{1,0:T(8,128)(2,1)S(1)} %get-tuple-element.48), channel_id=1, source_target_pairs={{8,0},{12,4},{0,8},{4,12},{9,1},{13,5},{1,9},{5,13},{10,2},{14,6},... | collective-permute-start | bytes 589832 | tf_op jit(solution)/shard_map/ppermute | solution.py:116
  37.4 7.9 %collective-permute-start.10 = (bf16[32,3200]{1,0:T(8,128)(2,1)S(1)}, bf16[32,3200]{1,0:T(8,128)(2,1)S(1)}, u32[]{:S(2)}, u32[]{:S(2)}) collective-permute-start(bf16[32,3200]{1,0:T(8,128)(2,1)S(1)} %slice.98), channel_id=1, source_target_pairs={{16,0},{0,16},{17,1},{1,17},{18,2},{2,18},{19,3},{3,19},{20,4},{4,... | collective-permute-start | bytes 614408 | tf_op jit(solution)/shard_map/ppermute | solution.py:116
  45.3 11.2 %collective-permute-start.14 = (bf16[64,3072]{1,0:T(8,128)(2,1)S(1)}, bf16[64,3072]{1,0:T(8,128)(2,1)S(1)}, u32[]{:S(2)}, u32[]{:S(2)}) collective-permute-start(bf16[64,3072]{1,0:T(8,128)(2,1)S(1)} %pad_maximum_fusion.11), channel_id=1, source_target_pairs={{16,0},{0,16},{17,1},{1,17},{18,2},{2,18},{19,3},{3,19},{20,4},{4,... | collective-permute-start | bytes 1179656 | tf_op jit(solution)/shard_map/ppermute | solution.py:116
  46.9 11.3 %collective-permute-start.13 = (bf16[64,3200]{1,0:T(8,128)(2,1)S(1)}, bf16[64,3200]{1,0:T(8,128)(2,1)S(1)}, u32[]{:S(2)}, u32[]{:S(2)}) collective-permute-start(bf16[64,3200]{1,0:T(8,128)(2,1)S(1)} %pad_maximum_fusion.7), channel_id=1, source_target_pairs={{8,0},{12,4},{0,8},{4,12},{9,1},{13,5},{1,9},{5,13},{10,2},{14,6},... | collective-permute-start | bytes 1228808 | tf_op jit(solution)/shard_map/ppermute | solution.py:116
  58.3 2.4 %collective-permute-start.17 = (bf16[128,3072]{1,0:T(8,128)(2,1)S(1)}, bf16[128,3072]{1,0:T(8,128)(2,1)S(1)}, u32[]{:S(2)}, u32[]{:S(2)}) collective-permute-start(bf16[128,3072]{1,0:T(8,128)(2,1)S(1)} %pad_maximum_fusion.5), channel_id=1, source_target_pairs={{4,0},{0,4},{12,8},{8,12},{5,1},{1,5},{13,9},{9,13},{6,2},{2,6},{1... | collective-permute-start | bytes 2359304 | tf_op jit(solution)/shard_map/ppermute | solution.py:116
  58.4 3.4 %collective-permute-start.16 = (bf16[128,3200]{1,0:T(8,128)(2,1)S(1)}, bf16[128,3200]{1,0:T(8,128)(2,1)S(1)}, u32[]{:S(2)}, u32[]{:S(2)}) collective-permute-start(bf16[128,3200]{1,0:T(8,128)(2,1)S(1)} %pad_maximum_fusion.2), channel_id=1, source_target_pairs={{4,0},{0,4},{12,8},{8,12},{5,1},{1,5},{13,9},{9,13},{6,2},{2,6},{1... | collective-permute-start | bytes 2457608 | tf_op jit(solution)/shard_map/ppermute | solution.py:116
  73.0 5.1 %collective-permute-start.21 = (bf16[128,3072]{1,0:T(8,128)(2,1)S(1)}, bf16[128,3072]{1,0:T(8,128)(2,1)S(1)}, u32[]{:S(2)}, u32[]{:S(2)}) collective-permute-start(bf16[128,3072]{1,0:T(8,128)(2,1)S(1)} %get-tuple-element.64), channel_id=1, source_target_pairs={{4,0},{0,4},{12,8},{8,12},{5,1},{1,5},{13,9},{9,13},{6,2},{2,6},{1... | collective-permute-start | bytes 2359304 | tf_op jit(solution)/shard_map/ppermute | solution.py:116
  77.7 2.4 %collective-permute-start.18 = (bf16[128,3200]{1,0:T(8,128)(2,1)S(1)}, bf16[128,3200]{1,0:T(8,128)(2,1)S(1)}, u32[]{:S(2)}, u32[]{:S(2)}) collective-permute-start(bf16[128,3200]{1,0:T(8,128)(2,1)S(1)} %get-tuple-element.61), channel_id=1, source_target_pairs={{4,0},{0,4},{12,8},{8,12},{5,1},{1,5},{13,9},{9,13},{6,2},{2,6},{1... | collective-permute-start | bytes 2457608 | tf_op jit(solution)/shard_map/ppermute | solution.py:116
  78.5 7.8 %collective-permute-start.25 = (bf16[64,1536]{1,0:T(8,128)(2,1)S(1)}, bf16[64,1536]{1,0:T(8,128)(2,1)S(1)}, u32[]{:S(2)}, u32[]{:S(2)}) collective-permute-start(bf16[64,1536]{1,0:T(8,128)(2,1)S(1)} %pad_maximum_fusion.13), channel_id=1, source_target_pairs={{16,0},{0,16},{17,1},{1,17},{18,2},{2,18},{19,3},{3,19},{20,4},{4,... | collective-permute-start | bytes 589832 | tf_op jit(solution)/shard_map/ppermute | solution.py:116
  79.1 8.3 %collective-permute-start.24 = (bf16[64,1536]{1,0:T(8,128)(2,1)S(1)}, bf16[64,1536]{1,0:T(8,128)(2,1)S(1)}, u32[]{:S(2)}, u32[]{:S(2)}) collective-permute-start(bf16[64,1536]{1,0:T(8,128)(2,1)S(1)} %concatenate.112), channel_id=1, source_target_pairs={{8,0},{12,4},{0,8},{4,12},{9,1},{13,5},{1,9},{5,13},{10,2},{14,6},... | collective-permute-start | bytes 589832 | tf_op jit(solution)/shard_map/ppermute | solution.py:116
  80.5 10.5 %collective-permute-start.20 = (bf16[64,1664]{1,0:T(8,128)(2,1)S(1)}, bf16[64,1664]{1,0:T(8,128)(2,1)S(1)}, u32[]{:S(2)}, u32[]{:S(2)}) collective-permute-start(bf16[64,1664]{1,0:T(8,128)(2,1)S(1)} %pad_maximum_fusion.12), channel_id=1, source_target_pairs={{16,0},{0,16},{17,1},{1,17},{18,2},{2,18},{19,3},{3,19},{20,4},{4,... | collective-permute-start | bytes 638984 | tf_op jit(solution)/shard_map/ppermute | solution.py:116
  82.0 9.0 %collective-permute-start.19 = (bf16[64,1536]{1,0:T(8,128)(2,1)S(1)}, bf16[64,1536]{1,0:T(8,128)(2,1)S(1)}, u32[]{:S(2)}, u32[]{:S(2)}) collective-permute-start(bf16[64,1536]{1,0:T(8,128)(2,1)S(1)} %concatenate.110), channel_id=1, source_target_pairs={{8,0},{12,4},{0,8},{4,12},{9,1},{13,5},{1,9},{5,13},{10,2},{14,6},... | collective-permute-start | bytes 589832 | tf_op jit(solution)/shard_map/ppermute | solution.py:116
  86.3 7.4 %collective-permute-start.30 = (bf16[32,1536]{1,0:T(8,128)(2,1)S(1)}, bf16[32,1536]{1,0:T(8,128)(2,1)S(1)}, u32[]{:S(2)}, u32[]{:S(2)}) collective-permute-start(bf16[32,1536]{1,0:T(8,128)(2,1)S(1)} %split.123), channel_id=1, source_target_pairs={{8,0},{12,4},{0,8},{4,12},{9,1},{13,5},{1,9},{5,13},{10,2},{14,6},... | collective-permute-start | bytes 294920 | tf_op jit(solution)/shard_map/ppermute | solution.py:116
  87.4 6.3 %collective-permute-start.29 = (bf16[32,1536]{1,0:T(8,128)(2,1)S(1)}, bf16[32,1536]{1,0:T(8,128)(2,1)S(1)}, u32[]{:S(2)}, u32[]{:S(2)}) collective-permute-start(bf16[32,1536]{1,0:T(8,128)(2,1)S(1)} %split.124), channel_id=1, source_target_pairs={{16,0},{0,16},{17,1},{1,17},{18,2},{2,18},{19,3},{3,19},{20,4},{4,... | collective-permute-start | bytes 294920 | tf_op jit(solution)/shard_map/ppermute | solution.py:116
  91.1 7.2 %collective-permute-start.22 = (bf16[32,1536]{1,0:T(8,128)(2,1)S(1)}, bf16[32,1536]{1,0:T(8,128)(2,1)S(1)}, u32[]{:S(2)}, u32[]{:S(2)}) collective-permute-start(bf16[32,1536]{1,0:T(8,128)(2,1)S(1)} %split.125), channel_id=1, source_target_pairs={{16,0},{0,16},{17,1},{1,17},{18,2},{2,18},{19,3},{3,19},{20,4},{4,... | collective-permute-start | bytes 294920 | tf_op jit(solution)/shard_map/ppermute | solution.py:116
  92.7 5.6 %collective-permute-start.23 = (bf16[32,1664]{1,0:T(8,128)(2,1)S(1)}, bf16[32,1664]{1,0:T(8,128)(2,1)S(1)}, u32[]{:S(2)}, u32[]{:S(2)}) collective-permute-start(bf16[32,1664]{1,0:T(8,128)(2,1)S(1)} %split.122), channel_id=1, source_target_pairs={{8,0},{12,4},{0,8},{4,12},{9,1},{13,5},{1,9},{5,13},{10,2},{14,6},... | collective-permute-start | bytes 319496 | tf_op jit(solution)/shard_map/ppermute | solution.py:116
  93.9 6.5 %collective-permute-start.31 = (bf16[8,3072]{1,0:T(8,128)(2,1)S(1)}, bf16[8,3072]{1,0:T(8,128)(2,1)S(1)}, u32[]{:S(2)}, u32[]{:S(2)}) collective-permute-start(bf16[8,3072]{1,0:T(8,128)(2,1)S(1)} %get-tuple-element.98), channel_id=1, source_target_pairs={{3,0},{0,1},{1,2},{2,3},{7,4},{4,5},{5,6},{6,7},{11,8},{8,9},{9,10... | collective-permute-start | bytes 147464 | tf_op jit(solution)/shard_map/ppermute | solution.py:112
  94.2 8.7 %collective-permute-start.32 = (bf16[8,3072]{1,0:T(8,128)(2,1)S(1)}, bf16[8,3072]{1,0:T(8,128)(2,1)S(1)}, u32[]{:S(2)}, u32[]{:S(2)}) collective-permute-start(bf16[8,3072]{1,0:T(8,128)(2,1)S(1)} %get-tuple-element.100), channel_id=1, source_target_pairs={{2,0},{3,1},{0,2},{1,3},{6,4},{7,5},{4,6},{5,7},{10,8},{11,9},{8,1... | collective-permute-start | bytes 147464 | tf_op jit(solution)/shard_map/ppermute | solution.py:112
  95.9 7.0 %collective-permute-start.33 = (bf16[8,3072]{1,0:T(8,128)(2,1)S(1)}, bf16[8,3072]{1,0:T(8,128)(2,1)S(1)}, u32[]{:S(2)}, u32[]{:S(2)}) collective-permute-start(bf16[8,3072]{1,0:T(8,128)(2,1)S(1)} %get-tuple-element.99), channel_id=1, source_target_pairs={{1,0},{2,1},{3,2},{0,3},{5,4},{6,5},{7,6},{4,7},{9,8},{10,9},{11,1... | collective-permute-start | bytes 147464 | tf_op jit(solution)/shard_map/ppermute | solution.py:112
  98.4 6.9 %copy-start.2 = (s32[8]{0:T(128)S(1)}, s32[8]{0:T(128)}, u32[]{:S(2)}) copy-start(s32[8]{0:T(128)} %param.10) | copy-start | bytes 100
  98.5 6.0 %collective-permute-start.26 = (bf16[8,3200]{1,0:T(8,128)(2,1)S(1)}, bf16[8,3200]{1,0:T(8,128)(2,1)S(1)}, u32[]{:S(2)}, u32[]{:S(2)}) collective-permute-start(bf16[8,3200]{1,0:T(8,128)(2,1)S(1)} %get-tuple-element.95), channel_id=1, source_target_pairs={{3,0},{0,1},{1,2},{2,3},{7,4},{4,5},{5,6},{6,7},{11,8},{8,9},{9,10... | collective-permute-start | bytes 153608 | tf_op jit(solution)/shard_map/ppermute | solution.py:112
  98.5 5.9 %collective-permute-start.27 = (bf16[8,3200]{1,0:T(8,128)(2,1)S(1)}, bf16[8,3200]{1,0:T(8,128)(2,1)S(1)}, u32[]{:S(2)}, u32[]{:S(2)}) collective-permute-start(bf16[8,3200]{1,0:T(8,128)(2,1)S(1)} %get-tuple-element.97), channel_id=1, source_target_pairs={{2,0},{3,1},{0,2},{1,3},{6,4},{7,5},{4,6},{5,7},{10,8},{11,9},{8,1... | collective-permute-start | bytes 153608 | tf_op jit(solution)/shard_map/ppermute | solution.py:112
  100.3 4.7 %collective-permute-start.28 = (bf16[8,3200]{1,0:T(8,128)(2,1)S(1)}, bf16[8,3200]{1,0:T(8,128)(2,1)S(1)}, u32[]{:S(2)}, u32[]{:S(2)}) collective-permute-start(bf16[8,3200]{1,0:T(8,128)(2,1)S(1)} %get-tuple-element.96), channel_id=1, source_target_pairs={{1,0},{2,1},{3,2},{0,3},{5,4},{6,5},{7,6},{4,7},{9,8},{10,9},{11,1... | collective-permute-start | bytes 153608 | tf_op jit(solution)/shard_map/ppermute | solution.py:112

commit v6 on v5

--- a/solution.py
+++ b/solution.py
@@ -133,12 +133,18 @@
 
 
 def gather_z(rows):
-    return [rows] + [shift(rows, "mp", k) for k in range(1, lax.axis_size("mp"))]
+    return jnp.concatenate([rows] + [shift(rows, "mp", k) for k in range(1, lax.axis_size("mp"))], axis=0)
+
+
+def gather_z_whole(rows):
+    size, count = lax.axis_size("mp"), rows.shape[0]
+    whole = lax.all_gather(rows, "mp", axis=0, tiled=True)
+    start = lax.axis_index("mp") * count
+    return lax.dynamic_slice_in_dim(jnp.concatenate([whole, whole], axis=0), start, size * count, 0)
 
 
 def gather_near(z_rows, cut):
-    rows = jnp.concatenate(z_rows, axis=0)
-    low, high = rows[:, :cut], rows[:, cut:]
+    low, high = z_rows[:, :cut], z_rows[:, cut:]
     return [low, swap_x(low)], [high, swap_y(high)]
 
 
@@ -373,9 +379,9 @@
     gate_second = jax.nn.sigmoid(second_logit - first_logit)
     gate_table = (first_hot * gate_first[:, None] + second_hot * gate_second[:, None]) * keep_rows[:, None]
     gate_table = jnp.pad(gate_table.astype(jnp.bfloat16), ((0, 0), (0, table - expert_count)))
-    grad_z = gather_z(after_others(jnp.concatenate([gate_table, out_grad], axis=1), token_z[1]))
+    grad_z = gather_z_whole(jnp.concatenate([gate_table, out_grad], axis=1))
     token_near = gather_near(token_z, half)
-    token_far = gather_far(*after_others(token_near, grad_z[1]))
+    token_far = gather_far(*token_near)
     grad_near = gather_near(after_others(grad_z, token_far), half + table)
     token_low, token_high = gather_core(token_near[0], token_far[0], token_near[1], token_far[1])
     before = multiply_tokens(0, token_low, gate_weight, up_weight)

time: 107 us -> 121 us (1.13)
  blocking collectives: 0 us -> 16.4 us
  starting transfers between devices: 41 us -> 34.4 us
  waiting for transfers between devices: 27.1 us -> 30.2 us
    all_gather x0 -> x1, blocking collectives: none -> 16.4 us  [gather_z_whole(): whole = lax.all_gather(rows, 'mp', axis=0, tiled=True)]
    ppermute x22, waiting for transfers between devices: 12.9 us -> 23.7 us  [swap(): lax.ppermute(value, axis, [(i ^ bit, i) for i in range(lax.axis_size(axis...]
    ppermute x12 -> x9, waiting for transfers between devices: 14.2 us -> 6.52 us  [shift(): lax.ppermute(value, axis, [((i + step) % size, i) for i in range(size)])]
    ppermute x12 -> x9, starting transfers between devices: 20.3 us -> 15 us  [shift(): lax.ppermute(value, axis, [((i + step) % size, i) for i in range(size)])]
    ppermute x22, starting transfers between devices: 20.8 us -> 19.4 us  [swap(): lax.ppermute(value, axis, [(i ^ bit, i) for i in range(lax.axis_size(axis...]
  transfers between devices with their start and end apart: 34 -> 31, of which waited for: 14 -> 14; matrix products, arithmetic and copies ran while one was open for 6% -> 7% of each run, Pallas kernels for 15% -> 14%
where the time goes in v6:
time: 121 us
  starting transfers between devices  34.4 us (28%)
  waiting for transfers between devices  30.2 us (25%)
  Pallas kernels  27.6 us (23%)
  blocking collectives  16.4 us (14%)
  other arithmetic  4.64 us (4%)
  local copies, waits for them, and re-layouts  4.23 us (3%)
  matrix products  2.15 us (2%)
    ppermute x22, waiting for transfers between devices, swap(): lax.ppermute(value, axis, [(i ^ bit, i) for i in range(lax.axis_size(axis...  23.7 us
    ppermute x22, starting transfers between devices, swap(): lax.ppermute(value, axis, [(i ^ bit, i) for i in range(lax.axis_size(axis...  19.4 us
    all_gather x1, blocking collectives, gather_z_whole(): whole = lax.all_gather(rows, 'mp', axis=0, tiled=True)  16.4 us
    ppermute x9, starting transfers between devices, shift(): lax.ppermute(value, axis, [((i + step) % size, i) for i in range(size)])  15 us
    pallas_call x2, Pallas kernels, multiply_tokens(): pl.pallas_call(functools.partial(token_kernel, first), out_shape=(pltpu.V...  12.1 us
    pallas_call x2, Pallas kernels, multiply_outputs(): pl.pallas_call(output_kernel, out_shape=(pltpu.VMEM((rows // 2, total), j...  8.99 us
    pallas_call x1, Pallas kernels, multiply_grads(): pl.pallas_call(grad_kernel, out_shape=(pltpu.VMEM((rows, hidden), jnp.bfl...  6.56 us
    ppermute x9, waiting for transfers between devices, shift(): lax.ppermute(value, axis, [((i + step) % size, i) for i in range(size)])  6.52 us
  transfers between devices with their start and end apart: 31, of which 14 were waited for; matrix products, arithmetic and copies ran while one was open for 7% of the time, Pallas kernels for 14%

profile of v6, /device:TPU:0, one launch (start us, length us, event | category | flops | bytes accessed | tf_op | source)
XLA Modules:
  0.0 120.8 jit_solution(2025095167496283983)
XLA Ops:
  0.7 4.1 %collective-permute-start.1 = (bf16[8,6144]{1,0:T(8,128)(2,1)}, bf16[8,6144]{1,0:T(8,128)(2,1)S(1)}, u32[]{:S(2)}, u32[]{:S(2)}) collective-permute-start(bf16[8,6144]{1,0:T(8,128)(2,1)} %param.8), channel_id=1, source_target_pairs={{2,0},{3,1},{0,2},{1,3},{6,4},{7,5},{4,6},{5,7},{10,8},{11,9},{8,1... | collective-permute-start | bytes 294920 | tf_op jit(solution)/shard_map/ppermute | solution.py:112
  4.8 1.3 %collective-permute-start = (bf16[8,6144]{1,0:T(8,128)(2,1)}, bf16[8,6144]{1,0:T(8,128)(2,1)S(1)}, u32[]{:S(2)}, u32[]{:S(2)}) collective-permute-start(bf16[8,6144]{1,0:T(8,128)(2,1)} %param.8), channel_id=1, source_target_pairs={{1,0},{2,1},{3,2},{0,3},{5,4},{6,5},{7,6},{4,7},{9,8},{10,9},{11,1... | collective-permute-start | bytes 294920 | tf_op jit(solution)/shard_map/ppermute | solution.py:112
  6.1 0.7 collective-permute-start.2
  6.8 0.9 constant_dynamic-update-slice_fusion.3
  7.7 0.7 convert_element_type.76
  8.4 0.8 slice_bitcast_fusion
  9.1 1.2 %select_reduce_fusion.3 = (f32[8]{0:T(128)S(1)}, f32[8]{0:T(128)S(1)}) fusion(s32[8]{0:T(128)S(1)} %get-tuple-element.90, s32[8]{0:T(128)S(1)} %get-tuple-element.89, bf16[8,6144]{1,0:T(8,128)(2,1)} %param.8, bf16[6144,4]{0,1:T(4,128)(2,1)S(1)} %copy-done), kind=kOutput, calls=%fused_computation.68 | convolution fusion | flops 393392 | bytes 147584 | tf_op jit(solution)/shard_map/dot_general | solution.py:375
  10.5 0.8 collective-permute-done.1
  11.3 1.8 %collective-permute-done.2 = bf16[8,6144]{1,0:T(8,128)(2,1)S(1)} collective-permute-done((bf16[8,6144]{1,0:T(8,128)(2,1)}, bf16[8,6144]{1,0:T(8,128)(2,1)S(1)}, u32[]{:S(2)}, u32[]{:S(2)}) %collective-permute-start.2) | collective-permute-done | bytes 98336 | tf_op jit(solution)/shard_map/ppermute | solution.py:112
  13.2 1.5 %collective-permute-start.5 = (bf16[32,3072]{1,0:T(8,128)(2,1)S(1)}, bf16[32,3072]{1,0:T(8,128)(2,1)S(1)}, u32[]{:S(2)}, u32[]{:S(2)}) collective-permute-start(bf16[32,3072]{1,0:T(8,128)(2,1)S(1)} %get-tuple-element.77), channel_id=1, source_target_pairs={{8,0},{12,4},{0,8},{4,12},{9,1},{13,5},{1,9},{5,13},{10,2},{14,6},... | collective-permute-start | bytes 589832 | tf_op jit(solution)/shard_map/ppermute | solution.py:116
  14.8 16.4 %all_gather.3 = bf16[32,6272]{1,0:T(8,128)(2,1)S(1)} all-gather(bf16[8,6272]{1,0:T(8,128)(2,1)S(1)} %fusion.5), channel_id=1, replica_groups=mesh['seq'=2,'expert'=4,'mp'=4] {'mp'}, dimensions={0}, use_global_device_ids=true | all-gather | bytes 501760 | tf_op jit(solution)/shard_map/all_gather | solution.py:141
  31.1 1.5 %collective-permute-start.3 = (bf16[32,3072]{1,0:T(8,128)(2,1)S(1)}, bf16[32,3072]{1,0:T(8,128)(2,1)S(1)}, u32[]{:S(2)}, u32[]{:S(2)}) collective-permute-start(bf16[32,3072]{1,0:T(8,128)(2,1)S(1)} %get-tuple-element.78), channel_id=1, source_target_pairs={{16,0},{0,16},{17,1},{1,17},{18,2},{2,18},{19,3},{3,19},{20,4},{4,... | collective-permute-start | bytes 589832 | tf_op jit(solution)/shard_map/ppermute | solution.py:116
  32.6 0.8 pad_maximum_fusion.10
  34.0 4.5 %collective-permute-done.3 = bf16[32,3072]{1,0:T(8,128)(2,1)S(1)} collective-permute-done((bf16[32,3072]{1,0:T(8,128)(2,1)S(1)}, bf16[32,3072]{1,0:T(8,128)(2,1)S(1)}, u32[]{:S(2)}, u32[]{:S(2)}) %collective-permute-start.3) | collective-permute-done | bytes 196640 | tf_op jit(solution)/shard_map/ppermute | solution.py:116
  38.5 0.8 pad_maximum_fusion.9
  39.9 2.9 %collective-permute-done.6 = bf16[64,3072]{1,0:T(8,128)(2,1)} collective-permute-done((bf16[64,3072]{1,0:T(8,128)(2,1)}, bf16[64,3072]{1,0:T(8,128)(2,1)}, u32[]{:S(2)}, u32[]{:S(2)}) %collective-permute-start.6) | collective-permute-done | bytes 393248 | tf_op jit(solution)/shard_map/ppermute | solution.py:116
  42.8 4.4 %collective-permute-done.4 = bf16[64,3072]{1,0:T(8,128)(2,1)S(1)} collective-permute-done((bf16[64,3072]{1,0:T(8,128)(2,1)}, bf16[64,3072]{1,0:T(8,128)(2,1)S(1)}, u32[]{:S(2)}, u32[]{:S(2)}) %collective-permute-start.4) | collective-permute-done | bytes 393248 | tf_op jit(solution)/shard_map/ppermute | solution.py:116
  47.3 1.5 %collective-permute-start.7 = (bf16[32,3200]{1,0:T(8,128)(2,1)S(1)}, bf16[32,3200]{1,0:T(8,128)(2,1)S(1)}, u32[]{:S(2)}, u32[]{:S(2)}) collective-permute-start(bf16[32,3200]{1,0:T(8,128)(2,1)S(1)} %slice.84), channel_id=1, source_target_pairs={{16,0},{0,16},{17,1},{1,17},{18,2},{2,18},{19,3},{3,19},{20,4},{4,... | collective-permute-start | bytes 614408 | tf_op jit(solution)/shard_map/ppermute | solution.py:116
  48.9 1.1 fusion.28
  51.1 0.9 constant_dynamic-update-slice_fusion.5
  52.2 6.0 %shard_map.95 = (f32[256,1024]{1,0:T(8,128)S(1)}, f32[256,1024]{1,0:T(8,128)S(1)}, bf16[3072,1024]{1,0:T(8,128)(2,1)S(1)}, bf16[3072,1024]{1,0:T(8,128)(2,1)S(1)}) custom-call(bf16[256,3072]{1,0:T(8,128)(2,1)S(1)} %pad_maximum_fusion.1.tokens, bf16[1,6144,1024]{2,1,0:T(8,128)(2,1)} %gate_weight.3, bf16[1,6144,1024]{2,1,0:T(8,128)(2,1)} %up_weight.3), custom_call_target="tpu_custom_call" | custom-call | flops 3221225472 | bytes 12582912 | tf_op jit(solution)/shard_map/pallas_call | solution.py:240
  58.2 0.7 collective-permute-start.11
  59.0 1.6 %collective-permute-start.10 = (bf16[64,3200]{1,0:T(8,128)(2,1)S(1)}, bf16[64,3200]{1,0:T(8,128)(2,1)S(1)}, u32[]{:S(2)}, u32[]{:S(2)}) collective-permute-start(bf16[64,3200]{1,0:T(8,128)(2,1)S(1)} %pad_maximum_fusion.7), channel_id=1, source_target_pairs={{8,0},{12,4},{0,8},{4,12},{9,1},{13,5},{1,9},{5,13},{10,2},{14,6},... | collective-permute-start | bytes 1228808 | tf_op jit(solution)/shard_map/ppermute | solution.py:116
  60.6 6.1 %shard_map.96 = (f32[256,1024]{1,0:T(8,128)S(1)}, f32[256,1024]{1,0:T(8,128)S(1)}, bf16[3072,1024]{1,0:T(8,128)(2,1)S(1)}, bf16[3072,1024]{1,0:T(8,128)(2,1)S(1)}) custom-call(bf16[256,3072]{1,0:T(8,128)(2,1)S(1)} %constant_dynamic-update-slice_fusion.4.tokens, bf16[1,6144,1024]{2,1,0:T(8,128)(2,1)} %gate_weight.3, bf16[1,6144,1024]{2,1,0:T(8,128)(2,1)} %up_weight.3, ...), custom_call_target="tpu_custom_call" | custom-call | flops 3221225472 | bytes 12582912 | tf_op jit(solution)/shard_map/pallas_call | solution.py:240
  66.7 2.4 %collective-permute-done.11 = bf16[64,3072]{1,0:T(8,128)(2,1)S(1)} collective-permute-done((bf16[64,3072]{1,0:T(8,128)(2,1)S(1)}, bf16[64,3072]{1,0:T(8,128)(2,1)S(1)}, u32[]{:S(2)}, u32[]{:S(2)}) %collective-permute-start.11) | collective-permute-done | bytes 393248 | tf_op jit(solution)/shard_map/ppermute | solution.py:116
  69.1 0.8 collective-permute-done.10
  70.8 1.6 %collective-permute-done.14 = bf16[128,3072]{1,0:T(8,128)(2,1)S(1)} collective-permute-done((bf16[128,3072]{1,0:T(8,128)(2,1)S(1)}, bf16[128,3072]{1,0:T(8,128)(2,1)S(1)}, u32[]{:S(2)}, u32[]{:S(2)}) %collective-permute-start.14) | collective-permute-done | bytes 786464 | tf_op jit(solution)/shard_map/ppermute | solution.py:116
  72.4 1.1 collective-permute-done.13
  73.7 6.6 %shard_map.97 = (bf16[256,1024]{1,0:T(8,128)(2,1)S(1)}, bf16[256,1024]{1,0:T(8,128)(2,1)S(1)}, bf16[256,128]{1,0:T(8,128)(2,1)S(1)}) custom-call(s32[1]{0:T(128)} %bitcast.expert, bf16[256,3200]{1,0:T(8,128)(2,1)S(1)} %pad_maximum_fusion.low, bf16[256,3072]{1,0:T(8,128)(2,1)S(1)} %constant_dynamic-update-slice_fusion.9.high, ...), custom_call_target="tpu_custom_call" | custom-call | flops 3221225472 | bytes 12582912 | tf_op jit(solution)/shard_map/pallas_call | solution.py:304
  80.2 4.5 %shard_map.99 = (f32[128,3072]{1,0:T(8,128)S(1)}, bf16[128,3072]{1,0:T(8,128)(2,1)S(1)}) custom-call(bf16[256,1024]{1,0:T(8,128)(2,1)S(1)} %get-tuple-element.39.grad_gate, bf16[256,1024]{1,0:T(8,128)(2,1)S(1)} %get-tuple-element.40.grad_up, bf16[3072,1024]{1,0:T(8,128)(2,1)S(1)} %get-tuple-element.46.gate_copy, bf16[3072,1024]{1,0:T(8,128)(2,1)S(1)} %get-tuple-element.47.up_copy), custom_call_target="tpu_custom_call" | custom-call | flops 3221225472 | bytes 3145728 | tf_op jit(solution)/shard_map/pallas_call | solution.py:350
  84.9 4.5 %shard_map.98 = (f32[128,3200]{1,0:T(8,128)S(1)}, bf16[128,3200]{1,0:T(8,128)(2,1)S(1)}) custom-call(bf16[256,1024]{1,0:T(8,128)(2,1)S(1)} %get-tuple-element.39.grad_gate, bf16[256,1024]{1,0:T(8,128)(2,1)S(1)} %get-tuple-element.40.grad_up, bf16[3072,1024]{1,0:T(8,128)(2,1)S(1)} %get-tuple-element.41.gate_copy, ...), custom_call_target="tpu_custom_call" | custom-call | flops 3221225472 | bytes 3145728 | tf_op jit(solution)/shard_map/pallas_call | solution.py:350
  90.2 1.5 %collective-permute-start.22 = (bf16[64,1536]{1,0:T(8,128)(2,1)S(1)}, bf16[64,1536]{1,0:T(8,128)(2,1)S(1)}, u32[]{:S(2)}, u32[]{:S(2)}) collective-permute-start(bf16[64,1536]{1,0:T(8,128)(2,1)S(1)} %pad_maximum_fusion.13), channel_id=1, source_target_pairs={{16,0},{0,16},{17,1},{1,17},{18,2},{2,18},{19,3},{3,19},{20,4},{4,... | collective-permute-start | bytes 589832 | tf_op jit(solution)/shard_map/ppermute | solution.py:116
  91.7 1.5 %collective-permute-start.21 = (bf16[64,1536]{1,0:T(8,128)(2,1)S(1)}, bf16[64,1536]{1,0:T(8,128)(2,1)S(1)}, u32[]{:S(2)}, u32[]{:S(2)}) collective-permute-start(bf16[64,1536]{1,0:T(8,128)(2,1)S(1)} %concatenate.112), channel_id=1, source_target_pairs={{8,0},{12,4},{0,8},{4,12},{9,1},{13,5},{1,9},{5,13},{10,2},{14,6},... | collective-permute-start | bytes 589832 | tf_op jit(solution)/shard_map/ppermute | solution.py:116
  93.6 0.6 collective-permute-start.16
  94.2 1.1 collective-permute-start.17
  95.3 4.2 %collective-permute-done.21 = bf16[64,1536]{1,0:T(8,128)(2,1)S(1)} collective-permute-done((bf16[64,1536]{1,0:T(8,128)(2,1)S(1)}, bf16[64,1536]{1,0:T(8,128)(2,1)S(1)}, u32[]{:S(2)}, u32[]{:S(2)}) %collective-permute-start.21) | collective-permute-done | bytes 196640 | tf_op jit(solution)/shard_map/ppermute | solution.py:116
  99.5 0.7 collective-permute-start.26
  100.3 1.6 %collective-permute-start.27 = (bf16[32,1536]{1,0:T(8,128)(2,1)S(1)}, bf16[32,1536]{1,0:T(8,128)(2,1)S(1)}, u32[]{:S(2)}, u32[]{:S(2)}) collective-permute-start(bf16[32,1536]{1,0:T(8,128)(2,1)S(1)} %split.123), channel_id=1, source_target_pairs={{8,0},{12,4},{0,8},{4,12},{9,1},{13,5},{1,9},{5,13},{10,2},{14,6},... | collective-permute-start | bytes 294920 | tf_op jit(solution)/shard_map/ppermute | solution.py:116
  101.9 1.7 %collective-permute-done.16 = bf16[64,1536]{1,0:T(8,128)(2,1)S(1)} collective-permute-done((bf16[64,1536]{1,0:T(8,128)(2,1)S(1)}, bf16[64,1536]{1,0:T(8,128)(2,1)S(1)}, u32[]{:S(2)}, u32[]{:S(2)}) %collective-permute-start.16) | collective-permute-done | bytes 196640 | tf_op jit(solution)/shard_map/ppermute | solution.py:116
  103.7 0.7 collective-permute-start.19
  104.4 1.5 %collective-permute-start.20 = (bf16[32,1664]{1,0:T(8,128)(2,1)S(1)}, bf16[32,1664]{1,0:T(8,128)(2,1)S(1)}, u32[]{:S(2)}, u32[]{:S(2)}) collective-permute-start(bf16[32,1664]{1,0:T(8,128)(2,1)S(1)} %split.122), channel_id=1, source_target_pairs={{8,0},{12,4},{0,8},{4,12},{9,1},{13,5},{1,9},{5,13},{10,2},{14,6},... | collective-permute-start | bytes 319496 | tf_op jit(solution)/shard_map/ppermute | solution.py:116
  106.1 3.8 %collective-permute-start.30 = (bf16[8,3072]{1,0:T(8,128)(2,1)S(1)}, bf16[8,3072]{1,0:T(8,128)(2,1)S(1)}, u32[]{:S(2)}, u32[]{:S(2)}) collective-permute-start(bf16[8,3072]{1,0:T(8,128)(2,1)S(1)} %get-tuple-element.83), channel_id=1, source_target_pairs={{1,0},{2,1},{3,2},{0,3},{5,4},{6,5},{7,6},{4,7},{9,8},{10,9},{11,1... | collective-permute-start | bytes 147464 | tf_op jit(solution)/shard_map/ppermute | solution.py:112
  110.1 0.6 collective-permute-start.23
  110.7 3.3 %collective-permute-start.25 = (bf16[8,3200]{1,0:T(8,128)(2,1)S(1)}, bf16[8,3200]{1,0:T(8,128)(2,1)S(1)}, u32[]{:S(2)}, u32[]{:S(2)}) collective-permute-start(bf16[8,3200]{1,0:T(8,128)(2,1)S(1)} %get-tuple-element.80), channel_id=1, source_target_pairs={{1,0},{2,1},{3,2},{0,3},{5,4},{6,5},{7,6},{4,7},{9,8},{10,9},{11,1... | collective-permute-start | bytes 153608 | tf_op jit(solution)/shard_map/ppermute | solution.py:112
  114.0 1.1 collective-permute-start.24
  115.1 1.3 %collective-permute-done.29 = bf16[8,3072]{1,0:T(8,128)(2,1)S(1)} collective-permute-done((bf16[8,3072]{1,0:T(8,128)(2,1)S(1)}, bf16[8,3072]{1,0:T(8,128)(2,1)S(1)}, u32[]{:S(2)}, u32[]{:S(2)}) %collective-permute-start.29) | collective-permute-done | bytes 49184 | tf_op jit(solution)/shard_map/ppermute | solution.py:112
  116.9 2.1 %collective-permute-done.24 = bf16[8,3200]{1,0:T(8,128)(2,1)S(1)} collective-permute-done((bf16[8,3200]{1,0:T(8,128)(2,1)S(1)}, bf16[8,3200]{1,0:T(8,128)(2,1)S(1)}, u32[]{:S(2)}, u32[]{:S(2)}) %collective-permute-start.24) | collective-permute-done | bytes 51232 | tf_op jit(solution)/shard_map/ppermute | solution.py:112
  119.3 0.9 fusion.4
  (93 shorter events, 6.9 us)
Async XLA Ops:
  0.6 8.5 %copy-start = (bf16[6144,4]{0,1:T(4,128)(2,1)S(1)}, bf16[6144,4]{0,1:T(4,128)(2,1)}, u32[]{:S(2)}) copy-start(bf16[6144,4]{0,1:T(4,128)(2,1)} %param.12) | copy-start | bytes 147460
  0.6 14.1 %copy-start.1 = (bf16[8,6144]{1,0:T(8,128)(2,1)S(1)}, bf16[8,6144]{1,0:T(8,128)(2,1)}, u32[]{:S(2)}) copy-start(bf16[8,6144]{1,0:T(8,128)(2,1)} %param.9) | copy-start | bytes 294916
  0.7 10.7 %collective-permute-start.1 = (bf16[8,6144]{1,0:T(8,128)(2,1)}, bf16[8,6144]{1,0:T(8,128)(2,1)S(1)}, u32[]{:S(2)}, u32[]{:S(2)}) collective-permute-start(bf16[8,6144]{1,0:T(8,128)(2,1)} %param.8), channel_id=1, source_target_pairs={{2,0},{3,1},{0,2},{1,3},{6,4},{7,5},{4,6},{5,7},{10,8},{11,9},{8,1... | collective-permute-start | bytes 294920 | tf_op jit(solution)/shard_map/ppermute | solution.py:112
  4.8 5.7 %collective-permute-start = (bf16[8,6144]{1,0:T(8,128)(2,1)}, bf16[8,6144]{1,0:T(8,128)(2,1)S(1)}, u32[]{:S(2)}, u32[]{:S(2)}) collective-permute-start(bf16[8,6144]{1,0:T(8,128)(2,1)} %param.8), channel_id=1, source_target_pairs={{1,0},{2,1},{3,2},{0,3},{5,4},{6,5},{7,6},{4,7},{9,8},{10,9},{11,1... | collective-permute-start | bytes 294920 | tf_op jit(solution)/shard_map/ppermute | solution.py:112
  6.1 7.0 %collective-permute-start.2 = (bf16[8,6144]{1,0:T(8,128)(2,1)}, bf16[8,6144]{1,0:T(8,128)(2,1)S(1)}, u32[]{:S(2)}, u32[]{:S(2)}) collective-permute-start(bf16[8,6144]{1,0:T(8,128)(2,1)} %param.8), channel_id=1, source_target_pairs={{3,0},{0,1},{1,2},{2,3},{7,4},{4,5},{5,6},{6,7},{11,8},{8,9},{9,10... | collective-permute-start | bytes 294920 | tf_op jit(solution)/shard_map/ppermute | solution.py:112
  13.2 19.4 %collective-permute-start.5 = (bf16[32,3072]{1,0:T(8,128)(2,1)S(1)}, bf16[32,3072]{1,0:T(8,128)(2,1)S(1)}, u32[]{:S(2)}, u32[]{:S(2)}) collective-permute-start(bf16[32,3072]{1,0:T(8,128)(2,1)S(1)} %get-tuple-element.77), channel_id=1, source_target_pairs={{8,0},{12,4},{0,8},{4,12},{9,1},{13,5},{1,9},{5,13},{10,2},{14,6},... | collective-permute-start | bytes 589832 | tf_op jit(solution)/shard_map/ppermute | solution.py:116
  31.1 7.3 %collective-permute-start.3 = (bf16[32,3072]{1,0:T(8,128)(2,1)S(1)}, bf16[32,3072]{1,0:T(8,128)(2,1)S(1)}, u32[]{:S(2)}, u32[]{:S(2)}) collective-permute-start(bf16[32,3072]{1,0:T(8,128)(2,1)S(1)} %get-tuple-element.78), channel_id=1, source_target_pairs={{16,0},{0,16},{17,1},{1,17},{18,2},{2,18},{19,3},{3,19},{20,4},{4,... | collective-permute-start | bytes 589832 | tf_op jit(solution)/shard_map/ppermute | solution.py:116
  33.4 9.4 %collective-permute-start.6 = (bf16[64,3072]{1,0:T(8,128)(2,1)}, bf16[64,3072]{1,0:T(8,128)(2,1)}, u32[]{:S(2)}, u32[]{:S(2)}) collective-permute-start(bf16[64,3072]{1,0:T(8,128)(2,1)} %pad_maximum_fusion.10), channel_id=1, source_target_pairs={{16,0},{0,16},{17,1},{1,17},{18,2},{2,18},{19,3},{3,19},{20,4},{4,... | collective-permute-start | bytes 1179656 | tf_op jit(solution)/shard_map/ppermute | solution.py:116
  39.3 8.0 %collective-permute-start.4 = (bf16[64,3072]{1,0:T(8,128)(2,1)}, bf16[64,3072]{1,0:T(8,128)(2,1)S(1)}, u32[]{:S(2)}, u32[]{:S(2)}) collective-permute-start(bf16[64,3072]{1,0:T(8,128)(2,1)} %pad_maximum_fusion.9), channel_id=1, source_target_pairs={{8,0},{12,4},{0,8},{4,12},{9,1},{13,5},{1,9},{5,13},{10,2},{14,6},... | collective-permute-start | bytes 1179656 | tf_op jit(solution)/shard_map/ppermute | solution.py:116
  47.3 10.9 %collective-permute-start.7 = (bf16[32,3200]{1,0:T(8,128)(2,1)S(1)}, bf16[32,3200]{1,0:T(8,128)(2,1)S(1)}, u32[]{:S(2)}, u32[]{:S(2)}) collective-permute-start(bf16[32,3200]{1,0:T(8,128)(2,1)S(1)} %slice.84), channel_id=1, source_target_pairs={{16,0},{0,16},{17,1},{1,17},{18,2},{2,18},{19,3},{3,19},{20,4},{4,... | collective-permute-start | bytes 614408 | tf_op jit(solution)/shard_map/ppermute | solution.py:116
  48.8 3.2 %collective-permute-start.9 = (bf16[128,3072]{1,0:T(8,128)(2,1)S(1)}, bf16[128,3072]{1,0:T(8,128)(2,1)S(1)}, u32[]{:S(2)}, u32[]{:S(2)}) collective-permute-start(bf16[128,3072]{1,0:T(8,128)(2,1)S(1)} %pad_maximum_fusion.3), channel_id=1, source_target_pairs={{4,0},{0,4},{12,8},{8,12},{5,1},{1,5},{13,9},{9,13},{6,2},{2,6},{1... | collective-permute-start | bytes 2359304 | tf_op jit(solution)/shard_map/ppermute | solution.py:116
  50.0 10.5 %collective-permute-start.12 = (bf16[128,3072]{1,0:T(8,128)(2,1)S(1)}, bf16[128,3072]{1,0:T(8,128)(2,1)S(1)}, u32[]{:S(2)}, u32[]{:S(2)}) collective-permute-start(bf16[128,3072]{1,0:T(8,128)(2,1)S(1)} %pad_maximum_fusion.4), channel_id=1, source_target_pairs={{4,0},{0,4},{12,8},{8,12},{5,1},{1,5},{13,9},{9,13},{6,2},{2,6},{1... | collective-permute-start | bytes 2359304 | tf_op jit(solution)/shard_map/ppermute | solution.py:116
  50.6 7.6 %collective-permute-start.8 = (bf16[32,3072]{1,0:T(8,128)(2,1)S(1)}, bf16[32,3072]{1,0:T(8,128)(2,1)S(1)}, u32[]{:S(2)}, u32[]{:S(2)}) collective-permute-start(bf16[32,3072]{1,0:T(8,128)(2,1)S(1)} %get-tuple-element.32), channel_id=1, source_target_pairs={{8,0},{12,4},{0,8},{4,12},{9,1},{13,5},{1,9},{5,13},{10,2},{14,6},... | collective-permute-start | bytes 589832 | tf_op jit(solution)/shard_map/ppermute | solution.py:116
  58.2 10.9 %collective-permute-start.11 = (bf16[64,3072]{1,0:T(8,128)(2,1)S(1)}, bf16[64,3072]{1,0:T(8,128)(2,1)S(1)}, u32[]{:S(2)}, u32[]{:S(2)}) collective-permute-start(bf16[64,3072]{1,0:T(8,128)(2,1)S(1)} %pad_maximum_fusion.11), channel_id=1, source_target_pairs={{16,0},{0,16},{17,1},{1,17},{18,2},{2,18},{19,3},{3,19},{20,4},{4,... | collective-permute-start | bytes 1179656 | tf_op jit(solution)/shard_map/ppermute | solution.py:116
  59.0 11.0 %collective-permute-start.10 = (bf16[64,3200]{1,0:T(8,128)(2,1)S(1)}, bf16[64,3200]{1,0:T(8,128)(2,1)S(1)}, u32[]{:S(2)}, u32[]{:S(2)}) collective-permute-start(bf16[64,3200]{1,0:T(8,128)(2,1)S(1)} %pad_maximum_fusion.7), channel_id=1, source_target_pairs={{8,0},{12,4},{0,8},{4,12},{9,1},{13,5},{1,9},{5,13},{10,2},{14,6},... | collective-permute-start | bytes 1228808 | tf_op jit(solution)/shard_map/ppermute | solution.py:116
  70.0 2.4 %collective-permute-start.14 = (bf16[128,3072]{1,0:T(8,128)(2,1)S(1)}, bf16[128,3072]{1,0:T(8,128)(2,1)S(1)}, u32[]{:S(2)}, u32[]{:S(2)}) collective-permute-start(bf16[128,3072]{1,0:T(8,128)(2,1)S(1)} %pad_maximum_fusion.5), channel_id=1, source_target_pairs={{4,0},{0,4},{12,8},{8,12},{5,1},{1,5},{13,9},{9,13},{6,2},{2,6},{1... | collective-permute-start | bytes 2359304 | tf_op jit(solution)/shard_map/ppermute | solution.py:116
  70.2 3.4 %collective-permute-start.13 = (bf16[128,3200]{1,0:T(8,128)(2,1)S(1)}, bf16[128,3200]{1,0:T(8,128)(2,1)S(1)}, u32[]{:S(2)}, u32[]{:S(2)}) collective-permute-start(bf16[128,3200]{1,0:T(8,128)(2,1)S(1)} %pad_maximum_fusion.2), channel_id=1, source_target_pairs={{4,0},{0,4},{12,8},{8,12},{5,1},{1,5},{13,9},{9,13},{6,2},{2,6},{1... | collective-permute-start | bytes 2457608 | tf_op jit(solution)/shard_map/ppermute | solution.py:116
  84.7 5.1 %collective-permute-start.18 = (bf16[128,3072]{1,0:T(8,128)(2,1)S(1)}, bf16[128,3072]{1,0:T(8,128)(2,1)S(1)}, u32[]{:S(2)}, u32[]{:S(2)}) collective-permute-start(bf16[128,3072]{1,0:T(8,128)(2,1)S(1)} %get-tuple-element.48), channel_id=1, source_target_pairs={{4,0},{0,4},{12,8},{8,12},{5,1},{1,5},{13,9},{9,13},{6,2},{2,6},{1... | collective-permute-start | bytes 2359304 | tf_op jit(solution)/shard_map/ppermute | solution.py:116
  89.5 3.8 %collective-permute-start.15 = (bf16[128,3200]{1,0:T(8,128)(2,1)S(1)}, bf16[128,3200]{1,0:T(8,128)(2,1)S(1)}, u32[]{:S(2)}, u32[]{:S(2)}) collective-permute-start(bf16[128,3200]{1,0:T(8,128)(2,1)S(1)} %get-tuple-element.45), channel_id=1, source_target_pairs={{4,0},{0,4},{12,8},{8,12},{5,1},{1,5},{13,9},{9,13},{6,2},{2,6},{1... | collective-permute-start | bytes 2457608 | tf_op jit(solution)/shard_map/ppermute | solution.py:116
  90.2 10.0 %collective-permute-start.22 = (bf16[64,1536]{1,0:T(8,128)(2,1)S(1)}, bf16[64,1536]{1,0:T(8,128)(2,1)S(1)}, u32[]{:S(2)}, u32[]{:S(2)}) collective-permute-start(bf16[64,1536]{1,0:T(8,128)(2,1)S(1)} %pad_maximum_fusion.13), channel_id=1, source_target_pairs={{16,0},{0,16},{17,1},{1,17},{18,2},{2,18},{19,3},{3,19},{20,4},{4,... | collective-permute-start | bytes 589832 | tf_op jit(solution)/shard_map/ppermute | solution.py:116
  91.7 7.8 %collective-permute-start.21 = (bf16[64,1536]{1,0:T(8,128)(2,1)S(1)}, bf16[64,1536]{1,0:T(8,128)(2,1)S(1)}, u32[]{:S(2)}, u32[]{:S(2)}) collective-permute-start(bf16[64,1536]{1,0:T(8,128)(2,1)S(1)} %concatenate.112), channel_id=1, source_target_pairs={{8,0},{12,4},{0,8},{4,12},{9,1},{13,5},{1,9},{5,13},{10,2},{14,6},... | collective-permute-start | bytes 589832 | tf_op jit(solution)/shard_map/ppermute | solution.py:116
  93.6 10.0 %collective-permute-start.16 = (bf16[64,1536]{1,0:T(8,128)(2,1)S(1)}, bf16[64,1536]{1,0:T(8,128)(2,1)S(1)}, u32[]{:S(2)}, u32[]{:S(2)}) collective-permute-start(bf16[64,1536]{1,0:T(8,128)(2,1)S(1)} %concatenate.110), channel_id=1, source_target_pairs={{8,0},{12,4},{0,8},{4,12},{9,1},{13,5},{1,9},{5,13},{10,2},{14,6},... | collective-permute-start | bytes 589832 | tf_op jit(solution)/shard_map/ppermute | solution.py:116
  94.2 9.5 %collective-permute-start.17 = (bf16[64,1664]{1,0:T(8,128)(2,1)S(1)}, bf16[64,1664]{1,0:T(8,128)(2,1)S(1)}, u32[]{:S(2)}, u32[]{:S(2)}) collective-permute-start(bf16[64,1664]{1,0:T(8,128)(2,1)S(1)} %pad_maximum_fusion.12), channel_id=1, source_target_pairs={{16,0},{0,16},{17,1},{1,17},{18,2},{2,18},{19,3},{3,19},{20,4},{4,... | collective-permute-start | bytes 638984 | tf_op jit(solution)/shard_map/ppermute | solution.py:116
  99.5 6.4 %collective-permute-start.26 = (bf16[32,1536]{1,0:T(8,128)(2,1)S(1)}, bf16[32,1536]{1,0:T(8,128)(2,1)S(1)}, u32[]{:S(2)}, u32[]{:S(2)}) collective-permute-start(bf16[32,1536]{1,0:T(8,128)(2,1)S(1)} %split.124), channel_id=1, source_target_pairs={{16,0},{0,16},{17,1},{1,17},{18,2},{2,18},{19,3},{3,19},{20,4},{4,... | collective-permute-start | bytes 294920 | tf_op jit(solution)/shard_map/ppermute | solution.py:116
  100.3 5.7 %collective-permute-start.27 = (bf16[32,1536]{1,0:T(8,128)(2,1)S(1)}, bf16[32,1536]{1,0:T(8,128)(2,1)S(1)}, u32[]{:S(2)}, u32[]{:S(2)}) collective-permute-start(bf16[32,1536]{1,0:T(8,128)(2,1)S(1)} %split.123), channel_id=1, source_target_pairs={{8,0},{12,4},{0,8},{4,12},{9,1},{13,5},{1,9},{5,13},{10,2},{14,6},... | collective-permute-start | bytes 294920 | tf_op jit(solution)/shard_map/ppermute | solution.py:116
  103.7 6.2 %collective-permute-start.19 = (bf16[32,1536]{1,0:T(8,128)(2,1)S(1)}, bf16[32,1536]{1,0:T(8,128)(2,1)S(1)}, u32[]{:S(2)}, u32[]{:S(2)}) collective-permute-start(bf16[32,1536]{1,0:T(8,128)(2,1)S(1)} %split.125), channel_id=1, source_target_pairs={{16,0},{0,16},{17,1},{1,17},{18,2},{2,18},{19,3},{3,19},{20,4},{4,... | collective-permute-start | bytes 294920 | tf_op jit(solution)/shard_map/ppermute | solution.py:116
  104.4 5.5 %collective-permute-start.20 = (bf16[32,1664]{1,0:T(8,128)(2,1)S(1)}, bf16[32,1664]{1,0:T(8,128)(2,1)S(1)}, u32[]{:S(2)}, u32[]{:S(2)}) collective-permute-start(bf16[32,1664]{1,0:T(8,128)(2,1)S(1)} %split.122), channel_id=1, source_target_pairs={{8,0},{12,4},{0,8},{4,12},{9,1},{13,5},{1,9},{5,13},{10,2},{14,6},... | collective-permute-start | bytes 319496 | tf_op jit(solution)/shard_map/ppermute | solution.py:116
  106.1 7.9 %collective-permute-start.28 = (bf16[8,3072]{1,0:T(8,128)(2,1)S(1)}, bf16[8,3072]{1,0:T(8,128)(2,1)S(1)}, u32[]{:S(2)}, u32[]{:S(2)}) collective-permute-start(bf16[8,3072]{1,0:T(8,128)(2,1)S(1)} %get-tuple-element.82), channel_id=1, source_target_pairs={{3,0},{0,1},{1,2},{2,3},{7,4},{4,5},{5,6},{6,7},{11,8},{8,9},{9,10... | collective-permute-start | bytes 147464 | tf_op jit(solution)/shard_map/ppermute | solution.py:112
  106.1 9.0 %collective-permute-start.30 = (bf16[8,3072]{1,0:T(8,128)(2,1)S(1)}, bf16[8,3072]{1,0:T(8,128)(2,1)S(1)}, u32[]{:S(2)}, u32[]{:S(2)}) collective-permute-start(bf16[8,3072]{1,0:T(8,128)(2,1)S(1)} %get-tuple-element.83), channel_id=1, source_target_pairs={{1,0},{2,1},{3,2},{0,3},{5,4},{6,5},{7,6},{4,7},{9,8},{10,9},{11,1... | collective-permute-start | bytes 147464 | tf_op jit(solution)/shard_map/ppermute | solution.py:112
  109.9 6.5 %collective-permute-start.29 = (bf16[8,3072]{1,0:T(8,128)(2,1)S(1)}, bf16[8,3072]{1,0:T(8,128)(2,1)S(1)}, u32[]{:S(2)}, u32[]{:S(2)}) collective-permute-start(bf16[8,3072]{1,0:T(8,128)(2,1)S(1)} %get-tuple-element.84), channel_id=1, source_target_pairs={{2,0},{3,1},{0,2},{1,3},{6,4},{7,5},{4,6},{5,7},{10,8},{11,9},{8,1... | collective-permute-start | bytes 147464 | tf_op jit(solution)/shard_map/ppermute | solution.py:112
  110.0 9.3 %copy-start.2 = (s32[8]{0:T(128)S(1)}, s32[8]{0:T(128)}, u32[]{:S(2)}) copy-start(s32[8]{0:T(128)} %param.10) | copy-start | bytes 100
  110.1 6.3 %collective-permute-start.23 = (bf16[8,3200]{1,0:T(8,128)(2,1)S(1)}, bf16[8,3200]{1,0:T(8,128)(2,1)S(1)}, u32[]{:S(2)}, u32[]{:S(2)}) collective-permute-start(bf16[8,3200]{1,0:T(8,128)(2,1)S(1)} %get-tuple-element.79), channel_id=1, source_target_pairs={{3,0},{0,1},{1,2},{2,3},{7,4},{4,5},{5,6},{6,7},{11,8},{8,9},{9,10... | collective-permute-start | bytes 153608 | tf_op jit(solution)/shard_map/ppermute | solution.py:112
  110.7 6.1 %collective-permute-start.25 = (bf16[8,3200]{1,0:T(8,128)(2,1)S(1)}, bf16[8,3200]{1,0:T(8,128)(2,1)S(1)}, u32[]{:S(2)}, u32[]{:S(2)}) collective-permute-start(bf16[8,3200]{1,0:T(8,128)(2,1)S(1)} %get-tuple-element.80), channel_id=1, source_target_pairs={{1,0},{2,1},{3,2},{0,3},{5,4},{6,5},{7,6},{4,7},{9,8},{10,9},{11,1... | collective-permute-start | bytes 153608 | tf_op jit(solution)/shard_map/ppermute | solution.py:112
  114.0 5.0 %collective-permute-start.24 = (bf16[8,3200]{1,0:T(8,128)(2,1)S(1)}, bf16[8,3200]{1,0:T(8,128)(2,1)S(1)}, u32[]{:S(2)}, u32[]{:S(2)}) collective-permute-start(bf16[8,3200]{1,0:T(8,128)(2,1)S(1)} %get-tuple-element.81), channel_id=1, source_target_pairs={{2,0},{3,1},{0,2},{1,3},{6,4},{7,5},{4,6},{5,7},{10,8},{11,9},{8,1... | collective-permute-start | bytes 153608 | tf_op jit(solution)/shard_map/ppermute | solution.py:112

commit v7 on v5

--- a/solution.py
+++ b/solution.py
@@ -196,59 +196,77 @@
     return pltpu.with_memory_space_constraint(value, pltpu.HBM)
 
 
-def token_kernel(first, tokens, gate_weight, up_weight, *refs):
-    before, (pre_gate, pre_up, gate_copy, up_copy, gate_sems, up_sems) = refs[:-6], refs[-6:]
-    width = tokens.shape[1]
-    depth = part_of(width, TOKEN_PART)
-    steps = width // depth
-
-    def copies(index):
-        source = pl.ds(pl.multiple_of(first + index * depth, depth), depth)
-        rows = pl.ds(pl.multiple_of(index * depth, depth), depth)
-        return (
-            pltpu.make_async_copy(gate_weight.at[0, source], gate_copy.at[rows], gate_sems.at[index]),
-            pltpu.make_async_copy(up_weight.at[0, source], up_copy.at[rows], up_sems.at[index]),
-        )
-
-    @pl.loop(0, steps)
-    def _(index):
-        for copy in copies(index):
-            copy.start()
-
-    pre_gate[...] = before[0][...] if before else jnp.zeros_like(pre_gate)
-    pre_up[...] = before[1][...] if before else jnp.zeros_like(pre_up)
-
-    @pl.loop(0, steps)
+def fetch_kernel(first, *refs):
+    count = (len(refs) - 1) // 2
+    sems = refs[-1]
+    copies = []
+    for index in range(count):
+        target = refs[count + index]
+        source = refs[index].at[0, pl.ds(first, target.shape[0])]
+        copies.append(pltpu.make_async_copy(source, target, sems.at[index]))
+    for copy in copies:
+        copy.start()
+    for copy in copies:
+        copy.wait()
+
+
+def fetch(first, length, *weights):
+    shapes = [(length, value.shape[2]) for value in weights]
+    return pl.pallas_call(
+        functools.partial(fetch_kernel, first),
+        out_shape=tuple(pltpu.VMEM(shape, jnp.bfloat16) for shape in shapes),
+        in_specs=[pl.BlockSpec(memory_space=pl.ANY)] * len(weights),
+        out_specs=(pl.BlockSpec(memory_space=pltpu.VMEM),) * len(weights),
+        scratch_shapes=[pltpu.SemaphoreType.DMA((len(weights),))],
+        compiler_params=pltpu.CompilerParams(vmem_limit_bytes=TOKEN_VMEM),
+        cost_estimate=pl.CostEstimate(
+            flops=0, bytes_accessed=sum(2 * rows * hidden for rows, hidden in shapes), transcendentals=0
+        ),
+    )(*[in_hbm(value) for value in weights])
+
+
+def token_kernel(first, tokens, gate, up, *refs):
+    pre_gate, pre_up = refs[2:4]
+    depth = part_of(tokens.shape[1], TOKEN_PART)
+    copies = []
+    if first:
+        for index in range(2):
+            source = refs[index].at[0, pl.ds(first, gate.shape[0])]
+            copies.append(pltpu.make_async_copy(source, refs[4 + index], refs[6].at[index]))
+    for copy in copies:
+        copy.start()
+    pre_gate[...] = jnp.zeros_like(pre_gate) if first else refs[0][...]
+    pre_up[...] = jnp.zeros_like(pre_up) if first else refs[1][...]
+
+    @pl.loop(0, tokens.shape[1] // depth)
     def _(step):
-        for copy in copies(step):
-            copy.wait()
         rows = pl.ds(pl.multiple_of(step * depth, depth), depth)
-        pre_gate[...] += product(tokens[:, rows], gate_copy[rows, :], 0)
-        pre_up[...] += product(tokens[:, rows], up_copy[rows, :], 0)
-
-
-def multiply_tokens(first, tokens, gate_weight, up_weight, *before):
+        pre_gate[...] += product(tokens[:, rows], gate[rows, :], 0)
+        pre_up[...] += product(tokens[:, rows], up[rows, :], 0)
+
+    for copy in copies:
+        copy.wait()
+
+
+def multiply_tokens(tokens, gate, up, first, *others):
     rows, width = tokens.shape
-    hidden = gate_weight.shape[2]
-    steps = width // part_of(width, TOKEN_PART)
+    hidden = gate.shape[1]
+    sums = (pltpu.VMEM((rows, hidden), jnp.float32),) * 2
+    fetched = (pltpu.VMEM(gate.shape, jnp.bfloat16),) * 2 if first else ()
+    if first:
+        others = [in_hbm(value) for value in others]
     return pl.pallas_call(
         functools.partial(token_kernel, first),
-        out_shape=(
-            pltpu.VMEM((rows, hidden), jnp.float32),
-            pltpu.VMEM((rows, hidden), jnp.float32),
-            pltpu.VMEM((width, hidden), jnp.bfloat16),
-            pltpu.VMEM((width, hidden), jnp.bfloat16),
-        ),
-        in_specs=[pl.BlockSpec(memory_space=pltpu.VMEM)]
-        + [pl.BlockSpec(memory_space=pl.ANY)] * 2
-        + [pl.BlockSpec(memory_space=pltpu.VMEM)] * len(before),
-        out_specs=(pl.BlockSpec(memory_space=pltpu.VMEM),) * 4,
-        scratch_shapes=[pltpu.SemaphoreType.DMA((steps,)), pltpu.SemaphoreType.DMA((steps,))],
+        out_shape=sums + fetched,
+        in_specs=[pl.BlockSpec(memory_space=pltpu.VMEM)] * 3
+        + [pl.BlockSpec(memory_space=pl.ANY if first else pltpu.VMEM)] * 2,
+        out_specs=(pl.BlockSpec(memory_space=pltpu.VMEM),) * len(sums + fetched),
+        scratch_shapes=[pltpu.SemaphoreType.DMA((2,))] if first else [],
         compiler_params=pltpu.CompilerParams(vmem_limit_bytes=TOKEN_VMEM),
         cost_estimate=pl.CostEstimate(
-            flops=4 * rows * width * hidden, bytes_accessed=4 * width * hidden, transcendentals=0
-        ),
-    )(tokens, in_hbm(gate_weight), in_hbm(up_weight), *before)
+            flops=4 * rows * width * hidden, bytes_accessed=2 * rows * width, transcendentals=0
+        ),
+    )(tokens, gate, up, *others)
 
 
 def grad_kernel(
@@ -374,20 +392,21 @@
     gate_table = (first_hot * gate_first[:, None] + second_hot * gate_second[:, None]) * keep_rows[:, None]
     gate_table = jnp.pad(gate_table.astype(jnp.bfloat16), ((0, 0), (0, table - expert_count)))
     grad_z = gather_z(after_others(jnp.concatenate([gate_table, out_grad], axis=1), token_z[1]))
+    gate_low, up_low = fetch(0, half, gate_weight, up_weight)
     token_near = gather_near(token_z, half)
-    token_far = gather_far(*after_others(token_near, grad_z[1]))
-    grad_near = gather_near(after_others(grad_z, token_far), half + table)
+    token_far = after_others(gather_far(*token_near), (gate_low, up_low))
+    grad_near = gather_near(grad_z, half + table)
+    grad_far = gather_far(*grad_near)
     token_low, token_high = gather_core(token_near[0], token_far[0], token_near[1], token_far[1])
-    before = multiply_tokens(0, token_low, gate_weight, up_weight)
-    grad_far = gather_far(*after_others(grad_near, before[0]))
-    after = multiply_tokens(half, token_high, gate_weight, up_weight, before[0], before[1])
-    grad_far = after_others(grad_far, after[0])
+    pre_gate, pre_up, gate_high, up_high = multiply_tokens(token_low, gate_low, up_low, half, gate_weight, up_weight)
+    grad_far = after_others(grad_far, pre_gate)
+    pre_gate, pre_up = multiply_tokens(token_high, gate_high, up_high, 0, pre_gate, pre_up)
     grad_halves = gather_core(grad_near[0], grad_far[0], grad_near[1], grad_far[1])
     expert = lax.axis_index("expert").astype(jnp.int32).reshape(1)
-    grad_gate, grad_up, dots = multiply_grads(expert, *grad_halves, after[0], after[1], down_weight)
-    kept, sent = multiply_outputs(grad_gate, grad_up, before[2], before[3], dots)
+    grad_gate, grad_up, dots = multiply_grads(expert, *grad_halves, pre_gate, pre_up, down_weight)
+    kept, sent = multiply_outputs(grad_gate, grad_up, gate_low, up_low, dots)
     chunk = scatter_core(kept, sent)
-    kept, sent = multiply_outputs(grad_gate, grad_up, after[2], after[3])
+    kept, sent = multiply_outputs(grad_gate, grad_up, gate_high, up_high)
     chunk = scatter_far(after_others(chunk, sent), half // 2)
     later = scatter_core(kept, sent)
     chunk = scatter_near(*after_others(chunk, later))

time: 107 us -> 107 us (level)
  starting transfers between devices: 41 us -> 37.9 us
  Pallas kernels: 27.6 us -> 29.5 us
    ppermute x22, waiting for transfers between devices: 12.9 us -> 20.7 us  [swap(): lax.ppermute(value, axis, [(i ^ bit, i) for i in range(lax.axis_size(axis...]
    ppermute x12, waiting for transfers between devices: 14.2 us -> 7.09 us  [shift(): lax.ppermute(value, axis, [((i + step) % size, i) for i in range(size)])]
    ppermute x22, starting transfers between devices: 20.8 us -> 18.9 us  [swap(): lax.ppermute(value, axis, [(i ^ bit, i) for i in range(lax.axis_size(axis...]
    unnamed x18 -> x22, local copies, waits for them, and re-layouts: 1.14 us -> 2.84 us
    pallas_call x2 -> x3, Pallas kernels: 12.1 us -> 13.7 us  [the longest x2 9.1 us: multiply_tokens(): pl.pallas_call(functools.partial(token_kernel, first), out_shape=sums + f...]
    ppermute x12, starting transfers between devices: 20.3 us -> 19 us  [shift(): lax.ppermute(value, axis, [((i + step) % size, i) for i in range(size)])]
  transfers between devices with their start and end apart: 34 -> 34, of which waited for: 14 -> 11; matrix products, arithmetic and copies ran while one was open for 6% -> 6% of each run, Pallas kernels for 15% -> 17%
where the time goes in v7:
time: 107 us
  starting transfers between devices  37.9 us (35%)
  Pallas kernels  29.5 us (28%)
  waiting for transfers between devices  27.8 us (26%)
  local copies, waits for them, and re-layouts  4.02 us (4%)
  other arithmetic  3.91 us (4%)
  matrix products  2.15 us (2%)
  between operations  1.26 us (1%)
    ppermute x22, waiting for transfers between devices, swap(): lax.ppermute(value, axis, [(i ^ bit, i) for i in range(lax.axis_size(axis...  20.7 us
    ppermute x12, starting transfers between devices, shift(): lax.ppermute(value, axis, [((i + step) % size, i) for i in range(size)])  19 us
    ppermute x22, starting transfers between devices, swap(): lax.ppermute(value, axis, [(i ^ bit, i) for i in range(lax.axis_size(axis...  18.9 us
    pallas_call x2, Pallas kernels, multiply_tokens(): pl.pallas_call(functools.partial(token_kernel, first), out_shape=sums + f...  9.1 us
    pallas_call x2, Pallas kernels, multiply_outputs(): pl.pallas_call(output_kernel, out_shape=(pltpu.VMEM((rows // 2, total), j...  9 us
    ppermute x12, waiting for transfers between devices, shift(): lax.ppermute(value, axis, [((i + step) % size, i) for i in range(size)])  7.09 us
    pallas_call x1, Pallas kernels, multiply_grads(): pl.pallas_call(grad_kernel, out_shape=(pltpu.VMEM((rows, hidden), jnp.bfl...  6.75 us
    pallas_call x1, Pallas kernels, fetch(): pl.pallas_call(functools.partial(fetch_kernel, first), out_shape=tuple((p...  4.62 us
  transfers between devices with their start and end apart: 34, of which 11 were waited for; matrix products, arithmetic and copies ran while one was open for 6% of the time, Pallas kernels for 17%

profile of v7, /device:TPU:0, one launch (start us, length us, event | category | flops | bytes accessed | tf_op | source)
XLA Modules:
  0.0 106.5 jit_solution(15312291220948544557)
XLA Ops:
  0.6 5.1 %collective-permute-start = (bf16[8,6144]{1,0:T(8,128)(2,1)}, bf16[8,6144]{1,0:T(8,128)(2,1)S(1)}, u32[]{:S(2)}, u32[]{:S(2)}) collective-permute-start(bf16[8,6144]{1,0:T(8,128)(2,1)} %param.8), channel_id=1, source_target_pairs={{1,0},{2,1},{3,2},{0,3},{5,4},{6,5},{7,6},{4,7},{9,8},{10,9},{11,1... | collective-permute-start | bytes 294920 | tf_op jit(solution)/shard_map/ppermute | solution.py:112
  5.8 1.0 collective-permute-start.9
  6.8 0.8 slice_bitcast_fusion
  7.5 0.7 convert_element_type.76
  8.2 1.2 %select_reduce_fusion.3 = (f32[8]{0:T(128)S(1)}, f32[8]{0:T(128)S(1)}) fusion(s32[8]{0:T(128)S(1)} %get-tuple-element.86, s32[8]{0:T(128)S(1)} %get-tuple-element.85, bf16[8,6144]{1,0:T(8,128)(2,1)} %param.8, bf16[6144,4]{0,1:T(4,128)(2,1)S(1)} %copy-done), kind=kOutput, calls=%fused_computation.69 | convolution fusion | flops 393392 | bytes 147584 | tf_op jit(solution)/shard_map/dot_general | solution.py:387
  9.5 0.9 fusion.4
  10.4 0.9 constant_dynamic-update-slice_fusion.7
  11.3 4.6 %shard_map.95 = (bf16[3072,1024]{1,0:T(8,128)(2,1)S(1)}, bf16[3072,1024]{1,0:T(8,128)(2,1)S(1)}) custom-call(bf16[1,6144,1024]{2,1,0:T(8,128)(2,1)} %refs_0_.3, bf16[1,6144,1024]{2,1,0:T(8,128)(2,1)} %refs_1_.3), custom_call_target="tpu_custom_call" | custom-call | bytes 12582912 | tf_op jit(solution)/shard_map/pallas_call | solution.py:215
  16.0 2.9 %collective-permute-start.1 = (bf16[8,6272]{1,0:T(8,128)(2,1)S(1)}, bf16[8,6272]{1,0:T(8,128)(2,1)S(1)}, u32[]{:S(2)}, u32[]{:S(2)}) collective-permute-start(bf16[8,6272]{1,0:T(8,128)(2,1)S(1)} %fusion.4), channel_id=1, source_target_pairs={{1,0},{2,1},{3,2},{0,3},{5,4},{6,5},{7,6},{4,7},{9,8},{10,9},{11,1... | collective-permute-start | bytes 301064 | tf_op jit(solution)/shard_map/ppermute | solution.py:112
  18.8 1.1 %collective-permute-start.2 = (bf16[8,6272]{1,0:T(8,128)(2,1)S(1)}, bf16[8,6272]{1,0:T(8,128)(2,1)S(1)}, u32[]{:S(2)}, u32[]{:S(2)}) collective-permute-start(bf16[8,6272]{1,0:T(8,128)(2,1)S(1)} %fusion.4), channel_id=1, source_target_pairs={{2,0},{3,1},{0,2},{1,3},{6,4},{7,5},{4,6},{5,7},{10,8},{11,9},{8,1... | collective-permute-start | bytes 301064 | tf_op jit(solution)/shard_map/ppermute | solution.py:112
  20.1 1.6 %collective-permute-start.10 = (bf16[32,3072]{1,0:T(8,128)(2,1)S(1)}, bf16[32,3072]{1,0:T(8,128)(2,1)S(1)}, u32[]{:S(2)}, u32[]{:S(2)}) collective-permute-start(bf16[32,3072]{1,0:T(8,128)(2,1)S(1)} %get-tuple-element.71), channel_id=1, source_target_pairs={{16,0},{0,16},{17,1},{1,17},{18,2},{2,18},{19,3},{3,19},{20,4},{4,... | collective-permute-start | bytes 589832 | tf_op jit(solution)/shard_map/ppermute | solution.py:116
  21.6 1.5 %collective-permute-start.12 = (bf16[32,3072]{1,0:T(8,128)(2,1)S(1)}, bf16[32,3072]{1,0:T(8,128)(2,1)S(1)}, u32[]{:S(2)}, u32[]{:S(2)}) collective-permute-start(bf16[32,3072]{1,0:T(8,128)(2,1)S(1)} %get-tuple-element.70), channel_id=1, source_target_pairs={{8,0},{12,4},{0,8},{4,12},{9,1},{13,5},{1,9},{5,13},{10,2},{14,6},... | collective-permute-start | bytes 589832 | tf_op jit(solution)/shard_map/ppermute | solution.py:116
  23.2 5.1 %collective-permute-done.2 = bf16[8,6272]{1,0:T(8,128)(2,1)S(1)} collective-permute-done((bf16[8,6272]{1,0:T(8,128)(2,1)S(1)}, bf16[8,6272]{1,0:T(8,128)(2,1)S(1)}, u32[]{:S(2)}, u32[]{:S(2)}) %collective-permute-start.2) | collective-permute-done | bytes 100384 | tf_op jit(solution)/shard_map/ppermute | solution.py:112
  28.3 1.6 %collective-permute-start.6 = (bf16[32,3072]{1,0:T(8,128)(2,1)S(1)}, bf16[32,3072]{1,0:T(8,128)(2,1)S(1)}, u32[]{:S(2)}, u32[]{:S(2)}) collective-permute-start(bf16[32,3072]{1,0:T(8,128)(2,1)S(1)} %get-tuple-element.65), channel_id=1, source_target_pairs={{8,0},{12,4},{0,8},{4,12},{9,1},{13,5},{1,9},{5,13},{10,2},{14,6},... | collective-permute-start | bytes 589832 | tf_op jit(solution)/shard_map/ppermute | solution.py:116
  29.9 1.5 %collective-permute-start.4 = (bf16[32,3200]{1,0:T(8,128)(2,1)S(1)}, bf16[32,3200]{1,0:T(8,128)(2,1)S(1)}, u32[]{:S(2)}, u32[]{:S(2)}) collective-permute-start(bf16[32,3200]{1,0:T(8,128)(2,1)S(1)} %slice.96), channel_id=1, source_target_pairs={{16,0},{0,16},{17,1},{1,17},{18,2},{2,18},{19,3},{3,19},{20,4},{4,... | collective-permute-start | bytes 614408 | tf_op jit(solution)/shard_map/ppermute | solution.py:116
  31.5 0.6 collective-permute-start.11
  32.1 0.6 collective-permute-start.13
  32.7 3.3 %collective-permute-done.6 = bf16[32,3072]{1,0:T(8,128)(2,1)S(1)} collective-permute-done((bf16[32,3072]{1,0:T(8,128)(2,1)S(1)}, bf16[32,3072]{1,0:T(8,128)(2,1)S(1)}, u32[]{:S(2)}, u32[]{:S(2)}) %collective-permute-start.6) | collective-permute-done | bytes 196640 | tf_op jit(solution)/shard_map/ppermute | solution.py:116
  36.0 1.9 %collective-permute-start.7 = (bf16[64,3072]{1,0:T(8,128)(2,1)S(1)}, bf16[64,3072]{1,0:T(8,128)(2,1)S(1)}, u32[]{:S(2)}, u32[]{:S(2)}) collective-permute-start(bf16[64,3072]{1,0:T(8,128)(2,1)S(1)} %pad_maximum_fusion.9), channel_id=1, source_target_pairs={{16,0},{0,16},{17,1},{1,17},{18,2},{2,18},{19,3},{3,19},{20,4},{4,... | collective-permute-start | bytes 1179656 | tf_op jit(solution)/shard_map/ppermute | solution.py:116
  38.0 1.5 %collective-permute-start.5 = (bf16[64,3200]{1,0:T(8,128)(2,1)S(1)}, bf16[64,3200]{1,0:T(8,128)(2,1)S(1)}, u32[]{:S(2)}, u32[]{:S(2)}) collective-permute-start(bf16[64,3200]{1,0:T(8,128)(2,1)S(1)} %pad_maximum_fusion.7), channel_id=1, source_target_pairs={{8,0},{12,4},{0,8},{4,12},{9,1},{13,5},{1,9},{5,13},{10,2},{14,6},... | collective-permute-start | bytes 1228808 | tf_op jit(solution)/shard_map/ppermute | solution.py:116
  39.5 4.9 %collective-permute-done.11 = bf16[64,3072]{1,0:T(8,128)(2,1)S(1)} collective-permute-done((bf16[64,3072]{1,0:T(8,128)(2,1)S(1)}, bf16[64,3072]{1,0:T(8,128)(2,1)S(1)}, u32[]{:S(2)}, u32[]{:S(2)}) %collective-permute-start.11) | collective-permute-done | bytes 393248 | tf_op jit(solution)/shard_map/ppermute | solution.py:116
  44.4 2.0 %collective-permute-done.13 = bf16[64,3072]{1,0:T(8,128)(2,1)S(1)} collective-permute-done((bf16[64,3072]{1,0:T(8,128)(2,1)S(1)}, bf16[64,3072]{1,0:T(8,128)(2,1)S(1)}, u32[]{:S(2)}, u32[]{:S(2)}) %collective-permute-start.13) | collective-permute-done | bytes 393248 | tf_op jit(solution)/shard_map/ppermute | solution.py:116
  46.6 0.6 collective-permute-start.14
  47.2 2.7 %collective-permute-done.14 = bf16[128,3072]{1,0:T(8,128)(2,1)S(1)} collective-permute-done((bf16[128,3072]{1,0:T(8,128)(2,1)S(1)}, bf16[128,3072]{1,0:T(8,128)(2,1)S(1)}, u32[]{:S(2)}, u32[]{:S(2)}) %collective-permute-start.14) | collective-permute-done | bytes 786464 | tf_op jit(solution)/shard_map/ppermute | solution.py:116
  50.1 4.6 %shard_map.96 = (f32[256,1024]{1,0:T(8,128)S(1)}, f32[256,1024]{1,0:T(8,128)S(1)}, bf16[3072,1024]{1,0:T(8,128)(2,1)S(1)}, bf16[3072,1024]{1,0:T(8,128)(2,1)S(1)}) custom-call(bf16[256,3072]{1,0:T(8,128)(2,1)S(1)} %pad_maximum_fusion.1.tokens, bf16[3072,1024]{1,0:T(8,128)(2,1)S(1)} %get-tuple-element.27.gate.gate_copy, ...), custom_call_target="tpu_custom_call" | custom-call | flops 3221225472 | bytes 1572864 | tf_op jit(solution)/shard_map/pallas_call | solution.py:258
  55.6 1.7 %copy-done.1 = bf16[3072,1024]{1,0:T(8,128)(2,1)} copy-done((bf16[3072,1024]{1,0:T(8,128)(2,1)}, bf16[3072,1024]{1,0:T(8,128)(2,1)S(1)}, u32[]{:S(2)}) %copy-start.1) | copy-done | bytes 6291480
  57.4 4.5 %shard_map.97 = (f32[256,1024]{1,0:T(8,128)S(1)}, f32[256,1024]{1,0:T(8,128)S(1)}) custom-call(bf16[256,3072]{1,0:T(8,128)(2,1)S(1)} %constant_dynamic-update-slice_fusion.13.tokens, bf16[3072,1024]{1,0:T(8,128)(2,1)S(1)} %get-tuple-element.34.gate.gate_copy, bf16[3072,1024]{1,0:T(8,128)(2,1)S(1)} %get-tuple-element.35.up.up_copy, ...), custom_call_target="tpu_custom_call" | custom-call | flops 3221225472 | bytes 1572864 | tf_op jit(solution)/shard_map/pallas_call | solution.py:258
  62.1 6.8 %shard_map.98 = (bf16[256,1024]{1,0:T(8,128)(2,1)S(1)}, bf16[256,1024]{1,0:T(8,128)(2,1)S(1)}, bf16[256,128]{1,0:T(8,128)(2,1)S(1)}) custom-call(s32[1]{0:T(128)} %bitcast.expert, bf16[256,3200]{1,0:T(8,128)(2,1)S(1)} %pad_maximum_fusion.low, bf16[256,3072]{1,0:T(8,128)(2,1)S(1)} %constant_dynamic-update-slice_fusion.8.high, ...), custom_call_target="tpu_custom_call" | custom-call | flops 3221225472 | bytes 12582912 | tf_op jit(solution)/shard_map/pallas_call | solution.py:316
  68.9 4.5 %shard_map.100 = (f32[128,3072]{1,0:T(8,128)S(1)}, bf16[128,3072]{1,0:T(8,128)(2,1)S(1)}) custom-call(bf16[256,1024]{1,0:T(8,128)(2,1)S(1)} %get-tuple-element.39.grad_gate, bf16[256,1024]{1,0:T(8,128)(2,1)S(1)} %get-tuple-element.40.grad_up, bf16[3072,1024]{1,0:T(8,128)(2,1)S(1)} %bitcast.11, bf16[3072,1024]{1,0:T(8,128)(2,1)S(1)} %get-tuple-element.35.up.up_copy), custom_call_target="tpu_custom_call" | custom-call | flops 3221225472 | bytes 3145728 | tf_op jit(solution)/shard_map/pallas_call | solution.py:362
  73.6 4.5 %shard_map.99 = (f32[128,3200]{1,0:T(8,128)S(1)}, bf16[128,3200]{1,0:T(8,128)(2,1)S(1)}) custom-call(bf16[256,1024]{1,0:T(8,128)(2,1)S(1)} %get-tuple-element.39.grad_gate, bf16[256,1024]{1,0:T(8,128)(2,1)S(1)} %get-tuple-element.40.grad_up, bf16[3072,1024]{1,0:T(8,128)(2,1)S(1)} %get-tuple-element.27.gate.gate_copy, ...), custom_call_target="tpu_custom_call" | custom-call | flops 3221225472 | bytes 3145728 | tf_op jit(solution)/shard_map/pallas_call | solution.py:362
  78.9 1.6 %collective-permute-start.25 = (bf16[64,1536]{1,0:T(8,128)(2,1)S(1)}, bf16[64,1536]{1,0:T(8,128)(2,1)S(1)}, u32[]{:S(2)}, u32[]{:S(2)}) collective-permute-start(bf16[64,1536]{1,0:T(8,128)(2,1)S(1)} %pad_maximum_fusion.13), channel_id=1, source_target_pairs={{16,0},{0,16},{17,1},{1,17},{18,2},{2,18},{19,3},{3,19},{20,4},{4,... | collective-permute-start | bytes 589832 | tf_op jit(solution)/shard_map/ppermute | solution.py:116
  80.4 0.5 collective-permute-start.24
  81.3 1.1 %collective-permute-start.20 = (bf16[64,1664]{1,0:T(8,128)(2,1)S(1)}, bf16[64,1664]{1,0:T(8,128)(2,1)S(1)}, u32[]{:S(2)}, u32[]{:S(2)}) collective-permute-start(bf16[64,1664]{1,0:T(8,128)(2,1)S(1)} %pad_maximum_fusion.12), channel_id=1, source_target_pairs={{16,0},{0,16},{17,1},{1,17},{18,2},{2,18},{19,3},{3,19},{20,4},{4,... | collective-permute-start | bytes 638984 | tf_op jit(solution)/shard_map/ppermute | solution.py:116
  82.4 1.0 collective-permute-start.19
  83.4 3.2 %collective-permute-done.25 = bf16[64,1536]{1,0:T(8,128)(2,1)S(1)} collective-permute-done((bf16[64,1536]{1,0:T(8,128)(2,1)S(1)}, bf16[64,1536]{1,0:T(8,128)(2,1)S(1)}, u32[]{:S(2)}, u32[]{:S(2)}) %collective-permute-start.25) | collective-permute-done | bytes 196640 | tf_op jit(solution)/shard_map/ppermute | solution.py:116
  86.7 0.4 collective-permute-start.30
  87.2 1.0 collective-permute-done.24
  88.3 0.7 collective-permute-start.29
  88.9 3.4 %collective-permute-done.19 = bf16[64,1536]{1,0:T(8,128)(2,1)S(1)} collective-permute-done((bf16[64,1536]{1,0:T(8,128)(2,1)S(1)}, bf16[64,1536]{1,0:T(8,128)(2,1)S(1)}, u32[]{:S(2)}, u32[]{:S(2)}) %collective-permute-start.19) | collective-permute-done | bytes 196640 | tf_op jit(solution)/shard_map/ppermute | solution.py:116
  92.5 0.6 collective-permute-start.22
  93.7 1.5 %collective-permute-start.32 = (bf16[8,3072]{1,0:T(8,128)(2,1)S(1)}, bf16[8,3072]{1,0:T(8,128)(2,1)S(1)}, u32[]{:S(2)}, u32[]{:S(2)}) collective-permute-start(bf16[8,3072]{1,0:T(8,128)(2,1)S(1)} %get-tuple-element.80), channel_id=1, source_target_pairs={{2,0},{3,1},{0,2},{1,3},{6,4},{7,5},{4,6},{5,7},{10,8},{11,9},{8,1... | collective-permute-start | bytes 147464 | tf_op jit(solution)/shard_map/ppermute | solution.py:112
  95.2 2.7 %collective-permute-start.33 = (bf16[8,3072]{1,0:T(8,128)(2,1)S(1)}, bf16[8,3072]{1,0:T(8,128)(2,1)S(1)}, u32[]{:S(2)}, u32[]{:S(2)}) collective-permute-start(bf16[8,3072]{1,0:T(8,128)(2,1)S(1)} %get-tuple-element.79), channel_id=1, source_target_pairs={{1,0},{2,1},{3,2},{0,3},{5,4},{6,5},{7,6},{4,7},{9,8},{10,9},{11,1... | collective-permute-start | bytes 147464 | tf_op jit(solution)/shard_map/ppermute | solution.py:112
  98.3 1.5 %collective-permute-start.27 = (bf16[8,3200]{1,0:T(8,128)(2,1)S(1)}, bf16[8,3200]{1,0:T(8,128)(2,1)S(1)}, u32[]{:S(2)}, u32[]{:S(2)}) collective-permute-start(bf16[8,3200]{1,0:T(8,128)(2,1)S(1)} %get-tuple-element.77), channel_id=1, source_target_pairs={{2,0},{3,1},{0,2},{1,3},{6,4},{7,5},{4,6},{5,7},{10,8},{11,9},{8,1... | collective-permute-start | bytes 153608 | tf_op jit(solution)/shard_map/ppermute | solution.py:112
  99.9 2.8 %collective-permute-start.28 = (bf16[8,3200]{1,0:T(8,128)(2,1)S(1)}, bf16[8,3200]{1,0:T(8,128)(2,1)S(1)}, u32[]{:S(2)}, u32[]{:S(2)}) collective-permute-start(bf16[8,3200]{1,0:T(8,128)(2,1)S(1)} %get-tuple-element.76), channel_id=1, source_target_pairs={{1,0},{2,1},{3,2},{0,3},{5,4},{6,5},{7,6},{4,7},{9,8},{10,9},{11,1... | collective-permute-start | bytes 153608 | tf_op jit(solution)/shard_map/ppermute | solution.py:112
  102.8 1.4 %collective-permute-done.26 = bf16[8,3200]{1,0:T(8,128)(2,1)S(1)} collective-permute-done((bf16[8,3200]{1,0:T(8,128)(2,1)S(1)}, bf16[8,3200]{1,0:T(8,128)(2,1)S(1)}, u32[]{:S(2)}, u32[]{:S(2)}) %collective-permute-start.26) | collective-permute-done | bytes 51232 | tf_op jit(solution)/shard_map/ppermute | solution.py:112
  104.2 0.5 collective-permute-done.28
  105.0 0.6 pad_maximum_fusion.14
  105.6 0.9 fusion.3
  (107 shorter events, 4.7 us)
Async XLA Ops:
  0.6 7.5 %copy-start = (bf16[6144,4]{0,1:T(4,128)(2,1)S(1)}, bf16[6144,4]{0,1:T(4,128)(2,1)}, u32[]{:S(2)}) copy-start(bf16[6144,4]{0,1:T(4,128)(2,1)} %param.12) | copy-start | bytes 147460
  0.6 15.3 %collective-permute-start = (bf16[8,6144]{1,0:T(8,128)(2,1)}, bf16[8,6144]{1,0:T(8,128)(2,1)S(1)}, u32[]{:S(2)}, u32[]{:S(2)}) collective-permute-start(bf16[8,6144]{1,0:T(8,128)(2,1)} %param.8), channel_id=1, source_target_pairs={{1,0},{2,1},{3,2},{0,3},{5,4},{6,5},{7,6},{4,7},{9,8},{10,9},{11,1... | collective-permute-start | bytes 294920 | tf_op jit(solution)/shard_map/ppermute | solution.py:112
  5.7 14.2 %collective-permute-start.8 = (bf16[8,6144]{1,0:T(8,128)(2,1)}, bf16[8,6144]{1,0:T(8,128)(2,1)S(1)}, u32[]{:S(2)}, u32[]{:S(2)}) collective-permute-start(bf16[8,6144]{1,0:T(8,128)(2,1)} %param.8), channel_id=1, source_target_pairs={{2,0},{3,1},{0,2},{1,3},{6,4},{7,5},{4,6},{5,7},{10,8},{11,9},{8,1... | collective-permute-start | bytes 294920 | tf_op jit(solution)/shard_map/ppermute | solution.py:112
  5.8 14.2 %collective-permute-start.9 = (bf16[8,6144]{1,0:T(8,128)(2,1)}, bf16[8,6144]{1,0:T(8,128)(2,1)S(1)}, u32[]{:S(2)}, u32[]{:S(2)}) collective-permute-start(bf16[8,6144]{1,0:T(8,128)(2,1)} %param.8), channel_id=1, source_target_pairs={{3,0},{0,1},{1,2},{2,3},{7,4},{4,5},{5,6},{6,7},{11,8},{8,9},{9,10... | collective-permute-start | bytes 294920 | tf_op jit(solution)/shard_map/ppermute | solution.py:112
  16.0 7.2 %collective-permute-start.1 = (bf16[8,6272]{1,0:T(8,128)(2,1)S(1)}, bf16[8,6272]{1,0:T(8,128)(2,1)S(1)}, u32[]{:S(2)}, u32[]{:S(2)}) collective-permute-start(bf16[8,6272]{1,0:T(8,128)(2,1)S(1)} %fusion.4), channel_id=1, source_target_pairs={{1,0},{2,1},{3,2},{0,3},{5,4},{6,5},{7,6},{4,7},{9,8},{10,9},{11,1... | collective-permute-start | bytes 301064 | tf_op jit(solution)/shard_map/ppermute | solution.py:112
  18.8 9.4 %collective-permute-start.2 = (bf16[8,6272]{1,0:T(8,128)(2,1)S(1)}, bf16[8,6272]{1,0:T(8,128)(2,1)S(1)}, u32[]{:S(2)}, u32[]{:S(2)}) collective-permute-start(bf16[8,6272]{1,0:T(8,128)(2,1)S(1)} %fusion.4), channel_id=1, source_target_pairs={{2,0},{3,1},{0,2},{1,3},{6,4},{7,5},{4,6},{5,7},{10,8},{11,9},{8,1... | collective-permute-start | bytes 301064 | tf_op jit(solution)/shard_map/ppermute | solution.py:112
  19.9 8.3 %collective-permute-start.3 = (bf16[8,6272]{1,0:T(8,128)(2,1)S(1)}, bf16[8,6272]{1,0:T(8,128)(2,1)S(1)}, u32[]{:S(2)}, u32[]{:S(2)}) collective-permute-start(bf16[8,6272]{1,0:T(8,128)(2,1)S(1)} %fusion.4), channel_id=1, source_target_pairs={{3,0},{0,1},{1,2},{2,3},{7,4},{4,5},{5,6},{6,7},{11,8},{8,9},{9,10... | collective-permute-start | bytes 301064 | tf_op jit(solution)/shard_map/ppermute | solution.py:112
  20.1 11.4 %collective-permute-start.10 = (bf16[32,3072]{1,0:T(8,128)(2,1)S(1)}, bf16[32,3072]{1,0:T(8,128)(2,1)S(1)}, u32[]{:S(2)}, u32[]{:S(2)}) collective-permute-start(bf16[32,3072]{1,0:T(8,128)(2,1)S(1)} %get-tuple-element.71), channel_id=1, source_target_pairs={{16,0},{0,16},{17,1},{1,17},{18,2},{2,18},{19,3},{3,19},{20,4},{4,... | collective-permute-start | bytes 589832 | tf_op jit(solution)/shard_map/ppermute | solution.py:116
  21.6 10.4 %collective-permute-start.12 = (bf16[32,3072]{1,0:T(8,128)(2,1)S(1)}, bf16[32,3072]{1,0:T(8,128)(2,1)S(1)}, u32[]{:S(2)}, u32[]{:S(2)}) collective-permute-start(bf16[32,3072]{1,0:T(8,128)(2,1)S(1)} %get-tuple-element.70), channel_id=1, source_target_pairs={{8,0},{12,4},{0,8},{4,12},{9,1},{13,5},{1,9},{5,13},{10,2},{14,6},... | collective-permute-start | bytes 589832 | tf_op jit(solution)/shard_map/ppermute | solution.py:116
  28.3 7.6 %collective-permute-start.6 = (bf16[32,3072]{1,0:T(8,128)(2,1)S(1)}, bf16[32,3072]{1,0:T(8,128)(2,1)S(1)}, u32[]{:S(2)}, u32[]{:S(2)}) collective-permute-start(bf16[32,3072]{1,0:T(8,128)(2,1)S(1)} %get-tuple-element.65), channel_id=1, source_target_pairs={{8,0},{12,4},{0,8},{4,12},{9,1},{13,5},{1,9},{5,13},{10,2},{14,6},... | collective-permute-start | bytes 589832 | tf_op jit(solution)/shard_map/ppermute | solution.py:116
  29.9 8.0 %collective-permute-start.4 = (bf16[32,3200]{1,0:T(8,128)(2,1)S(1)}, bf16[32,3200]{1,0:T(8,128)(2,1)S(1)}, u32[]{:S(2)}, u32[]{:S(2)}) collective-permute-start(bf16[32,3200]{1,0:T(8,128)(2,1)S(1)} %slice.96), channel_id=1, source_target_pairs={{16,0},{0,16},{17,1},{1,17},{18,2},{2,18},{19,3},{3,19},{20,4},{4,... | collective-permute-start | bytes 614408 | tf_op jit(solution)/shard_map/ppermute | solution.py:116
  31.5 12.9 %collective-permute-start.11 = (bf16[64,3072]{1,0:T(8,128)(2,1)S(1)}, bf16[64,3072]{1,0:T(8,128)(2,1)S(1)}, u32[]{:S(2)}, u32[]{:S(2)}) collective-permute-start(bf16[64,3072]{1,0:T(8,128)(2,1)S(1)} %pad_maximum_fusion.10), channel_id=1, source_target_pairs={{8,0},{12,4},{0,8},{4,12},{9,1},{13,5},{1,9},{5,13},{10,2},{14,6},... | collective-permute-start | bytes 1179656 | tf_op jit(solution)/shard_map/ppermute | solution.py:116
  32.1 14.3 %collective-permute-start.13 = (bf16[64,3072]{1,0:T(8,128)(2,1)S(1)}, bf16[64,3072]{1,0:T(8,128)(2,1)S(1)}, u32[]{:S(2)}, u32[]{:S(2)}) collective-permute-start(bf16[64,3072]{1,0:T(8,128)(2,1)S(1)} %pad_maximum_fusion.11), channel_id=1, source_target_pairs={{16,0},{0,16},{17,1},{1,17},{18,2},{2,18},{19,3},{3,19},{20,4},{4,... | collective-permute-start | bytes 1179656 | tf_op jit(solution)/shard_map/ppermute | solution.py:116
  36.0 18.7 %collective-permute-start.7 = (bf16[64,3072]{1,0:T(8,128)(2,1)S(1)}, bf16[64,3072]{1,0:T(8,128)(2,1)S(1)}, u32[]{:S(2)}, u32[]{:S(2)}) collective-permute-start(bf16[64,3072]{1,0:T(8,128)(2,1)S(1)} %pad_maximum_fusion.9), channel_id=1, source_target_pairs={{16,0},{0,16},{17,1},{1,17},{18,2},{2,18},{19,3},{3,19},{20,4},{4,... | collective-permute-start | bytes 1179656 | tf_op jit(solution)/shard_map/ppermute | solution.py:116
  38.0 16.7 %collective-permute-start.5 = (bf16[64,3200]{1,0:T(8,128)(2,1)S(1)}, bf16[64,3200]{1,0:T(8,128)(2,1)S(1)}, u32[]{:S(2)}, u32[]{:S(2)}) collective-permute-start(bf16[64,3200]{1,0:T(8,128)(2,1)S(1)} %pad_maximum_fusion.7), channel_id=1, source_target_pairs={{8,0},{12,4},{0,8},{4,12},{9,1},{13,5},{1,9},{5,13},{10,2},{14,6},... | collective-permute-start | bytes 1228808 | tf_op jit(solution)/shard_map/ppermute | solution.py:116
  46.5 9.1 %collective-permute-start.17 = (bf16[128,3072]{1,0:T(8,128)(2,1)S(1)}, bf16[128,3072]{1,0:T(8,128)(2,1)S(1)}, u32[]{:S(2)}, u32[]{:S(2)}) collective-permute-start(bf16[128,3072]{1,0:T(8,128)(2,1)S(1)} %pad_maximum_fusion.5), channel_id=1, source_target_pairs={{4,0},{0,4},{12,8},{8,12},{5,1},{1,5},{13,9},{9,13},{6,2},{2,6},{1... | collective-permute-start | bytes 2359304 | tf_op jit(solution)/shard_map/ppermute | solution.py:116
  46.6 3.3 %collective-permute-start.14 = (bf16[128,3072]{1,0:T(8,128)(2,1)S(1)}, bf16[128,3072]{1,0:T(8,128)(2,1)S(1)}, u32[]{:S(2)}, u32[]{:S(2)}) collective-permute-start(bf16[128,3072]{1,0:T(8,128)(2,1)S(1)} %pad_maximum_fusion.3), channel_id=1, source_target_pairs={{4,0},{0,4},{12,8},{8,12},{5,1},{1,5},{13,9},{9,13},{6,2},{2,6},{1... | collective-permute-start | bytes 2359304 | tf_op jit(solution)/shard_map/ppermute | solution.py:116
  54.7 2.7 %copy-start.1 = (bf16[3072,1024]{1,0:T(8,128)(2,1)}, bf16[3072,1024]{1,0:T(8,128)(2,1)S(1)}, u32[]{:S(2)}) copy-start(bf16[3072,1024]{1,0:T(8,128)(2,1)S(1)} %get-tuple-element.34.gate.gate_copy) | copy-start | bytes 18874372
  54.8 7.0 %collective-permute-start.16 = (bf16[128,3072]{1,0:T(8,128)(2,1)S(1)}, bf16[128,3072]{1,0:T(8,128)(2,1)S(1)}, u32[]{:S(2)}, u32[]{:S(2)}) collective-permute-start(bf16[128,3072]{1,0:T(8,128)(2,1)S(1)} %pad_maximum_fusion.4), channel_id=1, source_target_pairs={{4,0},{0,4},{12,8},{8,12},{5,1},{1,5},{13,9},{9,13},{6,2},{2,6},{1... | collective-permute-start | bytes 2359304 | tf_op jit(solution)/shard_map/ppermute | solution.py:116
  55.1 6.8 %collective-permute-start.15 = (bf16[128,3200]{1,0:T(8,128)(2,1)S(1)}, bf16[128,3200]{1,0:T(8,128)(2,1)S(1)}, u32[]{:S(2)}, u32[]{:S(2)}) collective-permute-start(bf16[128,3200]{1,0:T(8,128)(2,1)S(1)} %pad_maximum_fusion.2), channel_id=1, source_target_pairs={{4,0},{0,4},{12,8},{8,12},{5,1},{1,5},{13,9},{9,13},{6,2},{2,6},{1... | collective-permute-start | bytes 2457608 | tf_op jit(solution)/shard_map/ppermute | solution.py:116
  62.1 6.8 %slice-start = ((s8[6291456]{0:T(1024)(128)(4,1)}), s8[4194304]{0:T(1024)(128)(4,1)S(1)}, s32[]{:S(2)}) async-start(s8[6291456]{0:T(1024)(128)(4,1)} %bitcast.10), calls=%async_computation | async-start | bytes 8388608
  62.1 6.8 %slice-start.1 = ((s8[6291456]{0:T(1024)(128)(4,1)}), s8[2097152]{0:T(1024)(128)(4,1)S(1)}, s32[]{:S(2)}) async-start(s8[6291456]{0:T(1024)(128)(4,1)} %bitcast.10), calls=%async_computation.1 | async-start | bytes 4194304
  73.4 5.1 %collective-permute-start.21 = (bf16[128,3072]{1,0:T(8,128)(2,1)S(1)}, bf16[128,3072]{1,0:T(8,128)(2,1)S(1)}, u32[]{:S(2)}, u32[]{:S(2)}) collective-permute-start(bf16[128,3072]{1,0:T(8,128)(2,1)S(1)} %get-tuple-element.44), channel_id=1, source_target_pairs={{4,0},{0,4},{12,8},{8,12},{5,1},{1,5},{13,9},{9,13},{6,2},{2,6},{1... | collective-permute-start | bytes 2359304 | tf_op jit(solution)/shard_map/ppermute | solution.py:116
  78.1 2.9 %collective-permute-start.18 = (bf16[128,3200]{1,0:T(8,128)(2,1)S(1)}, bf16[128,3200]{1,0:T(8,128)(2,1)S(1)}, u32[]{:S(2)}, u32[]{:S(2)}) collective-permute-start(bf16[128,3200]{1,0:T(8,128)(2,1)S(1)} %get-tuple-element.43), channel_id=1, source_target_pairs={{4,0},{0,4},{12,8},{8,12},{5,1},{1,5},{13,9},{9,13},{6,2},{2,6},{1... | collective-permute-start | bytes 2457608 | tf_op jit(solution)/shard_map/ppermute | solution.py:116
  78.9 7.8 %collective-permute-start.25 = (bf16[64,1536]{1,0:T(8,128)(2,1)S(1)}, bf16[64,1536]{1,0:T(8,128)(2,1)S(1)}, u32[]{:S(2)}, u32[]{:S(2)}) collective-permute-start(bf16[64,1536]{1,0:T(8,128)(2,1)S(1)} %pad_maximum_fusion.13), channel_id=1, source_target_pairs={{16,0},{0,16},{17,1},{1,17},{18,2},{2,18},{19,3},{3,19},{20,4},{4,... | collective-permute-start | bytes 589832 | tf_op jit(solution)/shard_map/ppermute | solution.py:116
  80.4 7.8 %collective-permute-start.24 = (bf16[64,1536]{1,0:T(8,128)(2,1)S(1)}, bf16[64,1536]{1,0:T(8,128)(2,1)S(1)}, u32[]{:S(2)}, u32[]{:S(2)}) collective-permute-start(bf16[64,1536]{1,0:T(8,128)(2,1)S(1)} %concatenate.112), channel_id=1, source_target_pairs={{8,0},{12,4},{0,8},{4,12},{9,1},{13,5},{1,9},{5,13},{10,2},{14,6},... | collective-permute-start | bytes 589832 | tf_op jit(solution)/shard_map/ppermute | solution.py:116
  81.3 11.1 %collective-permute-start.20 = (bf16[64,1664]{1,0:T(8,128)(2,1)S(1)}, bf16[64,1664]{1,0:T(8,128)(2,1)S(1)}, u32[]{:S(2)}, u32[]{:S(2)}) collective-permute-start(bf16[64,1664]{1,0:T(8,128)(2,1)S(1)} %pad_maximum_fusion.12), channel_id=1, source_target_pairs={{16,0},{0,16},{17,1},{1,17},{18,2},{2,18},{19,3},{3,19},{20,4},{4,... | collective-permute-start | bytes 638984 | tf_op jit(solution)/shard_map/ppermute | solution.py:116
  82.4 9.9 %collective-permute-start.19 = (bf16[64,1536]{1,0:T(8,128)(2,1)S(1)}, bf16[64,1536]{1,0:T(8,128)(2,1)S(1)}, u32[]{:S(2)}, u32[]{:S(2)}) collective-permute-start(bf16[64,1536]{1,0:T(8,128)(2,1)S(1)} %concatenate.110), channel_id=1, source_target_pairs={{8,0},{12,4},{0,8},{4,12},{9,1},{13,5},{1,9},{5,13},{10,2},{14,6},... | collective-permute-start | bytes 589832 | tf_op jit(solution)/shard_map/ppermute | solution.py:116
  86.7 6.8 %collective-permute-start.30 = (bf16[32,1536]{1,0:T(8,128)(2,1)S(1)}, bf16[32,1536]{1,0:T(8,128)(2,1)S(1)}, u32[]{:S(2)}, u32[]{:S(2)}) collective-permute-start(bf16[32,1536]{1,0:T(8,128)(2,1)S(1)} %split.121), channel_id=1, source_target_pairs={{8,0},{12,4},{0,8},{4,12},{9,1},{13,5},{1,9},{5,13},{10,2},{14,6},... | collective-permute-start | bytes 294920 | tf_op jit(solution)/shard_map/ppermute | solution.py:116
  88.3 5.3 %collective-permute-start.29 = (bf16[32,1536]{1,0:T(8,128)(2,1)S(1)}, bf16[32,1536]{1,0:T(8,128)(2,1)S(1)}, u32[]{:S(2)}, u32[]{:S(2)}) collective-permute-start(bf16[32,1536]{1,0:T(8,128)(2,1)S(1)} %split.122), channel_id=1, source_target_pairs={{16,0},{0,16},{17,1},{1,17},{18,2},{2,18},{19,3},{3,19},{20,4},{4,... | collective-permute-start | bytes 294920 | tf_op jit(solution)/shard_map/ppermute | solution.py:116
  92.5 5.4 %collective-permute-start.22 = (bf16[32,1536]{1,0:T(8,128)(2,1)S(1)}, bf16[32,1536]{1,0:T(8,128)(2,1)S(1)}, u32[]{:S(2)}, u32[]{:S(2)}) collective-permute-start(bf16[32,1536]{1,0:T(8,128)(2,1)S(1)} %split.123), channel_id=1, source_target_pairs={{16,0},{0,16},{17,1},{1,17},{18,2},{2,18},{19,3},{3,19},{20,4},{4,... | collective-permute-start | bytes 294920 | tf_op jit(solution)/shard_map/ppermute | solution.py:116
  93.1 4.9 %collective-permute-start.23 = (bf16[32,1664]{1,0:T(8,128)(2,1)S(1)}, bf16[32,1664]{1,0:T(8,128)(2,1)S(1)}, u32[]{:S(2)}, u32[]{:S(2)}) collective-permute-start(bf16[32,1664]{1,0:T(8,128)(2,1)S(1)} %split.120), channel_id=1, source_target_pairs={{8,0},{12,4},{0,8},{4,12},{9,1},{13,5},{1,9},{5,13},{10,2},{14,6},... | collective-permute-start | bytes 319496 | tf_op jit(solution)/shard_map/ppermute | solution.py:116
  93.7 6.2 %collective-permute-start.31 = (bf16[8,3072]{1,0:T(8,128)(2,1)S(1)}, bf16[8,3072]{1,0:T(8,128)(2,1)S(1)}, u32[]{:S(2)}, u32[]{:S(2)}) collective-permute-start(bf16[8,3072]{1,0:T(8,128)(2,1)S(1)} %get-tuple-element.78), channel_id=1, source_target_pairs={{3,0},{0,1},{1,2},{2,3},{7,4},{4,5},{5,6},{6,7},{11,8},{8,9},{9,10... | collective-permute-start | bytes 147464 | tf_op jit(solution)/shard_map/ppermute | solution.py:112
  93.7 9.0 %collective-permute-start.32 = (bf16[8,3072]{1,0:T(8,128)(2,1)S(1)}, bf16[8,3072]{1,0:T(8,128)(2,1)S(1)}, u32[]{:S(2)}, u32[]{:S(2)}) collective-permute-start(bf16[8,3072]{1,0:T(8,128)(2,1)S(1)} %get-tuple-element.80), channel_id=1, source_target_pairs={{2,0},{3,1},{0,2},{1,3},{6,4},{7,5},{4,6},{5,7},{10,8},{11,9},{8,1... | collective-permute-start | bytes 147464 | tf_op jit(solution)/shard_map/ppermute | solution.py:112
  95.2 7.5 %collective-permute-start.33 = (bf16[8,3072]{1,0:T(8,128)(2,1)S(1)}, bf16[8,3072]{1,0:T(8,128)(2,1)S(1)}, u32[]{:S(2)}, u32[]{:S(2)}) collective-permute-start(bf16[8,3072]{1,0:T(8,128)(2,1)S(1)} %get-tuple-element.79), channel_id=1, source_target_pairs={{1,0},{2,1},{3,2},{0,3},{5,4},{6,5},{7,6},{4,7},{9,8},{10,9},{11,1... | collective-permute-start | bytes 147464 | tf_op jit(solution)/shard_map/ppermute | solution.py:112
  98.0 7.0 %copy-start.2 = (s32[8]{0:T(128)S(1)}, s32[8]{0:T(128)}, u32[]{:S(2)}) copy-start(s32[8]{0:T(128)} %param.10) | copy-start | bytes 100
  98.1 6.1 %collective-permute-start.26 = (bf16[8,3200]{1,0:T(8,128)(2,1)S(1)}, bf16[8,3200]{1,0:T(8,128)(2,1)S(1)}, u32[]{:S(2)}, u32[]{:S(2)}) collective-permute-start(bf16[8,3200]{1,0:T(8,128)(2,1)S(1)} %get-tuple-element.75), channel_id=1, source_target_pairs={{3,0},{0,1},{1,2},{2,3},{7,4},{4,5},{5,6},{6,7},{11,8},{8,9},{9,10... | collective-permute-start | bytes 153608 | tf_op jit(solution)/shard_map/ppermute | solution.py:112
  98.3 5.9 %collective-permute-start.27 = (bf16[8,3200]{1,0:T(8,128)(2,1)S(1)}, bf16[8,3200]{1,0:T(8,128)(2,1)S(1)}, u32[]{:S(2)}, u32[]{:S(2)}) collective-permute-start(bf16[8,3200]{1,0:T(8,128)(2,1)S(1)} %get-tuple-element.77), channel_id=1, source_target_pairs={{2,0},{3,1},{0,2},{1,3},{6,4},{7,5},{4,6},{5,7},{10,8},{11,9},{8,1... | collective-permute-start | bytes 153608 | tf_op jit(solution)/shard_map/ppermute | solution.py:112
  99.9 4.9 %collective-permute-start.28 = (bf16[8,3200]{1,0:T(8,128)(2,1)S(1)}, bf16[8,3200]{1,0:T(8,128)(2,1)S(1)}, u32[]{:S(2)}, u32[]{:S(2)}) collective-permute-start(bf16[8,3200]{1,0:T(8,128)(2,1)S(1)} %get-tuple-element.76), channel_id=1, source_target_pairs={{1,0},{2,1},{3,2},{0,3},{5,4},{6,5},{7,6},{4,7},{9,8},{10,9},{11,1... | collective-permute-start | bytes 153608 | tf_op jit(solution)/shard_map/ppermute | solution.py:112

commit v8 on v7

--- a/solution.py
+++ b/solution.py
@@ -11,9 +11,9 @@
 TOKEN_PART = 512
 HIDDEN_PART = 256
 COLUMN_PART = 512
-TOKEN_VMEM = 16 * 2 ** 20
-GRAD_VMEM = 20 * 2 ** 20
-OUTPUT_VMEM = 16 * 2 ** 20
+TOKEN_VMEM = 6 * 2 ** 20
+GRAD_VMEM = 12 * 2 ** 20
+OUTPUT_VMEM = 6 * 2 ** 20
 
 
 def routed_plan(tokens, out_grad, kept_mask, routes, router, gate_weight, up_weight, down_weight):
@@ -196,7 +196,7 @@
     return pltpu.with_memory_space_constraint(value, pltpu.HBM)
 
 
-def fetch_kernel(first, *refs):
+def fetch_kernel(first, _, *refs):
     count = (len(refs) - 1) // 2
     sems = refs[-1]
     copies = []
@@ -210,19 +210,19 @@
         copy.wait()
 
 
-def fetch(first, length, *weights):
+def fetch(first, length, earlier, *weights):
     shapes = [(length, value.shape[2]) for value in weights]
     return pl.pallas_call(
         functools.partial(fetch_kernel, first),
         out_shape=tuple(pltpu.VMEM(shape, jnp.bfloat16) for shape in shapes),
-        in_specs=[pl.BlockSpec(memory_space=pl.ANY)] * len(weights),
+        in_specs=[pl.BlockSpec(memory_space=pl.ANY)] * (1 + len(weights)),
         out_specs=(pl.BlockSpec(memory_space=pltpu.VMEM),) * len(weights),
         scratch_shapes=[pltpu.SemaphoreType.DMA((len(weights),))],
         compiler_params=pltpu.CompilerParams(vmem_limit_bytes=TOKEN_VMEM),
         cost_estimate=pl.CostEstimate(
             flops=0, bytes_accessed=sum(2 * rows * hidden for rows, hidden in shapes), transcendentals=0
         ),
-    )(*[in_hbm(value) for value in weights])
+    )(earlier, *[in_hbm(value) for value in weights])
 
 
 def token_kernel(first, tokens, gate, up, *refs):
@@ -274,16 +274,15 @@
 ):
     table = low.shape[1] - high.shape[1]
     half = high.shape[1]
-    hidden = down.shape[0]
-    depth = part_of(hidden, HIDDEN_PART)
-    steps = hidden // depth
+    depth = down.shape[1]
+    steps = pre_gate.shape[1] // depth
 
     def copy_of(index):
         rows = pl.ds(pl.multiple_of(index * depth, depth), depth)
-        return pltpu.make_async_copy(down_weight.at[0, rows], down.at[rows], down_sems.at[index])
-
-    @pl.loop(0, steps)
-    def _(index):
+        slot = lax.rem(index, 2)
+        return pltpu.make_async_copy(down_weight.at[0, rows], down.at[slot], down_sems.at[slot])
+
+    for index in range(min(2, steps)):
         copy_of(index).start()
 
     lanes = lax.broadcasted_iota(jnp.int32, (low.shape[0], table), 1)
@@ -295,8 +294,9 @@
     @pl.loop(0, steps)
     def _(step):
         copy_of(step).wait()
+        block = down.at[lax.rem(step, 2)]
         span = pl.ds(pl.multiple_of(step * depth, depth), depth)
-        grad_hidden = product(low[:, table:], down[span, :half], 1) + product(high[...], down[span, half:], 1)
+        grad_hidden = product(low[:, table:], block[:, :half], 1) + product(high[...], block[:, half:], 1)
         gates = pre_gate[:, span]
         ups = pre_up[:, span]
         sigma = jax.nn.sigmoid(gates)
@@ -305,6 +305,10 @@
         scaled = gate_rows[...] * grad_hidden
         grad_gate[:, span] = (scaled * ups * sigma * (1.0 + gates * (1.0 - sigma))).astype(jnp.bfloat16)
         grad_up[:, span] = (scaled * act).astype(jnp.bfloat16)
+
+        @pl.when(step + 2 < steps)
+        def _():
+            copy_of(step + 2).start()
 
     dots[...] = jnp.where(lanes == expert[0], dot_sums[...], 0.0).astype(jnp.bfloat16)
 
@@ -327,8 +331,8 @@
         scratch_shapes=[
             pltpu.VMEM((rows, 1), jnp.float32),
             pltpu.VMEM((rows, 1), jnp.float32),
-            pltpu.VMEM((hidden, width), jnp.bfloat16),
-            pltpu.SemaphoreType.DMA((hidden // part_of(hidden, HIDDEN_PART),)),
+            pltpu.VMEM((2, part_of(hidden, HIDDEN_PART), width), jnp.bfloat16),
+            pltpu.SemaphoreType.DMA((2,)),
         ],
         compiler_params=pltpu.CompilerParams(vmem_limit_bytes=GRAD_VMEM),
         cost_estimate=pl.CostEstimate(
@@ -392,9 +396,10 @@
     gate_table = (first_hot * gate_first[:, None] + second_hot * gate_second[:, None]) * keep_rows[:, None]
     gate_table = jnp.pad(gate_table.astype(jnp.bfloat16), ((0, 0), (0, table - expert_count)))
     grad_z = gather_z(after_others(jnp.concatenate([gate_table, out_grad], axis=1), token_z[1]))
-    gate_low, up_low = fetch(0, half, gate_weight, up_weight)
     token_near = gather_near(token_z, half)
-    token_far = after_others(gather_far(*token_near), (gate_low, up_low))
+    gate_low, up_low = fetch(0, half, token_near[0][0], gate_weight, up_weight)
+    token_near = after_others(token_near, (gate_low, up_low))
+    token_far = gather_far(*token_near)
     grad_near = gather_near(grad_z, half + table)
     grad_far = gather_far(*grad_near)
     token_low, token_high = gather_core(token_near[0], token_far[0], token_near[1], token_far[1])

time: 107 us -> 104 us (0.972)
  waiting for transfers between devices: 27.8 us -> 24 us
  starting transfers between devices: 37.9 us -> 40.2 us
  local copies, waits for them, and re-layouts: 4.02 us -> 2.28 us
    ppermute x12, waiting for transfers between devices: 7.09 us -> 3.1 us  [shift(): lax.ppermute(value, axis, [((i + step) % size, i) for i in range(size)])]
    ppermute x12, starting transfers between devices: 19 us -> 21.3 us  [shift(): lax.ppermute(value, axis, [((i + step) % size, i) for i in range(size)])]
    unnamed x22 -> x16, local copies, waits for them, and re-layouts: 2.84 us -> 1.07 us
  transfers between devices with their start and end apart: 34 -> 34, of which waited for: 11 -> 10; matrix products, arithmetic and copies ran while one was open for 6% -> 6% of each run, Pallas kernels for 17% -> 18%
where the time goes in v8:
time: 104 us
  starting transfers between devices  40.2 us (39%)
  Pallas kernels  30.1 us (29%)
  waiting for transfers between devices  24 us (23%)
  other arithmetic  3.9 us (4%)
  local copies, waits for them, and re-layouts  2.28 us (2%)
  matrix products  2.15 us (2%)
  between operations  1.2 us (1%)
    ppermute x12, starting transfers between devices, shift(): lax.ppermute(value, axis, [((i + step) % size, i) for i in range(size)])  21.3 us
    ppermute x22, waiting for transfers between devices, swap(): lax.ppermute(value, axis, [(i ^ bit, i) for i in range(lax.axis_size(axis...  20.9 us
    ppermute x22, starting transfers between devices, swap(): lax.ppermute(value, axis, [(i ^ bit, i) for i in range(lax.axis_size(axis...  18.8 us
    pallas_call x2, Pallas kernels, multiply_tokens(): pl.pallas_call(functools.partial(token_kernel, first), out_shape=sums + f...  9.08 us
    pallas_call x2, Pallas kernels, multiply_outputs(): pl.pallas_call(output_kernel, out_shape=(pltpu.VMEM((rows // 2, total), j...  8.99 us
    pallas_call x1, Pallas kernels, multiply_grads(): pl.pallas_call(grad_kernel, out_shape=(pltpu.VMEM((rows, hidden), jnp.bfl...  7.37 us
    pallas_call x1, Pallas kernels, fetch(): pl.pallas_call(functools.partial(fetch_kernel, first), out_shape=tuple((p...  4.62 us
    ppermute x12, waiting for transfers between devices, shift(): lax.ppermute(value, axis, [((i + step) % size, i) for i in range(size)])  3.1 us
  transfers between devices with their start and end apart: 34, of which 10 were waited for; matrix products, arithmetic and copies ran while one was open for 6% of the time, Pallas kernels for 18%

profile of v8, /device:TPU:0, one launch (start us, length us, event | category | flops | bytes accessed | tf_op | source)
XLA Modules:
  0.0 103.8 jit_solution(7025662554644742329)
XLA Ops:
  0.6 5.1 %collective-permute-start = (bf16[8,6144]{1,0:T(8,128)(2,1)}, bf16[8,6144]{1,0:T(8,128)(2,1)S(1)}, u32[]{:S(2)}, u32[]{:S(2)}) collective-permute-start(bf16[8,6144]{1,0:T(8,128)(2,1)} %param.8), channel_id=1, source_target_pairs={{1,0},{2,1},{3,2},{0,3},{5,4},{6,5},{7,6},{4,7},{9,8},{10,9},{11,1... | collective-permute-start | bytes 294920 | tf_op jit(solution)/shard_map/ppermute | solution.py:112
  5.8 1.0 collective-permute-start.9
  6.8 0.8 slice_bitcast_fusion
  7.5 0.7 convert_element_type.76
  8.2 1.2 %select_reduce_fusion.3 = (f32[8]{0:T(128)S(1)}, f32[8]{0:T(128)S(1)}) fusion(s32[8]{0:T(128)S(1)} %get-tuple-element.89, s32[8]{0:T(128)S(1)} %get-tuple-element.88, bf16[8,6144]{1,0:T(8,128)(2,1)} %param.8, bf16[6144,4]{0,1:T(4,128)(2,1)S(1)} %copy-done), kind=kOutput, calls=%fused_computation.69 | convolution fusion | flops 393392 | bytes 147584 | tf_op jit(solution)/shard_map/dot_general | solution.py:391
  9.5 0.9 fusion.4
  10.4 0.9 constant_dynamic-update-slice_fusion.7
  11.3 2.9 %collective-permute-start.1 = (bf16[8,6272]{1,0:T(8,128)(2,1)S(1)}, bf16[8,6272]{1,0:T(8,128)(2,1)S(1)}, u32[]{:S(2)}, u32[]{:S(2)}) collective-permute-start(bf16[8,6272]{1,0:T(8,128)(2,1)S(1)} %fusion.4), channel_id=1, source_target_pairs={{1,0},{2,1},{3,2},{0,3},{5,4},{6,5},{7,6},{4,7},{9,8},{10,9},{11,1... | collective-permute-start | bytes 301064 | tf_op jit(solution)/shard_map/ppermute | solution.py:112
  14.2 1.1 %collective-permute-start.2 = (bf16[8,6272]{1,0:T(8,128)(2,1)S(1)}, bf16[8,6272]{1,0:T(8,128)(2,1)S(1)}, u32[]{:S(2)}, u32[]{:S(2)}) collective-permute-start(bf16[8,6272]{1,0:T(8,128)(2,1)S(1)} %fusion.4), channel_id=1, source_target_pairs={{2,0},{3,1},{0,2},{1,3},{6,4},{7,5},{4,6},{5,7},{10,8},{11,9},{8,1... | collective-permute-start | bytes 301064 | tf_op jit(solution)/shard_map/ppermute | solution.py:112
  15.4 1.6 %collective-permute-start.10 = (bf16[32,3072]{1,0:T(8,128)(2,1)S(1)}, bf16[32,3072]{1,0:T(8,128)(2,1)S(1)}, u32[]{:S(2)}, u32[]{:S(2)}) collective-permute-start(bf16[32,3072]{1,0:T(8,128)(2,1)S(1)} %get-tuple-element.31._), channel_id=1, source_target_pairs={{16,0},{0,16},{17,1},{1,17},{18,2},{2,18},{19,3},{3,19},{20,4},{4,... | collective-permute-start | bytes 589832 | tf_op jit(solution)/shard_map/ppermute | solution.py:116
  17.0 1.5 %collective-permute-start.11 = (bf16[32,3072]{1,0:T(8,128)(2,1)S(1)}, bf16[32,3072]{1,0:T(8,128)(2,1)S(1)}, u32[]{:S(2)}, u32[]{:S(2)}) collective-permute-start(bf16[32,3072]{1,0:T(8,128)(2,1)S(1)} %get-tuple-element.36), channel_id=1, source_target_pairs={{8,0},{12,4},{0,8},{4,12},{9,1},{13,5},{1,9},{5,13},{10,2},{14,6},... | collective-permute-start | bytes 589832 | tf_op jit(solution)/shard_map/ppermute | solution.py:116
  18.5 4.6 %shard_map.95 = (bf16[3072,1024]{1,0:T(8,128)(2,1)S(1)}, bf16[3072,1024]{1,0:T(8,128)(2,1)S(1)}) custom-call(bf16[32,3072]{1,0:T(8,128)(2,1)S(1)} %get-tuple-element.31._, bf16[1,6144,1024]{2,1,0:T(8,128)(2,1)} %refs_0_.3, bf16[1,6144,1024]{2,1,0:T(8,128)(2,1)} %refs_1_.3), custom_call_target="tpu_custom_call" | custom-call | bytes 12582912 | tf_op jit(solution)/shard_map/pallas_call | solution.py:215
  23.7 1.6 %collective-permute-start.6 = (bf16[32,3072]{1,0:T(8,128)(2,1)S(1)}, bf16[32,3072]{1,0:T(8,128)(2,1)S(1)}, u32[]{:S(2)}, u32[]{:S(2)}) collective-permute-start(bf16[32,3072]{1,0:T(8,128)(2,1)S(1)} %get-tuple-element.69), channel_id=1, source_target_pairs={{8,0},{12,4},{0,8},{4,12},{9,1},{13,5},{1,9},{5,13},{10,2},{14,6},... | collective-permute-start | bytes 589832 | tf_op jit(solution)/shard_map/ppermute | solution.py:116
  25.3 1.5 %collective-permute-start.4 = (bf16[32,3200]{1,0:T(8,128)(2,1)S(1)}, bf16[32,3200]{1,0:T(8,128)(2,1)S(1)}, u32[]{:S(2)}, u32[]{:S(2)}) collective-permute-start(bf16[32,3200]{1,0:T(8,128)(2,1)S(1)} %slice.96), channel_id=1, source_target_pairs={{16,0},{0,16},{17,1},{1,17},{18,2},{2,18},{19,3},{3,19},{20,4},{4,... | collective-permute-start | bytes 614408 | tf_op jit(solution)/shard_map/ppermute | solution.py:116
  26.8 0.6 collective-permute-start.16
  27.5 0.6 collective-permute-start.12
  28.0 3.0 %collective-permute-done.6 = bf16[32,3072]{1,0:T(8,128)(2,1)S(1)} collective-permute-done((bf16[32,3072]{1,0:T(8,128)(2,1)S(1)}, bf16[32,3072]{1,0:T(8,128)(2,1)S(1)}, u32[]{:S(2)}, u32[]{:S(2)}) %collective-permute-start.6) | collective-permute-done | bytes 196640 | tf_op jit(solution)/shard_map/ppermute | solution.py:116
  31.1 1.6 %collective-permute-start.7 = (bf16[64,3072]{1,0:T(8,128)(2,1)S(1)}, bf16[64,3072]{1,0:T(8,128)(2,1)S(1)}, u32[]{:S(2)}, u32[]{:S(2)}) collective-permute-start(bf16[64,3072]{1,0:T(8,128)(2,1)S(1)} %pad_maximum_fusion.9), channel_id=1, source_target_pairs={{16,0},{0,16},{17,1},{1,17},{18,2},{2,18},{19,3},{3,19},{20,4},{4,... | collective-permute-start | bytes 1179656 | tf_op jit(solution)/shard_map/ppermute | solution.py:116
  32.6 0.7 collective-permute-done.4
  33.4 1.5 %collective-permute-start.5 = (bf16[64,3200]{1,0:T(8,128)(2,1)S(1)}, bf16[64,3200]{1,0:T(8,128)(2,1)S(1)}, u32[]{:S(2)}, u32[]{:S(2)}) collective-permute-start(bf16[64,3200]{1,0:T(8,128)(2,1)S(1)} %pad_maximum_fusion.7), channel_id=1, source_target_pairs={{8,0},{12,4},{0,8},{4,12},{9,1},{13,5},{1,9},{5,13},{10,2},{14,6},... | collective-permute-start | bytes 1228808 | tf_op jit(solution)/shard_map/ppermute | solution.py:116
  34.8 6.9 %collective-permute-done.16 = bf16[64,3072]{1,0:T(8,128)(2,1)S(1)} collective-permute-done((bf16[64,3072]{1,0:T(8,128)(2,1)S(1)}, bf16[64,3072]{1,0:T(8,128)(2,1)S(1)}, u32[]{:S(2)}, u32[]{:S(2)}) %collective-permute-start.16) | collective-permute-done | bytes 393248 | tf_op jit(solution)/shard_map/ppermute | solution.py:116
  42.0 0.6 collective-permute-start.13
  42.6 2.7 %collective-permute-done.13 = bf16[128,3072]{1,0:T(8,128)(2,1)S(1)} collective-permute-done((bf16[128,3072]{1,0:T(8,128)(2,1)S(1)}, bf16[128,3072]{1,0:T(8,128)(2,1)S(1)}, u32[]{:S(2)}, u32[]{:S(2)}) %collective-permute-start.13) | collective-permute-done | bytes 786464 | tf_op jit(solution)/shard_map/ppermute | solution.py:116
  45.4 4.6 %shard_map.96 = (f32[256,1024]{1,0:T(8,128)S(1)}, f32[256,1024]{1,0:T(8,128)S(1)}, bf16[3072,1024]{1,0:T(8,128)(2,1)S(1)}, bf16[3072,1024]{1,0:T(8,128)(2,1)S(1)}) custom-call(bf16[256,3072]{1,0:T(8,128)(2,1)S(1)} %pad_maximum_fusion.1.tokens, bf16[3072,1024]{1,0:T(8,128)(2,1)S(1)} %get-tuple-element.29.gate.gate_copy, ...), custom_call_target="tpu_custom_call" | custom-call | flops 3221225472 | bytes 1572864 | tf_op jit(solution)/shard_map/pallas_call | solution.py:258
  51.0 4.5 %shard_map.97 = (f32[256,1024]{1,0:T(8,128)S(1)}, f32[256,1024]{1,0:T(8,128)S(1)}) custom-call(bf16[256,3072]{1,0:T(8,128)(2,1)S(1)} %constant_dynamic-update-slice_fusion.13.tokens, bf16[3072,1024]{1,0:T(8,128)(2,1)S(1)} %get-tuple-element.38.gate.gate_copy, bf16[3072,1024]{1,0:T(8,128)(2,1)S(1)} %get-tuple-element.39.up.up_copy, ...), custom_call_target="tpu_custom_call" | custom-call | flops 3221225472 | bytes 1572864 | tf_op jit(solution)/shard_map/pallas_call | solution.py:258
  55.7 7.4 %shard_map.98 = (bf16[256,1024]{1,0:T(8,128)(2,1)S(1)}, bf16[256,1024]{1,0:T(8,128)(2,1)S(1)}, bf16[256,128]{1,0:T(8,128)(2,1)S(1)}) custom-call(s32[1]{0:T(128)} %bitcast.expert, bf16[256,3200]{1,0:T(8,128)(2,1)S(1)} %pad_maximum_fusion.low, bf16[256,3072]{1,0:T(8,128)(2,1)S(1)} %constant_dynamic-update-slice_fusion.8.high, ...), custom_call_target="tpu_custom_call" | custom-call | flops 3221225472 | bytes 12582912 | tf_op jit(solution)/shard_map/pallas_call | solution.py:320
  63.0 4.5 %shard_map.100 = (f32[128,3072]{1,0:T(8,128)S(1)}, bf16[128,3072]{1,0:T(8,128)(2,1)S(1)}) custom-call(bf16[256,1024]{1,0:T(8,128)(2,1)S(1)} %get-tuple-element.43.grad_gate, bf16[256,1024]{1,0:T(8,128)(2,1)S(1)} %get-tuple-element.44.grad_up, bf16[3072,1024]{1,0:T(8,128)(2,1)S(1)} %get-tuple-element.38.gate.gate_copy, ...), custom_call_target="tpu_custom_call" | custom-call | flops 3221225472 | bytes 3145728 | tf_op jit(solution)/shard_map/pallas_call | solution.py:366
  67.8 4.5 %shard_map.99 = (f32[128,3200]{1,0:T(8,128)S(1)}, bf16[128,3200]{1,0:T(8,128)(2,1)S(1)}) custom-call(bf16[256,1024]{1,0:T(8,128)(2,1)S(1)} %get-tuple-element.43.grad_gate, bf16[256,1024]{1,0:T(8,128)(2,1)S(1)} %get-tuple-element.44.grad_up, bf16[3072,1024]{1,0:T(8,128)(2,1)S(1)} %get-tuple-element.29.gate.gate_copy, ...), custom_call_target="tpu_custom_call" | custom-call | flops 3221225472 | bytes 3145728 | tf_op jit(solution)/shard_map/pallas_call | solution.py:366
  73.0 1.6 %collective-permute-start.25 = (bf16[64,1536]{1,0:T(8,128)(2,1)S(1)}, bf16[64,1536]{1,0:T(8,128)(2,1)S(1)}, u32[]{:S(2)}, u32[]{:S(2)}) collective-permute-start(bf16[64,1536]{1,0:T(8,128)(2,1)S(1)} %pad_maximum_fusion.13), channel_id=1, source_target_pairs={{16,0},{0,16},{17,1},{1,17},{18,2},{2,18},{19,3},{3,19},{20,4},{4,... | collective-permute-start | bytes 589832 | tf_op jit(solution)/shard_map/ppermute | solution.py:116
  74.6 0.5 collective-permute-start.24
  75.5 1.1 %collective-permute-start.20 = (bf16[64,1664]{1,0:T(8,128)(2,1)S(1)}, bf16[64,1664]{1,0:T(8,128)(2,1)S(1)}, u32[]{:S(2)}, u32[]{:S(2)}) collective-permute-start(bf16[64,1664]{1,0:T(8,128)(2,1)S(1)} %pad_maximum_fusion.12), channel_id=1, source_target_pairs={{16,0},{0,16},{17,1},{1,17},{18,2},{2,18},{19,3},{3,19},{20,4},{4,... | collective-permute-start | bytes 638984 | tf_op jit(solution)/shard_map/ppermute | solution.py:116
  76.6 1.0 collective-permute-start.19
  77.6 3.2 %collective-permute-done.25 = bf16[64,1536]{1,0:T(8,128)(2,1)S(1)} collective-permute-done((bf16[64,1536]{1,0:T(8,128)(2,1)S(1)}, bf16[64,1536]{1,0:T(8,128)(2,1)S(1)}, u32[]{:S(2)}, u32[]{:S(2)}) %collective-permute-start.25) | collective-permute-done | bytes 196640 | tf_op jit(solution)/shard_map/ppermute | solution.py:116
  80.9 0.6 collective-permute-start.30
  81.4 0.9 collective-permute-done.24
  82.4 0.6 collective-permute-start.29
  83.1 3.4 %collective-permute-done.19 = bf16[64,1536]{1,0:T(8,128)(2,1)S(1)} collective-permute-done((bf16[64,1536]{1,0:T(8,128)(2,1)S(1)}, bf16[64,1536]{1,0:T(8,128)(2,1)S(1)}, u32[]{:S(2)}, u32[]{:S(2)}) %collective-permute-start.19) | collective-permute-done | bytes 196640 | tf_op jit(solution)/shard_map/ppermute | solution.py:116
  86.6 0.6 collective-permute-start.22
  87.2 0.6 collective-permute-start.23
  87.9 2.6 %collective-permute-start.31 = (bf16[8,3072]{1,0:T(8,128)(2,1)S(1)}, bf16[8,3072]{1,0:T(8,128)(2,1)S(1)}, u32[]{:S(2)}, u32[]{:S(2)}) collective-permute-start(bf16[8,3072]{1,0:T(8,128)(2,1)S(1)} %get-tuple-element.81), channel_id=1, source_target_pairs={{3,0},{0,1},{1,2},{2,3},{7,4},{4,5},{5,6},{6,7},{11,8},{8,9},{9,10... | collective-permute-start | bytes 147464 | tf_op jit(solution)/shard_map/ppermute | solution.py:112
  90.5 1.9 %collective-permute-start.32 = (bf16[8,3072]{1,0:T(8,128)(2,1)S(1)}, bf16[8,3072]{1,0:T(8,128)(2,1)S(1)}, u32[]{:S(2)}, u32[]{:S(2)}) collective-permute-start(bf16[8,3072]{1,0:T(8,128)(2,1)S(1)} %get-tuple-element.83), channel_id=1, source_target_pairs={{2,0},{3,1},{0,2},{1,3},{6,4},{7,5},{4,6},{5,7},{10,8},{11,9},{8,1... | collective-permute-start | bytes 147464 | tf_op jit(solution)/shard_map/ppermute | solution.py:112
  92.4 2.8 %collective-permute-start.33 = (bf16[8,3072]{1,0:T(8,128)(2,1)S(1)}, bf16[8,3072]{1,0:T(8,128)(2,1)S(1)}, u32[]{:S(2)}, u32[]{:S(2)}) collective-permute-start(bf16[8,3072]{1,0:T(8,128)(2,1)S(1)} %get-tuple-element.82), channel_id=1, source_target_pairs={{1,0},{2,1},{3,2},{0,3},{5,4},{6,5},{7,6},{4,7},{9,8},{10,9},{11,1... | collective-permute-start | bytes 147464 | tf_op jit(solution)/shard_map/ppermute | solution.py:112
  95.5 0.6 collective-permute-start.27
  96.1 3.2 %collective-permute-start.28 = (bf16[8,3200]{1,0:T(8,128)(2,1)S(1)}, bf16[8,3200]{1,0:T(8,128)(2,1)S(1)}, u32[]{:S(2)}, u32[]{:S(2)}) collective-permute-start(bf16[8,3200]{1,0:T(8,128)(2,1)S(1)} %get-tuple-element.79), channel_id=1, source_target_pairs={{1,0},{2,1},{3,2},{0,3},{5,4},{6,5},{7,6},{4,7},{9,8},{10,9},{11,1... | collective-permute-start | bytes 153608 | tf_op jit(solution)/shard_map/ppermute | solution.py:112
  99.4 2.0 %collective-permute-done.26 = bf16[8,3200]{1,0:T(8,128)(2,1)S(1)} collective-permute-done((bf16[8,3200]{1,0:T(8,128)(2,1)S(1)}, bf16[8,3200]{1,0:T(8,128)(2,1)S(1)}, u32[]{:S(2)}, u32[]{:S(2)}) %collective-permute-start.26) | collective-permute-done | bytes 51232 | tf_op jit(solution)/shard_map/ppermute | solution.py:112
  101.4 0.6 collective-permute-done.28
  102.3 0.6 pad_maximum_fusion.14
  102.8 0.9 fusion.3
  (101 shorter events, 4.3 us)
Async XLA Ops:
  0.6 7.5 %copy-start = (bf16[6144,4]{0,1:T(4,128)(2,1)S(1)}, bf16[6144,4]{0,1:T(4,128)(2,1)}, u32[]{:S(2)}) copy-start(bf16[6144,4]{0,1:T(4,128)(2,1)} %param.12) | copy-start | bytes 147460
  0.6 10.7 %collective-permute-start = (bf16[8,6144]{1,0:T(8,128)(2,1)}, bf16[8,6144]{1,0:T(8,128)(2,1)S(1)}, u32[]{:S(2)}, u32[]{:S(2)}) collective-permute-start(bf16[8,6144]{1,0:T(8,128)(2,1)} %param.8), channel_id=1, source_target_pairs={{1,0},{2,1},{3,2},{0,3},{5,4},{6,5},{7,6},{4,7},{9,8},{10,9},{11,1... | collective-permute-start | bytes 294920 | tf_op jit(solution)/shard_map/ppermute | solution.py:112
  5.7 9.6 %collective-permute-start.8 = (bf16[8,6144]{1,0:T(8,128)(2,1)}, bf16[8,6144]{1,0:T(8,128)(2,1)S(1)}, u32[]{:S(2)}, u32[]{:S(2)}) collective-permute-start(bf16[8,6144]{1,0:T(8,128)(2,1)} %param.8), channel_id=1, source_target_pairs={{2,0},{3,1},{0,2},{1,3},{6,4},{7,5},{4,6},{5,7},{10,8},{11,9},{8,1... | collective-permute-start | bytes 294920 | tf_op jit(solution)/shard_map/ppermute | solution.py:112
  5.8 9.6 %collective-permute-start.9 = (bf16[8,6144]{1,0:T(8,128)(2,1)}, bf16[8,6144]{1,0:T(8,128)(2,1)S(1)}, u32[]{:S(2)}, u32[]{:S(2)}) collective-permute-start(bf16[8,6144]{1,0:T(8,128)(2,1)} %param.8), channel_id=1, source_target_pairs={{3,0},{0,1},{1,2},{2,3},{7,4},{4,5},{5,6},{6,7},{11,8},{8,9},{9,10... | collective-permute-start | bytes 294920 | tf_op jit(solution)/shard_map/ppermute | solution.py:112
  11.3 11.8 %collective-permute-start.1 = (bf16[8,6272]{1,0:T(8,128)(2,1)S(1)}, bf16[8,6272]{1,0:T(8,128)(2,1)S(1)}, u32[]{:S(2)}, u32[]{:S(2)}) collective-permute-start(bf16[8,6272]{1,0:T(8,128)(2,1)S(1)} %fusion.4), channel_id=1, source_target_pairs={{1,0},{2,1},{3,2},{0,3},{5,4},{6,5},{7,6},{4,7},{9,8},{10,9},{11,1... | collective-permute-start | bytes 301064 | tf_op jit(solution)/shard_map/ppermute | solution.py:112
  14.2 9.4 %collective-permute-start.2 = (bf16[8,6272]{1,0:T(8,128)(2,1)S(1)}, bf16[8,6272]{1,0:T(8,128)(2,1)S(1)}, u32[]{:S(2)}, u32[]{:S(2)}) collective-permute-start(bf16[8,6272]{1,0:T(8,128)(2,1)S(1)} %fusion.4), channel_id=1, source_target_pairs={{2,0},{3,1},{0,2},{1,3},{6,4},{7,5},{4,6},{5,7},{10,8},{11,9},{8,1... | collective-permute-start | bytes 301064 | tf_op jit(solution)/shard_map/ppermute | solution.py:112
  15.3 8.3 %collective-permute-start.3 = (bf16[8,6272]{1,0:T(8,128)(2,1)S(1)}, bf16[8,6272]{1,0:T(8,128)(2,1)S(1)}, u32[]{:S(2)}, u32[]{:S(2)}) collective-permute-start(bf16[8,6272]{1,0:T(8,128)(2,1)S(1)} %fusion.4), channel_id=1, source_target_pairs={{3,0},{0,1},{1,2},{2,3},{7,4},{4,5},{5,6},{6,7},{11,8},{8,9},{9,10... | collective-permute-start | bytes 301064 | tf_op jit(solution)/shard_map/ppermute | solution.py:112
  15.4 11.4 %collective-permute-start.10 = (bf16[32,3072]{1,0:T(8,128)(2,1)S(1)}, bf16[32,3072]{1,0:T(8,128)(2,1)S(1)}, u32[]{:S(2)}, u32[]{:S(2)}) collective-permute-start(bf16[32,3072]{1,0:T(8,128)(2,1)S(1)} %get-tuple-element.31._), channel_id=1, source_target_pairs={{16,0},{0,16},{17,1},{1,17},{18,2},{2,18},{19,3},{3,19},{20,4},{4,... | collective-permute-start | bytes 589832 | tf_op jit(solution)/shard_map/ppermute | solution.py:116
  17.0 9.8 %collective-permute-start.11 = (bf16[32,3072]{1,0:T(8,128)(2,1)S(1)}, bf16[32,3072]{1,0:T(8,128)(2,1)S(1)}, u32[]{:S(2)}, u32[]{:S(2)}) collective-permute-start(bf16[32,3072]{1,0:T(8,128)(2,1)S(1)} %get-tuple-element.36), channel_id=1, source_target_pairs={{8,0},{12,4},{0,8},{4,12},{9,1},{13,5},{1,9},{5,13},{10,2},{14,6},... | collective-permute-start | bytes 589832 | tf_op jit(solution)/shard_map/ppermute | solution.py:116
  23.7 7.3 %collective-permute-start.6 = (bf16[32,3072]{1,0:T(8,128)(2,1)S(1)}, bf16[32,3072]{1,0:T(8,128)(2,1)S(1)}, u32[]{:S(2)}, u32[]{:S(2)}) collective-permute-start(bf16[32,3072]{1,0:T(8,128)(2,1)S(1)} %get-tuple-element.69), channel_id=1, source_target_pairs={{8,0},{12,4},{0,8},{4,12},{9,1},{13,5},{1,9},{5,13},{10,2},{14,6},... | collective-permute-start | bytes 589832 | tf_op jit(solution)/shard_map/ppermute | solution.py:116
  25.3 8.0 %collective-permute-start.4 = (bf16[32,3200]{1,0:T(8,128)(2,1)S(1)}, bf16[32,3200]{1,0:T(8,128)(2,1)S(1)}, u32[]{:S(2)}, u32[]{:S(2)}) collective-permute-start(bf16[32,3200]{1,0:T(8,128)(2,1)S(1)} %slice.96), channel_id=1, source_target_pairs={{16,0},{0,16},{17,1},{1,17},{18,2},{2,18},{19,3},{3,19},{20,4},{4,... | collective-permute-start | bytes 614408 | tf_op jit(solution)/shard_map/ppermute | solution.py:116
  26.8 14.9 %collective-permute-start.16 = (bf16[64,3072]{1,0:T(8,128)(2,1)S(1)}, bf16[64,3072]{1,0:T(8,128)(2,1)S(1)}, u32[]{:S(2)}, u32[]{:S(2)}) collective-permute-start(bf16[64,3072]{1,0:T(8,128)(2,1)S(1)} %pad_maximum_fusion.11), channel_id=1, source_target_pairs={{16,0},{0,16},{17,1},{1,17},{18,2},{2,18},{19,3},{3,19},{20,4},{4,... | collective-permute-start | bytes 1179656 | tf_op jit(solution)/shard_map/ppermute | solution.py:116
  27.5 14.5 %collective-permute-start.12 = (bf16[64,3072]{1,0:T(8,128)(2,1)S(1)}, bf16[64,3072]{1,0:T(8,128)(2,1)S(1)}, u32[]{:S(2)}, u32[]{:S(2)}) collective-permute-start(bf16[64,3072]{1,0:T(8,128)(2,1)S(1)} %pad_maximum_fusion.10), channel_id=1, source_target_pairs={{8,0},{12,4},{0,8},{4,12},{9,1},{13,5},{1,9},{5,13},{10,2},{14,6},... | collective-permute-start | bytes 1179656 | tf_op jit(solution)/shard_map/ppermute | solution.py:116
  31.1 19.0 %collective-permute-start.7 = (bf16[64,3072]{1,0:T(8,128)(2,1)S(1)}, bf16[64,3072]{1,0:T(8,128)(2,1)S(1)}, u32[]{:S(2)}, u32[]{:S(2)}) collective-permute-start(bf16[64,3072]{1,0:T(8,128)(2,1)S(1)} %pad_maximum_fusion.9), channel_id=1, source_target_pairs={{16,0},{0,16},{17,1},{1,17},{18,2},{2,18},{19,3},{3,19},{20,4},{4,... | collective-permute-start | bytes 1179656 | tf_op jit(solution)/shard_map/ppermute | solution.py:116
  33.4 16.7 %collective-permute-start.5 = (bf16[64,3200]{1,0:T(8,128)(2,1)S(1)}, bf16[64,3200]{1,0:T(8,128)(2,1)S(1)}, u32[]{:S(2)}, u32[]{:S(2)}) collective-permute-start(bf16[64,3200]{1,0:T(8,128)(2,1)S(1)} %pad_maximum_fusion.7), channel_id=1, source_target_pairs={{8,0},{12,4},{0,8},{4,12},{9,1},{13,5},{1,9},{5,13},{10,2},{14,6},... | collective-permute-start | bytes 1228808 | tf_op jit(solution)/shard_map/ppermute | solution.py:116
  41.8 9.1 %collective-permute-start.17 = (bf16[128,3072]{1,0:T(8,128)(2,1)S(1)}, bf16[128,3072]{1,0:T(8,128)(2,1)S(1)}, u32[]{:S(2)}, u32[]{:S(2)}) collective-permute-start(bf16[128,3072]{1,0:T(8,128)(2,1)S(1)} %pad_maximum_fusion.5), channel_id=1, source_target_pairs={{4,0},{0,4},{12,8},{8,12},{5,1},{1,5},{13,9},{9,13},{6,2},{2,6},{1... | collective-permute-start | bytes 2359304 | tf_op jit(solution)/shard_map/ppermute | solution.py:116
  42.0 3.3 %collective-permute-start.13 = (bf16[128,3072]{1,0:T(8,128)(2,1)S(1)}, bf16[128,3072]{1,0:T(8,128)(2,1)S(1)}, u32[]{:S(2)}, u32[]{:S(2)}) collective-permute-start(bf16[128,3072]{1,0:T(8,128)(2,1)S(1)} %pad_maximum_fusion.3), channel_id=1, source_target_pairs={{4,0},{0,4},{12,8},{8,12},{5,1},{1,5},{13,9},{9,13},{6,2},{2,6},{1... | collective-permute-start | bytes 2359304 | tf_op jit(solution)/shard_map/ppermute | solution.py:116
  50.2 5.3 %collective-permute-start.15 = (bf16[128,3072]{1,0:T(8,128)(2,1)S(1)}, bf16[128,3072]{1,0:T(8,128)(2,1)S(1)}, u32[]{:S(2)}, u32[]{:S(2)}) collective-permute-start(bf16[128,3072]{1,0:T(8,128)(2,1)S(1)} %pad_maximum_fusion.4), channel_id=1, source_target_pairs={{4,0},{0,4},{12,8},{8,12},{5,1},{1,5},{13,9},{9,13},{6,2},{2,6},{1... | collective-permute-start | bytes 2359304 | tf_op jit(solution)/shard_map/ppermute | solution.py:116
  50.5 5.0 %collective-permute-start.14 = (bf16[128,3200]{1,0:T(8,128)(2,1)S(1)}, bf16[128,3200]{1,0:T(8,128)(2,1)S(1)}, u32[]{:S(2)}, u32[]{:S(2)}) collective-permute-start(bf16[128,3200]{1,0:T(8,128)(2,1)S(1)} %pad_maximum_fusion.2), channel_id=1, source_target_pairs={{4,0},{0,4},{12,8},{8,12},{5,1},{1,5},{13,9},{9,13},{6,2},{2,6},{1... | collective-permute-start | bytes 2457608 | tf_op jit(solution)/shard_map/ppermute | solution.py:116
  67.5 5.1 %collective-permute-start.21 = (bf16[128,3072]{1,0:T(8,128)(2,1)S(1)}, bf16[128,3072]{1,0:T(8,128)(2,1)S(1)}, u32[]{:S(2)}, u32[]{:S(2)}) collective-permute-start(bf16[128,3072]{1,0:T(8,128)(2,1)S(1)} %get-tuple-element.48), channel_id=1, source_target_pairs={{4,0},{0,4},{12,8},{8,12},{5,1},{1,5},{13,9},{9,13},{6,2},{2,6},{1... | collective-permute-start | bytes 2359304 | tf_op jit(solution)/shard_map/ppermute | solution.py:116
  72.3 2.8 %collective-permute-start.18 = (bf16[128,3200]{1,0:T(8,128)(2,1)S(1)}, bf16[128,3200]{1,0:T(8,128)(2,1)S(1)}, u32[]{:S(2)}, u32[]{:S(2)}) collective-permute-start(bf16[128,3200]{1,0:T(8,128)(2,1)S(1)} %get-tuple-element.47), channel_id=1, source_target_pairs={{4,0},{0,4},{12,8},{8,12},{5,1},{1,5},{13,9},{9,13},{6,2},{2,6},{1... | collective-permute-start | bytes 2457608 | tf_op jit(solution)/shard_map/ppermute | solution.py:116
  73.0 7.8 %collective-permute-start.25 = (bf16[64,1536]{1,0:T(8,128)(2,1)S(1)}, bf16[64,1536]{1,0:T(8,128)(2,1)S(1)}, u32[]{:S(2)}, u32[]{:S(2)}) collective-permute-start(bf16[64,1536]{1,0:T(8,128)(2,1)S(1)} %pad_maximum_fusion.13), channel_id=1, source_target_pairs={{16,0},{0,16},{17,1},{1,17},{18,2},{2,18},{19,3},{3,19},{20,4},{4,... | collective-permute-start | bytes 589832 | tf_op jit(solution)/shard_map/ppermute | solution.py:116
  74.6 7.8 %collective-permute-start.24 = (bf16[64,1536]{1,0:T(8,128)(2,1)S(1)}, bf16[64,1536]{1,0:T(8,128)(2,1)S(1)}, u32[]{:S(2)}, u32[]{:S(2)}) collective-permute-start(bf16[64,1536]{1,0:T(8,128)(2,1)S(1)} %concatenate.112), channel_id=1, source_target_pairs={{8,0},{12,4},{0,8},{4,12},{9,1},{13,5},{1,9},{5,13},{10,2},{14,6},... | collective-permute-start | bytes 589832 | tf_op jit(solution)/shard_map/ppermute | solution.py:116
  75.5 11.1 %collective-permute-start.20 = (bf16[64,1664]{1,0:T(8,128)(2,1)S(1)}, bf16[64,1664]{1,0:T(8,128)(2,1)S(1)}, u32[]{:S(2)}, u32[]{:S(2)}) collective-permute-start(bf16[64,1664]{1,0:T(8,128)(2,1)S(1)} %pad_maximum_fusion.12), channel_id=1, source_target_pairs={{16,0},{0,16},{17,1},{1,17},{18,2},{2,18},{19,3},{3,19},{20,4},{4,... | collective-permute-start | bytes 638984 | tf_op jit(solution)/shard_map/ppermute | solution.py:116
  76.6 9.9 %collective-permute-start.19 = (bf16[64,1536]{1,0:T(8,128)(2,1)S(1)}, bf16[64,1536]{1,0:T(8,128)(2,1)S(1)}, u32[]{:S(2)}, u32[]{:S(2)}) collective-permute-start(bf16[64,1536]{1,0:T(8,128)(2,1)S(1)} %concatenate.110), channel_id=1, source_target_pairs={{8,0},{12,4},{0,8},{4,12},{9,1},{13,5},{1,9},{5,13},{10,2},{14,6},... | collective-permute-start | bytes 589832 | tf_op jit(solution)/shard_map/ppermute | solution.py:116
  80.9 6.9 %collective-permute-start.30 = (bf16[32,1536]{1,0:T(8,128)(2,1)S(1)}, bf16[32,1536]{1,0:T(8,128)(2,1)S(1)}, u32[]{:S(2)}, u32[]{:S(2)}) collective-permute-start(bf16[32,1536]{1,0:T(8,128)(2,1)S(1)} %split.123), channel_id=1, source_target_pairs={{8,0},{12,4},{0,8},{4,12},{9,1},{13,5},{1,9},{5,13},{10,2},{14,6},... | collective-permute-start | bytes 294920 | tf_op jit(solution)/shard_map/ppermute | solution.py:116
  82.4 5.4 %collective-permute-start.29 = (bf16[32,1536]{1,0:T(8,128)(2,1)S(1)}, bf16[32,1536]{1,0:T(8,128)(2,1)S(1)}, u32[]{:S(2)}, u32[]{:S(2)}) collective-permute-start(bf16[32,1536]{1,0:T(8,128)(2,1)S(1)} %split.124), channel_id=1, source_target_pairs={{16,0},{0,16},{17,1},{1,17},{18,2},{2,18},{19,3},{3,19},{20,4},{4,... | collective-permute-start | bytes 294920 | tf_op jit(solution)/shard_map/ppermute | solution.py:116
  86.6 8.7 %collective-permute-start.22 = (bf16[32,1536]{1,0:T(8,128)(2,1)S(1)}, bf16[32,1536]{1,0:T(8,128)(2,1)S(1)}, u32[]{:S(2)}, u32[]{:S(2)}) collective-permute-start(bf16[32,1536]{1,0:T(8,128)(2,1)S(1)} %split.125), channel_id=1, source_target_pairs={{16,0},{0,16},{17,1},{1,17},{18,2},{2,18},{19,3},{3,19},{20,4},{4,... | collective-permute-start | bytes 294920 | tf_op jit(solution)/shard_map/ppermute | solution.py:116
  87.2 8.1 %collective-permute-start.23 = (bf16[32,1664]{1,0:T(8,128)(2,1)S(1)}, bf16[32,1664]{1,0:T(8,128)(2,1)S(1)}, u32[]{:S(2)}, u32[]{:S(2)}) collective-permute-start(bf16[32,1664]{1,0:T(8,128)(2,1)S(1)} %split.122), channel_id=1, source_target_pairs={{8,0},{12,4},{0,8},{4,12},{9,1},{13,5},{1,9},{5,13},{10,2},{14,6},... | collective-permute-start | bytes 319496 | tf_op jit(solution)/shard_map/ppermute | solution.py:116
  87.9 8.2 %collective-permute-start.31 = (bf16[8,3072]{1,0:T(8,128)(2,1)S(1)}, bf16[8,3072]{1,0:T(8,128)(2,1)S(1)}, u32[]{:S(2)}, u32[]{:S(2)}) collective-permute-start(bf16[8,3072]{1,0:T(8,128)(2,1)S(1)} %get-tuple-element.81), channel_id=1, source_target_pairs={{3,0},{0,1},{1,2},{2,3},{7,4},{4,5},{5,6},{6,7},{11,8},{8,9},{9,10... | collective-permute-start | bytes 147464 | tf_op jit(solution)/shard_map/ppermute | solution.py:112
  90.5 8.8 %collective-permute-start.32 = (bf16[8,3072]{1,0:T(8,128)(2,1)S(1)}, bf16[8,3072]{1,0:T(8,128)(2,1)S(1)}, u32[]{:S(2)}, u32[]{:S(2)}) collective-permute-start(bf16[8,3072]{1,0:T(8,128)(2,1)S(1)} %get-tuple-element.83), channel_id=1, source_target_pairs={{2,0},{3,1},{0,2},{1,3},{6,4},{7,5},{4,6},{5,7},{10,8},{11,9},{8,1... | collective-permute-start | bytes 147464 | tf_op jit(solution)/shard_map/ppermute | solution.py:112
  92.4 6.9 %collective-permute-start.33 = (bf16[8,3072]{1,0:T(8,128)(2,1)S(1)}, bf16[8,3072]{1,0:T(8,128)(2,1)S(1)}, u32[]{:S(2)}, u32[]{:S(2)}) collective-permute-start(bf16[8,3072]{1,0:T(8,128)(2,1)S(1)} %get-tuple-element.82), channel_id=1, source_target_pairs={{1,0},{2,1},{3,2},{0,3},{5,4},{6,5},{7,6},{4,7},{9,8},{10,9},{11,1... | collective-permute-start | bytes 147464 | tf_op jit(solution)/shard_map/ppermute | solution.py:112
  95.3 6.9 %copy-start.1 = (s32[8]{0:T(128)S(1)}, s32[8]{0:T(128)}, u32[]{:S(2)}) copy-start(s32[8]{0:T(128)} %param.10) | copy-start | bytes 100
  95.4 6.0 %collective-permute-start.26 = (bf16[8,3200]{1,0:T(8,128)(2,1)S(1)}, bf16[8,3200]{1,0:T(8,128)(2,1)S(1)}, u32[]{:S(2)}, u32[]{:S(2)}) collective-permute-start(bf16[8,3200]{1,0:T(8,128)(2,1)S(1)} %get-tuple-element.78), channel_id=1, source_target_pairs={{3,0},{0,1},{1,2},{2,3},{7,4},{4,5},{5,6},{6,7},{11,8},{8,9},{9,10... | collective-permute-start | bytes 153608 | tf_op jit(solution)/shard_map/ppermute | solution.py:112
  95.5 5.9 %collective-permute-start.27 = (bf16[8,3200]{1,0:T(8,128)(2,1)S(1)}, bf16[8,3200]{1,0:T(8,128)(2,1)S(1)}, u32[]{:S(2)}, u32[]{:S(2)}) collective-permute-start(bf16[8,3200]{1,0:T(8,128)(2,1)S(1)} %get-tuple-element.80), channel_id=1, source_target_pairs={{2,0},{3,1},{0,2},{1,3},{6,4},{7,5},{4,6},{5,7},{10,8},{11,9},{8,1... | collective-permute-start | bytes 153608 | tf_op jit(solution)/shard_map/ppermute | solution.py:112
  96.1 5.8 %collective-permute-start.28 = (bf16[8,3200]{1,0:T(8,128)(2,1)S(1)}, bf16[8,3200]{1,0:T(8,128)(2,1)S(1)}, u32[]{:S(2)}, u32[]{:S(2)}) collective-permute-start(bf16[8,3200]{1,0:T(8,128)(2,1)S(1)} %get-tuple-element.79), channel_id=1, source_target_pairs={{1,0},{2,1},{3,2},{0,3},{5,4},{6,5},{7,6},{4,7},{9,8},{10,9},{11,1... | collective-permute-start | bytes 153608 | tf_op jit(solution)/shard_map/ppermute | solution.py:112

commit v9 on v8

--- a/solution.py
+++ b/solution.py
@@ -12,7 +12,7 @@
 HIDDEN_PART = 256
 COLUMN_PART = 512
 TOKEN_VMEM = 6 * 2 ** 20
-GRAD_VMEM = 12 * 2 ** 20
+GRAD_VMEM = 10 * 2 ** 20
 OUTPUT_VMEM = 6 * 2 ** 20
 
 
@@ -270,19 +270,20 @@
 
 
 def grad_kernel(
-    expert, low, high, pre_gate, pre_up, down_weight, grad_gate, grad_up, dots, gate_rows, dot_sums, down, down_sems
+    expert, low, high, pre_gate, pre_up, down, down_weight, grad_gate, grad_up, dots, gate_rows, dot_sums, rest, sems
 ):
     table = low.shape[1] - high.shape[1]
     half = high.shape[1]
-    depth = down.shape[1]
-    steps = pre_gate.shape[1] // depth
+    ready = down.shape[0]
+    depth = part_of(ready, HIDDEN_PART)
+    steps = ready // depth
 
     def copy_of(index):
         rows = pl.ds(pl.multiple_of(index * depth, depth), depth)
-        slot = lax.rem(index, 2)
-        return pltpu.make_async_copy(down_weight.at[0, rows], down.at[slot], down_sems.at[slot])
-
-    for index in range(min(2, steps)):
+        source = pl.ds(pl.multiple_of(ready + index * depth, depth), depth)
+        return pltpu.make_async_copy(down_weight.at[0, source], rest.at[rows], sems.at[index])
+
+    for index in range(steps):
         copy_of(index).start()
 
     lanes = lax.broadcasted_iota(jnp.int32, (low.shape[0], table), 1)
@@ -291,12 +292,10 @@
     )
     dot_sums[...] = jnp.zeros_like(dot_sums)
 
-    @pl.loop(0, steps)
-    def _(step):
-        copy_of(step).wait()
-        block = down.at[lax.rem(step, 2)]
-        span = pl.ds(pl.multiple_of(step * depth, depth), depth)
-        grad_hidden = product(low[:, table:], block[:, :half], 1) + product(high[...], block[:, half:], 1)
+    def block(weights, first, step):
+        rows = pl.ds(pl.multiple_of(step * depth, depth), depth)
+        span = pl.ds(pl.multiple_of(first + step * depth, depth), depth)
+        grad_hidden = product(low[:, table:], weights[rows, :half], 1) + product(high[...], weights[rows, half:], 1)
         gates = pre_gate[:, span]
         ups = pre_up[:, span]
         sigma = jax.nn.sigmoid(gates)
@@ -306,14 +305,19 @@
         grad_gate[:, span] = (scaled * ups * sigma * (1.0 + gates * (1.0 - sigma))).astype(jnp.bfloat16)
         grad_up[:, span] = (scaled * act).astype(jnp.bfloat16)
 
-        @pl.when(step + 2 < steps)
-        def _():
-            copy_of(step + 2).start()
+    @pl.loop(0, steps)
+    def _(step):
+        block(down, 0, step)
+
+    @pl.loop(0, steps)
+    def _(step):
+        copy_of(step).wait()
+        block(rest, ready, step)
 
     dots[...] = jnp.where(lanes == expert[0], dot_sums[...], 0.0).astype(jnp.bfloat16)
 
 
-def multiply_grads(expert, low, high, pre_gate, pre_up, down_weight):
+def multiply_grads(expert, low, high, pre_gate, pre_up, down, down_weight):
     rows, hidden = pre_gate.shape
     width = down_weight.shape[2]
     table = low.shape[1] - high.shape[1]
@@ -325,20 +329,20 @@
             pltpu.VMEM((rows, table), jnp.bfloat16),
         ),
         in_specs=[pl.BlockSpec(memory_space=pltpu.SMEM)]
-        + [pl.BlockSpec(memory_space=pltpu.VMEM)] * 4
+        + [pl.BlockSpec(memory_space=pltpu.VMEM)] * 5
         + [pl.BlockSpec(memory_space=pl.ANY)],
         out_specs=(pl.BlockSpec(memory_space=pltpu.VMEM),) * 3,
         scratch_shapes=[
             pltpu.VMEM((rows, 1), jnp.float32),
             pltpu.VMEM((rows, 1), jnp.float32),
-            pltpu.VMEM((2, part_of(hidden, HIDDEN_PART), width), jnp.bfloat16),
-            pltpu.SemaphoreType.DMA((2,)),
+            pltpu.VMEM((hidden // 2, width), jnp.bfloat16),
+            pltpu.SemaphoreType.DMA((hidden // 2 // part_of(hidden // 2, HIDDEN_PART),)),
         ],
         compiler_params=pltpu.CompilerParams(vmem_limit_bytes=GRAD_VMEM),
         cost_estimate=pl.CostEstimate(
-            flops=2 * rows * width * hidden, bytes_accessed=2 * width * hidden, transcendentals=rows * hidden
-        ),
-    )(expert, low, high, pre_gate, pre_up, in_hbm(down_weight))
+            flops=2 * rows * width * hidden, bytes_accessed=width * hidden, transcendentals=rows * hidden
+        ),
+    )(expert, low, high, pre_gate, pre_up, down, in_hbm(down_weight))
 
 
 def output_kernel(grad_gate, grad_up, gate_copy, up_copy, *refs):
@@ -401,14 +405,16 @@
     token_near = after_others(token_near, (gate_low, up_low))
     token_far = gather_far(*token_near)
     grad_near = gather_near(grad_z, half + table)
-    grad_far = gather_far(*grad_near)
+    (down,) = fetch(0, down_weight.shape[1] // 2, grad_near[1][1], down_weight)
+    grad_far = gather_far(*after_others(grad_near, token_far))
+    token_far = after_others(token_far, down)
     token_low, token_high = gather_core(token_near[0], token_far[0], token_near[1], token_far[1])
     pre_gate, pre_up, gate_high, up_high = multiply_tokens(token_low, gate_low, up_low, half, gate_weight, up_weight)
     grad_far = after_others(grad_far, pre_gate)
     pre_gate, pre_up = multiply_tokens(token_high, gate_high, up_high, 0, pre_gate, pre_up)
     grad_halves = gather_core(grad_near[0], grad_far[0], grad_near[1], grad_far[1])
     expert = lax.axis_index("expert").astype(jnp.int32).reshape(1)
-    grad_gate, grad_up, dots = multiply_grads(expert, *grad_halves, pre_gate, pre_up, down_weight)
+    grad_gate, grad_up, dots = multiply_grads(expert, *grad_halves, pre_gate, pre_up, down, down_weight)
     kept, sent = multiply_outputs(grad_gate, grad_up, gate_low, up_low, dots)
     chunk = scatter_core(kept, sent)
     kept, sent = multiply_outputs(grad_gate, grad_up, gate_high, up_high)

time: 104 us -> 105 us (level)
    pallas_call x1 -> x2, Pallas kernels: 4.62 us -> 7.41 us  [fetch(): pl.pallas_call(functools.partial(fetch_kernel, first), out_shape=tuple((p...]
    pallas_call x1, Pallas kernels: 7.37 us -> 4.73 us  [multiply_grads(): pl.pallas_call(grad_kernel, out_shape=(pltpu.VMEM((rows, hidden), jnp.bfl...]
    ppermute x22, starting transfers between devices: 18.8 us -> 21.4 us  [swap(): lax.ppermute(value, axis, [(i ^ bit, i) for i in range(lax.axis_size(axis...]
    ppermute x12, starting transfers between devices: 21.3 us -> 19.8 us  [shift(): lax.ppermute(value, axis, [((i + step) % size, i) for i in range(size)])]
  transfers between devices with their start and end apart: 34 -> 34, of which waited for: 10 -> 9; matrix products, arithmetic and copies ran while one was open for 6% -> 6% of each run, Pallas kernels for 18% -> 20%
where the time goes in v9:
time: 105 us
  starting transfers between devices  41.2 us (39%)
  Pallas kernels  30.1 us (29%)
  waiting for transfers between devices  23.9 us (23%)
  other arithmetic  3.95 us (4%)
  local copies, waits for them, and re-layouts  2.29 us (2%)
  matrix products  2.14 us (2%)
  between operations  1.25 us (1%)
    ppermute x22, starting transfers between devices, swap(): lax.ppermute(value, axis, [(i ^ bit, i) for i in range(lax.axis_size(axis...  21.4 us
    ppermute x22, waiting for transfers between devices, swap(): lax.ppermute(value, axis, [(i ^ bit, i) for i in range(lax.axis_size(axis...  20.8 us
    ppermute x12, starting transfers between devices, shift(): lax.ppermute(value, axis, [((i + step) % size, i) for i in range(size)])  19.8 us
    pallas_call x2, Pallas kernels, multiply_tokens(): pl.pallas_call(functools.partial(token_kernel, first), out_shape=sums + f...  9.08 us
    pallas_call x2, Pallas kernels, multiply_outputs(): pl.pallas_call(output_kernel, out_shape=(pltpu.VMEM((rows // 2, total), j...  8.9 us
    pallas_call x2, Pallas kernels, fetch(): pl.pallas_call(functools.partial(fetch_kernel, first), out_shape=tuple((p...  7.41 us
    pallas_call x1, Pallas kernels, multiply_grads(): pl.pallas_call(grad_kernel, out_shape=(pltpu.VMEM((rows, hidden), jnp.bfl...  4.73 us
    ppermute x12, waiting for transfers between devices, shift(): lax.ppermute(value, axis, [((i + step) % size, i) for i in range(size)])  3.1 us
  transfers between devices with their start and end apart: 34, of which 9 were waited for; matrix products, arithmetic and copies ran while one was open for 6% of the time, Pallas kernels for 20%

profile of v9, /device:TPU:0, one launch (start us, length us, event | category | flops | bytes accessed | tf_op | source)
XLA Modules:
  0.0 104.8 jit_solution(7808026633732609847)
XLA Ops:
  0.6 5.1 %collective-permute-start = (bf16[8,6144]{1,0:T(8,128)(2,1)}, bf16[8,6144]{1,0:T(8,128)(2,1)S(1)}, u32[]{:S(2)}, u32[]{:S(2)}) collective-permute-start(bf16[8,6144]{1,0:T(8,128)(2,1)} %param.8), channel_id=1, source_target_pairs={{1,0},{2,1},{3,2},{0,3},{5,4},{6,5},{7,6},{4,7},{9,8},{10,9},{11,1... | collective-permute-start | bytes 294920 | tf_op jit(solution)/shard_map/ppermute | solution.py:112
  5.8 1.0 collective-permute-start.7
  6.8 0.8 slice_bitcast_fusion
  7.5 0.7 convert_element_type.76
  8.2 1.2 %select_reduce_fusion.3 = (f32[8]{0:T(128)S(1)}, f32[8]{0:T(128)S(1)}) fusion(s32[8]{0:T(128)S(1)} %get-tuple-element.101, s32[8]{0:T(128)S(1)} %get-tuple-element.100, bf16[8,6144]{1,0:T(8,128)(2,1)} %param.8, bf16[6144,4]{0,1:T(4,128)(2,1)S(1)} %copy-done), kind=kOutput, calls=%fused_computation.69 | convolution fusion | flops 393392 | bytes 147584 | tf_op jit(solution)/shard_map/dot_general | solution.py:395
  9.5 0.9 fusion.4
  10.4 0.9 constant_dynamic-update-slice_fusion.7
  11.3 2.9 %collective-permute-start.1 = (bf16[8,6272]{1,0:T(8,128)(2,1)S(1)}, bf16[8,6272]{1,0:T(8,128)(2,1)S(1)}, u32[]{:S(2)}, u32[]{:S(2)}) collective-permute-start(bf16[8,6272]{1,0:T(8,128)(2,1)S(1)} %fusion.4), channel_id=1, source_target_pairs={{1,0},{2,1},{3,2},{0,3},{5,4},{6,5},{7,6},{4,7},{9,8},{10,9},{11,1... | collective-permute-start | bytes 301064 | tf_op jit(solution)/shard_map/ppermute | solution.py:112
  14.2 1.1 %collective-permute-start.2 = (bf16[8,6272]{1,0:T(8,128)(2,1)S(1)}, bf16[8,6272]{1,0:T(8,128)(2,1)S(1)}, u32[]{:S(2)}, u32[]{:S(2)}) collective-permute-start(bf16[8,6272]{1,0:T(8,128)(2,1)S(1)} %fusion.4), channel_id=1, source_target_pairs={{2,0},{3,1},{0,2},{1,3},{6,4},{7,5},{4,6},{5,7},{10,8},{11,9},{8,1... | collective-permute-start | bytes 301064 | tf_op jit(solution)/shard_map/ppermute | solution.py:112
  15.4 1.6 %collective-permute-start.8 = (bf16[32,3072]{1,0:T(8,128)(2,1)S(1)}, bf16[32,3072]{1,0:T(8,128)(2,1)S(1)}, u32[]{:S(2)}, u32[]{:S(2)}) collective-permute-start(bf16[32,3072]{1,0:T(8,128)(2,1)S(1)} %get-tuple-element.37._), channel_id=1, source_target_pairs={{16,0},{0,16},{17,1},{1,17},{18,2},{2,18},{19,3},{3,19},{20,4},{4,... | collective-permute-start | bytes 589832 | tf_op jit(solution)/shard_map/ppermute | solution.py:116
  17.0 1.5 %collective-permute-start.9 = (bf16[32,3072]{1,0:T(8,128)(2,1)S(1)}, bf16[32,3072]{1,0:T(8,128)(2,1)S(1)}, u32[]{:S(2)}, u32[]{:S(2)}) collective-permute-start(bf16[32,3072]{1,0:T(8,128)(2,1)S(1)} %get-tuple-element.39), channel_id=1, source_target_pairs={{8,0},{12,4},{0,8},{4,12},{9,1},{13,5},{1,9},{5,13},{10,2},{14,6},... | collective-permute-start | bytes 589832 | tf_op jit(solution)/shard_map/ppermute | solution.py:116
  18.5 4.6 %shard_map.95 = (bf16[3072,1024]{1,0:T(8,128)(2,1)S(1)}, bf16[3072,1024]{1,0:T(8,128)(2,1)S(1)}) custom-call(bf16[32,3072]{1,0:T(8,128)(2,1)S(1)} %get-tuple-element.37._, bf16[1,6144,1024]{2,1,0:T(8,128)(2,1)} %refs_0_.5, bf16[1,6144,1024]{2,1,0:T(8,128)(2,1)} %refs_1_.3), custom_call_target="tpu_custom_call" | custom-call | bytes 12582912 | tf_op jit(solution)/shard_map/pallas_call | solution.py:215
  23.7 1.6 %collective-permute-start.11 = (bf16[64,3072]{1,0:T(8,128)(2,1)S(1)}, bf16[64,3072]{1,0:T(8,128)(2,1)S(1)}, u32[]{:S(2)}, u32[]{:S(2)}) collective-permute-start(bf16[64,3072]{1,0:T(8,128)(2,1)S(1)} %pad_maximum_fusion.10), channel_id=1, source_target_pairs={{16,0},{0,16},{17,1},{1,17},{18,2},{2,18},{19,3},{3,19},{20,4},{4,... | collective-permute-start | bytes 1179656 | tf_op jit(solution)/shard_map/ppermute | solution.py:116
  25.3 1.6 %collective-permute-start.10 = (bf16[64,3072]{1,0:T(8,128)(2,1)S(1)}, bf16[64,3072]{1,0:T(8,128)(2,1)S(1)}, u32[]{:S(2)}, u32[]{:S(2)}) collective-permute-start(bf16[64,3072]{1,0:T(8,128)(2,1)S(1)} %pad_maximum_fusion.9), channel_id=1, source_target_pairs={{8,0},{12,4},{0,8},{4,12},{9,1},{13,5},{1,9},{5,13},{10,2},{14,6},... | collective-permute-start | bytes 1179656 | tf_op jit(solution)/shard_map/ppermute | solution.py:116
  26.9 0.6 collective-permute-start.5
  28.1 10.9 %collective-permute-done.5._ = bf16[32,3072]{1,0:T(8,128)(2,1)S(1)} collective-permute-done((bf16[32,3072]{1,0:T(8,128)(2,1)S(1)}, bf16[32,3072]{1,0:T(8,128)(2,1)S(1)}, u32[]{:S(2)}, u32[]{:S(2)}) %collective-permute-start.5) | collective-permute-done | bytes 196640 | tf_op jit(solution)/shard_map/ppermute | solution.py:116
  39.0 2.8 %shard_map.96.down = bf16[512,6144]{1,0:T(8,128)(2,1)S(1)} custom-call(bf16[32,3072]{1,0:T(8,128)(2,1)S(1)} %collective-permute-done.5._, bf16[1,1024,6144]{2,1,0:T(8,128)(2,1)} %down_weight.1), custom_call_target="tpu_custom_call" | custom-call | bytes 6291456 | tf_op jit(solution)/shard_map/pallas_call | solution.py:215
  42.1 0.6 collective-permute-start.14
  42.7 0.6 collective-permute-start.13
  43.3 1.6 %collective-permute-start.12 = (bf16[64,3200]{1,0:T(8,128)(2,1)S(1)}, bf16[64,3200]{1,0:T(8,128)(2,1)S(1)}, u32[]{:S(2)}, u32[]{:S(2)}) collective-permute-start(bf16[64,3200]{1,0:T(8,128)(2,1)S(1)} %pad_maximum_fusion.7), channel_id=1, source_target_pairs={{8,0},{12,4},{0,8},{4,12},{9,1},{13,5},{1,9},{5,13},{10,2},{14,6},... | collective-permute-start | bytes 1228808 | tf_op jit(solution)/shard_map/ppermute | solution.py:116
  45.5 4.6 %shard_map.97 = (f32[256,1024]{1,0:T(8,128)S(1)}, f32[256,1024]{1,0:T(8,128)S(1)}, bf16[3072,1024]{1,0:T(8,128)(2,1)S(1)}, bf16[3072,1024]{1,0:T(8,128)(2,1)S(1)}) custom-call(bf16[256,3072]{1,0:T(8,128)(2,1)S(1)} %pad_maximum_fusion.1.tokens, bf16[3072,1024]{1,0:T(8,128)(2,1)S(1)} %get-tuple-element.35.gate.gate_copy, ...), custom_call_target="tpu_custom_call" | custom-call | flops 3221225472 | bytes 1572864 | tf_op jit(solution)/shard_map/pallas_call | solution.py:258
  50.1 3.7 %collective-permute-done.13 = bf16[64,3072]{1,0:T(8,128)(2,1)S(1)} collective-permute-done((bf16[64,3072]{1,0:T(8,128)(2,1)S(1)}, bf16[64,3072]{1,0:T(8,128)(2,1)S(1)}, u32[]{:S(2)}, u32[]{:S(2)}) %collective-permute-start.13) | collective-permute-done | bytes 393248 | tf_op jit(solution)/shard_map/ppermute | solution.py:116
  53.8 0.7 collective-permute-done.12
  54.8 0.6 collective-permute-start.15
  55.4 4.5 %shard_map.98 = (f32[256,1024]{1,0:T(8,128)S(1)}, f32[256,1024]{1,0:T(8,128)S(1)}) custom-call(bf16[256,3072]{1,0:T(8,128)(2,1)S(1)} %constant_dynamic-update-slice_fusion.13.tokens, bf16[3072,1024]{1,0:T(8,128)(2,1)S(1)} %get-tuple-element.50.gate.gate_copy, bf16[3072,1024]{1,0:T(8,128)(2,1)S(1)} %get-tuple-element.51.up.up_copy, ...), custom_call_target="tpu_custom_call" | custom-call | flops 3221225472 | bytes 1572864 | tf_op jit(solution)/shard_map/pallas_call | solution.py:258
  60.1 4.7 %shard_map.99 = (bf16[256,1024]{1,0:T(8,128)(2,1)S(1)}, bf16[256,1024]{1,0:T(8,128)(2,1)S(1)}, bf16[256,128]{1,0:T(8,128)(2,1)S(1)}) custom-call(s32[1]{0:T(128)} %bitcast.expert, bf16[256,3200]{1,0:T(8,128)(2,1)S(1)} %pad_maximum_fusion.low, bf16[256,3072]{1,0:T(8,128)(2,1)S(1)} %constant_dynamic-update-slice_fusion.8.high, ...), custom_call_target="tpu_custom_call" | custom-call | flops 3221225472 | bytes 6291456 | tf_op jit(solution)/shard_map/pallas_call | solution.py:324
  64.8 4.4 %shard_map.101 = (f32[128,3072]{1,0:T(8,128)S(1)}, bf16[128,3072]{1,0:T(8,128)(2,1)S(1)}) custom-call(bf16[256,1024]{1,0:T(8,128)(2,1)S(1)} %get-tuple-element.55.grad_gate, bf16[256,1024]{1,0:T(8,128)(2,1)S(1)} %get-tuple-element.56.grad_up, bf16[3072,1024]{1,0:T(8,128)(2,1)S(1)} %get-tuple-element.50.gate.gate_copy, ...), custom_call_target="tpu_custom_call" | custom-call | flops 3221225472 | bytes 3145728 | tf_op jit(solution)/shard_map/pallas_call | solution.py:370
  69.3 4.4 %shard_map.100 = (f32[128,3200]{1,0:T(8,128)S(1)}, bf16[128,3200]{1,0:T(8,128)(2,1)S(1)}) custom-call(bf16[256,1024]{1,0:T(8,128)(2,1)S(1)} %get-tuple-element.55.grad_gate, bf16[256,1024]{1,0:T(8,128)(2,1)S(1)} %get-tuple-element.56.grad_up, bf16[3072,1024]{1,0:T(8,128)(2,1)S(1)} %get-tuple-element.35.gate.gate_copy, ...), custom_call_target="tpu_custom_call" | custom-call | flops 3221225472 | bytes 3145728 | tf_op jit(solution)/shard_map/pallas_call | solution.py:370
  73.8 0.6 collective-permute-start.18
  74.7 1.5 %collective-permute-start.25 = (bf16[64,1536]{1,0:T(8,128)(2,1)S(1)}, bf16[64,1536]{1,0:T(8,128)(2,1)S(1)}, u32[]{:S(2)}, u32[]{:S(2)}) collective-permute-start(bf16[64,1536]{1,0:T(8,128)(2,1)S(1)} %pad_maximum_fusion.13), channel_id=1, source_target_pairs={{16,0},{0,16},{17,1},{1,17},{18,2},{2,18},{19,3},{3,19},{20,4},{4,... | collective-permute-start | bytes 589832 | tf_op jit(solution)/shard_map/ppermute | solution.py:116
  76.2 1.5 %collective-permute-start.24 = (bf16[64,1536]{1,0:T(8,128)(2,1)S(1)}, bf16[64,1536]{1,0:T(8,128)(2,1)S(1)}, u32[]{:S(2)}, u32[]{:S(2)}) collective-permute-start(bf16[64,1536]{1,0:T(8,128)(2,1)S(1)} %concatenate.112), channel_id=1, source_target_pairs={{8,0},{12,4},{0,8},{4,12},{9,1},{13,5},{1,9},{5,13},{10,2},{14,6},... | collective-permute-start | bytes 589832 | tf_op jit(solution)/shard_map/ppermute | solution.py:116
  78.2 0.6 collective-permute-start.20
  78.8 1.0 collective-permute-start.19
  79.8 2.7 %collective-permute-done.25 = bf16[64,1536]{1,0:T(8,128)(2,1)S(1)} collective-permute-done((bf16[64,1536]{1,0:T(8,128)(2,1)S(1)}, bf16[64,1536]{1,0:T(8,128)(2,1)S(1)}, u32[]{:S(2)}, u32[]{:S(2)}) %collective-permute-start.25) | collective-permute-done | bytes 196640 | tf_op jit(solution)/shard_map/ppermute | solution.py:116
  82.6 1.6 %collective-permute-start.30 = (bf16[32,1536]{1,0:T(8,128)(2,1)S(1)}, bf16[32,1536]{1,0:T(8,128)(2,1)S(1)}, u32[]{:S(2)}, u32[]{:S(2)}) collective-permute-start(bf16[32,1536]{1,0:T(8,128)(2,1)S(1)} %split.121), channel_id=1, source_target_pairs={{8,0},{12,4},{0,8},{4,12},{9,1},{13,5},{1,9},{5,13},{10,2},{14,6},... | collective-permute-start | bytes 294920 | tf_op jit(solution)/shard_map/ppermute | solution.py:116
  84.2 1.6 %collective-permute-start.29 = (bf16[32,1536]{1,0:T(8,128)(2,1)S(1)}, bf16[32,1536]{1,0:T(8,128)(2,1)S(1)}, u32[]{:S(2)}, u32[]{:S(2)}) collective-permute-start(bf16[32,1536]{1,0:T(8,128)(2,1)S(1)} %split.122), channel_id=1, source_target_pairs={{16,0},{0,16},{17,1},{1,17},{18,2},{2,18},{19,3},{3,19},{20,4},{4,... | collective-permute-start | bytes 294920 | tf_op jit(solution)/shard_map/ppermute | solution.py:116
  85.8 2.3 %collective-permute-done.19 = bf16[64,1536]{1,0:T(8,128)(2,1)S(1)} collective-permute-done((bf16[64,1536]{1,0:T(8,128)(2,1)S(1)}, bf16[64,1536]{1,0:T(8,128)(2,1)S(1)}, u32[]{:S(2)}, u32[]{:S(2)}) %collective-permute-start.19) | collective-permute-done | bytes 196640 | tf_op jit(solution)/shard_map/ppermute | solution.py:116
  88.2 0.6 collective-permute-start.22
  88.8 1.6 %collective-permute-start.23 = (bf16[32,1664]{1,0:T(8,128)(2,1)S(1)}, bf16[32,1664]{1,0:T(8,128)(2,1)S(1)}, u32[]{:S(2)}, u32[]{:S(2)}) collective-permute-start(bf16[32,1664]{1,0:T(8,128)(2,1)S(1)} %split.120), channel_id=1, source_target_pairs={{8,0},{12,4},{0,8},{4,12},{9,1},{13,5},{1,9},{5,13},{10,2},{14,6},... | collective-permute-start | bytes 319496 | tf_op jit(solution)/shard_map/ppermute | solution.py:116
  90.5 1.0 collective-permute-start.31
  91.5 2.0 %collective-permute-start.32 = (bf16[8,3072]{1,0:T(8,128)(2,1)S(1)}, bf16[8,3072]{1,0:T(8,128)(2,1)S(1)}, u32[]{:S(2)}, u32[]{:S(2)}) collective-permute-start(bf16[8,3072]{1,0:T(8,128)(2,1)S(1)} %get-tuple-element.95), channel_id=1, source_target_pairs={{2,0},{3,1},{0,2},{1,3},{6,4},{7,5},{4,6},{5,7},{10,8},{11,9},{8,1... | collective-permute-start | bytes 147464 | tf_op jit(solution)/shard_map/ppermute | solution.py:112
  93.5 2.8 %collective-permute-start.33 = (bf16[8,3072]{1,0:T(8,128)(2,1)S(1)}, bf16[8,3072]{1,0:T(8,128)(2,1)S(1)}, u32[]{:S(2)}, u32[]{:S(2)}) collective-permute-start(bf16[8,3072]{1,0:T(8,128)(2,1)S(1)} %get-tuple-element.94), channel_id=1, source_target_pairs={{1,0},{2,1},{3,2},{0,3},{5,4},{6,5},{7,6},{4,7},{9,8},{10,9},{11,1... | collective-permute-start | bytes 147464 | tf_op jit(solution)/shard_map/ppermute | solution.py:112
  96.5 0.6 collective-permute-start.27
  97.1 3.3 %collective-permute-start.28 = (bf16[8,3200]{1,0:T(8,128)(2,1)S(1)}, bf16[8,3200]{1,0:T(8,128)(2,1)S(1)}, u32[]{:S(2)}, u32[]{:S(2)}) collective-permute-start(bf16[8,3200]{1,0:T(8,128)(2,1)S(1)} %get-tuple-element.91), channel_id=1, source_target_pairs={{1,0},{2,1},{3,2},{0,3},{5,4},{6,5},{7,6},{4,7},{9,8},{10,9},{11,1... | collective-permute-start | bytes 153608 | tf_op jit(solution)/shard_map/ppermute | solution.py:112
  100.4 2.0 %collective-permute-done.26 = bf16[8,3200]{1,0:T(8,128)(2,1)S(1)} collective-permute-done((bf16[8,3200]{1,0:T(8,128)(2,1)S(1)}, bf16[8,3200]{1,0:T(8,128)(2,1)S(1)}, u32[]{:S(2)}, u32[]{:S(2)}) %collective-permute-start.26) | collective-permute-done | bytes 51232 | tf_op jit(solution)/shard_map/ppermute | solution.py:112
  102.4 0.6 collective-permute-done.28
  103.3 0.6 pad_maximum_fusion.14
  103.9 0.9 fusion.3
  (102 shorter events, 4.3 us)
Async XLA Ops:
  0.6 7.5 %copy-start = (bf16[6144,4]{0,1:T(4,128)(2,1)S(1)}, bf16[6144,4]{0,1:T(4,128)(2,1)}, u32[]{:S(2)}) copy-start(bf16[6144,4]{0,1:T(4,128)(2,1)} %param.12) | copy-start | bytes 147460
  0.6 10.7 %collective-permute-start = (bf16[8,6144]{1,0:T(8,128)(2,1)}, bf16[8,6144]{1,0:T(8,128)(2,1)S(1)}, u32[]{:S(2)}, u32[]{:S(2)}) collective-permute-start(bf16[8,6144]{1,0:T(8,128)(2,1)} %param.8), channel_id=1, source_target_pairs={{1,0},{2,1},{3,2},{0,3},{5,4},{6,5},{7,6},{4,7},{9,8},{10,9},{11,1... | collective-permute-start | bytes 294920 | tf_op jit(solution)/shard_map/ppermute | solution.py:112
  5.7 9.6 %collective-permute-start.6 = (bf16[8,6144]{1,0:T(8,128)(2,1)}, bf16[8,6144]{1,0:T(8,128)(2,1)S(1)}, u32[]{:S(2)}, u32[]{:S(2)}) collective-permute-start(bf16[8,6144]{1,0:T(8,128)(2,1)} %param.8), channel_id=1, source_target_pairs={{2,0},{3,1},{0,2},{1,3},{6,4},{7,5},{4,6},{5,7},{10,8},{11,9},{8,1... | collective-permute-start | bytes 294920 | tf_op jit(solution)/shard_map/ppermute | solution.py:112
  5.8 9.6 %collective-permute-start.7 = (bf16[8,6144]{1,0:T(8,128)(2,1)}, bf16[8,6144]{1,0:T(8,128)(2,1)S(1)}, u32[]{:S(2)}, u32[]{:S(2)}) collective-permute-start(bf16[8,6144]{1,0:T(8,128)(2,1)} %param.8), channel_id=1, source_target_pairs={{3,0},{0,1},{1,2},{2,3},{7,4},{4,5},{5,6},{6,7},{11,8},{8,9},{9,10... | collective-permute-start | bytes 294920 | tf_op jit(solution)/shard_map/ppermute | solution.py:112
  11.3 11.8 %collective-permute-start.1 = (bf16[8,6272]{1,0:T(8,128)(2,1)S(1)}, bf16[8,6272]{1,0:T(8,128)(2,1)S(1)}, u32[]{:S(2)}, u32[]{:S(2)}) collective-permute-start(bf16[8,6272]{1,0:T(8,128)(2,1)S(1)} %fusion.4), channel_id=1, source_target_pairs={{1,0},{2,1},{3,2},{0,3},{5,4},{6,5},{7,6},{4,7},{9,8},{10,9},{11,1... | collective-permute-start | bytes 301064 | tf_op jit(solution)/shard_map/ppermute | solution.py:112
  14.2 9.4 %collective-permute-start.2 = (bf16[8,6272]{1,0:T(8,128)(2,1)S(1)}, bf16[8,6272]{1,0:T(8,128)(2,1)S(1)}, u32[]{:S(2)}, u32[]{:S(2)}) collective-permute-start(bf16[8,6272]{1,0:T(8,128)(2,1)S(1)} %fusion.4), channel_id=1, source_target_pairs={{2,0},{3,1},{0,2},{1,3},{6,4},{7,5},{4,6},{5,7},{10,8},{11,9},{8,1... | collective-permute-start | bytes 301064 | tf_op jit(solution)/shard_map/ppermute | solution.py:112
  15.3 8.3 %collective-permute-start.3 = (bf16[8,6272]{1,0:T(8,128)(2,1)S(1)}, bf16[8,6272]{1,0:T(8,128)(2,1)S(1)}, u32[]{:S(2)}, u32[]{:S(2)}) collective-permute-start(bf16[8,6272]{1,0:T(8,128)(2,1)S(1)} %fusion.4), channel_id=1, source_target_pairs={{3,0},{0,1},{1,2},{2,3},{7,4},{4,5},{5,6},{6,7},{11,8},{8,9},{9,10... | collective-permute-start | bytes 301064 | tf_op jit(solution)/shard_map/ppermute | solution.py:112
  15.4 8.2 %collective-permute-start.8 = (bf16[32,3072]{1,0:T(8,128)(2,1)S(1)}, bf16[32,3072]{1,0:T(8,128)(2,1)S(1)}, u32[]{:S(2)}, u32[]{:S(2)}) collective-permute-start(bf16[32,3072]{1,0:T(8,128)(2,1)S(1)} %get-tuple-element.37._), channel_id=1, source_target_pairs={{16,0},{0,16},{17,1},{1,17},{18,2},{2,18},{19,3},{3,19},{20,4},{4,... | collective-permute-start | bytes 589832 | tf_op jit(solution)/shard_map/ppermute | solution.py:116
  17.0 6.7 %collective-permute-start.9 = (bf16[32,3072]{1,0:T(8,128)(2,1)S(1)}, bf16[32,3072]{1,0:T(8,128)(2,1)S(1)}, u32[]{:S(2)}, u32[]{:S(2)}) collective-permute-start(bf16[32,3072]{1,0:T(8,128)(2,1)S(1)} %get-tuple-element.39), channel_id=1, source_target_pairs={{8,0},{12,4},{0,8},{4,12},{9,1},{13,5},{1,9},{5,13},{10,2},{14,6},... | collective-permute-start | bytes 589832 | tf_op jit(solution)/shard_map/ppermute | solution.py:116
  23.7 18.1 %collective-permute-start.11 = (bf16[64,3072]{1,0:T(8,128)(2,1)S(1)}, bf16[64,3072]{1,0:T(8,128)(2,1)S(1)}, u32[]{:S(2)}, u32[]{:S(2)}) collective-permute-start(bf16[64,3072]{1,0:T(8,128)(2,1)S(1)} %pad_maximum_fusion.10), channel_id=1, source_target_pairs={{16,0},{0,16},{17,1},{1,17},{18,2},{2,18},{19,3},{3,19},{20,4},{4,... | collective-permute-start | bytes 1179656 | tf_op jit(solution)/shard_map/ppermute | solution.py:116
  25.3 16.5 %collective-permute-start.10 = (bf16[64,3072]{1,0:T(8,128)(2,1)S(1)}, bf16[64,3072]{1,0:T(8,128)(2,1)S(1)}, u32[]{:S(2)}, u32[]{:S(2)}) collective-permute-start(bf16[64,3072]{1,0:T(8,128)(2,1)S(1)} %pad_maximum_fusion.9), channel_id=1, source_target_pairs={{8,0},{12,4},{0,8},{4,12},{9,1},{13,5},{1,9},{5,13},{10,2},{14,6},... | collective-permute-start | bytes 1179656 | tf_op jit(solution)/shard_map/ppermute | solution.py:116
  26.9 12.0 %collective-permute-start.5 = (bf16[32,3072]{1,0:T(8,128)(2,1)S(1)}, bf16[32,3072]{1,0:T(8,128)(2,1)S(1)}, u32[]{:S(2)}, u32[]{:S(2)}) collective-permute-start(bf16[32,3072]{1,0:T(8,128)(2,1)S(1)} %get-tuple-element.43), channel_id=1, source_target_pairs={{8,0},{12,4},{0,8},{4,12},{9,1},{13,5},{1,9},{5,13},{10,2},{14,6},... | collective-permute-start | bytes 589832 | tf_op jit(solution)/shard_map/ppermute | solution.py:116
  27.5 15.1 %collective-permute-start.4 = (bf16[32,3200]{1,0:T(8,128)(2,1)S(1)}, bf16[32,3200]{1,0:T(8,128)(2,1)S(1)}, u32[]{:S(2)}, u32[]{:S(2)}) collective-permute-start(bf16[32,3200]{1,0:T(8,128)(2,1)S(1)} %slice.96), channel_id=1, source_target_pairs={{16,0},{0,16},{17,1},{1,17},{18,2},{2,18},{19,3},{3,19},{20,4},{4,... | collective-permute-start | bytes 614408 | tf_op jit(solution)/shard_map/ppermute | solution.py:116
  41.9 13.4 %collective-permute-start.17 = (bf16[128,3072]{1,0:T(8,128)(2,1)S(1)}, bf16[128,3072]{1,0:T(8,128)(2,1)S(1)}, u32[]{:S(2)}, u32[]{:S(2)}) collective-permute-start(bf16[128,3072]{1,0:T(8,128)(2,1)S(1)} %pad_maximum_fusion.5), channel_id=1, source_target_pairs={{4,0},{0,4},{12,8},{8,12},{5,1},{1,5},{13,9},{9,13},{6,2},{2,6},{1... | collective-permute-start | bytes 2359304 | tf_op jit(solution)/shard_map/ppermute | solution.py:116
  42.1 3.3 %collective-permute-start.14 = (bf16[128,3072]{1,0:T(8,128)(2,1)S(1)}, bf16[128,3072]{1,0:T(8,128)(2,1)S(1)}, u32[]{:S(2)}, u32[]{:S(2)}) collective-permute-start(bf16[128,3072]{1,0:T(8,128)(2,1)S(1)} %pad_maximum_fusion.3), channel_id=1, source_target_pairs={{4,0},{0,4},{12,8},{8,12},{5,1},{1,5},{13,9},{9,13},{6,2},{2,6},{1... | collective-permute-start | bytes 2359304 | tf_op jit(solution)/shard_map/ppermute | solution.py:116
  42.7 11.1 %collective-permute-start.13 = (bf16[64,3072]{1,0:T(8,128)(2,1)S(1)}, bf16[64,3072]{1,0:T(8,128)(2,1)S(1)}, u32[]{:S(2)}, u32[]{:S(2)}) collective-permute-start(bf16[64,3072]{1,0:T(8,128)(2,1)S(1)} %pad_maximum_fusion.11), channel_id=1, source_target_pairs={{16,0},{0,16},{17,1},{1,17},{18,2},{2,18},{19,3},{3,19},{20,4},{4,... | collective-permute-start | bytes 1179656 | tf_op jit(solution)/shard_map/ppermute | solution.py:116
  43.3 11.2 %collective-permute-start.12 = (bf16[64,3200]{1,0:T(8,128)(2,1)S(1)}, bf16[64,3200]{1,0:T(8,128)(2,1)S(1)}, u32[]{:S(2)}, u32[]{:S(2)}) collective-permute-start(bf16[64,3200]{1,0:T(8,128)(2,1)S(1)} %pad_maximum_fusion.7), channel_id=1, source_target_pairs={{8,0},{12,4},{0,8},{4,12},{9,1},{13,5},{1,9},{5,13},{10,2},{14,6},... | collective-permute-start | bytes 1228808 | tf_op jit(solution)/shard_map/ppermute | solution.py:116
  54.6 5.3 %collective-permute-start.16 = (bf16[128,3072]{1,0:T(8,128)(2,1)S(1)}, bf16[128,3072]{1,0:T(8,128)(2,1)S(1)}, u32[]{:S(2)}, u32[]{:S(2)}) collective-permute-start(bf16[128,3072]{1,0:T(8,128)(2,1)S(1)} %pad_maximum_fusion.4), channel_id=1, source_target_pairs={{4,0},{0,4},{12,8},{8,12},{5,1},{1,5},{13,9},{9,13},{6,2},{2,6},{1... | collective-permute-start | bytes 2359304 | tf_op jit(solution)/shard_map/ppermute | solution.py:116
  54.8 5.1 %collective-permute-start.15 = (bf16[128,3200]{1,0:T(8,128)(2,1)S(1)}, bf16[128,3200]{1,0:T(8,128)(2,1)S(1)}, u32[]{:S(2)}, u32[]{:S(2)}) collective-permute-start(bf16[128,3200]{1,0:T(8,128)(2,1)S(1)} %pad_maximum_fusion.2), channel_id=1, source_target_pairs={{4,0},{0,4},{12,8},{8,12},{5,1},{1,5},{13,9},{9,13},{6,2},{2,6},{1... | collective-permute-start | bytes 2457608 | tf_op jit(solution)/shard_map/ppermute | solution.py:116
  69.3 5.1 %collective-permute-start.21 = (bf16[128,3072]{1,0:T(8,128)(2,1)S(1)}, bf16[128,3072]{1,0:T(8,128)(2,1)S(1)}, u32[]{:S(2)}, u32[]{:S(2)}) collective-permute-start(bf16[128,3072]{1,0:T(8,128)(2,1)S(1)} %get-tuple-element.60), channel_id=1, source_target_pairs={{4,0},{0,4},{12,8},{8,12},{5,1},{1,5},{13,9},{9,13},{6,2},{2,6},{1... | collective-permute-start | bytes 2359304 | tf_op jit(solution)/shard_map/ppermute | solution.py:116
  73.8 4.0 %collective-permute-start.18 = (bf16[128,3200]{1,0:T(8,128)(2,1)S(1)}, bf16[128,3200]{1,0:T(8,128)(2,1)S(1)}, u32[]{:S(2)}, u32[]{:S(2)}) collective-permute-start(bf16[128,3200]{1,0:T(8,128)(2,1)S(1)} %get-tuple-element.59), channel_id=1, source_target_pairs={{4,0},{0,4},{12,8},{8,12},{5,1},{1,5},{13,9},{9,13},{6,2},{2,6},{1... | collective-permute-start | bytes 2457608 | tf_op jit(solution)/shard_map/ppermute | solution.py:116
  74.7 7.8 %collective-permute-start.25 = (bf16[64,1536]{1,0:T(8,128)(2,1)S(1)}, bf16[64,1536]{1,0:T(8,128)(2,1)S(1)}, u32[]{:S(2)}, u32[]{:S(2)}) collective-permute-start(bf16[64,1536]{1,0:T(8,128)(2,1)S(1)} %pad_maximum_fusion.13), channel_id=1, source_target_pairs={{16,0},{0,16},{17,1},{1,17},{18,2},{2,18},{19,3},{3,19},{20,4},{4,... | collective-permute-start | bytes 589832 | tf_op jit(solution)/shard_map/ppermute | solution.py:116
  76.2 7.9 %collective-permute-start.24 = (bf16[64,1536]{1,0:T(8,128)(2,1)S(1)}, bf16[64,1536]{1,0:T(8,128)(2,1)S(1)}, u32[]{:S(2)}, u32[]{:S(2)}) collective-permute-start(bf16[64,1536]{1,0:T(8,128)(2,1)S(1)} %concatenate.112), channel_id=1, source_target_pairs={{8,0},{12,4},{0,8},{4,12},{9,1},{13,5},{1,9},{5,13},{10,2},{14,6},... | collective-permute-start | bytes 589832 | tf_op jit(solution)/shard_map/ppermute | solution.py:116
  78.2 9.9 %collective-permute-start.20 = (bf16[64,1664]{1,0:T(8,128)(2,1)S(1)}, bf16[64,1664]{1,0:T(8,128)(2,1)S(1)}, u32[]{:S(2)}, u32[]{:S(2)}) collective-permute-start(bf16[64,1664]{1,0:T(8,128)(2,1)S(1)} %pad_maximum_fusion.12), channel_id=1, source_target_pairs={{16,0},{0,16},{17,1},{1,17},{18,2},{2,18},{19,3},{3,19},{20,4},{4,... | collective-permute-start | bytes 638984 | tf_op jit(solution)/shard_map/ppermute | solution.py:116
  78.8 9.3 %collective-permute-start.19 = (bf16[64,1536]{1,0:T(8,128)(2,1)S(1)}, bf16[64,1536]{1,0:T(8,128)(2,1)S(1)}, u32[]{:S(2)}, u32[]{:S(2)}) collective-permute-start(bf16[64,1536]{1,0:T(8,128)(2,1)S(1)} %concatenate.110), channel_id=1, source_target_pairs={{8,0},{12,4},{0,8},{4,12},{9,1},{13,5},{1,9},{5,13},{10,2},{14,6},... | collective-permute-start | bytes 589832 | tf_op jit(solution)/shard_map/ppermute | solution.py:116
  82.6 7.8 %collective-permute-start.30 = (bf16[32,1536]{1,0:T(8,128)(2,1)S(1)}, bf16[32,1536]{1,0:T(8,128)(2,1)S(1)}, u32[]{:S(2)}, u32[]{:S(2)}) collective-permute-start(bf16[32,1536]{1,0:T(8,128)(2,1)S(1)} %split.121), channel_id=1, source_target_pairs={{8,0},{12,4},{0,8},{4,12},{9,1},{13,5},{1,9},{5,13},{10,2},{14,6},... | collective-permute-start | bytes 294920 | tf_op jit(solution)/shard_map/ppermute | solution.py:116
  84.2 6.2 %collective-permute-start.29 = (bf16[32,1536]{1,0:T(8,128)(2,1)S(1)}, bf16[32,1536]{1,0:T(8,128)(2,1)S(1)}, u32[]{:S(2)}, u32[]{:S(2)}) collective-permute-start(bf16[32,1536]{1,0:T(8,128)(2,1)S(1)} %split.122), channel_id=1, source_target_pairs={{16,0},{0,16},{17,1},{1,17},{18,2},{2,18},{19,3},{3,19},{20,4},{4,... | collective-permute-start | bytes 294920 | tf_op jit(solution)/shard_map/ppermute | solution.py:116
  88.2 8.1 %collective-permute-start.22 = (bf16[32,1536]{1,0:T(8,128)(2,1)S(1)}, bf16[32,1536]{1,0:T(8,128)(2,1)S(1)}, u32[]{:S(2)}, u32[]{:S(2)}) collective-permute-start(bf16[32,1536]{1,0:T(8,128)(2,1)S(1)} %split.123), channel_id=1, source_target_pairs={{16,0},{0,16},{17,1},{1,17},{18,2},{2,18},{19,3},{3,19},{20,4},{4,... | collective-permute-start | bytes 294920 | tf_op jit(solution)/shard_map/ppermute | solution.py:116
  88.8 7.5 %collective-permute-start.23 = (bf16[32,1664]{1,0:T(8,128)(2,1)S(1)}, bf16[32,1664]{1,0:T(8,128)(2,1)S(1)}, u32[]{:S(2)}, u32[]{:S(2)}) collective-permute-start(bf16[32,1664]{1,0:T(8,128)(2,1)S(1)} %split.120), channel_id=1, source_target_pairs={{8,0},{12,4},{0,8},{4,12},{9,1},{13,5},{1,9},{5,13},{10,2},{14,6},... | collective-permute-start | bytes 319496 | tf_op jit(solution)/shard_map/ppermute | solution.py:116
  90.5 6.6 %collective-permute-start.31 = (bf16[8,3072]{1,0:T(8,128)(2,1)S(1)}, bf16[8,3072]{1,0:T(8,128)(2,1)S(1)}, u32[]{:S(2)}, u32[]{:S(2)}) collective-permute-start(bf16[8,3072]{1,0:T(8,128)(2,1)S(1)} %get-tuple-element.93), channel_id=1, source_target_pairs={{3,0},{0,1},{1,2},{2,3},{7,4},{4,5},{5,6},{6,7},{11,8},{8,9},{9,10... | collective-permute-start | bytes 147464 | tf_op jit(solution)/shard_map/ppermute | solution.py:112
  91.5 8.9 %collective-permute-start.32 = (bf16[8,3072]{1,0:T(8,128)(2,1)S(1)}, bf16[8,3072]{1,0:T(8,128)(2,1)S(1)}, u32[]{:S(2)}, u32[]{:S(2)}) collective-permute-start(bf16[8,3072]{1,0:T(8,128)(2,1)S(1)} %get-tuple-element.95), channel_id=1, source_target_pairs={{2,0},{3,1},{0,2},{1,3},{6,4},{7,5},{4,6},{5,7},{10,8},{11,9},{8,1... | collective-permute-start | bytes 147464 | tf_op jit(solution)/shard_map/ppermute | solution.py:112
  93.5 6.9 %collective-permute-start.33 = (bf16[8,3072]{1,0:T(8,128)(2,1)S(1)}, bf16[8,3072]{1,0:T(8,128)(2,1)S(1)}, u32[]{:S(2)}, u32[]{:S(2)}) collective-permute-start(bf16[8,3072]{1,0:T(8,128)(2,1)S(1)} %get-tuple-element.94), channel_id=1, source_target_pairs={{1,0},{2,1},{3,2},{0,3},{5,4},{6,5},{7,6},{4,7},{9,8},{10,9},{11,1... | collective-permute-start | bytes 147464 | tf_op jit(solution)/shard_map/ppermute | solution.py:112
  96.4 6.9 %copy-start.1 = (s32[8]{0:T(128)S(1)}, s32[8]{0:T(128)}, u32[]{:S(2)}) copy-start(s32[8]{0:T(128)} %param.10) | copy-start | bytes 100
  96.5 6.0 %collective-permute-start.26 = (bf16[8,3200]{1,0:T(8,128)(2,1)S(1)}, bf16[8,3200]{1,0:T(8,128)(2,1)S(1)}, u32[]{:S(2)}, u32[]{:S(2)}) collective-permute-start(bf16[8,3200]{1,0:T(8,128)(2,1)S(1)} %get-tuple-element.90), channel_id=1, source_target_pairs={{3,0},{0,1},{1,2},{2,3},{7,4},{4,5},{5,6},{6,7},{11,8},{8,9},{9,10... | collective-permute-start | bytes 153608 | tf_op jit(solution)/shard_map/ppermute | solution.py:112
  96.5 5.9 %collective-permute-start.27 = (bf16[8,3200]{1,0:T(8,128)(2,1)S(1)}, bf16[8,3200]{1,0:T(8,128)(2,1)S(1)}, u32[]{:S(2)}, u32[]{:S(2)}) collective-permute-start(bf16[8,3200]{1,0:T(8,128)(2,1)S(1)} %get-tuple-element.92), channel_id=1, source_target_pairs={{2,0},{3,1},{0,2},{1,3},{6,4},{7,5},{4,6},{5,7},{10,8},{11,9},{8,1... | collective-permute-start | bytes 153608 | tf_op jit(solution)/shard_map/ppermute | solution.py:112
  97.1 5.9 %collective-permute-start.28 = (bf16[8,3200]{1,0:T(8,128)(2,1)S(1)}, bf16[8,3200]{1,0:T(8,128)(2,1)S(1)}, u32[]{:S(2)}, u32[]{:S(2)}) collective-permute-start(bf16[8,3200]{1,0:T(8,128)(2,1)S(1)} %get-tuple-element.91), channel_id=1, source_target_pairs={{1,0},{2,1},{3,2},{0,3},{5,4},{6,5},{7,6},{4,7},{9,8},{10,9},{11,1... | collective-permute-start | bytes 153608 | tf_op jit(solution)/shard_map/ppermute | solution.py:112

commit v10 on v9

--- a/solution.py
+++ b/solution.py
@@ -405,13 +405,13 @@
     token_near = after_others(token_near, (gate_low, up_low))
     token_far = gather_far(*token_near)
     grad_near = gather_near(grad_z, half + table)
-    (down,) = fetch(0, down_weight.shape[1] // 2, grad_near[1][1], down_weight)
+    (down,) = fetch(0, down_weight.shape[1] // 2, token_near[1][1], down_weight)
     grad_far = gather_far(*after_others(grad_near, token_far))
     token_far = after_others(token_far, down)
     token_low, token_high = gather_core(token_near[0], token_far[0], token_near[1], token_far[1])
     pre_gate, pre_up, gate_high, up_high = multiply_tokens(token_low, gate_low, up_low, half, gate_weight, up_weight)
+    pre_gate, pre_up = multiply_tokens(token_high, gate_high, up_high, 0, pre_gate, pre_up)
     grad_far = after_others(grad_far, pre_gate)
-    pre_gate, pre_up = multiply_tokens(token_high, gate_high, up_high, 0, pre_gate, pre_up)
     grad_halves = gather_core(grad_near[0], grad_far[0], grad_near[1], grad_far[1])
     expert = lax.axis_index("expert").astype(jnp.int32).reshape(1)
     grad_gate, grad_up, dots = multiply_grads(expert, *grad_halves, pre_gate, pre_up, down, down_weight)

time: 105 us -> 98.5 us (0.938)
  waiting for transfers between devices: 23.9 us -> 20.5 us
  starting transfers between devices: 41.2 us -> 38 us
    ppermute x22, starting transfers between devices: 21.4 us -> 18.1 us  [swap(): lax.ppermute(value, axis, [(i ^ bit, i) for i in range(lax.axis_size(axis...]
    ppermute x22, waiting for transfers between devices: 20.8 us -> 17.5 us  [swap(): lax.ppermute(value, axis, [(i ^ bit, i) for i in range(lax.axis_size(axis...]
  transfers between devices with their start and end apart: 34 -> 34, of which waited for: 9 -> 11; matrix products, arithmetic and copies ran while one was open for 6% -> 6% of each run, Pallas kernels for 20% -> 21%
where the time goes in v10:
time: 98.5 us; the launch traced here: 98.2 us
  starting transfers between devices  38 us (39%)
  Pallas kernels  30.1 us (31%)
  waiting for transfers between devices  20.5 us (21%)
  other arithmetic  3.96 us (4%)
  local copies, waits for them, and re-layouts  2.29 us (2%)
  matrix products  2.15 us (2%)
  between operations  1.23 us (1%)
    ppermute x12, starting transfers between devices, shift(): lax.ppermute(value, axis, [((i + step) % size, i) for i in range(size)])  19.9 us
    ppermute x22, starting transfers between devices, swap(): lax.ppermute(value, axis, [(i ^ bit, i) for i in range(lax.axis_size(axis...  18.1 us
    ppermute x22, waiting for transfers between devices, swap(): lax.ppermute(value, axis, [(i ^ bit, i) for i in range(lax.axis_size(axis...  17.5 us
    pallas_call x2, Pallas kernels, multiply_tokens(): pl.pallas_call(functools.partial(token_kernel, first), out_shape=sums + f...  9.07 us
    pallas_call x2, Pallas kernels, multiply_outputs(): pl.pallas_call(output_kernel, out_shape=(pltpu.VMEM((rows // 2, total), j...  8.89 us
    pallas_call x2, Pallas kernels, fetch(): pl.pallas_call(functools.partial(fetch_kernel, first), out_shape=tuple((p...  7.41 us
    pallas_call x1, Pallas kernels, multiply_grads(): pl.pallas_call(grad_kernel, out_shape=(pltpu.VMEM((rows, hidden), jnp.bfl...  4.73 us
    ppermute x12, waiting for transfers between devices, shift(): lax.ppermute(value, axis, [((i + step) % size, i) for i in range(size)])  2.98 us
  transfers between devices with their start and end apart: 34, of which 11 were waited for; matrix products, arithmetic and copies ran while one was open for 6% of the time, Pallas kernels for 21%

profile of v10, /device:TPU:0, one launch (start us, length us, event | category | flops | bytes accessed | tf_op | source)
XLA Modules:
  0.0 98.2 jit_solution(629695680215886677)
XLA Ops:
  0.6 5.1 %collective-permute-start = (bf16[8,6144]{1,0:T(8,128)(2,1)}, bf16[8,6144]{1,0:T(8,128)(2,1)S(1)}, u32[]{:S(2)}, u32[]{:S(2)}) collective-permute-start(bf16[8,6144]{1,0:T(8,128)(2,1)} %param.8), channel_id=1, source_target_pairs={{1,0},{2,1},{3,2},{0,3},{5,4},{6,5},{7,6},{4,7},{9,8},{10,9},{11,1... | collective-permute-start | bytes 294920 | tf_op jit(solution)/shard_map/ppermute | solution.py:112
  5.8 1.0 %collective-permute-start.7 = (bf16[8,6144]{1,0:T(8,128)(2,1)}, bf16[8,6144]{1,0:T(8,128)(2,1)S(1)}, u32[]{:S(2)}, u32[]{:S(2)}) collective-permute-start(bf16[8,6144]{1,0:T(8,128)(2,1)} %param.8), channel_id=1, source_target_pairs={{3,0},{0,1},{1,2},{2,3},{7,4},{4,5},{5,6},{6,7},{11,8},{8,9},{9,10... | collective-permute-start | bytes 294920 | tf_op jit(solution)/shard_map/ppermute | solution.py:112
  6.8 0.8 slice_bitcast_fusion
  7.5 0.7 convert_element_type.76
  8.2 1.2 %select_reduce_fusion.3 = (f32[8]{0:T(128)S(1)}, f32[8]{0:T(128)S(1)}) fusion(s32[8]{0:T(128)S(1)} %get-tuple-element.101, s32[8]{0:T(128)S(1)} %get-tuple-element.100, bf16[8,6144]{1,0:T(8,128)(2,1)} %param.8, bf16[6144,4]{0,1:T(4,128)(2,1)S(1)} %copy-done), kind=kOutput, calls=%fused_computation.69 | convolution fusion | flops 393392 | bytes 147584 | tf_op jit(solution)/shard_map/dot_general | solution.py:395
  9.5 0.9 fusion.4
  10.4 0.9 constant_dynamic-update-slice_fusion.7
  11.3 2.9 %collective-permute-start.1 = (bf16[8,6272]{1,0:T(8,128)(2,1)S(1)}, bf16[8,6272]{1,0:T(8,128)(2,1)S(1)}, u32[]{:S(2)}, u32[]{:S(2)}) collective-permute-start(bf16[8,6272]{1,0:T(8,128)(2,1)S(1)} %fusion.4), channel_id=1, source_target_pairs={{1,0},{2,1},{3,2},{0,3},{5,4},{6,5},{7,6},{4,7},{9,8},{10,9},{11,1... | collective-permute-start | bytes 301064 | tf_op jit(solution)/shard_map/ppermute | solution.py:112
  14.2 1.1 %collective-permute-start.2 = (bf16[8,6272]{1,0:T(8,128)(2,1)S(1)}, bf16[8,6272]{1,0:T(8,128)(2,1)S(1)}, u32[]{:S(2)}, u32[]{:S(2)}) collective-permute-start(bf16[8,6272]{1,0:T(8,128)(2,1)S(1)} %fusion.4), channel_id=1, source_target_pairs={{2,0},{3,1},{0,2},{1,3},{6,4},{7,5},{4,6},{5,7},{10,8},{11,9},{8,1... | collective-permute-start | bytes 301064 | tf_op jit(solution)/shard_map/ppermute | solution.py:112
  15.4 1.6 %collective-permute-start.8 = (bf16[32,3072]{1,0:T(8,128)(2,1)S(1)}, bf16[32,3072]{1,0:T(8,128)(2,1)S(1)}, u32[]{:S(2)}, u32[]{:S(2)}) collective-permute-start(bf16[32,3072]{1,0:T(8,128)(2,1)S(1)} %get-tuple-element.37._), channel_id=1, source_target_pairs={{16,0},{0,16},{17,1},{1,17},{18,2},{2,18},{19,3},{3,19},{20,4},{4,... | collective-permute-start | bytes 589832 | tf_op jit(solution)/shard_map/ppermute | solution.py:116
  17.0 1.5 %collective-permute-start.9 = (bf16[32,3072]{1,0:T(8,128)(2,1)S(1)}, bf16[32,3072]{1,0:T(8,128)(2,1)S(1)}, u32[]{:S(2)}, u32[]{:S(2)}) collective-permute-start(bf16[32,3072]{1,0:T(8,128)(2,1)S(1)} %get-tuple-element.39), channel_id=1, source_target_pairs={{8,0},{12,4},{0,8},{4,12},{9,1},{13,5},{1,9},{5,13},{10,2},{14,6},... | collective-permute-start | bytes 589832 | tf_op jit(solution)/shard_map/ppermute | solution.py:116
  18.5 4.6 %shard_map.95 = (bf16[3072,1024]{1,0:T(8,128)(2,1)S(1)}, bf16[3072,1024]{1,0:T(8,128)(2,1)S(1)}) custom-call(bf16[32,3072]{1,0:T(8,128)(2,1)S(1)} %get-tuple-element.37._, bf16[1,6144,1024]{2,1,0:T(8,128)(2,1)} %refs_0_.5, bf16[1,6144,1024]{2,1,0:T(8,128)(2,1)} %refs_1_.3), custom_call_target="tpu_custom_call" | custom-call | bytes 12582912 | tf_op jit(solution)/shard_map/pallas_call | solution.py:215
  23.7 1.6 %collective-permute-start.11 = (bf16[64,3072]{1,0:T(8,128)(2,1)S(1)}, bf16[64,3072]{1,0:T(8,128)(2,1)S(1)}, u32[]{:S(2)}, u32[]{:S(2)}) collective-permute-start(bf16[64,3072]{1,0:T(8,128)(2,1)S(1)} %pad_maximum_fusion.10), channel_id=1, source_target_pairs={{16,0},{0,16},{17,1},{1,17},{18,2},{2,18},{19,3},{3,19},{20,4},{4,... | collective-permute-start | bytes 1179656 | tf_op jit(solution)/shard_map/ppermute | solution.py:116
  25.3 1.6 %collective-permute-start.10 = (bf16[64,3072]{1,0:T(8,128)(2,1)S(1)}, bf16[64,3072]{1,0:T(8,128)(2,1)S(1)}, u32[]{:S(2)}, u32[]{:S(2)}) collective-permute-start(bf16[64,3072]{1,0:T(8,128)(2,1)S(1)} %pad_maximum_fusion.9), channel_id=1, source_target_pairs={{8,0},{12,4},{0,8},{4,12},{9,1},{13,5},{1,9},{5,13},{10,2},{14,6},... | collective-permute-start | bytes 1179656 | tf_op jit(solution)/shard_map/ppermute | solution.py:116
  26.9 0.6 collective-permute-start.5
  28.0 2.8 %shard_map.96.down = bf16[512,6144]{1,0:T(8,128)(2,1)S(1)} custom-call(bf16[32,3072]{1,0:T(8,128)(2,1)S(1)} %collective-permute-done.9._, bf16[1,1024,6144]{2,1,0:T(8,128)(2,1)} %down_weight.1), custom_call_target="tpu_custom_call" | custom-call | bytes 6291456 | tf_op jit(solution)/shard_map/pallas_call | solution.py:215
  30.9 4.8 %collective-permute-done.11 = bf16[64,3072]{1,0:T(8,128)(2,1)S(1)} collective-permute-done((bf16[64,3072]{1,0:T(8,128)(2,1)S(1)}, bf16[64,3072]{1,0:T(8,128)(2,1)S(1)}, u32[]{:S(2)}, u32[]{:S(2)}) %collective-permute-start.11) | collective-permute-done | bytes 393248 | tf_op jit(solution)/shard_map/ppermute | solution.py:116
  35.6 1.2 %collective-permute-done.10 = bf16[64,3072]{1,0:T(8,128)(2,1)S(1)} collective-permute-done((bf16[64,3072]{1,0:T(8,128)(2,1)S(1)}, bf16[64,3072]{1,0:T(8,128)(2,1)S(1)}, u32[]{:S(2)}, u32[]{:S(2)}) %collective-permute-start.10) | collective-permute-done | bytes 393248 | tf_op jit(solution)/shard_map/ppermute | solution.py:116
  37.1 0.6 collective-permute-start.14
  37.7 1.3 %collective-permute-done.5 = bf16[32,3072]{1,0:T(8,128)(2,1)S(1)} collective-permute-done((bf16[32,3072]{1,0:T(8,128)(2,1)S(1)}, bf16[32,3072]{1,0:T(8,128)(2,1)S(1)}, u32[]{:S(2)}, u32[]{:S(2)}) %collective-permute-start.5) | collective-permute-done | bytes 196640 | tf_op jit(solution)/shard_map/ppermute | solution.py:116
  39.0 0.6 collective-permute-start.13
  39.6 1.6 %collective-permute-start.12 = (bf16[64,3200]{1,0:T(8,128)(2,1)S(1)}, bf16[64,3200]{1,0:T(8,128)(2,1)S(1)}, u32[]{:S(2)}, u32[]{:S(2)}) collective-permute-start(bf16[64,3200]{1,0:T(8,128)(2,1)S(1)} %pad_maximum_fusion.7), channel_id=1, source_target_pairs={{8,0},{12,4},{0,8},{4,12},{9,1},{13,5},{1,9},{5,13},{10,2},{14,6},... | collective-permute-start | bytes 1228808 | tf_op jit(solution)/shard_map/ppermute | solution.py:116
  41.4 4.6 %shard_map.97 = (f32[256,1024]{1,0:T(8,128)S(1)}, f32[256,1024]{1,0:T(8,128)S(1)}, bf16[3072,1024]{1,0:T(8,128)(2,1)S(1)}, bf16[3072,1024]{1,0:T(8,128)(2,1)S(1)}) custom-call(bf16[256,3072]{1,0:T(8,128)(2,1)S(1)} %pad_maximum_fusion.1.tokens, bf16[3072,1024]{1,0:T(8,128)(2,1)S(1)} %get-tuple-element.35.gate.gate_copy, ...), custom_call_target="tpu_custom_call" | custom-call | flops 3221225472 | bytes 1572864 | tf_op jit(solution)/shard_map/pallas_call | solution.py:258
  46.1 4.4 %shard_map.98 = (f32[256,1024]{1,0:T(8,128)S(1)}, f32[256,1024]{1,0:T(8,128)S(1)}) custom-call(bf16[256,3072]{1,0:T(8,128)(2,1)S(1)} %constant_dynamic-update-slice_fusion.8.tokens, bf16[3072,1024]{1,0:T(8,128)(2,1)S(1)} %get-tuple-element.47.gate.gate_copy, bf16[3072,1024]{1,0:T(8,128)(2,1)S(1)} %get-tuple-element.48.up.up_copy, ...), custom_call_target="tpu_custom_call" | custom-call | flops 3221225472 | bytes 1572864 | tf_op jit(solution)/shard_map/pallas_call | solution.py:258
  51.4 1.6 %collective-permute-done.17 = bf16[128,3072]{1,0:T(8,128)(2,1)S(1)} collective-permute-done((bf16[128,3072]{1,0:T(8,128)(2,1)S(1)}, bf16[128,3072]{1,0:T(8,128)(2,1)S(1)}, u32[]{:S(2)}, u32[]{:S(2)}) %collective-permute-start.17) | collective-permute-done | bytes 786464 | tf_op jit(solution)/shard_map/ppermute | solution.py:116
  53.1 1.1 %collective-permute-done.16 = bf16[128,3200]{1,0:T(8,128)(2,1)S(1)} collective-permute-done((bf16[128,3200]{1,0:T(8,128)(2,1)S(1)}, bf16[128,3200]{1,0:T(8,128)(2,1)S(1)}, u32[]{:S(2)}, u32[]{:S(2)}) %collective-permute-start.16) | collective-permute-done | bytes 819232 | tf_op jit(solution)/shard_map/ppermute | solution.py:116
  54.3 4.7 %shard_map.99 = (bf16[256,1024]{1,0:T(8,128)(2,1)S(1)}, bf16[256,1024]{1,0:T(8,128)(2,1)S(1)}, bf16[256,128]{1,0:T(8,128)(2,1)S(1)}) custom-call(s32[1]{0:T(128)} %bitcast.expert, bf16[256,3200]{1,0:T(8,128)(2,1)S(1)} %pad_maximum_fusion.low, bf16[256,3072]{1,0:T(8,128)(2,1)S(1)} %constant_dynamic-update-slice_fusion.13.high, ...), custom_call_target="tpu_custom_call" | custom-call | flops 3221225472 | bytes 6291456 | tf_op jit(solution)/shard_map/pallas_call | solution.py:324
  59.0 4.4 %shard_map.101 = (f32[128,3072]{1,0:T(8,128)S(1)}, bf16[128,3072]{1,0:T(8,128)(2,1)S(1)}) custom-call(bf16[256,1024]{1,0:T(8,128)(2,1)S(1)} %get-tuple-element.55.grad_gate, bf16[256,1024]{1,0:T(8,128)(2,1)S(1)} %get-tuple-element.56.grad_up, bf16[3072,1024]{1,0:T(8,128)(2,1)S(1)} %get-tuple-element.47.gate.gate_copy, ...), custom_call_target="tpu_custom_call" | custom-call | flops 3221225472 | bytes 3145728 | tf_op jit(solution)/shard_map/pallas_call | solution.py:370
  63.7 4.4 %shard_map.100 = (f32[128,3200]{1,0:T(8,128)S(1)}, bf16[128,3200]{1,0:T(8,128)(2,1)S(1)}) custom-call(bf16[256,1024]{1,0:T(8,128)(2,1)S(1)} %get-tuple-element.55.grad_gate, bf16[256,1024]{1,0:T(8,128)(2,1)S(1)} %get-tuple-element.56.grad_up, bf16[3072,1024]{1,0:T(8,128)(2,1)S(1)} %get-tuple-element.35.gate.gate_copy, ...), custom_call_target="tpu_custom_call" | custom-call | flops 3221225472 | bytes 3145728 | tf_op jit(solution)/shard_map/pallas_call | solution.py:370
  68.9 1.6 %collective-permute-start.25 = (bf16[64,1536]{1,0:T(8,128)(2,1)S(1)}, bf16[64,1536]{1,0:T(8,128)(2,1)S(1)}, u32[]{:S(2)}, u32[]{:S(2)}) collective-permute-start(bf16[64,1536]{1,0:T(8,128)(2,1)S(1)} %pad_maximum_fusion.13), channel_id=1, source_target_pairs={{16,0},{0,16},{17,1},{1,17},{18,2},{2,18},{19,3},{3,19},{20,4},{4,... | collective-permute-start | bytes 589832 | tf_op jit(solution)/shard_map/ppermute | solution.py:116
  71.4 1.1 %collective-permute-start.20 = (bf16[64,1664]{1,0:T(8,128)(2,1)S(1)}, bf16[64,1664]{1,0:T(8,128)(2,1)S(1)}, u32[]{:S(2)}, u32[]{:S(2)}) collective-permute-start(bf16[64,1664]{1,0:T(8,128)(2,1)S(1)} %pad_maximum_fusion.12), channel_id=1, source_target_pairs={{16,0},{0,16},{17,1},{1,17},{18,2},{2,18},{19,3},{3,19},{20,4},{4,... | collective-permute-start | bytes 638984 | tf_op jit(solution)/shard_map/ppermute | solution.py:116
  72.5 1.0 %collective-permute-start.19 = (bf16[64,1536]{1,0:T(8,128)(2,1)S(1)}, bf16[64,1536]{1,0:T(8,128)(2,1)S(1)}, u32[]{:S(2)}, u32[]{:S(2)}) collective-permute-start(bf16[64,1536]{1,0:T(8,128)(2,1)S(1)} %concatenate.110), channel_id=1, source_target_pairs={{8,0},{12,4},{0,8},{4,12},{9,1},{13,5},{1,9},{5,13},{10,2},{14,6},... | collective-permute-start | bytes 589832 | tf_op jit(solution)/shard_map/ppermute | solution.py:116
  73.5 3.2 %collective-permute-done.25 = bf16[64,1536]{1,0:T(8,128)(2,1)S(1)} collective-permute-done((bf16[64,1536]{1,0:T(8,128)(2,1)S(1)}, bf16[64,1536]{1,0:T(8,128)(2,1)S(1)}, u32[]{:S(2)}, u32[]{:S(2)}) %collective-permute-start.25) | collective-permute-done | bytes 196640 | tf_op jit(solution)/shard_map/ppermute | solution.py:116
  76.8 0.6 collective-permute-start.30
  77.4 0.9 collective-permute-done.24
  78.3 0.7 collective-permute-start.29
  79.0 3.4 %collective-permute-done.19 = bf16[64,1536]{1,0:T(8,128)(2,1)S(1)} collective-permute-done((bf16[64,1536]{1,0:T(8,128)(2,1)S(1)}, bf16[64,1536]{1,0:T(8,128)(2,1)S(1)}, u32[]{:S(2)}, u32[]{:S(2)}) %collective-permute-start.19) | collective-permute-done | bytes 196640 | tf_op jit(solution)/shard_map/ppermute | solution.py:116
  82.5 0.6 collective-permute-start.22
  83.1 0.6 collective-permute-start.23
  83.9 1.1 %collective-permute-start.31 = (bf16[8,3072]{1,0:T(8,128)(2,1)S(1)}, bf16[8,3072]{1,0:T(8,128)(2,1)S(1)}, u32[]{:S(2)}, u32[]{:S(2)}) collective-permute-start(bf16[8,3072]{1,0:T(8,128)(2,1)S(1)} %get-tuple-element.93), channel_id=1, source_target_pairs={{3,0},{0,1},{1,2},{2,3},{7,4},{4,5},{5,6},{6,7},{11,8},{8,9},{9,10... | collective-permute-start | bytes 147464 | tf_op jit(solution)/shard_map/ppermute | solution.py:112
  85.0 1.8 %collective-permute-start.32 = (bf16[8,3072]{1,0:T(8,128)(2,1)S(1)}, bf16[8,3072]{1,0:T(8,128)(2,1)S(1)}, u32[]{:S(2)}, u32[]{:S(2)}) collective-permute-start(bf16[8,3072]{1,0:T(8,128)(2,1)S(1)} %get-tuple-element.95), channel_id=1, source_target_pairs={{2,0},{3,1},{0,2},{1,3},{6,4},{7,5},{4,6},{5,7},{10,8},{11,9},{8,1... | collective-permute-start | bytes 147464 | tf_op jit(solution)/shard_map/ppermute | solution.py:112
  86.8 2.8 %collective-permute-start.33 = (bf16[8,3072]{1,0:T(8,128)(2,1)S(1)}, bf16[8,3072]{1,0:T(8,128)(2,1)S(1)}, u32[]{:S(2)}, u32[]{:S(2)}) collective-permute-start(bf16[8,3072]{1,0:T(8,128)(2,1)S(1)} %get-tuple-element.94), channel_id=1, source_target_pairs={{1,0},{2,1},{3,2},{0,3},{5,4},{6,5},{7,6},{4,7},{9,8},{10,9},{11,1... | collective-permute-start | bytes 147464 | tf_op jit(solution)/shard_map/ppermute | solution.py:112
  89.9 1.1 %collective-permute-start.27 = (bf16[8,3200]{1,0:T(8,128)(2,1)S(1)}, bf16[8,3200]{1,0:T(8,128)(2,1)S(1)}, u32[]{:S(2)}, u32[]{:S(2)}) collective-permute-start(bf16[8,3200]{1,0:T(8,128)(2,1)S(1)} %get-tuple-element.92), channel_id=1, source_target_pairs={{2,0},{3,1},{0,2},{1,3},{6,4},{7,5},{4,6},{5,7},{10,8},{11,9},{8,1... | collective-permute-start | bytes 153608 | tf_op jit(solution)/shard_map/ppermute | solution.py:112
  91.0 2.8 %collective-permute-start.28 = (bf16[8,3200]{1,0:T(8,128)(2,1)S(1)}, bf16[8,3200]{1,0:T(8,128)(2,1)S(1)}, u32[]{:S(2)}, u32[]{:S(2)}) collective-permute-start(bf16[8,3200]{1,0:T(8,128)(2,1)S(1)} %get-tuple-element.91), channel_id=1, source_target_pairs={{1,0},{2,1},{3,2},{0,3},{5,4},{6,5},{7,6},{4,7},{9,8},{10,9},{11,1... | collective-permute-start | bytes 153608 | tf_op jit(solution)/shard_map/ppermute | solution.py:112
  93.9 1.9 %collective-permute-done.26 = bf16[8,3200]{1,0:T(8,128)(2,1)S(1)} collective-permute-done((bf16[8,3200]{1,0:T(8,128)(2,1)S(1)}, bf16[8,3200]{1,0:T(8,128)(2,1)S(1)}, u32[]{:S(2)}, u32[]{:S(2)}) %collective-permute-start.26) | collective-permute-done | bytes 51232 | tf_op jit(solution)/shard_map/ppermute | solution.py:112
  95.8 0.6 collective-permute-done.28
  96.7 0.6 pad_maximum_fusion.14
  97.2 0.9 fusion.3
  (102 shorter events, 5.4 us)
Async XLA Ops:
  0.6 7.5 %copy-start = (bf16[6144,4]{0,1:T(4,128)(2,1)S(1)}, bf16[6144,4]{0,1:T(4,128)(2,1)}, u32[]{:S(2)}) copy-start(bf16[6144,4]{0,1:T(4,128)(2,1)} %param.12) | copy-start | bytes 147460
  0.6 10.7 %collective-permute-start = (bf16[8,6144]{1,0:T(8,128)(2,1)}, bf16[8,6144]{1,0:T(8,128)(2,1)S(1)}, u32[]{:S(2)}, u32[]{:S(2)}) collective-permute-start(bf16[8,6144]{1,0:T(8,128)(2,1)} %param.8), channel_id=1, source_target_pairs={{1,0},{2,1},{3,2},{0,3},{5,4},{6,5},{7,6},{4,7},{9,8},{10,9},{11,1... | collective-permute-start | bytes 294920 | tf_op jit(solution)/shard_map/ppermute | solution.py:112
  5.7 9.6 %collective-permute-start.6 = (bf16[8,6144]{1,0:T(8,128)(2,1)}, bf16[8,6144]{1,0:T(8,128)(2,1)S(1)}, u32[]{:S(2)}, u32[]{:S(2)}) collective-permute-start(bf16[8,6144]{1,0:T(8,128)(2,1)} %param.8), channel_id=1, source_target_pairs={{2,0},{3,1},{0,2},{1,3},{6,4},{7,5},{4,6},{5,7},{10,8},{11,9},{8,1... | collective-permute-start | bytes 294920 | tf_op jit(solution)/shard_map/ppermute | solution.py:112
  5.8 9.6 %collective-permute-start.7 = (bf16[8,6144]{1,0:T(8,128)(2,1)}, bf16[8,6144]{1,0:T(8,128)(2,1)S(1)}, u32[]{:S(2)}, u32[]{:S(2)}) collective-permute-start(bf16[8,6144]{1,0:T(8,128)(2,1)} %param.8), channel_id=1, source_target_pairs={{3,0},{0,1},{1,2},{2,3},{7,4},{4,5},{5,6},{6,7},{11,8},{8,9},{9,10... | collective-permute-start | bytes 294920 | tf_op jit(solution)/shard_map/ppermute | solution.py:112
  11.3 11.8 %collective-permute-start.1 = (bf16[8,6272]{1,0:T(8,128)(2,1)S(1)}, bf16[8,6272]{1,0:T(8,128)(2,1)S(1)}, u32[]{:S(2)}, u32[]{:S(2)}) collective-permute-start(bf16[8,6272]{1,0:T(8,128)(2,1)S(1)} %fusion.4), channel_id=1, source_target_pairs={{1,0},{2,1},{3,2},{0,3},{5,4},{6,5},{7,6},{4,7},{9,8},{10,9},{11,1... | collective-permute-start | bytes 301064 | tf_op jit(solution)/shard_map/ppermute | solution.py:112
  14.2 9.4 %collective-permute-start.2 = (bf16[8,6272]{1,0:T(8,128)(2,1)S(1)}, bf16[8,6272]{1,0:T(8,128)(2,1)S(1)}, u32[]{:S(2)}, u32[]{:S(2)}) collective-permute-start(bf16[8,6272]{1,0:T(8,128)(2,1)S(1)} %fusion.4), channel_id=1, source_target_pairs={{2,0},{3,1},{0,2},{1,3},{6,4},{7,5},{4,6},{5,7},{10,8},{11,9},{8,1... | collective-permute-start | bytes 301064 | tf_op jit(solution)/shard_map/ppermute | solution.py:112
  15.3 8.3 %collective-permute-start.3 = (bf16[8,6272]{1,0:T(8,128)(2,1)S(1)}, bf16[8,6272]{1,0:T(8,128)(2,1)S(1)}, u32[]{:S(2)}, u32[]{:S(2)}) collective-permute-start(bf16[8,6272]{1,0:T(8,128)(2,1)S(1)} %fusion.4), channel_id=1, source_target_pairs={{3,0},{0,1},{1,2},{2,3},{7,4},{4,5},{5,6},{6,7},{11,8},{8,9},{9,10... | collective-permute-start | bytes 301064 | tf_op jit(solution)/shard_map/ppermute | solution.py:112
  15.4 8.2 %collective-permute-start.8 = (bf16[32,3072]{1,0:T(8,128)(2,1)S(1)}, bf16[32,3072]{1,0:T(8,128)(2,1)S(1)}, u32[]{:S(2)}, u32[]{:S(2)}) collective-permute-start(bf16[32,3072]{1,0:T(8,128)(2,1)S(1)} %get-tuple-element.37._), channel_id=1, source_target_pairs={{16,0},{0,16},{17,1},{1,17},{18,2},{2,18},{19,3},{3,19},{20,4},{4,... | collective-permute-start | bytes 589832 | tf_op jit(solution)/shard_map/ppermute | solution.py:116
  17.0 6.7 %collective-permute-start.9 = (bf16[32,3072]{1,0:T(8,128)(2,1)S(1)}, bf16[32,3072]{1,0:T(8,128)(2,1)S(1)}, u32[]{:S(2)}, u32[]{:S(2)}) collective-permute-start(bf16[32,3072]{1,0:T(8,128)(2,1)S(1)} %get-tuple-element.39), channel_id=1, source_target_pairs={{8,0},{12,4},{0,8},{4,12},{9,1},{13,5},{1,9},{5,13},{10,2},{14,6},... | collective-permute-start | bytes 589832 | tf_op jit(solution)/shard_map/ppermute | solution.py:116
  23.7 11.9 %collective-permute-start.11 = (bf16[64,3072]{1,0:T(8,128)(2,1)S(1)}, bf16[64,3072]{1,0:T(8,128)(2,1)S(1)}, u32[]{:S(2)}, u32[]{:S(2)}) collective-permute-start(bf16[64,3072]{1,0:T(8,128)(2,1)S(1)} %pad_maximum_fusion.10), channel_id=1, source_target_pairs={{16,0},{0,16},{17,1},{1,17},{18,2},{2,18},{19,3},{3,19},{20,4},{4,... | collective-permute-start | bytes 1179656 | tf_op jit(solution)/shard_map/ppermute | solution.py:116
  25.3 11.6 %collective-permute-start.10 = (bf16[64,3072]{1,0:T(8,128)(2,1)S(1)}, bf16[64,3072]{1,0:T(8,128)(2,1)S(1)}, u32[]{:S(2)}, u32[]{:S(2)}) collective-permute-start(bf16[64,3072]{1,0:T(8,128)(2,1)S(1)} %pad_maximum_fusion.9), channel_id=1, source_target_pairs={{8,0},{12,4},{0,8},{4,12},{9,1},{13,5},{1,9},{5,13},{10,2},{14,6},... | collective-permute-start | bytes 1179656 | tf_op jit(solution)/shard_map/ppermute | solution.py:116
  26.9 12.0 %collective-permute-start.5 = (bf16[32,3072]{1,0:T(8,128)(2,1)S(1)}, bf16[32,3072]{1,0:T(8,128)(2,1)S(1)}, u32[]{:S(2)}, u32[]{:S(2)}) collective-permute-start(bf16[32,3072]{1,0:T(8,128)(2,1)S(1)} %get-tuple-element.43), channel_id=1, source_target_pairs={{8,0},{12,4},{0,8},{4,12},{9,1},{13,5},{1,9},{5,13},{10,2},{14,6},... | collective-permute-start | bytes 589832 | tf_op jit(solution)/shard_map/ppermute | solution.py:116
  27.5 11.5 %collective-permute-start.4 = (bf16[32,3200]{1,0:T(8,128)(2,1)S(1)}, bf16[32,3200]{1,0:T(8,128)(2,1)S(1)}, u32[]{:S(2)}, u32[]{:S(2)}) collective-permute-start(bf16[32,3200]{1,0:T(8,128)(2,1)S(1)} %slice.96), channel_id=1, source_target_pairs={{16,0},{0,16},{17,1},{1,17},{18,2},{2,18},{19,3},{3,19},{20,4},{4,... | collective-permute-start | bytes 614408 | tf_op jit(solution)/shard_map/ppermute | solution.py:116
  36.9 4.3 %collective-permute-start.15 = (bf16[128,3072]{1,0:T(8,128)(2,1)S(1)}, bf16[128,3072]{1,0:T(8,128)(2,1)S(1)}, u32[]{:S(2)}, u32[]{:S(2)}) collective-permute-start(bf16[128,3072]{1,0:T(8,128)(2,1)S(1)} %pad_maximum_fusion.4), channel_id=1, source_target_pairs={{4,0},{0,4},{12,8},{8,12},{5,1},{1,5},{13,9},{9,13},{6,2},{2,6},{1... | collective-permute-start | bytes 2359304 | tf_op jit(solution)/shard_map/ppermute | solution.py:116
  37.1 4.2 %collective-permute-start.14 = (bf16[128,3072]{1,0:T(8,128)(2,1)S(1)}, bf16[128,3072]{1,0:T(8,128)(2,1)S(1)}, u32[]{:S(2)}, u32[]{:S(2)}) collective-permute-start(bf16[128,3072]{1,0:T(8,128)(2,1)S(1)} %pad_maximum_fusion.3), channel_id=1, source_target_pairs={{4,0},{0,4},{12,8},{8,12},{5,1},{1,5},{13,9},{9,13},{6,2},{2,6},{1... | collective-permute-start | bytes 2359304 | tf_op jit(solution)/shard_map/ppermute | solution.py:116
  39.0 11.5 %collective-permute-start.13 = (bf16[64,3072]{1,0:T(8,128)(2,1)S(1)}, bf16[64,3072]{1,0:T(8,128)(2,1)S(1)}, u32[]{:S(2)}, u32[]{:S(2)}) collective-permute-start(bf16[64,3072]{1,0:T(8,128)(2,1)S(1)} %pad_maximum_fusion.11), channel_id=1, source_target_pairs={{16,0},{0,16},{17,1},{1,17},{18,2},{2,18},{19,3},{3,19},{20,4},{4,... | collective-permute-start | bytes 1179656 | tf_op jit(solution)/shard_map/ppermute | solution.py:116
  39.6 10.9 %collective-permute-start.12 = (bf16[64,3200]{1,0:T(8,128)(2,1)S(1)}, bf16[64,3200]{1,0:T(8,128)(2,1)S(1)}, u32[]{:S(2)}, u32[]{:S(2)}) collective-permute-start(bf16[64,3200]{1,0:T(8,128)(2,1)S(1)} %pad_maximum_fusion.7), channel_id=1, source_target_pairs={{8,0},{12,4},{0,8},{4,12},{9,1},{13,5},{1,9},{5,13},{10,2},{14,6},... | collective-permute-start | bytes 1228808 | tf_op jit(solution)/shard_map/ppermute | solution.py:116
  50.7 2.4 %collective-permute-start.17 = (bf16[128,3072]{1,0:T(8,128)(2,1)S(1)}, bf16[128,3072]{1,0:T(8,128)(2,1)S(1)}, u32[]{:S(2)}, u32[]{:S(2)}) collective-permute-start(bf16[128,3072]{1,0:T(8,128)(2,1)S(1)} %pad_maximum_fusion.5), channel_id=1, source_target_pairs={{4,0},{0,4},{12,8},{8,12},{5,1},{1,5},{13,9},{9,13},{6,2},{2,6},{1... | collective-permute-start | bytes 2359304 | tf_op jit(solution)/shard_map/ppermute | solution.py:116
  50.8 3.4 %collective-permute-start.16 = (bf16[128,3200]{1,0:T(8,128)(2,1)S(1)}, bf16[128,3200]{1,0:T(8,128)(2,1)S(1)}, u32[]{:S(2)}, u32[]{:S(2)}) collective-permute-start(bf16[128,3200]{1,0:T(8,128)(2,1)S(1)} %pad_maximum_fusion.2), channel_id=1, source_target_pairs={{4,0},{0,4},{12,8},{8,12},{5,1},{1,5},{13,9},{9,13},{6,2},{2,6},{1... | collective-permute-start | bytes 2457608 | tf_op jit(solution)/shard_map/ppermute | solution.py:116
  63.5 5.1 %collective-permute-start.21 = (bf16[128,3072]{1,0:T(8,128)(2,1)S(1)}, bf16[128,3072]{1,0:T(8,128)(2,1)S(1)}, u32[]{:S(2)}, u32[]{:S(2)}) collective-permute-start(bf16[128,3072]{1,0:T(8,128)(2,1)S(1)} %get-tuple-element.60), channel_id=1, source_target_pairs={{4,0},{0,4},{12,8},{8,12},{5,1},{1,5},{13,9},{9,13},{6,2},{2,6},{1... | collective-permute-start | bytes 2359304 | tf_op jit(solution)/shard_map/ppermute | solution.py:116
  68.1 2.9 %collective-permute-start.18 = (bf16[128,3200]{1,0:T(8,128)(2,1)S(1)}, bf16[128,3200]{1,0:T(8,128)(2,1)S(1)}, u32[]{:S(2)}, u32[]{:S(2)}) collective-permute-start(bf16[128,3200]{1,0:T(8,128)(2,1)S(1)} %get-tuple-element.59), channel_id=1, source_target_pairs={{4,0},{0,4},{12,8},{8,12},{5,1},{1,5},{13,9},{9,13},{6,2},{2,6},{1... | collective-permute-start | bytes 2457608 | tf_op jit(solution)/shard_map/ppermute | solution.py:116
  68.9 7.8 %collective-permute-start.25 = (bf16[64,1536]{1,0:T(8,128)(2,1)S(1)}, bf16[64,1536]{1,0:T(8,128)(2,1)S(1)}, u32[]{:S(2)}, u32[]{:S(2)}) collective-permute-start(bf16[64,1536]{1,0:T(8,128)(2,1)S(1)} %pad_maximum_fusion.13), channel_id=1, source_target_pairs={{16,0},{0,16},{17,1},{1,17},{18,2},{2,18},{19,3},{3,19},{20,4},{4,... | collective-permute-start | bytes 589832 | tf_op jit(solution)/shard_map/ppermute | solution.py:116
  70.5 7.8 %collective-permute-start.24 = (bf16[64,1536]{1,0:T(8,128)(2,1)S(1)}, bf16[64,1536]{1,0:T(8,128)(2,1)S(1)}, u32[]{:S(2)}, u32[]{:S(2)}) collective-permute-start(bf16[64,1536]{1,0:T(8,128)(2,1)S(1)} %concatenate.112), channel_id=1, source_target_pairs={{8,0},{12,4},{0,8},{4,12},{9,1},{13,5},{1,9},{5,13},{10,2},{14,6},... | collective-permute-start | bytes 589832 | tf_op jit(solution)/shard_map/ppermute | solution.py:116
  71.4 11.0 %collective-permute-start.20 = (bf16[64,1664]{1,0:T(8,128)(2,1)S(1)}, bf16[64,1664]{1,0:T(8,128)(2,1)S(1)}, u32[]{:S(2)}, u32[]{:S(2)}) collective-permute-start(bf16[64,1664]{1,0:T(8,128)(2,1)S(1)} %pad_maximum_fusion.12), channel_id=1, source_target_pairs={{16,0},{0,16},{17,1},{1,17},{18,2},{2,18},{19,3},{3,19},{20,4},{4,... | collective-permute-start | bytes 638984 | tf_op jit(solution)/shard_map/ppermute | solution.py:116
  72.5 9.9 %collective-permute-start.19 = (bf16[64,1536]{1,0:T(8,128)(2,1)S(1)}, bf16[64,1536]{1,0:T(8,128)(2,1)S(1)}, u32[]{:S(2)}, u32[]{:S(2)}) collective-permute-start(bf16[64,1536]{1,0:T(8,128)(2,1)S(1)} %concatenate.110), channel_id=1, source_target_pairs={{8,0},{12,4},{0,8},{4,12},{9,1},{13,5},{1,9},{5,13},{10,2},{14,6},... | collective-permute-start | bytes 589832 | tf_op jit(solution)/shard_map/ppermute | solution.py:116
  76.8 7.0 %collective-permute-start.30 = (bf16[32,1536]{1,0:T(8,128)(2,1)S(1)}, bf16[32,1536]{1,0:T(8,128)(2,1)S(1)}, u32[]{:S(2)}, u32[]{:S(2)}) collective-permute-start(bf16[32,1536]{1,0:T(8,128)(2,1)S(1)} %split.121), channel_id=1, source_target_pairs={{8,0},{12,4},{0,8},{4,12},{9,1},{13,5},{1,9},{5,13},{10,2},{14,6},... | collective-permute-start | bytes 294920 | tf_op jit(solution)/shard_map/ppermute | solution.py:116
  78.3 5.5 %collective-permute-start.29 = (bf16[32,1536]{1,0:T(8,128)(2,1)S(1)}, bf16[32,1536]{1,0:T(8,128)(2,1)S(1)}, u32[]{:S(2)}, u32[]{:S(2)}) collective-permute-start(bf16[32,1536]{1,0:T(8,128)(2,1)S(1)} %split.122), channel_id=1, source_target_pairs={{16,0},{0,16},{17,1},{1,17},{18,2},{2,18},{19,3},{3,19},{20,4},{4,... | collective-permute-start | bytes 294920 | tf_op jit(solution)/shard_map/ppermute | solution.py:116
  82.5 7.1 %collective-permute-start.22 = (bf16[32,1536]{1,0:T(8,128)(2,1)S(1)}, bf16[32,1536]{1,0:T(8,128)(2,1)S(1)}, u32[]{:S(2)}, u32[]{:S(2)}) collective-permute-start(bf16[32,1536]{1,0:T(8,128)(2,1)S(1)} %split.123), channel_id=1, source_target_pairs={{16,0},{0,16},{17,1},{1,17},{18,2},{2,18},{19,3},{3,19},{20,4},{4,... | collective-permute-start | bytes 294920 | tf_op jit(solution)/shard_map/ppermute | solution.py:116
  83.1 6.6 %collective-permute-start.23 = (bf16[32,1664]{1,0:T(8,128)(2,1)S(1)}, bf16[32,1664]{1,0:T(8,128)(2,1)S(1)}, u32[]{:S(2)}, u32[]{:S(2)}) collective-permute-start(bf16[32,1664]{1,0:T(8,128)(2,1)S(1)} %split.120), channel_id=1, source_target_pairs={{8,0},{12,4},{0,8},{4,12},{9,1},{13,5},{1,9},{5,13},{10,2},{14,6},... | collective-permute-start | bytes 319496 | tf_op jit(solution)/shard_map/ppermute | solution.py:116
  83.9 7.1 %collective-permute-start.31 = (bf16[8,3072]{1,0:T(8,128)(2,1)S(1)}, bf16[8,3072]{1,0:T(8,128)(2,1)S(1)}, u32[]{:S(2)}, u32[]{:S(2)}) collective-permute-start(bf16[8,3072]{1,0:T(8,128)(2,1)S(1)} %get-tuple-element.93), channel_id=1, source_target_pairs={{3,0},{0,1},{1,2},{2,3},{7,4},{4,5},{5,6},{6,7},{11,8},{8,9},{9,10... | collective-permute-start | bytes 147464 | tf_op jit(solution)/shard_map/ppermute | solution.py:112
  85.0 8.8 %collective-permute-start.32 = (bf16[8,3072]{1,0:T(8,128)(2,1)S(1)}, bf16[8,3072]{1,0:T(8,128)(2,1)S(1)}, u32[]{:S(2)}, u32[]{:S(2)}) collective-permute-start(bf16[8,3072]{1,0:T(8,128)(2,1)S(1)} %get-tuple-element.95), channel_id=1, source_target_pairs={{2,0},{3,1},{0,2},{1,3},{6,4},{7,5},{4,6},{5,7},{10,8},{11,9},{8,1... | collective-permute-start | bytes 147464 | tf_op jit(solution)/shard_map/ppermute | solution.py:112
  86.8 7.0 %collective-permute-start.33 = (bf16[8,3072]{1,0:T(8,128)(2,1)S(1)}, bf16[8,3072]{1,0:T(8,128)(2,1)S(1)}, u32[]{:S(2)}, u32[]{:S(2)}) collective-permute-start(bf16[8,3072]{1,0:T(8,128)(2,1)S(1)} %get-tuple-element.94), channel_id=1, source_target_pairs={{1,0},{2,1},{3,2},{0,3},{5,4},{6,5},{7,6},{4,7},{9,8},{10,9},{11,1... | collective-permute-start | bytes 147464 | tf_op jit(solution)/shard_map/ppermute | solution.py:112
  89.7 6.9 %copy-start.1 = (s32[8]{0:T(128)S(1)}, s32[8]{0:T(128)}, u32[]{:S(2)}) copy-start(s32[8]{0:T(128)} %param.10) | copy-start | bytes 100
  89.8 6.0 %collective-permute-start.26 = (bf16[8,3200]{1,0:T(8,128)(2,1)S(1)}, bf16[8,3200]{1,0:T(8,128)(2,1)S(1)}, u32[]{:S(2)}, u32[]{:S(2)}) collective-permute-start(bf16[8,3200]{1,0:T(8,128)(2,1)S(1)} %get-tuple-element.90), channel_id=1, source_target_pairs={{3,0},{0,1},{1,2},{2,3},{7,4},{4,5},{5,6},{6,7},{11,8},{8,9},{9,10... | collective-permute-start | bytes 153608 | tf_op jit(solution)/shard_map/ppermute | solution.py:112
  89.9 5.9 %collective-permute-start.27 = (bf16[8,3200]{1,0:T(8,128)(2,1)S(1)}, bf16[8,3200]{1,0:T(8,128)(2,1)S(1)}, u32[]{:S(2)}, u32[]{:S(2)}) collective-permute-start(bf16[8,3200]{1,0:T(8,128)(2,1)S(1)} %get-tuple-element.92), channel_id=1, source_target_pairs={{2,0},{3,1},{0,2},{1,3},{6,4},{7,5},{4,6},{5,7},{10,8},{11,9},{8,1... | collective-permute-start | bytes 153608 | tf_op jit(solution)/shard_map/ppermute | solution.py:112
  91.0 5.4 %collective-permute-start.28 = (bf16[8,3200]{1,0:T(8,128)(2,1)S(1)}, bf16[8,3200]{1,0:T(8,128)(2,1)S(1)}, u32[]{:S(2)}, u32[]{:S(2)}) collective-permute-start(bf16[8,3200]{1,0:T(8,128)(2,1)S(1)} %get-tuple-element.91), channel_id=1, source_target_pairs={{1,0},{2,1},{3,2},{0,3},{5,4},{6,5},{7,6},{4,7},{9,8},{10,9},{11,1... | collective-permute-start | bytes 153608 | tf_op jit(solution)/shard_map/ppermute | solution.py:112

commit v11 on v10

--- a/solution.py
+++ b/solution.py
@@ -9,8 +9,8 @@
 from jax.sharding import PartitionSpec as P
 
 TOKEN_PART = 512
-HIDDEN_PART = 256
-COLUMN_PART = 512
+HIDDEN_PART = 512
+COLUMN_PART = 1024
 TOKEN_VMEM = 6 * 2 ** 20
 GRAD_VMEM = 10 * 2 ** 20
 OUTPUT_VMEM = 6 * 2 ** 20
@@ -225,9 +225,9 @@
     )(earlier, *[in_hbm(value) for value in weights])
 
 
-def token_kernel(first, tokens, gate, up, *refs):
+def token_kernel(first, offset, length, tokens, gate, up, *refs):
     pre_gate, pre_up = refs[2:4]
-    depth = part_of(tokens.shape[1], TOKEN_PART)
+    depth = part_of(length, TOKEN_PART)
     copies = []
     if first:
         for index in range(2):
@@ -238,9 +238,9 @@
     pre_gate[...] = jnp.zeros_like(pre_gate) if first else refs[0][...]
     pre_up[...] = jnp.zeros_like(pre_up) if first else refs[1][...]
 
-    @pl.loop(0, tokens.shape[1] // depth)
+    @pl.loop(0, length // depth)
     def _(step):
-        rows = pl.ds(pl.multiple_of(step * depth, depth), depth)
+        rows = pl.ds(pl.multiple_of(offset + step * depth, depth), depth)
         pre_gate[...] += product(tokens[:, rows], gate[rows, :], 0)
         pre_up[...] += product(tokens[:, rows], up[rows, :], 0)
 
@@ -248,15 +248,14 @@
         copy.wait()
 
 
-def multiply_tokens(tokens, gate, up, first, *others):
-    rows, width = tokens.shape
-    hidden = gate.shape[1]
+def multiply_tokens(tokens, gate, up, offset, length, first, *others):
+    rows, hidden = tokens.shape[0], gate.shape[1]
     sums = (pltpu.VMEM((rows, hidden), jnp.float32),) * 2
     fetched = (pltpu.VMEM(gate.shape, jnp.bfloat16),) * 2 if first else ()
     if first:
         others = [in_hbm(value) for value in others]
     return pl.pallas_call(
-        functools.partial(token_kernel, first),
+        functools.partial(token_kernel, first, offset, length),
         out_shape=sums + fetched,
         in_specs=[pl.BlockSpec(memory_space=pltpu.VMEM)] * 3
         + [pl.BlockSpec(memory_space=pl.ANY if first else pltpu.VMEM)] * 2,
@@ -264,7 +263,7 @@
         scratch_shapes=[pltpu.SemaphoreType.DMA((2,))] if first else [],
         compiler_params=pltpu.CompilerParams(vmem_limit_bytes=TOKEN_VMEM),
         cost_estimate=pl.CostEstimate(
-            flops=4 * rows * width * hidden, bytes_accessed=2 * rows * width, transcendentals=0
+            flops=4 * rows * length * hidden, bytes_accessed=2 * rows * length, transcendentals=0
         ),
     )(tokens, gate, up, *others)
 
@@ -295,7 +294,7 @@
     def block(weights, first, step):
         rows = pl.ds(pl.multiple_of(step * depth, depth), depth)
         span = pl.ds(pl.multiple_of(first + step * depth, depth), depth)
-        grad_hidden = product(low[:, table:], weights[rows, :half], 1) + product(high[...], weights[rows, half:], 1)
+        grad_hidden = (product(weights[rows, :half], low[:, table:], 1) + product(weights[rows, half:], high[...], 1)).T
         gates = pre_gate[:, span]
         ups = pre_up[:, span]
         sigma = jax.nn.sigmoid(gates)
@@ -354,7 +353,7 @@
     @pl.loop(0, columns // part)
     def _(step):
         span = pl.ds(pl.multiple_of(step * part, part), part)
-        result = product(grad_gate[...], gate_copy[span, :], 1) + product(grad_up[...], up_copy[span, :], 1)
+        result = (product(gate_copy[span, :], grad_gate[...], 1) + product(up_copy[span, :], grad_up[...], 1)).T
         kept[:, span] = result[:rows]
         sent[:, span] = result[rows:].astype(jnp.bfloat16)
 
@@ -389,7 +388,7 @@
     first_hot = (routes[:, 0:1] == columns).astype(jnp.float32)
     second_hot = (routes[:, 1:2] == columns).astype(jnp.float32)
     keep_rows = kept_mask.astype(jnp.float32)
-    half = width // 2
+    half, quarter = width // 2, width // 4
     table = 128
     token_z = gather_z(tokens)
     logits = jnp.dot(tokens, router, preferred_element_type=jnp.float32)
@@ -409,9 +408,12 @@
     grad_far = gather_far(*after_others(grad_near, token_far))
     token_far = after_others(token_far, down)
     token_low, token_high = gather_core(token_near[0], token_far[0], token_near[1], token_far[1])
-    pre_gate, pre_up, gate_high, up_high = multiply_tokens(token_low, gate_low, up_low, half, gate_weight, up_weight)
-    pre_gate, pre_up = multiply_tokens(token_high, gate_high, up_high, 0, pre_gate, pre_up)
+    pre_gate, pre_up, gate_high, up_high = multiply_tokens(
+        token_low, gate_low, up_low, 0, half, half, gate_weight, up_weight
+    )
+    pre_gate, pre_up = multiply_tokens(token_high, gate_high, up_high, 0, quarter, 0, pre_gate, pre_up)
     grad_far = after_others(grad_far, pre_gate)
+    pre_gate, pre_up = multiply_tokens(token_high, gate_high, up_high, quarter, quarter, 0, pre_gate, pre_up)
     grad_halves = gather_core(grad_near[0], grad_far[0], grad_near[1], grad_far[1])
     expert = lax.axis_index("expert").astype(jnp.int32).reshape(1)
     grad_gate, grad_up, dots = multiply_grads(expert, *grad_halves, pre_gate, pre_up, down, down_weight)

time: 98.5 us -> 100 us (1.015)
  waiting for transfers between devices: 20.5 us -> 17.1 us
  starting transfers between devices: 38 us -> 41.2 us
  Pallas kernels: 30.1 us -> 32.3 us
    ppermute x22, waiting for transfers between devices: 17.5 us -> 14 us  [swap(): lax.ppermute(value, axis, [(i ^ bit, i) for i in range(lax.axis_size(axis...]
    ppermute x22, starting transfers between devices: 18.1 us -> 21.4 us  [swap(): lax.ppermute(value, axis, [(i ^ bit, i) for i in range(lax.axis_size(axis...]
    pallas_call x1, Pallas kernels: 4.73 us -> 7.53 us  [multiply_grads(): pl.pallas_call(grad_kernel, out_shape=(pltpu.VMEM((rows, hidden), jnp.bfl...]
    pallas_call x2 -> x3, Pallas kernels: 9.07 us -> 9.21 us  [multiply_tokens(): pl.pallas_call(functools.partial(token_kernel, first, offset, length), ou...]
where the time goes in v11:
time: 100 us
  starting transfers between devices  41.2 us (41%)
  Pallas kernels  32.3 us (32%)
  waiting for transfers between devices  17.1 us (17%)
  other arithmetic  3.92 us (4%)
  local copies, waits for them, and re-layouts  2.29 us (2%)
  matrix products  2.15 us (2%)
  between operations  1.24 us (1%)
    ppermute x22, starting transfers between devices, swap(): lax.ppermute(value, axis, [(i ^ bit, i) for i in range(lax.axis_size(axis...  21.4 us
    ppermute x12, starting transfers between devices, shift(): lax.ppermute(value, axis, [((i + step) % size, i) for i in range(size)])  19.8 us
    ppermute x22, waiting for transfers between devices, swap(): lax.ppermute(value, axis, [(i ^ bit, i) for i in range(lax.axis_size(axis...  14 us
    pallas_call x3, Pallas kernels, multiply_tokens(): pl.pallas_call(functools.partial(token_kernel, first, offset, length), ou...  9.21 us
    pallas_call x2, Pallas kernels, multiply_outputs(): pl.pallas_call(output_kernel, out_shape=(pltpu.VMEM((rows // 2, total), j...  8.15 us
    pallas_call x1, Pallas kernels, multiply_grads(): pl.pallas_call(grad_kernel, out_shape=(pltpu.VMEM((rows, hidden), jnp.bfl...  7.53 us
    pallas_call x2, Pallas kernels, fetch(): pl.pallas_call(functools.partial(fetch_kernel, first), out_shape=tuple((p...  7.41 us
    ppermute x12, waiting for transfers between devices, shift(): lax.ppermute(value, axis, [((i + step) % size, i) for i in range(size)])  3.1 us
  transfers between devices with their start and end apart: 34, of which 11 were waited for; matrix products, arithmetic and copies ran while one was open for 6% of the time, Pallas kernels for 21%

profile of v11, /device:TPU:0, one launch (start us, length us, event | category | flops | bytes accessed | tf_op | source)
XLA Modules:
  0.0 100.2 jit_solution(11905529523580077143)
XLA Ops:
  0.6 5.1 %collective-permute-start = (bf16[8,6144]{1,0:T(8,128)(2,1)}, bf16[8,6144]{1,0:T(8,128)(2,1)S(1)}, u32[]{:S(2)}, u32[]{:S(2)}) collective-permute-start(bf16[8,6144]{1,0:T(8,128)(2,1)} %param.8), channel_id=1, source_target_pairs={{1,0},{2,1},{3,2},{0,3},{5,4},{6,5},{7,6},{4,7},{9,8},{10,9},{11,1... | collective-permute-start | bytes 294920 | tf_op jit(solution)/shard_map/ppermute | solution.py:112
  5.8 1.0 %collective-permute-start.7 = (bf16[8,6144]{1,0:T(8,128)(2,1)}, bf16[8,6144]{1,0:T(8,128)(2,1)S(1)}, u32[]{:S(2)}, u32[]{:S(2)}) collective-permute-start(bf16[8,6144]{1,0:T(8,128)(2,1)} %param.8), channel_id=1, source_target_pairs={{3,0},{0,1},{1,2},{2,3},{7,4},{4,5},{5,6},{6,7},{11,8},{8,9},{9,10... | collective-permute-start | bytes 294920 | tf_op jit(solution)/shard_map/ppermute | solution.py:112
  6.8 0.8 slice_bitcast_fusion
  7.5 0.7 convert_element_type.76
  8.2 1.2 %select_reduce_fusion.3 = (f32[8]{0:T(128)S(1)}, f32[8]{0:T(128)S(1)}) fusion(s32[8]{0:T(128)S(1)} %get-tuple-element.105, s32[8]{0:T(128)S(1)} %get-tuple-element.104, bf16[8,6144]{1,0:T(8,128)(2,1)} %param.8, bf16[6144,4]{0,1:T(4,128)(2,1)S(1)} %copy-done), kind=kOutput, calls=%fused_computation.69 | convolution fusion | flops 393392 | bytes 147584 | tf_op jit(solution)/shard_map/dot_general | solution.py:394
  9.5 0.9 fusion.4
  10.4 0.9 constant_dynamic-update-slice_fusion.7
  11.3 2.9 %collective-permute-start.1 = (bf16[8,6272]{1,0:T(8,128)(2,1)S(1)}, bf16[8,6272]{1,0:T(8,128)(2,1)S(1)}, u32[]{:S(2)}, u32[]{:S(2)}) collective-permute-start(bf16[8,6272]{1,0:T(8,128)(2,1)S(1)} %fusion.4), channel_id=1, source_target_pairs={{1,0},{2,1},{3,2},{0,3},{5,4},{6,5},{7,6},{4,7},{9,8},{10,9},{11,1... | collective-permute-start | bytes 301064 | tf_op jit(solution)/shard_map/ppermute | solution.py:112
  14.2 1.1 %collective-permute-start.2 = (bf16[8,6272]{1,0:T(8,128)(2,1)S(1)}, bf16[8,6272]{1,0:T(8,128)(2,1)S(1)}, u32[]{:S(2)}, u32[]{:S(2)}) collective-permute-start(bf16[8,6272]{1,0:T(8,128)(2,1)S(1)} %fusion.4), channel_id=1, source_target_pairs={{2,0},{3,1},{0,2},{1,3},{6,4},{7,5},{4,6},{5,7},{10,8},{11,9},{8,1... | collective-permute-start | bytes 301064 | tf_op jit(solution)/shard_map/ppermute | solution.py:112
  15.4 1.6 %collective-permute-start.8 = (bf16[32,3072]{1,0:T(8,128)(2,1)S(1)}, bf16[32,3072]{1,0:T(8,128)(2,1)S(1)}, u32[]{:S(2)}, u32[]{:S(2)}) collective-permute-start(bf16[32,3072]{1,0:T(8,128)(2,1)S(1)} %get-tuple-element.39._), channel_id=1, source_target_pairs={{16,0},{0,16},{17,1},{1,17},{18,2},{2,18},{19,3},{3,19},{20,4},{4,... | collective-permute-start | bytes 589832 | tf_op jit(solution)/shard_map/ppermute | solution.py:116
  17.0 1.5 %collective-permute-start.9 = (bf16[32,3072]{1,0:T(8,128)(2,1)S(1)}, bf16[32,3072]{1,0:T(8,128)(2,1)S(1)}, u32[]{:S(2)}, u32[]{:S(2)}) collective-permute-start(bf16[32,3072]{1,0:T(8,128)(2,1)S(1)} %get-tuple-element.41), channel_id=1, source_target_pairs={{8,0},{12,4},{0,8},{4,12},{9,1},{13,5},{1,9},{5,13},{10,2},{14,6},... | collective-permute-start | bytes 589832 | tf_op jit(solution)/shard_map/ppermute | solution.py:116
  18.5 4.6 %shard_map.95 = (bf16[3072,1024]{1,0:T(8,128)(2,1)S(1)}, bf16[3072,1024]{1,0:T(8,128)(2,1)S(1)}) custom-call(bf16[32,3072]{1,0:T(8,128)(2,1)S(1)} %get-tuple-element.39._, bf16[1,6144,1024]{2,1,0:T(8,128)(2,1)} %refs_0_.5, bf16[1,6144,1024]{2,1,0:T(8,128)(2,1)} %refs_1_.3), custom_call_target="tpu_custom_call" | custom-call | bytes 12582912 | tf_op jit(solution)/shard_map/pallas_call | solution.py:215
  23.7 1.6 %collective-permute-start.11 = (bf16[64,3072]{1,0:T(8,128)(2,1)S(1)}, bf16[64,3072]{1,0:T(8,128)(2,1)S(1)}, u32[]{:S(2)}, u32[]{:S(2)}) collective-permute-start(bf16[64,3072]{1,0:T(8,128)(2,1)S(1)} %pad_maximum_fusion.10), channel_id=1, source_target_pairs={{16,0},{0,16},{17,1},{1,17},{18,2},{2,18},{19,3},{3,19},{20,4},{4,... | collective-permute-start | bytes 1179656 | tf_op jit(solution)/shard_map/ppermute | solution.py:116
  25.3 1.6 %collective-permute-start.10 = (bf16[64,3072]{1,0:T(8,128)(2,1)S(1)}, bf16[64,3072]{1,0:T(8,128)(2,1)S(1)}, u32[]{:S(2)}, u32[]{:S(2)}) collective-permute-start(bf16[64,3072]{1,0:T(8,128)(2,1)S(1)} %pad_maximum_fusion.9), channel_id=1, source_target_pairs={{8,0},{12,4},{0,8},{4,12},{9,1},{13,5},{1,9},{5,13},{10,2},{14,6},... | collective-permute-start | bytes 1179656 | tf_op jit(solution)/shard_map/ppermute | solution.py:116
  26.9 0.6 collective-permute-start.5
  28.0 2.8 %shard_map.96.down = bf16[512,6144]{1,0:T(8,128)(2,1)S(1)} custom-call(bf16[32,3072]{1,0:T(8,128)(2,1)S(1)} %collective-permute-done.9._, bf16[1,1024,6144]{2,1,0:T(8,128)(2,1)} %down_weight.1), custom_call_target="tpu_custom_call" | custom-call | bytes 6291456 | tf_op jit(solution)/shard_map/pallas_call | solution.py:215
  30.9 4.8 %collective-permute-done.11 = bf16[64,3072]{1,0:T(8,128)(2,1)S(1)} collective-permute-done((bf16[64,3072]{1,0:T(8,128)(2,1)S(1)}, bf16[64,3072]{1,0:T(8,128)(2,1)S(1)}, u32[]{:S(2)}, u32[]{:S(2)}) %collective-permute-start.11) | collective-permute-done | bytes 393248 | tf_op jit(solution)/shard_map/ppermute | solution.py:116
  35.6 1.2 %collective-permute-done.10 = bf16[64,3072]{1,0:T(8,128)(2,1)S(1)} collective-permute-done((bf16[64,3072]{1,0:T(8,128)(2,1)S(1)}, bf16[64,3072]{1,0:T(8,128)(2,1)S(1)}, u32[]{:S(2)}, u32[]{:S(2)}) %collective-permute-start.10) | collective-permute-done | bytes 393248 | tf_op jit(solution)/shard_map/ppermute | solution.py:116
  37.1 0.6 collective-permute-start.14
  37.7 1.3 %collective-permute-done.5 = bf16[32,3072]{1,0:T(8,128)(2,1)S(1)} collective-permute-done((bf16[32,3072]{1,0:T(8,128)(2,1)S(1)}, bf16[32,3072]{1,0:T(8,128)(2,1)S(1)}, u32[]{:S(2)}, u32[]{:S(2)}) %collective-permute-start.5) | collective-permute-done | bytes 196640 | tf_op jit(solution)/shard_map/ppermute | solution.py:116
  39.0 0.6 collective-permute-start.13
  39.6 1.6 %collective-permute-start.12 = (bf16[64,3200]{1,0:T(8,128)(2,1)S(1)}, bf16[64,3200]{1,0:T(8,128)(2,1)S(1)}, u32[]{:S(2)}, u32[]{:S(2)}) collective-permute-start(bf16[64,3200]{1,0:T(8,128)(2,1)S(1)} %pad_maximum_fusion.7), channel_id=1, source_target_pairs={{8,0},{12,4},{0,8},{4,12},{9,1},{13,5},{1,9},{5,13},{10,2},{14,6},... | collective-permute-start | bytes 1228808 | tf_op jit(solution)/shard_map/ppermute | solution.py:116
  41.4 4.6 %shard_map.97 = (f32[256,1024]{1,0:T(8,128)S(1)}, f32[256,1024]{1,0:T(8,128)S(1)}, bf16[3072,1024]{1,0:T(8,128)(2,1)S(1)}, bf16[3072,1024]{1,0:T(8,128)(2,1)S(1)}) custom-call(bf16[256,3072]{1,0:T(8,128)(2,1)S(1)} %pad_maximum_fusion.1.tokens, bf16[3072,1024]{1,0:T(8,128)(2,1)S(1)} %get-tuple-element.37.gate.gate_copy, ...), custom_call_target="tpu_custom_call" | custom-call | flops 3221225472 | bytes 1572864 | tf_op jit(solution)/shard_map/pallas_call | solution.py:257
  46.1 2.3 %shard_map.98 = (f32[256,1024]{1,0:T(8,128)S(1)}, f32[256,1024]{1,0:T(8,128)S(1)}) custom-call(bf16[256,3072]{1,0:T(8,128)(2,1)S(1)} %constant_dynamic-update-slice_fusion.8.tokens, bf16[3072,1024]{1,0:T(8,128)(2,1)S(1)} %get-tuple-element.49.gate.gate_copy, bf16[3072,1024]{1,0:T(8,128)(2,1)S(1)} %get-tuple-element.50.up.up_copy, ...), custom_call_target="tpu_custom_call" | custom-call | flops 1610612736 | bytes 786432 | tf_op jit(solution)/shard_map/pallas_call | solution.py:257
  48.9 0.7 collective-permute-done.12
  49.8 0.6 collective-permute-start.16
  50.4 2.3 %shard_map.99 = (f32[256,1024]{1,0:T(8,128)S(1)}, f32[256,1024]{1,0:T(8,128)S(1)}) custom-call(bf16[256,3072]{1,0:T(8,128)(2,1)S(1)} %constant_dynamic-update-slice_fusion.8.tokens, bf16[3072,1024]{1,0:T(8,128)(2,1)S(1)} %get-tuple-element.49.gate.gate_copy, bf16[3072,1024]{1,0:T(8,128)(2,1)S(1)} %get-tuple-element.50.up.up_copy, ...), custom_call_target="tpu_custom_call" | custom-call | flops 1610612736 | bytes 786432 | tf_op jit(solution)/shard_map/pallas_call | solution.py:257
  53.3 7.5 %shard_map.100 = (bf16[256,1024]{1,0:T(8,128)(2,1)S(1)}, bf16[256,1024]{1,0:T(8,128)(2,1)S(1)}, bf16[256,128]{1,0:T(8,128)(2,1)S(1)}) custom-call(s32[1]{0:T(128)} %bitcast.expert, bf16[256,3200]{1,0:T(8,128)(2,1)S(1)} %pad_maximum_fusion.low, bf16[256,3072]{1,0:T(8,128)(2,1)S(1)} %constant_dynamic-update-slice_fusion.13.high, ...), custom_call_target="tpu_custom_call" | custom-call | flops 3221225472 | bytes 6291456 | tf_op jit(solution)/shard_map/pallas_call | solution.py:323
  60.9 4.1 %shard_map.102 = (f32[128,3072]{1,0:T(8,128)S(1)}, bf16[128,3072]{1,0:T(8,128)(2,1)S(1)}) custom-call(bf16[256,1024]{1,0:T(8,128)(2,1)S(1)} %get-tuple-element.59.grad_gate, bf16[256,1024]{1,0:T(8,128)(2,1)S(1)} %get-tuple-element.60.grad_up, bf16[3072,1024]{1,0:T(8,128)(2,1)S(1)} %get-tuple-element.49.gate.gate_copy, ...), custom_call_target="tpu_custom_call" | custom-call | flops 3221225472 | bytes 3145728 | tf_op jit(solution)/shard_map/pallas_call | solution.py:369
  65.1 4.1 %shard_map.101 = (f32[128,3200]{1,0:T(8,128)S(1)}, bf16[128,3200]{1,0:T(8,128)(2,1)S(1)}) custom-call(bf16[256,1024]{1,0:T(8,128)(2,1)S(1)} %get-tuple-element.59.grad_gate, bf16[256,1024]{1,0:T(8,128)(2,1)S(1)} %get-tuple-element.60.grad_up, bf16[3072,1024]{1,0:T(8,128)(2,1)S(1)} %get-tuple-element.37.gate.gate_copy, ...), custom_call_target="tpu_custom_call" | custom-call | flops 3221225472 | bytes 3145728 | tf_op jit(solution)/shard_map/pallas_call | solution.py:369
  70.0 1.6 %collective-permute-start.25 = (bf16[64,1536]{1,0:T(8,128)(2,1)S(1)}, bf16[64,1536]{1,0:T(8,128)(2,1)S(1)}, u32[]{:S(2)}, u32[]{:S(2)}) collective-permute-start(bf16[64,1536]{1,0:T(8,128)(2,1)S(1)} %pad_maximum_fusion.13), channel_id=1, source_target_pairs={{16,0},{0,16},{17,1},{1,17},{18,2},{2,18},{19,3},{3,19},{20,4},{4,... | collective-permute-start | bytes 589832 | tf_op jit(solution)/shard_map/ppermute | solution.py:116
  71.5 1.5 %collective-permute-start.24 = (bf16[64,1536]{1,0:T(8,128)(2,1)S(1)}, bf16[64,1536]{1,0:T(8,128)(2,1)S(1)}, u32[]{:S(2)}, u32[]{:S(2)}) collective-permute-start(bf16[64,1536]{1,0:T(8,128)(2,1)S(1)} %concatenate.112), channel_id=1, source_target_pairs={{8,0},{12,4},{0,8},{4,12},{9,1},{13,5},{1,9},{5,13},{10,2},{14,6},... | collective-permute-start | bytes 589832 | tf_op jit(solution)/shard_map/ppermute | solution.py:116
  73.5 0.6 collective-permute-start.20
  74.1 1.0 %collective-permute-start.19 = (bf16[64,1536]{1,0:T(8,128)(2,1)S(1)}, bf16[64,1536]{1,0:T(8,128)(2,1)S(1)}, u32[]{:S(2)}, u32[]{:S(2)}) collective-permute-start(bf16[64,1536]{1,0:T(8,128)(2,1)S(1)} %concatenate.110), channel_id=1, source_target_pairs={{8,0},{12,4},{0,8},{4,12},{9,1},{13,5},{1,9},{5,13},{10,2},{14,6},... | collective-permute-start | bytes 589832 | tf_op jit(solution)/shard_map/ppermute | solution.py:116
  75.1 2.7 %collective-permute-done.25 = bf16[64,1536]{1,0:T(8,128)(2,1)S(1)} collective-permute-done((bf16[64,1536]{1,0:T(8,128)(2,1)S(1)}, bf16[64,1536]{1,0:T(8,128)(2,1)S(1)}, u32[]{:S(2)}, u32[]{:S(2)}) %collective-permute-start.25) | collective-permute-done | bytes 196640 | tf_op jit(solution)/shard_map/ppermute | solution.py:116
  77.8 1.6 %collective-permute-start.30 = (bf16[32,1536]{1,0:T(8,128)(2,1)S(1)}, bf16[32,1536]{1,0:T(8,128)(2,1)S(1)}, u32[]{:S(2)}, u32[]{:S(2)}) collective-permute-start(bf16[32,1536]{1,0:T(8,128)(2,1)S(1)} %split.121), channel_id=1, source_target_pairs={{8,0},{12,4},{0,8},{4,12},{9,1},{13,5},{1,9},{5,13},{10,2},{14,6},... | collective-permute-start | bytes 294920 | tf_op jit(solution)/shard_map/ppermute | solution.py:116
  79.5 1.6 %collective-permute-start.29 = (bf16[32,1536]{1,0:T(8,128)(2,1)S(1)}, bf16[32,1536]{1,0:T(8,128)(2,1)S(1)}, u32[]{:S(2)}, u32[]{:S(2)}) collective-permute-start(bf16[32,1536]{1,0:T(8,128)(2,1)S(1)} %split.122), channel_id=1, source_target_pairs={{16,0},{0,16},{17,1},{1,17},{18,2},{2,18},{19,3},{3,19},{20,4},{4,... | collective-permute-start | bytes 294920 | tf_op jit(solution)/shard_map/ppermute | solution.py:116
  81.1 2.4 %collective-permute-done.19 = bf16[64,1536]{1,0:T(8,128)(2,1)S(1)} collective-permute-done((bf16[64,1536]{1,0:T(8,128)(2,1)S(1)}, bf16[64,1536]{1,0:T(8,128)(2,1)S(1)}, u32[]{:S(2)}, u32[]{:S(2)}) %collective-permute-start.19) | collective-permute-done | bytes 196640 | tf_op jit(solution)/shard_map/ppermute | solution.py:116
  83.6 0.6 collective-permute-start.22
  84.2 1.6 %collective-permute-start.23 = (bf16[32,1664]{1,0:T(8,128)(2,1)S(1)}, bf16[32,1664]{1,0:T(8,128)(2,1)S(1)}, u32[]{:S(2)}, u32[]{:S(2)}) collective-permute-start(bf16[32,1664]{1,0:T(8,128)(2,1)S(1)} %split.120), channel_id=1, source_target_pairs={{8,0},{12,4},{0,8},{4,12},{9,1},{13,5},{1,9},{5,13},{10,2},{14,6},... | collective-permute-start | bytes 319496 | tf_op jit(solution)/shard_map/ppermute | solution.py:116
  85.9 0.9 collective-permute-start.31
  86.9 2.0 %collective-permute-start.32 = (bf16[8,3072]{1,0:T(8,128)(2,1)S(1)}, bf16[8,3072]{1,0:T(8,128)(2,1)S(1)}, u32[]{:S(2)}, u32[]{:S(2)}) collective-permute-start(bf16[8,3072]{1,0:T(8,128)(2,1)S(1)} %get-tuple-element.99), channel_id=1, source_target_pairs={{2,0},{3,1},{0,2},{1,3},{6,4},{7,5},{4,6},{5,7},{10,8},{11,9},{8,1... | collective-permute-start | bytes 147464 | tf_op jit(solution)/shard_map/ppermute | solution.py:112
  88.9 2.8 %collective-permute-start.33 = (bf16[8,3072]{1,0:T(8,128)(2,1)S(1)}, bf16[8,3072]{1,0:T(8,128)(2,1)S(1)}, u32[]{:S(2)}, u32[]{:S(2)}) collective-permute-start(bf16[8,3072]{1,0:T(8,128)(2,1)S(1)} %get-tuple-element.98), channel_id=1, source_target_pairs={{1,0},{2,1},{3,2},{0,3},{5,4},{6,5},{7,6},{4,7},{9,8},{10,9},{11,1... | collective-permute-start | bytes 147464 | tf_op jit(solution)/shard_map/ppermute | solution.py:112
  92.5 3.3 %collective-permute-start.28 = (bf16[8,3200]{1,0:T(8,128)(2,1)S(1)}, bf16[8,3200]{1,0:T(8,128)(2,1)S(1)}, u32[]{:S(2)}, u32[]{:S(2)}) collective-permute-start(bf16[8,3200]{1,0:T(8,128)(2,1)S(1)} %get-tuple-element.95), channel_id=1, source_target_pairs={{1,0},{2,1},{3,2},{0,3},{5,4},{6,5},{7,6},{4,7},{9,8},{10,9},{11,1... | collective-permute-start | bytes 153608 | tf_op jit(solution)/shard_map/ppermute | solution.py:112
  95.8 2.0 %collective-permute-done.26 = bf16[8,3200]{1,0:T(8,128)(2,1)S(1)} collective-permute-done((bf16[8,3200]{1,0:T(8,128)(2,1)S(1)}, bf16[8,3200]{1,0:T(8,128)(2,1)S(1)}, u32[]{:S(2)}, u32[]{:S(2)}) %collective-permute-start.26) | collective-permute-done | bytes 51232 | tf_op jit(solution)/shard_map/ppermute | solution.py:112
  97.8 0.6 collective-permute-done.28
  98.7 0.6 pad_maximum_fusion.14
  99.3 0.9 fusion.3
  (103 shorter events, 5.8 us)
Async XLA Ops:
  0.6 7.5 %copy-start = (bf16[6144,4]{0,1:T(4,128)(2,1)S(1)}, bf16[6144,4]{0,1:T(4,128)(2,1)}, u32[]{:S(2)}) copy-start(bf16[6144,4]{0,1:T(4,128)(2,1)} %param.12) | copy-start | bytes 147460
  0.6 10.7 %collective-permute-start = (bf16[8,6144]{1,0:T(8,128)(2,1)}, bf16[8,6144]{1,0:T(8,128)(2,1)S(1)}, u32[]{:S(2)}, u32[]{:S(2)}) collective-permute-start(bf16[8,6144]{1,0:T(8,128)(2,1)} %param.8), channel_id=1, source_target_pairs={{1,0},{2,1},{3,2},{0,3},{5,4},{6,5},{7,6},{4,7},{9,8},{10,9},{11,1... | collective-permute-start | bytes 294920 | tf_op jit(solution)/shard_map/ppermute | solution.py:112
  5.7 9.6 %collective-permute-start.6 = (bf16[8,6144]{1,0:T(8,128)(2,1)}, bf16[8,6144]{1,0:T(8,128)(2,1)S(1)}, u32[]{:S(2)}, u32[]{:S(2)}) collective-permute-start(bf16[8,6144]{1,0:T(8,128)(2,1)} %param.8), channel_id=1, source_target_pairs={{2,0},{3,1},{0,2},{1,3},{6,4},{7,5},{4,6},{5,7},{10,8},{11,9},{8,1... | collective-permute-start | bytes 294920 | tf_op jit(solution)/shard_map/ppermute | solution.py:112
  5.8 9.6 %collective-permute-start.7 = (bf16[8,6144]{1,0:T(8,128)(2,1)}, bf16[8,6144]{1,0:T(8,128)(2,1)S(1)}, u32[]{:S(2)}, u32[]{:S(2)}) collective-permute-start(bf16[8,6144]{1,0:T(8,128)(2,1)} %param.8), channel_id=1, source_target_pairs={{3,0},{0,1},{1,2},{2,3},{7,4},{4,5},{5,6},{6,7},{11,8},{8,9},{9,10... | collective-permute-start | bytes 294920 | tf_op jit(solution)/shard_map/ppermute | solution.py:112
  11.3 11.8 %collective-permute-start.1 = (bf16[8,6272]{1,0:T(8,128)(2,1)S(1)}, bf16[8,6272]{1,0:T(8,128)(2,1)S(1)}, u32[]{:S(2)}, u32[]{:S(2)}) collective-permute-start(bf16[8,6272]{1,0:T(8,128)(2,1)S(1)} %fusion.4), channel_id=1, source_target_pairs={{1,0},{2,1},{3,2},{0,3},{5,4},{6,5},{7,6},{4,7},{9,8},{10,9},{11,1... | collective-permute-start | bytes 301064 | tf_op jit(solution)/shard_map/ppermute | solution.py:112
  14.2 9.4 %collective-permute-start.2 = (bf16[8,6272]{1,0:T(8,128)(2,1)S(1)}, bf16[8,6272]{1,0:T(8,128)(2,1)S(1)}, u32[]{:S(2)}, u32[]{:S(2)}) collective-permute-start(bf16[8,6272]{1,0:T(8,128)(2,1)S(1)} %fusion.4), channel_id=1, source_target_pairs={{2,0},{3,1},{0,2},{1,3},{6,4},{7,5},{4,6},{5,7},{10,8},{11,9},{8,1... | collective-permute-start | bytes 301064 | tf_op jit(solution)/shard_map/ppermute | solution.py:112
  15.3 8.3 %collective-permute-start.3 = (bf16[8,6272]{1,0:T(8,128)(2,1)S(1)}, bf16[8,6272]{1,0:T(8,128)(2,1)S(1)}, u32[]{:S(2)}, u32[]{:S(2)}) collective-permute-start(bf16[8,6272]{1,0:T(8,128)(2,1)S(1)} %fusion.4), channel_id=1, source_target_pairs={{3,0},{0,1},{1,2},{2,3},{7,4},{4,5},{5,6},{6,7},{11,8},{8,9},{9,10... | collective-permute-start | bytes 301064 | tf_op jit(solution)/shard_map/ppermute | solution.py:112
  15.4 8.2 %collective-permute-start.8 = (bf16[32,3072]{1,0:T(8,128)(2,1)S(1)}, bf16[32,3072]{1,0:T(8,128)(2,1)S(1)}, u32[]{:S(2)}, u32[]{:S(2)}) collective-permute-start(bf16[32,3072]{1,0:T(8,128)(2,1)S(1)} %get-tuple-element.39._), channel_id=1, source_target_pairs={{16,0},{0,16},{17,1},{1,17},{18,2},{2,18},{19,3},{3,19},{20,4},{4,... | collective-permute-start | bytes 589832 | tf_op jit(solution)/shard_map/ppermute | solution.py:116
  17.0 6.7 %collective-permute-start.9 = (bf16[32,3072]{1,0:T(8,128)(2,1)S(1)}, bf16[32,3072]{1,0:T(8,128)(2,1)S(1)}, u32[]{:S(2)}, u32[]{:S(2)}) collective-permute-start(bf16[32,3072]{1,0:T(8,128)(2,1)S(1)} %get-tuple-element.41), channel_id=1, source_target_pairs={{8,0},{12,4},{0,8},{4,12},{9,1},{13,5},{1,9},{5,13},{10,2},{14,6},... | collective-permute-start | bytes 589832 | tf_op jit(solution)/shard_map/ppermute | solution.py:116
  23.7 11.9 %collective-permute-start.11 = (bf16[64,3072]{1,0:T(8,128)(2,1)S(1)}, bf16[64,3072]{1,0:T(8,128)(2,1)S(1)}, u32[]{:S(2)}, u32[]{:S(2)}) collective-permute-start(bf16[64,3072]{1,0:T(8,128)(2,1)S(1)} %pad_maximum_fusion.10), channel_id=1, source_target_pairs={{16,0},{0,16},{17,1},{1,17},{18,2},{2,18},{19,3},{3,19},{20,4},{4,... | collective-permute-start | bytes 1179656 | tf_op jit(solution)/shard_map/ppermute | solution.py:116
  25.3 11.6 %collective-permute-start.10 = (bf16[64,3072]{1,0:T(8,128)(2,1)S(1)}, bf16[64,3072]{1,0:T(8,128)(2,1)S(1)}, u32[]{:S(2)}, u32[]{:S(2)}) collective-permute-start(bf16[64,3072]{1,0:T(8,128)(2,1)S(1)} %pad_maximum_fusion.9), channel_id=1, source_target_pairs={{8,0},{12,4},{0,8},{4,12},{9,1},{13,5},{1,9},{5,13},{10,2},{14,6},... | collective-permute-start | bytes 1179656 | tf_op jit(solution)/shard_map/ppermute | solution.py:116
  26.9 12.0 %collective-permute-start.5 = (bf16[32,3072]{1,0:T(8,128)(2,1)S(1)}, bf16[32,3072]{1,0:T(8,128)(2,1)S(1)}, u32[]{:S(2)}, u32[]{:S(2)}) collective-permute-start(bf16[32,3072]{1,0:T(8,128)(2,1)S(1)} %get-tuple-element.45), channel_id=1, source_target_pairs={{8,0},{12,4},{0,8},{4,12},{9,1},{13,5},{1,9},{5,13},{10,2},{14,6},... | collective-permute-start | bytes 589832 | tf_op jit(solution)/shard_map/ppermute | solution.py:116
  27.5 11.5 %collective-permute-start.4 = (bf16[32,3200]{1,0:T(8,128)(2,1)S(1)}, bf16[32,3200]{1,0:T(8,128)(2,1)S(1)}, u32[]{:S(2)}, u32[]{:S(2)}) collective-permute-start(bf16[32,3200]{1,0:T(8,128)(2,1)S(1)} %slice.96), channel_id=1, source_target_pairs={{16,0},{0,16},{17,1},{1,17},{18,2},{2,18},{19,3},{3,19},{20,4},{4,... | collective-permute-start | bytes 614408 | tf_op jit(solution)/shard_map/ppermute | solution.py:116
  36.9 4.3 %collective-permute-start.15 = (bf16[128,3072]{1,0:T(8,128)(2,1)S(1)}, bf16[128,3072]{1,0:T(8,128)(2,1)S(1)}, u32[]{:S(2)}, u32[]{:S(2)}) collective-permute-start(bf16[128,3072]{1,0:T(8,128)(2,1)S(1)} %pad_maximum_fusion.4), channel_id=1, source_target_pairs={{4,0},{0,4},{12,8},{8,12},{5,1},{1,5},{13,9},{9,13},{6,2},{2,6},{1... | collective-permute-start | bytes 2359304 | tf_op jit(solution)/shard_map/ppermute | solution.py:116
  37.1 4.3 %collective-permute-start.14 = (bf16[128,3072]{1,0:T(8,128)(2,1)S(1)}, bf16[128,3072]{1,0:T(8,128)(2,1)S(1)}, u32[]{:S(2)}, u32[]{:S(2)}) collective-permute-start(bf16[128,3072]{1,0:T(8,128)(2,1)S(1)} %pad_maximum_fusion.3), channel_id=1, source_target_pairs={{4,0},{0,4},{12,8},{8,12},{5,1},{1,5},{13,9},{9,13},{6,2},{2,6},{1... | collective-permute-start | bytes 2359304 | tf_op jit(solution)/shard_map/ppermute | solution.py:116
  39.0 9.8 %collective-permute-start.13 = (bf16[64,3072]{1,0:T(8,128)(2,1)S(1)}, bf16[64,3072]{1,0:T(8,128)(2,1)S(1)}, u32[]{:S(2)}, u32[]{:S(2)}) collective-permute-start(bf16[64,3072]{1,0:T(8,128)(2,1)S(1)} %pad_maximum_fusion.11), channel_id=1, source_target_pairs={{16,0},{0,16},{17,1},{1,17},{18,2},{2,18},{19,3},{3,19},{20,4},{4,... | collective-permute-start | bytes 1179656 | tf_op jit(solution)/shard_map/ppermute | solution.py:116
  39.6 9.9 %collective-permute-start.12 = (bf16[64,3200]{1,0:T(8,128)(2,1)S(1)}, bf16[64,3200]{1,0:T(8,128)(2,1)S(1)}, u32[]{:S(2)}, u32[]{:S(2)}) collective-permute-start(bf16[64,3200]{1,0:T(8,128)(2,1)S(1)} %pad_maximum_fusion.7), channel_id=1, source_target_pairs={{8,0},{12,4},{0,8},{4,12},{9,1},{13,5},{1,9},{5,13},{10,2},{14,6},... | collective-permute-start | bytes 1228808 | tf_op jit(solution)/shard_map/ppermute | solution.py:116
  49.7 3.1 %collective-permute-start.17 = (bf16[128,3072]{1,0:T(8,128)(2,1)S(1)}, bf16[128,3072]{1,0:T(8,128)(2,1)S(1)}, u32[]{:S(2)}, u32[]{:S(2)}) collective-permute-start(bf16[128,3072]{1,0:T(8,128)(2,1)S(1)} %pad_maximum_fusion.5), channel_id=1, source_target_pairs={{4,0},{0,4},{12,8},{8,12},{5,1},{1,5},{13,9},{9,13},{6,2},{2,6},{1... | collective-permute-start | bytes 2359304 | tf_op jit(solution)/shard_map/ppermute | solution.py:116
  49.8 3.4 %collective-permute-start.16 = (bf16[128,3200]{1,0:T(8,128)(2,1)S(1)}, bf16[128,3200]{1,0:T(8,128)(2,1)S(1)}, u32[]{:S(2)}, u32[]{:S(2)}) collective-permute-start(bf16[128,3200]{1,0:T(8,128)(2,1)S(1)} %pad_maximum_fusion.2), channel_id=1, source_target_pairs={{4,0},{0,4},{12,8},{8,12},{5,1},{1,5},{13,9},{9,13},{6,2},{2,6},{1... | collective-permute-start | bytes 2457608 | tf_op jit(solution)/shard_map/ppermute | solution.py:116
  64.9 4.7 %collective-permute-start.21 = (bf16[128,3072]{1,0:T(8,128)(2,1)S(1)}, bf16[128,3072]{1,0:T(8,128)(2,1)S(1)}, u32[]{:S(2)}, u32[]{:S(2)}) collective-permute-start(bf16[128,3072]{1,0:T(8,128)(2,1)S(1)} %get-tuple-element.64), channel_id=1, source_target_pairs={{4,0},{0,4},{12,8},{8,12},{5,1},{1,5},{13,9},{9,13},{6,2},{2,6},{1... | collective-permute-start | bytes 2359304 | tf_op jit(solution)/shard_map/ppermute | solution.py:116
  69.2 3.9 %collective-permute-start.18 = (bf16[128,3200]{1,0:T(8,128)(2,1)S(1)}, bf16[128,3200]{1,0:T(8,128)(2,1)S(1)}, u32[]{:S(2)}, u32[]{:S(2)}) collective-permute-start(bf16[128,3200]{1,0:T(8,128)(2,1)S(1)} %get-tuple-element.63), channel_id=1, source_target_pairs={{4,0},{0,4},{12,8},{8,12},{5,1},{1,5},{13,9},{9,13},{6,2},{2,6},{1... | collective-permute-start | bytes 2457608 | tf_op jit(solution)/shard_map/ppermute | solution.py:116
  70.0 7.8 %collective-permute-start.25 = (bf16[64,1536]{1,0:T(8,128)(2,1)S(1)}, bf16[64,1536]{1,0:T(8,128)(2,1)S(1)}, u32[]{:S(2)}, u32[]{:S(2)}) collective-permute-start(bf16[64,1536]{1,0:T(8,128)(2,1)S(1)} %pad_maximum_fusion.13), channel_id=1, source_target_pairs={{16,0},{0,16},{17,1},{1,17},{18,2},{2,18},{19,3},{3,19},{20,4},{4,... | collective-permute-start | bytes 589832 | tf_op jit(solution)/shard_map/ppermute | solution.py:116
  71.5 7.9 %collective-permute-start.24 = (bf16[64,1536]{1,0:T(8,128)(2,1)S(1)}, bf16[64,1536]{1,0:T(8,128)(2,1)S(1)}, u32[]{:S(2)}, u32[]{:S(2)}) collective-permute-start(bf16[64,1536]{1,0:T(8,128)(2,1)S(1)} %concatenate.112), channel_id=1, source_target_pairs={{8,0},{12,4},{0,8},{4,12},{9,1},{13,5},{1,9},{5,13},{10,2},{14,6},... | collective-permute-start | bytes 589832 | tf_op jit(solution)/shard_map/ppermute | solution.py:116
  73.5 10.0 %collective-permute-start.20 = (bf16[64,1664]{1,0:T(8,128)(2,1)S(1)}, bf16[64,1664]{1,0:T(8,128)(2,1)S(1)}, u32[]{:S(2)}, u32[]{:S(2)}) collective-permute-start(bf16[64,1664]{1,0:T(8,128)(2,1)S(1)} %pad_maximum_fusion.12), channel_id=1, source_target_pairs={{16,0},{0,16},{17,1},{1,17},{18,2},{2,18},{19,3},{3,19},{20,4},{4,... | collective-permute-start | bytes 638984 | tf_op jit(solution)/shard_map/ppermute | solution.py:116
  74.1 9.4 %collective-permute-start.19 = (bf16[64,1536]{1,0:T(8,128)(2,1)S(1)}, bf16[64,1536]{1,0:T(8,128)(2,1)S(1)}, u32[]{:S(2)}, u32[]{:S(2)}) collective-permute-start(bf16[64,1536]{1,0:T(8,128)(2,1)S(1)} %concatenate.110), channel_id=1, source_target_pairs={{8,0},{12,4},{0,8},{4,12},{9,1},{13,5},{1,9},{5,13},{10,2},{14,6},... | collective-permute-start | bytes 589832 | tf_op jit(solution)/shard_map/ppermute | solution.py:116
  77.8 7.9 %collective-permute-start.30 = (bf16[32,1536]{1,0:T(8,128)(2,1)S(1)}, bf16[32,1536]{1,0:T(8,128)(2,1)S(1)}, u32[]{:S(2)}, u32[]{:S(2)}) collective-permute-start(bf16[32,1536]{1,0:T(8,128)(2,1)S(1)} %split.121), channel_id=1, source_target_pairs={{8,0},{12,4},{0,8},{4,12},{9,1},{13,5},{1,9},{5,13},{10,2},{14,6},... | collective-permute-start | bytes 294920 | tf_op jit(solution)/shard_map/ppermute | solution.py:116
  79.5 6.3 %collective-permute-start.29 = (bf16[32,1536]{1,0:T(8,128)(2,1)S(1)}, bf16[32,1536]{1,0:T(8,128)(2,1)S(1)}, u32[]{:S(2)}, u32[]{:S(2)}) collective-permute-start(bf16[32,1536]{1,0:T(8,128)(2,1)S(1)} %split.122), channel_id=1, source_target_pairs={{16,0},{0,16},{17,1},{1,17},{18,2},{2,18},{19,3},{3,19},{20,4},{4,... | collective-permute-start | bytes 294920 | tf_op jit(solution)/shard_map/ppermute | solution.py:116
  83.6 8.1 %collective-permute-start.22 = (bf16[32,1536]{1,0:T(8,128)(2,1)S(1)}, bf16[32,1536]{1,0:T(8,128)(2,1)S(1)}, u32[]{:S(2)}, u32[]{:S(2)}) collective-permute-start(bf16[32,1536]{1,0:T(8,128)(2,1)S(1)} %split.123), channel_id=1, source_target_pairs={{16,0},{0,16},{17,1},{1,17},{18,2},{2,18},{19,3},{3,19},{20,4},{4,... | collective-permute-start | bytes 294920 | tf_op jit(solution)/shard_map/ppermute | solution.py:116
  84.2 7.5 %collective-permute-start.23 = (bf16[32,1664]{1,0:T(8,128)(2,1)S(1)}, bf16[32,1664]{1,0:T(8,128)(2,1)S(1)}, u32[]{:S(2)}, u32[]{:S(2)}) collective-permute-start(bf16[32,1664]{1,0:T(8,128)(2,1)S(1)} %split.120), channel_id=1, source_target_pairs={{8,0},{12,4},{0,8},{4,12},{9,1},{13,5},{1,9},{5,13},{10,2},{14,6},... | collective-permute-start | bytes 319496 | tf_op jit(solution)/shard_map/ppermute | solution.py:116
  85.9 6.6 %collective-permute-start.31 = (bf16[8,3072]{1,0:T(8,128)(2,1)S(1)}, bf16[8,3072]{1,0:T(8,128)(2,1)S(1)}, u32[]{:S(2)}, u32[]{:S(2)}) collective-permute-start(bf16[8,3072]{1,0:T(8,128)(2,1)S(1)} %get-tuple-element.97), channel_id=1, source_target_pairs={{3,0},{0,1},{1,2},{2,3},{7,4},{4,5},{5,6},{6,7},{11,8},{8,9},{9,10... | collective-permute-start | bytes 147464 | tf_op jit(solution)/shard_map/ppermute | solution.py:112
  86.9 8.9 %collective-permute-start.32 = (bf16[8,3072]{1,0:T(8,128)(2,1)S(1)}, bf16[8,3072]{1,0:T(8,128)(2,1)S(1)}, u32[]{:S(2)}, u32[]{:S(2)}) collective-permute-start(bf16[8,3072]{1,0:T(8,128)(2,1)S(1)} %get-tuple-element.99), channel_id=1, source_target_pairs={{2,0},{3,1},{0,2},{1,3},{6,4},{7,5},{4,6},{5,7},{10,8},{11,9},{8,1... | collective-permute-start | bytes 147464 | tf_op jit(solution)/shard_map/ppermute | solution.py:112
  88.9 6.9 %collective-permute-start.33 = (bf16[8,3072]{1,0:T(8,128)(2,1)S(1)}, bf16[8,3072]{1,0:T(8,128)(2,1)S(1)}, u32[]{:S(2)}, u32[]{:S(2)}) collective-permute-start(bf16[8,3072]{1,0:T(8,128)(2,1)S(1)} %get-tuple-element.98), channel_id=1, source_target_pairs={{1,0},{2,1},{3,2},{0,3},{5,4},{6,5},{7,6},{4,7},{9,8},{10,9},{11,1... | collective-permute-start | bytes 147464 | tf_op jit(solution)/shard_map/ppermute | solution.py:112
  91.8 6.9 %copy-start.1 = (s32[8]{0:T(128)S(1)}, s32[8]{0:T(128)}, u32[]{:S(2)}) copy-start(s32[8]{0:T(128)} %param.10) | copy-start | bytes 100
  91.9 6.0 %collective-permute-start.26 = (bf16[8,3200]{1,0:T(8,128)(2,1)S(1)}, bf16[8,3200]{1,0:T(8,128)(2,1)S(1)}, u32[]{:S(2)}, u32[]{:S(2)}) collective-permute-start(bf16[8,3200]{1,0:T(8,128)(2,1)S(1)} %get-tuple-element.94), channel_id=1, source_target_pairs={{3,0},{0,1},{1,2},{2,3},{7,4},{4,5},{5,6},{6,7},{11,8},{8,9},{9,10... | collective-permute-start | bytes 153608 | tf_op jit(solution)/shard_map/ppermute | solution.py:112
  91.9 5.9 %collective-permute-start.27 = (bf16[8,3200]{1,0:T(8,128)(2,1)S(1)}, bf16[8,3200]{1,0:T(8,128)(2,1)S(1)}, u32[]{:S(2)}, u32[]{:S(2)}) collective-permute-start(bf16[8,3200]{1,0:T(8,128)(2,1)S(1)} %get-tuple-element.96), channel_id=1, source_target_pairs={{2,0},{3,1},{0,2},{1,3},{6,4},{7,5},{4,6},{5,7},{10,8},{11,9},{8,1... | collective-permute-start | bytes 153608 | tf_op jit(solution)/shard_map/ppermute | solution.py:112
  92.5 5.9 %collective-permute-start.28 = (bf16[8,3200]{1,0:T(8,128)(2,1)S(1)}, bf16[8,3200]{1,0:T(8,128)(2,1)S(1)}, u32[]{:S(2)}, u32[]{:S(2)}) collective-permute-start(bf16[8,3200]{1,0:T(8,128)(2,1)S(1)} %get-tuple-element.95), channel_id=1, source_target_pairs={{1,0},{2,1},{3,2},{0,3},{5,4},{6,5},{7,6},{4,7},{9,8},{10,9},{11,1... | collective-permute-start | bytes 153608 | tf_op jit(solution)/shard_map/ppermute | solution.py:112

commit v12 on v11

--- a/solution.py
+++ b/solution.py
@@ -9,8 +9,8 @@
 from jax.sharding import PartitionSpec as P
 
 TOKEN_PART = 512
-HIDDEN_PART = 512
-COLUMN_PART = 1024
+HIDDEN_PART = 256
+COLUMN_PART = 1536
 TOKEN_VMEM = 6 * 2 ** 20
 GRAD_VMEM = 10 * 2 ** 20
 OUTPUT_VMEM = 6 * 2 ** 20
@@ -107,11 +107,6 @@
     gate_grad = jnp.stack([grad_first, grad_second], axis=1)
     return (d_tokens, gate_grad)
 
-def shift(value, axis, step):
-    size = lax.axis_size(axis)
-    return lax.ppermute(value, axis, [((i + step) % size, i) for i in range(size)])
-
-
 def swap(value, axis, bit):
     return lax.ppermute(value, axis, [(i ^ bit, i) for i in range(lax.axis_size(axis))])
 
@@ -133,7 +128,7 @@
 
 
 def gather_z(rows):
-    return [rows] + [shift(rows, "mp", k) for k in range(1, lax.axis_size("mp"))]
+    return [rows] + [swap(rows, "mp", k) for k in range(1, lax.axis_size("mp"))]
 
 
 def gather_near(z_rows, cut):
@@ -180,7 +175,7 @@
     rows = total.shape[0] // size
     result = total[:rows]
     for k in range(1, size):
-        result = result + send(total[k * rows:(k + 1) * rows], lambda value: shift(value, "mp", size - k))
+        result = result + send(total[k * rows:(k + 1) * rows], lambda value: swap(value, "mp", k))
     return result
 
 
@@ -294,7 +289,7 @@
     def block(weights, first, step):
         rows = pl.ds(pl.multiple_of(step * depth, depth), depth)
         span = pl.ds(pl.multiple_of(first + step * depth, depth), depth)
-        grad_hidden = (product(weights[rows, :half], low[:, table:], 1) + product(weights[rows, half:], high[...], 1)).T
+        grad_hidden = product(low[:, table:], weights[rows, :half], 1) + product(high[...], weights[rows, half:], 1)
         gates = pre_gate[:, span]
         ups = pre_up[:, span]
         sigma = jax.nn.sigmoid(gates)
@@ -441,7 +436,7 @@
 
 
 def solution(mesh):
-    gathers = mesh.shape["seq"] == 2 and mesh.shape["expert"] == 4
+    gathers = mesh.shape["seq"] == 2 and mesh.shape["expert"] == 4 and mesh.shape["mp"] in (2, 4)
     return jax.shard_map(
         gathered_plan if gathers else routed_plan,
         mesh=mesh,

time: 100 us -> 97.9 us (0.979)
  Pallas kernels: 32.3 us -> 29 us
    ppermute x12 -> x0, starting transfers between devices: 19.8 us -> none  [shift(): lax.ppermute(value, axis, [((i + step) % size, i) for i in range(size)])]
    ppermute x22 -> x34, starting transfers between devices: 21.4 us -> 40.9 us  [swap(): lax.ppermute(value, axis, [(i ^ bit, i) for i in range(lax.axis_size(axis...]
    ppermute x22 -> x34, waiting for transfers between devices: 14 us -> 18 us  [swap(): lax.ppermute(value, axis, [(i ^ bit, i) for i in range(lax.axis_size(axis...]
    ppermute x12 -> x0, waiting for transfers between devices: 3.1 us -> none  [shift(): lax.ppermute(value, axis, [((i + step) % size, i) for i in range(size)])]
    pallas_call x1, Pallas kernels: 7.53 us -> 4.73 us  [multiply_grads(): pl.pallas_call(grad_kernel, out_shape=(pltpu.VMEM((rows, hidden), jnp.bfl...]
  transfers between devices with their start and end apart: 34 -> 34, of which waited for: 11 -> 12; matrix products, arithmetic and copies ran while one was open for 6% -> 6% of each run, Pallas kernels for 21% -> 21%
where the time goes in v12:
time: 97.9 us; the launch traced here: 97.6 us
  starting transfers between devices  40.9 us (42%)
  Pallas kernels  29 us (30%)
  waiting for transfers between devices  18 us (18%)
  other arithmetic  3.92 us (4%)
  local copies, waits for them, and re-layouts  2.3 us (2%)
  matrix products  2.15 us (2%)
  between operations  1.25 us (1%)
    ppermute x34, starting transfers between devices, swap(): lax.ppermute(value, axis, [(i ^ bit, i) for i in range(lax.axis_size(axis...  40.9 us
    ppermute x34, waiting for transfers between devices, swap(): lax.ppermute(value, axis, [(i ^ bit, i) for i in range(lax.axis_size(axis...  18 us
    pallas_call x3, Pallas kernels, multiply_tokens(): pl.pallas_call(functools.partial(token_kernel, first, offset, length), ou...  9.24 us
    pallas_call x2, Pallas kernels, multiply_outputs(): pl.pallas_call(output_kernel, out_shape=(pltpu.VMEM((rows // 2, total), j...  7.65 us
    pallas_call x2, Pallas kernels, fetch(): pl.pallas_call(functools.partial(fetch_kernel, first), out_shape=tuple((p...  7.41 us
    pallas_call x1, Pallas kernels, multiply_grads(): pl.pallas_call(grad_kernel, out_shape=(pltpu.VMEM((rows, hidden), jnp.bfl...  4.73 us
  transfers between devices with their start and end apart: 34, of which 12 were waited for; matrix products, arithmetic and copies ran while one was open for 6% of the time, Pallas kernels for 21%

profile of v12, /device:TPU:0, one launch (start us, length us, event | category | flops | bytes accessed | tf_op | source)
XLA Modules:
  0.0 97.6 jit_solution(998871057903838591)
XLA Ops:
  0.6 3.1 %collective-permute-start = (bf16[8,6144]{1,0:T(8,128)(2,1)}, bf16[8,6144]{1,0:T(8,128)(2,1)S(1)}, u32[]{:S(2)}, u32[]{:S(2)}) collective-permute-start(bf16[8,6144]{1,0:T(8,128)(2,1)} %param.8), channel_id=1, source_target_pairs={{1,0},{0,1},{3,2},{2,3},{5,4},{4,5},{7,6},{6,7},{9,8},{8,9},{11,10... | collective-permute-start | bytes 294920 | tf_op jit(solution)/shard_map/ppermute | solution.py:111
  3.7 2.6 %collective-permute-start.6 = (bf16[8,6144]{1,0:T(8,128)(2,1)}, bf16[8,6144]{1,0:T(8,128)(2,1)S(1)}, u32[]{:S(2)}, u32[]{:S(2)}) collective-permute-start(bf16[8,6144]{1,0:T(8,128)(2,1)} %param.8), channel_id=1, source_target_pairs={{2,0},{3,1},{0,2},{1,3},{6,4},{7,5},{4,6},{5,7},{10,8},{11,9},{8,1... | collective-permute-start | bytes 294920 | tf_op jit(solution)/shard_map/ppermute | solution.py:111
  6.3 0.8 slice_bitcast_fusion
  7.1 0.7 convert_element_type.76
  7.7 1.2 %select_reduce_fusion.3 = (f32[8]{0:T(128)S(1)}, f32[8]{0:T(128)S(1)}) fusion(s32[8]{0:T(128)S(1)} %get-tuple-element.105, s32[8]{0:T(128)S(1)} %get-tuple-element.104, bf16[8,6144]{1,0:T(8,128)(2,1)} %param.8, bf16[6144,4]{0,1:T(4,128)(2,1)S(1)} %copy-done), kind=kOutput, calls=%fused_computation.69 | convolution fusion | flops 393392 | bytes 147584 | tf_op jit(solution)/shard_map/dot_general | solution.py:389
  9.1 0.9 fusion.4
  10.0 0.9 constant_dynamic-update-slice_fusion.7
  10.9 1.0 collective-permute-start.1
  11.8 3.5 %collective-permute-start.2 = (bf16[8,6272]{1,0:T(8,128)(2,1)S(1)}, bf16[8,6272]{1,0:T(8,128)(2,1)S(1)}, u32[]{:S(2)}, u32[]{:S(2)}) collective-permute-start(bf16[8,6272]{1,0:T(8,128)(2,1)S(1)} %fusion.4), channel_id=1, source_target_pairs={{2,0},{3,1},{0,2},{1,3},{6,4},{7,5},{4,6},{5,7},{10,8},{11,9},{8,1... | collective-permute-start | bytes 301064 | tf_op jit(solution)/shard_map/ppermute | solution.py:111
  15.4 1.8 %collective-permute-start.8 = (bf16[32,3072]{1,0:T(8,128)(2,1)S(1)}, bf16[32,3072]{1,0:T(8,128)(2,1)S(1)}, u32[]{:S(2)}, u32[]{:S(2)}) collective-permute-start(bf16[32,3072]{1,0:T(8,128)(2,1)S(1)} %get-tuple-element.39._), channel_id=1, source_target_pairs={{16,0},{0,16},{17,1},{1,17},{18,2},{2,18},{19,3},{3,19},{20,4},{4,... | collective-permute-start | bytes 589832 | tf_op jit(solution)/shard_map/ppermute | solution.py:111
  17.2 1.5 %collective-permute-start.9 = (bf16[32,3072]{1,0:T(8,128)(2,1)S(1)}, bf16[32,3072]{1,0:T(8,128)(2,1)S(1)}, u32[]{:S(2)}, u32[]{:S(2)}) collective-permute-start(bf16[32,3072]{1,0:T(8,128)(2,1)S(1)} %get-tuple-element.41), channel_id=1, source_target_pairs={{8,0},{12,4},{0,8},{4,12},{9,1},{13,5},{1,9},{5,13},{10,2},{14,6},... | collective-permute-start | bytes 589832 | tf_op jit(solution)/shard_map/ppermute | solution.py:111
  18.7 4.6 %shard_map.95 = (bf16[3072,1024]{1,0:T(8,128)(2,1)S(1)}, bf16[3072,1024]{1,0:T(8,128)(2,1)S(1)}) custom-call(bf16[32,3072]{1,0:T(8,128)(2,1)S(1)} %get-tuple-element.39._, bf16[1,6144,1024]{2,1,0:T(8,128)(2,1)} %refs_0_.5, bf16[1,6144,1024]{2,1,0:T(8,128)(2,1)} %refs_1_.3), custom_call_target="tpu_custom_call" | custom-call | bytes 12582912 | tf_op jit(solution)/shard_map/pallas_call | solution.py:210
  23.5 0.6 collective-permute-start.11
  24.1 1.6 %collective-permute-start.10 = (bf16[64,3072]{1,0:T(8,128)(2,1)S(1)}, bf16[64,3072]{1,0:T(8,128)(2,1)S(1)}, u32[]{:S(2)}, u32[]{:S(2)}) collective-permute-start(bf16[64,3072]{1,0:T(8,128)(2,1)S(1)} %pad_maximum_fusion.9), channel_id=1, source_target_pairs={{8,0},{12,4},{0,8},{4,12},{9,1},{13,5},{1,9},{5,13},{10,2},{14,6},... | collective-permute-start | bytes 1179656 | tf_op jit(solution)/shard_map/ppermute | solution.py:111
  25.8 0.6 collective-permute-start.5
  26.4 1.5 %collective-permute-start.4 = (bf16[32,3200]{1,0:T(8,128)(2,1)S(1)}, bf16[32,3200]{1,0:T(8,128)(2,1)S(1)}, u32[]{:S(2)}, u32[]{:S(2)}) collective-permute-start(bf16[32,3200]{1,0:T(8,128)(2,1)S(1)} %slice.96), channel_id=1, source_target_pairs={{16,0},{0,16},{17,1},{1,17},{18,2},{2,18},{19,3},{3,19},{20,4},{4,... | collective-permute-start | bytes 614408 | tf_op jit(solution)/shard_map/ppermute | solution.py:111
  27.8 2.8 %shard_map.96.down = bf16[512,6144]{1,0:T(8,128)(2,1)S(1)} custom-call(bf16[32,3072]{1,0:T(8,128)(2,1)S(1)} %collective-permute-done.9._, bf16[1,1024,6144]{2,1,0:T(8,128)(2,1)} %down_weight.1), custom_call_target="tpu_custom_call" | custom-call | bytes 6291456 | tf_op jit(solution)/shard_map/pallas_call | solution.py:210
  30.7 3.8 %collective-permute-done.11 = bf16[64,3072]{1,0:T(8,128)(2,1)S(1)} collective-permute-done((bf16[64,3072]{1,0:T(8,128)(2,1)S(1)}, bf16[64,3072]{1,0:T(8,128)(2,1)S(1)}, u32[]{:S(2)}, u32[]{:S(2)}) %collective-permute-start.11) | collective-permute-done | bytes 393248 | tf_op jit(solution)/shard_map/ppermute | solution.py:111
  35.8 1.3 %collective-permute-done.5 = bf16[32,3072]{1,0:T(8,128)(2,1)S(1)} collective-permute-done((bf16[32,3072]{1,0:T(8,128)(2,1)S(1)}, bf16[32,3072]{1,0:T(8,128)(2,1)S(1)}, u32[]{:S(2)}, u32[]{:S(2)}) %collective-permute-start.5) | collective-permute-done | bytes 196640 | tf_op jit(solution)/shard_map/ppermute | solution.py:111
  37.1 1.3 %collective-permute-start.13 = (bf16[64,3072]{1,0:T(8,128)(2,1)S(1)}, bf16[64,3072]{1,0:T(8,128)(2,1)S(1)}, u32[]{:S(2)}, u32[]{:S(2)}) collective-permute-start(bf16[64,3072]{1,0:T(8,128)(2,1)S(1)} %pad_maximum_fusion.11), channel_id=1, source_target_pairs={{16,0},{0,16},{17,1},{1,17},{18,2},{2,18},{19,3},{3,19},{20,4},{4,... | collective-permute-start | bytes 1179656 | tf_op jit(solution)/shard_map/ppermute | solution.py:111
  38.4 0.9 collective-permute-start.12
  39.5 4.7 %shard_map.97 = (f32[256,1024]{1,0:T(8,128)S(1)}, f32[256,1024]{1,0:T(8,128)S(1)}, bf16[3072,1024]{1,0:T(8,128)(2,1)S(1)}, bf16[3072,1024]{1,0:T(8,128)(2,1)S(1)}) custom-call(bf16[256,3072]{1,0:T(8,128)(2,1)S(1)} %pad_maximum_fusion.1.tokens, bf16[3072,1024]{1,0:T(8,128)(2,1)S(1)} %get-tuple-element.37.gate.gate_copy, ...), custom_call_target="tpu_custom_call" | custom-call | flops 3221225472 | bytes 1572864 | tf_op jit(solution)/shard_map/pallas_call | solution.py:252
  44.2 2.3 %shard_map.98 = (f32[256,1024]{1,0:T(8,128)S(1)}, f32[256,1024]{1,0:T(8,128)S(1)}) custom-call(bf16[256,3072]{1,0:T(8,128)(2,1)S(1)} %constant_dynamic-update-slice_fusion.8.tokens, bf16[3072,1024]{1,0:T(8,128)(2,1)S(1)} %get-tuple-element.49.gate.gate_copy, bf16[3072,1024]{1,0:T(8,128)(2,1)S(1)} %get-tuple-element.50.up.up_copy, ...), custom_call_target="tpu_custom_call" | custom-call | flops 1610612736 | bytes 786432 | tf_op jit(solution)/shard_map/pallas_call | solution.py:252
  46.9 1.4 %collective-permute-done.12 = bf16[64,3200]{1,0:T(8,128)(2,1)S(1)} collective-permute-done((bf16[64,3200]{1,0:T(8,128)(2,1)S(1)}, bf16[64,3200]{1,0:T(8,128)(2,1)S(1)}, u32[]{:S(2)}, u32[]{:S(2)}) %collective-permute-start.12) | collective-permute-done | bytes 409632 | tf_op jit(solution)/shard_map/ppermute | solution.py:111
  49.2 2.3 %shard_map.99 = (f32[256,1024]{1,0:T(8,128)S(1)}, f32[256,1024]{1,0:T(8,128)S(1)}) custom-call(bf16[256,3072]{1,0:T(8,128)(2,1)S(1)} %constant_dynamic-update-slice_fusion.8.tokens, bf16[3072,1024]{1,0:T(8,128)(2,1)S(1)} %get-tuple-element.49.gate.gate_copy, bf16[3072,1024]{1,0:T(8,128)(2,1)S(1)} %get-tuple-element.50.up.up_copy, ...), custom_call_target="tpu_custom_call" | custom-call | flops 1610612736 | bytes 786432 | tf_op jit(solution)/shard_map/pallas_call | solution.py:252
  52.1 4.7 %shard_map.100 = (bf16[256,1024]{1,0:T(8,128)(2,1)S(1)}, bf16[256,1024]{1,0:T(8,128)(2,1)S(1)}, bf16[256,128]{1,0:T(8,128)(2,1)S(1)}) custom-call(s32[1]{0:T(128)} %bitcast.expert, bf16[256,3200]{1,0:T(8,128)(2,1)S(1)} %pad_maximum_fusion.low, bf16[256,3072]{1,0:T(8,128)(2,1)S(1)} %constant_dynamic-update-slice_fusion.13.high, ...), custom_call_target="tpu_custom_call" | custom-call | flops 3221225472 | bytes 6291456 | tf_op jit(solution)/shard_map/pallas_call | solution.py:318
  56.9 3.8 %shard_map.102 = (f32[128,3072]{1,0:T(8,128)S(1)}, bf16[128,3072]{1,0:T(8,128)(2,1)S(1)}) custom-call(bf16[256,1024]{1,0:T(8,128)(2,1)S(1)} %get-tuple-element.59.grad_gate, bf16[256,1024]{1,0:T(8,128)(2,1)S(1)} %get-tuple-element.60.grad_up, bf16[3072,1024]{1,0:T(8,128)(2,1)S(1)} %get-tuple-element.49.gate.gate_copy, ...), custom_call_target="tpu_custom_call" | custom-call | flops 3221225472 | bytes 3145728 | tf_op jit(solution)/shard_map/pallas_call | solution.py:364
  60.9 3.8 %shard_map.101 = (f32[128,3200]{1,0:T(8,128)S(1)}, bf16[128,3200]{1,0:T(8,128)(2,1)S(1)}) custom-call(bf16[256,1024]{1,0:T(8,128)(2,1)S(1)} %get-tuple-element.59.grad_gate, bf16[256,1024]{1,0:T(8,128)(2,1)S(1)} %get-tuple-element.60.grad_up, bf16[3072,1024]{1,0:T(8,128)(2,1)S(1)} %get-tuple-element.37.gate.gate_copy, ...), custom_call_target="tpu_custom_call" | custom-call | flops 3221225472 | bytes 3145728 | tf_op jit(solution)/shard_map/pallas_call | solution.py:364
  65.5 0.8 collective-permute-start.25
  66.3 1.5 %collective-permute-start.24 = (bf16[64,1536]{1,0:T(8,128)(2,1)S(1)}, bf16[64,1536]{1,0:T(8,128)(2,1)S(1)}, u32[]{:S(2)}, u32[]{:S(2)}) collective-permute-start(bf16[64,1536]{1,0:T(8,128)(2,1)S(1)} %concatenate.112), channel_id=1, source_target_pairs={{8,0},{12,4},{0,8},{4,12},{9,1},{13,5},{1,9},{5,13},{10,2},{14,6},... | collective-permute-start | bytes 589832 | tf_op jit(solution)/shard_map/ppermute | solution.py:111
  68.3 0.6 collective-permute-start.20
  68.9 1.2 %collective-permute-start.19 = (bf16[64,1536]{1,0:T(8,128)(2,1)S(1)}, bf16[64,1536]{1,0:T(8,128)(2,1)S(1)}, u32[]{:S(2)}, u32[]{:S(2)}) collective-permute-start(bf16[64,1536]{1,0:T(8,128)(2,1)S(1)} %concatenate.110), channel_id=1, source_target_pairs={{8,0},{12,4},{0,8},{4,12},{9,1},{13,5},{1,9},{5,13},{10,2},{14,6},... | collective-permute-start | bytes 589832 | tf_op jit(solution)/shard_map/ppermute | solution.py:111
  70.1 3.2 %collective-permute-done.25 = bf16[64,1536]{1,0:T(8,128)(2,1)S(1)} collective-permute-done((bf16[64,1536]{1,0:T(8,128)(2,1)S(1)}, bf16[64,1536]{1,0:T(8,128)(2,1)S(1)}, u32[]{:S(2)}, u32[]{:S(2)}) %collective-permute-start.25) | collective-permute-done | bytes 196640 | tf_op jit(solution)/shard_map/ppermute | solution.py:111
  73.4 0.9 collective-permute-start.30
  74.3 1.6 %collective-permute-start.29 = (bf16[32,1536]{1,0:T(8,128)(2,1)S(1)}, bf16[32,1536]{1,0:T(8,128)(2,1)S(1)}, u32[]{:S(2)}, u32[]{:S(2)}) collective-permute-start(bf16[32,1536]{1,0:T(8,128)(2,1)S(1)} %split.122), channel_id=1, source_target_pairs={{16,0},{0,16},{17,1},{1,17},{18,2},{2,18},{19,3},{3,19},{20,4},{4,... | collective-permute-start | bytes 294920 | tf_op jit(solution)/shard_map/ppermute | solution.py:111
  75.9 2.4 %collective-permute-done.19 = bf16[64,1536]{1,0:T(8,128)(2,1)S(1)} collective-permute-done((bf16[64,1536]{1,0:T(8,128)(2,1)S(1)}, bf16[64,1536]{1,0:T(8,128)(2,1)S(1)}, u32[]{:S(2)}, u32[]{:S(2)}) %collective-permute-start.19) | collective-permute-done | bytes 196640 | tf_op jit(solution)/shard_map/ppermute | solution.py:111
  78.4 1.3 %collective-permute-start.22 = (bf16[32,1536]{1,0:T(8,128)(2,1)S(1)}, bf16[32,1536]{1,0:T(8,128)(2,1)S(1)}, u32[]{:S(2)}, u32[]{:S(2)}) collective-permute-start(bf16[32,1536]{1,0:T(8,128)(2,1)S(1)} %split.123), channel_id=1, source_target_pairs={{16,0},{0,16},{17,1},{1,17},{18,2},{2,18},{19,3},{3,19},{20,4},{4,... | collective-permute-start | bytes 294920 | tf_op jit(solution)/shard_map/ppermute | solution.py:111
  79.7 0.9 collective-permute-start.23
  80.7 3.5 %collective-permute-start.31 = (bf16[8,3072]{1,0:T(8,128)(2,1)S(1)}, bf16[8,3072]{1,0:T(8,128)(2,1)S(1)}, u32[]{:S(2)}, u32[]{:S(2)}) collective-permute-start(bf16[8,3072]{1,0:T(8,128)(2,1)S(1)} %get-tuple-element.97), channel_id=1, source_target_pairs={{1,0},{0,1},{3,2},{2,3},{5,4},{4,5},{7,6},{6,7},{9,8},{8,9},{11,10... | collective-permute-start | bytes 147464 | tf_op jit(solution)/shard_map/ppermute | solution.py:111
  84.2 1.1 %collective-permute-start.32 = (bf16[8,3072]{1,0:T(8,128)(2,1)S(1)}, bf16[8,3072]{1,0:T(8,128)(2,1)S(1)}, u32[]{:S(2)}, u32[]{:S(2)}) collective-permute-start(bf16[8,3072]{1,0:T(8,128)(2,1)S(1)} %get-tuple-element.99), channel_id=1, source_target_pairs={{2,0},{3,1},{0,2},{1,3},{6,4},{7,5},{4,6},{5,7},{10,8},{11,9},{8,1... | collective-permute-start | bytes 147464 | tf_op jit(solution)/shard_map/ppermute | solution.py:111
  85.3 1.4 %collective-permute-start.33 = (bf16[8,3072]{1,0:T(8,128)(2,1)S(1)}, bf16[8,3072]{1,0:T(8,128)(2,1)S(1)}, u32[]{:S(2)}, u32[]{:S(2)}) collective-permute-start(bf16[8,3072]{1,0:T(8,128)(2,1)S(1)} %get-tuple-element.98), channel_id=1, source_target_pairs={{3,0},{2,1},{1,2},{0,3},{7,4},{6,5},{5,6},{4,7},{11,8},{10,9},{9,1... | collective-permute-start | bytes 147464 | tf_op jit(solution)/shard_map/ppermute | solution.py:111
  86.8 1.1 %collective-permute-start.26 = (bf16[8,3200]{1,0:T(8,128)(2,1)S(1)}, bf16[8,3200]{1,0:T(8,128)(2,1)S(1)}, u32[]{:S(2)}, u32[]{:S(2)}) collective-permute-start(bf16[8,3200]{1,0:T(8,128)(2,1)S(1)} %get-tuple-element.94), channel_id=1, source_target_pairs={{1,0},{0,1},{3,2},{2,3},{5,4},{4,5},{7,6},{6,7},{9,8},{8,9},{11,10... | collective-permute-start | bytes 153608 | tf_op jit(solution)/shard_map/ppermute | solution.py:111
  87.9 2.0 %collective-permute-start.27 = (bf16[8,3200]{1,0:T(8,128)(2,1)S(1)}, bf16[8,3200]{1,0:T(8,128)(2,1)S(1)}, u32[]{:S(2)}, u32[]{:S(2)}) collective-permute-start(bf16[8,3200]{1,0:T(8,128)(2,1)S(1)} %get-tuple-element.96), channel_id=1, source_target_pairs={{2,0},{3,1},{0,2},{1,3},{6,4},{7,5},{4,6},{5,7},{10,8},{11,9},{8,1... | collective-permute-start | bytes 153608 | tf_op jit(solution)/shard_map/ppermute | solution.py:111
  89.9 1.4 %collective-permute-start.28 = (bf16[8,3200]{1,0:T(8,128)(2,1)S(1)}, bf16[8,3200]{1,0:T(8,128)(2,1)S(1)}, u32[]{:S(2)}, u32[]{:S(2)}) collective-permute-start(bf16[8,3200]{1,0:T(8,128)(2,1)S(1)} %get-tuple-element.95), channel_id=1, source_target_pairs={{3,0},{2,1},{1,2},{0,3},{7,4},{6,5},{5,6},{4,7},{11,8},{10,9},{9,1... | collective-permute-start | bytes 153608 | tf_op jit(solution)/shard_map/ppermute | solution.py:111
  92.1 1.4 %collective-permute-done.27 = bf16[8,3200]{1,0:T(8,128)(2,1)S(1)} collective-permute-done((bf16[8,3200]{1,0:T(8,128)(2,1)S(1)}, bf16[8,3200]{1,0:T(8,128)(2,1)S(1)}, u32[]{:S(2)}, u32[]{:S(2)}) %collective-permute-start.27) | collective-permute-done | bytes 51232 | tf_op jit(solution)/shard_map/ppermute | solution.py:111
  93.5 2.3 %collective-permute-done.28 = bf16[8,3200]{1,0:T(8,128)(2,1)S(1)} collective-permute-done((bf16[8,3200]{1,0:T(8,128)(2,1)S(1)}, bf16[8,3200]{1,0:T(8,128)(2,1)S(1)}, u32[]{:S(2)}, u32[]{:S(2)}) %collective-permute-start.28) | collective-permute-done | bytes 51232 | tf_op jit(solution)/shard_map/ppermute | solution.py:111
  96.1 0.6 pad_maximum_fusion.14
  96.7 0.9 fusion.3
  (103 shorter events, 6.6 us)
Async XLA Ops:
  0.6 7.1 %copy-start = (bf16[6144,4]{0,1:T(4,128)(2,1)S(1)}, bf16[6144,4]{0,1:T(4,128)(2,1)}, u32[]{:S(2)}) copy-start(bf16[6144,4]{0,1:T(4,128)(2,1)} %param.12) | copy-start | bytes 147460
  0.6 10.2 %collective-permute-start = (bf16[8,6144]{1,0:T(8,128)(2,1)}, bf16[8,6144]{1,0:T(8,128)(2,1)S(1)}, u32[]{:S(2)}, u32[]{:S(2)}) collective-permute-start(bf16[8,6144]{1,0:T(8,128)(2,1)} %param.8), channel_id=1, source_target_pairs={{1,0},{0,1},{3,2},{2,3},{5,4},{4,5},{7,6},{6,7},{9,8},{8,9},{11,10... | collective-permute-start | bytes 294920 | tf_op jit(solution)/shard_map/ppermute | solution.py:111
  3.7 11.6 %collective-permute-start.6 = (bf16[8,6144]{1,0:T(8,128)(2,1)}, bf16[8,6144]{1,0:T(8,128)(2,1)S(1)}, u32[]{:S(2)}, u32[]{:S(2)}) collective-permute-start(bf16[8,6144]{1,0:T(8,128)(2,1)} %param.8), channel_id=1, source_target_pairs={{2,0},{3,1},{0,2},{1,3},{6,4},{7,5},{4,6},{5,7},{10,8},{11,9},{8,1... | collective-permute-start | bytes 294920 | tf_op jit(solution)/shard_map/ppermute | solution.py:111
  6.3 9.1 %collective-permute-start.7 = (bf16[8,6144]{1,0:T(8,128)(2,1)}, bf16[8,6144]{1,0:T(8,128)(2,1)S(1)}, u32[]{:S(2)}, u32[]{:S(2)}) collective-permute-start(bf16[8,6144]{1,0:T(8,128)(2,1)} %param.8), channel_id=1, source_target_pairs={{3,0},{2,1},{1,2},{0,3},{7,4},{6,5},{5,6},{4,7},{11,8},{10,9},{9,1... | collective-permute-start | bytes 294920 | tf_op jit(solution)/shard_map/ppermute | solution.py:111
  10.9 12.5 %collective-permute-start.1 = (bf16[8,6272]{1,0:T(8,128)(2,1)S(1)}, bf16[8,6272]{1,0:T(8,128)(2,1)S(1)}, u32[]{:S(2)}, u32[]{:S(2)}) collective-permute-start(bf16[8,6272]{1,0:T(8,128)(2,1)S(1)} %fusion.4), channel_id=1, source_target_pairs={{1,0},{0,1},{3,2},{2,3},{5,4},{4,5},{7,6},{6,7},{9,8},{8,9},{11,10... | collective-permute-start | bytes 301064 | tf_op jit(solution)/shard_map/ppermute | solution.py:111
  11.8 11.5 %collective-permute-start.2 = (bf16[8,6272]{1,0:T(8,128)(2,1)S(1)}, bf16[8,6272]{1,0:T(8,128)(2,1)S(1)}, u32[]{:S(2)}, u32[]{:S(2)}) collective-permute-start(bf16[8,6272]{1,0:T(8,128)(2,1)S(1)} %fusion.4), channel_id=1, source_target_pairs={{2,0},{3,1},{0,2},{1,3},{6,4},{7,5},{4,6},{5,7},{10,8},{11,9},{8,1... | collective-permute-start | bytes 301064 | tf_op jit(solution)/shard_map/ppermute | solution.py:111
  15.3 8.1 %collective-permute-start.3 = (bf16[8,6272]{1,0:T(8,128)(2,1)S(1)}, bf16[8,6272]{1,0:T(8,128)(2,1)S(1)}, u32[]{:S(2)}, u32[]{:S(2)}) collective-permute-start(bf16[8,6272]{1,0:T(8,128)(2,1)S(1)} %fusion.4), channel_id=1, source_target_pairs={{3,0},{2,1},{1,2},{0,3},{7,4},{6,5},{5,6},{4,7},{11,8},{10,9},{9,1... | collective-permute-start | bytes 301064 | tf_op jit(solution)/shard_map/ppermute | solution.py:111
  15.4 8.0 %collective-permute-start.8 = (bf16[32,3072]{1,0:T(8,128)(2,1)S(1)}, bf16[32,3072]{1,0:T(8,128)(2,1)S(1)}, u32[]{:S(2)}, u32[]{:S(2)}) collective-permute-start(bf16[32,3072]{1,0:T(8,128)(2,1)S(1)} %get-tuple-element.39._), channel_id=1, source_target_pairs={{16,0},{0,16},{17,1},{1,17},{18,2},{2,18},{19,3},{3,19},{20,4},{4,... | collective-permute-start | bytes 589832 | tf_op jit(solution)/shard_map/ppermute | solution.py:111
  17.2 6.2 %collective-permute-start.9 = (bf16[32,3072]{1,0:T(8,128)(2,1)S(1)}, bf16[32,3072]{1,0:T(8,128)(2,1)S(1)}, u32[]{:S(2)}, u32[]{:S(2)}) collective-permute-start(bf16[32,3072]{1,0:T(8,128)(2,1)S(1)} %get-tuple-element.41), channel_id=1, source_target_pairs={{8,0},{12,4},{0,8},{4,12},{9,1},{13,5},{1,9},{5,13},{10,2},{14,6},... | collective-permute-start | bytes 589832 | tf_op jit(solution)/shard_map/ppermute | solution.py:111
  23.5 10.9 %collective-permute-start.11 = (bf16[64,3072]{1,0:T(8,128)(2,1)S(1)}, bf16[64,3072]{1,0:T(8,128)(2,1)S(1)}, u32[]{:S(2)}, u32[]{:S(2)}) collective-permute-start(bf16[64,3072]{1,0:T(8,128)(2,1)S(1)} %pad_maximum_fusion.10), channel_id=1, source_target_pairs={{16,0},{0,16},{17,1},{1,17},{18,2},{2,18},{19,3},{3,19},{20,4},{4,... | collective-permute-start | bytes 1179656 | tf_op jit(solution)/shard_map/ppermute | solution.py:111
  24.1 10.8 %collective-permute-start.10 = (bf16[64,3072]{1,0:T(8,128)(2,1)S(1)}, bf16[64,3072]{1,0:T(8,128)(2,1)S(1)}, u32[]{:S(2)}, u32[]{:S(2)}) collective-permute-start(bf16[64,3072]{1,0:T(8,128)(2,1)S(1)} %pad_maximum_fusion.9), channel_id=1, source_target_pairs={{8,0},{12,4},{0,8},{4,12},{9,1},{13,5},{1,9},{5,13},{10,2},{14,6},... | collective-permute-start | bytes 1179656 | tf_op jit(solution)/shard_map/ppermute | solution.py:111
  25.8 11.3 %collective-permute-start.5 = (bf16[32,3072]{1,0:T(8,128)(2,1)S(1)}, bf16[32,3072]{1,0:T(8,128)(2,1)S(1)}, u32[]{:S(2)}, u32[]{:S(2)}) collective-permute-start(bf16[32,3072]{1,0:T(8,128)(2,1)S(1)} %get-tuple-element.45), channel_id=1, source_target_pairs={{8,0},{12,4},{0,8},{4,12},{9,1},{13,5},{1,9},{5,13},{10,2},{14,6},... | collective-permute-start | bytes 589832 | tf_op jit(solution)/shard_map/ppermute | solution.py:111
  26.4 10.7 %collective-permute-start.4 = (bf16[32,3200]{1,0:T(8,128)(2,1)S(1)}, bf16[32,3200]{1,0:T(8,128)(2,1)S(1)}, u32[]{:S(2)}, u32[]{:S(2)}) collective-permute-start(bf16[32,3200]{1,0:T(8,128)(2,1)S(1)} %slice.96), channel_id=1, source_target_pairs={{16,0},{0,16},{17,1},{1,17},{18,2},{2,18},{19,3},{3,19},{20,4},{4,... | collective-permute-start | bytes 614408 | tf_op jit(solution)/shard_map/ppermute | solution.py:111
  35.0 4.3 %collective-permute-start.15 = (bf16[128,3072]{1,0:T(8,128)(2,1)S(1)}, bf16[128,3072]{1,0:T(8,128)(2,1)S(1)}, u32[]{:S(2)}, u32[]{:S(2)}) collective-permute-start(bf16[128,3072]{1,0:T(8,128)(2,1)S(1)} %pad_maximum_fusion.4), channel_id=1, source_target_pairs={{4,0},{0,4},{12,8},{8,12},{5,1},{1,5},{13,9},{9,13},{6,2},{2,6},{1... | collective-permute-start | bytes 2359304 | tf_op jit(solution)/shard_map/ppermute | solution.py:111
  35.2 4.3 %collective-permute-start.14 = (bf16[128,3072]{1,0:T(8,128)(2,1)S(1)}, bf16[128,3072]{1,0:T(8,128)(2,1)S(1)}, u32[]{:S(2)}, u32[]{:S(2)}) collective-permute-start(bf16[128,3072]{1,0:T(8,128)(2,1)S(1)} %pad_maximum_fusion.3), channel_id=1, source_target_pairs={{4,0},{0,4},{12,8},{8,12},{5,1},{1,5},{13,9},{9,13},{6,2},{2,6},{1... | collective-permute-start | bytes 2359304 | tf_op jit(solution)/shard_map/ppermute | solution.py:111
  37.1 9.8 %collective-permute-start.13 = (bf16[64,3072]{1,0:T(8,128)(2,1)S(1)}, bf16[64,3072]{1,0:T(8,128)(2,1)S(1)}, u32[]{:S(2)}, u32[]{:S(2)}) collective-permute-start(bf16[64,3072]{1,0:T(8,128)(2,1)S(1)} %pad_maximum_fusion.11), channel_id=1, source_target_pairs={{16,0},{0,16},{17,1},{1,17},{18,2},{2,18},{19,3},{3,19},{20,4},{4,... | collective-permute-start | bytes 1179656 | tf_op jit(solution)/shard_map/ppermute | solution.py:111
  38.4 9.9 %collective-permute-start.12 = (bf16[64,3200]{1,0:T(8,128)(2,1)S(1)}, bf16[64,3200]{1,0:T(8,128)(2,1)S(1)}, u32[]{:S(2)}, u32[]{:S(2)}) collective-permute-start(bf16[64,3200]{1,0:T(8,128)(2,1)S(1)} %pad_maximum_fusion.7), channel_id=1, source_target_pairs={{8,0},{12,4},{0,8},{4,12},{9,1},{13,5},{1,9},{5,13},{10,2},{14,6},... | collective-permute-start | bytes 1228808 | tf_op jit(solution)/shard_map/ppermute | solution.py:111
  48.5 3.1 %collective-permute-start.17 = (bf16[128,3072]{1,0:T(8,128)(2,1)S(1)}, bf16[128,3072]{1,0:T(8,128)(2,1)S(1)}, u32[]{:S(2)}, u32[]{:S(2)}) collective-permute-start(bf16[128,3072]{1,0:T(8,128)(2,1)S(1)} %pad_maximum_fusion.5), channel_id=1, source_target_pairs={{4,0},{0,4},{12,8},{8,12},{5,1},{1,5},{13,9},{9,13},{6,2},{2,6},{1... | collective-permute-start | bytes 2359304 | tf_op jit(solution)/shard_map/ppermute | solution.py:111
  48.6 3.4 %collective-permute-start.16 = (bf16[128,3200]{1,0:T(8,128)(2,1)S(1)}, bf16[128,3200]{1,0:T(8,128)(2,1)S(1)}, u32[]{:S(2)}, u32[]{:S(2)}) collective-permute-start(bf16[128,3200]{1,0:T(8,128)(2,1)S(1)} %pad_maximum_fusion.2), channel_id=1, source_target_pairs={{4,0},{0,4},{12,8},{8,12},{5,1},{1,5},{13,9},{9,13},{6,2},{2,6},{1... | collective-permute-start | bytes 2457608 | tf_op jit(solution)/shard_map/ppermute | solution.py:111
  60.7 4.5 %collective-permute-start.21 = (bf16[128,3072]{1,0:T(8,128)(2,1)S(1)}, bf16[128,3072]{1,0:T(8,128)(2,1)S(1)}, u32[]{:S(2)}, u32[]{:S(2)}) collective-permute-start(bf16[128,3072]{1,0:T(8,128)(2,1)S(1)} %get-tuple-element.64), channel_id=1, source_target_pairs={{4,0},{0,4},{12,8},{8,12},{5,1},{1,5},{13,9},{9,13},{6,2},{2,6},{1... | collective-permute-start | bytes 2359304 | tf_op jit(solution)/shard_map/ppermute | solution.py:111
  64.7 3.1 %collective-permute-start.18 = (bf16[128,3200]{1,0:T(8,128)(2,1)S(1)}, bf16[128,3200]{1,0:T(8,128)(2,1)S(1)}, u32[]{:S(2)}, u32[]{:S(2)}) collective-permute-start(bf16[128,3200]{1,0:T(8,128)(2,1)S(1)} %get-tuple-element.63), channel_id=1, source_target_pairs={{4,0},{0,4},{12,8},{8,12},{5,1},{1,5},{13,9},{9,13},{6,2},{2,6},{1... | collective-permute-start | bytes 2457608 | tf_op jit(solution)/shard_map/ppermute | solution.py:111
  65.5 7.8 %collective-permute-start.25 = (bf16[64,1536]{1,0:T(8,128)(2,1)S(1)}, bf16[64,1536]{1,0:T(8,128)(2,1)S(1)}, u32[]{:S(2)}, u32[]{:S(2)}) collective-permute-start(bf16[64,1536]{1,0:T(8,128)(2,1)S(1)} %pad_maximum_fusion.13), channel_id=1, source_target_pairs={{16,0},{0,16},{17,1},{1,17},{18,2},{2,18},{19,3},{3,19},{20,4},{4,... | collective-permute-start | bytes 589832 | tf_op jit(solution)/shard_map/ppermute | solution.py:111
  66.3 7.9 %collective-permute-start.24 = (bf16[64,1536]{1,0:T(8,128)(2,1)S(1)}, bf16[64,1536]{1,0:T(8,128)(2,1)S(1)}, u32[]{:S(2)}, u32[]{:S(2)}) collective-permute-start(bf16[64,1536]{1,0:T(8,128)(2,1)S(1)} %concatenate.112), channel_id=1, source_target_pairs={{8,0},{12,4},{0,8},{4,12},{9,1},{13,5},{1,9},{5,13},{10,2},{14,6},... | collective-permute-start | bytes 589832 | tf_op jit(solution)/shard_map/ppermute | solution.py:111
  68.3 10.0 %collective-permute-start.20 = (bf16[64,1664]{1,0:T(8,128)(2,1)S(1)}, bf16[64,1664]{1,0:T(8,128)(2,1)S(1)}, u32[]{:S(2)}, u32[]{:S(2)}) collective-permute-start(bf16[64,1664]{1,0:T(8,128)(2,1)S(1)} %pad_maximum_fusion.12), channel_id=1, source_target_pairs={{16,0},{0,16},{17,1},{1,17},{18,2},{2,18},{19,3},{3,19},{20,4},{4,... | collective-permute-start | bytes 638984 | tf_op jit(solution)/shard_map/ppermute | solution.py:111
  68.9 9.4 %collective-permute-start.19 = (bf16[64,1536]{1,0:T(8,128)(2,1)S(1)}, bf16[64,1536]{1,0:T(8,128)(2,1)S(1)}, u32[]{:S(2)}, u32[]{:S(2)}) collective-permute-start(bf16[64,1536]{1,0:T(8,128)(2,1)S(1)} %concatenate.110), channel_id=1, source_target_pairs={{8,0},{12,4},{0,8},{4,12},{9,1},{13,5},{1,9},{5,13},{10,2},{14,6},... | collective-permute-start | bytes 589832 | tf_op jit(solution)/shard_map/ppermute | solution.py:111
  73.4 7.2 %collective-permute-start.30 = (bf16[32,1536]{1,0:T(8,128)(2,1)S(1)}, bf16[32,1536]{1,0:T(8,128)(2,1)S(1)}, u32[]{:S(2)}, u32[]{:S(2)}) collective-permute-start(bf16[32,1536]{1,0:T(8,128)(2,1)S(1)} %split.121), channel_id=1, source_target_pairs={{8,0},{12,4},{0,8},{4,12},{9,1},{13,5},{1,9},{5,13},{10,2},{14,6},... | collective-permute-start | bytes 294920 | tf_op jit(solution)/shard_map/ppermute | solution.py:111
  74.3 6.3 %collective-permute-start.29 = (bf16[32,1536]{1,0:T(8,128)(2,1)S(1)}, bf16[32,1536]{1,0:T(8,128)(2,1)S(1)}, u32[]{:S(2)}, u32[]{:S(2)}) collective-permute-start(bf16[32,1536]{1,0:T(8,128)(2,1)S(1)} %split.122), channel_id=1, source_target_pairs={{16,0},{0,16},{17,1},{1,17},{18,2},{2,18},{19,3},{3,19},{20,4},{4,... | collective-permute-start | bytes 294920 | tf_op jit(solution)/shard_map/ppermute | solution.py:111
  78.4 8.3 %collective-permute-start.22 = (bf16[32,1536]{1,0:T(8,128)(2,1)S(1)}, bf16[32,1536]{1,0:T(8,128)(2,1)S(1)}, u32[]{:S(2)}, u32[]{:S(2)}) collective-permute-start(bf16[32,1536]{1,0:T(8,128)(2,1)S(1)} %split.123), channel_id=1, source_target_pairs={{16,0},{0,16},{17,1},{1,17},{18,2},{2,18},{19,3},{3,19},{20,4},{4,... | collective-permute-start | bytes 294920 | tf_op jit(solution)/shard_map/ppermute | solution.py:111
  79.7 7.0 %collective-permute-start.23 = (bf16[32,1664]{1,0:T(8,128)(2,1)S(1)}, bf16[32,1664]{1,0:T(8,128)(2,1)S(1)}, u32[]{:S(2)}, u32[]{:S(2)}) collective-permute-start(bf16[32,1664]{1,0:T(8,128)(2,1)S(1)} %split.120), channel_id=1, source_target_pairs={{8,0},{12,4},{0,8},{4,12},{9,1},{13,5},{1,9},{5,13},{10,2},{14,6},... | collective-permute-start | bytes 319496 | tf_op jit(solution)/shard_map/ppermute | solution.py:111
  80.7 9.2 %collective-permute-start.31 = (bf16[8,3072]{1,0:T(8,128)(2,1)S(1)}, bf16[8,3072]{1,0:T(8,128)(2,1)S(1)}, u32[]{:S(2)}, u32[]{:S(2)}) collective-permute-start(bf16[8,3072]{1,0:T(8,128)(2,1)S(1)} %get-tuple-element.97), channel_id=1, source_target_pairs={{1,0},{0,1},{3,2},{2,3},{5,4},{4,5},{7,6},{6,7},{9,8},{8,9},{11,10... | collective-permute-start | bytes 147464 | tf_op jit(solution)/shard_map/ppermute | solution.py:111
  84.2 7.1 %collective-permute-start.32 = (bf16[8,3072]{1,0:T(8,128)(2,1)S(1)}, bf16[8,3072]{1,0:T(8,128)(2,1)S(1)}, u32[]{:S(2)}, u32[]{:S(2)}) collective-permute-start(bf16[8,3072]{1,0:T(8,128)(2,1)S(1)} %get-tuple-element.99), channel_id=1, source_target_pairs={{2,0},{3,1},{0,2},{1,3},{6,4},{7,5},{4,6},{5,7},{10,8},{11,9},{8,1... | collective-permute-start | bytes 147464 | tf_op jit(solution)/shard_map/ppermute | solution.py:111
  85.3 6.3 %collective-permute-start.33 = (bf16[8,3072]{1,0:T(8,128)(2,1)S(1)}, bf16[8,3072]{1,0:T(8,128)(2,1)S(1)}, u32[]{:S(2)}, u32[]{:S(2)}) collective-permute-start(bf16[8,3072]{1,0:T(8,128)(2,1)S(1)} %get-tuple-element.98), channel_id=1, source_target_pairs={{3,0},{2,1},{1,2},{0,3},{7,4},{6,5},{5,6},{4,7},{11,8},{10,9},{9,1... | collective-permute-start | bytes 147464 | tf_op jit(solution)/shard_map/ppermute | solution.py:111
  86.7 9.3 %copy-start.1 = (s32[8]{0:T(128)S(1)}, s32[8]{0:T(128)}, u32[]{:S(2)}) copy-start(s32[8]{0:T(128)} %param.10) | copy-start | bytes 100
  86.8 5.3 %collective-permute-start.26 = (bf16[8,3200]{1,0:T(8,128)(2,1)S(1)}, bf16[8,3200]{1,0:T(8,128)(2,1)S(1)}, u32[]{:S(2)}, u32[]{:S(2)}) collective-permute-start(bf16[8,3200]{1,0:T(8,128)(2,1)S(1)} %get-tuple-element.94), channel_id=1, source_target_pairs={{1,0},{0,1},{3,2},{2,3},{5,4},{4,5},{7,6},{6,7},{9,8},{8,9},{11,10... | collective-permute-start | bytes 153608 | tf_op jit(solution)/shard_map/ppermute | solution.py:111
  87.9 5.6 %collective-permute-start.27 = (bf16[8,3200]{1,0:T(8,128)(2,1)S(1)}, bf16[8,3200]{1,0:T(8,128)(2,1)S(1)}, u32[]{:S(2)}, u32[]{:S(2)}) collective-permute-start(bf16[8,3200]{1,0:T(8,128)(2,1)S(1)} %get-tuple-element.96), channel_id=1, source_target_pairs={{2,0},{3,1},{0,2},{1,3},{6,4},{7,5},{4,6},{5,7},{10,8},{11,9},{8,1... | collective-permute-start | bytes 153608 | tf_op jit(solution)/shard_map/ppermute | solution.py:111
  89.9 5.9 %collective-permute-start.28 = (bf16[8,3200]{1,0:T(8,128)(2,1)S(1)}, bf16[8,3200]{1,0:T(8,128)(2,1)S(1)}, u32[]{:S(2)}, u32[]{:S(2)}) collective-permute-start(bf16[8,3200]{1,0:T(8,128)(2,1)S(1)} %get-tuple-element.95), channel_id=1, source_target_pairs={{3,0},{2,1},{1,2},{0,3},{7,4},{6,5},{5,6},{4,7},{11,8},{10,9},{9,1... | collective-permute-start | bytes 153608 | tf_op jit(solution)/shard_map/ppermute | solution.py:111

commit v13 on v12

--- a/solution.py
+++ b/solution.py
@@ -220,18 +220,19 @@
     )(earlier, *[in_hbm(value) for value in weights])
 
 
-def token_kernel(first, offset, length, tokens, gate, up, *refs):
-    pre_gate, pre_up = refs[2:4]
+def token_kernel(offset, length, sources, summed, tokens, gate, up, *refs):
+    before, refs = refs[:summed], refs[summed:]
+    count = len(sources)
+    weights, (pre_gate, pre_up), fetched = refs[:count], refs[count:count + 2], refs[count + 2:2 * count + 2]
     depth = part_of(length, TOKEN_PART)
     copies = []
-    if first:
-        for index in range(2):
-            source = refs[index].at[0, pl.ds(first, gate.shape[0])]
-            copies.append(pltpu.make_async_copy(source, refs[4 + index], refs[6].at[index]))
+    for index in range(count):
+        source = weights[index].at[0, pl.ds(sources[index], fetched[index].shape[0])]
+        copies.append(pltpu.make_async_copy(source, fetched[index], refs[-1].at[index]))
     for copy in copies:
         copy.start()
-    pre_gate[...] = jnp.zeros_like(pre_gate) if first else refs[0][...]
-    pre_up[...] = jnp.zeros_like(pre_up) if first else refs[1][...]
+    pre_gate[...] = before[0][...] if summed else jnp.zeros_like(pre_gate)
+    pre_up[...] = before[1][...] if summed else jnp.zeros_like(pre_up)
 
     @pl.loop(0, length // depth)
     def _(step):
@@ -243,24 +244,24 @@
         copy.wait()
 
 
-def multiply_tokens(tokens, gate, up, offset, length, first, *others):
+def multiply_tokens(tokens, gate, up, offset, length, sums=(), wanted=()):
     rows, hidden = tokens.shape[0], gate.shape[1]
-    sums = (pltpu.VMEM((rows, hidden), jnp.float32),) * 2
-    fetched = (pltpu.VMEM(gate.shape, jnp.bfloat16),) * 2 if first else ()
-    if first:
-        others = [in_hbm(value) for value in others]
+    shapes = [(count, value.shape[2]) for value, _, count in wanted]
+    sources = tuple(first for _, first, _ in wanted)
+    out_shape = (pltpu.VMEM((rows, hidden), jnp.float32),) * 2
+    out_shape += tuple(pltpu.VMEM(shape, jnp.bfloat16) for shape in shapes)
     return pl.pallas_call(
-        functools.partial(token_kernel, first, offset, length),
-        out_shape=sums + fetched,
-        in_specs=[pl.BlockSpec(memory_space=pltpu.VMEM)] * 3
-        + [pl.BlockSpec(memory_space=pl.ANY if first else pltpu.VMEM)] * 2,
-        out_specs=(pl.BlockSpec(memory_space=pltpu.VMEM),) * len(sums + fetched),
-        scratch_shapes=[pltpu.SemaphoreType.DMA((2,))] if first else [],
+        functools.partial(token_kernel, offset, length, sources, len(sums)),
+        out_shape=out_shape,
+        in_specs=[pl.BlockSpec(memory_space=pltpu.VMEM)] * (3 + len(sums))
+        + [pl.BlockSpec(memory_space=pl.ANY)] * len(wanted),
+        out_specs=(pl.BlockSpec(memory_space=pltpu.VMEM),) * len(out_shape),
+        scratch_shapes=[pltpu.SemaphoreType.DMA((len(wanted),))] if wanted else [],
         compiler_params=pltpu.CompilerParams(vmem_limit_bytes=TOKEN_VMEM),
         cost_estimate=pl.CostEstimate(
             flops=4 * rows * length * hidden, bytes_accessed=2 * rows * length, transcendentals=0
         ),
-    )(tokens, gate, up, *others)
+    )(tokens, gate, up, *sums, *[in_hbm(value) for value, _, _ in wanted])
 
 
 def grad_kernel(
@@ -395,20 +396,23 @@
     gate_table = jnp.pad(gate_table.astype(jnp.bfloat16), ((0, 0), (0, table - expert_count)))
     grad_z = gather_z(after_others(jnp.concatenate([gate_table, out_grad], axis=1), token_z[1]))
     token_near = gather_near(token_z, half)
-    gate_low, up_low = fetch(0, half, token_near[0][0], gate_weight, up_weight)
-    token_near = after_others(token_near, (gate_low, up_low))
+    (gate_low,) = fetch(0, half, token_near[0][0], gate_weight)
+    token_near = after_others(token_near, gate_low)
     token_far = gather_far(*token_near)
-    grad_near = gather_near(grad_z, half + table)
-    (down,) = fetch(0, down_weight.shape[1] // 2, token_near[1][1], down_weight)
+    (up_low,) = fetch(0, half, token_near[1][1], up_weight)
+    grad_near = gather_near(after_others(grad_z, token_near), half + table)
     grad_far = gather_far(*after_others(grad_near, token_far))
-    token_far = after_others(token_far, down)
+    token_far = after_others(token_far, up_low)
     token_low, token_high = gather_core(token_near[0], token_far[0], token_near[1], token_far[1])
     pre_gate, pre_up, gate_high, up_high = multiply_tokens(
-        token_low, gate_low, up_low, 0, half, half, gate_weight, up_weight
-    )
-    pre_gate, pre_up = multiply_tokens(token_high, gate_high, up_high, 0, quarter, 0, pre_gate, pre_up)
+        token_low, gate_low, up_low, 0, half, (), ((gate_weight, half, half), (up_weight, half, half))
+    )
+    pre_gate, pre_up = multiply_tokens(token_high, gate_high, up_high, 0, quarter, (pre_gate, pre_up))
     grad_far = after_others(grad_far, pre_gate)
-    pre_gate, pre_up = multiply_tokens(token_high, gate_high, up_high, quarter, quarter, 0, pre_gate, pre_up)
+    pre_gate, pre_up, down = multiply_tokens(
+        token_high, gate_high, up_high, quarter, quarter, (pre_gate, pre_up),
+        ((down_weight, 0, down_weight.shape[1] // 2),),
+    )
     grad_halves = gather_core(grad_near[0], grad_far[0], grad_near[1], grad_far[1])
     expert = lax.axis_index("expert").astype(jnp.int32).reshape(1)
     grad_gate, grad_up, dots = multiply_grads(expert, *grad_halves, pre_gate, pre_up, down, down_weight)

time: 97.9 us -> 97 us (level)
  waiting for transfers between devices: 18 us -> 24 us
  starting transfers between devices: 40.9 us -> 36.3 us
  Pallas kernels: 29 us -> 27.7 us
    ppermute x34, waiting for transfers between devices: 18 us -> 24 us  [swap(): lax.ppermute(value, axis, [(i ^ bit, i) for i in range(lax.axis_size(axis...]
    ppermute x34, starting transfers between devices: 40.9 us -> 36.3 us  [swap(): lax.ppermute(value, axis, [(i ^ bit, i) for i in range(lax.axis_size(axis...]
    pallas_call x2, Pallas kernels: 7.41 us -> 5.59 us  [fetch(): pl.pallas_call(functools.partial(fetch_kernel, first), out_shape=tuple((p...]
  transfers between devices with their start and end apart: 34 -> 34, of which waited for: 12 -> 14; matrix products, arithmetic and copies ran while one was open for 6% -> 6% of each run, Pallas kernels for 21% -> 20%
where the time goes in v13:
time: 97 us; the launch traced here: 96.7 us
  starting transfers between devices  36.3 us (37%)
  Pallas kernels  27.7 us (29%)
  waiting for transfers between devices  24 us (25%)
  other arithmetic  2.99 us (3%)
  local copies, waits for them, and re-layouts  2.36 us (2%)
  matrix products  2.15 us (2%)
  between operations  1.22 us (1%)
    ppermute x34, starting transfers between devices, swap(): lax.ppermute(value, axis, [(i ^ bit, i) for i in range(lax.axis_size(axis...  36.3 us
    ppermute x34, waiting for transfers between devices, swap(): lax.ppermute(value, axis, [(i ^ bit, i) for i in range(lax.axis_size(axis...  24 us
    pallas_call x3, Pallas kernels, multiply_tokens(): pl.pallas_call(functools.partial(token_kernel, offset, length, sources, l...  9.74 us
    pallas_call x2, Pallas kernels, multiply_outputs(): pl.pallas_call(output_kernel, out_shape=(pltpu.VMEM((rows // 2, total), j...  7.66 us
    pallas_call x2, Pallas kernels, fetch(): pl.pallas_call(functools.partial(fetch_kernel, first), out_shape=tuple((p...  5.59 us
    pallas_call x1, Pallas kernels, multiply_grads(): pl.pallas_call(grad_kernel, out_shape=(pltpu.VMEM((rows, hidden), jnp.bfl...  4.72 us
  transfers between devices with their start and end apart: 34, of which 14 were waited for; matrix products, arithmetic and copies ran while one was open for 6% of the time, Pallas kernels for 20%

profile of v13, /device:TPU:0, one launch (start us, length us, event | category | flops | bytes accessed | tf_op | source)
XLA Modules:
  0.0 96.7 jit_solution(7351233078501876812)
XLA Ops:
  0.7 3.1 %collective-permute-start = (bf16[8,6144]{1,0:T(8,128)(2,1)}, bf16[8,6144]{1,0:T(8,128)(2,1)S(1)}, u32[]{:S(2)}, u32[]{:S(2)}) collective-permute-start(bf16[8,6144]{1,0:T(8,128)(2,1)} %param.8), channel_id=1, source_target_pairs={{1,0},{0,1},{3,2},{2,3},{5,4},{4,5},{7,6},{6,7},{9,8},{8,9},{11,10... | collective-permute-start | bytes 294920 | tf_op jit(solution)/shard_map/ppermute | solution.py:111
  3.7 2.6 %collective-permute-start.4 = (bf16[8,6144]{1,0:T(8,128)(2,1)}, bf16[8,6144]{1,0:T(8,128)(2,1)S(1)}, u32[]{:S(2)}, u32[]{:S(2)}) collective-permute-start(bf16[8,6144]{1,0:T(8,128)(2,1)} %param.8), channel_id=1, source_target_pairs={{2,0},{3,1},{0,2},{1,3},{6,4},{7,5},{4,6},{5,7},{10,8},{11,9},{8,1... | collective-permute-start | bytes 294920 | tf_op jit(solution)/shard_map/ppermute | solution.py:111
  6.3 1.0 constant_dynamic-update-slice_fusion.3
  7.3 0.8 slice_bitcast_fusion
  8.1 0.7 convert_element_type.76
  8.7 1.2 %select_reduce_fusion.3 = (f32[8]{0:T(128)S(1)}, f32[8]{0:T(128)S(1)}) fusion(s32[8]{0:T(128)S(1)} %get-tuple-element.111, s32[8]{0:T(128)S(1)} %get-tuple-element.110, bf16[8,6144]{1,0:T(8,128)(2,1)} %param.8, bf16[6144,4]{0,1:T(4,128)(2,1)S(1)} %copy-done), kind=kOutput, calls=%fused_computation.69 | convolution fusion | flops 393392 | bytes 147584 | tf_op jit(solution)/shard_map/dot_general | solution.py:390
  10.1 4.3 %collective-permute-done.4 = bf16[8,6144]{1,0:T(8,128)(2,1)S(1)} collective-permute-done((bf16[8,6144]{1,0:T(8,128)(2,1)}, bf16[8,6144]{1,0:T(8,128)(2,1)S(1)}, u32[]{:S(2)}, u32[]{:S(2)}) %collective-permute-start.4) | collective-permute-done | bytes 98336 | tf_op jit(solution)/shard_map/ppermute | solution.py:111
  14.5 1.6 %collective-permute-start.6 = (bf16[32,3072]{1,0:T(8,128)(2,1)S(1)}, bf16[32,3072]{1,0:T(8,128)(2,1)S(1)}, u32[]{:S(2)}, u32[]{:S(2)}) collective-permute-start(bf16[32,3072]{1,0:T(8,128)(2,1)S(1)} %get-tuple-element.40._), channel_id=1, source_target_pairs={{16,0},{0,16},{17,1},{1,17},{18,2},{2,18},{19,3},{3,19},{20,4},{4,... | collective-permute-start | bytes 589832 | tf_op jit(solution)/shard_map/ppermute | solution.py:111
  16.0 1.5 %collective-permute-start.7 = (bf16[32,3072]{1,0:T(8,128)(2,1)S(1)}, bf16[32,3072]{1,0:T(8,128)(2,1)S(1)}, u32[]{:S(2)}, u32[]{:S(2)}) collective-permute-start(bf16[32,3072]{1,0:T(8,128)(2,1)S(1)} %get-tuple-element.42), channel_id=1, source_target_pairs={{8,0},{12,4},{0,8},{4,12},{9,1},{13,5},{1,9},{5,13},{10,2},{14,6},... | collective-permute-start | bytes 589832 | tf_op jit(solution)/shard_map/ppermute | solution.py:111
  17.6 1.7 %collective-permute-start.1 = (bf16[8,6272]{1,0:T(8,128)(2,1)S(1)}, bf16[8,6272]{1,0:T(8,128)(2,1)S(1)}, u32[]{:S(2)}, u32[]{:S(2)}) collective-permute-start(bf16[8,6272]{1,0:T(8,128)(2,1)S(1)} %fusion.4), channel_id=1, source_target_pairs={{1,0},{0,1},{3,2},{2,3},{5,4},{4,5},{7,6},{6,7},{9,8},{8,9},{11,10... | collective-permute-start | bytes 301064 | tf_op jit(solution)/shard_map/ppermute | solution.py:111
  19.2 1.4 %collective-permute-start.2 = (bf16[8,6272]{1,0:T(8,128)(2,1)S(1)}, bf16[8,6272]{1,0:T(8,128)(2,1)S(1)}, u32[]{:S(2)}, u32[]{:S(2)}) collective-permute-start(bf16[8,6272]{1,0:T(8,128)(2,1)S(1)} %fusion.4), channel_id=1, source_target_pairs={{2,0},{3,1},{0,2},{1,3},{6,4},{7,5},{4,6},{5,7},{10,8},{11,9},{8,1... | collective-permute-start | bytes 301064 | tf_op jit(solution)/shard_map/ppermute | solution.py:111
  20.6 1.4 %collective-permute-start.3 = (bf16[8,6272]{1,0:T(8,128)(2,1)S(1)}, bf16[8,6272]{1,0:T(8,128)(2,1)S(1)}, u32[]{:S(2)}, u32[]{:S(2)}) collective-permute-start(bf16[8,6272]{1,0:T(8,128)(2,1)S(1)} %fusion.4), channel_id=1, source_target_pairs={{3,0},{2,1},{1,2},{0,3},{7,4},{6,5},{5,6},{4,7},{11,8},{10,9},{9,1... | collective-permute-start | bytes 301064 | tf_op jit(solution)/shard_map/ppermute | solution.py:111
  22.0 2.8 %shard_map.95.gate.gate_copy = bf16[3072,1024]{1,0:T(8,128)(2,1)S(1)} custom-call(bf16[32,3072]{1,0:T(8,128)(2,1)S(1)} %get-tuple-element.40._, bf16[1,6144,1024]{2,1,0:T(8,128)(2,1)} %refs_0_.5), custom_call_target="tpu_custom_call" | custom-call | bytes 6291456 | tf_op jit(solution)/shard_map/pallas_call | solution.py:210
  24.9 0.6 collective-permute-start.11
  25.5 0.6 collective-permute-start.10
  26.1 2.0 %collective-permute-done.2 = bf16[8,6272]{1,0:T(8,128)(2,1)S(1)} collective-permute-done((bf16[8,6272]{1,0:T(8,128)(2,1)S(1)}, bf16[8,6272]{1,0:T(8,128)(2,1)S(1)}, u32[]{:S(2)}, u32[]{:S(2)}) %collective-permute-start.2) | collective-permute-done | bytes 100384 | tf_op jit(solution)/shard_map/ppermute | solution.py:111
  28.2 2.8 %shard_map.96.up.up_copy = bf16[3072,1024]{1,0:T(8,128)(2,1)S(1)} custom-call(bf16[32,3072]{1,0:T(8,128)(2,1)S(1)} %collective-permute-done.7._, bf16[1,6144,1024]{2,1,0:T(8,128)(2,1)} %refs_1_.1), custom_call_target="tpu_custom_call" | custom-call | bytes 6291456 | tf_op jit(solution)/shard_map/pallas_call | solution.py:210
  31.0 0.6 collective-permute-start.9
  32.1 3.2 %collective-permute-done.11 = bf16[64,3072]{1,0:T(8,128)(2,1)S(1)} collective-permute-done((bf16[64,3072]{1,0:T(8,128)(2,1)S(1)}, bf16[64,3072]{1,0:T(8,128)(2,1)S(1)}, u32[]{:S(2)}, u32[]{:S(2)}) %collective-permute-start.11) | collective-permute-done | bytes 393248 | tf_op jit(solution)/shard_map/ppermute | solution.py:111
  36.4 1.3 %collective-permute-done.9 = bf16[32,3072]{1,0:T(8,128)(2,1)S(1)} collective-permute-done((bf16[32,3072]{1,0:T(8,128)(2,1)S(1)}, bf16[32,3072]{1,0:T(8,128)(2,1)S(1)}, u32[]{:S(2)}, u32[]{:S(2)}) %collective-permute-start.9) | collective-permute-done | bytes 196640 | tf_op jit(solution)/shard_map/ppermute | solution.py:111
  37.8 1.6 %collective-permute-start.13 = (bf16[64,3072]{1,0:T(8,128)(2,1)S(1)}, bf16[64,3072]{1,0:T(8,128)(2,1)S(1)}, u32[]{:S(2)}, u32[]{:S(2)}) collective-permute-start(bf16[64,3072]{1,0:T(8,128)(2,1)S(1)} %pad_maximum_fusion.11), channel_id=1, source_target_pairs={{16,0},{0,16},{17,1},{1,17},{18,2},{2,18},{19,3},{3,19},{20,4},{4,... | collective-permute-start | bytes 1179656 | tf_op jit(solution)/shard_map/ppermute | solution.py:111
  39.3 0.6 collective-permute-start.12
  40.1 4.7 %shard_map.97 = (f32[256,1024]{1,0:T(8,128)S(1)}, f32[256,1024]{1,0:T(8,128)S(1)}, bf16[3072,1024]{1,0:T(8,128)(2,1)S(1)}, bf16[3072,1024]{1,0:T(8,128)(2,1)S(1)}) custom-call(bf16[256,3072]{1,0:T(8,128)(2,1)S(1)} %pad_maximum_fusion.1.tokens, bf16[3072,1024]{1,0:T(8,128)(2,1)S(1)} %shard_map.95.gate.gate_copy, bf16[3072,1024]{1,0:T(8,128)(2,1)S(1)} %shard_map.96.up.up_copy, ...), custom_call_target="tpu_custom_call" | custom-call | flops 3221225472 | bytes 1572864 | tf_op jit(solution)/shard_map/pallas_call | solution.py:253
  44.8 2.3 %shard_map.98 = (f32[256,1024]{1,0:T(8,128)S(1)}, f32[256,1024]{1,0:T(8,128)S(1)}) custom-call(bf16[256,3072]{1,0:T(8,128)(2,1)S(1)} %constant_dynamic-update-slice_fusion.8.tokens, bf16[3072,1024]{1,0:T(8,128)(2,1)S(1)} %get-tuple-element.54.gate.gate_copy, bf16[3072,1024]{1,0:T(8,128)(2,1)S(1)} %get-tuple-element.55.up.up_copy, ...), custom_call_target="tpu_custom_call" | custom-call | flops 1610612736 | bytes 786432 | tf_op jit(solution)/shard_map/pallas_call | solution.py:253
  47.6 1.7 %collective-permute-done.12 = bf16[64,3200]{1,0:T(8,128)(2,1)S(1)} collective-permute-done((bf16[64,3200]{1,0:T(8,128)(2,1)S(1)}, bf16[64,3200]{1,0:T(8,128)(2,1)S(1)}, u32[]{:S(2)}, u32[]{:S(2)}) %collective-permute-start.12) | collective-permute-done | bytes 409632 | tf_op jit(solution)/shard_map/ppermute | solution.py:111
  49.5 0.6 collective-permute-start.16
  50.1 2.8 %shard_map.99 = (f32[256,1024]{1,0:T(8,128)S(1)}, f32[256,1024]{1,0:T(8,128)S(1)}, bf16[512,6144]{1,0:T(8,128)(2,1)S(1)}) custom-call(bf16[256,3072]{1,0:T(8,128)(2,1)S(1)} %constant_dynamic-update-slice_fusion.8.tokens, bf16[3072,1024]{1,0:T(8,128)(2,1)S(1)} %get-tuple-element.54.gate.gate_copy, bf16[3072,1024]{1,0:T(8,128)(2,1)S(1)} %get-tuple-element.55.up.up_copy, ...), custom_call_target="tpu_custom_call" | custom-call | flops 1610612736 | bytes 786432 | tf_op jit(solution)/shard_map/pallas_call | solution.py:253
  53.1 4.7 %shard_map.100 = (bf16[256,1024]{1,0:T(8,128)(2,1)S(1)}, bf16[256,1024]{1,0:T(8,128)(2,1)S(1)}, bf16[256,128]{1,0:T(8,128)(2,1)S(1)}) custom-call(s32[1]{0:T(128)} %bitcast.expert, bf16[256,3200]{1,0:T(8,128)(2,1)S(1)} %pad_maximum_fusion.low, bf16[256,3072]{1,0:T(8,128)(2,1)S(1)} %constant_dynamic-update-slice_fusion.13.high, ...), custom_call_target="tpu_custom_call" | custom-call | flops 3221225472 | bytes 6291456 | tf_op jit(solution)/shard_map/pallas_call | solution.py:319
  57.9 3.8 %shard_map.102 = (f32[128,3072]{1,0:T(8,128)S(1)}, bf16[128,3072]{1,0:T(8,128)(2,1)S(1)}) custom-call(bf16[256,1024]{1,0:T(8,128)(2,1)S(1)} %get-tuple-element.65.grad_gate, bf16[256,1024]{1,0:T(8,128)(2,1)S(1)} %get-tuple-element.66.grad_up, bf16[3072,1024]{1,0:T(8,128)(2,1)S(1)} %get-tuple-element.54.gate.gate_copy, ...), custom_call_target="tpu_custom_call" | custom-call | flops 3221225472 | bytes 3145728 | tf_op jit(solution)/shard_map/pallas_call | solution.py:365
  61.8 3.8 %shard_map.101 = (f32[128,3200]{1,0:T(8,128)S(1)}, bf16[128,3200]{1,0:T(8,128)(2,1)S(1)}) custom-call(bf16[256,1024]{1,0:T(8,128)(2,1)S(1)} %get-tuple-element.65.grad_gate, bf16[256,1024]{1,0:T(8,128)(2,1)S(1)} %get-tuple-element.66.grad_up, bf16[3072,1024]{1,0:T(8,128)(2,1)S(1)} %shard_map.95.gate.gate_copy, bf16[3072,1024]{1,0:T(8,128)(2,1)S(1)} %shard_map.96.up.up_copy, ...), custom_call_target="tpu_custom_call" | custom-call | flops 3221225472 | bytes 3145728 | tf_op jit(solution)/shard_map/pallas_call | solution.py:365
  66.5 0.6 collective-permute-start.25
  68.5 1.1 %collective-permute-start.20 = (bf16[64,1664]{1,0:T(8,128)(2,1)S(1)}, bf16[64,1664]{1,0:T(8,128)(2,1)S(1)}, u32[]{:S(2)}, u32[]{:S(2)}) collective-permute-start(bf16[64,1664]{1,0:T(8,128)(2,1)S(1)} %pad_maximum_fusion.12), channel_id=1, source_target_pairs={{16,0},{0,16},{17,1},{1,17},{18,2},{2,18},{19,3},{3,19},{20,4},{4,... | collective-permute-start | bytes 638984 | tf_op jit(solution)/shard_map/ppermute | solution.py:111
  69.6 1.5 %collective-permute-start.19 = (bf16[64,1536]{1,0:T(8,128)(2,1)S(1)}, bf16[64,1536]{1,0:T(8,128)(2,1)S(1)}, u32[]{:S(2)}, u32[]{:S(2)}) collective-permute-start(bf16[64,1536]{1,0:T(8,128)(2,1)S(1)} %concatenate.110), channel_id=1, source_target_pairs={{8,0},{12,4},{0,8},{4,12},{9,1},{13,5},{1,9},{5,13},{10,2},{14,6},... | collective-permute-start | bytes 589832 | tf_op jit(solution)/shard_map/ppermute | solution.py:111
  71.1 3.2 %collective-permute-done.25 = bf16[64,1536]{1,0:T(8,128)(2,1)S(1)} collective-permute-done((bf16[64,1536]{1,0:T(8,128)(2,1)S(1)}, bf16[64,1536]{1,0:T(8,128)(2,1)S(1)}, u32[]{:S(2)}, u32[]{:S(2)}) %collective-permute-start.25) | collective-permute-done | bytes 196640 | tf_op jit(solution)/shard_map/ppermute | solution.py:111
  74.4 0.6 collective-permute-start.30
  75.0 1.5 %collective-permute-start.29 = (bf16[32,1536]{1,0:T(8,128)(2,1)S(1)}, bf16[32,1536]{1,0:T(8,128)(2,1)S(1)}, u32[]{:S(2)}, u32[]{:S(2)}) collective-permute-start(bf16[32,1536]{1,0:T(8,128)(2,1)S(1)} %split.122), channel_id=1, source_target_pairs={{16,0},{0,16},{17,1},{1,17},{18,2},{2,18},{19,3},{3,19},{20,4},{4,... | collective-permute-start | bytes 294920 | tf_op jit(solution)/shard_map/ppermute | solution.py:111
  76.5 2.4 %collective-permute-done.19 = bf16[64,1536]{1,0:T(8,128)(2,1)S(1)} collective-permute-done((bf16[64,1536]{1,0:T(8,128)(2,1)S(1)}, bf16[64,1536]{1,0:T(8,128)(2,1)S(1)}, u32[]{:S(2)}, u32[]{:S(2)}) %collective-permute-start.19) | collective-permute-done | bytes 196640 | tf_op jit(solution)/shard_map/ppermute | solution.py:111
  79.0 1.6 %collective-permute-start.22 = (bf16[32,1536]{1,0:T(8,128)(2,1)S(1)}, bf16[32,1536]{1,0:T(8,128)(2,1)S(1)}, u32[]{:S(2)}, u32[]{:S(2)}) collective-permute-start(bf16[32,1536]{1,0:T(8,128)(2,1)S(1)} %split.123), channel_id=1, source_target_pairs={{16,0},{0,16},{17,1},{1,17},{18,2},{2,18},{19,3},{3,19},{20,4},{4,... | collective-permute-start | bytes 294920 | tf_op jit(solution)/shard_map/ppermute | solution.py:111
  80.6 0.6 collective-permute-start.23
  81.3 1.0 %collective-permute-start.31 = (bf16[8,3072]{1,0:T(8,128)(2,1)S(1)}, bf16[8,3072]{1,0:T(8,128)(2,1)S(1)}, u32[]{:S(2)}, u32[]{:S(2)}) collective-permute-start(bf16[8,3072]{1,0:T(8,128)(2,1)S(1)} %get-tuple-element.103), channel_id=1, source_target_pairs={{1,0},{0,1},{3,2},{2,3},{5,4},{4,5},{7,6},{6,7},{9,8},{8,9},{11,10... | collective-permute-start | bytes 147464 | tf_op jit(solution)/shard_map/ppermute | solution.py:111
  82.3 2.1 %collective-permute-start.32 = (bf16[8,3072]{1,0:T(8,128)(2,1)S(1)}, bf16[8,3072]{1,0:T(8,128)(2,1)S(1)}, u32[]{:S(2)}, u32[]{:S(2)}) collective-permute-start(bf16[8,3072]{1,0:T(8,128)(2,1)S(1)} %get-tuple-element.105), channel_id=1, source_target_pairs={{2,0},{3,1},{0,2},{1,3},{6,4},{7,5},{4,6},{5,7},{10,8},{11,9},{8,1... | collective-permute-start | bytes 147464 | tf_op jit(solution)/shard_map/ppermute | solution.py:111
  84.4 1.4 %collective-permute-start.33 = (bf16[8,3072]{1,0:T(8,128)(2,1)S(1)}, bf16[8,3072]{1,0:T(8,128)(2,1)S(1)}, u32[]{:S(2)}, u32[]{:S(2)}) collective-permute-start(bf16[8,3072]{1,0:T(8,128)(2,1)S(1)} %get-tuple-element.104), channel_id=1, source_target_pairs={{3,0},{2,1},{1,2},{0,3},{7,4},{6,5},{5,6},{4,7},{11,8},{10,9},{9,1... | collective-permute-start | bytes 147464 | tf_op jit(solution)/shard_map/ppermute | solution.py:111
  86.5 2.5 %collective-permute-start.27 = (bf16[8,3200]{1,0:T(8,128)(2,1)S(1)}, bf16[8,3200]{1,0:T(8,128)(2,1)S(1)}, u32[]{:S(2)}, u32[]{:S(2)}) collective-permute-start(bf16[8,3200]{1,0:T(8,128)(2,1)S(1)} %get-tuple-element.102), channel_id=1, source_target_pairs={{2,0},{3,1},{0,2},{1,3},{6,4},{7,5},{4,6},{5,7},{10,8},{11,9},{8,1... | collective-permute-start | bytes 153608 | tf_op jit(solution)/shard_map/ppermute | solution.py:111
  89.0 1.4 %collective-permute-start.28 = (bf16[8,3200]{1,0:T(8,128)(2,1)S(1)}, bf16[8,3200]{1,0:T(8,128)(2,1)S(1)}, u32[]{:S(2)}, u32[]{:S(2)}) collective-permute-start(bf16[8,3200]{1,0:T(8,128)(2,1)S(1)} %get-tuple-element.101), channel_id=1, source_target_pairs={{3,0},{2,1},{1,2},{0,3},{7,4},{6,5},{5,6},{4,7},{11,8},{10,9},{9,1... | collective-permute-start | bytes 153608 | tf_op jit(solution)/shard_map/ppermute | solution.py:111
  91.2 0.7 collective-permute-done.27
  91.9 3.0 %collective-permute-done.28 = bf16[8,3200]{1,0:T(8,128)(2,1)S(1)} collective-permute-done((bf16[8,3200]{1,0:T(8,128)(2,1)S(1)}, bf16[8,3200]{1,0:T(8,128)(2,1)S(1)}, u32[]{:S(2)}, u32[]{:S(2)}) %collective-permute-start.28) | collective-permute-done | bytes 51232 | tf_op jit(solution)/shard_map/ppermute | solution.py:111
  95.2 0.6 pad_maximum_fusion.14
  95.8 0.9 fusion.3
  (105 shorter events, 7.4 us)
Async XLA Ops:
  0.6 8.1 %copy-start = (bf16[6144,4]{0,1:T(4,128)(2,1)S(1)}, bf16[6144,4]{0,1:T(4,128)(2,1)}, u32[]{:S(2)}) copy-start(bf16[6144,4]{0,1:T(4,128)(2,1)} %param.12) | copy-start | bytes 147460
  0.6 16.9 %copy-start.1 = (bf16[8,6144]{1,0:T(8,128)(2,1)S(1)}, bf16[8,6144]{1,0:T(8,128)(2,1)}, u32[]{:S(2)}) copy-start(bf16[8,6144]{1,0:T(8,128)(2,1)} %param.9) | copy-start | bytes 294916
  0.7 9.4 %collective-permute-start = (bf16[8,6144]{1,0:T(8,128)(2,1)}, bf16[8,6144]{1,0:T(8,128)(2,1)S(1)}, u32[]{:S(2)}, u32[]{:S(2)}) collective-permute-start(bf16[8,6144]{1,0:T(8,128)(2,1)} %param.8), channel_id=1, source_target_pairs={{1,0},{0,1},{3,2},{2,3},{5,4},{4,5},{7,6},{6,7},{9,8},{8,9},{11,10... | collective-permute-start | bytes 294920 | tf_op jit(solution)/shard_map/ppermute | solution.py:111
  3.7 10.6 %collective-permute-start.4 = (bf16[8,6144]{1,0:T(8,128)(2,1)}, bf16[8,6144]{1,0:T(8,128)(2,1)S(1)}, u32[]{:S(2)}, u32[]{:S(2)}) collective-permute-start(bf16[8,6144]{1,0:T(8,128)(2,1)} %param.8), channel_id=1, source_target_pairs={{2,0},{3,1},{0,2},{1,3},{6,4},{7,5},{4,6},{5,7},{10,8},{11,9},{8,1... | collective-permute-start | bytes 294920 | tf_op jit(solution)/shard_map/ppermute | solution.py:111
  6.3 8.1 %collective-permute-start.5 = (bf16[8,6144]{1,0:T(8,128)(2,1)}, bf16[8,6144]{1,0:T(8,128)(2,1)S(1)}, u32[]{:S(2)}, u32[]{:S(2)}) collective-permute-start(bf16[8,6144]{1,0:T(8,128)(2,1)} %param.8), channel_id=1, source_target_pairs={{3,0},{2,1},{1,2},{0,3},{7,4},{6,5},{5,6},{4,7},{11,8},{10,9},{9,1... | collective-permute-start | bytes 294920 | tf_op jit(solution)/shard_map/ppermute | solution.py:111
  14.5 10.4 %collective-permute-start.6 = (bf16[32,3072]{1,0:T(8,128)(2,1)S(1)}, bf16[32,3072]{1,0:T(8,128)(2,1)S(1)}, u32[]{:S(2)}, u32[]{:S(2)}) collective-permute-start(bf16[32,3072]{1,0:T(8,128)(2,1)S(1)} %get-tuple-element.40._), channel_id=1, source_target_pairs={{16,0},{0,16},{17,1},{1,17},{18,2},{2,18},{19,3},{3,19},{20,4},{4,... | collective-permute-start | bytes 589832 | tf_op jit(solution)/shard_map/ppermute | solution.py:111
  16.0 8.8 %collective-permute-start.7 = (bf16[32,3072]{1,0:T(8,128)(2,1)S(1)}, bf16[32,3072]{1,0:T(8,128)(2,1)S(1)}, u32[]{:S(2)}, u32[]{:S(2)}) collective-permute-start(bf16[32,3072]{1,0:T(8,128)(2,1)S(1)} %get-tuple-element.42), channel_id=1, source_target_pairs={{8,0},{12,4},{0,8},{4,12},{9,1},{13,5},{1,9},{5,13},{10,2},{14,6},... | collective-permute-start | bytes 589832 | tf_op jit(solution)/shard_map/ppermute | solution.py:111
  17.6 8.5 %collective-permute-start.1 = (bf16[8,6272]{1,0:T(8,128)(2,1)S(1)}, bf16[8,6272]{1,0:T(8,128)(2,1)S(1)}, u32[]{:S(2)}, u32[]{:S(2)}) collective-permute-start(bf16[8,6272]{1,0:T(8,128)(2,1)S(1)} %fusion.4), channel_id=1, source_target_pairs={{1,0},{0,1},{3,2},{2,3},{5,4},{4,5},{7,6},{6,7},{9,8},{8,9},{11,10... | collective-permute-start | bytes 301064 | tf_op jit(solution)/shard_map/ppermute | solution.py:111
  19.2 8.9 %collective-permute-start.2 = (bf16[8,6272]{1,0:T(8,128)(2,1)S(1)}, bf16[8,6272]{1,0:T(8,128)(2,1)S(1)}, u32[]{:S(2)}, u32[]{:S(2)}) collective-permute-start(bf16[8,6272]{1,0:T(8,128)(2,1)S(1)} %fusion.4), channel_id=1, source_target_pairs={{2,0},{3,1},{0,2},{1,3},{6,4},{7,5},{4,6},{5,7},{10,8},{11,9},{8,1... | collective-permute-start | bytes 301064 | tf_op jit(solution)/shard_map/ppermute | solution.py:111
  20.6 7.4 %collective-permute-start.3 = (bf16[8,6272]{1,0:T(8,128)(2,1)S(1)}, bf16[8,6272]{1,0:T(8,128)(2,1)S(1)}, u32[]{:S(2)}, u32[]{:S(2)}) collective-permute-start(bf16[8,6272]{1,0:T(8,128)(2,1)S(1)} %fusion.4), channel_id=1, source_target_pairs={{3,0},{2,1},{1,2},{0,3},{7,4},{6,5},{5,6},{4,7},{11,8},{10,9},{9,1... | collective-permute-start | bytes 301064 | tf_op jit(solution)/shard_map/ppermute | solution.py:111
  24.9 10.5 %collective-permute-start.11 = (bf16[64,3072]{1,0:T(8,128)(2,1)S(1)}, bf16[64,3072]{1,0:T(8,128)(2,1)S(1)}, u32[]{:S(2)}, u32[]{:S(2)}) collective-permute-start(bf16[64,3072]{1,0:T(8,128)(2,1)S(1)} %pad_maximum_fusion.10), channel_id=1, source_target_pairs={{16,0},{0,16},{17,1},{1,17},{18,2},{2,18},{19,3},{3,19},{20,4},{4,... | collective-permute-start | bytes 1179656 | tf_op jit(solution)/shard_map/ppermute | solution.py:111
  25.5 10.1 %collective-permute-start.10 = (bf16[64,3072]{1,0:T(8,128)(2,1)S(1)}, bf16[64,3072]{1,0:T(8,128)(2,1)S(1)}, u32[]{:S(2)}, u32[]{:S(2)}) collective-permute-start(bf16[64,3072]{1,0:T(8,128)(2,1)S(1)} %pad_maximum_fusion.9), channel_id=1, source_target_pairs={{8,0},{12,4},{0,8},{4,12},{9,1},{13,5},{1,9},{5,13},{10,2},{14,6},... | collective-permute-start | bytes 1179656 | tf_op jit(solution)/shard_map/ppermute | solution.py:111
  31.0 6.7 %collective-permute-start.9 = (bf16[32,3072]{1,0:T(8,128)(2,1)S(1)}, bf16[32,3072]{1,0:T(8,128)(2,1)S(1)}, u32[]{:S(2)}, u32[]{:S(2)}) collective-permute-start(bf16[32,3072]{1,0:T(8,128)(2,1)S(1)} %get-tuple-element.50), channel_id=1, source_target_pairs={{8,0},{12,4},{0,8},{4,12},{9,1},{13,5},{1,9},{5,13},{10,2},{14,6},... | collective-permute-start | bytes 589832 | tf_op jit(solution)/shard_map/ppermute | solution.py:111
  31.6 6.1 %collective-permute-start.8 = (bf16[32,3200]{1,0:T(8,128)(2,1)S(1)}, bf16[32,3200]{1,0:T(8,128)(2,1)S(1)}, u32[]{:S(2)}, u32[]{:S(2)}) collective-permute-start(bf16[32,3200]{1,0:T(8,128)(2,1)S(1)} %slice.98), channel_id=1, source_target_pairs={{16,0},{0,16},{17,1},{1,17},{18,2},{2,18},{19,3},{3,19},{20,4},{4,... | collective-permute-start | bytes 614408 | tf_op jit(solution)/shard_map/ppermute | solution.py:111
  35.7 4.3 %collective-permute-start.15 = (bf16[128,3072]{1,0:T(8,128)(2,1)S(1)}, bf16[128,3072]{1,0:T(8,128)(2,1)S(1)}, u32[]{:S(2)}, u32[]{:S(2)}) collective-permute-start(bf16[128,3072]{1,0:T(8,128)(2,1)S(1)} %pad_maximum_fusion.4), channel_id=1, source_target_pairs={{4,0},{0,4},{12,8},{8,12},{5,1},{1,5},{13,9},{9,13},{6,2},{2,6},{1... | collective-permute-start | bytes 2359304 | tf_op jit(solution)/shard_map/ppermute | solution.py:111
  35.9 4.2 %collective-permute-start.14 = (bf16[128,3072]{1,0:T(8,128)(2,1)S(1)}, bf16[128,3072]{1,0:T(8,128)(2,1)S(1)}, u32[]{:S(2)}, u32[]{:S(2)}) collective-permute-start(bf16[128,3072]{1,0:T(8,128)(2,1)S(1)} %pad_maximum_fusion.3), channel_id=1, source_target_pairs={{4,0},{0,4},{12,8},{8,12},{5,1},{1,5},{13,9},{9,13},{6,2},{2,6},{1... | collective-permute-start | bytes 2359304 | tf_op jit(solution)/shard_map/ppermute | solution.py:111
  37.8 9.8 %collective-permute-start.13 = (bf16[64,3072]{1,0:T(8,128)(2,1)S(1)}, bf16[64,3072]{1,0:T(8,128)(2,1)S(1)}, u32[]{:S(2)}, u32[]{:S(2)}) collective-permute-start(bf16[64,3072]{1,0:T(8,128)(2,1)S(1)} %pad_maximum_fusion.11), channel_id=1, source_target_pairs={{16,0},{0,16},{17,1},{1,17},{18,2},{2,18},{19,3},{3,19},{20,4},{4,... | collective-permute-start | bytes 1179656 | tf_op jit(solution)/shard_map/ppermute | solution.py:111
  39.3 9.9 %collective-permute-start.12 = (bf16[64,3200]{1,0:T(8,128)(2,1)S(1)}, bf16[64,3200]{1,0:T(8,128)(2,1)S(1)}, u32[]{:S(2)}, u32[]{:S(2)}) collective-permute-start(bf16[64,3200]{1,0:T(8,128)(2,1)S(1)} %pad_maximum_fusion.7), channel_id=1, source_target_pairs={{8,0},{12,4},{0,8},{4,12},{9,1},{13,5},{1,9},{5,13},{10,2},{14,6},... | collective-permute-start | bytes 1228808 | tf_op jit(solution)/shard_map/ppermute | solution.py:111
  49.4 3.5 %collective-permute-start.17 = (bf16[128,3072]{1,0:T(8,128)(2,1)S(1)}, bf16[128,3072]{1,0:T(8,128)(2,1)S(1)}, u32[]{:S(2)}, u32[]{:S(2)}) collective-permute-start(bf16[128,3072]{1,0:T(8,128)(2,1)S(1)} %pad_maximum_fusion.5), channel_id=1, source_target_pairs={{4,0},{0,4},{12,8},{8,12},{5,1},{1,5},{13,9},{9,13},{6,2},{2,6},{1... | collective-permute-start | bytes 2359304 | tf_op jit(solution)/shard_map/ppermute | solution.py:111
  49.5 3.5 %collective-permute-start.16 = (bf16[128,3200]{1,0:T(8,128)(2,1)S(1)}, bf16[128,3200]{1,0:T(8,128)(2,1)S(1)}, u32[]{:S(2)}, u32[]{:S(2)}) collective-permute-start(bf16[128,3200]{1,0:T(8,128)(2,1)S(1)} %pad_maximum_fusion.2), channel_id=1, source_target_pairs={{4,0},{0,4},{12,8},{8,12},{5,1},{1,5},{13,9},{9,13},{6,2},{2,6},{1... | collective-permute-start | bytes 2457608 | tf_op jit(solution)/shard_map/ppermute | solution.py:111
  61.7 4.5 %collective-permute-start.21 = (bf16[128,3072]{1,0:T(8,128)(2,1)S(1)}, bf16[128,3072]{1,0:T(8,128)(2,1)S(1)}, u32[]{:S(2)}, u32[]{:S(2)}) collective-permute-start(bf16[128,3072]{1,0:T(8,128)(2,1)S(1)} %get-tuple-element.70), channel_id=1, source_target_pairs={{4,0},{0,4},{12,8},{8,12},{5,1},{1,5},{13,9},{9,13},{6,2},{2,6},{1... | collective-permute-start | bytes 2359304 | tf_op jit(solution)/shard_map/ppermute | solution.py:111
  65.6 2.5 %collective-permute-start.18 = (bf16[128,3200]{1,0:T(8,128)(2,1)S(1)}, bf16[128,3200]{1,0:T(8,128)(2,1)S(1)}, u32[]{:S(2)}, u32[]{:S(2)}) collective-permute-start(bf16[128,3200]{1,0:T(8,128)(2,1)S(1)} %get-tuple-element.69), channel_id=1, source_target_pairs={{4,0},{0,4},{12,8},{8,12},{5,1},{1,5},{13,9},{9,13},{6,2},{2,6},{1... | collective-permute-start | bytes 2457608 | tf_op jit(solution)/shard_map/ppermute | solution.py:111
  66.5 7.8 %collective-permute-start.25 = (bf16[64,1536]{1,0:T(8,128)(2,1)S(1)}, bf16[64,1536]{1,0:T(8,128)(2,1)S(1)}, u32[]{:S(2)}, u32[]{:S(2)}) collective-permute-start(bf16[64,1536]{1,0:T(8,128)(2,1)S(1)} %pad_maximum_fusion.13), channel_id=1, source_target_pairs={{16,0},{0,16},{17,1},{1,17},{18,2},{2,18},{19,3},{3,19},{20,4},{4,... | collective-permute-start | bytes 589832 | tf_op jit(solution)/shard_map/ppermute | solution.py:111
  67.1 7.9 %collective-permute-start.24 = (bf16[64,1536]{1,0:T(8,128)(2,1)S(1)}, bf16[64,1536]{1,0:T(8,128)(2,1)S(1)}, u32[]{:S(2)}, u32[]{:S(2)}) collective-permute-start(bf16[64,1536]{1,0:T(8,128)(2,1)S(1)} %concatenate.112), channel_id=1, source_target_pairs={{8,0},{12,4},{0,8},{4,12},{9,1},{13,5},{1,9},{5,13},{10,2},{14,6},... | collective-permute-start | bytes 589832 | tf_op jit(solution)/shard_map/ppermute | solution.py:111
  68.5 10.5 %collective-permute-start.20 = (bf16[64,1664]{1,0:T(8,128)(2,1)S(1)}, bf16[64,1664]{1,0:T(8,128)(2,1)S(1)}, u32[]{:S(2)}, u32[]{:S(2)}) collective-permute-start(bf16[64,1664]{1,0:T(8,128)(2,1)S(1)} %pad_maximum_fusion.12), channel_id=1, source_target_pairs={{16,0},{0,16},{17,1},{1,17},{18,2},{2,18},{19,3},{3,19},{20,4},{4,... | collective-permute-start | bytes 638984 | tf_op jit(solution)/shard_map/ppermute | solution.py:111
  69.6 9.4 %collective-permute-start.19 = (bf16[64,1536]{1,0:T(8,128)(2,1)S(1)}, bf16[64,1536]{1,0:T(8,128)(2,1)S(1)}, u32[]{:S(2)}, u32[]{:S(2)}) collective-permute-start(bf16[64,1536]{1,0:T(8,128)(2,1)S(1)} %concatenate.110), channel_id=1, source_target_pairs={{8,0},{12,4},{0,8},{4,12},{9,1},{13,5},{1,9},{5,13},{10,2},{14,6},... | collective-permute-start | bytes 589832 | tf_op jit(solution)/shard_map/ppermute | solution.py:111
  74.4 6.8 %collective-permute-start.30 = (bf16[32,1536]{1,0:T(8,128)(2,1)S(1)}, bf16[32,1536]{1,0:T(8,128)(2,1)S(1)}, u32[]{:S(2)}, u32[]{:S(2)}) collective-permute-start(bf16[32,1536]{1,0:T(8,128)(2,1)S(1)} %split.121), channel_id=1, source_target_pairs={{8,0},{12,4},{0,8},{4,12},{9,1},{13,5},{1,9},{5,13},{10,2},{14,6},... | collective-permute-start | bytes 294920 | tf_op jit(solution)/shard_map/ppermute | solution.py:111
  75.0 6.2 %collective-permute-start.29 = (bf16[32,1536]{1,0:T(8,128)(2,1)S(1)}, bf16[32,1536]{1,0:T(8,128)(2,1)S(1)}, u32[]{:S(2)}, u32[]{:S(2)}) collective-permute-start(bf16[32,1536]{1,0:T(8,128)(2,1)S(1)} %split.122), channel_id=1, source_target_pairs={{16,0},{0,16},{17,1},{1,17},{18,2},{2,18},{19,3},{3,19},{20,4},{4,... | collective-permute-start | bytes 294920 | tf_op jit(solution)/shard_map/ppermute | solution.py:111
  79.0 6.7 %collective-permute-start.22 = (bf16[32,1536]{1,0:T(8,128)(2,1)S(1)}, bf16[32,1536]{1,0:T(8,128)(2,1)S(1)}, u32[]{:S(2)}, u32[]{:S(2)}) collective-permute-start(bf16[32,1536]{1,0:T(8,128)(2,1)S(1)} %split.123), channel_id=1, source_target_pairs={{16,0},{0,16},{17,1},{1,17},{18,2},{2,18},{19,3},{3,19},{20,4},{4,... | collective-permute-start | bytes 294920 | tf_op jit(solution)/shard_map/ppermute | solution.py:111
  80.6 5.2 %collective-permute-start.23 = (bf16[32,1664]{1,0:T(8,128)(2,1)S(1)}, bf16[32,1664]{1,0:T(8,128)(2,1)S(1)}, u32[]{:S(2)}, u32[]{:S(2)}) collective-permute-start(bf16[32,1664]{1,0:T(8,128)(2,1)S(1)} %split.120), channel_id=1, source_target_pairs={{8,0},{12,4},{0,8},{4,12},{9,1},{13,5},{1,9},{5,13},{10,2},{14,6},... | collective-permute-start | bytes 319496 | tf_op jit(solution)/shard_map/ppermute | solution.py:111
  81.3 7.7 %collective-permute-start.31 = (bf16[8,3072]{1,0:T(8,128)(2,1)S(1)}, bf16[8,3072]{1,0:T(8,128)(2,1)S(1)}, u32[]{:S(2)}, u32[]{:S(2)}) collective-permute-start(bf16[8,3072]{1,0:T(8,128)(2,1)S(1)} %get-tuple-element.103), channel_id=1, source_target_pairs={{1,0},{0,1},{3,2},{2,3},{5,4},{4,5},{7,6},{6,7},{9,8},{8,9},{11,10... | collective-permute-start | bytes 147464 | tf_op jit(solution)/shard_map/ppermute | solution.py:111
  82.3 8.1 %collective-permute-start.32 = (bf16[8,3072]{1,0:T(8,128)(2,1)S(1)}, bf16[8,3072]{1,0:T(8,128)(2,1)S(1)}, u32[]{:S(2)}, u32[]{:S(2)}) collective-permute-start(bf16[8,3072]{1,0:T(8,128)(2,1)S(1)} %get-tuple-element.105), channel_id=1, source_target_pairs={{2,0},{3,1},{0,2},{1,3},{6,4},{7,5},{4,6},{5,7},{10,8},{11,9},{8,1... | collective-permute-start | bytes 147464 | tf_op jit(solution)/shard_map/ppermute | solution.py:111
  84.4 6.3 %collective-permute-start.33 = (bf16[8,3072]{1,0:T(8,128)(2,1)S(1)}, bf16[8,3072]{1,0:T(8,128)(2,1)S(1)}, u32[]{:S(2)}, u32[]{:S(2)}) collective-permute-start(bf16[8,3072]{1,0:T(8,128)(2,1)S(1)} %get-tuple-element.104), channel_id=1, source_target_pairs={{3,0},{2,1},{1,2},{0,3},{7,4},{6,5},{5,6},{4,7},{11,8},{10,9},{9,1... | collective-permute-start | bytes 147464 | tf_op jit(solution)/shard_map/ppermute | solution.py:111
  85.8 9.3 %copy-start.2 = (s32[8]{0:T(128)S(1)}, s32[8]{0:T(128)}, u32[]{:S(2)}) copy-start(s32[8]{0:T(128)} %param.10) | copy-start | bytes 100
  85.9 5.3 %collective-permute-start.26 = (bf16[8,3200]{1,0:T(8,128)(2,1)S(1)}, bf16[8,3200]{1,0:T(8,128)(2,1)S(1)}, u32[]{:S(2)}, u32[]{:S(2)}) collective-permute-start(bf16[8,3200]{1,0:T(8,128)(2,1)S(1)} %get-tuple-element.100), channel_id=1, source_target_pairs={{1,0},{0,1},{3,2},{2,3},{5,4},{4,5},{7,6},{6,7},{9,8},{8,9},{11,10... | collective-permute-start | bytes 153608 | tf_op jit(solution)/shard_map/ppermute | solution.py:111
  86.5 5.4 %collective-permute-start.27 = (bf16[8,3200]{1,0:T(8,128)(2,1)S(1)}, bf16[8,3200]{1,0:T(8,128)(2,1)S(1)}, u32[]{:S(2)}, u32[]{:S(2)}) collective-permute-start(bf16[8,3200]{1,0:T(8,128)(2,1)S(1)} %get-tuple-element.102), channel_id=1, source_target_pairs={{2,0},{3,1},{0,2},{1,3},{6,4},{7,5},{4,6},{5,7},{10,8},{11,9},{8,1... | collective-permute-start | bytes 153608 | tf_op jit(solution)/shard_map/ppermute | solution.py:111
  89.0 5.9 %collective-permute-start.28 = (bf16[8,3200]{1,0:T(8,128)(2,1)S(1)}, bf16[8,3200]{1,0:T(8,128)(2,1)S(1)}, u32[]{:S(2)}, u32[]{:S(2)}) collective-permute-start(bf16[8,3200]{1,0:T(8,128)(2,1)S(1)} %get-tuple-element.101), channel_id=1, source_target_pairs={{3,0},{2,1},{1,2},{0,3},{7,4},{6,5},{5,6},{4,7},{11,8},{10,9},{9,1... | collective-permute-start | bytes 153608 | tf_op jit(solution)/shard_map/ppermute | solution.py:111

commit v14 on v13

--- a/solution.py
+++ b/solution.py
@@ -220,6 +220,44 @@
     )(earlier, *[in_hbm(value) for value in weights])
 
 
+def first_token_kernel(sources, tokens, gate, gate_weight, up_weight, pre_gate, pre_up, up, gate_next, up_next, sems):
+    copies = []
+    for index, (weight, fetched) in enumerate(((up_weight, up), (gate_weight, gate_next), (up_weight, up_next))):
+        source = weight.at[0, pl.ds(sources[index], fetched.shape[0])]
+        copies.append(pltpu.make_async_copy(source, fetched, sems.at[index]))
+    for copy in copies:
+        copy.start()
+    depth = part_of(tokens.shape[1], TOKEN_PART)
+    for sums, weight in ((pre_gate, gate), (pre_up, up)):
+        sums[...] = jnp.zeros_like(sums)
+        if weight is up:
+            copies[0].wait()
+
+        @pl.loop(0, tokens.shape[1] // depth)
+        def _(step):
+            rows = pl.ds(pl.multiple_of(step * depth, depth), depth)
+            sums[...] += product(tokens[:, rows], weight[rows, :], 0)
+
+    for copy in copies[1:]:
+        copy.wait()
+
+
+def multiply_first_tokens(tokens, gate, gate_weight, up_weight):
+    rows, length = tokens.shape
+    hidden = gate.shape[1]
+    return pl.pallas_call(
+        functools.partial(first_token_kernel, (0, length, length)),
+        out_shape=(pltpu.VMEM((rows, hidden), jnp.float32),) * 2 + (pltpu.VMEM(gate.shape, jnp.bfloat16),) * 3,
+        in_specs=[pl.BlockSpec(memory_space=pltpu.VMEM)] * 2 + [pl.BlockSpec(memory_space=pl.ANY)] * 2,
+        out_specs=(pl.BlockSpec(memory_space=pltpu.VMEM),) * 5,
+        scratch_shapes=[pltpu.SemaphoreType.DMA((3,))],
+        compiler_params=pltpu.CompilerParams(vmem_limit_bytes=TOKEN_VMEM),
+        cost_estimate=pl.CostEstimate(
+            flops=4 * rows * length * hidden, bytes_accessed=6 * length * hidden, transcendentals=0
+        ),
+    )(tokens, gate, in_hbm(gate_weight), in_hbm(up_weight))
+
+
 def token_kernel(offset, length, sources, summed, tokens, gate, up, *refs):
     before, refs = refs[:summed], refs[summed:]
     count = len(sources)
@@ -394,19 +432,15 @@
     gate_second = jax.nn.sigmoid(second_logit - first_logit)
     gate_table = (first_hot * gate_first[:, None] + second_hot * gate_second[:, None]) * keep_rows[:, None]
     gate_table = jnp.pad(gate_table.astype(jnp.bfloat16), ((0, 0), (0, table - expert_count)))
-    grad_z = gather_z(after_others(jnp.concatenate([gate_table, out_grad], axis=1), token_z[1]))
-    token_near = gather_near(token_z, half)
-    (gate_low,) = fetch(0, half, token_near[0][0], gate_weight)
-    token_near = after_others(token_near, gate_low)
+    grad_rows = jnp.concatenate([gate_table, out_grad], axis=1)
+    (gate_low,) = fetch(0, half, grad_rows, gate_weight)
+    grad_z = gather_z(after_others(grad_rows, token_z[1]))
+    token_near = lax.optimization_barrier(gather_near(after_others(token_z, gate_low), half))
     token_far = gather_far(*token_near)
-    (up_low,) = fetch(0, half, token_near[1][1], up_weight)
     grad_near = gather_near(after_others(grad_z, token_near), half + table)
     grad_far = gather_far(*after_others(grad_near, token_far))
-    token_far = after_others(token_far, up_low)
     token_low, token_high = gather_core(token_near[0], token_far[0], token_near[1], token_far[1])
-    pre_gate, pre_up, gate_high, up_high = multiply_tokens(
-        token_low, gate_low, up_low, 0, half, (), ((gate_weight, half, half), (up_weight, half, half))
-    )
+    pre_gate, pre_up, up_low, gate_high, up_high = multiply_first_tokens(token_low, gate_low, gate_weight, up_weight)
     pre_gate, pre_up = multiply_tokens(token_high, gate_high, up_high, 0, quarter, (pre_gate, pre_up))
     grad_far = after_others(grad_far, pre_gate)
     pre_gate, pre_up, down = multiply_tokens(

time: 97 us -> 97.9 us (level)
  waiting for transfers between devices: 24 us -> 21.5 us
  local copies, waits for them, and re-layouts: 2.36 us -> 4.08 us
  starting transfers between devices: 36.3 us -> 37.9 us
  Pallas kernels: 27.7 us -> 26.7 us
    pallas_call x0 -> x1, Pallas kernels: none -> 6.43 us  [multiply_first_tokens(): pl.pallas_call(functools.partial(first_token_kernel, (0, length, length))...]
    pallas_call x3 -> x2, Pallas kernels: 9.74 us -> 5.09 us  [multiply_tokens(): pl.pallas_call(functools.partial(token_kernel, offset, length, sources, l...]
    pallas_call x2 -> x1, Pallas kernels: 5.59 us -> 2.83 us  [fetch(): pl.pallas_call(functools.partial(fetch_kernel, first), out_shape=tuple((p...]
    ppermute x34, waiting for transfers between devices: 24 us -> 21.5 us  [swap(): lax.ppermute(value, axis, [(i ^ bit, i) for i in range(lax.axis_size(axis...]
    unnamed x18 -> x24, local copies, waits for them, and re-layouts: 1.14 us -> 2.86 us
    ppermute x34, starting transfers between devices: 36.3 us -> 37.9 us  [swap(): lax.ppermute(value, axis, [(i ^ bit, i) for i in range(lax.axis_size(axis...]
  transfers between devices with their start and end apart: 34 -> 34, of which waited for: 14 -> 12; matrix products, arithmetic and copies ran while one was open for 6% -> 6% of each run, Pallas kernels for 20% -> 19%
where the time goes in v14:
time: 97.9 us; the launch traced here: 97.6 us
  starting transfers between devices  37.9 us (39%)
  Pallas kernels  26.7 us (27%)
  waiting for transfers between devices  21.5 us (22%)
  local copies, waits for them, and re-layouts  4.08 us (4%)
  other arithmetic  3.94 us (4%)
  matrix products  2.15 us (2%)
  between operations  1.28 us (1%)
    ppermute x34, starting transfers between devices, swap(): lax.ppermute(value, axis, [(i ^ bit, i) for i in range(lax.axis_size(axis...  37.9 us
    ppermute x34, waiting for transfers between devices, swap(): lax.ppermute(value, axis, [(i ^ bit, i) for i in range(lax.axis_size(axis...  21.5 us
    pallas_call x2, Pallas kernels, multiply_outputs(): pl.pallas_call(output_kernel, out_shape=(pltpu.VMEM((rows // 2, total), j...  7.66 us
    pallas_call x1, Pallas kernels, multiply_first_tokens(): pl.pallas_call(functools.partial(first_token_kernel, (0, length, length))...  6.43 us
    pallas_call x2, Pallas kernels, multiply_tokens(): pl.pallas_call(functools.partial(token_kernel, offset, length, sources, l...  5.09 us
    pallas_call x1, Pallas kernels, multiply_grads(): pl.pallas_call(grad_kernel, out_shape=(pltpu.VMEM((rows, hidden), jnp.bfl...  4.73 us
    unnamed x24, local copies, waits for them, and re-layouts  2.86 us
    pallas_call x1, Pallas kernels, fetch(): pl.pallas_call(functools.partial(fetch_kernel, first), out_shape=tuple((p...  2.83 us
  transfers between devices with their start and end apart: 34, of which 12 were waited for; matrix products, arithmetic and copies ran while one was open for 6% of the time, Pallas kernels for 19%

profile of v14, /device:TPU:0, one launch (start us, length us, event | category | flops | bytes accessed | tf_op | source)
XLA Modules:
  0.0 97.6 jit_solution(3037344705629746684)
XLA Ops:
  0.6 3.1 %collective-permute-start = (bf16[8,6144]{1,0:T(8,128)(2,1)}, bf16[8,6144]{1,0:T(8,128)(2,1)S(1)}, u32[]{:S(2)}, u32[]{:S(2)}) collective-permute-start(bf16[8,6144]{1,0:T(8,128)(2,1)} %param.8), channel_id=1, source_target_pairs={{1,0},{0,1},{3,2},{2,3},{5,4},{4,5},{7,6},{6,7},{9,8},{8,9},{11,10... | collective-permute-start | bytes 294920 | tf_op jit(solution)/shard_map/ppermute | solution.py:111
  3.7 2.6 %collective-permute-start.4 = (bf16[8,6144]{1,0:T(8,128)(2,1)}, bf16[8,6144]{1,0:T(8,128)(2,1)S(1)}, u32[]{:S(2)}, u32[]{:S(2)}) collective-permute-start(bf16[8,6144]{1,0:T(8,128)(2,1)} %param.8), channel_id=1, source_target_pairs={{2,0},{3,1},{0,2},{1,3},{6,4},{7,5},{4,6},{5,7},{10,8},{11,9},{8,1... | collective-permute-start | bytes 294920 | tf_op jit(solution)/shard_map/ppermute | solution.py:111
  6.3 0.8 slice_bitcast_fusion
  7.1 0.7 convert_element_type.76
  7.7 1.2 %select_reduce_fusion.3 = (f32[8]{0:T(128)S(1)}, f32[8]{0:T(128)S(1)}) fusion(s32[8]{0:T(128)S(1)} %get-tuple-element.117, s32[8]{0:T(128)S(1)} %get-tuple-element.116, bf16[8,6144]{1,0:T(8,128)(2,1)} %param.8, bf16[6144,4]{0,1:T(4,128)(2,1)S(1)} %copy-done), kind=kOutput, calls=%fused_computation.69 | convolution fusion | flops 393392 | bytes 147584 | tf_op jit(solution)/shard_map/dot_general | solution.py:428
  9.1 0.9 fusion.4._
  10.0 2.8 %shard_map.95.gate.gate_copy = bf16[3072,1024]{1,0:T(8,128)(2,1)S(1)} custom-call(bf16[8,6272]{1,0:T(8,128)(2,1)S(1)} %fusion.4._, bf16[1,6144,1024]{2,1,0:T(8,128)(2,1)} %gate_weight.1), custom_call_target="tpu_custom_call" | custom-call | bytes 6291456 | tf_op jit(solution)/shard_map/pallas_call | solution.py:210
  12.8 2.7 %copy-done.1 = bf16[3072,1024]{1,0:T(8,128)(2,1)} copy-done((bf16[3072,1024]{1,0:T(8,128)(2,1)}, bf16[3072,1024]{1,0:T(8,128)(2,1)S(1)}, u32[]{:S(2)}) %copy-start.1) | copy-done | bytes 6291480
  15.6 1.8 %collective-permute-start.6 = (bf16[32,3072]{1,0:T(8,128)(2,1)S(1)}, bf16[32,3072]{1,0:T(8,128)(2,1)S(1)}, u32[]{:S(2)}, u32[]{:S(2)}) collective-permute-start(bf16[32,3072]{1,0:T(8,128)(2,1)S(1)} %get-tuple-element.47), channel_id=1, source_target_pairs={{16,0},{0,16},{17,1},{1,17},{18,2},{2,18},{19,3},{3,19},{20,4},{4,... | collective-permute-start | bytes 589832 | tf_op jit(solution)/shard_map/ppermute | solution.py:111
  17.4 1.5 %collective-permute-start.7 = (bf16[32,3072]{1,0:T(8,128)(2,1)S(1)}, bf16[32,3072]{1,0:T(8,128)(2,1)S(1)}, u32[]{:S(2)}, u32[]{:S(2)}) collective-permute-start(bf16[32,3072]{1,0:T(8,128)(2,1)S(1)} %get-tuple-element.49), channel_id=1, source_target_pairs={{8,0},{12,4},{0,8},{4,12},{9,1},{13,5},{1,9},{5,13},{10,2},{14,6},... | collective-permute-start | bytes 589832 | tf_op jit(solution)/shard_map/ppermute | solution.py:111
  18.9 0.7 collective-permute-start.1
  19.6 3.5 %collective-permute-start.2 = (bf16[8,6272]{1,0:T(8,128)(2,1)S(1)}, bf16[8,6272]{1,0:T(8,128)(2,1)S(1)}, u32[]{:S(2)}, u32[]{:S(2)}) collective-permute-start(bf16[8,6272]{1,0:T(8,128)(2,1)S(1)} %fusion.4._), channel_id=1, source_target_pairs={{2,0},{3,1},{0,2},{1,3},{6,4},{7,5},{4,6},{5,7},{10,8},{11,9},{8,1... | collective-permute-start | bytes 301064 | tf_op jit(solution)/shard_map/ppermute | solution.py:111
  23.3 1.3 %collective-permute-start.10 = (bf16[64,3072]{1,0:T(8,128)(2,1)S(1)}, bf16[64,3072]{1,0:T(8,128)(2,1)S(1)}, u32[]{:S(2)}, u32[]{:S(2)}) collective-permute-start(bf16[64,3072]{1,0:T(8,128)(2,1)S(1)} %pad_maximum_fusion.9), channel_id=1, source_target_pairs={{8,0},{12,4},{0,8},{4,12},{9,1},{13,5},{1,9},{5,13},{10,2},{14,6},... | collective-permute-start | bytes 1179656 | tf_op jit(solution)/shard_map/ppermute | solution.py:111
  24.7 0.6 collective-permute-start.11
  25.3 3.2 %collective-permute-done.2 = bf16[8,6272]{1,0:T(8,128)(2,1)S(1)} collective-permute-done((bf16[8,6272]{1,0:T(8,128)(2,1)S(1)}, bf16[8,6272]{1,0:T(8,128)(2,1)S(1)}, u32[]{:S(2)}, u32[]{:S(2)}) %collective-permute-start.2) | collective-permute-done | bytes 100384 | tf_op jit(solution)/shard_map/ppermute | solution.py:111
  28.5 1.1 %collective-permute-done.3 = bf16[8,6272]{1,0:T(8,128)(2,1)S(1)} collective-permute-done((bf16[8,6272]{1,0:T(8,128)(2,1)S(1)}, bf16[8,6272]{1,0:T(8,128)(2,1)S(1)}, u32[]{:S(2)}, u32[]{:S(2)}) %collective-permute-start.3) | collective-permute-done | bytes 100384 | tf_op jit(solution)/shard_map/ppermute | solution.py:111
  29.8 0.6 collective-permute-start.9
  30.9 3.2 %collective-permute-done.10 = bf16[64,3072]{1,0:T(8,128)(2,1)S(1)} collective-permute-done((bf16[64,3072]{1,0:T(8,128)(2,1)S(1)}, bf16[64,3072]{1,0:T(8,128)(2,1)S(1)}, u32[]{:S(2)}, u32[]{:S(2)}) %collective-permute-start.10) | collective-permute-done | bytes 393248 | tf_op jit(solution)/shard_map/ppermute | solution.py:111
  34.2 1.4 %collective-permute-done.11 = bf16[64,3072]{1,0:T(8,128)(2,1)S(1)} collective-permute-done((bf16[64,3072]{1,0:T(8,128)(2,1)S(1)}, bf16[64,3072]{1,0:T(8,128)(2,1)S(1)}, u32[]{:S(2)}, u32[]{:S(2)}) %collective-permute-start.11) | collective-permute-done | bytes 393248 | tf_op jit(solution)/shard_map/ppermute | solution.py:111
  36.3 1.5 %collective-permute-done.8 = bf16[32,3200]{1,0:T(8,128)(2,1)S(1)} collective-permute-done((bf16[32,3200]{1,0:T(8,128)(2,1)S(1)}, bf16[32,3200]{1,0:T(8,128)(2,1)S(1)}, u32[]{:S(2)}, u32[]{:S(2)}) %collective-permute-start.8) | collective-permute-done | bytes 204832 | tf_op jit(solution)/shard_map/ppermute | solution.py:111
  37.8 0.6 collective-permute-start.13
  38.5 0.6 collective-permute-start.12
  39.4 6.4 %shard_map.96 = (f32[256,1024]{1,0:T(8,128)S(1)}, f32[256,1024]{1,0:T(8,128)S(1)}, bf16[3072,1024]{1,0:T(8,128)(2,1)S(1)}, bf16[3072,1024]{1,0:T(8,128)(2,1)S(1)}, bf16[3072,1024]{1,0:T(8,128)(2,1)S(1)}) custom-call(bf16[256,3072]{1,0:T(8,128)(2,1)S(1)} %pad_maximum_fusion.1.tokens, bf16[3072,1024]{1,0:T(8,128)(2,1)S(1)} %bitcast.11, ...), custom_call_target="tpu_custom_call" | custom-call | flops 3221225472 | bytes 18874368 | tf_op jit(solution)/shard_map/pallas_call | solution.py:248
  45.8 2.3 %shard_map.97 = (f32[256,1024]{1,0:T(8,128)S(1)}, f32[256,1024]{1,0:T(8,128)S(1)}) custom-call(bf16[256,3072]{1,0:T(8,128)(2,1)S(1)} %constant_dynamic-update-slice_fusion.8.tokens, bf16[3072,1024]{1,0:T(8,128)(2,1)S(1)} %get-tuple-element.59.gate.gate_copy, bf16[3072,1024]{1,0:T(8,128)(2,1)S(1)} %get-tuple-element.60.up.up_copy, ...), custom_call_target="tpu_custom_call" | custom-call | flops 1610612736 | bytes 786432 | tf_op jit(solution)/shard_map/pallas_call | solution.py:291
  48.4 0.6 collective-permute-start.16
  49.0 2.8 %shard_map.98 = (f32[256,1024]{1,0:T(8,128)S(1)}, f32[256,1024]{1,0:T(8,128)S(1)}, bf16[512,6144]{1,0:T(8,128)(2,1)S(1)}) custom-call(bf16[256,3072]{1,0:T(8,128)(2,1)S(1)} %constant_dynamic-update-slice_fusion.8.tokens, bf16[3072,1024]{1,0:T(8,128)(2,1)S(1)} %get-tuple-element.59.gate.gate_copy, bf16[3072,1024]{1,0:T(8,128)(2,1)S(1)} %get-tuple-element.60.up.up_copy, ...), custom_call_target="tpu_custom_call" | custom-call | flops 1610612736 | bytes 786432 | tf_op jit(solution)/shard_map/pallas_call | solution.py:291
  52.1 4.7 %shard_map.99 = (bf16[256,1024]{1,0:T(8,128)(2,1)S(1)}, bf16[256,1024]{1,0:T(8,128)(2,1)S(1)}, bf16[256,128]{1,0:T(8,128)(2,1)S(1)}) custom-call(s32[1]{0:T(128)} %bitcast.expert, bf16[256,3200]{1,0:T(8,128)(2,1)S(1)} %pad_maximum_fusion.low, bf16[256,3072]{1,0:T(8,128)(2,1)S(1)} %constant_dynamic-update-slice_fusion.13.high, ...), custom_call_target="tpu_custom_call" | custom-call | flops 3221225472 | bytes 6291456 | tf_op jit(solution)/shard_map/pallas_call | solution.py:357
  56.8 3.8 %shard_map.101 = (f32[128,3072]{1,0:T(8,128)S(1)}, bf16[128,3072]{1,0:T(8,128)(2,1)S(1)}) custom-call(bf16[256,1024]{1,0:T(8,128)(2,1)S(1)} %get-tuple-element.70.grad_gate, bf16[256,1024]{1,0:T(8,128)(2,1)S(1)} %get-tuple-element.71.grad_up, bf16[3072,1024]{1,0:T(8,128)(2,1)S(1)} %get-tuple-element.59.gate.gate_copy, ...), custom_call_target="tpu_custom_call" | custom-call | flops 3221225472 | bytes 3145728 | tf_op jit(solution)/shard_map/pallas_call | solution.py:403
  60.7 3.8 %shard_map.100 = (f32[128,3200]{1,0:T(8,128)S(1)}, bf16[128,3200]{1,0:T(8,128)(2,1)S(1)}) custom-call(bf16[256,1024]{1,0:T(8,128)(2,1)S(1)} %get-tuple-element.70.grad_gate, bf16[256,1024]{1,0:T(8,128)(2,1)S(1)} %get-tuple-element.71.grad_up, bf16[3072,1024]{1,0:T(8,128)(2,1)S(1)} %bitcast.11, bf16[3072,1024]{1,0:T(8,128)(2,1)S(1)} %get-tuple-element.72.up_copy, ...), custom_call_target="tpu_custom_call" | custom-call | flops 3221225472 | bytes 3145728 | tf_op jit(solution)/shard_map/pallas_call | solution.py:403
  64.6 0.6 collective-permute-start.18
  65.4 1.6 %collective-permute-start.25 = (bf16[64,1536]{1,0:T(8,128)(2,1)S(1)}, bf16[64,1536]{1,0:T(8,128)(2,1)S(1)}, u32[]{:S(2)}, u32[]{:S(2)}) collective-permute-start(bf16[64,1536]{1,0:T(8,128)(2,1)S(1)} %pad_maximum_fusion.13), channel_id=1, source_target_pairs={{16,0},{0,16},{17,1},{1,17},{18,2},{2,18},{19,3},{3,19},{20,4},{4,... | collective-permute-start | bytes 589832 | tf_op jit(solution)/shard_map/ppermute | solution.py:111
  67.0 1.4 %collective-permute-start.24 = (bf16[64,1536]{1,0:T(8,128)(2,1)S(1)}, bf16[64,1536]{1,0:T(8,128)(2,1)S(1)}, u32[]{:S(2)}, u32[]{:S(2)}) collective-permute-start(bf16[64,1536]{1,0:T(8,128)(2,1)S(1)} %concatenate.112), channel_id=1, source_target_pairs={{8,0},{12,4},{0,8},{4,12},{9,1},{13,5},{1,9},{5,13},{10,2},{14,6},... | collective-permute-start | bytes 589832 | tf_op jit(solution)/shard_map/ppermute | solution.py:111
  68.8 0.6 collective-permute-start.20
  69.4 1.0 %collective-permute-start.19 = (bf16[64,1536]{1,0:T(8,128)(2,1)S(1)}, bf16[64,1536]{1,0:T(8,128)(2,1)S(1)}, u32[]{:S(2)}, u32[]{:S(2)}) collective-permute-start(bf16[64,1536]{1,0:T(8,128)(2,1)S(1)} %concatenate.110), channel_id=1, source_target_pairs={{8,0},{12,4},{0,8},{4,12},{9,1},{13,5},{1,9},{5,13},{10,2},{14,6},... | collective-permute-start | bytes 589832 | tf_op jit(solution)/shard_map/ppermute | solution.py:111
  70.4 2.9 %collective-permute-done.25 = bf16[64,1536]{1,0:T(8,128)(2,1)S(1)} collective-permute-done((bf16[64,1536]{1,0:T(8,128)(2,1)S(1)}, bf16[64,1536]{1,0:T(8,128)(2,1)S(1)}, u32[]{:S(2)}, u32[]{:S(2)}) %collective-permute-start.25) | collective-permute-done | bytes 196640 | tf_op jit(solution)/shard_map/ppermute | solution.py:111
  73.3 1.4 %collective-permute-start.30 = (bf16[32,1536]{1,0:T(8,128)(2,1)S(1)}, bf16[32,1536]{1,0:T(8,128)(2,1)S(1)}, u32[]{:S(2)}, u32[]{:S(2)}) collective-permute-start(bf16[32,1536]{1,0:T(8,128)(2,1)S(1)} %split.123), channel_id=1, source_target_pairs={{8,0},{12,4},{0,8},{4,12},{9,1},{13,5},{1,9},{5,13},{10,2},{14,6},... | collective-permute-start | bytes 294920 | tf_op jit(solution)/shard_map/ppermute | solution.py:111
  74.9 1.6 %collective-permute-start.29 = (bf16[32,1536]{1,0:T(8,128)(2,1)S(1)}, bf16[32,1536]{1,0:T(8,128)(2,1)S(1)}, u32[]{:S(2)}, u32[]{:S(2)}) collective-permute-start(bf16[32,1536]{1,0:T(8,128)(2,1)S(1)} %split.124), channel_id=1, source_target_pairs={{16,0},{0,16},{17,1},{1,17},{18,2},{2,18},{19,3},{3,19},{20,4},{4,... | collective-permute-start | bytes 294920 | tf_op jit(solution)/shard_map/ppermute | solution.py:111
  76.4 2.4 %collective-permute-done.19 = bf16[64,1536]{1,0:T(8,128)(2,1)S(1)} collective-permute-done((bf16[64,1536]{1,0:T(8,128)(2,1)S(1)}, bf16[64,1536]{1,0:T(8,128)(2,1)S(1)}, u32[]{:S(2)}, u32[]{:S(2)}) %collective-permute-start.19) | collective-permute-done | bytes 196640 | tf_op jit(solution)/shard_map/ppermute | solution.py:111
  78.9 0.6 collective-permute-start.22
  79.6 1.4 %collective-permute-start.23 = (bf16[32,1664]{1,0:T(8,128)(2,1)S(1)}, bf16[32,1664]{1,0:T(8,128)(2,1)S(1)}, u32[]{:S(2)}, u32[]{:S(2)}) collective-permute-start(bf16[32,1664]{1,0:T(8,128)(2,1)S(1)} %split.122), channel_id=1, source_target_pairs={{8,0},{12,4},{0,8},{4,12},{9,1},{13,5},{1,9},{5,13},{10,2},{14,6},... | collective-permute-start | bytes 319496 | tf_op jit(solution)/shard_map/ppermute | solution.py:111
  81.1 0.7 collective-permute-start.31
  81.8 3.5 %collective-permute-start.32 = (bf16[8,3072]{1,0:T(8,128)(2,1)S(1)}, bf16[8,3072]{1,0:T(8,128)(2,1)S(1)}, u32[]{:S(2)}, u32[]{:S(2)}) collective-permute-start(bf16[8,3072]{1,0:T(8,128)(2,1)S(1)} %get-tuple-element.111), channel_id=1, source_target_pairs={{2,0},{3,1},{0,2},{1,3},{6,4},{7,5},{4,6},{5,7},{10,8},{11,9},{8,1... | collective-permute-start | bytes 147464 | tf_op jit(solution)/shard_map/ppermute | solution.py:111
  86.1 3.8 %collective-permute-start.27 = (bf16[8,3200]{1,0:T(8,128)(2,1)S(1)}, bf16[8,3200]{1,0:T(8,128)(2,1)S(1)}, u32[]{:S(2)}, u32[]{:S(2)}) collective-permute-start(bf16[8,3200]{1,0:T(8,128)(2,1)S(1)} %get-tuple-element.108), channel_id=1, source_target_pairs={{2,0},{3,1},{0,2},{1,3},{6,4},{7,5},{4,6},{5,7},{10,8},{11,9},{8,1... | collective-permute-start | bytes 153608 | tf_op jit(solution)/shard_map/ppermute | solution.py:111
  89.9 0.7 collective-permute-start.28
  90.6 1.1 %collective-permute-done.33 = bf16[8,3072]{1,0:T(8,128)(2,1)S(1)} collective-permute-done((bf16[8,3072]{1,0:T(8,128)(2,1)S(1)}, bf16[8,3072]{1,0:T(8,128)(2,1)S(1)}, u32[]{:S(2)}, u32[]{:S(2)}) %collective-permute-start.33) | collective-permute-done | bytes 49184 | tf_op jit(solution)/shard_map/ppermute | solution.py:111
  92.3 3.6 %collective-permute-done.28 = bf16[8,3200]{1,0:T(8,128)(2,1)S(1)} collective-permute-done((bf16[8,3200]{1,0:T(8,128)(2,1)S(1)}, bf16[8,3200]{1,0:T(8,128)(2,1)S(1)}, u32[]{:S(2)}, u32[]{:S(2)}) %collective-permute-start.28) | collective-permute-done | bytes 51232 | tf_op jit(solution)/shard_map/ppermute | solution.py:111
  96.1 0.6 pad_maximum_fusion.14
  96.7 0.9 fusion.3
  (111 shorter events, 5.2 us)
Async XLA Ops:
  0.6 7.1 %copy-start = (bf16[6144,4]{0,1:T(4,128)(2,1)S(1)}, bf16[6144,4]{0,1:T(4,128)(2,1)}, u32[]{:S(2)}) copy-start(bf16[6144,4]{0,1:T(4,128)(2,1)} %param.12) | copy-start | bytes 147460
  0.6 14.8 %collective-permute-start = (bf16[8,6144]{1,0:T(8,128)(2,1)}, bf16[8,6144]{1,0:T(8,128)(2,1)S(1)}, u32[]{:S(2)}, u32[]{:S(2)}) collective-permute-start(bf16[8,6144]{1,0:T(8,128)(2,1)} %param.8), channel_id=1, source_target_pairs={{1,0},{0,1},{3,2},{2,3},{5,4},{4,5},{7,6},{6,7},{9,8},{8,9},{11,10... | collective-permute-start | bytes 294920 | tf_op jit(solution)/shard_map/ppermute | solution.py:111
  3.7 11.8 %collective-permute-start.4 = (bf16[8,6144]{1,0:T(8,128)(2,1)}, bf16[8,6144]{1,0:T(8,128)(2,1)S(1)}, u32[]{:S(2)}, u32[]{:S(2)}) collective-permute-start(bf16[8,6144]{1,0:T(8,128)(2,1)} %param.8), channel_id=1, source_target_pairs={{2,0},{3,1},{0,2},{1,3},{6,4},{7,5},{4,6},{5,7},{10,8},{11,9},{8,1... | collective-permute-start | bytes 294920 | tf_op jit(solution)/shard_map/ppermute | solution.py:111
  6.3 9.2 %collective-permute-start.5 = (bf16[8,6144]{1,0:T(8,128)(2,1)}, bf16[8,6144]{1,0:T(8,128)(2,1)S(1)}, u32[]{:S(2)}, u32[]{:S(2)}) collective-permute-start(bf16[8,6144]{1,0:T(8,128)(2,1)} %param.8), channel_id=1, source_target_pairs={{3,0},{2,1},{1,2},{0,3},{7,4},{6,5},{5,6},{4,7},{11,8},{10,9},{9,1... | collective-permute-start | bytes 294920 | tf_op jit(solution)/shard_map/ppermute | solution.py:111
  10.0 5.5 %copy-start.2 = (bf16[8,6144]{1,0:T(8,128)(2,1)S(1)}, bf16[8,6144]{1,0:T(8,128)(2,1)}, u32[]{:S(2)}) copy-start(bf16[8,6144]{1,0:T(8,128)(2,1)} %param.8) | copy-start | bytes 294916
  12.8 2.7 %copy-start.1 = (bf16[3072,1024]{1,0:T(8,128)(2,1)}, bf16[3072,1024]{1,0:T(8,128)(2,1)S(1)}, u32[]{:S(2)}) copy-start(bf16[3072,1024]{1,0:T(8,128)(2,1)S(1)} %shard_map.95.gate.gate_copy) | copy-start | bytes 18874372
  15.6 7.7 %collective-permute-start.6 = (bf16[32,3072]{1,0:T(8,128)(2,1)S(1)}, bf16[32,3072]{1,0:T(8,128)(2,1)S(1)}, u32[]{:S(2)}, u32[]{:S(2)}) collective-permute-start(bf16[32,3072]{1,0:T(8,128)(2,1)S(1)} %get-tuple-element.47), channel_id=1, source_target_pairs={{16,0},{0,16},{17,1},{1,17},{18,2},{2,18},{19,3},{3,19},{20,4},{4,... | collective-permute-start | bytes 589832 | tf_op jit(solution)/shard_map/ppermute | solution.py:111
  17.4 5.9 %collective-permute-start.7 = (bf16[32,3072]{1,0:T(8,128)(2,1)S(1)}, bf16[32,3072]{1,0:T(8,128)(2,1)S(1)}, u32[]{:S(2)}, u32[]{:S(2)}) collective-permute-start(bf16[32,3072]{1,0:T(8,128)(2,1)S(1)} %get-tuple-element.49), channel_id=1, source_target_pairs={{8,0},{12,4},{0,8},{4,12},{9,1},{13,5},{1,9},{5,13},{10,2},{14,6},... | collective-permute-start | bytes 589832 | tf_op jit(solution)/shard_map/ppermute | solution.py:111
  18.9 6.4 %collective-permute-start.1 = (bf16[8,6272]{1,0:T(8,128)(2,1)S(1)}, bf16[8,6272]{1,0:T(8,128)(2,1)S(1)}, u32[]{:S(2)}, u32[]{:S(2)}) collective-permute-start(bf16[8,6272]{1,0:T(8,128)(2,1)S(1)} %fusion.4._), channel_id=1, source_target_pairs={{1,0},{0,1},{3,2},{2,3},{5,4},{4,5},{7,6},{6,7},{9,8},{8,9},{11,10... | collective-permute-start | bytes 301064 | tf_op jit(solution)/shard_map/ppermute | solution.py:111
  19.6 9.0 %collective-permute-start.2 = (bf16[8,6272]{1,0:T(8,128)(2,1)S(1)}, bf16[8,6272]{1,0:T(8,128)(2,1)S(1)}, u32[]{:S(2)}, u32[]{:S(2)}) collective-permute-start(bf16[8,6272]{1,0:T(8,128)(2,1)S(1)} %fusion.4._), channel_id=1, source_target_pairs={{2,0},{3,1},{0,2},{1,3},{6,4},{7,5},{4,6},{5,7},{10,8},{11,9},{8,1... | collective-permute-start | bytes 301064 | tf_op jit(solution)/shard_map/ppermute | solution.py:111
  23.1 6.5 %collective-permute-start.3 = (bf16[8,6272]{1,0:T(8,128)(2,1)S(1)}, bf16[8,6272]{1,0:T(8,128)(2,1)S(1)}, u32[]{:S(2)}, u32[]{:S(2)}) collective-permute-start(bf16[8,6272]{1,0:T(8,128)(2,1)S(1)} %fusion.4._), channel_id=1, source_target_pairs={{3,0},{2,1},{1,2},{0,3},{7,4},{6,5},{5,6},{4,7},{11,8},{10,9},{9,1... | collective-permute-start | bytes 301064 | tf_op jit(solution)/shard_map/ppermute | solution.py:111
  23.3 10.8 %collective-permute-start.10 = (bf16[64,3072]{1,0:T(8,128)(2,1)S(1)}, bf16[64,3072]{1,0:T(8,128)(2,1)S(1)}, u32[]{:S(2)}, u32[]{:S(2)}) collective-permute-start(bf16[64,3072]{1,0:T(8,128)(2,1)S(1)} %pad_maximum_fusion.9), channel_id=1, source_target_pairs={{8,0},{12,4},{0,8},{4,12},{9,1},{13,5},{1,9},{5,13},{10,2},{14,6},... | collective-permute-start | bytes 1179656 | tf_op jit(solution)/shard_map/ppermute | solution.py:111
  24.7 14.7 %slice-start = ((s8[6291456]{0:T(1024)(128)(4,1)}), s8[4194304]{0:T(1024)(128)(4,1)S(1)}, s32[]{:S(2)}) async-start(s8[6291456]{0:T(1024)(128)(4,1)} %bitcast.10), calls=%async_computation | async-start | bytes 8388608
  24.7 10.9 %collective-permute-start.11 = (bf16[64,3072]{1,0:T(8,128)(2,1)S(1)}, bf16[64,3072]{1,0:T(8,128)(2,1)S(1)}, u32[]{:S(2)}, u32[]{:S(2)}) collective-permute-start(bf16[64,3072]{1,0:T(8,128)(2,1)S(1)} %pad_maximum_fusion.10), channel_id=1, source_target_pairs={{16,0},{0,16},{17,1},{1,17},{18,2},{2,18},{19,3},{3,19},{20,4},{4,... | collective-permute-start | bytes 1179656 | tf_op jit(solution)/shard_map/ppermute | solution.py:111
  29.8 6.5 %collective-permute-start.9 = (bf16[32,3072]{1,0:T(8,128)(2,1)S(1)}, bf16[32,3072]{1,0:T(8,128)(2,1)S(1)}, u32[]{:S(2)}, u32[]{:S(2)}) collective-permute-start(bf16[32,3072]{1,0:T(8,128)(2,1)S(1)} %get-tuple-element.57), channel_id=1, source_target_pairs={{8,0},{12,4},{0,8},{4,12},{9,1},{13,5},{1,9},{5,13},{10,2},{14,6},... | collective-permute-start | bytes 589832 | tf_op jit(solution)/shard_map/ppermute | solution.py:111
  30.3 7.5 %collective-permute-start.8 = (bf16[32,3200]{1,0:T(8,128)(2,1)S(1)}, bf16[32,3200]{1,0:T(8,128)(2,1)S(1)}, u32[]{:S(2)}, u32[]{:S(2)}) collective-permute-start(bf16[32,3200]{1,0:T(8,128)(2,1)S(1)} %slice.98), channel_id=1, source_target_pairs={{16,0},{0,16},{17,1},{1,17},{18,2},{2,18},{19,3},{3,19},{20,4},{4,... | collective-permute-start | bytes 614408 | tf_op jit(solution)/shard_map/ppermute | solution.py:111
  34.2 5.0 %collective-permute-start.15 = (bf16[128,3072]{1,0:T(8,128)(2,1)S(1)}, bf16[128,3072]{1,0:T(8,128)(2,1)S(1)}, u32[]{:S(2)}, u32[]{:S(2)}) collective-permute-start(bf16[128,3072]{1,0:T(8,128)(2,1)S(1)} %pad_maximum_fusion.4), channel_id=1, source_target_pairs={{4,0},{0,4},{12,8},{8,12},{5,1},{1,5},{13,9},{9,13},{6,2},{2,6},{1... | collective-permute-start | bytes 2359304 | tf_op jit(solution)/shard_map/ppermute | solution.py:111
  35.7 3.7 %slice-start.1 = ((s8[6291456]{0:T(1024)(128)(4,1)}), s8[2097152]{0:T(1024)(128)(4,1)S(1)}, s32[]{:S(2)}) async-start(s8[6291456]{0:T(1024)(128)(4,1)} %bitcast.10), calls=%async_computation.1 | async-start | bytes 4194304
  35.7 3.5 %collective-permute-start.14 = (bf16[128,3072]{1,0:T(8,128)(2,1)S(1)}, bf16[128,3072]{1,0:T(8,128)(2,1)S(1)}, u32[]{:S(2)}, u32[]{:S(2)}) collective-permute-start(bf16[128,3072]{1,0:T(8,128)(2,1)S(1)} %pad_maximum_fusion.3), channel_id=1, source_target_pairs={{4,0},{0,4},{12,8},{8,12},{5,1},{1,5},{13,9},{9,13},{6,2},{2,6},{1... | collective-permute-start | bytes 2359304 | tf_op jit(solution)/shard_map/ppermute | solution.py:111
  37.8 10.2 %collective-permute-start.13 = (bf16[64,3072]{1,0:T(8,128)(2,1)S(1)}, bf16[64,3072]{1,0:T(8,128)(2,1)S(1)}, u32[]{:S(2)}, u32[]{:S(2)}) collective-permute-start(bf16[64,3072]{1,0:T(8,128)(2,1)S(1)} %pad_maximum_fusion.11), channel_id=1, source_target_pairs={{16,0},{0,16},{17,1},{1,17},{18,2},{2,18},{19,3},{3,19},{20,4},{4,... | collective-permute-start | bytes 1179656 | tf_op jit(solution)/shard_map/ppermute | solution.py:111
  38.5 9.7 %collective-permute-start.12 = (bf16[64,3200]{1,0:T(8,128)(2,1)S(1)}, bf16[64,3200]{1,0:T(8,128)(2,1)S(1)}, u32[]{:S(2)}, u32[]{:S(2)}) collective-permute-start(bf16[64,3200]{1,0:T(8,128)(2,1)S(1)} %pad_maximum_fusion.7), channel_id=1, source_target_pairs={{8,0},{12,4},{0,8},{4,12},{9,1},{13,5},{1,9},{5,13},{10,2},{14,6},... | collective-permute-start | bytes 1228808 | tf_op jit(solution)/shard_map/ppermute | solution.py:111
  48.3 3.5 %collective-permute-start.17 = (bf16[128,3072]{1,0:T(8,128)(2,1)S(1)}, bf16[128,3072]{1,0:T(8,128)(2,1)S(1)}, u32[]{:S(2)}, u32[]{:S(2)}) collective-permute-start(bf16[128,3072]{1,0:T(8,128)(2,1)S(1)} %pad_maximum_fusion.5), channel_id=1, source_target_pairs={{4,0},{0,4},{12,8},{8,12},{5,1},{1,5},{13,9},{9,13},{6,2},{2,6},{1... | collective-permute-start | bytes 2359304 | tf_op jit(solution)/shard_map/ppermute | solution.py:111
  48.4 3.5 %collective-permute-start.16 = (bf16[128,3200]{1,0:T(8,128)(2,1)S(1)}, bf16[128,3200]{1,0:T(8,128)(2,1)S(1)}, u32[]{:S(2)}, u32[]{:S(2)}) collective-permute-start(bf16[128,3200]{1,0:T(8,128)(2,1)S(1)} %pad_maximum_fusion.2), channel_id=1, source_target_pairs={{4,0},{0,4},{12,8},{8,12},{5,1},{1,5},{13,9},{9,13},{6,2},{2,6},{1... | collective-permute-start | bytes 2457608 | tf_op jit(solution)/shard_map/ppermute | solution.py:111
  60.6 4.5 %collective-permute-start.21 = (bf16[128,3072]{1,0:T(8,128)(2,1)S(1)}, bf16[128,3072]{1,0:T(8,128)(2,1)S(1)}, u32[]{:S(2)}, u32[]{:S(2)}) collective-permute-start(bf16[128,3072]{1,0:T(8,128)(2,1)S(1)} %get-tuple-element.76), channel_id=1, source_target_pairs={{4,0},{0,4},{12,8},{8,12},{5,1},{1,5},{13,9},{9,13},{6,2},{2,6},{1... | collective-permute-start | bytes 2359304 | tf_op jit(solution)/shard_map/ppermute | solution.py:111
  64.6 3.9 %collective-permute-start.18 = (bf16[128,3200]{1,0:T(8,128)(2,1)S(1)}, bf16[128,3200]{1,0:T(8,128)(2,1)S(1)}, u32[]{:S(2)}, u32[]{:S(2)}) collective-permute-start(bf16[128,3200]{1,0:T(8,128)(2,1)S(1)} %get-tuple-element.75), channel_id=1, source_target_pairs={{4,0},{0,4},{12,8},{8,12},{5,1},{1,5},{13,9},{9,13},{6,2},{2,6},{1... | collective-permute-start | bytes 2457608 | tf_op jit(solution)/shard_map/ppermute | solution.py:111
  65.4 7.8 %collective-permute-start.25 = (bf16[64,1536]{1,0:T(8,128)(2,1)S(1)}, bf16[64,1536]{1,0:T(8,128)(2,1)S(1)}, u32[]{:S(2)}, u32[]{:S(2)}) collective-permute-start(bf16[64,1536]{1,0:T(8,128)(2,1)S(1)} %pad_maximum_fusion.13), channel_id=1, source_target_pairs={{16,0},{0,16},{17,1},{1,17},{18,2},{2,18},{19,3},{3,19},{20,4},{4,... | collective-permute-start | bytes 589832 | tf_op jit(solution)/shard_map/ppermute | solution.py:111
  67.0 7.8 %collective-permute-start.24 = (bf16[64,1536]{1,0:T(8,128)(2,1)S(1)}, bf16[64,1536]{1,0:T(8,128)(2,1)S(1)}, u32[]{:S(2)}, u32[]{:S(2)}) collective-permute-start(bf16[64,1536]{1,0:T(8,128)(2,1)S(1)} %concatenate.112), channel_id=1, source_target_pairs={{8,0},{12,4},{0,8},{4,12},{9,1},{13,5},{1,9},{5,13},{10,2},{14,6},... | collective-permute-start | bytes 589832 | tf_op jit(solution)/shard_map/ppermute | solution.py:111
  68.8 10.1 %collective-permute-start.20 = (bf16[64,1664]{1,0:T(8,128)(2,1)S(1)}, bf16[64,1664]{1,0:T(8,128)(2,1)S(1)}, u32[]{:S(2)}, u32[]{:S(2)}) collective-permute-start(bf16[64,1664]{1,0:T(8,128)(2,1)S(1)} %pad_maximum_fusion.12), channel_id=1, source_target_pairs={{16,0},{0,16},{17,1},{1,17},{18,2},{2,18},{19,3},{3,19},{20,4},{4,... | collective-permute-start | bytes 638984 | tf_op jit(solution)/shard_map/ppermute | solution.py:111
  69.4 9.4 %collective-permute-start.19 = (bf16[64,1536]{1,0:T(8,128)(2,1)S(1)}, bf16[64,1536]{1,0:T(8,128)(2,1)S(1)}, u32[]{:S(2)}, u32[]{:S(2)}) collective-permute-start(bf16[64,1536]{1,0:T(8,128)(2,1)S(1)} %concatenate.110), channel_id=1, source_target_pairs={{8,0},{12,4},{0,8},{4,12},{9,1},{13,5},{1,9},{5,13},{10,2},{14,6},... | collective-permute-start | bytes 589832 | tf_op jit(solution)/shard_map/ppermute | solution.py:111
  73.3 7.7 %collective-permute-start.30 = (bf16[32,1536]{1,0:T(8,128)(2,1)S(1)}, bf16[32,1536]{1,0:T(8,128)(2,1)S(1)}, u32[]{:S(2)}, u32[]{:S(2)}) collective-permute-start(bf16[32,1536]{1,0:T(8,128)(2,1)S(1)} %split.123), channel_id=1, source_target_pairs={{8,0},{12,4},{0,8},{4,12},{9,1},{13,5},{1,9},{5,13},{10,2},{14,6},... | collective-permute-start | bytes 294920 | tf_op jit(solution)/shard_map/ppermute | solution.py:111
  74.9 6.2 %collective-permute-start.29 = (bf16[32,1536]{1,0:T(8,128)(2,1)S(1)}, bf16[32,1536]{1,0:T(8,128)(2,1)S(1)}, u32[]{:S(2)}, u32[]{:S(2)}) collective-permute-start(bf16[32,1536]{1,0:T(8,128)(2,1)S(1)} %split.124), channel_id=1, source_target_pairs={{16,0},{0,16},{17,1},{1,17},{18,2},{2,18},{19,3},{3,19},{20,4},{4,... | collective-permute-start | bytes 294920 | tf_op jit(solution)/shard_map/ppermute | solution.py:111
  78.9 6.6 %collective-permute-start.22 = (bf16[32,1536]{1,0:T(8,128)(2,1)S(1)}, bf16[32,1536]{1,0:T(8,128)(2,1)S(1)}, u32[]{:S(2)}, u32[]{:S(2)}) collective-permute-start(bf16[32,1536]{1,0:T(8,128)(2,1)S(1)} %split.125), channel_id=1, source_target_pairs={{16,0},{0,16},{17,1},{1,17},{18,2},{2,18},{19,3},{3,19},{20,4},{4,... | collective-permute-start | bytes 294920 | tf_op jit(solution)/shard_map/ppermute | solution.py:111
  79.6 6.1 %collective-permute-start.23 = (bf16[32,1664]{1,0:T(8,128)(2,1)S(1)}, bf16[32,1664]{1,0:T(8,128)(2,1)S(1)}, u32[]{:S(2)}, u32[]{:S(2)}) collective-permute-start(bf16[32,1664]{1,0:T(8,128)(2,1)S(1)} %split.122), channel_id=1, source_target_pairs={{8,0},{12,4},{0,8},{4,12},{9,1},{13,5},{1,9},{5,13},{10,2},{14,6},... | collective-permute-start | bytes 319496 | tf_op jit(solution)/shard_map/ppermute | solution.py:111
  81.1 8.8 %collective-permute-start.31 = (bf16[8,3072]{1,0:T(8,128)(2,1)S(1)}, bf16[8,3072]{1,0:T(8,128)(2,1)S(1)}, u32[]{:S(2)}, u32[]{:S(2)}) collective-permute-start(bf16[8,3072]{1,0:T(8,128)(2,1)S(1)} %get-tuple-element.109), channel_id=1, source_target_pairs={{1,0},{0,1},{3,2},{2,3},{5,4},{4,5},{7,6},{6,7},{9,8},{8,9},{11,10... | collective-permute-start | bytes 147464 | tf_op jit(solution)/shard_map/ppermute | solution.py:111
  81.8 8.8 %collective-permute-start.32 = (bf16[8,3072]{1,0:T(8,128)(2,1)S(1)}, bf16[8,3072]{1,0:T(8,128)(2,1)S(1)}, u32[]{:S(2)}, u32[]{:S(2)}) collective-permute-start(bf16[8,3072]{1,0:T(8,128)(2,1)S(1)} %get-tuple-element.111), channel_id=1, source_target_pairs={{2,0},{3,1},{0,2},{1,3},{6,4},{7,5},{4,6},{5,7},{10,8},{11,9},{8,1... | collective-permute-start | bytes 147464 | tf_op jit(solution)/shard_map/ppermute | solution.py:111
  85.3 6.4 %collective-permute-start.33 = (bf16[8,3072]{1,0:T(8,128)(2,1)S(1)}, bf16[8,3072]{1,0:T(8,128)(2,1)S(1)}, u32[]{:S(2)}, u32[]{:S(2)}) collective-permute-start(bf16[8,3072]{1,0:T(8,128)(2,1)S(1)} %get-tuple-element.110), channel_id=1, source_target_pairs={{3,0},{2,1},{1,2},{0,3},{7,4},{6,5},{5,6},{4,7},{11,8},{10,9},{9,1... | collective-permute-start | bytes 147464 | tf_op jit(solution)/shard_map/ppermute | solution.py:111
  85.7 10.4 %copy-start.3 = (s32[8]{0:T(128)S(1)}, s32[8]{0:T(128)}, u32[]{:S(2)}) copy-start(s32[8]{0:T(128)} %param.10) | copy-start | bytes 100
  85.8 6.0 %collective-permute-start.26 = (bf16[8,3200]{1,0:T(8,128)(2,1)S(1)}, bf16[8,3200]{1,0:T(8,128)(2,1)S(1)}, u32[]{:S(2)}, u32[]{:S(2)}) collective-permute-start(bf16[8,3200]{1,0:T(8,128)(2,1)S(1)} %get-tuple-element.106), channel_id=1, source_target_pairs={{1,0},{0,1},{3,2},{2,3},{5,4},{4,5},{7,6},{6,7},{9,8},{8,9},{11,10... | collective-permute-start | bytes 153608 | tf_op jit(solution)/shard_map/ppermute | solution.py:111
  86.1 6.2 %collective-permute-start.27 = (bf16[8,3200]{1,0:T(8,128)(2,1)S(1)}, bf16[8,3200]{1,0:T(8,128)(2,1)S(1)}, u32[]{:S(2)}, u32[]{:S(2)}) collective-permute-start(bf16[8,3200]{1,0:T(8,128)(2,1)S(1)} %get-tuple-element.108), channel_id=1, source_target_pairs={{2,0},{3,1},{0,2},{1,3},{6,4},{7,5},{4,6},{5,7},{10,8},{11,9},{8,1... | collective-permute-start | bytes 153608 | tf_op jit(solution)/shard_map/ppermute | solution.py:111
  89.9 5.9 %collective-permute-start.28 = (bf16[8,3200]{1,0:T(8,128)(2,1)S(1)}, bf16[8,3200]{1,0:T(8,128)(2,1)S(1)}, u32[]{:S(2)}, u32[]{:S(2)}) collective-permute-start(bf16[8,3200]{1,0:T(8,128)(2,1)S(1)} %get-tuple-element.107), channel_id=1, source_target_pairs={{3,0},{2,1},{1,2},{0,3},{7,4},{6,5},{5,6},{4,7},{11,8},{10,9},{9,1... | collective-permute-start | bytes 153608 | tf_op jit(solution)/shard_map/ppermute | solution.py:111

commit v15 on v13

--- a/solution.py
+++ b/solution.py
@@ -407,12 +407,12 @@
     pre_gate, pre_up, gate_high, up_high = multiply_tokens(
         token_low, gate_low, up_low, 0, half, (), ((gate_weight, half, half), (up_weight, half, half))
     )
-    pre_gate, pre_up = multiply_tokens(token_high, gate_high, up_high, 0, quarter, (pre_gate, pre_up))
+    pre_gate, pre_up, down = multiply_tokens(
+        token_high, gate_high, up_high, 0, quarter, (pre_gate, pre_up),
+        ((down_weight, 0, down_weight.shape[1] // 2),),
+    )
     grad_far = after_others(grad_far, pre_gate)
-    pre_gate, pre_up, down = multiply_tokens(
-        token_high, gate_high, up_high, quarter, quarter, (pre_gate, pre_up),
-        ((down_weight, 0, down_weight.shape[1] // 2),),
-    )
+    pre_gate, pre_up = multiply_tokens(token_high, gate_high, up_high, quarter, quarter, (pre_gate, pre_up))
     grad_halves = gather_core(grad_near[0], grad_far[0], grad_near[1], grad_far[1])
     expert = lax.axis_index("expert").astype(jnp.int32).reshape(1)
     grad_gate, grad_up, dots = multiply_grads(expert, *grad_halves, pre_gate, pre_up, down, down_weight)

time: 97 us -> 97 us (level)
  no operation moved by 1% of the time
where the time goes in v15:
time: 97 us; the launch traced here: 96.7 us
  starting transfers between devices  36.3 us (37%)
  Pallas kernels  27.7 us (29%)
  waiting for transfers between devices  24 us (25%)
  other arithmetic  2.99 us (3%)
  local copies, waits for them, and re-layouts  2.36 us (2%)
  matrix products  2.15 us (2%)
  between operations  1.22 us (1%)
    ppermute x34, starting transfers between devices, swap(): lax.ppermute(value, axis, [(i ^ bit, i) for i in range(lax.axis_size(axis...  36.3 us
    ppermute x34, waiting for transfers between devices, swap(): lax.ppermute(value, axis, [(i ^ bit, i) for i in range(lax.axis_size(axis...  24 us
    pallas_call x3, Pallas kernels, multiply_tokens(): pl.pallas_call(functools.partial(token_kernel, offset, length, sources, l...  9.75 us
    pallas_call x2, Pallas kernels, multiply_outputs(): pl.pallas_call(output_kernel, out_shape=(pltpu.VMEM((rows // 2, total), j...  7.66 us
    pallas_call x2, Pallas kernels, fetch(): pl.pallas_call(functools.partial(fetch_kernel, first), out_shape=tuple((p...  5.59 us
    pallas_call x1, Pallas kernels, multiply_grads(): pl.pallas_call(grad_kernel, out_shape=(pltpu.VMEM((rows, hidden), jnp.bfl...  4.72 us
  transfers between devices with their start and end apart: 34, of which 14 were waited for; matrix products, arithmetic and copies ran while one was open for 6% of the time, Pallas kernels for 20%

profile of v15, /device:TPU:0, one launch (start us, length us, event | category | flops | bytes accessed | tf_op | source)
XLA Modules:
  0.0 96.7 jit_solution(15770918080221993355)
XLA Ops:
  0.7 3.1 %collective-permute-start = (bf16[8,6144]{1,0:T(8,128)(2,1)}, bf16[8,6144]{1,0:T(8,128)(2,1)S(1)}, u32[]{:S(2)}, u32[]{:S(2)}) collective-permute-start(bf16[8,6144]{1,0:T(8,128)(2,1)} %param.8), channel_id=1, source_target_pairs={{1,0},{0,1},{3,2},{2,3},{5,4},{4,5},{7,6},{6,7},{9,8},{8,9},{11,10... | collective-permute-start | bytes 294920 | tf_op jit(solution)/shard_map/ppermute | solution.py:111
  3.7 2.6 %collective-permute-start.4 = (bf16[8,6144]{1,0:T(8,128)(2,1)}, bf16[8,6144]{1,0:T(8,128)(2,1)S(1)}, u32[]{:S(2)}, u32[]{:S(2)}) collective-permute-start(bf16[8,6144]{1,0:T(8,128)(2,1)} %param.8), channel_id=1, source_target_pairs={{2,0},{3,1},{0,2},{1,3},{6,4},{7,5},{4,6},{5,7},{10,8},{11,9},{8,1... | collective-permute-start | bytes 294920 | tf_op jit(solution)/shard_map/ppermute | solution.py:111
  6.3 1.0 constant_dynamic-update-slice_fusion.3
  7.3 0.8 slice_bitcast_fusion
  8.1 0.7 convert_element_type.76
  8.7 1.2 %select_reduce_fusion.3 = (f32[8]{0:T(128)S(1)}, f32[8]{0:T(128)S(1)}) fusion(s32[8]{0:T(128)S(1)} %get-tuple-element.111, s32[8]{0:T(128)S(1)} %get-tuple-element.110, bf16[8,6144]{1,0:T(8,128)(2,1)} %param.8, bf16[6144,4]{0,1:T(4,128)(2,1)S(1)} %copy-done), kind=kOutput, calls=%fused_computation.69 | convolution fusion | flops 393392 | bytes 147584 | tf_op jit(solution)/shard_map/dot_general | solution.py:390
  10.1 4.3 %collective-permute-done.4 = bf16[8,6144]{1,0:T(8,128)(2,1)S(1)} collective-permute-done((bf16[8,6144]{1,0:T(8,128)(2,1)}, bf16[8,6144]{1,0:T(8,128)(2,1)S(1)}, u32[]{:S(2)}, u32[]{:S(2)}) %collective-permute-start.4) | collective-permute-done | bytes 98336 | tf_op jit(solution)/shard_map/ppermute | solution.py:111
  14.5 1.6 %collective-permute-start.6 = (bf16[32,3072]{1,0:T(8,128)(2,1)S(1)}, bf16[32,3072]{1,0:T(8,128)(2,1)S(1)}, u32[]{:S(2)}, u32[]{:S(2)}) collective-permute-start(bf16[32,3072]{1,0:T(8,128)(2,1)S(1)} %get-tuple-element.40._), channel_id=1, source_target_pairs={{16,0},{0,16},{17,1},{1,17},{18,2},{2,18},{19,3},{3,19},{20,4},{4,... | collective-permute-start | bytes 589832 | tf_op jit(solution)/shard_map/ppermute | solution.py:111
  16.0 1.5 %collective-permute-start.7 = (bf16[32,3072]{1,0:T(8,128)(2,1)S(1)}, bf16[32,3072]{1,0:T(8,128)(2,1)S(1)}, u32[]{:S(2)}, u32[]{:S(2)}) collective-permute-start(bf16[32,3072]{1,0:T(8,128)(2,1)S(1)} %get-tuple-element.42), channel_id=1, source_target_pairs={{8,0},{12,4},{0,8},{4,12},{9,1},{13,5},{1,9},{5,13},{10,2},{14,6},... | collective-permute-start | bytes 589832 | tf_op jit(solution)/shard_map/ppermute | solution.py:111
  17.6 1.7 %collective-permute-start.1 = (bf16[8,6272]{1,0:T(8,128)(2,1)S(1)}, bf16[8,6272]{1,0:T(8,128)(2,1)S(1)}, u32[]{:S(2)}, u32[]{:S(2)}) collective-permute-start(bf16[8,6272]{1,0:T(8,128)(2,1)S(1)} %fusion.4), channel_id=1, source_target_pairs={{1,0},{0,1},{3,2},{2,3},{5,4},{4,5},{7,6},{6,7},{9,8},{8,9},{11,10... | collective-permute-start | bytes 301064 | tf_op jit(solution)/shard_map/ppermute | solution.py:111
  19.2 1.4 %collective-permute-start.2 = (bf16[8,6272]{1,0:T(8,128)(2,1)S(1)}, bf16[8,6272]{1,0:T(8,128)(2,1)S(1)}, u32[]{:S(2)}, u32[]{:S(2)}) collective-permute-start(bf16[8,6272]{1,0:T(8,128)(2,1)S(1)} %fusion.4), channel_id=1, source_target_pairs={{2,0},{3,1},{0,2},{1,3},{6,4},{7,5},{4,6},{5,7},{10,8},{11,9},{8,1... | collective-permute-start | bytes 301064 | tf_op jit(solution)/shard_map/ppermute | solution.py:111
  20.6 1.4 %collective-permute-start.3 = (bf16[8,6272]{1,0:T(8,128)(2,1)S(1)}, bf16[8,6272]{1,0:T(8,128)(2,1)S(1)}, u32[]{:S(2)}, u32[]{:S(2)}) collective-permute-start(bf16[8,6272]{1,0:T(8,128)(2,1)S(1)} %fusion.4), channel_id=1, source_target_pairs={{3,0},{2,1},{1,2},{0,3},{7,4},{6,5},{5,6},{4,7},{11,8},{10,9},{9,1... | collective-permute-start | bytes 301064 | tf_op jit(solution)/shard_map/ppermute | solution.py:111
  22.0 2.8 %shard_map.95.gate.gate_copy = bf16[3072,1024]{1,0:T(8,128)(2,1)S(1)} custom-call(bf16[32,3072]{1,0:T(8,128)(2,1)S(1)} %get-tuple-element.40._, bf16[1,6144,1024]{2,1,0:T(8,128)(2,1)} %refs_0_.5), custom_call_target="tpu_custom_call" | custom-call | bytes 6291456 | tf_op jit(solution)/shard_map/pallas_call | solution.py:210
  24.9 0.6 collective-permute-start.11
  25.5 0.6 collective-permute-start.10
  26.1 2.0 %collective-permute-done.2 = bf16[8,6272]{1,0:T(8,128)(2,1)S(1)} collective-permute-done((bf16[8,6272]{1,0:T(8,128)(2,1)S(1)}, bf16[8,6272]{1,0:T(8,128)(2,1)S(1)}, u32[]{:S(2)}, u32[]{:S(2)}) %collective-permute-start.2) | collective-permute-done | bytes 100384 | tf_op jit(solution)/shard_map/ppermute | solution.py:111
  28.2 2.8 %shard_map.96.up.up_copy = bf16[3072,1024]{1,0:T(8,128)(2,1)S(1)} custom-call(bf16[32,3072]{1,0:T(8,128)(2,1)S(1)} %collective-permute-done.7._, bf16[1,6144,1024]{2,1,0:T(8,128)(2,1)} %refs_1_.1), custom_call_target="tpu_custom_call" | custom-call | bytes 6291456 | tf_op jit(solution)/shard_map/pallas_call | solution.py:210
  31.0 0.6 collective-permute-start.9
  32.1 3.2 %collective-permute-done.11 = bf16[64,3072]{1,0:T(8,128)(2,1)S(1)} collective-permute-done((bf16[64,3072]{1,0:T(8,128)(2,1)S(1)}, bf16[64,3072]{1,0:T(8,128)(2,1)S(1)}, u32[]{:S(2)}, u32[]{:S(2)}) %collective-permute-start.11) | collective-permute-done | bytes 393248 | tf_op jit(solution)/shard_map/ppermute | solution.py:111
  36.4 1.3 %collective-permute-done.9 = bf16[32,3072]{1,0:T(8,128)(2,1)S(1)} collective-permute-done((bf16[32,3072]{1,0:T(8,128)(2,1)S(1)}, bf16[32,3072]{1,0:T(8,128)(2,1)S(1)}, u32[]{:S(2)}, u32[]{:S(2)}) %collective-permute-start.9) | collective-permute-done | bytes 196640 | tf_op jit(solution)/shard_map/ppermute | solution.py:111
  37.8 1.6 %collective-permute-start.13 = (bf16[64,3072]{1,0:T(8,128)(2,1)S(1)}, bf16[64,3072]{1,0:T(8,128)(2,1)S(1)}, u32[]{:S(2)}, u32[]{:S(2)}) collective-permute-start(bf16[64,3072]{1,0:T(8,128)(2,1)S(1)} %pad_maximum_fusion.11), channel_id=1, source_target_pairs={{16,0},{0,16},{17,1},{1,17},{18,2},{2,18},{19,3},{3,19},{20,4},{4,... | collective-permute-start | bytes 1179656 | tf_op jit(solution)/shard_map/ppermute | solution.py:111
  39.3 0.6 collective-permute-start.12
  40.1 4.7 %shard_map.97 = (f32[256,1024]{1,0:T(8,128)S(1)}, f32[256,1024]{1,0:T(8,128)S(1)}, bf16[3072,1024]{1,0:T(8,128)(2,1)S(1)}, bf16[3072,1024]{1,0:T(8,128)(2,1)S(1)}) custom-call(bf16[256,3072]{1,0:T(8,128)(2,1)S(1)} %pad_maximum_fusion.1.tokens, bf16[3072,1024]{1,0:T(8,128)(2,1)S(1)} %shard_map.95.gate.gate_copy, bf16[3072,1024]{1,0:T(8,128)(2,1)S(1)} %shard_map.96.up.up_copy, ...), custom_call_target="tpu_custom_call" | custom-call | flops 3221225472 | bytes 1572864 | tf_op jit(solution)/shard_map/pallas_call | solution.py:253
  44.8 2.8 %shard_map.98 = (f32[256,1024]{1,0:T(8,128)S(1)}, f32[256,1024]{1,0:T(8,128)S(1)}, bf16[512,6144]{1,0:T(8,128)(2,1)S(1)}) custom-call(bf16[256,3072]{1,0:T(8,128)(2,1)S(1)} %constant_dynamic-update-slice_fusion.8.tokens, bf16[3072,1024]{1,0:T(8,128)(2,1)S(1)} %get-tuple-element.54.gate.gate_copy, bf16[3072,1024]{1,0:T(8,128)(2,1)S(1)} %get-tuple-element.55.up.up_copy, ...), custom_call_target="tpu_custom_call" | custom-call | flops 1610612736 | bytes 786432 | tf_op jit(solution)/shard_map/pallas_call | solution.py:253
  47.6 1.7 %collective-permute-done.12 = bf16[64,3200]{1,0:T(8,128)(2,1)S(1)} collective-permute-done((bf16[64,3200]{1,0:T(8,128)(2,1)S(1)}, bf16[64,3200]{1,0:T(8,128)(2,1)S(1)}, u32[]{:S(2)}, u32[]{:S(2)}) %collective-permute-start.12) | collective-permute-done | bytes 409632 | tf_op jit(solution)/shard_map/ppermute | solution.py:111
  49.5 0.6 collective-permute-start.16
  50.1 2.3 %shard_map.99 = (f32[256,1024]{1,0:T(8,128)S(1)}, f32[256,1024]{1,0:T(8,128)S(1)}) custom-call(bf16[256,3072]{1,0:T(8,128)(2,1)S(1)} %constant_dynamic-update-slice_fusion.8.tokens, bf16[3072,1024]{1,0:T(8,128)(2,1)S(1)} %get-tuple-element.54.gate.gate_copy, bf16[3072,1024]{1,0:T(8,128)(2,1)S(1)} %get-tuple-element.55.up.up_copy, ...), custom_call_target="tpu_custom_call" | custom-call | flops 1610612736 | bytes 786432 | tf_op jit(solution)/shard_map/pallas_call | solution.py:253
  53.0 4.7 %shard_map.100 = (bf16[256,1024]{1,0:T(8,128)(2,1)S(1)}, bf16[256,1024]{1,0:T(8,128)(2,1)S(1)}, bf16[256,128]{1,0:T(8,128)(2,1)S(1)}) custom-call(s32[1]{0:T(128)} %bitcast.expert, bf16[256,3200]{1,0:T(8,128)(2,1)S(1)} %pad_maximum_fusion.low, bf16[256,3072]{1,0:T(8,128)(2,1)S(1)} %constant_dynamic-update-slice_fusion.13.high, ...), custom_call_target="tpu_custom_call" | custom-call | flops 3221225472 | bytes 6291456 | tf_op jit(solution)/shard_map/pallas_call | solution.py:319
  57.7 3.8 %shard_map.102 = (f32[128,3072]{1,0:T(8,128)S(1)}, bf16[128,3072]{1,0:T(8,128)(2,1)S(1)}) custom-call(bf16[256,1024]{1,0:T(8,128)(2,1)S(1)} %get-tuple-element.65.grad_gate, bf16[256,1024]{1,0:T(8,128)(2,1)S(1)} %get-tuple-element.66.grad_up, bf16[3072,1024]{1,0:T(8,128)(2,1)S(1)} %get-tuple-element.54.gate.gate_copy, ...), custom_call_target="tpu_custom_call" | custom-call | flops 3221225472 | bytes 3145728 | tf_op jit(solution)/shard_map/pallas_call | solution.py:365
  61.8 3.8 %shard_map.101 = (f32[128,3200]{1,0:T(8,128)S(1)}, bf16[128,3200]{1,0:T(8,128)(2,1)S(1)}) custom-call(bf16[256,1024]{1,0:T(8,128)(2,1)S(1)} %get-tuple-element.65.grad_gate, bf16[256,1024]{1,0:T(8,128)(2,1)S(1)} %get-tuple-element.66.grad_up, bf16[3072,1024]{1,0:T(8,128)(2,1)S(1)} %shard_map.95.gate.gate_copy, bf16[3072,1024]{1,0:T(8,128)(2,1)S(1)} %shard_map.96.up.up_copy, ...), custom_call_target="tpu_custom_call" | custom-call | flops 3221225472 | bytes 3145728 | tf_op jit(solution)/shard_map/pallas_call | solution.py:365
  66.4 0.6 collective-permute-start.25
  68.4 1.1 %collective-permute-start.20 = (bf16[64,1664]{1,0:T(8,128)(2,1)S(1)}, bf16[64,1664]{1,0:T(8,128)(2,1)S(1)}, u32[]{:S(2)}, u32[]{:S(2)}) collective-permute-start(bf16[64,1664]{1,0:T(8,128)(2,1)S(1)} %pad_maximum_fusion.12), channel_id=1, source_target_pairs={{16,0},{0,16},{17,1},{1,17},{18,2},{2,18},{19,3},{3,19},{20,4},{4,... | collective-permute-start | bytes 638984 | tf_op jit(solution)/shard_map/ppermute | solution.py:111
  69.4 1.5 %collective-permute-start.19 = (bf16[64,1536]{1,0:T(8,128)(2,1)S(1)}, bf16[64,1536]{1,0:T(8,128)(2,1)S(1)}, u32[]{:S(2)}, u32[]{:S(2)}) collective-permute-start(bf16[64,1536]{1,0:T(8,128)(2,1)S(1)} %concatenate.110), channel_id=1, source_target_pairs={{8,0},{12,4},{0,8},{4,12},{9,1},{13,5},{1,9},{5,13},{10,2},{14,6},... | collective-permute-start | bytes 589832 | tf_op jit(solution)/shard_map/ppermute | solution.py:111
  71.0 3.2 %collective-permute-done.25 = bf16[64,1536]{1,0:T(8,128)(2,1)S(1)} collective-permute-done((bf16[64,1536]{1,0:T(8,128)(2,1)S(1)}, bf16[64,1536]{1,0:T(8,128)(2,1)S(1)}, u32[]{:S(2)}, u32[]{:S(2)}) %collective-permute-start.25) | collective-permute-done | bytes 196640 | tf_op jit(solution)/shard_map/ppermute | solution.py:111
  74.3 0.6 collective-permute-start.30
  74.9 1.5 %collective-permute-start.29 = (bf16[32,1536]{1,0:T(8,128)(2,1)S(1)}, bf16[32,1536]{1,0:T(8,128)(2,1)S(1)}, u32[]{:S(2)}, u32[]{:S(2)}) collective-permute-start(bf16[32,1536]{1,0:T(8,128)(2,1)S(1)} %split.122), channel_id=1, source_target_pairs={{16,0},{0,16},{17,1},{1,17},{18,2},{2,18},{19,3},{3,19},{20,4},{4,... | collective-permute-start | bytes 294920 | tf_op jit(solution)/shard_map/ppermute | solution.py:111
  76.4 2.5 %collective-permute-done.19 = bf16[64,1536]{1,0:T(8,128)(2,1)S(1)} collective-permute-done((bf16[64,1536]{1,0:T(8,128)(2,1)S(1)}, bf16[64,1536]{1,0:T(8,128)(2,1)S(1)}, u32[]{:S(2)}, u32[]{:S(2)}) %collective-permute-start.19) | collective-permute-done | bytes 196640 | tf_op jit(solution)/shard_map/ppermute | solution.py:111
  79.0 1.6 %collective-permute-start.22 = (bf16[32,1536]{1,0:T(8,128)(2,1)S(1)}, bf16[32,1536]{1,0:T(8,128)(2,1)S(1)}, u32[]{:S(2)}, u32[]{:S(2)}) collective-permute-start(bf16[32,1536]{1,0:T(8,128)(2,1)S(1)} %split.123), channel_id=1, source_target_pairs={{16,0},{0,16},{17,1},{1,17},{18,2},{2,18},{19,3},{3,19},{20,4},{4,... | collective-permute-start | bytes 294920 | tf_op jit(solution)/shard_map/ppermute | solution.py:111
  80.6 0.6 collective-permute-start.23
  81.3 1.0 %collective-permute-start.31 = (bf16[8,3072]{1,0:T(8,128)(2,1)S(1)}, bf16[8,3072]{1,0:T(8,128)(2,1)S(1)}, u32[]{:S(2)}, u32[]{:S(2)}) collective-permute-start(bf16[8,3072]{1,0:T(8,128)(2,1)S(1)} %get-tuple-element.103), channel_id=1, source_target_pairs={{1,0},{0,1},{3,2},{2,3},{5,4},{4,5},{7,6},{6,7},{9,8},{8,9},{11,10... | collective-permute-start | bytes 147464 | tf_op jit(solution)/shard_map/ppermute | solution.py:111
  82.3 2.1 %collective-permute-start.32 = (bf16[8,3072]{1,0:T(8,128)(2,1)S(1)}, bf16[8,3072]{1,0:T(8,128)(2,1)S(1)}, u32[]{:S(2)}, u32[]{:S(2)}) collective-permute-start(bf16[8,3072]{1,0:T(8,128)(2,1)S(1)} %get-tuple-element.105), channel_id=1, source_target_pairs={{2,0},{3,1},{0,2},{1,3},{6,4},{7,5},{4,6},{5,7},{10,8},{11,9},{8,1... | collective-permute-start | bytes 147464 | tf_op jit(solution)/shard_map/ppermute | solution.py:111
  84.4 1.4 %collective-permute-start.33 = (bf16[8,3072]{1,0:T(8,128)(2,1)S(1)}, bf16[8,3072]{1,0:T(8,128)(2,1)S(1)}, u32[]{:S(2)}, u32[]{:S(2)}) collective-permute-start(bf16[8,3072]{1,0:T(8,128)(2,1)S(1)} %get-tuple-element.104), channel_id=1, source_target_pairs={{3,0},{2,1},{1,2},{0,3},{7,4},{6,5},{5,6},{4,7},{11,8},{10,9},{9,1... | collective-permute-start | bytes 147464 | tf_op jit(solution)/shard_map/ppermute | solution.py:111
  86.5 2.5 %collective-permute-start.27 = (bf16[8,3200]{1,0:T(8,128)(2,1)S(1)}, bf16[8,3200]{1,0:T(8,128)(2,1)S(1)}, u32[]{:S(2)}, u32[]{:S(2)}) collective-permute-start(bf16[8,3200]{1,0:T(8,128)(2,1)S(1)} %get-tuple-element.102), channel_id=1, source_target_pairs={{2,0},{3,1},{0,2},{1,3},{6,4},{7,5},{4,6},{5,7},{10,8},{11,9},{8,1... | collective-permute-start | bytes 153608 | tf_op jit(solution)/shard_map/ppermute | solution.py:111
  89.0 1.4 %collective-permute-start.28 = (bf16[8,3200]{1,0:T(8,128)(2,1)S(1)}, bf16[8,3200]{1,0:T(8,128)(2,1)S(1)}, u32[]{:S(2)}, u32[]{:S(2)}) collective-permute-start(bf16[8,3200]{1,0:T(8,128)(2,1)S(1)} %get-tuple-element.101), channel_id=1, source_target_pairs={{3,0},{2,1},{1,2},{0,3},{7,4},{6,5},{5,6},{4,7},{11,8},{10,9},{9,1... | collective-permute-start | bytes 153608 | tf_op jit(solution)/shard_map/ppermute | solution.py:111
  91.2 0.7 collective-permute-done.27
  91.9 3.0 %collective-permute-done.28 = bf16[8,3200]{1,0:T(8,128)(2,1)S(1)} collective-permute-done((bf16[8,3200]{1,0:T(8,128)(2,1)S(1)}, bf16[8,3200]{1,0:T(8,128)(2,1)S(1)}, u32[]{:S(2)}, u32[]{:S(2)}) %collective-permute-start.28) | collective-permute-done | bytes 51232 | tf_op jit(solution)/shard_map/ppermute | solution.py:111
  95.2 0.6 pad_maximum_fusion.14
  95.8 0.9 fusion.3
  (105 shorter events, 7.3 us)
Async XLA Ops:
  0.6 8.1 %copy-start = (bf16[6144,4]{0,1:T(4,128)(2,1)S(1)}, bf16[6144,4]{0,1:T(4,128)(2,1)}, u32[]{:S(2)}) copy-start(bf16[6144,4]{0,1:T(4,128)(2,1)} %param.12) | copy-start | bytes 147460
  0.6 16.9 %copy-start.1 = (bf16[8,6144]{1,0:T(8,128)(2,1)S(1)}, bf16[8,6144]{1,0:T(8,128)(2,1)}, u32[]{:S(2)}) copy-start(bf16[8,6144]{1,0:T(8,128)(2,1)} %param.9) | copy-start | bytes 294916
  0.7 9.4 %collective-permute-start = (bf16[8,6144]{1,0:T(8,128)(2,1)}, bf16[8,6144]{1,0:T(8,128)(2,1)S(1)}, u32[]{:S(2)}, u32[]{:S(2)}) collective-permute-start(bf16[8,6144]{1,0:T(8,128)(2,1)} %param.8), channel_id=1, source_target_pairs={{1,0},{0,1},{3,2},{2,3},{5,4},{4,5},{7,6},{6,7},{9,8},{8,9},{11,10... | collective-permute-start | bytes 294920 | tf_op jit(solution)/shard_map/ppermute | solution.py:111
  3.7 10.6 %collective-permute-start.4 = (bf16[8,6144]{1,0:T(8,128)(2,1)}, bf16[8,6144]{1,0:T(8,128)(2,1)S(1)}, u32[]{:S(2)}, u32[]{:S(2)}) collective-permute-start(bf16[8,6144]{1,0:T(8,128)(2,1)} %param.8), channel_id=1, source_target_pairs={{2,0},{3,1},{0,2},{1,3},{6,4},{7,5},{4,6},{5,7},{10,8},{11,9},{8,1... | collective-permute-start | bytes 294920 | tf_op jit(solution)/shard_map/ppermute | solution.py:111
  6.3 8.1 %collective-permute-start.5 = (bf16[8,6144]{1,0:T(8,128)(2,1)}, bf16[8,6144]{1,0:T(8,128)(2,1)S(1)}, u32[]{:S(2)}, u32[]{:S(2)}) collective-permute-start(bf16[8,6144]{1,0:T(8,128)(2,1)} %param.8), channel_id=1, source_target_pairs={{3,0},{2,1},{1,2},{0,3},{7,4},{6,5},{5,6},{4,7},{11,8},{10,9},{9,1... | collective-permute-start | bytes 294920 | tf_op jit(solution)/shard_map/ppermute | solution.py:111
  14.5 10.4 %collective-permute-start.6 = (bf16[32,3072]{1,0:T(8,128)(2,1)S(1)}, bf16[32,3072]{1,0:T(8,128)(2,1)S(1)}, u32[]{:S(2)}, u32[]{:S(2)}) collective-permute-start(bf16[32,3072]{1,0:T(8,128)(2,1)S(1)} %get-tuple-element.40._), channel_id=1, source_target_pairs={{16,0},{0,16},{17,1},{1,17},{18,2},{2,18},{19,3},{3,19},{20,4},{4,... | collective-permute-start | bytes 589832 | tf_op jit(solution)/shard_map/ppermute | solution.py:111
  16.0 8.8 %collective-permute-start.7 = (bf16[32,3072]{1,0:T(8,128)(2,1)S(1)}, bf16[32,3072]{1,0:T(8,128)(2,1)S(1)}, u32[]{:S(2)}, u32[]{:S(2)}) collective-permute-start(bf16[32,3072]{1,0:T(8,128)(2,1)S(1)} %get-tuple-element.42), channel_id=1, source_target_pairs={{8,0},{12,4},{0,8},{4,12},{9,1},{13,5},{1,9},{5,13},{10,2},{14,6},... | collective-permute-start | bytes 589832 | tf_op jit(solution)/shard_map/ppermute | solution.py:111
  17.6 8.5 %collective-permute-start.1 = (bf16[8,6272]{1,0:T(8,128)(2,1)S(1)}, bf16[8,6272]{1,0:T(8,128)(2,1)S(1)}, u32[]{:S(2)}, u32[]{:S(2)}) collective-permute-start(bf16[8,6272]{1,0:T(8,128)(2,1)S(1)} %fusion.4), channel_id=1, source_target_pairs={{1,0},{0,1},{3,2},{2,3},{5,4},{4,5},{7,6},{6,7},{9,8},{8,9},{11,10... | collective-permute-start | bytes 301064 | tf_op jit(solution)/shard_map/ppermute | solution.py:111
  19.2 8.9 %collective-permute-start.2 = (bf16[8,6272]{1,0:T(8,128)(2,1)S(1)}, bf16[8,6272]{1,0:T(8,128)(2,1)S(1)}, u32[]{:S(2)}, u32[]{:S(2)}) collective-permute-start(bf16[8,6272]{1,0:T(8,128)(2,1)S(1)} %fusion.4), channel_id=1, source_target_pairs={{2,0},{3,1},{0,2},{1,3},{6,4},{7,5},{4,6},{5,7},{10,8},{11,9},{8,1... | collective-permute-start | bytes 301064 | tf_op jit(solution)/shard_map/ppermute | solution.py:111
  20.6 7.4 %collective-permute-start.3 = (bf16[8,6272]{1,0:T(8,128)(2,1)S(1)}, bf16[8,6272]{1,0:T(8,128)(2,1)S(1)}, u32[]{:S(2)}, u32[]{:S(2)}) collective-permute-start(bf16[8,6272]{1,0:T(8,128)(2,1)S(1)} %fusion.4), channel_id=1, source_target_pairs={{3,0},{2,1},{1,2},{0,3},{7,4},{6,5},{5,6},{4,7},{11,8},{10,9},{9,1... | collective-permute-start | bytes 301064 | tf_op jit(solution)/shard_map/ppermute | solution.py:111
  24.9 10.5 %collective-permute-start.11 = (bf16[64,3072]{1,0:T(8,128)(2,1)S(1)}, bf16[64,3072]{1,0:T(8,128)(2,1)S(1)}, u32[]{:S(2)}, u32[]{:S(2)}) collective-permute-start(bf16[64,3072]{1,0:T(8,128)(2,1)S(1)} %pad_maximum_fusion.10), channel_id=1, source_target_pairs={{16,0},{0,16},{17,1},{1,17},{18,2},{2,18},{19,3},{3,19},{20,4},{4,... | collective-permute-start | bytes 1179656 | tf_op jit(solution)/shard_map/ppermute | solution.py:111
  25.5 10.1 %collective-permute-start.10 = (bf16[64,3072]{1,0:T(8,128)(2,1)S(1)}, bf16[64,3072]{1,0:T(8,128)(2,1)S(1)}, u32[]{:S(2)}, u32[]{:S(2)}) collective-permute-start(bf16[64,3072]{1,0:T(8,128)(2,1)S(1)} %pad_maximum_fusion.9), channel_id=1, source_target_pairs={{8,0},{12,4},{0,8},{4,12},{9,1},{13,5},{1,9},{5,13},{10,2},{14,6},... | collective-permute-start | bytes 1179656 | tf_op jit(solution)/shard_map/ppermute | solution.py:111
  31.0 6.7 %collective-permute-start.9 = (bf16[32,3072]{1,0:T(8,128)(2,1)S(1)}, bf16[32,3072]{1,0:T(8,128)(2,1)S(1)}, u32[]{:S(2)}, u32[]{:S(2)}) collective-permute-start(bf16[32,3072]{1,0:T(8,128)(2,1)S(1)} %get-tuple-element.50), channel_id=1, source_target_pairs={{8,0},{12,4},{0,8},{4,12},{9,1},{13,5},{1,9},{5,13},{10,2},{14,6},... | collective-permute-start | bytes 589832 | tf_op jit(solution)/shard_map/ppermute | solution.py:111
  31.6 6.1 %collective-permute-start.8 = (bf16[32,3200]{1,0:T(8,128)(2,1)S(1)}, bf16[32,3200]{1,0:T(8,128)(2,1)S(1)}, u32[]{:S(2)}, u32[]{:S(2)}) collective-permute-start(bf16[32,3200]{1,0:T(8,128)(2,1)S(1)} %slice.98), channel_id=1, source_target_pairs={{16,0},{0,16},{17,1},{1,17},{18,2},{2,18},{19,3},{3,19},{20,4},{4,... | collective-permute-start | bytes 614408 | tf_op jit(solution)/shard_map/ppermute | solution.py:111
  35.7 4.3 %collective-permute-start.15 = (bf16[128,3072]{1,0:T(8,128)(2,1)S(1)}, bf16[128,3072]{1,0:T(8,128)(2,1)S(1)}, u32[]{:S(2)}, u32[]{:S(2)}) collective-permute-start(bf16[128,3072]{1,0:T(8,128)(2,1)S(1)} %pad_maximum_fusion.4), channel_id=1, source_target_pairs={{4,0},{0,4},{12,8},{8,12},{5,1},{1,5},{13,9},{9,13},{6,2},{2,6},{1... | collective-permute-start | bytes 2359304 | tf_op jit(solution)/shard_map/ppermute | solution.py:111
  35.9 4.2 %collective-permute-start.14 = (bf16[128,3072]{1,0:T(8,128)(2,1)S(1)}, bf16[128,3072]{1,0:T(8,128)(2,1)S(1)}, u32[]{:S(2)}, u32[]{:S(2)}) collective-permute-start(bf16[128,3072]{1,0:T(8,128)(2,1)S(1)} %pad_maximum_fusion.3), channel_id=1, source_target_pairs={{4,0},{0,4},{12,8},{8,12},{5,1},{1,5},{13,9},{9,13},{6,2},{2,6},{1... | collective-permute-start | bytes 2359304 | tf_op jit(solution)/shard_map/ppermute | solution.py:111
  37.8 9.8 %collective-permute-start.13 = (bf16[64,3072]{1,0:T(8,128)(2,1)S(1)}, bf16[64,3072]{1,0:T(8,128)(2,1)S(1)}, u32[]{:S(2)}, u32[]{:S(2)}) collective-permute-start(bf16[64,3072]{1,0:T(8,128)(2,1)S(1)} %pad_maximum_fusion.11), channel_id=1, source_target_pairs={{16,0},{0,16},{17,1},{1,17},{18,2},{2,18},{19,3},{3,19},{20,4},{4,... | collective-permute-start | bytes 1179656 | tf_op jit(solution)/shard_map/ppermute | solution.py:111
  39.3 9.9 %collective-permute-start.12 = (bf16[64,3200]{1,0:T(8,128)(2,1)S(1)}, bf16[64,3200]{1,0:T(8,128)(2,1)S(1)}, u32[]{:S(2)}, u32[]{:S(2)}) collective-permute-start(bf16[64,3200]{1,0:T(8,128)(2,1)S(1)} %pad_maximum_fusion.7), channel_id=1, source_target_pairs={{8,0},{12,4},{0,8},{4,12},{9,1},{13,5},{1,9},{5,13},{10,2},{14,6},... | collective-permute-start | bytes 1228808 | tf_op jit(solution)/shard_map/ppermute | solution.py:111
  49.4 3.1 %collective-permute-start.17 = (bf16[128,3072]{1,0:T(8,128)(2,1)S(1)}, bf16[128,3072]{1,0:T(8,128)(2,1)S(1)}, u32[]{:S(2)}, u32[]{:S(2)}) collective-permute-start(bf16[128,3072]{1,0:T(8,128)(2,1)S(1)} %pad_maximum_fusion.5), channel_id=1, source_target_pairs={{4,0},{0,4},{12,8},{8,12},{5,1},{1,5},{13,9},{9,13},{6,2},{2,6},{1... | collective-permute-start | bytes 2359304 | tf_op jit(solution)/shard_map/ppermute | solution.py:111
  49.5 3.4 %collective-permute-start.16 = (bf16[128,3200]{1,0:T(8,128)(2,1)S(1)}, bf16[128,3200]{1,0:T(8,128)(2,1)S(1)}, u32[]{:S(2)}, u32[]{:S(2)}) collective-permute-start(bf16[128,3200]{1,0:T(8,128)(2,1)S(1)} %pad_maximum_fusion.2), channel_id=1, source_target_pairs={{4,0},{0,4},{12,8},{8,12},{5,1},{1,5},{13,9},{9,13},{6,2},{2,6},{1... | collective-permute-start | bytes 2457608 | tf_op jit(solution)/shard_map/ppermute | solution.py:111
  61.6 4.5 %collective-permute-start.21 = (bf16[128,3072]{1,0:T(8,128)(2,1)S(1)}, bf16[128,3072]{1,0:T(8,128)(2,1)S(1)}, u32[]{:S(2)}, u32[]{:S(2)}) collective-permute-start(bf16[128,3072]{1,0:T(8,128)(2,1)S(1)} %get-tuple-element.70), channel_id=1, source_target_pairs={{4,0},{0,4},{12,8},{8,12},{5,1},{1,5},{13,9},{9,13},{6,2},{2,6},{1... | collective-permute-start | bytes 2359304 | tf_op jit(solution)/shard_map/ppermute | solution.py:111
  65.6 2.4 %collective-permute-start.18 = (bf16[128,3200]{1,0:T(8,128)(2,1)S(1)}, bf16[128,3200]{1,0:T(8,128)(2,1)S(1)}, u32[]{:S(2)}, u32[]{:S(2)}) collective-permute-start(bf16[128,3200]{1,0:T(8,128)(2,1)S(1)} %get-tuple-element.69), channel_id=1, source_target_pairs={{4,0},{0,4},{12,8},{8,12},{5,1},{1,5},{13,9},{9,13},{6,2},{2,6},{1... | collective-permute-start | bytes 2457608 | tf_op jit(solution)/shard_map/ppermute | solution.py:111
  66.4 7.8 %collective-permute-start.25 = (bf16[64,1536]{1,0:T(8,128)(2,1)S(1)}, bf16[64,1536]{1,0:T(8,128)(2,1)S(1)}, u32[]{:S(2)}, u32[]{:S(2)}) collective-permute-start(bf16[64,1536]{1,0:T(8,128)(2,1)S(1)} %pad_maximum_fusion.13), channel_id=1, source_target_pairs={{16,0},{0,16},{17,1},{1,17},{18,2},{2,18},{19,3},{3,19},{20,4},{4,... | collective-permute-start | bytes 589832 | tf_op jit(solution)/shard_map/ppermute | solution.py:111
  67.0 7.9 %collective-permute-start.24 = (bf16[64,1536]{1,0:T(8,128)(2,1)S(1)}, bf16[64,1536]{1,0:T(8,128)(2,1)S(1)}, u32[]{:S(2)}, u32[]{:S(2)}) collective-permute-start(bf16[64,1536]{1,0:T(8,128)(2,1)S(1)} %concatenate.112), channel_id=1, source_target_pairs={{8,0},{12,4},{0,8},{4,12},{9,1},{13,5},{1,9},{5,13},{10,2},{14,6},... | collective-permute-start | bytes 589832 | tf_op jit(solution)/shard_map/ppermute | solution.py:111
  68.4 10.6 %collective-permute-start.20 = (bf16[64,1664]{1,0:T(8,128)(2,1)S(1)}, bf16[64,1664]{1,0:T(8,128)(2,1)S(1)}, u32[]{:S(2)}, u32[]{:S(2)}) collective-permute-start(bf16[64,1664]{1,0:T(8,128)(2,1)S(1)} %pad_maximum_fusion.12), channel_id=1, source_target_pairs={{16,0},{0,16},{17,1},{1,17},{18,2},{2,18},{19,3},{3,19},{20,4},{4,... | collective-permute-start | bytes 638984 | tf_op jit(solution)/shard_map/ppermute | solution.py:111
  69.4 9.5 %collective-permute-start.19 = (bf16[64,1536]{1,0:T(8,128)(2,1)S(1)}, bf16[64,1536]{1,0:T(8,128)(2,1)S(1)}, u32[]{:S(2)}, u32[]{:S(2)}) collective-permute-start(bf16[64,1536]{1,0:T(8,128)(2,1)S(1)} %concatenate.110), channel_id=1, source_target_pairs={{8,0},{12,4},{0,8},{4,12},{9,1},{13,5},{1,9},{5,13},{10,2},{14,6},... | collective-permute-start | bytes 589832 | tf_op jit(solution)/shard_map/ppermute | solution.py:111
  74.3 6.9 %collective-permute-start.30 = (bf16[32,1536]{1,0:T(8,128)(2,1)S(1)}, bf16[32,1536]{1,0:T(8,128)(2,1)S(1)}, u32[]{:S(2)}, u32[]{:S(2)}) collective-permute-start(bf16[32,1536]{1,0:T(8,128)(2,1)S(1)} %split.121), channel_id=1, source_target_pairs={{8,0},{12,4},{0,8},{4,12},{9,1},{13,5},{1,9},{5,13},{10,2},{14,6},... | collective-permute-start | bytes 294920 | tf_op jit(solution)/shard_map/ppermute | solution.py:111
  74.9 6.3 %collective-permute-start.29 = (bf16[32,1536]{1,0:T(8,128)(2,1)S(1)}, bf16[32,1536]{1,0:T(8,128)(2,1)S(1)}, u32[]{:S(2)}, u32[]{:S(2)}) collective-permute-start(bf16[32,1536]{1,0:T(8,128)(2,1)S(1)} %split.122), channel_id=1, source_target_pairs={{16,0},{0,16},{17,1},{1,17},{18,2},{2,18},{19,3},{3,19},{20,4},{4,... | collective-permute-start | bytes 294920 | tf_op jit(solution)/shard_map/ppermute | solution.py:111
  79.0 6.7 %collective-permute-start.22 = (bf16[32,1536]{1,0:T(8,128)(2,1)S(1)}, bf16[32,1536]{1,0:T(8,128)(2,1)S(1)}, u32[]{:S(2)}, u32[]{:S(2)}) collective-permute-start(bf16[32,1536]{1,0:T(8,128)(2,1)S(1)} %split.123), channel_id=1, source_target_pairs={{16,0},{0,16},{17,1},{1,17},{18,2},{2,18},{19,3},{3,19},{20,4},{4,... | collective-permute-start | bytes 294920 | tf_op jit(solution)/shard_map/ppermute | solution.py:111
  80.6 5.2 %collective-permute-start.23 = (bf16[32,1664]{1,0:T(8,128)(2,1)S(1)}, bf16[32,1664]{1,0:T(8,128)(2,1)S(1)}, u32[]{:S(2)}, u32[]{:S(2)}) collective-permute-start(bf16[32,1664]{1,0:T(8,128)(2,1)S(1)} %split.120), channel_id=1, source_target_pairs={{8,0},{12,4},{0,8},{4,12},{9,1},{13,5},{1,9},{5,13},{10,2},{14,6},... | collective-permute-start | bytes 319496 | tf_op jit(solution)/shard_map/ppermute | solution.py:111
  81.3 7.7 %collective-permute-start.31 = (bf16[8,3072]{1,0:T(8,128)(2,1)S(1)}, bf16[8,3072]{1,0:T(8,128)(2,1)S(1)}, u32[]{:S(2)}, u32[]{:S(2)}) collective-permute-start(bf16[8,3072]{1,0:T(8,128)(2,1)S(1)} %get-tuple-element.103), channel_id=1, source_target_pairs={{1,0},{0,1},{3,2},{2,3},{5,4},{4,5},{7,6},{6,7},{9,8},{8,9},{11,10... | collective-permute-start | bytes 147464 | tf_op jit(solution)/shard_map/ppermute | solution.py:111
  82.3 8.1 %collective-permute-start.32 = (bf16[8,3072]{1,0:T(8,128)(2,1)S(1)}, bf16[8,3072]{1,0:T(8,128)(2,1)S(1)}, u32[]{:S(2)}, u32[]{:S(2)}) collective-permute-start(bf16[8,3072]{1,0:T(8,128)(2,1)S(1)} %get-tuple-element.105), channel_id=1, source_target_pairs={{2,0},{3,1},{0,2},{1,3},{6,4},{7,5},{4,6},{5,7},{10,8},{11,9},{8,1... | collective-permute-start | bytes 147464 | tf_op jit(solution)/shard_map/ppermute | solution.py:111
  84.4 6.3 %collective-permute-start.33 = (bf16[8,3072]{1,0:T(8,128)(2,1)S(1)}, bf16[8,3072]{1,0:T(8,128)(2,1)S(1)}, u32[]{:S(2)}, u32[]{:S(2)}) collective-permute-start(bf16[8,3072]{1,0:T(8,128)(2,1)S(1)} %get-tuple-element.104), channel_id=1, source_target_pairs={{3,0},{2,1},{1,2},{0,3},{7,4},{6,5},{5,6},{4,7},{11,8},{10,9},{9,1... | collective-permute-start | bytes 147464 | tf_op jit(solution)/shard_map/ppermute | solution.py:111
  85.8 9.3 %copy-start.2 = (s32[8]{0:T(128)S(1)}, s32[8]{0:T(128)}, u32[]{:S(2)}) copy-start(s32[8]{0:T(128)} %param.10) | copy-start | bytes 100
  85.9 5.3 %collective-permute-start.26 = (bf16[8,3200]{1,0:T(8,128)(2,1)S(1)}, bf16[8,3200]{1,0:T(8,128)(2,1)S(1)}, u32[]{:S(2)}, u32[]{:S(2)}) collective-permute-start(bf16[8,3200]{1,0:T(8,128)(2,1)S(1)} %get-tuple-element.100), channel_id=1, source_target_pairs={{1,0},{0,1},{3,2},{2,3},{5,4},{4,5},{7,6},{6,7},{9,8},{8,9},{11,10... | collective-permute-start | bytes 153608 | tf_op jit(solution)/shard_map/ppermute | solution.py:111
  86.5 5.4 %collective-permute-start.27 = (bf16[8,3200]{1,0:T(8,128)(2,1)S(1)}, bf16[8,3200]{1,0:T(8,128)(2,1)S(1)}, u32[]{:S(2)}, u32[]{:S(2)}) collective-permute-start(bf16[8,3200]{1,0:T(8,128)(2,1)S(1)} %get-tuple-element.102), channel_id=1, source_target_pairs={{2,0},{3,1},{0,2},{1,3},{6,4},{7,5},{4,6},{5,7},{10,8},{11,9},{8,1... | collective-permute-start | bytes 153608 | tf_op jit(solution)/shard_map/ppermute | solution.py:111
  89.0 5.9 %collective-permute-start.28 = (bf16[8,3200]{1,0:T(8,128)(2,1)S(1)}, bf16[8,3200]{1,0:T(8,128)(2,1)S(1)}, u32[]{:S(2)}, u32[]{:S(2)}) collective-permute-start(bf16[8,3200]{1,0:T(8,128)(2,1)S(1)} %get-tuple-element.101), channel_id=1, source_target_pairs={{3,0},{2,1},{1,2},{0,3},{7,4},{6,5},{5,6},{4,7},{11,8},{10,9},{9,1... | collective-permute-start | bytes 153608 | tf_op jit(solution)/shard_map/ppermute | solution.py:111

commit v16 on v13

--- a/solution.py
+++ b/solution.py
@@ -395,14 +395,13 @@
     gate_table = (first_hot * gate_first[:, None] + second_hot * gate_second[:, None]) * keep_rows[:, None]
     gate_table = jnp.pad(gate_table.astype(jnp.bfloat16), ((0, 0), (0, table - expert_count)))
     grad_z = gather_z(after_others(jnp.concatenate([gate_table, out_grad], axis=1), token_z[1]))
-    token_near = gather_near(token_z, half)
-    (gate_low,) = fetch(0, half, token_near[0][0], gate_weight)
-    token_near = after_others(token_near, gate_low)
+    token_near = lax.optimization_barrier(gather_near(token_z, half))
     token_far = gather_far(*token_near)
+    (gate_low,) = fetch(0, half, token_near[1][1], gate_weight)
     (up_low,) = fetch(0, half, token_near[1][1], up_weight)
-    grad_near = gather_near(after_others(grad_z, token_near), half + table)
+    grad_near = gather_near(after_others(grad_z, gate_low), half + table)
     grad_far = gather_far(*after_others(grad_near, token_far))
-    token_far = after_others(token_far, up_low)
+    token_far = after_others(token_far, (gate_low, up_low))
     token_low, token_high = gather_core(token_near[0], token_far[0], token_near[1], token_far[1])
     pre_gate, pre_up, gate_high, up_high = multiply_tokens(
         token_low, gate_low, up_low, 0, half, (), ((gate_weight, half, half), (up_weight, half, half))

time: 97 us -> 95.8 us (0.988)
  waiting for transfers between devices: 24 us -> 22.7 us
    ppermute x34, waiting for transfers between devices: 24 us -> 22.7 us  [swap(): lax.ppermute(value, axis, [(i ^ bit, i) for i in range(lax.axis_size(axis...]
  transfers between devices with their start and end apart: 34 -> 34, of which waited for: 14 -> 10; matrix products, arithmetic and copies ran while one was open for 6% -> 6% of each run, Pallas kernels for 20% -> 20%
where the time goes in v16:
time: 95.8 us; the launch traced here: 95.4 us
  starting transfers between devices  36.2 us (38%)
  Pallas kernels  27.7 us (29%)
  waiting for transfers between devices  22.7 us (24%)
  other arithmetic  3 us (3%)
  local copies, waits for them, and re-layouts  2.37 us (2%)
  matrix products  2.15 us (2%)
  between operations  1.27 us (1%)
    ppermute x34, starting transfers between devices, swap(): lax.ppermute(value, axis, [(i ^ bit, i) for i in range(lax.axis_size(axis...  36.2 us
    ppermute x34, waiting for transfers between devices, swap(): lax.ppermute(value, axis, [(i ^ bit, i) for i in range(lax.axis_size(axis...  22.7 us
    pallas_call x3, Pallas kernels, multiply_tokens(): pl.pallas_call(functools.partial(token_kernel, offset, length, sources, l...  9.75 us
    pallas_call x2, Pallas kernels, multiply_outputs(): pl.pallas_call(output_kernel, out_shape=(pltpu.VMEM((rows // 2, total), j...  7.66 us
    pallas_call x2, Pallas kernels, fetch(): pl.pallas_call(functools.partial(fetch_kernel, first), out_shape=tuple((p...  5.59 us
    pallas_call x1, Pallas kernels, multiply_grads(): pl.pallas_call(grad_kernel, out_shape=(pltpu.VMEM((rows, hidden), jnp.bfl...  4.73 us
  transfers between devices with their start and end apart: 34, of which 10 were waited for; matrix products, arithmetic and copies ran while one was open for 6% of the time, Pallas kernels for 20%

profile of v16, /device:TPU:0, one launch (start us, length us, event | category | flops | bytes accessed | tf_op | source)
XLA Modules:
  0.0 95.4 jit_solution(5892331114153360785)
XLA Ops:
  0.7 3.1 %collective-permute-start = (bf16[8,6144]{1,0:T(8,128)(2,1)}, bf16[8,6144]{1,0:T(8,128)(2,1)S(1)}, u32[]{:S(2)}, u32[]{:S(2)}) collective-permute-start(bf16[8,6144]{1,0:T(8,128)(2,1)} %param.8), channel_id=1, source_target_pairs={{1,0},{0,1},{3,2},{2,3},{5,4},{4,5},{7,6},{6,7},{9,8},{8,9},{11,10... | collective-permute-start | bytes 294920 | tf_op jit(solution)/shard_map/ppermute | solution.py:111
  3.7 2.6 %collective-permute-start.4 = (bf16[8,6144]{1,0:T(8,128)(2,1)}, bf16[8,6144]{1,0:T(8,128)(2,1)S(1)}, u32[]{:S(2)}, u32[]{:S(2)}) collective-permute-start(bf16[8,6144]{1,0:T(8,128)(2,1)} %param.8), channel_id=1, source_target_pairs={{2,0},{3,1},{0,2},{1,3},{6,4},{7,5},{4,6},{5,7},{10,8},{11,9},{8,1... | collective-permute-start | bytes 294920 | tf_op jit(solution)/shard_map/ppermute | solution.py:111
  6.3 1.0 %constant_dynamic-update-slice_fusion.3 = bf16[32,6144]{1,0:T(8,128)(2,1)S(1)} fusion(bf16[8,6144]{1,0:T(8,128)(2,1)} %param.8), kind=kLoop, calls=%fused_computation.45 | loop fusion | bytes 196608
  7.3 0.8 slice_bitcast_fusion
  8.1 0.7 convert_element_type.76
  8.7 1.2 %select_reduce_fusion.3 = (f32[8]{0:T(128)S(1)}, f32[8]{0:T(128)S(1)}) fusion(s32[8]{0:T(128)S(1)} %get-tuple-element.111, s32[8]{0:T(128)S(1)} %get-tuple-element.110, bf16[8,6144]{1,0:T(8,128)(2,1)} %param.8, bf16[6144,4]{0,1:T(4,128)(2,1)S(1)} %copy-done), kind=kOutput, calls=%fused_computation.69 | convolution fusion | flops 393392 | bytes 147584 | tf_op jit(solution)/shard_map/dot_general | solution.py:390
  10.1 4.3 %collective-permute-done.4 = bf16[8,6144]{1,0:T(8,128)(2,1)S(1)} collective-permute-done((bf16[8,6144]{1,0:T(8,128)(2,1)}, bf16[8,6144]{1,0:T(8,128)(2,1)S(1)}, u32[]{:S(2)}, u32[]{:S(2)}) %collective-permute-start.4) | collective-permute-done | bytes 98336 | tf_op jit(solution)/shard_map/ppermute | solution.py:111
  14.5 1.6 %collective-permute-start.6 = (bf16[32,3072]{1,0:T(8,128)(2,1)S(1)}, bf16[32,3072]{1,0:T(8,128)(2,1)S(1)}, u32[]{:S(2)}, u32[]{:S(2)}) collective-permute-start(bf16[32,3072]{1,0:T(8,128)(2,1)S(1)} %get-tuple-element.45), channel_id=1, source_target_pairs={{16,0},{0,16},{17,1},{1,17},{18,2},{2,18},{19,3},{3,19},{20,4},{4,... | collective-permute-start | bytes 589832 | tf_op jit(solution)/shard_map/ppermute | solution.py:111
  16.0 1.5 %collective-permute-start.7 = (bf16[32,3072]{1,0:T(8,128)(2,1)S(1)}, bf16[32,3072]{1,0:T(8,128)(2,1)S(1)}, u32[]{:S(2)}, u32[]{:S(2)}) collective-permute-start(bf16[32,3072]{1,0:T(8,128)(2,1)S(1)} %get-tuple-element.47), channel_id=1, source_target_pairs={{8,0},{12,4},{0,8},{4,12},{9,1},{13,5},{1,9},{5,13},{10,2},{14,6},... | collective-permute-start | bytes 589832 | tf_op jit(solution)/shard_map/ppermute | solution.py:111
  17.6 1.7 %collective-permute-start.1 = (bf16[8,6272]{1,0:T(8,128)(2,1)S(1)}, bf16[8,6272]{1,0:T(8,128)(2,1)S(1)}, u32[]{:S(2)}, u32[]{:S(2)}) collective-permute-start(bf16[8,6272]{1,0:T(8,128)(2,1)S(1)} %fusion.4), channel_id=1, source_target_pairs={{1,0},{0,1},{3,2},{2,3},{5,4},{4,5},{7,6},{6,7},{9,8},{8,9},{11,10... | collective-permute-start | bytes 301064 | tf_op jit(solution)/shard_map/ppermute | solution.py:111
  19.2 1.4 %collective-permute-start.2 = (bf16[8,6272]{1,0:T(8,128)(2,1)S(1)}, bf16[8,6272]{1,0:T(8,128)(2,1)S(1)}, u32[]{:S(2)}, u32[]{:S(2)}) collective-permute-start(bf16[8,6272]{1,0:T(8,128)(2,1)S(1)} %fusion.4), channel_id=1, source_target_pairs={{2,0},{3,1},{0,2},{1,3},{6,4},{7,5},{4,6},{5,7},{10,8},{11,9},{8,1... | collective-permute-start | bytes 301064 | tf_op jit(solution)/shard_map/ppermute | solution.py:111
  20.6 1.4 %collective-permute-start.3 = (bf16[8,6272]{1,0:T(8,128)(2,1)S(1)}, bf16[8,6272]{1,0:T(8,128)(2,1)S(1)}, u32[]{:S(2)}, u32[]{:S(2)}) collective-permute-start(bf16[8,6272]{1,0:T(8,128)(2,1)S(1)} %fusion.4), channel_id=1, source_target_pairs={{3,0},{2,1},{1,2},{0,3},{7,4},{6,5},{5,6},{4,7},{11,8},{10,9},{9,1... | collective-permute-start | bytes 301064 | tf_op jit(solution)/shard_map/ppermute | solution.py:111
  22.1 0.6 collective-permute-start.11
  22.7 1.3 %collective-permute-start.10 = (bf16[64,3072]{1,0:T(8,128)(2,1)S(1)}, bf16[64,3072]{1,0:T(8,128)(2,1)S(1)}, u32[]{:S(2)}, u32[]{:S(2)}) collective-permute-start(bf16[64,3072]{1,0:T(8,128)(2,1)S(1)} %pad_maximum_fusion.9), channel_id=1, source_target_pairs={{8,0},{12,4},{0,8},{4,12},{9,1},{13,5},{1,9},{5,13},{10,2},{14,6},... | collective-permute-start | bytes 1179656 | tf_op jit(solution)/shard_map/ppermute | solution.py:111
  23.9 2.8 %shard_map.95.gate.gate_copy = bf16[3072,1024]{1,0:T(8,128)(2,1)S(1)} custom-call(bf16[32,3072]{1,0:T(8,128)(2,1)S(1)} %collective-permute-done.7._, bf16[1,6144,1024]{2,1,0:T(8,128)(2,1)} %refs_0_.5), custom_call_target="tpu_custom_call" | custom-call | bytes 6291456 | tf_op jit(solution)/shard_map/pallas_call | solution.py:210
  26.8 1.3 %collective-permute-done.2 = bf16[8,6272]{1,0:T(8,128)(2,1)S(1)} collective-permute-done((bf16[8,6272]{1,0:T(8,128)(2,1)S(1)}, bf16[8,6272]{1,0:T(8,128)(2,1)S(1)}, u32[]{:S(2)}, u32[]{:S(2)}) %collective-permute-start.2) | collective-permute-done | bytes 100384 | tf_op jit(solution)/shard_map/ppermute | solution.py:111
  28.2 2.8 %shard_map.96.up.up_copy = bf16[3072,1024]{1,0:T(8,128)(2,1)S(1)} custom-call(bf16[32,3072]{1,0:T(8,128)(2,1)S(1)} %collective-permute-done.7._, bf16[1,6144,1024]{2,1,0:T(8,128)(2,1)} %refs_1_.1), custom_call_target="tpu_custom_call" | custom-call | bytes 6291456 | tf_op jit(solution)/shard_map/pallas_call | solution.py:210
  31.0 0.6 collective-permute-start.9
  33.0 3.8 %collective-permute-done.9 = bf16[32,3072]{1,0:T(8,128)(2,1)S(1)} collective-permute-done((bf16[32,3072]{1,0:T(8,128)(2,1)S(1)}, bf16[32,3072]{1,0:T(8,128)(2,1)S(1)}, u32[]{:S(2)}, u32[]{:S(2)}) %collective-permute-start.9) | collective-permute-done | bytes 196640 | tf_op jit(solution)/shard_map/ppermute | solution.py:111
  36.7 1.9 %collective-permute-done.8 = bf16[32,3200]{1,0:T(8,128)(2,1)S(1)} collective-permute-done((bf16[32,3200]{1,0:T(8,128)(2,1)S(1)}, bf16[32,3200]{1,0:T(8,128)(2,1)S(1)}, u32[]{:S(2)}, u32[]{:S(2)}) %collective-permute-start.8) | collective-permute-done | bytes 204832 | tf_op jit(solution)/shard_map/ppermute | solution.py:111
  38.8 1.7 %collective-permute-start.12 = (bf16[64,3200]{1,0:T(8,128)(2,1)S(1)}, bf16[64,3200]{1,0:T(8,128)(2,1)S(1)}, u32[]{:S(2)}, u32[]{:S(2)}) collective-permute-start(bf16[64,3200]{1,0:T(8,128)(2,1)S(1)} %pad_maximum_fusion.7), channel_id=1, source_target_pairs={{8,0},{12,4},{0,8},{4,12},{9,1},{13,5},{1,9},{5,13},{10,2},{14,6},... | collective-permute-start | bytes 1228808 | tf_op jit(solution)/shard_map/ppermute | solution.py:111
  40.7 4.7 %shard_map.97 = (f32[256,1024]{1,0:T(8,128)S(1)}, f32[256,1024]{1,0:T(8,128)S(1)}, bf16[3072,1024]{1,0:T(8,128)(2,1)S(1)}, bf16[3072,1024]{1,0:T(8,128)(2,1)S(1)}) custom-call(bf16[256,3072]{1,0:T(8,128)(2,1)S(1)} %pad_maximum_fusion.1.tokens, bf16[3072,1024]{1,0:T(8,128)(2,1)S(1)} %shard_map.95.gate.gate_copy, bf16[3072,1024]{1,0:T(8,128)(2,1)S(1)} %shard_map.96.up.up_copy, ...), custom_call_target="tpu_custom_call" | custom-call | flops 3221225472 | bytes 1572864 | tf_op jit(solution)/shard_map/pallas_call | solution.py:253
  45.4 2.3 %shard_map.98 = (f32[256,1024]{1,0:T(8,128)S(1)}, f32[256,1024]{1,0:T(8,128)S(1)}) custom-call(bf16[256,3072]{1,0:T(8,128)(2,1)S(1)} %constant_dynamic-update-slice_fusion.8.tokens, bf16[3072,1024]{1,0:T(8,128)(2,1)S(1)} %get-tuple-element.54.gate.gate_copy, bf16[3072,1024]{1,0:T(8,128)(2,1)S(1)} %get-tuple-element.55.up.up_copy, ...), custom_call_target="tpu_custom_call" | custom-call | flops 1610612736 | bytes 786432 | tf_op jit(solution)/shard_map/pallas_call | solution.py:253
  47.9 0.6 collective-permute-start.16
  48.5 2.8 %shard_map.99 = (f32[256,1024]{1,0:T(8,128)S(1)}, f32[256,1024]{1,0:T(8,128)S(1)}, bf16[512,6144]{1,0:T(8,128)(2,1)S(1)}) custom-call(bf16[256,3072]{1,0:T(8,128)(2,1)S(1)} %constant_dynamic-update-slice_fusion.8.tokens, bf16[3072,1024]{1,0:T(8,128)(2,1)S(1)} %get-tuple-element.54.gate.gate_copy, bf16[3072,1024]{1,0:T(8,128)(2,1)S(1)} %get-tuple-element.55.up.up_copy, ...), custom_call_target="tpu_custom_call" | custom-call | flops 1610612736 | bytes 786432 | tf_op jit(solution)/shard_map/pallas_call | solution.py:253
  51.6 4.7 %shard_map.100 = (bf16[256,1024]{1,0:T(8,128)(2,1)S(1)}, bf16[256,1024]{1,0:T(8,128)(2,1)S(1)}, bf16[256,128]{1,0:T(8,128)(2,1)S(1)}) custom-call(s32[1]{0:T(128)} %bitcast.expert, bf16[256,3200]{1,0:T(8,128)(2,1)S(1)} %pad_maximum_fusion.low, bf16[256,3072]{1,0:T(8,128)(2,1)S(1)} %constant_dynamic-update-slice_fusion.13.high, ...), custom_call_target="tpu_custom_call" | custom-call | flops 3221225472 | bytes 6291456 | tf_op jit(solution)/shard_map/pallas_call | solution.py:319
  56.3 3.8 %shard_map.102 = (f32[128,3072]{1,0:T(8,128)S(1)}, bf16[128,3072]{1,0:T(8,128)(2,1)S(1)}) custom-call(bf16[256,1024]{1,0:T(8,128)(2,1)S(1)} %get-tuple-element.65.grad_gate, bf16[256,1024]{1,0:T(8,128)(2,1)S(1)} %get-tuple-element.66.grad_up, bf16[3072,1024]{1,0:T(8,128)(2,1)S(1)} %get-tuple-element.54.gate.gate_copy, ...), custom_call_target="tpu_custom_call" | custom-call | flops 3221225472 | bytes 3145728 | tf_op jit(solution)/shard_map/pallas_call | solution.py:365
  60.2 3.8 %shard_map.101 = (f32[128,3200]{1,0:T(8,128)S(1)}, bf16[128,3200]{1,0:T(8,128)(2,1)S(1)}) custom-call(bf16[256,1024]{1,0:T(8,128)(2,1)S(1)} %get-tuple-element.65.grad_gate, bf16[256,1024]{1,0:T(8,128)(2,1)S(1)} %get-tuple-element.66.grad_up, bf16[3072,1024]{1,0:T(8,128)(2,1)S(1)} %shard_map.95.gate.gate_copy, bf16[3072,1024]{1,0:T(8,128)(2,1)S(1)} %shard_map.96.up.up_copy, ...), custom_call_target="tpu_custom_call" | custom-call | flops 3221225472 | bytes 3145728 | tf_op jit(solution)/shard_map/pallas_call | solution.py:365
  64.9 2.1 %collective-permute-start.25 = (bf16[64,1536]{1,0:T(8,128)(2,1)S(1)}, bf16[64,1536]{1,0:T(8,128)(2,1)S(1)}, u32[]{:S(2)}, u32[]{:S(2)}) collective-permute-start(bf16[64,1536]{1,0:T(8,128)(2,1)S(1)} %pad_maximum_fusion.13), channel_id=1, source_target_pairs={{16,0},{0,16},{17,1},{1,17},{18,2},{2,18},{19,3},{3,19},{20,4},{4,... | collective-permute-start | bytes 589832 | tf_op jit(solution)/shard_map/ppermute | solution.py:111
  67.0 0.8 collective-permute-start.24
  68.1 0.9 collective-permute-start.20
  69.0 0.8 collective-permute-start.19
  69.8 3.0 %collective-permute-done.25 = bf16[64,1536]{1,0:T(8,128)(2,1)S(1)} collective-permute-done((bf16[64,1536]{1,0:T(8,128)(2,1)S(1)}, bf16[64,1536]{1,0:T(8,128)(2,1)S(1)}, u32[]{:S(2)}, u32[]{:S(2)}) %collective-permute-start.25) | collective-permute-done | bytes 196640 | tf_op jit(solution)/shard_map/ppermute | solution.py:111
  72.8 0.8 collective-permute-start.30
  73.6 1.2 %collective-permute-done.24 = bf16[64,1536]{1,0:T(8,128)(2,1)S(1)} collective-permute-done((bf16[64,1536]{1,0:T(8,128)(2,1)S(1)}, bf16[64,1536]{1,0:T(8,128)(2,1)S(1)}, u32[]{:S(2)}, u32[]{:S(2)}) %collective-permute-start.24) | collective-permute-done | bytes 196640 | tf_op jit(solution)/shard_map/ppermute | solution.py:111
  74.9 0.9 collective-permute-start.29
  75.8 3.0 %collective-permute-done.19 = bf16[64,1536]{1,0:T(8,128)(2,1)S(1)} collective-permute-done((bf16[64,1536]{1,0:T(8,128)(2,1)S(1)}, bf16[64,1536]{1,0:T(8,128)(2,1)S(1)}, u32[]{:S(2)}, u32[]{:S(2)}) %collective-permute-start.19) | collective-permute-done | bytes 196640 | tf_op jit(solution)/shard_map/ppermute | solution.py:111
  79.5 0.8 collective-permute-start.23
  80.4 1.3 %collective-permute-start.31 = (bf16[8,3072]{1,0:T(8,128)(2,1)S(1)}, bf16[8,3072]{1,0:T(8,128)(2,1)S(1)}, u32[]{:S(2)}, u32[]{:S(2)}) collective-permute-start(bf16[8,3072]{1,0:T(8,128)(2,1)S(1)} %get-tuple-element.103), channel_id=1, source_target_pairs={{1,0},{0,1},{3,2},{2,3},{5,4},{4,5},{7,6},{6,7},{9,8},{8,9},{11,10... | collective-permute-start | bytes 147464 | tf_op jit(solution)/shard_map/ppermute | solution.py:111
  81.7 1.4 %collective-permute-start.32 = (bf16[8,3072]{1,0:T(8,128)(2,1)S(1)}, bf16[8,3072]{1,0:T(8,128)(2,1)S(1)}, u32[]{:S(2)}, u32[]{:S(2)}) collective-permute-start(bf16[8,3072]{1,0:T(8,128)(2,1)S(1)} %get-tuple-element.105), channel_id=1, source_target_pairs={{2,0},{3,1},{0,2},{1,3},{6,4},{7,5},{4,6},{5,7},{10,8},{11,9},{8,1... | collective-permute-start | bytes 147464 | tf_op jit(solution)/shard_map/ppermute | solution.py:111
  83.1 1.7 %collective-permute-start.33 = (bf16[8,3072]{1,0:T(8,128)(2,1)S(1)}, bf16[8,3072]{1,0:T(8,128)(2,1)S(1)}, u32[]{:S(2)}, u32[]{:S(2)}) collective-permute-start(bf16[8,3072]{1,0:T(8,128)(2,1)S(1)} %get-tuple-element.104), channel_id=1, source_target_pairs={{3,0},{2,1},{1,2},{0,3},{7,4},{6,5},{5,6},{4,7},{11,8},{10,9},{9,1... | collective-permute-start | bytes 147464 | tf_op jit(solution)/shard_map/ppermute | solution.py:111
  85.5 2.3 %collective-permute-start.27 = (bf16[8,3200]{1,0:T(8,128)(2,1)S(1)}, bf16[8,3200]{1,0:T(8,128)(2,1)S(1)}, u32[]{:S(2)}, u32[]{:S(2)}) collective-permute-start(bf16[8,3200]{1,0:T(8,128)(2,1)S(1)} %get-tuple-element.102), channel_id=1, source_target_pairs={{2,0},{3,1},{0,2},{1,3},{6,4},{7,5},{4,6},{5,7},{10,8},{11,9},{8,1... | collective-permute-start | bytes 153608 | tf_op jit(solution)/shard_map/ppermute | solution.py:111
  87.7 1.7 %collective-permute-start.28 = (bf16[8,3200]{1,0:T(8,128)(2,1)S(1)}, bf16[8,3200]{1,0:T(8,128)(2,1)S(1)}, u32[]{:S(2)}, u32[]{:S(2)}) collective-permute-start(bf16[8,3200]{1,0:T(8,128)(2,1)S(1)} %get-tuple-element.101), channel_id=1, source_target_pairs={{3,0},{2,1},{1,2},{0,3},{7,4},{6,5},{5,6},{4,7},{11,8},{10,9},{9,1... | collective-permute-start | bytes 153608 | tf_op jit(solution)/shard_map/ppermute | solution.py:111
  89.5 0.6 collective-permute-done.26
  90.1 1.0 %collective-permute-done.27 = bf16[8,3200]{1,0:T(8,128)(2,1)S(1)} collective-permute-done((bf16[8,3200]{1,0:T(8,128)(2,1)S(1)}, bf16[8,3200]{1,0:T(8,128)(2,1)S(1)}, u32[]{:S(2)}, u32[]{:S(2)}) %collective-permute-start.27) | collective-permute-done | bytes 51232 | tf_op jit(solution)/shard_map/ppermute | solution.py:111
  91.1 2.6 %collective-permute-done.28 = bf16[8,3200]{1,0:T(8,128)(2,1)S(1)} collective-permute-done((bf16[8,3200]{1,0:T(8,128)(2,1)S(1)}, bf16[8,3200]{1,0:T(8,128)(2,1)S(1)}, u32[]{:S(2)}, u32[]{:S(2)}) %collective-permute-start.28) | collective-permute-done | bytes 51232 | tf_op jit(solution)/shard_map/ppermute | solution.py:111
  93.9 0.6 pad_maximum_fusion.14
  94.5 0.9 fusion.3
  (105 shorter events, 5.4 us)
Async XLA Ops:
  0.6 8.1 %copy-start = (bf16[6144,4]{0,1:T(4,128)(2,1)S(1)}, bf16[6144,4]{0,1:T(4,128)(2,1)}, u32[]{:S(2)}) copy-start(bf16[6144,4]{0,1:T(4,128)(2,1)} %param.12) | copy-start | bytes 147460
  0.6 16.9 %copy-start.1 = (bf16[8,6144]{1,0:T(8,128)(2,1)S(1)}, bf16[8,6144]{1,0:T(8,128)(2,1)}, u32[]{:S(2)}) copy-start(bf16[8,6144]{1,0:T(8,128)(2,1)} %param.9) | copy-start | bytes 294916
  0.7 9.4 %collective-permute-start = (bf16[8,6144]{1,0:T(8,128)(2,1)}, bf16[8,6144]{1,0:T(8,128)(2,1)S(1)}, u32[]{:S(2)}, u32[]{:S(2)}) collective-permute-start(bf16[8,6144]{1,0:T(8,128)(2,1)} %param.8), channel_id=1, source_target_pairs={{1,0},{0,1},{3,2},{2,3},{5,4},{4,5},{7,6},{6,7},{9,8},{8,9},{11,10... | collective-permute-start | bytes 294920 | tf_op jit(solution)/shard_map/ppermute | solution.py:111
  3.7 10.6 %collective-permute-start.4 = (bf16[8,6144]{1,0:T(8,128)(2,1)}, bf16[8,6144]{1,0:T(8,128)(2,1)S(1)}, u32[]{:S(2)}, u32[]{:S(2)}) collective-permute-start(bf16[8,6144]{1,0:T(8,128)(2,1)} %param.8), channel_id=1, source_target_pairs={{2,0},{3,1},{0,2},{1,3},{6,4},{7,5},{4,6},{5,7},{10,8},{11,9},{8,1... | collective-permute-start | bytes 294920 | tf_op jit(solution)/shard_map/ppermute | solution.py:111
  6.3 8.1 %collective-permute-start.5 = (bf16[8,6144]{1,0:T(8,128)(2,1)}, bf16[8,6144]{1,0:T(8,128)(2,1)S(1)}, u32[]{:S(2)}, u32[]{:S(2)}) collective-permute-start(bf16[8,6144]{1,0:T(8,128)(2,1)} %param.8), channel_id=1, source_target_pairs={{3,0},{2,1},{1,2},{0,3},{7,4},{6,5},{5,6},{4,7},{11,8},{10,9},{9,1... | collective-permute-start | bytes 294920 | tf_op jit(solution)/shard_map/ppermute | solution.py:111
  14.5 7.6 %collective-permute-start.6 = (bf16[32,3072]{1,0:T(8,128)(2,1)S(1)}, bf16[32,3072]{1,0:T(8,128)(2,1)S(1)}, u32[]{:S(2)}, u32[]{:S(2)}) collective-permute-start(bf16[32,3072]{1,0:T(8,128)(2,1)S(1)} %get-tuple-element.45), channel_id=1, source_target_pairs={{16,0},{0,16},{17,1},{1,17},{18,2},{2,18},{19,3},{3,19},{20,4},{4,... | collective-permute-start | bytes 589832 | tf_op jit(solution)/shard_map/ppermute | solution.py:111
  16.0 6.0 %collective-permute-start.7 = (bf16[32,3072]{1,0:T(8,128)(2,1)S(1)}, bf16[32,3072]{1,0:T(8,128)(2,1)S(1)}, u32[]{:S(2)}, u32[]{:S(2)}) collective-permute-start(bf16[32,3072]{1,0:T(8,128)(2,1)S(1)} %get-tuple-element.47), channel_id=1, source_target_pairs={{8,0},{12,4},{0,8},{4,12},{9,1},{13,5},{1,9},{5,13},{10,2},{14,6},... | collective-permute-start | bytes 589832 | tf_op jit(solution)/shard_map/ppermute | solution.py:111
  17.6 9.2 %collective-permute-start.1 = (bf16[8,6272]{1,0:T(8,128)(2,1)S(1)}, bf16[8,6272]{1,0:T(8,128)(2,1)S(1)}, u32[]{:S(2)}, u32[]{:S(2)}) collective-permute-start(bf16[8,6272]{1,0:T(8,128)(2,1)S(1)} %fusion.4), channel_id=1, source_target_pairs={{1,0},{0,1},{3,2},{2,3},{5,4},{4,5},{7,6},{6,7},{9,8},{8,9},{11,10... | collective-permute-start | bytes 301064 | tf_op jit(solution)/shard_map/ppermute | solution.py:111
  19.2 8.9 %collective-permute-start.2 = (bf16[8,6272]{1,0:T(8,128)(2,1)S(1)}, bf16[8,6272]{1,0:T(8,128)(2,1)S(1)}, u32[]{:S(2)}, u32[]{:S(2)}) collective-permute-start(bf16[8,6272]{1,0:T(8,128)(2,1)S(1)} %fusion.4), channel_id=1, source_target_pairs={{2,0},{3,1},{0,2},{1,3},{6,4},{7,5},{4,6},{5,7},{10,8},{11,9},{8,1... | collective-permute-start | bytes 301064 | tf_op jit(solution)/shard_map/ppermute | solution.py:111
  20.6 7.4 %collective-permute-start.3 = (bf16[8,6272]{1,0:T(8,128)(2,1)S(1)}, bf16[8,6272]{1,0:T(8,128)(2,1)S(1)}, u32[]{:S(2)}, u32[]{:S(2)}) collective-permute-start(bf16[8,6272]{1,0:T(8,128)(2,1)S(1)} %fusion.4), channel_id=1, source_target_pairs={{3,0},{2,1},{1,2},{0,3},{7,4},{6,5},{5,6},{4,7},{11,8},{10,9},{9,1... | collective-permute-start | bytes 301064 | tf_op jit(solution)/shard_map/ppermute | solution.py:111
  22.1 10.1 %collective-permute-start.11 = (bf16[64,3072]{1,0:T(8,128)(2,1)S(1)}, bf16[64,3072]{1,0:T(8,128)(2,1)S(1)}, u32[]{:S(2)}, u32[]{:S(2)}) collective-permute-start(bf16[64,3072]{1,0:T(8,128)(2,1)S(1)} %pad_maximum_fusion.10), channel_id=1, source_target_pairs={{16,0},{0,16},{17,1},{1,17},{18,2},{2,18},{19,3},{3,19},{20,4},{4,... | collective-permute-start | bytes 1179656 | tf_op jit(solution)/shard_map/ppermute | solution.py:111
  22.7 9.5 %collective-permute-start.10 = (bf16[64,3072]{1,0:T(8,128)(2,1)S(1)}, bf16[64,3072]{1,0:T(8,128)(2,1)S(1)}, u32[]{:S(2)}, u32[]{:S(2)}) collective-permute-start(bf16[64,3072]{1,0:T(8,128)(2,1)S(1)} %pad_maximum_fusion.9), channel_id=1, source_target_pairs={{8,0},{12,4},{0,8},{4,12},{9,1},{13,5},{1,9},{5,13},{10,2},{14,6},... | collective-permute-start | bytes 1179656 | tf_op jit(solution)/shard_map/ppermute | solution.py:111
  31.0 5.7 %collective-permute-start.9 = (bf16[32,3072]{1,0:T(8,128)(2,1)S(1)}, bf16[32,3072]{1,0:T(8,128)(2,1)S(1)}, u32[]{:S(2)}, u32[]{:S(2)}) collective-permute-start(bf16[32,3072]{1,0:T(8,128)(2,1)S(1)} %get-tuple-element.50), channel_id=1, source_target_pairs={{8,0},{12,4},{0,8},{4,12},{9,1},{13,5},{1,9},{5,13},{10,2},{14,6},... | collective-permute-start | bytes 589832 | tf_op jit(solution)/shard_map/ppermute | solution.py:111
  31.6 7.1 %collective-permute-start.8 = (bf16[32,3200]{1,0:T(8,128)(2,1)S(1)}, bf16[32,3200]{1,0:T(8,128)(2,1)S(1)}, u32[]{:S(2)}, u32[]{:S(2)}) collective-permute-start(bf16[32,3200]{1,0:T(8,128)(2,1)S(1)} %slice.98), channel_id=1, source_target_pairs={{16,0},{0,16},{17,1},{1,17},{18,2},{2,18},{19,3},{3,19},{20,4},{4,... | collective-permute-start | bytes 614408 | tf_op jit(solution)/shard_map/ppermute | solution.py:111
  32.2 8.3 %collective-permute-start.15 = (bf16[128,3072]{1,0:T(8,128)(2,1)S(1)}, bf16[128,3072]{1,0:T(8,128)(2,1)S(1)}, u32[]{:S(2)}, u32[]{:S(2)}) collective-permute-start(bf16[128,3072]{1,0:T(8,128)(2,1)S(1)} %pad_maximum_fusion.4), channel_id=1, source_target_pairs={{4,0},{0,4},{12,8},{8,12},{5,1},{1,5},{13,9},{9,13},{6,2},{2,6},{1... | collective-permute-start | bytes 2359304 | tf_op jit(solution)/shard_map/ppermute | solution.py:111
  32.4 8.2 %collective-permute-start.14 = (bf16[128,3072]{1,0:T(8,128)(2,1)S(1)}, bf16[128,3072]{1,0:T(8,128)(2,1)S(1)}, u32[]{:S(2)}, u32[]{:S(2)}) collective-permute-start(bf16[128,3072]{1,0:T(8,128)(2,1)S(1)} %pad_maximum_fusion.3), channel_id=1, source_target_pairs={{4,0},{0,4},{12,8},{8,12},{5,1},{1,5},{13,9},{9,13},{6,2},{2,6},{1... | collective-permute-start | bytes 2359304 | tf_op jit(solution)/shard_map/ppermute | solution.py:111
  38.7 9.0 %collective-permute-start.13 = (bf16[64,3072]{1,0:T(8,128)(2,1)S(1)}, bf16[64,3072]{1,0:T(8,128)(2,1)S(1)}, u32[]{:S(2)}, u32[]{:S(2)}) collective-permute-start(bf16[64,3072]{1,0:T(8,128)(2,1)S(1)} %pad_maximum_fusion.11), channel_id=1, source_target_pairs={{16,0},{0,16},{17,1},{1,17},{18,2},{2,18},{19,3},{3,19},{20,4},{4,... | collective-permute-start | bytes 1179656 | tf_op jit(solution)/shard_map/ppermute | solution.py:111
  38.8 8.9 %collective-permute-start.12 = (bf16[64,3200]{1,0:T(8,128)(2,1)S(1)}, bf16[64,3200]{1,0:T(8,128)(2,1)S(1)}, u32[]{:S(2)}, u32[]{:S(2)}) collective-permute-start(bf16[64,3200]{1,0:T(8,128)(2,1)S(1)} %pad_maximum_fusion.7), channel_id=1, source_target_pairs={{8,0},{12,4},{0,8},{4,12},{9,1},{13,5},{1,9},{5,13},{10,2},{14,6},... | collective-permute-start | bytes 1228808 | tf_op jit(solution)/shard_map/ppermute | solution.py:111
  47.8 3.5 %collective-permute-start.17 = (bf16[128,3072]{1,0:T(8,128)(2,1)S(1)}, bf16[128,3072]{1,0:T(8,128)(2,1)S(1)}, u32[]{:S(2)}, u32[]{:S(2)}) collective-permute-start(bf16[128,3072]{1,0:T(8,128)(2,1)S(1)} %pad_maximum_fusion.5), channel_id=1, source_target_pairs={{4,0},{0,4},{12,8},{8,12},{5,1},{1,5},{13,9},{9,13},{6,2},{2,6},{1... | collective-permute-start | bytes 2359304 | tf_op jit(solution)/shard_map/ppermute | solution.py:111
  47.9 3.5 %collective-permute-start.16 = (bf16[128,3200]{1,0:T(8,128)(2,1)S(1)}, bf16[128,3200]{1,0:T(8,128)(2,1)S(1)}, u32[]{:S(2)}, u32[]{:S(2)}) collective-permute-start(bf16[128,3200]{1,0:T(8,128)(2,1)S(1)} %pad_maximum_fusion.2), channel_id=1, source_target_pairs={{4,0},{0,4},{12,8},{8,12},{5,1},{1,5},{13,9},{9,13},{6,2},{2,6},{1... | collective-permute-start | bytes 2457608 | tf_op jit(solution)/shard_map/ppermute | solution.py:111
  60.1 4.5 %collective-permute-start.21 = (bf16[128,3072]{1,0:T(8,128)(2,1)S(1)}, bf16[128,3072]{1,0:T(8,128)(2,1)S(1)}, u32[]{:S(2)}, u32[]{:S(2)}) collective-permute-start(bf16[128,3072]{1,0:T(8,128)(2,1)S(1)} %get-tuple-element.70), channel_id=1, source_target_pairs={{4,0},{0,4},{12,8},{8,12},{5,1},{1,5},{13,9},{9,13},{6,2},{2,6},{1... | collective-permute-start | bytes 2359304 | tf_op jit(solution)/shard_map/ppermute | solution.py:111
  64.1 3.7 %collective-permute-start.18 = (bf16[128,3200]{1,0:T(8,128)(2,1)S(1)}, bf16[128,3200]{1,0:T(8,128)(2,1)S(1)}, u32[]{:S(2)}, u32[]{:S(2)}) collective-permute-start(bf16[128,3200]{1,0:T(8,128)(2,1)S(1)} %get-tuple-element.69), channel_id=1, source_target_pairs={{4,0},{0,4},{12,8},{8,12},{5,1},{1,5},{13,9},{9,13},{6,2},{2,6},{1... | collective-permute-start | bytes 2457608 | tf_op jit(solution)/shard_map/ppermute | solution.py:111
  64.9 7.8 %collective-permute-start.25 = (bf16[64,1536]{1,0:T(8,128)(2,1)S(1)}, bf16[64,1536]{1,0:T(8,128)(2,1)S(1)}, u32[]{:S(2)}, u32[]{:S(2)}) collective-permute-start(bf16[64,1536]{1,0:T(8,128)(2,1)S(1)} %pad_maximum_fusion.13), channel_id=1, source_target_pairs={{16,0},{0,16},{17,1},{1,17},{18,2},{2,18},{19,3},{3,19},{20,4},{4,... | collective-permute-start | bytes 589832 | tf_op jit(solution)/shard_map/ppermute | solution.py:111
  67.0 7.8 %collective-permute-start.24 = (bf16[64,1536]{1,0:T(8,128)(2,1)S(1)}, bf16[64,1536]{1,0:T(8,128)(2,1)S(1)}, u32[]{:S(2)}, u32[]{:S(2)}) collective-permute-start(bf16[64,1536]{1,0:T(8,128)(2,1)S(1)} %concatenate.112), channel_id=1, source_target_pairs={{8,0},{12,4},{0,8},{4,12},{9,1},{13,5},{1,9},{5,13},{10,2},{14,6},... | collective-permute-start | bytes 589832 | tf_op jit(solution)/shard_map/ppermute | solution.py:111
  68.1 10.7 %collective-permute-start.20 = (bf16[64,1664]{1,0:T(8,128)(2,1)S(1)}, bf16[64,1664]{1,0:T(8,128)(2,1)S(1)}, u32[]{:S(2)}, u32[]{:S(2)}) collective-permute-start(bf16[64,1664]{1,0:T(8,128)(2,1)S(1)} %pad_maximum_fusion.12), channel_id=1, source_target_pairs={{16,0},{0,16},{17,1},{1,17},{18,2},{2,18},{19,3},{3,19},{20,4},{4,... | collective-permute-start | bytes 638984 | tf_op jit(solution)/shard_map/ppermute | solution.py:111
  69.0 9.8 %collective-permute-start.19 = (bf16[64,1536]{1,0:T(8,128)(2,1)S(1)}, bf16[64,1536]{1,0:T(8,128)(2,1)S(1)}, u32[]{:S(2)}, u32[]{:S(2)}) collective-permute-start(bf16[64,1536]{1,0:T(8,128)(2,1)S(1)} %concatenate.110), channel_id=1, source_target_pairs={{8,0},{12,4},{0,8},{4,12},{9,1},{13,5},{1,9},{5,13},{10,2},{14,6},... | collective-permute-start | bytes 589832 | tf_op jit(solution)/shard_map/ppermute | solution.py:111
  72.8 7.5 %collective-permute-start.30 = (bf16[32,1536]{1,0:T(8,128)(2,1)S(1)}, bf16[32,1536]{1,0:T(8,128)(2,1)S(1)}, u32[]{:S(2)}, u32[]{:S(2)}) collective-permute-start(bf16[32,1536]{1,0:T(8,128)(2,1)S(1)} %split.121), channel_id=1, source_target_pairs={{8,0},{12,4},{0,8},{4,12},{9,1},{13,5},{1,9},{5,13},{10,2},{14,6},... | collective-permute-start | bytes 294920 | tf_op jit(solution)/shard_map/ppermute | solution.py:111
  74.9 5.5 %collective-permute-start.29 = (bf16[32,1536]{1,0:T(8,128)(2,1)S(1)}, bf16[32,1536]{1,0:T(8,128)(2,1)S(1)}, u32[]{:S(2)}, u32[]{:S(2)}) collective-permute-start(bf16[32,1536]{1,0:T(8,128)(2,1)S(1)} %split.122), channel_id=1, source_target_pairs={{16,0},{0,16},{17,1},{1,17},{18,2},{2,18},{19,3},{3,19},{20,4},{4,... | collective-permute-start | bytes 294920 | tf_op jit(solution)/shard_map/ppermute | solution.py:111
  78.9 5.9 %collective-permute-start.22 = (bf16[32,1536]{1,0:T(8,128)(2,1)S(1)}, bf16[32,1536]{1,0:T(8,128)(2,1)S(1)}, u32[]{:S(2)}, u32[]{:S(2)}) collective-permute-start(bf16[32,1536]{1,0:T(8,128)(2,1)S(1)} %split.123), channel_id=1, source_target_pairs={{16,0},{0,16},{17,1},{1,17},{18,2},{2,18},{19,3},{3,19},{20,4},{4,... | collective-permute-start | bytes 294920 | tf_op jit(solution)/shard_map/ppermute | solution.py:111
  79.5 5.4 %collective-permute-start.23 = (bf16[32,1664]{1,0:T(8,128)(2,1)S(1)}, bf16[32,1664]{1,0:T(8,128)(2,1)S(1)}, u32[]{:S(2)}, u32[]{:S(2)}) collective-permute-start(bf16[32,1664]{1,0:T(8,128)(2,1)S(1)} %split.120), channel_id=1, source_target_pairs={{8,0},{12,4},{0,8},{4,12},{9,1},{13,5},{1,9},{5,13},{10,2},{14,6},... | collective-permute-start | bytes 319496 | tf_op jit(solution)/shard_map/ppermute | solution.py:111
  80.4 7.3 %collective-permute-start.31 = (bf16[8,3072]{1,0:T(8,128)(2,1)S(1)}, bf16[8,3072]{1,0:T(8,128)(2,1)S(1)}, u32[]{:S(2)}, u32[]{:S(2)}) collective-permute-start(bf16[8,3072]{1,0:T(8,128)(2,1)S(1)} %get-tuple-element.103), channel_id=1, source_target_pairs={{1,0},{0,1},{3,2},{2,3},{5,4},{4,5},{7,6},{6,7},{9,8},{8,9},{11,10... | collective-permute-start | bytes 147464 | tf_op jit(solution)/shard_map/ppermute | solution.py:111
  81.7 7.8 %collective-permute-start.32 = (bf16[8,3072]{1,0:T(8,128)(2,1)S(1)}, bf16[8,3072]{1,0:T(8,128)(2,1)S(1)}, u32[]{:S(2)}, u32[]{:S(2)}) collective-permute-start(bf16[8,3072]{1,0:T(8,128)(2,1)S(1)} %get-tuple-element.105), channel_id=1, source_target_pairs={{2,0},{3,1},{0,2},{1,3},{6,4},{7,5},{4,6},{5,7},{10,8},{11,9},{8,1... | collective-permute-start | bytes 147464 | tf_op jit(solution)/shard_map/ppermute | solution.py:111
  83.1 6.4 %collective-permute-start.33 = (bf16[8,3072]{1,0:T(8,128)(2,1)S(1)}, bf16[8,3072]{1,0:T(8,128)(2,1)S(1)}, u32[]{:S(2)}, u32[]{:S(2)}) collective-permute-start(bf16[8,3072]{1,0:T(8,128)(2,1)S(1)} %get-tuple-element.104), channel_id=1, source_target_pairs={{3,0},{2,1},{1,2},{0,3},{7,4},{6,5},{5,6},{4,7},{11,8},{10,9},{9,1... | collective-permute-start | bytes 147464 | tf_op jit(solution)/shard_map/ppermute | solution.py:111
  84.9 9.0 %copy-start.2 = (s32[8]{0:T(128)S(1)}, s32[8]{0:T(128)}, u32[]{:S(2)}) copy-start(s32[8]{0:T(128)} %param.10) | copy-start | bytes 100
  85.0 5.1 %collective-permute-start.26 = (bf16[8,3200]{1,0:T(8,128)(2,1)S(1)}, bf16[8,3200]{1,0:T(8,128)(2,1)S(1)}, u32[]{:S(2)}, u32[]{:S(2)}) collective-permute-start(bf16[8,3200]{1,0:T(8,128)(2,1)S(1)} %get-tuple-element.100), channel_id=1, source_target_pairs={{1,0},{0,1},{3,2},{2,3},{5,4},{4,5},{7,6},{6,7},{9,8},{8,9},{11,10... | collective-permute-start | bytes 153608 | tf_op jit(solution)/shard_map/ppermute | solution.py:111
  85.5 5.6 %collective-permute-start.27 = (bf16[8,3200]{1,0:T(8,128)(2,1)S(1)}, bf16[8,3200]{1,0:T(8,128)(2,1)S(1)}, u32[]{:S(2)}, u32[]{:S(2)}) collective-permute-start(bf16[8,3200]{1,0:T(8,128)(2,1)S(1)} %get-tuple-element.102), channel_id=1, source_target_pairs={{2,0},{3,1},{0,2},{1,3},{6,4},{7,5},{4,6},{5,7},{10,8},{11,9},{8,1... | collective-permute-start | bytes 153608 | tf_op jit(solution)/shard_map/ppermute | solution.py:111
  87.7 5.9 %collective-permute-start.28 = (bf16[8,3200]{1,0:T(8,128)(2,1)S(1)}, bf16[8,3200]{1,0:T(8,128)(2,1)S(1)}, u32[]{:S(2)}, u32[]{:S(2)}) collective-permute-start(bf16[8,3200]{1,0:T(8,128)(2,1)S(1)} %get-tuple-element.101), channel_id=1, source_target_pairs={{3,0},{2,1},{1,2},{0,3},{7,4},{6,5},{5,6},{4,7},{11,8},{10,9},{9,1... | collective-permute-start | bytes 153608 | tf_op jit(solution)/shard_map/ppermute | solution.py:111

commit v17 on v16

--- a/solution.py
+++ b/solution.py
@@ -406,12 +406,12 @@
     pre_gate, pre_up, gate_high, up_high = multiply_tokens(
         token_low, gate_low, up_low, 0, half, (), ((gate_weight, half, half), (up_weight, half, half))
     )
-    pre_gate, pre_up = multiply_tokens(token_high, gate_high, up_high, 0, quarter, (pre_gate, pre_up))
+    pre_gate, pre_up, down = multiply_tokens(
+        token_high, gate_high, up_high, 0, quarter, (pre_gate, pre_up),
+        ((down_weight, 0, down_weight.shape[1] // 2),),
+    )
     grad_far = after_others(grad_far, pre_gate)
-    pre_gate, pre_up, down = multiply_tokens(
-        token_high, gate_high, up_high, quarter, quarter, (pre_gate, pre_up),
-        ((down_weight, 0, down_weight.shape[1] // 2),),
-    )
+    pre_gate, pre_up = multiply_tokens(token_high, gate_high, up_high, quarter, quarter, (pre_gate, pre_up))
     grad_halves = gather_core(grad_near[0], grad_far[0], grad_near[1], grad_far[1])
     expert = lax.axis_index("expert").astype(jnp.int32).reshape(1)
     grad_gate, grad_up, dots = multiply_grads(expert, *grad_halves, pre_gate, pre_up, down, down_weight)

time: 95.8 us -> 95.8 us (level)
  waiting for transfers between devices: 22.7 us -> 24.1 us
  starting transfers between devices: 36.2 us -> 34.9 us
    ppermute x34, waiting for transfers between devices: 22.7 us -> 24.1 us  [swap(): lax.ppermute(value, axis, [(i ^ bit, i) for i in range(lax.axis_size(axis...]
    ppermute x34, starting transfers between devices: 36.2 us -> 34.9 us  [swap(): lax.ppermute(value, axis, [(i ^ bit, i) for i in range(lax.axis_size(axis...]
  transfers between devices with their start and end apart: 34 -> 34, of which waited for: 10 -> 11; matrix products, arithmetic and copies ran while one was open for 6% -> 6% of each run, Pallas kernels for 20% -> 20%
where the time goes in v17:
time: 95.8 us; the launch traced here: 95.5 us
  starting transfers between devices  34.9 us (36%)
  Pallas kernels  27.7 us (29%)
  waiting for transfers between devices  24.1 us (25%)
  other arithmetic  3 us (3%)
  local copies, waits for them, and re-layouts  2.36 us (2%)
  matrix products  2.15 us (2%)
  between operations  1.26 us (1%)
    ppermute x34, starting transfers between devices, swap(): lax.ppermute(value, axis, [(i ^ bit, i) for i in range(lax.axis_size(axis...  34.9 us
    ppermute x34, waiting for transfers between devices, swap(): lax.ppermute(value, axis, [(i ^ bit, i) for i in range(lax.axis_size(axis...  24.1 us
    pallas_call x3, Pallas kernels, multiply_tokens(): pl.pallas_call(functools.partial(token_kernel, offset, length, sources, l...  9.76 us
    pallas_call x2, Pallas kernels, multiply_outputs(): pl.pallas_call(output_kernel, out_shape=(pltpu.VMEM((rows // 2, total), j...  7.66 us
    pallas_call x2, Pallas kernels, fetch(): pl.pallas_call(functools.partial(fetch_kernel, first), out_shape=tuple((p...  5.59 us
    pallas_call x1, Pallas kernels, multiply_grads(): pl.pallas_call(grad_kernel, out_shape=(pltpu.VMEM((rows, hidden), jnp.bfl...  4.73 us
  transfers between devices with their start and end apart: 34, of which 11 were waited for; matrix products, arithmetic and copies ran while one was open for 6% of the time, Pallas kernels for 20%

profile of v17, /device:TPU:0, one launch (start us, length us, event | category | flops | bytes accessed | tf_op | source)
XLA Modules:
  0.0 95.5 jit_solution(7057041822583296767)
XLA Ops:
  0.7 3.1 %collective-permute-start = (bf16[8,6144]{1,0:T(8,128)(2,1)}, bf16[8,6144]{1,0:T(8,128)(2,1)S(1)}, u32[]{:S(2)}, u32[]{:S(2)}) collective-permute-start(bf16[8,6144]{1,0:T(8,128)(2,1)} %param.8), channel_id=1, source_target_pairs={{1,0},{0,1},{3,2},{2,3},{5,4},{4,5},{7,6},{6,7},{9,8},{8,9},{11,10... | collective-permute-start | bytes 294920 | tf_op jit(solution)/shard_map/ppermute | solution.py:111
  3.7 2.6 %collective-permute-start.4 = (bf16[8,6144]{1,0:T(8,128)(2,1)}, bf16[8,6144]{1,0:T(8,128)(2,1)S(1)}, u32[]{:S(2)}, u32[]{:S(2)}) collective-permute-start(bf16[8,6144]{1,0:T(8,128)(2,1)} %param.8), channel_id=1, source_target_pairs={{2,0},{3,1},{0,2},{1,3},{6,4},{7,5},{4,6},{5,7},{10,8},{11,9},{8,1... | collective-permute-start | bytes 294920 | tf_op jit(solution)/shard_map/ppermute | solution.py:111
  6.3 1.0 %constant_dynamic-update-slice_fusion.3 = bf16[32,6144]{1,0:T(8,128)(2,1)S(1)} fusion(bf16[8,6144]{1,0:T(8,128)(2,1)} %param.8), kind=kLoop, calls=%fused_computation.45 | loop fusion | bytes 196608
  7.3 0.8 slice_bitcast_fusion
  8.1 0.7 convert_element_type.76
  8.7 1.2 %select_reduce_fusion.3 = (f32[8]{0:T(128)S(1)}, f32[8]{0:T(128)S(1)}) fusion(s32[8]{0:T(128)S(1)} %get-tuple-element.111, s32[8]{0:T(128)S(1)} %get-tuple-element.110, bf16[8,6144]{1,0:T(8,128)(2,1)} %param.8, bf16[6144,4]{0,1:T(4,128)(2,1)S(1)} %copy-done), kind=kOutput, calls=%fused_computation.69 | convolution fusion | flops 393392 | bytes 147584 | tf_op jit(solution)/shard_map/dot_general | solution.py:390
  10.1 4.3 %collective-permute-done.4 = bf16[8,6144]{1,0:T(8,128)(2,1)S(1)} collective-permute-done((bf16[8,6144]{1,0:T(8,128)(2,1)}, bf16[8,6144]{1,0:T(8,128)(2,1)S(1)}, u32[]{:S(2)}, u32[]{:S(2)}) %collective-permute-start.4) | collective-permute-done | bytes 98336 | tf_op jit(solution)/shard_map/ppermute | solution.py:111
  14.5 1.6 %collective-permute-start.6 = (bf16[32,3072]{1,0:T(8,128)(2,1)S(1)}, bf16[32,3072]{1,0:T(8,128)(2,1)S(1)}, u32[]{:S(2)}, u32[]{:S(2)}) collective-permute-start(bf16[32,3072]{1,0:T(8,128)(2,1)S(1)} %get-tuple-element.45), channel_id=1, source_target_pairs={{16,0},{0,16},{17,1},{1,17},{18,2},{2,18},{19,3},{3,19},{20,4},{4,... | collective-permute-start | bytes 589832 | tf_op jit(solution)/shard_map/ppermute | solution.py:111
  16.0 1.5 %collective-permute-start.7 = (bf16[32,3072]{1,0:T(8,128)(2,1)S(1)}, bf16[32,3072]{1,0:T(8,128)(2,1)S(1)}, u32[]{:S(2)}, u32[]{:S(2)}) collective-permute-start(bf16[32,3072]{1,0:T(8,128)(2,1)S(1)} %get-tuple-element.47), channel_id=1, source_target_pairs={{8,0},{12,4},{0,8},{4,12},{9,1},{13,5},{1,9},{5,13},{10,2},{14,6},... | collective-permute-start | bytes 589832 | tf_op jit(solution)/shard_map/ppermute | solution.py:111
  17.6 1.7 %collective-permute-start.1 = (bf16[8,6272]{1,0:T(8,128)(2,1)S(1)}, bf16[8,6272]{1,0:T(8,128)(2,1)S(1)}, u32[]{:S(2)}, u32[]{:S(2)}) collective-permute-start(bf16[8,6272]{1,0:T(8,128)(2,1)S(1)} %fusion.4), channel_id=1, source_target_pairs={{1,0},{0,1},{3,2},{2,3},{5,4},{4,5},{7,6},{6,7},{9,8},{8,9},{11,10... | collective-permute-start | bytes 301064 | tf_op jit(solution)/shard_map/ppermute | solution.py:111
  19.2 1.4 %collective-permute-start.2 = (bf16[8,6272]{1,0:T(8,128)(2,1)S(1)}, bf16[8,6272]{1,0:T(8,128)(2,1)S(1)}, u32[]{:S(2)}, u32[]{:S(2)}) collective-permute-start(bf16[8,6272]{1,0:T(8,128)(2,1)S(1)} %fusion.4), channel_id=1, source_target_pairs={{2,0},{3,1},{0,2},{1,3},{6,4},{7,5},{4,6},{5,7},{10,8},{11,9},{8,1... | collective-permute-start | bytes 301064 | tf_op jit(solution)/shard_map/ppermute | solution.py:111
  20.6 1.4 %collective-permute-start.3 = (bf16[8,6272]{1,0:T(8,128)(2,1)S(1)}, bf16[8,6272]{1,0:T(8,128)(2,1)S(1)}, u32[]{:S(2)}, u32[]{:S(2)}) collective-permute-start(bf16[8,6272]{1,0:T(8,128)(2,1)S(1)} %fusion.4), channel_id=1, source_target_pairs={{3,0},{2,1},{1,2},{0,3},{7,4},{6,5},{5,6},{4,7},{11,8},{10,9},{9,1... | collective-permute-start | bytes 301064 | tf_op jit(solution)/shard_map/ppermute | solution.py:111
  22.1 0.6 collective-permute-start.11
  22.7 1.3 %collective-permute-start.10 = (bf16[64,3072]{1,0:T(8,128)(2,1)S(1)}, bf16[64,3072]{1,0:T(8,128)(2,1)S(1)}, u32[]{:S(2)}, u32[]{:S(2)}) collective-permute-start(bf16[64,3072]{1,0:T(8,128)(2,1)S(1)} %pad_maximum_fusion.9), channel_id=1, source_target_pairs={{8,0},{12,4},{0,8},{4,12},{9,1},{13,5},{1,9},{5,13},{10,2},{14,6},... | collective-permute-start | bytes 1179656 | tf_op jit(solution)/shard_map/ppermute | solution.py:111
  23.9 2.8 %shard_map.95.gate.gate_copy = bf16[3072,1024]{1,0:T(8,128)(2,1)S(1)} custom-call(bf16[32,3072]{1,0:T(8,128)(2,1)S(1)} %collective-permute-done.7._, bf16[1,6144,1024]{2,1,0:T(8,128)(2,1)} %refs_0_.5), custom_call_target="tpu_custom_call" | custom-call | bytes 6291456 | tf_op jit(solution)/shard_map/pallas_call | solution.py:210
  26.8 1.3 %collective-permute-done.2 = bf16[8,6272]{1,0:T(8,128)(2,1)S(1)} collective-permute-done((bf16[8,6272]{1,0:T(8,128)(2,1)S(1)}, bf16[8,6272]{1,0:T(8,128)(2,1)S(1)}, u32[]{:S(2)}, u32[]{:S(2)}) %collective-permute-start.2) | collective-permute-done | bytes 100384 | tf_op jit(solution)/shard_map/ppermute | solution.py:111
  28.2 2.8 %shard_map.96.up.up_copy = bf16[3072,1024]{1,0:T(8,128)(2,1)S(1)} custom-call(bf16[32,3072]{1,0:T(8,128)(2,1)S(1)} %collective-permute-done.7._, bf16[1,6144,1024]{2,1,0:T(8,128)(2,1)} %refs_1_.1), custom_call_target="tpu_custom_call" | custom-call | bytes 6291456 | tf_op jit(solution)/shard_map/pallas_call | solution.py:210
  31.0 0.6 collective-permute-start.9
  31.6 0.5 collective-permute-start.8
  32.4 0.6 collective-permute-start.14
  33.0 3.8 %collective-permute-done.9 = bf16[32,3072]{1,0:T(8,128)(2,1)S(1)} collective-permute-done((bf16[32,3072]{1,0:T(8,128)(2,1)S(1)}, bf16[32,3072]{1,0:T(8,128)(2,1)S(1)}, u32[]{:S(2)}, u32[]{:S(2)}) %collective-permute-start.9) | collective-permute-done | bytes 196640 | tf_op jit(solution)/shard_map/ppermute | solution.py:111
  36.7 1.9 %collective-permute-done.8 = bf16[32,3200]{1,0:T(8,128)(2,1)S(1)} collective-permute-done((bf16[32,3200]{1,0:T(8,128)(2,1)S(1)}, bf16[32,3200]{1,0:T(8,128)(2,1)S(1)}, u32[]{:S(2)}, u32[]{:S(2)}) %collective-permute-start.8) | collective-permute-done | bytes 204832 | tf_op jit(solution)/shard_map/ppermute | solution.py:111
  38.8 1.7 %collective-permute-start.12 = (bf16[64,3200]{1,0:T(8,128)(2,1)S(1)}, bf16[64,3200]{1,0:T(8,128)(2,1)S(1)}, u32[]{:S(2)}, u32[]{:S(2)}) collective-permute-start(bf16[64,3200]{1,0:T(8,128)(2,1)S(1)} %pad_maximum_fusion.7), channel_id=1, source_target_pairs={{8,0},{12,4},{0,8},{4,12},{9,1},{13,5},{1,9},{5,13},{10,2},{14,6},... | collective-permute-start | bytes 1228808 | tf_op jit(solution)/shard_map/ppermute | solution.py:111
  40.7 4.7 %shard_map.97 = (f32[256,1024]{1,0:T(8,128)S(1)}, f32[256,1024]{1,0:T(8,128)S(1)}, bf16[3072,1024]{1,0:T(8,128)(2,1)S(1)}, bf16[3072,1024]{1,0:T(8,128)(2,1)S(1)}) custom-call(bf16[256,3072]{1,0:T(8,128)(2,1)S(1)} %pad_maximum_fusion.1.tokens, bf16[3072,1024]{1,0:T(8,128)(2,1)S(1)} %shard_map.95.gate.gate_copy, bf16[3072,1024]{1,0:T(8,128)(2,1)S(1)} %shard_map.96.up.up_copy, ...), custom_call_target="tpu_custom_call" | custom-call | flops 3221225472 | bytes 1572864 | tf_op jit(solution)/shard_map/pallas_call | solution.py:253
  45.4 2.8 %shard_map.98 = (f32[256,1024]{1,0:T(8,128)S(1)}, f32[256,1024]{1,0:T(8,128)S(1)}, bf16[512,6144]{1,0:T(8,128)(2,1)S(1)}) custom-call(bf16[256,3072]{1,0:T(8,128)(2,1)S(1)} %constant_dynamic-update-slice_fusion.8.tokens, bf16[3072,1024]{1,0:T(8,128)(2,1)S(1)} %get-tuple-element.54.gate.gate_copy, bf16[3072,1024]{1,0:T(8,128)(2,1)S(1)} %get-tuple-element.55.up.up_copy, ...), custom_call_target="tpu_custom_call" | custom-call | flops 1610612736 | bytes 786432 | tf_op jit(solution)/shard_map/pallas_call | solution.py:253
  48.4 0.6 collective-permute-start.16
  49.0 2.3 %shard_map.99 = (f32[256,1024]{1,0:T(8,128)S(1)}, f32[256,1024]{1,0:T(8,128)S(1)}) custom-call(bf16[256,3072]{1,0:T(8,128)(2,1)S(1)} %constant_dynamic-update-slice_fusion.8.tokens, bf16[3072,1024]{1,0:T(8,128)(2,1)S(1)} %get-tuple-element.54.gate.gate_copy, bf16[3072,1024]{1,0:T(8,128)(2,1)S(1)} %get-tuple-element.55.up.up_copy, ...), custom_call_target="tpu_custom_call" | custom-call | flops 1610612736 | bytes 786432 | tf_op jit(solution)/shard_map/pallas_call | solution.py:253
  51.9 4.7 %shard_map.100 = (bf16[256,1024]{1,0:T(8,128)(2,1)S(1)}, bf16[256,1024]{1,0:T(8,128)(2,1)S(1)}, bf16[256,128]{1,0:T(8,128)(2,1)S(1)}) custom-call(s32[1]{0:T(128)} %bitcast.expert, bf16[256,3200]{1,0:T(8,128)(2,1)S(1)} %pad_maximum_fusion.low, bf16[256,3072]{1,0:T(8,128)(2,1)S(1)} %constant_dynamic-update-slice_fusion.13.high, ...), custom_call_target="tpu_custom_call" | custom-call | flops 3221225472 | bytes 6291456 | tf_op jit(solution)/shard_map/pallas_call | solution.py:319
  56.7 3.8 %shard_map.102 = (f32[128,3072]{1,0:T(8,128)S(1)}, bf16[128,3072]{1,0:T(8,128)(2,1)S(1)}) custom-call(bf16[256,1024]{1,0:T(8,128)(2,1)S(1)} %get-tuple-element.65.grad_gate, bf16[256,1024]{1,0:T(8,128)(2,1)S(1)} %get-tuple-element.66.grad_up, bf16[3072,1024]{1,0:T(8,128)(2,1)S(1)} %get-tuple-element.54.gate.gate_copy, ...), custom_call_target="tpu_custom_call" | custom-call | flops 3221225472 | bytes 3145728 | tf_op jit(solution)/shard_map/pallas_call | solution.py:365
  60.7 3.8 %shard_map.101 = (f32[128,3200]{1,0:T(8,128)S(1)}, bf16[128,3200]{1,0:T(8,128)(2,1)S(1)}) custom-call(bf16[256,1024]{1,0:T(8,128)(2,1)S(1)} %get-tuple-element.65.grad_gate, bf16[256,1024]{1,0:T(8,128)(2,1)S(1)} %get-tuple-element.66.grad_up, bf16[3072,1024]{1,0:T(8,128)(2,1)S(1)} %shard_map.95.gate.gate_copy, bf16[3072,1024]{1,0:T(8,128)(2,1)S(1)} %shard_map.96.up.up_copy, ...), custom_call_target="tpu_custom_call" | custom-call | flops 3221225472 | bytes 3145728 | tf_op jit(solution)/shard_map/pallas_call | solution.py:365
  65.3 2.1 %collective-permute-start.25 = (bf16[64,1536]{1,0:T(8,128)(2,1)S(1)}, bf16[64,1536]{1,0:T(8,128)(2,1)S(1)}, u32[]{:S(2)}, u32[]{:S(2)}) collective-permute-start(bf16[64,1536]{1,0:T(8,128)(2,1)S(1)} %pad_maximum_fusion.13), channel_id=1, source_target_pairs={{16,0},{0,16},{17,1},{1,17},{18,2},{2,18},{19,3},{3,19},{20,4},{4,... | collective-permute-start | bytes 589832 | tf_op jit(solution)/shard_map/ppermute | solution.py:111
  68.2 1.2 %collective-permute-start.20 = (bf16[64,1664]{1,0:T(8,128)(2,1)S(1)}, bf16[64,1664]{1,0:T(8,128)(2,1)S(1)}, u32[]{:S(2)}, u32[]{:S(2)}) collective-permute-start(bf16[64,1664]{1,0:T(8,128)(2,1)S(1)} %pad_maximum_fusion.12), channel_id=1, source_target_pairs={{16,0},{0,16},{17,1},{1,17},{18,2},{2,18},{19,3},{3,19},{20,4},{4,... | collective-permute-start | bytes 638984 | tf_op jit(solution)/shard_map/ppermute | solution.py:111
  69.4 0.6 collective-permute-start.19
  69.9 3.1 %collective-permute-done.25 = bf16[64,1536]{1,0:T(8,128)(2,1)S(1)} collective-permute-done((bf16[64,1536]{1,0:T(8,128)(2,1)S(1)}, bf16[64,1536]{1,0:T(8,128)(2,1)S(1)}, u32[]{:S(2)}, u32[]{:S(2)}) %collective-permute-start.25) | collective-permute-done | bytes 196640 | tf_op jit(solution)/shard_map/ppermute | solution.py:111
  73.2 0.5 collective-permute-start.30
  73.6 1.5 %collective-permute-done.24 = bf16[64,1536]{1,0:T(8,128)(2,1)S(1)} collective-permute-done((bf16[64,1536]{1,0:T(8,128)(2,1)S(1)}, bf16[64,1536]{1,0:T(8,128)(2,1)S(1)}, u32[]{:S(2)}, u32[]{:S(2)}) %collective-permute-start.24) | collective-permute-done | bytes 196640 | tf_op jit(solution)/shard_map/ppermute | solution.py:111
  75.2 0.6 collective-permute-start.29
  75.8 3.5 %collective-permute-done.19 = bf16[64,1536]{1,0:T(8,128)(2,1)S(1)} collective-permute-done((bf16[64,1536]{1,0:T(8,128)(2,1)S(1)}, bf16[64,1536]{1,0:T(8,128)(2,1)S(1)}, u32[]{:S(2)}, u32[]{:S(2)}) %collective-permute-start.19) | collective-permute-done | bytes 196640 | tf_op jit(solution)/shard_map/ppermute | solution.py:111
  79.9 0.5 collective-permute-start.23
  80.5 1.2 %collective-permute-start.31 = (bf16[8,3072]{1,0:T(8,128)(2,1)S(1)}, bf16[8,3072]{1,0:T(8,128)(2,1)S(1)}, u32[]{:S(2)}, u32[]{:S(2)}) collective-permute-start(bf16[8,3072]{1,0:T(8,128)(2,1)S(1)} %get-tuple-element.103), channel_id=1, source_target_pairs={{1,0},{0,1},{3,2},{2,3},{5,4},{4,5},{7,6},{6,7},{9,8},{8,9},{11,10... | collective-permute-start | bytes 147464 | tf_op jit(solution)/shard_map/ppermute | solution.py:111
  81.7 1.5 %collective-permute-start.32 = (bf16[8,3072]{1,0:T(8,128)(2,1)S(1)}, bf16[8,3072]{1,0:T(8,128)(2,1)S(1)}, u32[]{:S(2)}, u32[]{:S(2)}) collective-permute-start(bf16[8,3072]{1,0:T(8,128)(2,1)S(1)} %get-tuple-element.105), channel_id=1, source_target_pairs={{2,0},{3,1},{0,2},{1,3},{6,4},{7,5},{4,6},{5,7},{10,8},{11,9},{8,1... | collective-permute-start | bytes 147464 | tf_op jit(solution)/shard_map/ppermute | solution.py:111
  83.2 1.8 %collective-permute-start.33 = (bf16[8,3072]{1,0:T(8,128)(2,1)S(1)}, bf16[8,3072]{1,0:T(8,128)(2,1)S(1)}, u32[]{:S(2)}, u32[]{:S(2)}) collective-permute-start(bf16[8,3072]{1,0:T(8,128)(2,1)S(1)} %get-tuple-element.104), channel_id=1, source_target_pairs={{3,0},{2,1},{1,2},{0,3},{7,4},{6,5},{5,6},{4,7},{11,8},{10,9},{9,1... | collective-permute-start | bytes 147464 | tf_op jit(solution)/shard_map/ppermute | solution.py:111
  85.4 2.4 %collective-permute-start.27 = (bf16[8,3200]{1,0:T(8,128)(2,1)S(1)}, bf16[8,3200]{1,0:T(8,128)(2,1)S(1)}, u32[]{:S(2)}, u32[]{:S(2)}) collective-permute-start(bf16[8,3200]{1,0:T(8,128)(2,1)S(1)} %get-tuple-element.102), channel_id=1, source_target_pairs={{2,0},{3,1},{0,2},{1,3},{6,4},{7,5},{4,6},{5,7},{10,8},{11,9},{8,1... | collective-permute-start | bytes 153608 | tf_op jit(solution)/shard_map/ppermute | solution.py:111
  87.8 1.8 %collective-permute-start.28 = (bf16[8,3200]{1,0:T(8,128)(2,1)S(1)}, bf16[8,3200]{1,0:T(8,128)(2,1)S(1)}, u32[]{:S(2)}, u32[]{:S(2)}) collective-permute-start(bf16[8,3200]{1,0:T(8,128)(2,1)S(1)} %get-tuple-element.101), channel_id=1, source_target_pairs={{3,0},{2,1},{1,2},{0,3},{7,4},{6,5},{5,6},{4,7},{11,8},{10,9},{9,1... | collective-permute-start | bytes 153608 | tf_op jit(solution)/shard_map/ppermute | solution.py:111
  89.8 2.1 %collective-permute-done.27 = bf16[8,3200]{1,0:T(8,128)(2,1)S(1)} collective-permute-done((bf16[8,3200]{1,0:T(8,128)(2,1)S(1)}, bf16[8,3200]{1,0:T(8,128)(2,1)S(1)}, u32[]{:S(2)}, u32[]{:S(2)}) %collective-permute-start.27) | collective-permute-done | bytes 51232 | tf_op jit(solution)/shard_map/ppermute | solution.py:111
  92.0 1.7 %collective-permute-done.28 = bf16[8,3200]{1,0:T(8,128)(2,1)S(1)} collective-permute-done((bf16[8,3200]{1,0:T(8,128)(2,1)S(1)}, bf16[8,3200]{1,0:T(8,128)(2,1)S(1)}, u32[]{:S(2)}, u32[]{:S(2)}) %collective-permute-start.28) | collective-permute-done | bytes 51232 | tf_op jit(solution)/shard_map/ppermute | solution.py:111
  94.0 0.6 pad_maximum_fusion.14
  94.6 0.9 fusion.3
  (105 shorter events, 5.2 us)
Async XLA Ops:
  0.6 8.1 %copy-start = (bf16[6144,4]{0,1:T(4,128)(2,1)S(1)}, bf16[6144,4]{0,1:T(4,128)(2,1)}, u32[]{:S(2)}) copy-start(bf16[6144,4]{0,1:T(4,128)(2,1)} %param.12) | copy-start | bytes 147460
  0.6 16.9 %copy-start.1 = (bf16[8,6144]{1,0:T(8,128)(2,1)S(1)}, bf16[8,6144]{1,0:T(8,128)(2,1)}, u32[]{:S(2)}) copy-start(bf16[8,6144]{1,0:T(8,128)(2,1)} %param.9) | copy-start | bytes 294916
  0.7 9.4 %collective-permute-start = (bf16[8,6144]{1,0:T(8,128)(2,1)}, bf16[8,6144]{1,0:T(8,128)(2,1)S(1)}, u32[]{:S(2)}, u32[]{:S(2)}) collective-permute-start(bf16[8,6144]{1,0:T(8,128)(2,1)} %param.8), channel_id=1, source_target_pairs={{1,0},{0,1},{3,2},{2,3},{5,4},{4,5},{7,6},{6,7},{9,8},{8,9},{11,10... | collective-permute-start | bytes 294920 | tf_op jit(solution)/shard_map/ppermute | solution.py:111
  3.7 10.6 %collective-permute-start.4 = (bf16[8,6144]{1,0:T(8,128)(2,1)}, bf16[8,6144]{1,0:T(8,128)(2,1)S(1)}, u32[]{:S(2)}, u32[]{:S(2)}) collective-permute-start(bf16[8,6144]{1,0:T(8,128)(2,1)} %param.8), channel_id=1, source_target_pairs={{2,0},{3,1},{0,2},{1,3},{6,4},{7,5},{4,6},{5,7},{10,8},{11,9},{8,1... | collective-permute-start | bytes 294920 | tf_op jit(solution)/shard_map/ppermute | solution.py:111
  6.3 8.1 %collective-permute-start.5 = (bf16[8,6144]{1,0:T(8,128)(2,1)}, bf16[8,6144]{1,0:T(8,128)(2,1)S(1)}, u32[]{:S(2)}, u32[]{:S(2)}) collective-permute-start(bf16[8,6144]{1,0:T(8,128)(2,1)} %param.8), channel_id=1, source_target_pairs={{3,0},{2,1},{1,2},{0,3},{7,4},{6,5},{5,6},{4,7},{11,8},{10,9},{9,1... | collective-permute-start | bytes 294920 | tf_op jit(solution)/shard_map/ppermute | solution.py:111
  14.5 7.6 %collective-permute-start.6 = (bf16[32,3072]{1,0:T(8,128)(2,1)S(1)}, bf16[32,3072]{1,0:T(8,128)(2,1)S(1)}, u32[]{:S(2)}, u32[]{:S(2)}) collective-permute-start(bf16[32,3072]{1,0:T(8,128)(2,1)S(1)} %get-tuple-element.45), channel_id=1, source_target_pairs={{16,0},{0,16},{17,1},{1,17},{18,2},{2,18},{19,3},{3,19},{20,4},{4,... | collective-permute-start | bytes 589832 | tf_op jit(solution)/shard_map/ppermute | solution.py:111
  16.0 6.0 %collective-permute-start.7 = (bf16[32,3072]{1,0:T(8,128)(2,1)S(1)}, bf16[32,3072]{1,0:T(8,128)(2,1)S(1)}, u32[]{:S(2)}, u32[]{:S(2)}) collective-permute-start(bf16[32,3072]{1,0:T(8,128)(2,1)S(1)} %get-tuple-element.47), channel_id=1, source_target_pairs={{8,0},{12,4},{0,8},{4,12},{9,1},{13,5},{1,9},{5,13},{10,2},{14,6},... | collective-permute-start | bytes 589832 | tf_op jit(solution)/shard_map/ppermute | solution.py:111
  17.6 9.2 %collective-permute-start.1 = (bf16[8,6272]{1,0:T(8,128)(2,1)S(1)}, bf16[8,6272]{1,0:T(8,128)(2,1)S(1)}, u32[]{:S(2)}, u32[]{:S(2)}) collective-permute-start(bf16[8,6272]{1,0:T(8,128)(2,1)S(1)} %fusion.4), channel_id=1, source_target_pairs={{1,0},{0,1},{3,2},{2,3},{5,4},{4,5},{7,6},{6,7},{9,8},{8,9},{11,10... | collective-permute-start | bytes 301064 | tf_op jit(solution)/shard_map/ppermute | solution.py:111
  19.2 8.9 %collective-permute-start.2 = (bf16[8,6272]{1,0:T(8,128)(2,1)S(1)}, bf16[8,6272]{1,0:T(8,128)(2,1)S(1)}, u32[]{:S(2)}, u32[]{:S(2)}) collective-permute-start(bf16[8,6272]{1,0:T(8,128)(2,1)S(1)} %fusion.4), channel_id=1, source_target_pairs={{2,0},{3,1},{0,2},{1,3},{6,4},{7,5},{4,6},{5,7},{10,8},{11,9},{8,1... | collective-permute-start | bytes 301064 | tf_op jit(solution)/shard_map/ppermute | solution.py:111
  20.6 7.4 %collective-permute-start.3 = (bf16[8,6272]{1,0:T(8,128)(2,1)S(1)}, bf16[8,6272]{1,0:T(8,128)(2,1)S(1)}, u32[]{:S(2)}, u32[]{:S(2)}) collective-permute-start(bf16[8,6272]{1,0:T(8,128)(2,1)S(1)} %fusion.4), channel_id=1, source_target_pairs={{3,0},{2,1},{1,2},{0,3},{7,4},{6,5},{5,6},{4,7},{11,8},{10,9},{9,1... | collective-permute-start | bytes 301064 | tf_op jit(solution)/shard_map/ppermute | solution.py:111
  22.1 10.1 %collective-permute-start.11 = (bf16[64,3072]{1,0:T(8,128)(2,1)S(1)}, bf16[64,3072]{1,0:T(8,128)(2,1)S(1)}, u32[]{:S(2)}, u32[]{:S(2)}) collective-permute-start(bf16[64,3072]{1,0:T(8,128)(2,1)S(1)} %pad_maximum_fusion.10), channel_id=1, source_target_pairs={{16,0},{0,16},{17,1},{1,17},{18,2},{2,18},{19,3},{3,19},{20,4},{4,... | collective-permute-start | bytes 1179656 | tf_op jit(solution)/shard_map/ppermute | solution.py:111
  22.7 9.5 %collective-permute-start.10 = (bf16[64,3072]{1,0:T(8,128)(2,1)S(1)}, bf16[64,3072]{1,0:T(8,128)(2,1)S(1)}, u32[]{:S(2)}, u32[]{:S(2)}) collective-permute-start(bf16[64,3072]{1,0:T(8,128)(2,1)S(1)} %pad_maximum_fusion.9), channel_id=1, source_target_pairs={{8,0},{12,4},{0,8},{4,12},{9,1},{13,5},{1,9},{5,13},{10,2},{14,6},... | collective-permute-start | bytes 1179656 | tf_op jit(solution)/shard_map/ppermute | solution.py:111
  31.0 5.7 %collective-permute-start.9 = (bf16[32,3072]{1,0:T(8,128)(2,1)S(1)}, bf16[32,3072]{1,0:T(8,128)(2,1)S(1)}, u32[]{:S(2)}, u32[]{:S(2)}) collective-permute-start(bf16[32,3072]{1,0:T(8,128)(2,1)S(1)} %get-tuple-element.50), channel_id=1, source_target_pairs={{8,0},{12,4},{0,8},{4,12},{9,1},{13,5},{1,9},{5,13},{10,2},{14,6},... | collective-permute-start | bytes 589832 | tf_op jit(solution)/shard_map/ppermute | solution.py:111
  31.6 7.1 %collective-permute-start.8 = (bf16[32,3200]{1,0:T(8,128)(2,1)S(1)}, bf16[32,3200]{1,0:T(8,128)(2,1)S(1)}, u32[]{:S(2)}, u32[]{:S(2)}) collective-permute-start(bf16[32,3200]{1,0:T(8,128)(2,1)S(1)} %slice.98), channel_id=1, source_target_pairs={{16,0},{0,16},{17,1},{1,17},{18,2},{2,18},{19,3},{3,19},{20,4},{4,... | collective-permute-start | bytes 614408 | tf_op jit(solution)/shard_map/ppermute | solution.py:111
  32.2 8.3 %collective-permute-start.15 = (bf16[128,3072]{1,0:T(8,128)(2,1)S(1)}, bf16[128,3072]{1,0:T(8,128)(2,1)S(1)}, u32[]{:S(2)}, u32[]{:S(2)}) collective-permute-start(bf16[128,3072]{1,0:T(8,128)(2,1)S(1)} %pad_maximum_fusion.4), channel_id=1, source_target_pairs={{4,0},{0,4},{12,8},{8,12},{5,1},{1,5},{13,9},{9,13},{6,2},{2,6},{1... | collective-permute-start | bytes 2359304 | tf_op jit(solution)/shard_map/ppermute | solution.py:111
  32.4 8.2 %collective-permute-start.14 = (bf16[128,3072]{1,0:T(8,128)(2,1)S(1)}, bf16[128,3072]{1,0:T(8,128)(2,1)S(1)}, u32[]{:S(2)}, u32[]{:S(2)}) collective-permute-start(bf16[128,3072]{1,0:T(8,128)(2,1)S(1)} %pad_maximum_fusion.3), channel_id=1, source_target_pairs={{4,0},{0,4},{12,8},{8,12},{5,1},{1,5},{13,9},{9,13},{6,2},{2,6},{1... | collective-permute-start | bytes 2359304 | tf_op jit(solution)/shard_map/ppermute | solution.py:111
  38.7 9.5 %collective-permute-start.13 = (bf16[64,3072]{1,0:T(8,128)(2,1)S(1)}, bf16[64,3072]{1,0:T(8,128)(2,1)S(1)}, u32[]{:S(2)}, u32[]{:S(2)}) collective-permute-start(bf16[64,3072]{1,0:T(8,128)(2,1)S(1)} %pad_maximum_fusion.11), channel_id=1, source_target_pairs={{16,0},{0,16},{17,1},{1,17},{18,2},{2,18},{19,3},{3,19},{20,4},{4,... | collective-permute-start | bytes 1179656 | tf_op jit(solution)/shard_map/ppermute | solution.py:111
  38.8 9.4 %collective-permute-start.12 = (bf16[64,3200]{1,0:T(8,128)(2,1)S(1)}, bf16[64,3200]{1,0:T(8,128)(2,1)S(1)}, u32[]{:S(2)}, u32[]{:S(2)}) collective-permute-start(bf16[64,3200]{1,0:T(8,128)(2,1)S(1)} %pad_maximum_fusion.7), channel_id=1, source_target_pairs={{8,0},{12,4},{0,8},{4,12},{9,1},{13,5},{1,9},{5,13},{10,2},{14,6},... | collective-permute-start | bytes 1228808 | tf_op jit(solution)/shard_map/ppermute | solution.py:111
  48.3 3.1 %collective-permute-start.17 = (bf16[128,3072]{1,0:T(8,128)(2,1)S(1)}, bf16[128,3072]{1,0:T(8,128)(2,1)S(1)}, u32[]{:S(2)}, u32[]{:S(2)}) collective-permute-start(bf16[128,3072]{1,0:T(8,128)(2,1)S(1)} %pad_maximum_fusion.5), channel_id=1, source_target_pairs={{4,0},{0,4},{12,8},{8,12},{5,1},{1,5},{13,9},{9,13},{6,2},{2,6},{1... | collective-permute-start | bytes 2359304 | tf_op jit(solution)/shard_map/ppermute | solution.py:111
  48.4 3.4 %collective-permute-start.16 = (bf16[128,3200]{1,0:T(8,128)(2,1)S(1)}, bf16[128,3200]{1,0:T(8,128)(2,1)S(1)}, u32[]{:S(2)}, u32[]{:S(2)}) collective-permute-start(bf16[128,3200]{1,0:T(8,128)(2,1)S(1)} %pad_maximum_fusion.2), channel_id=1, source_target_pairs={{4,0},{0,4},{12,8},{8,12},{5,1},{1,5},{13,9},{9,13},{6,2},{2,6},{1... | collective-permute-start | bytes 2457608 | tf_op jit(solution)/shard_map/ppermute | solution.py:111
  60.5 4.5 %collective-permute-start.21 = (bf16[128,3072]{1,0:T(8,128)(2,1)S(1)}, bf16[128,3072]{1,0:T(8,128)(2,1)S(1)}, u32[]{:S(2)}, u32[]{:S(2)}) collective-permute-start(bf16[128,3072]{1,0:T(8,128)(2,1)S(1)} %get-tuple-element.70), channel_id=1, source_target_pairs={{4,0},{0,4},{12,8},{8,12},{5,1},{1,5},{13,9},{9,13},{6,2},{2,6},{1... | collective-permute-start | bytes 2359304 | tf_op jit(solution)/shard_map/ppermute | solution.py:111
  64.6 3.3 %collective-permute-start.18 = (bf16[128,3200]{1,0:T(8,128)(2,1)S(1)}, bf16[128,3200]{1,0:T(8,128)(2,1)S(1)}, u32[]{:S(2)}, u32[]{:S(2)}) collective-permute-start(bf16[128,3200]{1,0:T(8,128)(2,1)S(1)} %get-tuple-element.69), channel_id=1, source_target_pairs={{4,0},{0,4},{12,8},{8,12},{5,1},{1,5},{13,9},{9,13},{6,2},{2,6},{1... | collective-permute-start | bytes 2457608 | tf_op jit(solution)/shard_map/ppermute | solution.py:111
  65.3 7.8 %collective-permute-start.25 = (bf16[64,1536]{1,0:T(8,128)(2,1)S(1)}, bf16[64,1536]{1,0:T(8,128)(2,1)S(1)}, u32[]{:S(2)}, u32[]{:S(2)}) collective-permute-start(bf16[64,1536]{1,0:T(8,128)(2,1)S(1)} %pad_maximum_fusion.13), channel_id=1, source_target_pairs={{16,0},{0,16},{17,1},{1,17},{18,2},{2,18},{19,3},{3,19},{20,4},{4,... | collective-permute-start | bytes 589832 | tf_op jit(solution)/shard_map/ppermute | solution.py:111
  67.4 7.8 %collective-permute-start.24 = (bf16[64,1536]{1,0:T(8,128)(2,1)S(1)}, bf16[64,1536]{1,0:T(8,128)(2,1)S(1)}, u32[]{:S(2)}, u32[]{:S(2)}) collective-permute-start(bf16[64,1536]{1,0:T(8,128)(2,1)S(1)} %concatenate.112), channel_id=1, source_target_pairs={{8,0},{12,4},{0,8},{4,12},{9,1},{13,5},{1,9},{5,13},{10,2},{14,6},... | collective-permute-start | bytes 589832 | tf_op jit(solution)/shard_map/ppermute | solution.py:111
  68.2 11.2 %collective-permute-start.20 = (bf16[64,1664]{1,0:T(8,128)(2,1)S(1)}, bf16[64,1664]{1,0:T(8,128)(2,1)S(1)}, u32[]{:S(2)}, u32[]{:S(2)}) collective-permute-start(bf16[64,1664]{1,0:T(8,128)(2,1)S(1)} %pad_maximum_fusion.12), channel_id=1, source_target_pairs={{16,0},{0,16},{17,1},{1,17},{18,2},{2,18},{19,3},{3,19},{20,4},{4,... | collective-permute-start | bytes 638984 | tf_op jit(solution)/shard_map/ppermute | solution.py:111
  69.4 9.9 %collective-permute-start.19 = (bf16[64,1536]{1,0:T(8,128)(2,1)S(1)}, bf16[64,1536]{1,0:T(8,128)(2,1)S(1)}, u32[]{:S(2)}, u32[]{:S(2)}) collective-permute-start(bf16[64,1536]{1,0:T(8,128)(2,1)S(1)} %concatenate.110), channel_id=1, source_target_pairs={{8,0},{12,4},{0,8},{4,12},{9,1},{13,5},{1,9},{5,13},{10,2},{14,6},... | collective-permute-start | bytes 589832 | tf_op jit(solution)/shard_map/ppermute | solution.py:111
  73.2 7.2 %collective-permute-start.30 = (bf16[32,1536]{1,0:T(8,128)(2,1)S(1)}, bf16[32,1536]{1,0:T(8,128)(2,1)S(1)}, u32[]{:S(2)}, u32[]{:S(2)}) collective-permute-start(bf16[32,1536]{1,0:T(8,128)(2,1)S(1)} %split.121), channel_id=1, source_target_pairs={{8,0},{12,4},{0,8},{4,12},{9,1},{13,5},{1,9},{5,13},{10,2},{14,6},... | collective-permute-start | bytes 294920 | tf_op jit(solution)/shard_map/ppermute | solution.py:111
  75.2 5.1 %collective-permute-start.29 = (bf16[32,1536]{1,0:T(8,128)(2,1)S(1)}, bf16[32,1536]{1,0:T(8,128)(2,1)S(1)}, u32[]{:S(2)}, u32[]{:S(2)}) collective-permute-start(bf16[32,1536]{1,0:T(8,128)(2,1)S(1)} %split.122), channel_id=1, source_target_pairs={{16,0},{0,16},{17,1},{1,17},{18,2},{2,18},{19,3},{3,19},{20,4},{4,... | collective-permute-start | bytes 294920 | tf_op jit(solution)/shard_map/ppermute | solution.py:111
  79.4 5.5 %collective-permute-start.22 = (bf16[32,1536]{1,0:T(8,128)(2,1)S(1)}, bf16[32,1536]{1,0:T(8,128)(2,1)S(1)}, u32[]{:S(2)}, u32[]{:S(2)}) collective-permute-start(bf16[32,1536]{1,0:T(8,128)(2,1)S(1)} %split.123), channel_id=1, source_target_pairs={{16,0},{0,16},{17,1},{1,17},{18,2},{2,18},{19,3},{3,19},{20,4},{4,... | collective-permute-start | bytes 294920 | tf_op jit(solution)/shard_map/ppermute | solution.py:111
  79.9 5.1 %collective-permute-start.23 = (bf16[32,1664]{1,0:T(8,128)(2,1)S(1)}, bf16[32,1664]{1,0:T(8,128)(2,1)S(1)}, u32[]{:S(2)}, u32[]{:S(2)}) collective-permute-start(bf16[32,1664]{1,0:T(8,128)(2,1)S(1)} %split.120), channel_id=1, source_target_pairs={{8,0},{12,4},{0,8},{4,12},{9,1},{13,5},{1,9},{5,13},{10,2},{14,6},... | collective-permute-start | bytes 319496 | tf_op jit(solution)/shard_map/ppermute | solution.py:111
  80.5 7.3 %collective-permute-start.31 = (bf16[8,3072]{1,0:T(8,128)(2,1)S(1)}, bf16[8,3072]{1,0:T(8,128)(2,1)S(1)}, u32[]{:S(2)}, u32[]{:S(2)}) collective-permute-start(bf16[8,3072]{1,0:T(8,128)(2,1)S(1)} %get-tuple-element.103), channel_id=1, source_target_pairs={{1,0},{0,1},{3,2},{2,3},{5,4},{4,5},{7,6},{6,7},{9,8},{8,9},{11,10... | collective-permute-start | bytes 147464 | tf_op jit(solution)/shard_map/ppermute | solution.py:111
  81.7 7.8 %collective-permute-start.32 = (bf16[8,3072]{1,0:T(8,128)(2,1)S(1)}, bf16[8,3072]{1,0:T(8,128)(2,1)S(1)}, u32[]{:S(2)}, u32[]{:S(2)}) collective-permute-start(bf16[8,3072]{1,0:T(8,128)(2,1)S(1)} %get-tuple-element.105), channel_id=1, source_target_pairs={{2,0},{3,1},{0,2},{1,3},{6,4},{7,5},{4,6},{5,7},{10,8},{11,9},{8,1... | collective-permute-start | bytes 147464 | tf_op jit(solution)/shard_map/ppermute | solution.py:111
  83.2 6.4 %collective-permute-start.33 = (bf16[8,3072]{1,0:T(8,128)(2,1)S(1)}, bf16[8,3072]{1,0:T(8,128)(2,1)S(1)}, u32[]{:S(2)}, u32[]{:S(2)}) collective-permute-start(bf16[8,3072]{1,0:T(8,128)(2,1)S(1)} %get-tuple-element.104), channel_id=1, source_target_pairs={{3,0},{2,1},{1,2},{0,3},{7,4},{6,5},{5,6},{4,7},{11,8},{10,9},{9,1... | collective-permute-start | bytes 147464 | tf_op jit(solution)/shard_map/ppermute | solution.py:111
  85.0 9.0 %copy-start.2 = (s32[8]{0:T(128)S(1)}, s32[8]{0:T(128)}, u32[]{:S(2)}) copy-start(s32[8]{0:T(128)} %param.10) | copy-start | bytes 100
  85.1 4.7 %collective-permute-start.26 = (bf16[8,3200]{1,0:T(8,128)(2,1)S(1)}, bf16[8,3200]{1,0:T(8,128)(2,1)S(1)}, u32[]{:S(2)}, u32[]{:S(2)}) collective-permute-start(bf16[8,3200]{1,0:T(8,128)(2,1)S(1)} %get-tuple-element.100), channel_id=1, source_target_pairs={{1,0},{0,1},{3,2},{2,3},{5,4},{4,5},{7,6},{6,7},{9,8},{8,9},{11,10... | collective-permute-start | bytes 153608 | tf_op jit(solution)/shard_map/ppermute | solution.py:111
  85.4 6.5 %collective-permute-start.27 = (bf16[8,3200]{1,0:T(8,128)(2,1)S(1)}, bf16[8,3200]{1,0:T(8,128)(2,1)S(1)}, u32[]{:S(2)}, u32[]{:S(2)}) collective-permute-start(bf16[8,3200]{1,0:T(8,128)(2,1)S(1)} %get-tuple-element.102), channel_id=1, source_target_pairs={{2,0},{3,1},{0,2},{1,3},{6,4},{7,5},{4,6},{5,7},{10,8},{11,9},{8,1... | collective-permute-start | bytes 153608 | tf_op jit(solution)/shard_map/ppermute | solution.py:111
  87.8 5.9 %collective-permute-start.28 = (bf16[8,3200]{1,0:T(8,128)(2,1)S(1)}, bf16[8,3200]{1,0:T(8,128)(2,1)S(1)}, u32[]{:S(2)}, u32[]{:S(2)}) collective-permute-start(bf16[8,3200]{1,0:T(8,128)(2,1)S(1)} %get-tuple-element.101), channel_id=1, source_target_pairs={{3,0},{2,1},{1,2},{0,3},{7,4},{6,5},{5,6},{4,7},{11,8},{10,9},{9,1... | collective-permute-start | bytes 153608 | tf_op jit(solution)/shard_map/ppermute | solution.py:111
